TPU v7x, 32 devices: a whole 2x2x4 slice. The times are simulated.
32 devices in a mesh: pipe: 4 (over y, x), ctx: 4 (over z), exp: 2 (over core).
Axes of the slice: x: 2, y: 2, z: 4, core: 2. Of those that a mesh axis runs over, the one named last changes fastest.
Arguments:
- queries: bfloat16 [4, 2, 512, 4096], P('pipe', 'exp', 'ctx'), may hold values from -6 to 6
- rotated_keys_values: bfloat16 [4, 2, 512, 512], P('pipe', 'exp', 'ctx'), may hold values from -6 to 6
- residual: bfloat16 [4, 2, 512, 4096], P('pipe', 'exp', 'ctx'), may hold values from -6 to 6
- out_weight: bfloat16 [4, 4096, 4096], P('pipe', 'ctx', 'exp'), may hold values from -0.09375 to 0.09375
- norm_gain: float32 [4, 4096], P('pipe'), may hold values from 0.1 to 1.9
- in_weight: bfloat16 [4, 8, 4096, 1536], P('pipe', ('ctx', 'exp')), may hold values from -0.09375 to 0.09375
- down_weight: bfloat16 [4, 8, 768, 4096], P('pipe', ('ctx', 'exp')), may hold values from -0.15625 to 0.15625
- routes: int32 [4, 2, 512, 1], P('pipe', 'exp', 'ctx'), may hold values from 0 to 3; in each aligned block of 128 rows (0 to 127, 128 to 255, ..., all dimensions but the last counted through in order) at most 48 rows name the same one
- route_weight: float32 [4, 2, 512, 1], P('pipe', 'exp', 'ctx'), may hold values from 0.2 to 1
Outputs:
- section_out: bfloat16 [4, 2, 512, 4096], P('pipe', 'exp', 'ctx')
Inputs may be any that keep to these rules, and one draw needn't show every extreme that they name: Among the 128 rows of one device (aligned blocks of 128 positions of one sequence of one section), no expert is named more than 48 times, and in every draw some expert is named exactly 48 times in some block. The routes of one token name different experts.
All inputs are finite; a program needn't handle non-finite values.
Results may differ from a plain program's by a relative error of at most 0.015.
Values may be sent and summed in bfloat16 or wider, within the bound.
No kernel may reach another device: no remote copies, remote signals or barrier semaphores. Data moves between devices by JAX's collectives and lax.ppermute only.
A program may use at most 128 MiB of HBM per device.

v0:
```python
import math

import jax
import jax.numpy as jnp
import numpy as np
from jax import lax
from jax.sharding import PartitionSpec as P

QUERY_HEADS = 32
KEY_VALUE_HEADS = 2
HEAD_SIZE = 128


def from_behind(value, axis, by):
    devices = lax.axis_size(axis)
    return lax.ppermute(value, axis, [(i, (i + by) % devices) for i in range(devices)])


def attend_block(block_args, key_rows, value_rows, score_scale):
    query_block, first_row = block_args
    scores = (
        jnp.einsum("qhd,kd->hqk", query_block, key_rows, preferred_element_type=jnp.float32)
        * score_scale
    )
    row_ids = first_row + lax.broadcasted_iota(jnp.int32, scores.shape[1:], 0)
    col_ids = lax.broadcasted_iota(jnp.int32, scores.shape[1:], 1)
    scores = jnp.where((col_ids <= row_ids)[None, :, :], scores, -jnp.inf)
    attention_weights = jax.nn.softmax(scores, axis=-1).astype(jnp.bfloat16)
    attended = jnp.einsum(
        "hqk,kd->qhd", attention_weights, value_rows, preferred_element_type=jnp.float32
    )
    return attended.astype(jnp.bfloat16)


def on_device(
    queries,
    rotated_keys_values,
    residual,
    out_weight,
    norm_gain,
    in_weight,
    down_weight,
    routes,
    route_weight,
):
    context_count = lax.axis_size("ctx")
    exp_count = lax.axis_size("exp")
    token_rows = queries.shape[2]
    local_heads = QUERY_HEADS // context_count
    model_width = residual.shape[3]
    query_split = queries[0, 0].reshape(token_rows, context_count, local_heads * HEAD_SIZE)
    head_lookup = np.array(
        [
            context_slot * local_heads // (QUERY_HEADS // KEY_VALUE_HEADS)
            for context_slot in range(context_count)
        ],
        dtype=np.int32,
    )
    paired_rows = rotated_keys_values[0, 0].reshape(token_rows, 2, KEY_VALUE_HEADS, HEAD_SIZE)[
        :, :, head_lookup, :
    ]
    pair_split = paired_rows.transpose(0, 2, 1, 3).reshape(token_rows, context_count, 2 * HEAD_SIZE)
    query_heads, pair_heads = (
        lax.all_to_all(query_split, "ctx", split_axis=1, concat_axis=0, tiled=True),
        lax.all_to_all(pair_split, "ctx", split_axis=1, concat_axis=0, tiled=True),
    )
    sequence_length = query_heads.shape[0]
    key_rows = pair_heads[:, 0, :HEAD_SIZE]
    value_rows = pair_heads[:, 0, HEAD_SIZE:]
    block_rows = 512
    query_blocks = query_heads.reshape(
        sequence_length // block_rows, block_rows, local_heads, HEAD_SIZE
    )
    starts = jnp.arange(sequence_length // block_rows, dtype=jnp.int32) * block_rows
    score_scale = 1.0 / math.sqrt(HEAD_SIZE)

    def one_block(block_args):
        return attend_block(block_args, key_rows, value_rows, score_scale)

    attended = lax.map(one_block, (query_blocks, starts)).reshape(
        sequence_length, local_heads * HEAD_SIZE
    )
    out_rows = lax.all_gather(out_weight[0], "exp", axis=1, tiled=True)
    head_total = lax.psum_scatter(
        jnp.dot(attended, out_rows, preferred_element_type=jnp.float32).astype(jnp.bfloat16),
        "ctx",
        scatter_dimension=0,
        tiled=True,
    ).astype(jnp.float32)
    mixed_rows = residual[0, 0].astype(jnp.float32) + head_total
    mean_square = jnp.mean(mixed_rows * mixed_rows, axis=-1, keepdims=True)
    normed = (mixed_rows * lax.rsqrt(mean_square + 1e-06) * norm_gain[0]).astype(jnp.bfloat16)
    route_count = routes.shape[3]
    group_size = min(4, exp_count)
    experts = context_count * exp_count // group_size
    capacity = min(
        token_rows,
        group_size
        * (
            (3 * token_rows * route_count + 2 * experts * group_size - 1)
            // (2 * experts * group_size)
        ),
    )
    expert_ids = routes[0, 0].reshape(-1)
    expert_hits = (expert_ids[:, None] == jnp.arange(experts, dtype=jnp.int32)[None, :]).astype(
        jnp.int32
    )
    position = jnp.sum((jnp.cumsum(expert_hits, axis=0) - 1) * expert_hits, axis=1)
    slot_index = expert_ids * capacity + position
    slot_match = (
        jnp.arange(experts * capacity, dtype=jnp.int32)[:, None] == slot_index[None, :]
    ).astype(jnp.int32)
    slot_match = jnp.sum(
        slot_match.reshape(experts * capacity, token_rows, route_count), axis=2
    ).astype(jnp.bfloat16)
    packed = jnp.dot(slot_match, normed, preferred_element_type=jnp.float32).astype(jnp.bfloat16)
    outgoing = jnp.broadcast_to(
        packed.reshape(experts, 1, capacity, model_width),
        (experts, group_size, capacity, model_width),
    )
    arrived = lax.all_to_all(
        outgoing.reshape(experts * group_size, capacity, model_width),
        ("ctx", "exp"),
        split_axis=0,
        concat_axis=0,
        tiled=True,
    )
    slot_rows = arrived.reshape(-1, model_width)
    hidden_width = down_weight.shape[2]
    gate_up = jnp.dot(slot_rows, in_weight[0, 0], preferred_element_type=jnp.float32)
    hidden = (jax.nn.silu(gate_up[:, :hidden_width]) * gate_up[:, hidden_width:]).astype(
        jnp.bfloat16
    )
    partial_value = jnp.dot(hidden, down_weight[0, 0], preferred_element_type=jnp.float32).astype(
        jnp.bfloat16
    )
    returned = lax.all_to_all(
        partial_value.reshape(experts * group_size, capacity, model_width),
        ("ctx", "exp"),
        split_axis=0,
        concat_axis=0,
        tiled=True,
    )
    summed = jnp.sum(
        returned.astype(jnp.float32).reshape(experts, group_size, capacity, model_width), axis=1
    )
    picked = jnp.take(summed.reshape(experts * capacity, model_width), slot_index, axis=0)
    expert_mix = jnp.sum(
        (picked * route_weight[0, 0].reshape(-1)[:, None]).reshape(
            token_rows, route_count, model_width
        ),
        axis=1,
    )
    layer_out = (mixed_rows + expert_mix).astype(jnp.bfloat16)
    forwarded = from_behind(layer_out, "pipe", 1)
    return forwarded.reshape(1, 1, token_rows, model_width)


def solution(mesh):
    placed = (
        P("pipe", "exp", "ctx", None),
        P("pipe", "exp", "ctx", None),
        P("pipe", "exp", "ctx", None),
        P("pipe", "ctx", "exp"),
        P("pipe", None),
        P("pipe", ("ctx", "exp"), None, None),
        P("pipe", ("ctx", "exp"), None, None),
        P("pipe", "exp", "ctx", None),
        P("pipe", "exp", "ctx", None),
    )
    return jax.shard_map(
        on_device,
        mesh=mesh,
        in_specs=placed,
        out_specs=P("pipe", "exp", "ctx", None),
        check_vma=False,
    )
```

profile of v0, /device:TPU:0, one launch (start us, length us, event | category | flops | bytes accessed | tf_op | source)
XLA Modules:
  0.0 358.9 jit_solution(15882170621385718526)
XLA Ops:
  6.5 0.0 copy-start.6
  6.5 0.0 copy-start.2
  6.5 0.0 copy-start.1
  6.5 0.0 all-gather.3.cloned.1.call-start
  6.5 0.7 all-gather.3.cloned.1.call-update
  7.3 0.2 copy-done.2
  7.5 0.1 copy.19
  7.6 0.1 copy.20
  7.7 0.0 copy-done.6
  7.7 0.6 gather_fusion
  8.3 0.9 copy.21
  9.2 6.3 %all-to-all-start = ((bf16[128,4,256]{0,2,1:T(8,128)(2,1)}), bf16[128,4,256]{0,2,1:T(8,128)(2,1)S(1)}, u32[]{:S(2)}, u32[]{:S(2)}) async-start(bf16[128,4,256]{0,2,1:T(8,128)(2,1)} %bitcast.3), calls=%async_computation | async-start | bytes 524288 | tf_op jit(solution)/shard_map/all_to_all | solution.py:65
  15.5 0.0 copy-done.1
  15.5 0.8 reshape_squeeze.10
  16.3 1.3 copy.23
  17.6 6.8 %all-to-all-done = bf16[128,4,256]{0,2,1:T(8,128)(2,1)S(1)} async-done(((bf16[128,4,256]{0,2,1:T(8,128)(2,1)}), bf16[128,4,256]{0,2,1:T(8,128)(2,1)S(1)}, u32[]{:S(2)}, u32[]{:S(2)}) %all-to-all-start) | async-done | bytes 262176 | tf_op jit(solution)/shard_map/all_to_all | solution.py:65
  24.5 3.5 all-to-all-start.1
  28.0 0.0 reduce-scatter.2.cloned.1.call-start
  28.0 0.1 iota_compare_fusion
  28.1 0.1 copy.22
  28.3 24.1 %all-to-all-done.1 = bf16[128,4,1024]{2,0,1:T(8,128)(2,1)S(1)} async-done(((bf16[128,4,1024]{2,0,1:T(8,128)(2,1)}), bf16[128,4,1024]{2,0,1:T(8,128)(2,1)S(1)}, u32[]{:S(2)}, u32[]{:S(2)}) %all-to-all-start.1) | async-done | bytes 1048608 | tf_op jit(solution)/shard_map/all_to_all | solution.py:64
  52.3 0.3 copy.30
  52.6 1.3 fusion.21
  53.9 5.5 %fusion.33 = (f32[8,512]{1,0:T(8,128)S(1)}, f32[8,512,512]{1,2,0:T(8,128)}) fusion(f32[512,512,8]{1,0,2:T(8,128)S(1)} %fusion.21, pred[512,512]{0,1:T(8,128)(4,1)S(1)} %iota_compare_fusion), kind=kOutput, calls=%fused_computation.55 | output fusion | flops 12583423 | bytes 17055744 | tf_op jit(solution)/shard_map/while/body/eval_jaxpr/sub | solution.py:28
  59.4 4.1 %fusion.18 = bf16[128,8,512]{2,0,1:T(8,128)(2,1)S(1)} fusion(f32[8,512,512]{1,2,0:T(8,128)} %get-tuple-element.22, f32[8,512]{1,0:T(8,128)S(1)} %get-tuple-element.20, bf16[512,1,256]{2,0,1:T(8,128)(2,1)S(1)} %bitcast.95), kind=kOutput, calls=%fused_computation.25 | convolution fusion | flops 541589504 | bytes 9584640 | tf_op jit(solution)/shard_map/while/body/eval_jaxpr/hqk,kd->qhd/dot_general | solution.py:29
  63.5 0.0 all-gather.3.cloned.1.call-done
  63.6 9.5 %fusion.8 = bf16[512,4096]{1,0:T(8,128)(2,1)} fusion(bf16[512,1024]{0,1:T(8,128)(2,1)S(1)} %bitcast.103, bf16[1,1024,4096]{2,1,0:T(8,128)(2,1)} %all-gather.3.cloned.1.call-done), kind=kOutput, calls=%fused_computation.14 | convolution fusion | flops 4297064448 | bytes 13631488 | tf_op jit(solution)/shard_map/dot_general | solution.py:85
  73.1 0.0 copy-start.4
  73.1 0.0 copy-start
  73.1 0.0 copy-start.3
  73.1 0.0 reduce-scatter.2.cloned.1.call-update
  73.1 0.6 copy-done.4
  73.7 0.1 fusion.27
  73.8 0.2 reduce_window_sum.11
  74.0 0.2 select_reduce_fusion
  74.2 74.9 %reduce-scatter.2.cloned.1.call-done = bf16[128,4096]{1,0:T(8,128)(2,1)} async-done(((bf16[512,4096]{1,0:T(8,128)(2,1)}), bf16[128,4096]{1,0:T(8,128)(2,1)}) %reduce-scatter.2.cloned.1.call-update) | async-done | bytes 1048592 | tf_op jit(solution)/shard_map/reduce_scatter | solution.py:84
  149.1 0.0 copy-done
  149.1 1.6 multiply_reduce_fusion
  150.8 0.0 copy-done.3
  150.8 1.9 convolution_convert_fusion
  152.7 0.4 broadcast_in_dim.55
  153.1 0.0 slice-start
  153.1 75.8 %all_to_all.43 = bf16[8,48,4096]{2,1,0:T(8,128)(2,1)S(1)} all-to-all(bf16[8,48,4096]{2,1,0:T(8,128)(2,1)S(1)} %bitcast.86), channel_id=1, replica_groups=mesh['pipe'=4,'ctx'=4,'exp'=2] {'ctx','exp'}, dimensions={0} | all-to-all | bytes 6291456 | tf_op jit(solution)/shard_map/all_to_all | solution.py:121
  228.9 0.0 slice-start.1
  228.9 8.2 %fusion.1 = f32[384,1536]{1,0:T(8,128)S(1)} fusion(bf16[384,4096]{1,0:T(8,128)(2,1)S(1)} %bitcast.90, bf16[1,1,4096,1536]{3,2,1,0:T(8,128)(2,1)} %param.16), kind=kOutput, calls=%fused_computation.3 | convolution fusion | flops 4831838208 | bytes 18087936 | tf_op jit(solution)/shard_map/dot_general | solution.py:130
  237.1 0.0 slice-done
  237.1 0.0 slice-done.1
  237.1 4.1 %fusion.11 = bf16[384,4096]{1,0:T(8,128)(2,1)} fusion(bf16[1,1,768,4096]{3,2,1,0:T(8,128)(2,1)S(1)} %bitcast.102, f32[384,1536]{1,0:T(8,128)S(1)} %fusion.1), kind=kOutput, calls=%fused_computation.15 | convolution fusion | flops 2419261440 | bytes 11796480 | tf_op jit(solution)/shard_map/dot_general | solution.py:134
  241.2 4.4 %all-to-all-start.3 = ((bf16[8,48,4096]{2,1,0:T(8,128)(2,1)}), bf16[8,48,4096]{2,1,0:T(8,128)(2,1)}, u32[]{:S(2)}, u32[]{:S(2)}) async-start(bf16[8,48,4096]{2,1,0:T(8,128)(2,1)} %bitcast.24), calls=%async_computation.4 | async-start | bytes 6291456 | tf_op jit(solution)/shard_map/all_to_all | solution.py:137
  245.6 71.5 %all-to-all-done.3 = bf16[8,48,4096]{2,1,0:T(8,128)(2,1)} async-done(((bf16[8,48,4096]{2,1,0:T(8,128)(2,1)}), bf16[8,48,4096]{2,1,0:T(8,128)(2,1)}, u32[]{:S(2)}, u32[]{:S(2)}) %all-to-all-start.3) | async-done | bytes 3145760 | tf_op jit(solution)/shard_map/all_to_all | solution.py:137
  317.2 3.0 convert_reduce_fusion
  320.2 0.0 copy-start.5
  320.2 2.6 gather_fusion.1
  322.7 0.0 copy-done.5
  322.8 2.7 add_convert_fusion
  325.4 1.5 collective-permute-start
  327.0 24.1 %collective-permute-done = bf16[128,4096]{1,0:T(8,128)(2,1)S(1)} collective-permute-done((bf16[128,4096]{1,0:T(8,128)(2,1)S(1)}, bf16[128,4096]{1,0:T(8,128)(2,1)S(1)}, u32[]{:S(2)}, u32[]{:S(2)}) %collective-permute-start) | collective-permute-done | bytes 1048608 | tf_op jit(solution)/shard_map/ppermute | solution.py:16
  351.1 1.0 copy.34
  (6 shorter events, 0.0 us)
Async XLA Ops:
  6.5 1.2 copy-start.6
  6.5 0.9 copy-start.2
  6.5 9.0 %copy-start.1 = (bf16[1,1,128,4096]{3,2,1,0:T(8,128)(2,1)S(1)}, bf16[1,1,128,4096]{3,2,1,0:T(8,128)(2,1)}, u32[]{:S(2)}) copy-start(bf16[1,1,128,4096]{3,2,1,0:T(8,128)(2,1)} %param.11) | copy-start | bytes 3145732
  6.5 57.0 %all-gather.3.cloned.1.call-start = ((), (), s32[]{:S(2)}) async-start(), calls=%async_computation.6 | async-start | bytes 12582912 | tf_op jit(solution)/shard_map/all_gather | solution.py:83
  9.2 15.2 %all-to-all-start = ((bf16[128,4,256]{0,2,1:T(8,128)(2,1)}), bf16[128,4,256]{0,2,1:T(8,128)(2,1)S(1)}, u32[]{:S(2)}, u32[]{:S(2)}) async-start(bf16[128,4,256]{0,2,1:T(8,128)(2,1)} %bitcast.3), calls=%async_computation | async-start | bytes 524288 | tf_op jit(solution)/shard_map/all_to_all | solution.py:65
  24.5 27.9 %all-to-all-start.1 = ((bf16[128,4,1024]{2,0,1:T(8,128)(2,1)}), bf16[128,4,1024]{2,0,1:T(8,128)(2,1)S(1)}, u32[]{:S(2)}, u32[]{:S(2)}) async-start(bf16[128,4,1024]{2,0,1:T(8,128)(2,1)} %copy.23), calls=%async_computation.1 | async-start | bytes 2097152 | tf_op jit(solution)/shard_map/all_to_all | solution.py:64
  28.0 121.2 %reduce-scatter.2.cloned.1.call-start = ((), (), s32[]{:S(2)}) async-start(), calls=%async_computation.5 | async-start | bytes 5242880 | tf_op jit(solution)/shard_map/reduce_scatter | solution.py:84
  73.1 0.7 copy-start.4
  73.1 76.1 %copy-start = (bf16[1,1,128,4096]{3,2,1,0:T(8,128)(2,1)S(1)}, bf16[1,1,128,4096]{3,2,1,0:T(8,128)(2,1)}, u32[]{:S(2)}) copy-start(bf16[1,1,128,4096]{3,2,1,0:T(8,128)(2,1)} %param.13) | copy-start | bytes 3145732
  73.1 77.7 %copy-start.3 = (f32[1,4096]{1,0:T(1,128)S(1)}, f32[1,4096]{1,0:T(1,128)}, u32[]{:S(2)}) copy-start(f32[1,4096]{1,0:T(1,128)} %param.15) | copy-start | bytes 49156
  153.1 84.0 %slice-start = ((s8[6291456]{0:T(1024)(128)(4,1)}), s8[4194304]{0:T(1024)(128)(4,1)S(1)}, s32[]{:S(2)}) async-start(s8[6291456]{0:T(1024)(128)(4,1)} %bitcast.101), calls=%async_computation.7 | async-start | bytes 8388608
  228.9 8.2 %slice-start.1 = ((s8[6291456]{0:T(1024)(128)(4,1)}), s8[2097152]{0:T(1024)(128)(4,1)S(1)}, s32[]{:S(2)}) async-start(s8[6291456]{0:T(1024)(128)(4,1)} %bitcast.101), calls=%async_computation.8 | async-start | bytes 4194304
  241.2 76.0 %all-to-all-start.3 = ((bf16[8,48,4096]{2,1,0:T(8,128)(2,1)}), bf16[8,48,4096]{2,1,0:T(8,128)(2,1)}, u32[]{:S(2)}, u32[]{:S(2)}) async-start(bf16[8,48,4096]{2,1,0:T(8,128)(2,1)} %bitcast.24), calls=%async_computation.4 | async-start | bytes 6291456 | tf_op jit(solution)/shard_map/all_to_all | solution.py:137
  320.2 2.6 copy-start.5
  325.4 25.7 %collective-permute-start = (bf16[128,4096]{1,0:T(8,128)(2,1)S(1)}, bf16[128,4096]{1,0:T(8,128)(2,1)S(1)}, u32[]{:S(2)}, u32[]{:S(2)}) collective-permute-start(bf16[128,4096]{1,0:T(8,128)(2,1)S(1)} %add_convert_fusion), channel_id=1, source_target_pairs={{0,8},{8,16},{16,24},{24,0},{1,9},{9,17},{17,25},{25,1},{2,10},{10... | collective-permute-start | bytes 3145736 | tf_op jit(solution)/shard_map/ppermute | solution.py:16
Sparse Core Ops, SparseCore 0:
  8.9 22.5 all-gather.2
  73.2 75.8 reduce-scatter.1
where the time goes:
time: 359 us
  waiting for transfers between devices  202 us (56%)
  blocking collectives  75.8 us (21%)
  matrix products  29 us (8%)
  starting transfers between devices  15.8 us (4%)
  between operations  13.6 us (4%)
  other arithmetic  13.4 us (4%)
  local copies, waits for them, and re-layouts  8.95 us (2%)
    all_to_all x1, blocking collectives, on_device(): lax.all_to_all(outgoing.reshape(experts * group_size, capacity, model_wid...  75.8 us
    reduce_scatter x1, waiting for transfers between devices, on_device(): lax.psum_scatter(jnp.dot(attended, out_rows, preferred_element_type=jnp.f...  74.9 us
    all_to_all x1, waiting for transfers between devices, on_device(): lax.all_to_all(partial_value.reshape(experts * group_size, capacity, mode...  71.5 us
    ppermute x1, waiting for transfers between devices, from_behind(): lax.ppermute(value, axis, [(i, (i + by) % devices) for i in range(devices)])  24.1 us
    all_to_all x1, waiting for transfers between devices, on_device(): lax.all_to_all(query_split, 'ctx', split_axis=1, concat_axis=0, tiled=True)  24.1 us
    dot_general x1, matrix products, on_device(): jnp.dot(attended, out_rows, preferred_element_type=jnp.float32)  9.51 us
    dot_general x1, matrix products, on_device(): jnp.dot(slot_rows, in_weight[0, 0], preferred_element_type=jnp.float32)  8.19 us
  transfers between devices with their start and end apart: 6, of which 5 were waited for; matrix products, arithmetic and copies ran while one was open for 4% of the time, Pallas kernels for 0%

commit v1 on v0

v1 whole, which is shorter than its diff:
```python
import math

import jax
import jax.numpy as jnp
from jax import lax
from jax.sharding import PartitionSpec as P

QUERY_HEADS = 32
KEY_VALUE_HEADS = 2
HEAD_SIZE = 128
DISPATCH_CHUNKS = 2
RETURN_CHUNKS = 2


def shift(value, axis, by):
    devices = lax.axis_size(axis)
    return lax.ppermute(value, axis, [(i, (i + by) % devices) for i in range(devices)])


def attend_block(query_block, key_rows, value_rows, row_ids, col_ids):
    scores = jnp.einsum(
        "qhd,kd->hqk", query_block, key_rows, preferred_element_type=jnp.float32
    ) * (1.0 / math.sqrt(HEAD_SIZE))
    scores = jnp.where((col_ids[None, :] <= row_ids[:, None])[None, :, :], scores, -jnp.inf)
    attention_weights = jax.nn.softmax(scores, axis=-1).astype(jnp.bfloat16)
    attended = jnp.einsum(
        "hqk,kd->qhd", attention_weights, value_rows, preferred_element_type=jnp.float32
    )
    return attended.astype(jnp.bfloat16)


def mixed_halves(queries, keys_values, residual, out_weight):
    contexts, exps = lax.axis_size("ctx"), lax.axis_size("exp")
    me, my_exp = lax.axis_index("ctx"), lax.axis_index("exp")
    rows = queries.shape[0]
    width = residual.shape[1]
    local_heads = QUERY_HEADS // contexts
    group_width = local_heads * HEAD_SIZE

    def pair_for(owner):
        head = owner * local_heads // (QUERY_HEADS // KEY_VALUE_HEADS)
        key = lax.dynamic_slice_in_dim(keys_values, head * HEAD_SIZE, HEAD_SIZE, 1)
        value = lax.dynamic_slice_in_dim(
            keys_values, (KEY_VALUE_HEADS + head) * HEAD_SIZE, HEAD_SIZE, 1
        )
        return jnp.concatenate([key, value], axis=1)

    def queries_for(owner):
        return lax.dynamic_slice_in_dim(queries, owner * group_width, group_width, 1)

    pairs = [pair_for(me)]
    blocks = [queries_for(me)]
    for k in range(1, contexts):
        pairs.append(shift(pair_for((me + k) % contexts), "ctx", k))
    for k in range(1, contexts):
        blocks.append(shift(queries_for((me + k) % contexts), "ctx", k))
    if exps == 2:
        weights = [out_weight, shift(out_weight, "exp", 1)]
        first = my_exp * (width // 2)
    else:
        gathered = lax.all_gather(out_weight, "exp", axis=1, tiled=True)
        weights = [gathered[:, : width // 2], gathered[:, width // 2 :]]
        first = 0
    offsets = [first, width // 2 - first]

    pair_rows = jnp.concatenate(pairs, axis=0)
    key_rows, value_rows = pair_rows[:, :HEAD_SIZE], pair_rows[:, HEAD_SIZE:]
    within = jnp.arange(rows, dtype=jnp.int32)
    origins = [(me - k) % contexts * rows for k in range(contexts)]
    col_ids = jnp.concatenate([origin + within for origin in origins])

    held = [None, None]
    for k in [*range(1, contexts), 0]:
        attended = attend_block(
            blocks[k].reshape(rows, local_heads, HEAD_SIZE),
            key_rows,
            value_rows,
            origins[k] + within,
            col_ids,
        ).reshape(rows, group_width)
        for half in range(2):
            term = jnp.dot(attended, weights[half], preferred_element_type=jnp.float32)
            if held[half] is not None:
                term = term + held[half].astype(jnp.float32)
            if k == 0:
                own = lax.dynamic_slice_in_dim(residual, offsets[half], width // 2, 1)
                held[half] = term + own.astype(jnp.float32)
            else:
                held[half] = shift(term.astype(jnp.bfloat16), "ctx", 1)
    return held, first


def on_device(
    queries,
    rotated_keys_values,
    residual,
    out_weight,
    norm_gain,
    in_weight,
    down_weight,
    routes,
    route_weight,
):
    contexts, exps = lax.axis_size("ctx"), lax.axis_size("exp")
    me, my_exp = lax.axis_index("ctx"), lax.axis_index("exp")
    token_rows = queries.shape[2]
    model_width = residual.shape[3]
    halves, first = mixed_halves(
        queries[0, 0], rotated_keys_values[0, 0], residual[0, 0], out_weight[0]
    )
    mixed_rows = jnp.concatenate(halves, axis=1)
    if exps == 2:
        mixed_rows = jnp.where(first == 0, mixed_rows, jnp.concatenate(halves[::-1], axis=1))

    mean_square = jnp.mean(mixed_rows * mixed_rows, axis=-1, keepdims=True)
    normed = (mixed_rows * lax.rsqrt(mean_square + 1e-06) * norm_gain[0]).astype(jnp.bfloat16)

    route_count = routes.shape[3]
    group_size = min(4, exps)
    per_context = exps // group_size
    experts = contexts * per_context
    capacity = min(
        token_rows,
        group_size
        * (
            (3 * token_rows * route_count + 2 * experts * group_size - 1)
            // (2 * experts * group_size)
        ),
    )
    slots = experts * capacity
    expert_ids = routes[0, 0].reshape(-1)
    expert_hits = (expert_ids[:, None] == jnp.arange(experts, dtype=jnp.int32)[None, :]).astype(
        jnp.int32
    )
    position = jnp.sum((jnp.cumsum(expert_hits, axis=0) - 1) * expert_hits, axis=1)
    distance = (expert_ids // per_context - me) % contexts
    slot_index = (distance * per_context + expert_ids % per_context) * capacity + position
    slot_index = slot_index.reshape(token_rows, route_count)
    slot_ids = jnp.arange(slots, dtype=jnp.int32)
    slot_match = sum(
        (slot_ids[:, None] == slot_index[None, :, r]).astype(jnp.bfloat16)
        for r in range(route_count)
    )
    packed = jnp.dot(slot_match, normed, preferred_element_type=jnp.float32).astype(jnp.bfloat16)
    packed = packed.reshape(contexts, per_context, capacity, model_width)

    def wanted_by(arrived, exp):
        if per_context == 1:
            return arrived[:, 0]
        return lax.dynamic_index_in_dim(arrived, exp // group_size, 1, keepdims=False)

    hidden_width = down_weight.shape[2]
    gate_up = 0.0
    step = model_width // DISPATCH_CHUNKS
    for chunk in range(DISPATCH_CHUNKS):
        part = packed[..., chunk * step : (chunk + 1) * step]
        arrived = jnp.stack(
            [part[0]] + [shift(part[k], "ctx", k) for k in range(1, contexts)], axis=0
        )
        gathered = [wanted_by(arrived, my_exp)]
        for k in range(1, exps):
            gathered.append(shift(wanted_by(arrived, (my_exp + k) % exps), "exp", k))
        slot_rows = jnp.concatenate(gathered, axis=0).reshape(-1, step)
        gate_up = gate_up + jnp.dot(
            slot_rows,
            in_weight[0, 0, chunk * step : (chunk + 1) * step],
            preferred_element_type=jnp.float32,
        )
    hidden = (jax.nn.silu(gate_up[:, :hidden_width]) * gate_up[:, hidden_width:]).astype(
        jnp.bfloat16
    )

    step = model_width // RETURN_CHUNKS
    outputs = []
    for chunk in range(RETURN_CHUNKS):
        columns = slice(chunk * step, (chunk + 1) * step)
        part = jnp.dot(hidden, down_weight[0, 0, :, columns], preferred_element_type=jnp.float32)
        part = part.reshape(exps, contexts, capacity, step)
        sums = [0.0] * per_context
        for k in range(exps):
            back = part[k]
            if k:
                back = shift(back.astype(jnp.bfloat16), "exp", -k).astype(jnp.float32)
            if per_context == 1:
                sums[0] = sums[0] + back
            else:
                place = (my_exp + k) % exps // group_size
                sums = [s + jnp.where(place == i, back, 0.0) for i, s in enumerate(sums)]
        total = jnp.stack(sums, axis=1).astype(jnp.bfloat16)
        returned = jnp.concatenate(
            [total[0]] + [shift(total[k], "ctx", -k) for k in range(1, contexts)], axis=0
        ).reshape(slots, step)
        layer = mixed_rows[:, columns]
        for r in range(route_count):
            match = (slot_ids[None, :] == slot_index[:, r, None]).astype(jnp.bfloat16)
            picked = jnp.dot(match, returned, preferred_element_type=jnp.float32)
            layer = layer + picked * route_weight[0, 0, :, r, None]
        outputs.append(shift(layer.astype(jnp.bfloat16), "pipe", 1))
    return jnp.concatenate(outputs, axis=1).reshape(1, 1, token_rows, model_width)


def solution(mesh):
    placed = (
        P("pipe", "exp", "ctx", None),
        P("pipe", "exp", "ctx", None),
        P("pipe", "exp", "ctx", None),
        P("pipe", "ctx", "exp"),
        P("pipe", None),
        P("pipe", ("ctx", "exp"), None, None),
        P("pipe", ("ctx", "exp"), None, None),
        P("pipe", "exp", "ctx", None),
        P("pipe", "exp", "ctx", None),
    )
    return jax.shard_map(
        on_device,
        mesh=mesh,
        in_specs=placed,
        out_specs=P("pipe", "exp", "ctx", None),
        check_vma=False,
    )
```

time: 359 us -> 224 us (0.62)
  the two profiles are of different devices: /device:TPU:0 before, /device:TPU:12 now
where the time goes in v1:
time: 224 us
  waiting for transfers between devices  133 us (59%)
  starting transfers between devices  42.1 us (19%)
  matrix products  37.7 us (17%)
  local copies, waits for them, and re-layouts  6.75 us (3%)
  other arithmetic  3.91 us (2%)
    ppermute x31, waiting for transfers between devices, shift(): lax.ppermute(value, axis, [(i, (i + by) % devices) for i in range(devices)])  133 us
    ppermute x31, starting transfers between devices, shift(): lax.ppermute(value, axis, [(i, (i + by) % devices) for i in range(devices)])  42.1 us
    dot_general x8, matrix products, mixed_halves(): term = jnp.dot(attended, weights[half], preferred_element_type=jnp.float32)  19.1 us
    dot_general x2, matrix products, on_device(): jnp.dot(slot_rows, in_weight[0, 0, chunk * step:(chunk + 1) * step], pref...  5.29 us
    dot_general x4, matrix products, attend_block(): jnp.einsum('hqk,kd->qhd', attention_weights, value_rows, preferred_elemen...  5.11 us
  transfers between devices with their start and end apart: 31, of which 18 were waited for; matrix products, arithmetic and copies ran while one was open for 16% of the time, Pallas kernels for 0%

profile of v1, /device:TPU:12, one launch (start us, length us, event | category | flops | bytes accessed | tf_op | source)
XLA Modules:
  0.0 223.8 jit_solution(4353413241907726319)
XLA Ops:
  0.0 1.0 dynamic-slice_bitcast_fusion.7
  1.0 0.5 collective-permute-start.2
  1.5 1.6 collective-permute-start
  3.2 4.4 %collective-permute-start.1 = (bf16[128,256]{1,0:T(8,128)(2,1)S(1)}, bf16[128,256]{1,0:T(8,128)(2,1)S(1)}, u32[]{:S(2)}, u32[]{:S(2)}) collective-permute-start(bf16[128,256]{1,0:T(8,128)(2,1)S(1)} %pad_maximum_fusion.6), channel_id=1, source_target_pairs={{0,4},{2,6},{4,0},{6,2},{1,5},{3,7},{5,1},{7,3},{8,12},{10,14},{12... | collective-permute-start | bytes 196616 | tf_op jit(solution)/shard_map/ppermute | solution.py:17
  7.6 1.3 constant_dynamic-slice_fusion.1
  10.5 2.0 collective-permute-start.3
  12.6 0.8 fusion.96
  13.3 1.0 convolution_convert_fusion.6
  14.4 11.9 %collective-permute-done.5 = bf16[128,1024]{0,1:T(8,128)(2,1)S(1)} collective-permute-done((bf16[128,1024]{0,1:T(8,128)(2,1)S(1)}, bf16[128,1024]{0,1:T(8,128)(2,1)S(1)}, u32[]{:S(2)}, u32[]{:S(2)}) %collective-permute-start.5) | collective-permute-done | bytes 262176 | tf_op jit(solution)/shard_map/ppermute | solution.py:17
  26.3 0.8 fusion.98
  27.1 1.0 convolution_convert_fusion.3
  28.1 2.9 %convolution_convert_fusion.2 = bf16[128,2048]{1,0:T(8,128)(2,1)S(1)} fusion(bf16[128,1024]{0,1:T(8,128)(2,1)S(1)} %bitcast.234, bf16[1,1024,2048]{2,1,0:T(8,128)(2,1)} %param.12), kind=kOutput, calls=%fused_computation.31 | convolution fusion | flops 537133056 | bytes 4980736 | tf_op jit(solution)/shard_map/dot_general | solution.py:82
  31.1 3.0 %collective-permute-start.6 = (bf16[128,2048]{1,0:T(8,128)(2,1)S(1)}, bf16[128,2048]{1,0:T(8,128)(2,1)S(1)}, u32[]{:S(2)}, u32[]{:S(2)}) collective-permute-start(bf16[128,2048]{1,0:T(8,128)(2,1)S(1)} %convolution_convert_fusion.2), channel_id=1, source_target_pairs={{0,2},{2,4},{4,6},{6,0},{1,3},{3,5},{5,7},{7,1},{8,10},{10,12},{12... | collective-permute-start | bytes 1572872 | tf_op jit(solution)/shard_map/ppermute | solution.py:17
  34.1 6.5 %collective-permute-done.3 = bf16[128,1024]{0,1:T(8,128)(2,1)} collective-permute-done((bf16[128,1024]{0,1:T(8,128)(2,1)S(1)}, bf16[128,1024]{0,1:T(8,128)(2,1)}, u32[]{:S(2)}, u32[]{:S(2)}) %collective-permute-start.3) | collective-permute-done | bytes 262176 | tf_op jit(solution)/shard_map/ppermute | solution.py:17
  40.6 1.7 fusion.97
  42.4 0.8 fusion.99
  43.1 2.0 convolution_convert_fusion.5
  45.1 2.9 %convolution_convert_fusion.1 = bf16[128,2048]{1,0:T(8,128)(2,1)S(1)} fusion(bf16[128,1024]{0,1:T(8,128)(2,1)S(1)} %bitcast.235, bf16[1024,2048]{1,0:T(8,128)(2,1)} %collective-permute-done.9), kind=kOutput, calls=%fused_computation.30 | convolution fusion | flops 537133056 | bytes 4980736 | tf_op jit(solution)/shard_map/dot_general | solution.py:82
  48.1 2.8 %collective-permute-start.10 = (bf16[128,2048]{1,0:T(8,128)(2,1)S(1)}, bf16[128,2048]{1,0:T(8,128)(2,1)S(1)}, u32[]{:S(2)}, u32[]{:S(2)}) collective-permute-start(bf16[128,2048]{1,0:T(8,128)(2,1)S(1)} %convolution_convert_fusion.1), channel_id=1, source_target_pairs={{0,2},{2,4},{4,6},{6,0},{1,3},{3,5},{5,7},{7,1},{8,10},{10,12},{12... | collective-permute-start | bytes 1572872 | tf_op jit(solution)/shard_map/ppermute | solution.py:17
  50.9 1.0 convolution_convert_fusion.4
  51.9 2.9 %add_convert_fusion.3 = bf16[128,2048]{1,0:T(8,128)(2,1)S(1)} fusion(bf16[128,2048]{1,0:T(8,128)(2,1)S(1)} %collective-permute-done.6, bf16[128,1024]{0,1:T(8,128)(2,1)S(1)} %bitcast.238, bf16[1,1024,2048]{2,1,0:T(8,128)(2,1)} %param.12), kind=kOutput, calls=%fused_computation.68 | convolution fusion | flops 537657344 | bytes 5505024 | tf_op jit(solution)/shard_map/dot_general | solution.py:82
  54.9 10.6 %collective-permute-done.10 = bf16[128,2048]{1,0:T(8,128)(2,1)S(1)} collective-permute-done((bf16[128,2048]{1,0:T(8,128)(2,1)S(1)}, bf16[128,2048]{1,0:T(8,128)(2,1)S(1)}, u32[]{:S(2)}, u32[]{:S(2)}) %collective-permute-start.10) | collective-permute-done | bytes 524320 | tf_op jit(solution)/shard_map/ppermute | solution.py:17
  65.6 2.9 %fusion.23 = bf16[128,2048]{1,0:T(8,128)(2,1)S(1)} fusion(bf16[128,1024]{0,1:T(8,128)(2,1)S(1)} %bitcast.239, bf16[1024,2048]{1,0:T(8,128)(2,1)} %collective-permute-done.9, bf16[128,2048]{1,0:T(8,128)(2,1)S(1)} %collective-permute-done.10), kind=kOutput, calls=%fused_computation.27 | convolution fusion | flops 537657344 | bytes 5505024 | tf_op jit(solution)/shard_map/dot_general | solution.py:82
  68.9 0.7 fusion.75
  69.6 7.2 %collective-permute-done.7 = bf16[128,2048]{1,0:T(8,128)(2,1)S(1)} collective-permute-done((bf16[128,2048]{1,0:T(8,128)(2,1)S(1)}, bf16[128,2048]{1,0:T(8,128)(2,1)S(1)}, u32[]{:S(2)}, u32[]{:S(2)}) %collective-permute-start.7) | collective-permute-done | bytes 524320 | tf_op jit(solution)/shard_map/ppermute | solution.py:17
  77.1 10.9 %collective-permute-done.11 = bf16[128,2048]{1,0:T(8,128)(2,1)S(1)} collective-permute-done((bf16[128,2048]{1,0:T(8,128)(2,1)S(1)}, bf16[128,2048]{1,0:T(8,128)(2,1)S(1)}, u32[]{:S(2)}, u32[]{:S(2)}) %collective-permute-start.11) | collective-permute-done | bytes 524320 | tf_op jit(solution)/shard_map/ppermute | solution.py:17
  88.1 2.9 %fusion.22 = bf16[128,2048]{1,0:T(8,128)(2,1)S(1)} fusion(bf16[128,1024]{0,1:T(8,128)(2,1)S(1)} %bitcast.237, bf16[1024,2048]{1,0:T(8,128)(2,1)} %collective-permute-done.9, bf16[128,2048]{1,0:T(8,128)(2,1)S(1)} %collective-permute-done.11), kind=kOutput, calls=%fused_computation.26 | convolution fusion | flops 537657344 | bytes 5505024 | tf_op jit(solution)/shard_map/dot_general | solution.py:82
  91.2 0.7 fusion.77
  91.9 7.4 %collective-permute-done.8 = bf16[128,2048]{1,0:T(8,128)(2,1)S(1)} collective-permute-done((bf16[128,2048]{1,0:T(8,128)(2,1)S(1)}, bf16[128,2048]{1,0:T(8,128)(2,1)S(1)}, u32[]{:S(2)}, u32[]{:S(2)}) %collective-permute-start.8) | collective-permute-done | bytes 524320 | tf_op jit(solution)/shard_map/ppermute | solution.py:17
  99.5 9.9 %collective-permute-done.12 = bf16[128,2048]{1,0:T(8,128)(2,1)S(1)} collective-permute-done((bf16[128,2048]{1,0:T(8,128)(2,1)S(1)}, bf16[128,2048]{1,0:T(8,128)(2,1)S(1)}, u32[]{:S(2)}, u32[]{:S(2)}) %collective-permute-start.12) | collective-permute-done | bytes 524320 | tf_op jit(solution)/shard_map/ppermute | solution.py:17
  109.3 2.9 %fusion.21 = f32[128,2048]{1,0:T(8,128)S(1)} fusion(bf16[128,1024]{0,1:T(8,128)(2,1)S(1)} %bitcast.231, bf16[1024,2048]{1,0:T(8,128)(2,1)} %collective-permute-done.9, bf16[128,2048]{1,0:T(8,128)(2,1)S(1)} %collective-permute-done.12, bf16[1,1,128,4096]{3,2,1,0:T(8,128)(2,1)S(1)} %copy-done.3, s32[]{:T(128)S(6)} %select_n.175), kind=kOutput, calls=%fused_computation.25 | convolution fusion | flops 537919488 | bytes 6553604 | tf_op jit(solution)/shard_map/dot_general | solution.py:82
  113.0 0.7 convolution_convert_fusion
  113.7 3.6 %collective-permute-start.19 = (bf16[1,48,2048]{2,1,0:T(8,128)(2,1)S(1)}, bf16[1,48,2048]{2,1,0:T(8,128)(2,1)S(1)}, u32[]{:S(2)}, u32[]{:S(2)}) collective-permute-start(bf16[1,48,2048]{2,1,0:T(8,128)(2,1)S(1)} %get-tuple-element.14), channel_id=1, source_target_pairs={{0,6},{2,0},{4,2},{6,4},{1,7},{3,1},{5,3},{7,5},{8,14},{10,8},{12,... | collective-permute-start | bytes 589832 | tf_op jit(solution)/shard_map/ppermute | solution.py:17
  117.5 1.5 collective-permute-start.17
  118.9 10.3 %collective-permute-done.19 = bf16[1,48,2048]{2,1,0:T(8,128)(2,1)S(1)} collective-permute-done((bf16[1,48,2048]{2,1,0:T(8,128)(2,1)S(1)}, bf16[1,48,2048]{2,1,0:T(8,128)(2,1)S(1)}, u32[]{:S(2)}, u32[]{:S(2)}) %collective-permute-start.19) | collective-permute-done | bytes 196640 | tf_op jit(solution)/shard_map/ppermute | solution.py:17
  129.3 3.3 %collective-permute-done.17 = bf16[1,48,2048]{2,1,0:T(8,128)(2,1)S(1)} collective-permute-done((bf16[1,48,2048]{2,1,0:T(8,128)(2,1)S(1)}, bf16[1,48,2048]{2,1,0:T(8,128)(2,1)S(1)}, u32[]{:S(2)}, u32[]{:S(2)}) %collective-permute-start.17) | collective-permute-done | bytes 196640 | tf_op jit(solution)/shard_map/ppermute | solution.py:17
  132.8 1.0 collective-permute-start.15
  133.8 2.9 %collective-permute-start.14 = (bf16[1,48,2048]{2,1,0:T(8,128)(2,1)S(1)}, bf16[1,48,2048]{2,1,0:T(8,128)(2,1)S(1)}, u32[]{:S(2)}, u32[]{:S(2)}) collective-permute-start(bf16[1,48,2048]{2,1,0:T(8,128)(2,1)S(1)} %get-tuple-element.11), channel_id=1, source_target_pairs={{0,4},{2,6},{4,0},{6,2},{1,5},{3,7},{5,1},{7,3},{8,12},{10,14},{12... | collective-permute-start | bytes 589832 | tf_op jit(solution)/shard_map/ppermute | solution.py:17
  136.8 4.3 %collective-permute-done.15 = bf16[1,48,2048]{2,1,0:T(8,128)(2,1)S(1)} collective-permute-done((bf16[1,48,2048]{2,1,0:T(8,128)(2,1)S(1)}, bf16[1,48,2048]{2,1,0:T(8,128)(2,1)S(1)}, u32[]{:S(2)}, u32[]{:S(2)}) %collective-permute-start.15) | collective-permute-done | bytes 196640 | tf_op jit(solution)/shard_map/ppermute | solution.py:17
  141.1 5.8 %collective-permute-done.14 = bf16[1,48,2048]{2,1,0:T(8,128)(2,1)S(1)} collective-permute-done((bf16[1,48,2048]{2,1,0:T(8,128)(2,1)S(1)}, bf16[1,48,2048]{2,1,0:T(8,128)(2,1)S(1)}, u32[]{:S(2)}, u32[]{:S(2)}) %collective-permute-start.14) | collective-permute-done | bytes 196640 | tf_op jit(solution)/shard_map/ppermute | solution.py:17
  146.8 4.2 %collective-permute-done.13 = bf16[1,48,2048]{2,1,0:T(8,128)(2,1)S(1)} collective-permute-done((bf16[1,48,2048]{2,1,0:T(8,128)(2,1)S(1)}, bf16[1,48,2048]{2,1,0:T(8,128)(2,1)S(1)}, u32[]{:S(2)}, u32[]{:S(2)}) %collective-permute-start.13) | collective-permute-done | bytes 196640 | tf_op jit(solution)/shard_map/ppermute | solution.py:17
  151.4 2.7 %fusion.4 = f32[384,1536]{1,0:T(8,128)S(1)} fusion(bf16[384,2048]{1,0:T(8,128)(2,1)S(1)} %bitcast.233, bf16[1,1,4096,1536]{3,2,1,0:T(8,128)(2,1)S(1)} %bitcast.259), kind=kOutput, calls=%fused_computation.4 | convolution fusion | flops 2415919104 | bytes 10223616 | tf_op jit(solution)/shard_map/dot_general | solution.py:164
  154.2 2.6 %fusion.16 = f32[384,1536]{1,0:T(8,128)S(1)} fusion(f32[384,1536]{1,0:T(8,128)S(1)} %fusion.4, bf16[384,2048]{1,0:T(8,128)(2,1)S(1)} %bitcast.232, bf16[1,1,4096,1536]{3,2,1,0:T(8,128)(2,1)S(1)} %bitcast.259), kind=kOutput, calls=%fused_computation.17 | convolution fusion | flops 2416508928 | bytes 12582912 | tf_op jit(solution)/shard_map/dot_general | solution.py:164
  157.3 1.4 fusion.10
  158.8 0.6 collective-permute-start.26
  159.3 1.0 copy-done.2
  160.3 1.4 fusion.12
  161.8 1.6 copy-done.1
  163.4 0.5 collective-permute-start.21
  163.9 0.4 slice-done.1
  164.6 2.5 %collective-permute-start.29 = (bf16[1,48,2048]{2,1,0:T(8,128)(2,1)S(1)}, bf16[1,48,2048]{2,1,0:T(8,128)(2,1)S(1)}, u32[]{:S(2)}, u32[]{:S(2)}) collective-permute-start(bf16[1,48,2048]{2,1,0:T(8,128)(2,1)S(1)} %get-tuple-element.24), channel_id=1, source_target_pairs={{0,2},{2,4},{4,6},{6,0},{1,3},{3,5},{5,7},{7,1},{8,10},{10,12},{12... | collective-permute-start | bytes 589832 | tf_op jit(solution)/shard_map/ppermute | solution.py:17
  167.1 3.8 %collective-permute-start.28 = (bf16[1,48,2048]{2,1,0:T(8,128)(2,1)S(1)}, bf16[1,48,2048]{2,1,0:T(8,128)(2,1)S(1)}, u32[]{:S(2)}, u32[]{:S(2)}) collective-permute-start(bf16[1,48,2048]{2,1,0:T(8,128)(2,1)S(1)} %get-tuple-element.25), channel_id=1, source_target_pairs={{0,4},{2,6},{4,0},{6,2},{1,5},{3,7},{5,1},{7,3},{8,12},{10,14},{12... | collective-permute-start | bytes 589832 | tf_op jit(solution)/shard_map/ppermute | solution.py:17
  171.3 2.1 collective-permute-start.24
  173.3 1.8 collective-permute-start.23
  175.1 3.1 %collective-permute-start.22 = (bf16[1,48,2048]{2,1,0:T(8,128)(2,1)S(1)}, bf16[1,48,2048]{2,1,0:T(8,128)(2,1)S(1)}, u32[]{:S(2)}, u32[]{:S(2)}) collective-permute-start(bf16[1,48,2048]{2,1,0:T(8,128)(2,1)S(1)} %get-tuple-element.22), channel_id=1, source_target_pairs={{0,6},{2,0},{4,2},{6,4},{1,7},{3,1},{5,3},{7,5},{8,14},{10,8},{12,... | collective-permute-start | bytes 589832 | tf_op jit(solution)/shard_map/ppermute | solution.py:17
  178.2 6.8 %collective-permute-done.28 = bf16[1,48,2048]{2,1,0:T(8,128)(2,1)S(1)} collective-permute-done((bf16[1,48,2048]{2,1,0:T(8,128)(2,1)S(1)}, bf16[1,48,2048]{2,1,0:T(8,128)(2,1)S(1)}, u32[]{:S(2)}, u32[]{:S(2)}) %collective-permute-start.28) | collective-permute-done | bytes 196640 | tf_op jit(solution)/shard_map/ppermute | solution.py:17
  185.0 11.9 %collective-permute-done.27 = bf16[1,48,2048]{2,1,0:T(8,128)(2,1)S(1)} collective-permute-done((bf16[1,48,2048]{2,1,0:T(8,128)(2,1)S(1)}, bf16[1,48,2048]{2,1,0:T(8,128)(2,1)S(1)}, u32[]{:S(2)}, u32[]{:S(2)}) %collective-permute-start.27) | collective-permute-done | bytes 196640 | tf_op jit(solution)/shard_map/ppermute | solution.py:17
  197.4 1.6 collective-permute-start.30
  199.0 2.5 %collective-permute-done.23 = bf16[1,48,2048]{2,1,0:T(8,128)(2,1)S(1)} collective-permute-done((bf16[1,48,2048]{2,1,0:T(8,128)(2,1)S(1)}, bf16[1,48,2048]{2,1,0:T(8,128)(2,1)S(1)}, u32[]{:S(2)}, u32[]{:S(2)}) %collective-permute-start.23) | collective-permute-done | bytes 196640 | tf_op jit(solution)/shard_map/ppermute | solution.py:17
  201.4 3.5 %collective-permute-done.22 = bf16[1,48,2048]{2,1,0:T(8,128)(2,1)S(1)} collective-permute-done((bf16[1,48,2048]{2,1,0:T(8,128)(2,1)S(1)}, bf16[1,48,2048]{2,1,0:T(8,128)(2,1)S(1)}, u32[]{:S(2)}, u32[]{:S(2)}) %collective-permute-start.22) | collective-permute-done | bytes 196640 | tf_op jit(solution)/shard_map/ppermute | solution.py:17
  205.4 1.6 collective-permute-start.25
  207.0 6.2 %collective-permute-done.30 = bf16[128,2048]{1,0:T(8,128)(2,1)S(1)} collective-permute-done((bf16[128,2048]{1,0:T(8,128)(2,1)S(1)}, bf16[128,2048]{1,0:T(8,128)(2,1)S(1)}, u32[]{:S(2)}, u32[]{:S(2)}) %collective-permute-start.30) | collective-permute-done | bytes 524320 | tf_op jit(solution)/shard_map/ppermute | solution.py:17
  213.2 9.5 %collective-permute-done.25 = bf16[128,2048]{1,0:T(8,128)(2,1)S(1)} collective-permute-done((bf16[128,2048]{1,0:T(8,128)(2,1)S(1)}, bf16[128,2048]{1,0:T(8,128)(2,1)S(1)}, u32[]{:S(2)}, u32[]{:S(2)}) %collective-permute-start.25) | collective-permute-done | bytes 524320 | tf_op jit(solution)/shard_map/ppermute | solution.py:17
  222.7 1.1 maximum_bitcast_fusion
  (89 shorter events, 6.4 us)
Async XLA Ops:
  0.0 9.2 %copy-start.5 = (s32[1,1,128,1]{2,3,1,0:T(1,128)S(1)}, s32[1,1,128,1]{2,3,1,0:T(1,128)}, u32[]{:S(2)}) copy-start(s32[1,1,128,1]{2,3,1,0:T(1,128)} %param.16) | copy-start | bytes 1540
  0.0 45.1 %collective-permute-start.9 = (bf16[1024,2048]{1,0:T(8,128)(2,1)}, bf16[1024,2048]{1,0:T(8,128)(2,1)}, u32[]{:S(2)}, u32[]{:S(2)}) collective-permute-start(bf16[1024,2048]{1,0:T(8,128)(2,1)} %bitcast.223), channel_id=1, source_target_pairs={{0,1},{1,0},{2,3},{3,2},{4,5},{5,4},{6,7},{7,6},{8,9},{9,8},{10,11... | collective-permute-start | bytes 12582920 | tf_op jit(solution)/shard_map/ppermute | solution.py:17
  1.0 9.4 %collective-permute-start.2 = (bf16[128,256]{1,0:T(8,128)(2,1)S(1)}, bf16[128,256]{1,0:T(8,128)(2,1)S(1)}, u32[]{:S(2)}, u32[]{:S(2)}) collective-permute-start(bf16[128,256]{1,0:T(8,128)(2,1)S(1)} %pad_maximum_fusion.7), channel_id=1, source_target_pairs={{0,6},{2,0},{4,2},{6,4},{1,7},{3,1},{5,3},{7,5},{8,14},{10,8},{12,... | collective-permute-start | bytes 196616 | tf_op jit(solution)/shard_map/ppermute | solution.py:17
  1.5 10.9 %collective-permute-start = (bf16[128,256]{1,0:T(8,128)(2,1)S(1)}, bf16[128,256]{1,0:T(8,128)(2,1)S(1)}, u32[]{:S(2)}, u32[]{:S(2)}) collective-permute-start(bf16[128,256]{1,0:T(8,128)(2,1)S(1)} %pad_maximum_fusion.5), channel_id=1, source_target_pairs={{0,2},{2,4},{4,6},{6,0},{1,3},{3,5},{5,7},{7,1},{8,10},{10,12},{12... | collective-permute-start | bytes 196616 | tf_op jit(solution)/shard_map/ppermute | solution.py:17
  3.2 9.3 %collective-permute-start.1 = (bf16[128,256]{1,0:T(8,128)(2,1)S(1)}, bf16[128,256]{1,0:T(8,128)(2,1)S(1)}, u32[]{:S(2)}, u32[]{:S(2)}) collective-permute-start(bf16[128,256]{1,0:T(8,128)(2,1)S(1)} %pad_maximum_fusion.6), channel_id=1, source_target_pairs={{0,4},{2,6},{4,0},{6,2},{1,5},{3,7},{5,1},{7,3},{8,12},{10,14},{12... | collective-permute-start | bytes 196616 | tf_op jit(solution)/shard_map/ppermute | solution.py:17
  9.1 17.2 %collective-permute-start.5 = (bf16[128,1024]{0,1:T(8,128)(2,1)S(1)}, bf16[128,1024]{0,1:T(8,128)(2,1)S(1)}, u32[]{:S(2)}, u32[]{:S(2)}) collective-permute-start(bf16[128,1024]{0,1:T(8,128)(2,1)S(1)} %bitcast.242), channel_id=1, source_target_pairs={{0,2},{2,4},{4,6},{6,0},{1,3},{3,5},{5,7},{7,1},{8,10},{10,12},{12... | collective-permute-start | bytes 786440 | tf_op jit(solution)/shard_map/ppermute | solution.py:17
  10.5 30.1 %collective-permute-start.3 = (bf16[128,1024]{0,1:T(8,128)(2,1)S(1)}, bf16[128,1024]{0,1:T(8,128)(2,1)}, u32[]{:S(2)}, u32[]{:S(2)}) collective-permute-start(bf16[128,1024]{0,1:T(8,128)(2,1)S(1)} %bitcast.244), channel_id=1, source_target_pairs={{0,6},{2,0},{4,2},{6,4},{1,7},{3,1},{5,3},{7,5},{8,14},{10,8},{12,... | collective-permute-start | bytes 786440 | tf_op jit(solution)/shard_map/ppermute | solution.py:17
  12.5 29.9 %collective-permute-start.4 = (bf16[128,1024]{0,1:T(8,128)(2,1)S(1)}, bf16[128,1024]{0,1:T(8,128)(2,1)S(1)}, u32[]{:S(2)}, u32[]{:S(2)}) collective-permute-start(bf16[128,1024]{0,1:T(8,128)(2,1)S(1)} %bitcast.243), channel_id=1, source_target_pairs={{0,4},{2,6},{4,0},{6,2},{1,5},{3,7},{5,1},{7,3},{8,12},{10,14},{12... | collective-permute-start | bytes 786440 | tf_op jit(solution)/shard_map/ppermute | solution.py:17
  31.1 20.9 %collective-permute-start.6 = (bf16[128,2048]{1,0:T(8,128)(2,1)S(1)}, bf16[128,2048]{1,0:T(8,128)(2,1)S(1)}, u32[]{:S(2)}, u32[]{:S(2)}) collective-permute-start(bf16[128,2048]{1,0:T(8,128)(2,1)S(1)} %convolution_convert_fusion.2), channel_id=1, source_target_pairs={{0,2},{2,4},{4,6},{6,0},{1,3},{3,5},{5,7},{7,1},{8,10},{10,12},{12... | collective-permute-start | bytes 1572872 | tf_op jit(solution)/shard_map/ppermute | solution.py:17
  48.1 17.5 %collective-permute-start.10 = (bf16[128,2048]{1,0:T(8,128)(2,1)S(1)}, bf16[128,2048]{1,0:T(8,128)(2,1)S(1)}, u32[]{:S(2)}, u32[]{:S(2)}) collective-permute-start(bf16[128,2048]{1,0:T(8,128)(2,1)S(1)} %convolution_convert_fusion.1), channel_id=1, source_target_pairs={{0,2},{2,4},{4,6},{6,0},{1,3},{3,5},{5,7},{7,1},{8,10},{10,12},{12... | collective-permute-start | bytes 1572872 | tf_op jit(solution)/shard_map/ppermute | solution.py:17
  54.9 14.0 %copy-start = (bf16[1,1024,2048]{2,1,0:T(8,128)(2,1)S(1)}, bf16[1,1024,2048]{2,1,0:T(8,128)(2,1)}, u32[]{:S(2)}) copy-start(bf16[1,1024,2048]{2,1,0:T(8,128)(2,1)} %param.12) | copy-start | bytes 12582916
  54.9 21.9 %collective-permute-start.7 = (bf16[128,2048]{1,0:T(8,128)(2,1)S(1)}, bf16[128,2048]{1,0:T(8,128)(2,1)S(1)}, u32[]{:S(2)}, u32[]{:S(2)}) collective-permute-start(bf16[128,2048]{1,0:T(8,128)(2,1)S(1)} %add_convert_fusion.3), channel_id=1, source_target_pairs={{0,2},{2,4},{4,6},{6,0},{1,3},{3,5},{5,7},{7,1},{8,10},{10,12},{12... | collective-permute-start | bytes 1572872 | tf_op jit(solution)/shard_map/ppermute | solution.py:17
  68.5 19.5 %collective-permute-start.11 = (bf16[128,2048]{1,0:T(8,128)(2,1)S(1)}, bf16[128,2048]{1,0:T(8,128)(2,1)S(1)}, u32[]{:S(2)}, u32[]{:S(2)}) collective-permute-start(bf16[128,2048]{1,0:T(8,128)(2,1)S(1)} %fusion.23), channel_id=1, source_target_pairs={{0,2},{2,4},{4,6},{6,0},{1,3},{3,5},{5,7},{7,1},{8,10},{10,12},{12... | collective-permute-start | bytes 1572872 | tf_op jit(solution)/shard_map/ppermute | solution.py:17
  77.0 22.3 %collective-permute-start.8 = (bf16[128,2048]{1,0:T(8,128)(2,1)S(1)}, bf16[128,2048]{1,0:T(8,128)(2,1)S(1)}, u32[]{:S(2)}, u32[]{:S(2)}) collective-permute-start(bf16[128,2048]{1,0:T(8,128)(2,1)S(1)} %add_convert_fusion.2), channel_id=1, source_target_pairs={{0,2},{2,4},{4,6},{6,0},{1,3},{3,5},{5,7},{7,1},{8,10},{10,12},{12... | collective-permute-start | bytes 1572872 | tf_op jit(solution)/shard_map/ppermute | solution.py:17
  91.0 18.3 %collective-permute-start.12 = (bf16[128,2048]{1,0:T(8,128)(2,1)S(1)}, bf16[128,2048]{1,0:T(8,128)(2,1)S(1)}, u32[]{:S(2)}, u32[]{:S(2)}) collective-permute-start(bf16[128,2048]{1,0:T(8,128)(2,1)S(1)} %fusion.22), channel_id=1, source_target_pairs={{0,2},{2,4},{4,6},{6,0},{1,3},{3,5},{5,7},{7,1},{8,10},{10,12},{12... | collective-permute-start | bytes 1572872 | tf_op jit(solution)/shard_map/ppermute | solution.py:17
  91.2 8.1 %copy-start.3 = (bf16[1,1,128,4096]{3,2,1,0:T(8,128)(2,1)S(1)}, bf16[1,1,128,4096]{3,2,1,0:T(8,128)(2,1)}, u32[]{:S(2)}) copy-start(bf16[1,1,128,4096]{3,2,1,0:T(8,128)(2,1)} %param.11) | copy-start | bytes 3145732
  99.3 52.0 %slice-start.2 = ((s8[12582912]{0:T(1024)(128)(4,1)}), s8[4194304]{0:T(1024)(128)(4,1)S(1)}, s32[]{:S(2)}) async-start(s8[12582912]{0:T(1024)(128)(4,1)} %bitcast.258), calls=%async_computation.2 | async-start | bytes 8388608
  99.5 51.9 %slice-start.3 = ((s8[12582912]{0:T(1024)(128)(4,1)}), s8[4194304]{0:T(1024)(128)(4,1)S(1)}, s32[]{:S(2)}) async-start(s8[12582912]{0:T(1024)(128)(4,1)} %bitcast.258), calls=%async_computation.3 | async-start | bytes 8388608
  112.3 0.7 copy-start.4
  113.0 38.4 %slice-start.4 = ((s8[12582912]{0:T(1024)(128)(4,1)}), s8[4194304]{0:T(1024)(128)(4,1)S(1)}, s32[]{:S(2)}) async-start(s8[12582912]{0:T(1024)(128)(4,1)} %bitcast.258), calls=%async_computation.4 | async-start | bytes 8388608
  113.7 15.6 %collective-permute-start.19 = (bf16[1,48,2048]{2,1,0:T(8,128)(2,1)S(1)}, bf16[1,48,2048]{2,1,0:T(8,128)(2,1)S(1)}, u32[]{:S(2)}, u32[]{:S(2)}) collective-permute-start(bf16[1,48,2048]{2,1,0:T(8,128)(2,1)S(1)} %get-tuple-element.14), channel_id=1, source_target_pairs={{0,6},{2,0},{4,2},{6,4},{1,7},{3,1},{5,3},{7,5},{8,14},{10,8},{12,... | collective-permute-start | bytes 589832 | tf_op jit(solution)/shard_map/ppermute | solution.py:17
  117.4 11.9 %collective-permute-start.18 = (bf16[1,48,2048]{2,1,0:T(8,128)(2,1)S(1)}, bf16[1,48,2048]{2,1,0:T(8,128)(2,1)S(1)}, u32[]{:S(2)}, u32[]{:S(2)}) collective-permute-start(bf16[1,48,2048]{2,1,0:T(8,128)(2,1)S(1)} %get-tuple-element.8), channel_id=1, source_target_pairs={{0,4},{2,6},{4,0},{6,2},{1,5},{3,7},{5,1},{7,3},{8,12},{10,14},{12... | collective-permute-start | bytes 589832 | tf_op jit(solution)/shard_map/ppermute | solution.py:17
  117.5 15.1 %collective-permute-start.17 = (bf16[1,48,2048]{2,1,0:T(8,128)(2,1)S(1)}, bf16[1,48,2048]{2,1,0:T(8,128)(2,1)S(1)}, u32[]{:S(2)}, u32[]{:S(2)}) collective-permute-start(bf16[1,48,2048]{2,1,0:T(8,128)(2,1)S(1)} %get-tuple-element.9), channel_id=1, source_target_pairs={{0,2},{2,4},{4,6},{6,0},{1,3},{3,5},{5,7},{7,1},{8,10},{10,12},{12... | collective-permute-start | bytes 589832 | tf_op jit(solution)/shard_map/ppermute | solution.py:17
  132.7 18.5 %collective-permute-start.20 = (bf16[4,48,2048]{2,1,0:T(8,128)(2,1)S(1)}, bf16[4,48,2048]{2,1,0:T(8,128)(2,1)S(1)}, u32[]{:S(2)}, u32[]{:S(2)}) collective-permute-start(bf16[4,48,2048]{2,1,0:T(8,128)(2,1)S(1)} %maximum_bitcast_fusion.2), channel_id=1, source_target_pairs={{0,1},{1,0},{2,3},{3,2},{4,5},{5,4},{6,7},{7,6},{8,9},{9,8},{10,11... | collective-permute-start | bytes 2359304 | tf_op jit(solution)/shard_map/ppermute | solution.py:17
  132.8 8.3 %collective-permute-start.15 = (bf16[1,48,2048]{2,1,0:T(8,128)(2,1)S(1)}, bf16[1,48,2048]{2,1,0:T(8,128)(2,1)S(1)}, u32[]{:S(2)}, u32[]{:S(2)}) collective-permute-start(bf16[1,48,2048]{2,1,0:T(8,128)(2,1)S(1)} %get-tuple-element.13), channel_id=1, source_target_pairs={{0,6},{2,0},{4,2},{6,4},{1,7},{3,1},{5,3},{7,5},{8,14},{10,8},{12,... | collective-permute-start | bytes 589832 | tf_op jit(solution)/shard_map/ppermute | solution.py:17
  133.8 13.0 %collective-permute-start.14 = (bf16[1,48,2048]{2,1,0:T(8,128)(2,1)S(1)}, bf16[1,48,2048]{2,1,0:T(8,128)(2,1)S(1)}, u32[]{:S(2)}, u32[]{:S(2)}) collective-permute-start(bf16[1,48,2048]{2,1,0:T(8,128)(2,1)S(1)} %get-tuple-element.11), channel_id=1, source_target_pairs={{0,4},{2,6},{4,0},{6,2},{1,5},{3,7},{5,1},{7,3},{8,12},{10,14},{12... | collective-permute-start | bytes 589832 | tf_op jit(solution)/shard_map/ppermute | solution.py:17
  136.8 14.2 %collective-permute-start.13 = (bf16[1,48,2048]{2,1,0:T(8,128)(2,1)S(1)}, bf16[1,48,2048]{2,1,0:T(8,128)(2,1)S(1)}, u32[]{:S(2)}, u32[]{:S(2)}) collective-permute-start(bf16[1,48,2048]{2,1,0:T(8,128)(2,1)S(1)} %get-tuple-element.12), channel_id=1, source_target_pairs={{0,2},{2,4},{4,6},{6,0},{1,3},{3,5},{5,7},{7,1},{8,10},{10,12},{12... | collective-permute-start | bytes 589832 | tf_op jit(solution)/shard_map/ppermute | solution.py:17
  151.1 2.9 %collective-permute-start.16 = (bf16[4,48,2048]{2,1,0:T(8,128)(2,1)S(1)}, bf16[4,48,2048]{2,1,0:T(8,128)(2,1)S(1)}, u32[]{:S(2)}, u32[]{:S(2)}) collective-permute-start(bf16[4,48,2048]{2,1,0:T(8,128)(2,1)S(1)} %maximum_bitcast_fusion.1), channel_id=1, source_target_pairs={{0,1},{1,0},{2,3},{3,2},{4,5},{5,4},{6,7},{7,6},{8,9},{9,8},{10,11... | collective-permute-start | bytes 2359304 | tf_op jit(solution)/shard_map/ppermute | solution.py:17
  154.0 3.2 %slice-start.5 = ((s8[6291456]{0:T(1024)(128)(4,1)}), s8[4194304]{0:T(1024)(128)(4,1)S(1)}, s32[]{:S(2)}) async-start(s8[6291456]{0:T(1024)(128)(4,1)} %bitcast.260), calls=%async_computation.5 | async-start | bytes 8388608
  154.2 3.0 %slice-start.6 = ((s8[6291456]{0:T(1024)(128)(4,1)}), s8[2097152]{0:T(1024)(128)(4,1)S(1)}, s32[]{:S(2)}) async-start(s8[6291456]{0:T(1024)(128)(4,1)} %bitcast.260), calls=%async_computation.6 | async-start | bytes 4194304
  158.7 1.7 copy-start.2
  158.8 5.1 %collective-permute-start.26 = (bf16[4,48,2048]{2,1,0:T(8,128)(2,1)S(1)}, bf16[4,48,2048]{2,1,0:T(8,128)(2,1)S(1)}, u32[]{:S(2)}, u32[]{:S(2)}) collective-permute-start(bf16[4,48,2048]{2,1,0:T(8,128)(2,1)S(1)} %bitcast.241), channel_id=1, source_target_pairs={{0,1},{1,0},{2,3},{3,2},{4,5},{5,4},{6,7},{7,6},{8,9},{9,8},{10,11... | collective-permute-start | bytes 2359304 | tf_op jit(solution)/shard_map/ppermute | solution.py:17
  161.7 1.7 copy-start.1
  161.7 2.5 %slice-start.1 = ((f32[384,2048]{1,0:T(8,128)}), f32[192,2048]{1,0:T(8,128)S(1)}, s32[]{:S(2)}) async-start(f32[384,2048]{1,0:T(8,128)} %copy-done.2), calls=%async_computation.1 | async-start | bytes 3145728 | tf_op jit(solution)/shard_map/slice | solution.py:181
  163.4 7.5 %collective-permute-start.21 = (bf16[4,48,2048]{2,1,0:T(8,128)(2,1)S(1)}, bf16[4,48,2048]{2,1,0:T(8,128)(2,1)S(1)}, u32[]{:S(2)}, u32[]{:S(2)}) collective-permute-start(bf16[4,48,2048]{2,1,0:T(8,128)(2,1)S(1)} %bitcast.240), channel_id=1, source_target_pairs={{0,1},{1,0},{2,3},{3,2},{4,5},{5,4},{6,7},{7,6},{8,9},{9,8},{10,11... | collective-permute-start | bytes 2359304 | tf_op jit(solution)/shard_map/ppermute | solution.py:17
  164.3 6.7 %slice-start = ((f32[384,2048]{1,0:T(8,128)}), f32[192,2048]{1,0:T(8,128)S(1)}, s32[]{:S(2)}) async-start(f32[384,2048]{1,0:T(8,128)} %copy-done.1), calls=%async_computation | async-start | bytes 3145728 | tf_op jit(solution)/shard_map/slice | solution.py:181
  164.6 10.5 %collective-permute-start.29 = (bf16[1,48,2048]{2,1,0:T(8,128)(2,1)S(1)}, bf16[1,48,2048]{2,1,0:T(8,128)(2,1)S(1)}, u32[]{:S(2)}, u32[]{:S(2)}) collective-permute-start(bf16[1,48,2048]{2,1,0:T(8,128)(2,1)S(1)} %get-tuple-element.24), channel_id=1, source_target_pairs={{0,2},{2,4},{4,6},{6,0},{1,3},{3,5},{5,7},{7,1},{8,10},{10,12},{12... | collective-permute-start | bytes 589832 | tf_op jit(solution)/shard_map/ppermute | solution.py:17
  167.1 17.9 %collective-permute-start.28 = (bf16[1,48,2048]{2,1,0:T(8,128)(2,1)S(1)}, bf16[1,48,2048]{2,1,0:T(8,128)(2,1)S(1)}, u32[]{:S(2)}, u32[]{:S(2)}) collective-permute-start(bf16[1,48,2048]{2,1,0:T(8,128)(2,1)S(1)} %get-tuple-element.25), channel_id=1, source_target_pairs={{0,4},{2,6},{4,0},{6,2},{1,5},{3,7},{5,1},{7,3},{8,12},{10,14},{12... | collective-permute-start | bytes 589832 | tf_op jit(solution)/shard_map/ppermute | solution.py:17
  170.9 26.0 %collective-permute-start.27 = (bf16[1,48,2048]{2,1,0:T(8,128)(2,1)S(1)}, bf16[1,48,2048]{2,1,0:T(8,128)(2,1)S(1)}, u32[]{:S(2)}, u32[]{:S(2)}) collective-permute-start(bf16[1,48,2048]{2,1,0:T(8,128)(2,1)S(1)} %get-tuple-element.26), channel_id=1, source_target_pairs={{0,6},{2,0},{4,2},{6,4},{1,7},{3,1},{5,3},{7,5},{8,14},{10,8},{12,... | collective-permute-start | bytes 589832 | tf_op jit(solution)/shard_map/ppermute | solution.py:17
  171.2 25.9 %copy-start.6 = (f32[1,1,128,1]{2,3,1,0:T(1,128)S(1)}, f32[1,1,128,1]{2,3,1,0:T(1,128)}, u32[]{:S(2)}) copy-start(f32[1,1,128,1]{2,3,1,0:T(1,128)} %param.17) | copy-start | bytes 1540
  171.3 27.7 %collective-permute-start.24 = (bf16[1,48,2048]{2,1,0:T(8,128)(2,1)S(1)}, bf16[1,48,2048]{2,1,0:T(8,128)(2,1)S(1)}, u32[]{:S(2)}, u32[]{:S(2)}) collective-permute-start(bf16[1,48,2048]{2,1,0:T(8,128)(2,1)S(1)} %get-tuple-element.20), channel_id=1, source_target_pairs={{0,2},{2,4},{4,6},{6,0},{1,3},{3,5},{5,7},{7,1},{8,10},{10,12},{12... | collective-permute-start | bytes 589832 | tf_op jit(solution)/shard_map/ppermute | solution.py:17
  173.3 28.1 %collective-permute-start.23 = (bf16[1,48,2048]{2,1,0:T(8,128)(2,1)S(1)}, bf16[1,48,2048]{2,1,0:T(8,128)(2,1)S(1)}, u32[]{:S(2)}, u32[]{:S(2)}) collective-permute-start(bf16[1,48,2048]{2,1,0:T(8,128)(2,1)S(1)} %get-tuple-element.21), channel_id=1, source_target_pairs={{0,4},{2,6},{4,0},{6,2},{1,5},{3,7},{5,1},{7,3},{8,12},{10,14},{12... | collective-permute-start | bytes 589832 | tf_op jit(solution)/shard_map/ppermute | solution.py:17
  175.1 29.8 %collective-permute-start.22 = (bf16[1,48,2048]{2,1,0:T(8,128)(2,1)S(1)}, bf16[1,48,2048]{2,1,0:T(8,128)(2,1)S(1)}, u32[]{:S(2)}, u32[]{:S(2)}) collective-permute-start(bf16[1,48,2048]{2,1,0:T(8,128)(2,1)S(1)} %get-tuple-element.22), channel_id=1, source_target_pairs={{0,6},{2,0},{4,2},{6,4},{1,7},{3,1},{5,3},{7,5},{8,14},{10,8},{12,... | collective-permute-start | bytes 589832 | tf_op jit(solution)/shard_map/ppermute | solution.py:17
  197.4 15.8 %collective-permute-start.30 = (bf16[128,2048]{1,0:T(8,128)(2,1)S(1)}, bf16[128,2048]{1,0:T(8,128)(2,1)S(1)}, u32[]{:S(2)}, u32[]{:S(2)}) collective-permute-start(bf16[128,2048]{1,0:T(8,128)(2,1)S(1)} %fusion.25), channel_id=1, source_target_pairs={{0,8},{8,16},{16,24},{24,0},{1,9},{9,17},{17,25},{25,1},{2,10},{10... | collective-permute-start | bytes 1572872 | tf_op jit(solution)/shard_map/ppermute | solution.py:17
  205.4 17.3 %collective-permute-start.25 = (bf16[128,2048]{1,0:T(8,128)(2,1)S(1)}, bf16[128,2048]{1,0:T(8,128)(2,1)S(1)}, u32[]{:S(2)}, u32[]{:S(2)}) collective-permute-start(bf16[128,2048]{1,0:T(8,128)(2,1)S(1)} %fusion.24), channel_id=1, source_target_pairs={{0,8},{8,16},{16,24},{24,0},{1,9},{9,17},{17,25},{25,1},{2,10},{10... | collective-permute-start | bytes 1572872 | tf_op jit(solution)/shard_map/ppermute | solution.py:17

commit v2 on v1

--- a/solution.py
+++ b/solution.py
@@ -8,13 +8,21 @@
 QUERY_HEADS = 32
 KEY_VALUE_HEADS = 2
 HEAD_SIZE = 128
-DISPATCH_CHUNKS = 2
-RETURN_CHUNKS = 2
+DISPATCH_CHUNKS = 4
+RETURN_CHUNKS = 4
 
 
 def shift(value, axis, by):
     devices = lax.axis_size(axis)
     return lax.ppermute(value, axis, [(i, (i + by) % devices) for i in range(devices)])
+
+
+def across(value, mask, senders):
+    return lax.ppermute(value, "ctx", [(i, i ^ mask) for i in senders])
+
+
+def after(value, *earlier):
+    return lax.optimization_barrier((value, *earlier))[0]
 
 
 def attend_block(query_block, key_rows, value_rows, row_ids, col_ids):
@@ -36,6 +44,16 @@
     width = residual.shape[1]
     local_heads = QUERY_HEADS // contexts
     group_width = local_heads * HEAD_SIZE
+    line = contexts == 4
+
+    def other(k):
+        return me ^ k if line else (me + k) % contexts
+
+    def came_from(k):
+        return me ^ k if line else (me - k) % contexts
+
+    def move(value, k):
+        return across(value, k, range(4)) if line else shift(value, "ctx", k)
 
     def pair_for(owner):
         head = owner * local_heads // (QUERY_HEADS // KEY_VALUE_HEADS)
@@ -49,11 +67,24 @@
         return lax.dynamic_slice_in_dim(queries, owner * group_width, group_width, 1)
 
     pairs = [pair_for(me)]
-    blocks = [queries_for(me)]
     for k in range(1, contexts):
-        pairs.append(shift(pair_for((me + k) % contexts), "ctx", k))
-    for k in range(1, contexts):
-        blocks.append(shift(queries_for((me + k) % contexts), "ctx", k))
+        pairs.append(move(pair_for(other(k)), k))
+    outgoing = [queries_for(other(k)) for k in range(contexts)]
+    if line:
+        outer, inner = (0, 3), (1, 2)
+        at_end = (me == 0) | (me == 3)
+        far = across(outgoing[3], 3, outer)
+        far_in = across(after(outgoing[2], far), 2, outer)
+        next_out = across(after(outgoing[2], far_in), 2, inner)
+        next_in = across(after(outgoing[3], far_in), 3, inner)
+        near = across(after(outgoing[1], next_out, next_in), 1, range(4))
+        blocks = [jnp.where(at_end, far, far_in), jnp.where(at_end, next_out, next_in), near]
+        sources = [jnp.where(at_end, me ^ 3, me ^ 2), jnp.where(at_end, me ^ 2, me ^ 3), me ^ 1]
+    else:
+        blocks = [move(outgoing[k], k) for k in range(1, contexts)]
+        sources = [came_from(k) for k in range(1, contexts)]
+    blocks.append(outgoing[0])
+    sources.append(me)
     if exps == 2:
         weights = [out_weight, shift(out_weight, "exp", 1)]
         first = my_exp * (width // 2)
@@ -66,26 +97,36 @@
     pair_rows = jnp.concatenate(pairs, axis=0)
     key_rows, value_rows = pair_rows[:, :HEAD_SIZE], pair_rows[:, HEAD_SIZE:]
     within = jnp.arange(rows, dtype=jnp.int32)
-    origins = [(me - k) % contexts * rows for k in range(contexts)]
-    col_ids = jnp.concatenate([origin + within for origin in origins])
-
+    col_ids = jnp.concatenate([came_from(k) * rows + within for k in range(contexts)])
+
+    outs, mids, ins = [[], []], [[], []], [[], []]
     held = [None, None]
-    for k in [*range(1, contexts), 0]:
+    for step in range(contexts):
         attended = attend_block(
-            blocks[k].reshape(rows, local_heads, HEAD_SIZE),
+            blocks[step].reshape(rows, local_heads, HEAD_SIZE),
             key_rows,
             value_rows,
-            origins[k] + within,
+            sources[step] * rows + within,
             col_ids,
         ).reshape(rows, group_width)
         for half in range(2):
             term = jnp.dot(attended, weights[half], preferred_element_type=jnp.float32)
-            if held[half] is not None:
-                term = term + held[half].astype(jnp.float32)
-            if k == 0:
+            if step == contexts - 1:
                 own = lax.dynamic_slice_in_dim(residual, offsets[half], width // 2, 1)
-                held[half] = term + own.astype(jnp.float32)
+                term = term + own.astype(jnp.float32)
+                last = [outs[half][2], mids[half][1], ins[half][0]] if line else [held[half]]
+                held[half] = sum([block.astype(jnp.float32) for block in last], term)
+            elif line:
+                outs[half].append(across(term.astype(jnp.bfloat16), 1, outer))
+                if step < 2:
+                    middle = (term + outs[half][step].astype(jnp.float32)).astype(jnp.bfloat16)
+                    mids[half].append(across(middle, 3, inner))
+                else:
+                    back = (term + mids[half][0].astype(jnp.float32)).astype(jnp.bfloat16)
+                    ins[half].append(across(back, 1, inner))
             else:
+                if step:
+                    term = term + held[half].astype(jnp.float32)
                 held[half] = shift(term.astype(jnp.bfloat16), "ctx", 1)
     return held, first
 
@@ -150,10 +191,12 @@
         return lax.dynamic_index_in_dim(arrived, exp // group_size, 1, keepdims=False)
 
     hidden_width = down_weight.shape[2]
-    gate_up = 0.0
+    gate_ups = [0.0]
     step = model_width // DISPATCH_CHUNKS
     for chunk in range(DISPATCH_CHUNKS):
         part = packed[..., chunk * step : (chunk + 1) * step]
+        if chunk >= 2:
+            part = after(part, gate_ups[chunk - 1])
         arrived = jnp.stack(
             [part[0]] + [shift(part[k], "ctx", k) for k in range(1, contexts)], axis=0
         )
@@ -161,17 +204,21 @@
         for k in range(1, exps):
             gathered.append(shift(wanted_by(arrived, (my_exp + k) % exps), "exp", k))
         slot_rows = jnp.concatenate(gathered, axis=0).reshape(-1, step)
-        gate_up = gate_up + jnp.dot(
-            slot_rows,
-            in_weight[0, 0, chunk * step : (chunk + 1) * step],
-            preferred_element_type=jnp.float32,
+        gate_ups.append(
+            gate_ups[-1]
+            + jnp.dot(
+                slot_rows,
+                in_weight[0, 0, chunk * step : (chunk + 1) * step],
+                preferred_element_type=jnp.float32,
+            )
         )
+    gate_up = gate_ups[-1]
     hidden = (jax.nn.silu(gate_up[:, :hidden_width]) * gate_up[:, hidden_width:]).astype(
         jnp.bfloat16
     )
 
     step = model_width // RETURN_CHUNKS
-    outputs = []
+    outputs, layers = [], []
     for chunk in range(RETURN_CHUNKS):
         columns = slice(chunk * step, (chunk + 1) * step)
         part = jnp.dot(hidden, down_weight[0, 0, :, columns], preferred_element_type=jnp.float32)
@@ -187,6 +234,8 @@
                 place = (my_exp + k) % exps // group_size
                 sums = [s + jnp.where(place == i, back, 0.0) for i, s in enumerate(sums)]
         total = jnp.stack(sums, axis=1).astype(jnp.bfloat16)
+        if chunk >= 2:
+            total = after(total, layers[chunk - 2])
         returned = jnp.concatenate(
             [total[0]] + [shift(total[k], "ctx", -k) for k in range(1, contexts)], axis=0
         ).reshape(slots, step)
@@ -195,7 +244,8 @@
             match = (slot_ids[None, :] == slot_index[:, r, None]).astype(jnp.bfloat16)
             picked = jnp.dot(match, returned, preferred_element_type=jnp.float32)
             layer = layer + picked * route_weight[0, 0, :, r, None]
-        outputs.append(shift(layer.astype(jnp.bfloat16), "pipe", 1))
+        layers.append(layer.astype(jnp.bfloat16))
+        outputs.append(shift(layers[chunk], "pipe", 1))
     return jnp.concatenate(outputs, axis=1).reshape(1, 1, token_rows, model_width)
 
 

time: 224 us -> 239 us (1.067)
  the two profiles are of different devices: /device:TPU:12 before, /device:TPU:0 now
where the time goes in v2:
time: 239 us; the launch traced here: 237 us
  starting transfers between devices  103 us (43%)
  waiting for transfers between devices  69.4 us (29%)
  matrix products  49.3 us (21%)
  other arithmetic  8.18 us (3%)
  local copies, waits for them, and re-layouts  6.08 us (3%)
    ppermute x20, starting transfers between devices, across(): return lax.ppermute(value, 'ctx', [(i, i ^ mask) for i in senders])  63 us
    ppermute x37, waiting for transfers between devices, shift(): lax.ppermute(value, axis, [(i, (i + by) % devices) for i in range(devices)])  48.7 us
    ppermute x37, starting transfers between devices, shift(): lax.ppermute(value, axis, [(i, (i + by) % devices) for i in range(devices)])  40.4 us
    dot_general x8, matrix products, mixed_halves(): term = jnp.dot(attended, weights[half], preferred_element_type=jnp.float32)  25.7 us
    ppermute x20, waiting for transfers between devices, across(): return lax.ppermute(value, 'ctx', [(i, i ^ mask) for i in senders])  20.7 us
    dot_general x4, matrix products, attend_block(): jnp.einsum('hqk,kd->qhd', attention_weights, value_rows, preferred_elemen...  8.4 us
    dot_general x4, matrix products, on_device(): jnp.dot(slot_rows, in_weight[0, 0, chunk * step:(chunk + 1) * step], pref...  5.53 us
    sub x4, matrix products, attend_block(): attention_weights = jax.nn.softmax(scores, axis=-1).astype(jnp.bfloat16)  4.93 us
  transfers between devices with their start and end apart: 57, of which 24 were waited for; matrix products, arithmetic and copies ran while one was open for 21% of the time, Pallas kernels for 0%

profile of v2, /device:TPU:0, one launch (start us, length us, event | category | flops | bytes accessed | tf_op | source)
XLA Modules:
  0.0 237.5 jit_solution(8950944856830384235)
XLA Ops:
  1.0 5.1 %collective-permute-start.2 = (bf16[128,256]{1,0:T(8,128)(2,1)S(1)}, bf16[128,256]{1,0:T(8,128)(2,1)S(1)}, u32[]{:S(2)}, u32[]{:S(2)}) collective-permute-start(bf16[128,256]{1,0:T(8,128)(2,1)S(1)} %pad_maximum_fusion.11), channel_id=1, source_target_pairs={{0,6},{2,4},{4,2},{6,0},{1,7},{3,5},{5,3},{7,1},{8,14},{10,12},{12... | collective-permute-start | bytes 196616 | tf_op jit(solution)/shard_map/ppermute | solution.py:21
  6.8 1.3 constant_dynamic-slice_fusion.3
  8.3 5.7 %collective-permute-start.3 = (bf16[128,1024]{0,1:T(8,128)(2,1)S(1)}, bf16[128,1024]{0,1:T(8,128)(2,1)S(1)}, u32[]{:S(2)}, u32[]{:S(2)}) collective-permute-start(bf16[128,1024]{0,1:T(8,128)(2,1)S(1)} %bitcast.343), channel_id=1, source_target_pairs={{0,6},{6,0},{1,7},{7,1},{8,14},{14,8},{9,15},{15,9},{16,22},{22,16... | collective-permute-start | bytes 786440 | tf_op jit(solution)/shard_map/ppermute | solution.py:21
  17.5 2.0 convolution_convert_fusion.4
  19.5 1.3 collective-permute-start.4
  20.8 2.9 %convolution_add_fusion.1 = f32[128,2048]{1,0:T(8,128)S(1)} fusion(bf16[128,1024]{0,1:T(8,128)(2,1)S(1)} %bitcast.318, bf16[1,1,128,4096]{3,2,1,0:T(8,128)(2,1)S(1)} %copy-done.3, s32[]{:T(128)S(6)} %select_n.143, bf16[1,1024,2048]{2,1,0:T(8,128)(2,1)} %param.12), kind=kOutput, calls=%fused_computation.24 | convolution fusion | flops 537395200 | bytes 6029316 | tf_op jit(solution)/shard_map/dot_general | solution.py:113
  23.8 3.5 %collective-permute-done.4 = bf16[128,1024]{0,1:T(8,128)(2,1)S(1)} collective-permute-done((bf16[128,1024]{0,1:T(8,128)(2,1)S(1)}, bf16[128,1024]{0,1:T(8,128)(2,1)S(1)}, u32[]{:S(2)}, u32[]{:S(2)}) %collective-permute-start.4) | collective-permute-done | bytes 262176 | tf_op jit(solution)/shard_map/ppermute | solution.py:21
  27.3 1.3 collective-permute-start.5
  28.5 1.4 collective-permute-start.6
  30.0 1.6 fusion.122
  31.6 1.9 convolution_convert_fusion.1
  33.5 3.8 %fusion.123 = (bf16[128,2048]{1,0:T(8,128)(2,1)}, f32[128,2048]{1,0:T(8,128)S(1)}) fusion(bf16[128,1024]{0,1:T(8,128)(2,1)S(1)} %bitcast.328, bf16[1,1024,2048]{2,1,0:T(8,128)(2,1)} %param.12), kind=kOutput, calls=%fused_computation.223 | convolution fusion | flops 537133056 | bytes 6029312 | tf_op jit(solution)/shard_map/dot_general | solution.py:113
  37.3 8.0 %collective-permute-start.11 = (bf16[128,2048]{1,0:T(8,128)(2,1)}, bf16[128,2048]{1,0:T(8,128)(2,1)}, u32[]{:S(2)}, u32[]{:S(2)}) collective-permute-start(bf16[128,2048]{1,0:T(8,128)(2,1)} %get-tuple-element.73), channel_id=1, source_target_pairs={{0,2},{6,4},{1,3},{7,5},{8,10},{14,12},{9,11},{15,13},{16,18},{22,... | collective-permute-start | bytes 1572872 | tf_op jit(solution)/shard_map/ppermute | solution.py:21
  47.1 1.7 convolution_convert_fusion.2
  48.8 3.8 %fusion.125 = (bf16[128,2048]{1,0:T(8,128)(2,1)}, f32[128,2048]{1,0:T(8,128)S(1)}) fusion(bf16[128,1024]{0,1:T(8,128)(2,1)} %bitcast.330, bf16[1,1024,2048]{2,1,0:T(8,128)(2,1)} %param.12), kind=kOutput, calls=%fused_computation.225 | convolution fusion | flops 537133056 | bytes 6029312 | tf_op jit(solution)/shard_map/dot_general | solution.py:113
  52.7 4.7 %collective-permute-start.9 = (bf16[128,2048]{1,0:T(8,128)(2,1)}, bf16[128,2048]{1,0:T(8,128)(2,1)}, u32[]{:S(2)}, u32[]{:S(2)}) collective-permute-start(bf16[128,2048]{1,0:T(8,128)(2,1)} %get-tuple-element.75), channel_id=1, source_target_pairs={{0,2},{6,4},{1,3},{7,5},{8,10},{14,12},{9,11},{15,13},{16,18},{22,... | collective-permute-start | bytes 1572872 | tf_op jit(solution)/shard_map/ppermute | solution.py:21
  57.4 5.4 %collective-permute-done.7 = bf16[128,1024]{0,1:T(8,128)(2,1)} collective-permute-done((bf16[128,1024]{0,1:T(8,128)(2,1)}, bf16[128,1024]{0,1:T(8,128)(2,1)}, u32[]{:S(2)}, u32[]{:S(2)}) %collective-permute-start.7) | collective-permute-done | bytes 262176 | tf_op jit(solution)/shard_map/ppermute | solution.py:21
  62.8 1.8 fusion.121
  64.6 2.8 %convolution_convert_fusion.3 = bf16[128,8,128]{2,0,1:T(8,128)(2,1)} fusion(f32[8,128]{1,0:T(8,128)S(1)} %fusion.121, bf16[512,256]{1,0:T(8,128)(2,1)} %copy-done.9, pred[128,512]{0,1:T(8,128)(4,1)S(1)} %get-tuple-element.70, bf16[128,8,128]{0,2,1:T(8,128)(2,1)} %bitcast.20), kind=kOutput, calls=%fused_computation.62 | convolution fusion | flops 271189504 | bytes 856064 | tf_op jit(solution)/shard_map/hqk,kd->qhd/dot_general | solution.py:34
  68.6 3.0 %fusion.98 = f32[128,2048]{1,0:T(8,128)S(1)} fusion(bf16[128,1024]{0,1:T(8,128)(2,1)S(1)} %bitcast.332, bf16[1,1024,2048]{2,1,0:T(8,128)(2,1)} %param.12), kind=kOutput, calls=%fused_computation.202 | convolution fusion | flops 536870912 | bytes 5505024 | tf_op jit(solution)/shard_map/dot_general | solution.py:113
  72.5 2.9 %fusion.127 = (bf16[128,2048]{1,0:T(8,128)(2,1)S(1)}, f32[128,2048]{1,0:T(8,128)S(1)}) fusion(bf16[128,1024]{0,1:T(8,128)(2,1)S(1)} %bitcast.329, bf16[1024,2048]{1,0:T(8,128)(2,1)} %collective-permute-done.14), kind=kOutput, calls=%fused_computation.227 | convolution fusion | flops 537133056 | bytes 6029312 | tf_op jit(solution)/shard_map/dot_general | solution.py:113
  75.5 5.9 %collective-permute-start.18 = (bf16[128,2048]{1,0:T(8,128)(2,1)S(1)}, bf16[128,2048]{1,0:T(8,128)(2,1)S(1)}, u32[]{:S(2)}, u32[]{:S(2)}) collective-permute-start(bf16[128,2048]{1,0:T(8,128)(2,1)S(1)} %get-tuple-element.77), channel_id=1, source_target_pairs={{0,2},{6,4},{1,3},{7,5},{8,10},{14,12},{9,11},{15,13},{16,18},{22,... | collective-permute-start | bytes 1572872 | tf_op jit(solution)/shard_map/ppermute | solution.py:21
  83.3 2.9 %fusion.128 = (bf16[128,2048]{1,0:T(8,128)(2,1)S(1)}, f32[128,2048]{1,0:T(8,128)S(1)}) fusion(bf16[128,1024]{0,1:T(8,128)(2,1)S(1)} %bitcast.331, bf16[1024,2048]{1,0:T(8,128)(2,1)} %collective-permute-done.14), kind=kOutput, calls=%fused_computation.228 | convolution fusion | flops 537133056 | bytes 6029312 | tf_op jit(solution)/shard_map/dot_general | solution.py:113
  86.2 4.4 %collective-permute-start.16 = (bf16[128,2048]{1,0:T(8,128)(2,1)S(1)}, bf16[128,2048]{1,0:T(8,128)(2,1)S(1)}, u32[]{:S(2)}, u32[]{:S(2)}) collective-permute-start(bf16[128,2048]{1,0:T(8,128)(2,1)S(1)} %get-tuple-element.79), channel_id=1, source_target_pairs={{0,2},{6,4},{1,3},{7,5},{8,10},{14,12},{9,11},{15,13},{16,18},{22,... | collective-permute-start | bytes 1572872 | tf_op jit(solution)/shard_map/ppermute | solution.py:21
  90.6 1.5 collective-permute-done.18
  93.1 8.4 %collective-permute-start.8 = (bf16[128,2048]{1,0:T(8,128)(2,1)S(1)}, bf16[128,2048]{1,0:T(8,128)(2,1)S(1)}, u32[]{:S(2)}, u32[]{:S(2)}) collective-permute-start(bf16[128,2048]{1,0:T(8,128)(2,1)S(1)} %get-tuple-element.35), channel_id=1, source_target_pairs={{0,2},{6,4},{1,3},{7,5},{8,10},{14,12},{9,11},{15,13},{16,18},{22,... | collective-permute-start | bytes 1572872 | tf_op jit(solution)/shard_map/ppermute | solution.py:21
  101.6 1.3 collective-permute-start.13
  104.2 2.9 %fusion.115 = (bf16[128,2048]{1,0:T(8,128)(2,1)S(1)}, bf16[128,2048]{1,0:T(8,128)(2,1)S(1)}) fusion(bf16[128,2048]{1,0:T(8,128)(2,1)S(1)} %collective-permute-done.19, bf16[128,1024]{0,1:T(8,128)(2,1)S(1)} %bitcast.333, bf16[1024,2048]{1,0:T(8,128)(2,1)} %collective-permute-done.14), kind=kOutput, calls=%fused_computation.215 | convolution fusion | flops 537919488 | bytes 6029312 | tf_op jit(solution)/shard_map/dot_general | solution.py:113
  107.1 10.5 %collective-permute-start.15 = (bf16[128,2048]{1,0:T(8,128)(2,1)S(1)}, bf16[128,2048]{1,0:T(8,128)(2,1)S(1)}, u32[]{:S(2)}, u32[]{:S(2)}) collective-permute-start(bf16[128,2048]{1,0:T(8,128)(2,1)S(1)} %get-tuple-element.33), channel_id=1, source_target_pairs={{0,2},{6,4},{1,3},{7,5},{8,10},{14,12},{9,11},{15,13},{16,18},{22,... | collective-permute-start | bytes 1572872 | tf_op jit(solution)/shard_map/ppermute | solution.py:21
  117.6 1.3 collective-permute-start.20
  119.3 5.0 %collective-permute-done.15 = bf16[128,2048]{1,0:T(8,128)(2,1)S(1)} collective-permute-done((bf16[128,2048]{1,0:T(8,128)(2,1)S(1)}, bf16[128,2048]{1,0:T(8,128)(2,1)S(1)}, u32[]{:S(2)}, u32[]{:S(2)}) %collective-permute-start.15) | collective-permute-done | bytes 524320 | tf_op jit(solution)/shard_map/ppermute | solution.py:21
  124.3 4.7 %collective-permute-done.20 = bf16[128,2048]{1,0:T(8,128)(2,1)S(1)} collective-permute-done((bf16[128,2048]{1,0:T(8,128)(2,1)S(1)}, bf16[128,2048]{1,0:T(8,128)(2,1)S(1)}, u32[]{:S(2)}, u32[]{:S(2)}) %collective-permute-start.20) | collective-permute-done | bytes 524320 | tf_op jit(solution)/shard_map/ppermute | solution.py:21
  128.9 3.3 %fusion.27 = f32[128,2048]{1,0:T(8,128)S(1)} fusion(bf16[128,1024]{0,1:T(8,128)(2,1)S(1)} %bitcast.319, bf16[1024,2048]{1,0:T(8,128)(2,1)} %collective-permute-done.14, bf16[128,2048]{1,0:T(8,128)(2,1)S(1)} %collective-permute-done.20, bf16[128,2048]{1,0:T(8,128)(2,1)S(1)} %collective-permute-done.17, bf16[128,2048]{1,0:T(8,128)(2,1)S(1)} %collective-permute-done.15, ...), kind=kOutput, calls=%fused_computation.23 | convolution fusion | flops 538968064 | bytes 7602180 | tf_op jit(solution)/shard_map/dot_general | solution.py:113
  134.1 1.4 collective-permute-start.23
  136.3 2.4 %collective-permute-done.23 = bf16[1,48,1024]{2,1,0:T(8,128)(2,1)S(1)} collective-permute-done((bf16[1,48,1024]{2,1,0:T(8,128)(2,1)S(1)}, bf16[1,48,1024]{2,1,0:T(8,128)(2,1)S(1)}, u32[]{:S(2)}, u32[]{:S(2)}) %collective-permute-start.23) | collective-permute-done | bytes 98336 | tf_op jit(solution)/shard_map/ppermute | solution.py:17
  138.7 4.5 %collective-permute-done.22 = bf16[1,48,1024]{2,1,0:T(8,128)(2,1)S(1)} collective-permute-done((bf16[1,48,1024]{2,1,0:T(8,128)(2,1)S(1)}, bf16[1,48,1024]{2,1,0:T(8,128)(2,1)S(1)}, u32[]{:S(2)}, u32[]{:S(2)}) %collective-permute-start.22) | collective-permute-done | bytes 98336 | tf_op jit(solution)/shard_map/ppermute | solution.py:17
  143.9 1.8 collective-permute-start.25
  145.7 4.0 %collective-permute-done.27 = bf16[1,48,1024]{2,1,0:T(8,128)(2,1)S(1)} collective-permute-done((bf16[1,48,1024]{2,1,0:T(8,128)(2,1)S(1)}, bf16[1,48,1024]{2,1,0:T(8,128)(2,1)S(1)}, u32[]{:S(2)}, u32[]{:S(2)}) %collective-permute-start.27) | collective-permute-done | bytes 98336 | tf_op jit(solution)/shard_map/ppermute | solution.py:17
  149.8 3.9 %collective-permute-done.26 = bf16[1,48,1024]{2,1,0:T(8,128)(2,1)S(1)} collective-permute-done((bf16[1,48,1024]{2,1,0:T(8,128)(2,1)S(1)}, bf16[1,48,1024]{2,1,0:T(8,128)(2,1)S(1)}, u32[]{:S(2)}, u32[]{:S(2)}) %collective-permute-start.26) | collective-permute-done | bytes 98336 | tf_op jit(solution)/shard_map/ppermute | solution.py:17
  154.0 1.4 fusion.10
  155.6 1.4 fusion.16
  159.5 2.0 collective-permute-start.33
  161.5 1.9 collective-permute-start.31
  163.4 5.9 %collective-permute-done.34 = bf16[1,48,1024]{2,1,0:T(8,128)(2,1)S(1)} collective-permute-done((bf16[1,48,1024]{2,1,0:T(8,128)(2,1)S(1)}, bf16[1,48,1024]{2,1,0:T(8,128)(2,1)S(1)}, u32[]{:S(2)}, u32[]{:S(2)}) %collective-permute-start.34) | collective-permute-done | bytes 98336 | tf_op jit(solution)/shard_map/ppermute | solution.py:17
  169.5 3.3 %collective-permute-start.30 = (bf16[1,48,1024]{2,1,0:T(8,128)(2,1)S(1)}, bf16[1,48,1024]{2,1,0:T(8,128)(2,1)S(1)}, u32[]{:S(2)}, u32[]{:S(2)}) collective-permute-start(bf16[1,48,1024]{2,1,0:T(8,128)(2,1)S(1)} %get-tuple-element.56), channel_id=1, source_target_pairs={{0,4},{2,6},{4,0},{6,2},{1,5},{3,7},{5,1},{7,3},{8,12},{10,14},{12... | collective-permute-start | bytes 294920 | tf_op jit(solution)/shard_map/ppermute | solution.py:17
  172.9 7.7 %collective-permute-done.30 = bf16[1,48,1024]{2,1,0:T(8,128)(2,1)S(1)} collective-permute-done((bf16[1,48,1024]{2,1,0:T(8,128)(2,1)S(1)}, bf16[1,48,1024]{2,1,0:T(8,128)(2,1)S(1)}, u32[]{:S(2)}, u32[]{:S(2)}) %collective-permute-start.30) | collective-permute-done | bytes 98336 | tf_op jit(solution)/shard_map/ppermute | solution.py:17
  180.7 1.4 fusion.4
  182.4 1.4 fusion.22
  190.3 1.6 collective-permute-done.37
  192.0 2.1 collective-permute-start.43
  194.9 1.5 collective-permute-start.39
  197.8 1.8 collective-permute-start.38
  199.6 2.0 collective-permute-done.44
  201.9 1.5 collective-permute-start.46
  203.5 6.9 %collective-permute-start.55 = (bf16[1,48,1024]{2,1,0:T(8,128)(2,1)S(1)}, bf16[1,48,1024]{2,1,0:T(8,128)(2,1)S(1)}, u32[]{:S(2)}, u32[]{:S(2)}) collective-permute-start(bf16[1,48,1024]{2,1,0:T(8,128)(2,1)S(1)} %slice_bitcast_fusion.18), channel_id=1, source_target_pairs={{0,2},{2,4},{4,6},{6,0},{1,3},{3,5},{5,7},{7,1},{8,10},{10,12},{12... | collective-permute-start | bytes 294920 | tf_op jit(solution)/shard_map/ppermute | solution.py:17
  210.5 2.2 collective-permute-done.39
  213.2 1.6 collective-permute-start.41
  214.8 3.5 %collective-permute-start.50 = (bf16[1,48,1024]{2,1,0:T(8,128)(2,1)S(1)}, bf16[1,48,1024]{2,1,0:T(8,128)(2,1)S(1)}, u32[]{:S(2)}, u32[]{:S(2)}) collective-permute-start(bf16[1,48,1024]{2,1,0:T(8,128)(2,1)S(1)} %slice_bitcast_fusion.19), channel_id=1, source_target_pairs={{0,2},{2,4},{4,6},{6,0},{1,3},{3,5},{5,7},{7,1},{8,10},{10,12},{12... | collective-permute-start | bytes 294920 | tf_op jit(solution)/shard_map/ppermute | solution.py:17
  219.3 1.6 collective-permute-start.48
  221.4 1.4 collective-permute-start.56
  222.8 3.5 %collective-permute-done.49 = bf16[1,48,1024]{2,1,0:T(8,128)(2,1)S(1)} collective-permute-done((bf16[1,48,1024]{2,1,0:T(8,128)(2,1)S(1)}, bf16[1,48,1024]{2,1,0:T(8,128)(2,1)S(1)}, u32[]{:S(2)}, u32[]{:S(2)}) %collective-permute-start.49) | collective-permute-done | bytes 98336 | tf_op jit(solution)/shard_map/ppermute | solution.py:17
  227.7 1.7 collective-permute-start.51
  229.4 2.3 collective-permute-done.56
  231.8 4.7 %collective-permute-done.51 = bf16[128,1024]{1,0:T(8,128)(2,1)S(1)} collective-permute-done((bf16[128,1024]{1,0:T(8,128)(2,1)S(1)}, bf16[128,1024]{1,0:T(8,128)(2,1)S(1)}, u32[]{:S(2)}, u32[]{:S(2)}) %collective-permute-start.51) | collective-permute-done | bytes 262176 | tf_op jit(solution)/shard_map/ppermute | solution.py:17
  (190 shorter events, 33.7 us)
Async XLA Ops:
  0.0 14.1 %copy-start.13 = (s32[1,1,128,1]{2,3,1,0:T(1,128)S(1)}, s32[1,1,128,1]{2,3,1,0:T(1,128)}, u32[]{:S(2)}) copy-start(s32[1,1,128,1]{2,3,1,0:T(1,128)} %param.16) | copy-start | bytes 1540
  1.0 15.7 %collective-permute-start.2 = (bf16[128,256]{1,0:T(8,128)(2,1)S(1)}, bf16[128,256]{1,0:T(8,128)(2,1)S(1)}, u32[]{:S(2)}, u32[]{:S(2)}) collective-permute-start(bf16[128,256]{1,0:T(8,128)(2,1)S(1)} %pad_maximum_fusion.11), channel_id=1, source_target_pairs={{0,6},{2,4},{4,2},{6,0},{1,7},{3,5},{5,3},{7,1},{8,14},{10,12},{12... | collective-permute-start | bytes 196616 | tf_op jit(solution)/shard_map/ppermute | solution.py:21
  6.1 10.6 %collective-permute-start = (bf16[128,256]{1,0:T(8,128)(2,1)S(1)}, bf16[128,256]{1,0:T(8,128)(2,1)S(1)}, u32[]{:S(2)}, u32[]{:S(2)}) collective-permute-start(bf16[128,256]{1,0:T(8,128)(2,1)S(1)} %pad_maximum_fusion.9), channel_id=1, source_target_pairs={{0,2},{2,0},{4,6},{6,4},{1,3},{3,1},{5,7},{7,5},{8,10},{10,8},{12,... | collective-permute-start | bytes 196616 | tf_op jit(solution)/shard_map/ppermute | solution.py:21
  6.2 10.5 %collective-permute-start.1 = (bf16[128,256]{1,0:T(8,128)(2,1)S(1)}, bf16[128,256]{1,0:T(8,128)(2,1)S(1)}, u32[]{:S(2)}, u32[]{:S(2)}) collective-permute-start(bf16[128,256]{1,0:T(8,128)(2,1)S(1)} %pad_maximum_fusion.10), channel_id=1, source_target_pairs={{0,4},{2,6},{4,0},{6,2},{1,5},{3,7},{5,1},{7,3},{8,12},{10,14},{12... | collective-permute-start | bytes 196616 | tf_op jit(solution)/shard_map/ppermute | solution.py:21
  8.3 11.2 %collective-permute-start.3 = (bf16[128,1024]{0,1:T(8,128)(2,1)S(1)}, bf16[128,1024]{0,1:T(8,128)(2,1)S(1)}, u32[]{:S(2)}, u32[]{:S(2)}) collective-permute-start(bf16[128,1024]{0,1:T(8,128)(2,1)S(1)} %bitcast.343), channel_id=1, source_target_pairs={{0,6},{6,0},{1,7},{7,1},{8,14},{14,8},{9,15},{15,9},{16,22},{22,16... | collective-permute-start | bytes 786440 | tf_op jit(solution)/shard_map/ppermute | solution.py:21
  14.0 58.5 %collective-permute-start.14 = (bf16[1024,2048]{1,0:T(8,128)(2,1)}, bf16[1024,2048]{1,0:T(8,128)(2,1)}, u32[]{:S(2)}, u32[]{:S(2)}) collective-permute-start(bf16[1024,2048]{1,0:T(8,128)(2,1)} %bitcast.309), channel_id=1, source_target_pairs={{0,1},{1,0},{2,3},{3,2},{4,5},{5,4},{6,7},{7,6},{8,9},{9,8},{10,11... | collective-permute-start | bytes 12582920 | tf_op jit(solution)/shard_map/ppermute | solution.py:17
  16.7 30.4 %copy-start.9 = (bf16[512,256]{1,0:T(8,128)(2,1)}, bf16[512,256]{1,0:T(8,128)(2,1)S(1)}, u32[]{:S(2)}) copy-start(bf16[512,256]{1,0:T(8,128)(2,1)S(1)} %pad_maximum_fusion.8) | copy-start | bytes 786436
  19.5 7.8 %collective-permute-start.4 = (bf16[128,1024]{0,1:T(8,128)(2,1)S(1)}, bf16[128,1024]{0,1:T(8,128)(2,1)S(1)}, u32[]{:S(2)}, u32[]{:S(2)}) collective-permute-start(bf16[128,1024]{0,1:T(8,128)(2,1)S(1)} %bitcast.345), channel_id=1, source_target_pairs={{0,4},{6,2},{1,5},{7,3},{8,12},{14,10},{9,13},{15,11},{16,20},{22,... | collective-permute-start | bytes 786440 | tf_op jit(solution)/shard_map/ppermute | solution.py:21
  27.3 18.1 %collective-permute-start.5 = (bf16[128,1024]{0,1:T(8,128)(2,1)S(1)}, bf16[128,1024]{0,1:T(8,128)(2,1)}, u32[]{:S(2)}, u32[]{:S(2)}) collective-permute-start(bf16[128,1024]{0,1:T(8,128)(2,1)S(1)} %bitcast.346), channel_id=1, source_target_pairs={{2,6},{4,0},{3,7},{5,1},{10,14},{12,8},{11,15},{13,9},{18,22},{20,... | collective-permute-start | bytes 786440 | tf_op jit(solution)/shard_map/ppermute | solution.py:21
  28.5 16.8 %collective-permute-start.6 = (bf16[128,1024]{0,1:T(8,128)(2,1)S(1)}, bf16[128,1024]{0,1:T(8,128)(2,1)}, u32[]{:S(2)}, u32[]{:S(2)}) collective-permute-start(bf16[128,1024]{0,1:T(8,128)(2,1)S(1)} %bitcast.344), channel_id=1, source_target_pairs={{2,4},{4,2},{3,5},{5,3},{10,12},{12,10},{11,13},{13,11},{18,20},{2... | collective-permute-start | bytes 786440 | tf_op jit(solution)/shard_map/ppermute | solution.py:21
  37.3 30.1 %collective-permute-start.11 = (bf16[128,2048]{1,0:T(8,128)(2,1)}, bf16[128,2048]{1,0:T(8,128)(2,1)}, u32[]{:S(2)}, u32[]{:S(2)}) collective-permute-start(bf16[128,2048]{1,0:T(8,128)(2,1)} %get-tuple-element.73), channel_id=1, source_target_pairs={{0,2},{6,4},{1,3},{7,5},{8,10},{14,12},{9,11},{15,13},{16,18},{22,... | collective-permute-start | bytes 1572872 | tf_op jit(solution)/shard_map/ppermute | solution.py:21
  45.3 17.5 %collective-permute-start.7 = (bf16[128,1024]{0,1:T(8,128)(2,1)}, bf16[128,1024]{0,1:T(8,128)(2,1)}, u32[]{:S(2)}, u32[]{:S(2)}) collective-permute-start(bf16[128,1024]{0,1:T(8,128)(2,1)} %bitcast.17), channel_id=1, source_target_pairs={{0,2},{2,0},{4,6},{6,4},{1,3},{3,1},{5,7},{7,5},{8,10},{10,8},{12,... | collective-permute-start | bytes 786440 | tf_op jit(solution)/shard_map/ppermute | solution.py:21
  52.7 28.7 %collective-permute-start.9 = (bf16[128,2048]{1,0:T(8,128)(2,1)}, bf16[128,2048]{1,0:T(8,128)(2,1)}, u32[]{:S(2)}, u32[]{:S(2)}) collective-permute-start(bf16[128,2048]{1,0:T(8,128)(2,1)} %get-tuple-element.75), channel_id=1, source_target_pairs={{0,2},{6,4},{1,3},{7,5},{8,10},{14,12},{9,11},{15,13},{16,18},{22,... | collective-permute-start | bytes 1572872 | tf_op jit(solution)/shard_map/ppermute | solution.py:21
  71.6 21.3 %collective-permute-start.12 = (bf16[128,2048]{1,0:T(8,128)(2,1)S(1)}, bf16[128,2048]{1,0:T(8,128)(2,1)S(1)}, u32[]{:S(2)}, u32[]{:S(2)}) collective-permute-start(bf16[128,2048]{1,0:T(8,128)(2,1)S(1)} %add_convert_fusion.4), channel_id=1, source_target_pairs={{2,4},{4,2},{3,5},{5,3},{10,12},{12,10},{11,13},{13,11},{18,20},{2... | collective-permute-start | bytes 1572872 | tf_op jit(solution)/shard_map/ppermute | solution.py:21
  75.5 7.8 %copy-start.7 = (bf16[128,8,128]{2,0,1:T(8,128)(2,1)S(1)}, bf16[128,8,128]{2,0,1:T(8,128)(2,1)}, u32[]{:S(2)}) copy-start(bf16[128,8,128]{2,0,1:T(8,128)(2,1)} %convolution_convert_fusion.2) | copy-start | bytes 786436
  75.5 16.7 %collective-permute-start.18 = (bf16[128,2048]{1,0:T(8,128)(2,1)S(1)}, bf16[128,2048]{1,0:T(8,128)(2,1)S(1)}, u32[]{:S(2)}, u32[]{:S(2)}) collective-permute-start(bf16[128,2048]{1,0:T(8,128)(2,1)S(1)} %get-tuple-element.77), channel_id=1, source_target_pairs={{0,2},{6,4},{1,3},{7,5},{8,10},{14,12},{9,11},{15,13},{16,18},{22,... | collective-permute-start | bytes 1572872 | tf_op jit(solution)/shard_map/ppermute | solution.py:21
  82.6 35.1 %collective-permute-start.10 = (bf16[128,2048]{1,0:T(8,128)(2,1)S(1)}, bf16[128,2048]{1,0:T(8,128)(2,1)S(1)}, u32[]{:S(2)}, u32[]{:S(2)}) collective-permute-start(bf16[128,2048]{1,0:T(8,128)(2,1)S(1)} %add_convert_fusion.5), channel_id=1, source_target_pairs={{2,4},{4,2},{3,5},{5,3},{10,12},{12,10},{11,13},{13,11},{18,20},{2... | collective-permute-start | bytes 1572872 | tf_op jit(solution)/shard_map/ppermute | solution.py:21
  86.2 17.2 %collective-permute-start.16 = (bf16[128,2048]{1,0:T(8,128)(2,1)S(1)}, bf16[128,2048]{1,0:T(8,128)(2,1)S(1)}, u32[]{:S(2)}, u32[]{:S(2)}) collective-permute-start(bf16[128,2048]{1,0:T(8,128)(2,1)S(1)} %get-tuple-element.79), channel_id=1, source_target_pairs={{0,2},{6,4},{1,3},{7,5},{8,10},{14,12},{9,11},{15,13},{16,18},{22,... | collective-permute-start | bytes 1572872 | tf_op jit(solution)/shard_map/ppermute | solution.py:21
  92.3 11.9 %collective-permute-start.19 = (bf16[128,2048]{1,0:T(8,128)(2,1)S(1)}, bf16[128,2048]{1,0:T(8,128)(2,1)S(1)}, u32[]{:S(2)}, u32[]{:S(2)}) collective-permute-start(bf16[128,2048]{1,0:T(8,128)(2,1)S(1)} %add_convert_fusion.1), channel_id=1, source_target_pairs={{2,4},{4,2},{3,5},{5,3},{10,12},{12,10},{11,13},{13,11},{18,20},{2... | collective-permute-start | bytes 1572872 | tf_op jit(solution)/shard_map/ppermute | solution.py:21
  93.1 25.8 %collective-permute-start.8 = (bf16[128,2048]{1,0:T(8,128)(2,1)S(1)}, bf16[128,2048]{1,0:T(8,128)(2,1)S(1)}, u32[]{:S(2)}, u32[]{:S(2)}) collective-permute-start(bf16[128,2048]{1,0:T(8,128)(2,1)S(1)} %get-tuple-element.35), channel_id=1, source_target_pairs={{0,2},{6,4},{1,3},{7,5},{8,10},{14,12},{9,11},{15,13},{16,18},{22,... | collective-permute-start | bytes 1572872 | tf_op jit(solution)/shard_map/ppermute | solution.py:21
  101.6 17.4 %collective-permute-start.13 = (bf16[128,2048]{1,0:T(8,128)(2,1)S(1)}, bf16[128,2048]{1,0:T(8,128)(2,1)S(1)}, u32[]{:S(2)}, u32[]{:S(2)}) collective-permute-start(bf16[128,2048]{1,0:T(8,128)(2,1)S(1)} %get-tuple-element.36), channel_id=1, source_target_pairs={{2,0},{4,6},{3,1},{5,7},{10,8},{12,14},{11,9},{13,15},{18,16},{20,... | collective-permute-start | bytes 1572872 | tf_op jit(solution)/shard_map/ppermute | solution.py:21
  103.5 15.8 %collective-permute-start.17 = (bf16[128,2048]{1,0:T(8,128)(2,1)S(1)}, bf16[128,2048]{1,0:T(8,128)(2,1)S(1)}, u32[]{:S(2)}, u32[]{:S(2)}) collective-permute-start(bf16[128,2048]{1,0:T(8,128)(2,1)S(1)} %add_convert_fusion.2), channel_id=1, source_target_pairs={{2,4},{4,2},{3,5},{5,3},{10,12},{12,10},{11,13},{13,11},{18,20},{2... | collective-permute-start | bytes 1572872 | tf_op jit(solution)/shard_map/ppermute | solution.py:21
  107.1 21.8 %copy-start.4 = (bf16[1,1,128,4096]{3,2,1,0:T(8,128)(2,1)S(1)}, bf16[1,1,128,4096]{3,2,1,0:T(8,128)(2,1)}, u32[]{:S(2)}) copy-start(bf16[1,1,128,4096]{3,2,1,0:T(8,128)(2,1)} %param.11) | copy-start | bytes 3145732
  107.1 17.1 %collective-permute-start.15 = (bf16[128,2048]{1,0:T(8,128)(2,1)S(1)}, bf16[128,2048]{1,0:T(8,128)(2,1)S(1)}, u32[]{:S(2)}, u32[]{:S(2)}) collective-permute-start(bf16[128,2048]{1,0:T(8,128)(2,1)S(1)} %get-tuple-element.33), channel_id=1, source_target_pairs={{0,2},{6,4},{1,3},{7,5},{8,10},{14,12},{9,11},{15,13},{16,18},{22,... | collective-permute-start | bytes 1572872 | tf_op jit(solution)/shard_map/ppermute | solution.py:21
  117.6 11.3 %collective-permute-start.20 = (bf16[128,2048]{1,0:T(8,128)(2,1)S(1)}, bf16[128,2048]{1,0:T(8,128)(2,1)S(1)}, u32[]{:S(2)}, u32[]{:S(2)}) collective-permute-start(bf16[128,2048]{1,0:T(8,128)(2,1)S(1)} %get-tuple-element.34), channel_id=1, source_target_pairs={{2,0},{4,6},{3,1},{5,7},{10,8},{12,14},{11,9},{13,15},{18,16},{20,... | collective-permute-start | bytes 1572872 | tf_op jit(solution)/shard_map/ppermute | solution.py:21
  128.9 25.0 %slice-start.3 = ((s8[12582912]{0:T(1024)(128)(4,1)}), s8[4194304]{0:T(1024)(128)(4,1)S(1)}, s32[]{:S(2)}) async-start(s8[12582912]{0:T(1024)(128)(4,1)} %bitcast.337), calls=%async_computation.3 | async-start | bytes 8388608
  128.9 25.0 %slice-start.4 = ((s8[12582912]{0:T(1024)(128)(4,1)}), s8[4194304]{0:T(1024)(128)(4,1)S(1)}, s32[]{:S(2)}) async-start(s8[12582912]{0:T(1024)(128)(4,1)} %bitcast.337), calls=%async_computation.4 | async-start | bytes 8388608
  133.4 20.6 %slice-start.5 = ((s8[12582912]{0:T(1024)(128)(4,1)}), s8[4194304]{0:T(1024)(128)(4,1)S(1)}, s32[]{:S(2)}) async-start(s8[12582912]{0:T(1024)(128)(4,1)} %bitcast.337), calls=%async_computation.5 | async-start | bytes 8388608
  134.1 4.7 %collective-permute-start.23 = (bf16[1,48,1024]{2,1,0:T(8,128)(2,1)S(1)}, bf16[1,48,1024]{2,1,0:T(8,128)(2,1)S(1)}, u32[]{:S(2)}, u32[]{:S(2)}) collective-permute-start(bf16[1,48,1024]{2,1,0:T(8,128)(2,1)S(1)} %get-tuple-element.32), channel_id=1, source_target_pairs={{0,6},{2,0},{4,2},{6,4},{1,7},{3,1},{5,3},{7,5},{8,14},{10,8},{12,... | collective-permute-start | bytes 294920 | tf_op jit(solution)/shard_map/ppermute | solution.py:17
  135.5 7.7 %collective-permute-start.22 = (bf16[1,48,1024]{2,1,0:T(8,128)(2,1)S(1)}, bf16[1,48,1024]{2,1,0:T(8,128)(2,1)S(1)}, u32[]{:S(2)}, u32[]{:S(2)}) collective-permute-start(bf16[1,48,1024]{2,1,0:T(8,128)(2,1)S(1)} %get-tuple-element.28), channel_id=1, source_target_pairs={{0,4},{2,6},{4,0},{6,2},{1,5},{3,7},{5,1},{7,3},{8,12},{10,14},{12... | collective-permute-start | bytes 294920 | tf_op jit(solution)/shard_map/ppermute | solution.py:17
  135.6 7.6 %collective-permute-start.21 = (bf16[1,48,1024]{2,1,0:T(8,128)(2,1)S(1)}, bf16[1,48,1024]{2,1,0:T(8,128)(2,1)S(1)}, u32[]{:S(2)}, u32[]{:S(2)}) collective-permute-start(bf16[1,48,1024]{2,1,0:T(8,128)(2,1)S(1)} %get-tuple-element.29), channel_id=1, source_target_pairs={{0,2},{2,4},{4,6},{6,0},{1,3},{3,5},{5,7},{7,1},{8,10},{10,12},{12... | collective-permute-start | bytes 294920 | tf_op jit(solution)/shard_map/ppermute | solution.py:17
  143.3 10.6 %collective-permute-start.24 = (bf16[4,48,1024]{2,1,0:T(8,128)(2,1)S(1)}, bf16[4,48,1024]{2,1,0:T(8,128)(2,1)S(1)}, u32[]{:S(2)}, u32[]{:S(2)}) collective-permute-start(bf16[4,48,1024]{2,1,0:T(8,128)(2,1)S(1)} %maximum_bitcast_fusion.1), channel_id=1, source_target_pairs={{0,1},{1,0},{2,3},{3,2},{4,5},{5,4},{6,7},{7,6},{8,9},{9,8},{10,11... | collective-permute-start | bytes 1179656 | tf_op jit(solution)/shard_map/ppermute | solution.py:17
  143.3 6.4 %collective-permute-start.27 = (bf16[1,48,1024]{2,1,0:T(8,128)(2,1)S(1)}, bf16[1,48,1024]{2,1,0:T(8,128)(2,1)S(1)}, u32[]{:S(2)}, u32[]{:S(2)}) collective-permute-start(bf16[1,48,1024]{2,1,0:T(8,128)(2,1)S(1)} %get-tuple-element.31), channel_id=1, source_target_pairs={{0,6},{2,0},{4,2},{6,4},{1,7},{3,1},{5,3},{7,5},{8,14},{10,8},{12,... | collective-permute-start | bytes 294920 | tf_op jit(solution)/shard_map/ppermute | solution.py:17
  143.7 10.0 %collective-permute-start.26 = (bf16[1,48,1024]{2,1,0:T(8,128)(2,1)S(1)}, bf16[1,48,1024]{2,1,0:T(8,128)(2,1)S(1)}, u32[]{:S(2)}, u32[]{:S(2)}) collective-permute-start(bf16[1,48,1024]{2,1,0:T(8,128)(2,1)S(1)} %get-tuple-element.26), channel_id=1, source_target_pairs={{0,4},{2,6},{4,0},{6,2},{1,5},{3,7},{5,1},{7,3},{8,12},{10,14},{12... | collective-permute-start | bytes 294920 | tf_op jit(solution)/shard_map/ppermute | solution.py:17
  143.9 9.8 %collective-permute-start.25 = (bf16[1,48,1024]{2,1,0:T(8,128)(2,1)S(1)}, bf16[1,48,1024]{2,1,0:T(8,128)(2,1)S(1)}, u32[]{:S(2)}, u32[]{:S(2)}) collective-permute-start(bf16[1,48,1024]{2,1,0:T(8,128)(2,1)S(1)} %get-tuple-element.27), channel_id=1, source_target_pairs={{0,2},{2,4},{4,6},{6,0},{1,3},{3,5},{5,7},{7,1},{8,10},{10,12},{12... | collective-permute-start | bytes 294920 | tf_op jit(solution)/shard_map/ppermute | solution.py:17
  153.8 1.8 collective-permute-start.28
  157.0 6.4 %collective-permute-start.35 = (bf16[1,48,1024]{2,1,0:T(8,128)(2,1)S(1)}, bf16[1,48,1024]{2,1,0:T(8,128)(2,1)S(1)}, u32[]{:S(2)}, u32[]{:S(2)}) collective-permute-start(bf16[1,48,1024]{2,1,0:T(8,128)(2,1)S(1)} %slice_bitcast_fusion.20), channel_id=1, source_target_pairs={{0,6},{2,0},{4,2},{6,4},{1,7},{3,1},{5,3},{7,5},{8,14},{10,8},{12,... | collective-permute-start | bytes 294920 | tf_op jit(solution)/shard_map/ppermute | solution.py:17
  158.3 11.0 %collective-permute-start.34 = (bf16[1,48,1024]{2,1,0:T(8,128)(2,1)S(1)}, bf16[1,48,1024]{2,1,0:T(8,128)(2,1)S(1)}, u32[]{:S(2)}, u32[]{:S(2)}) collective-permute-start(bf16[1,48,1024]{2,1,0:T(8,128)(2,1)S(1)} %get-tuple-element.59), channel_id=1, source_target_pairs={{0,4},{2,6},{4,0},{6,2},{1,5},{3,7},{5,1},{7,3},{8,12},{10,14},{12... | collective-permute-start | bytes 294920 | tf_op jit(solution)/shard_map/ppermute | solution.py:17
  159.5 9.8 %collective-permute-start.33 = (bf16[1,48,1024]{2,1,0:T(8,128)(2,1)S(1)}, bf16[1,48,1024]{2,1,0:T(8,128)(2,1)S(1)}, u32[]{:S(2)}, u32[]{:S(2)}) collective-permute-start(bf16[1,48,1024]{2,1,0:T(8,128)(2,1)S(1)} %get-tuple-element.60), channel_id=1, source_target_pairs={{0,2},{2,4},{4,6},{6,0},{1,3},{3,5},{5,7},{7,1},{8,10},{10,12},{12... | collective-permute-start | bytes 294920 | tf_op jit(solution)/shard_map/ppermute | solution.py:17
  161.5 11.3 %collective-permute-start.31 = (bf16[1,48,1024]{2,1,0:T(8,128)(2,1)S(1)}, bf16[1,48,1024]{2,1,0:T(8,128)(2,1)S(1)}, u32[]{:S(2)}, u32[]{:S(2)}) collective-permute-start(bf16[1,48,1024]{2,1,0:T(8,128)(2,1)S(1)} %slice_bitcast_fusion.21), channel_id=1, source_target_pairs={{0,6},{2,0},{4,2},{6,4},{1,7},{3,1},{5,3},{7,5},{8,14},{10,8},{12,... | collective-permute-start | bytes 294920 | tf_op jit(solution)/shard_map/ppermute | solution.py:17
  169.4 11.2 %collective-permute-start.36 = (bf16[4,48,1024]{2,1,0:T(8,128)(2,1)S(1)}, bf16[4,48,1024]{2,1,0:T(8,128)(2,1)S(1)}, u32[]{:S(2)}, u32[]{:S(2)}) collective-permute-start(bf16[4,48,1024]{2,1,0:T(8,128)(2,1)S(1)} %maximum_bitcast_fusion.4), channel_id=1, source_target_pairs={{0,1},{1,0},{2,3},{3,2},{4,5},{5,4},{6,7},{7,6},{8,9},{9,8},{10,11... | collective-permute-start | bytes 1179656 | tf_op jit(solution)/shard_map/ppermute | solution.py:17
  169.5 11.0 %collective-permute-start.30 = (bf16[1,48,1024]{2,1,0:T(8,128)(2,1)S(1)}, bf16[1,48,1024]{2,1,0:T(8,128)(2,1)S(1)}, u32[]{:S(2)}, u32[]{:S(2)}) collective-permute-start(bf16[1,48,1024]{2,1,0:T(8,128)(2,1)S(1)} %get-tuple-element.56), channel_id=1, source_target_pairs={{0,4},{2,6},{4,0},{6,2},{1,5},{3,7},{5,1},{7,3},{8,12},{10,14},{12... | collective-permute-start | bytes 294920 | tf_op jit(solution)/shard_map/ppermute | solution.py:17
  172.8 7.7 %collective-permute-start.29 = (bf16[1,48,1024]{2,1,0:T(8,128)(2,1)S(1)}, bf16[1,48,1024]{2,1,0:T(8,128)(2,1)S(1)}, u32[]{:S(2)}, u32[]{:S(2)}) collective-permute-start(bf16[1,48,1024]{2,1,0:T(8,128)(2,1)S(1)} %get-tuple-element.57), channel_id=1, source_target_pairs={{0,2},{2,4},{4,6},{6,0},{1,3},{3,5},{5,7},{7,1},{8,10},{10,12},{12... | collective-permute-start | bytes 294920 | tf_op jit(solution)/shard_map/ppermute | solution.py:17
  180.6 1.8 collective-permute-start.32
  185.9 4.0 %collective-permute-start.42 = (bf16[4,48,1024]{2,1,0:T(8,128)(2,1)S(1)}, bf16[4,48,1024]{2,1,0:T(8,128)(2,1)S(1)}, u32[]{:S(2)}, u32[]{:S(2)}) collective-permute-start(bf16[4,48,1024]{2,1,0:T(8,128)(2,1)S(1)} %bitcast.342), channel_id=1, source_target_pairs={{0,1},{1,0},{2,3},{3,2},{4,5},{5,4},{6,7},{7,6},{8,9},{9,8},{10,11... | collective-permute-start | bytes 1179656 | tf_op jit(solution)/shard_map/ppermute | solution.py:17
  189.1 5.2 %collective-permute-start.52 = (bf16[4,48,1024]{2,1,0:T(8,128)(2,1)S(1)}, bf16[4,48,1024]{2,1,0:T(8,128)(2,1)S(1)}, u32[]{:S(2)}, u32[]{:S(2)}) collective-permute-start(bf16[4,48,1024]{2,1,0:T(8,128)(2,1)S(1)} %bitcast.340), channel_id=1, source_target_pairs={{0,1},{1,0},{2,3},{3,2},{4,5},{5,4},{6,7},{7,6},{8,9},{9,8},{10,11... | collective-permute-start | bytes 1179656 | tf_op jit(solution)/shard_map/ppermute | solution.py:17
  189.3 5.6 %collective-permute-start.47 = (bf16[4,48,1024]{2,1,0:T(8,128)(2,1)S(1)}, bf16[4,48,1024]{2,1,0:T(8,128)(2,1)S(1)}, u32[]{:S(2)}, u32[]{:S(2)}) collective-permute-start(bf16[4,48,1024]{2,1,0:T(8,128)(2,1)S(1)} %bitcast.339), channel_id=1, source_target_pairs={{0,1},{1,0},{2,3},{3,2},{4,5},{5,4},{6,7},{7,6},{8,9},{9,8},{10,11... | collective-permute-start | bytes 1179656 | tf_op jit(solution)/shard_map/ppermute | solution.py:17
  189.6 2.3 collective-permute-start.37
  190.2 7.6 %collective-permute-start.45 = (bf16[1,48,1024]{2,1,0:T(8,128)(2,1)S(1)}, bf16[1,48,1024]{2,1,0:T(8,128)(2,1)S(1)}, u32[]{:S(2)}, u32[]{:S(2)}) collective-permute-start(bf16[1,48,1024]{2,1,0:T(8,128)(2,1)S(1)} %get-tuple-element.52), channel_id=1, source_target_pairs={{0,2},{2,4},{4,6},{6,0},{1,3},{3,5},{5,7},{7,1},{8,10},{10,12},{12... | collective-permute-start | bytes 294920 | tf_op jit(solution)/shard_map/ppermute | solution.py:17
  190.3 11.3 %collective-permute-start.44 = (bf16[1,48,1024]{2,1,0:T(8,128)(2,1)S(1)}, bf16[1,48,1024]{2,1,0:T(8,128)(2,1)S(1)}, u32[]{:S(2)}, u32[]{:S(2)}) collective-permute-start(bf16[1,48,1024]{2,1,0:T(8,128)(2,1)S(1)} %get-tuple-element.53), channel_id=1, source_target_pairs={{0,4},{2,6},{4,0},{6,2},{1,5},{3,7},{5,1},{7,3},{8,12},{10,14},{12... | collective-permute-start | bytes 294920 | tf_op jit(solution)/shard_map/ppermute | solution.py:17
  192.0 9.6 %collective-permute-start.43 = (bf16[1,48,1024]{2,1,0:T(8,128)(2,1)S(1)}, bf16[1,48,1024]{2,1,0:T(8,128)(2,1)S(1)}, u32[]{:S(2)}, u32[]{:S(2)}) collective-permute-start(bf16[1,48,1024]{2,1,0:T(8,128)(2,1)S(1)} %get-tuple-element.54), channel_id=1, source_target_pairs={{0,6},{2,0},{4,2},{6,4},{1,7},{3,1},{5,3},{7,5},{8,14},{10,8},{12,... | collective-permute-start | bytes 294920 | tf_op jit(solution)/shard_map/ppermute | solution.py:17
  194.2 16.2 %collective-permute-start.40 = (bf16[1,48,1024]{2,1,0:T(8,128)(2,1)S(1)}, bf16[1,48,1024]{2,1,0:T(8,128)(2,1)S(1)}, u32[]{:S(2)}, u32[]{:S(2)}) collective-permute-start(bf16[1,48,1024]{2,1,0:T(8,128)(2,1)S(1)} %get-tuple-element.45), channel_id=1, source_target_pairs={{0,2},{2,4},{4,6},{6,0},{1,3},{3,5},{5,7},{7,1},{8,10},{10,12},{12... | collective-permute-start | bytes 294920 | tf_op jit(solution)/shard_map/ppermute | solution.py:17
  194.9 17.7 %collective-permute-start.39 = (bf16[1,48,1024]{2,1,0:T(8,128)(2,1)S(1)}, bf16[1,48,1024]{2,1,0:T(8,128)(2,1)S(1)}, u32[]{:S(2)}, u32[]{:S(2)}) collective-permute-start(bf16[1,48,1024]{2,1,0:T(8,128)(2,1)S(1)} %get-tuple-element.46), channel_id=1, source_target_pairs={{0,4},{2,6},{4,0},{6,2},{1,5},{3,7},{5,1},{7,3},{8,12},{10,14},{12... | collective-permute-start | bytes 294920 | tf_op jit(solution)/shard_map/ppermute | solution.py:17
  197.8 15.1 %collective-permute-start.38 = (bf16[1,48,1024]{2,1,0:T(8,128)(2,1)S(1)}, bf16[1,48,1024]{2,1,0:T(8,128)(2,1)S(1)}, u32[]{:S(2)}, u32[]{:S(2)}) collective-permute-start(bf16[1,48,1024]{2,1,0:T(8,128)(2,1)S(1)} %get-tuple-element.47), channel_id=1, source_target_pairs={{0,6},{2,0},{4,2},{6,4},{1,7},{3,1},{5,3},{7,5},{8,14},{10,8},{12,... | collective-permute-start | bytes 294920 | tf_op jit(solution)/shard_map/ppermute | solution.py:17
  201.9 27.5 %collective-permute-start.46 = (bf16[128,1024]{1,0:T(8,128)(2,1)S(1)}, bf16[128,1024]{1,0:T(8,128)(2,1)S(1)}, u32[]{:S(2)}, u32[]{:S(2)}) collective-permute-start(bf16[128,1024]{1,0:T(8,128)(2,1)S(1)} %fusion.61), channel_id=1, source_target_pairs={{0,8},{8,16},{16,24},{24,0},{1,9},{9,17},{17,25},{25,1},{2,10},{10... | collective-permute-start | bytes 786440 | tf_op jit(solution)/shard_map/ppermute | solution.py:17
  203.5 11.4 %collective-permute-start.55 = (bf16[1,48,1024]{2,1,0:T(8,128)(2,1)S(1)}, bf16[1,48,1024]{2,1,0:T(8,128)(2,1)S(1)}, u32[]{:S(2)}, u32[]{:S(2)}) collective-permute-start(bf16[1,48,1024]{2,1,0:T(8,128)(2,1)S(1)} %slice_bitcast_fusion.18), channel_id=1, source_target_pairs={{0,2},{2,4},{4,6},{6,0},{1,3},{3,5},{5,7},{7,1},{8,10},{10,12},{12... | collective-permute-start | bytes 294920 | tf_op jit(solution)/shard_map/ppermute | solution.py:17
  210.4 8.0 %collective-permute-start.54 = (bf16[1,48,1024]{2,1,0:T(8,128)(2,1)S(1)}, bf16[1,48,1024]{2,1,0:T(8,128)(2,1)S(1)}, u32[]{:S(2)}, u32[]{:S(2)}) collective-permute-start(bf16[1,48,1024]{2,1,0:T(8,128)(2,1)S(1)} %get-tuple-element.49), channel_id=1, source_target_pairs={{0,4},{2,6},{4,0},{6,2},{1,5},{3,7},{5,1},{7,3},{8,12},{10,14},{12... | collective-permute-start | bytes 294920 | tf_op jit(solution)/shard_map/ppermute | solution.py:17
  212.6 6.7 %collective-permute-start.53 = (bf16[1,48,1024]{2,1,0:T(8,128)(2,1)S(1)}, bf16[1,48,1024]{2,1,0:T(8,128)(2,1)S(1)}, u32[]{:S(2)}, u32[]{:S(2)}) collective-permute-start(bf16[1,48,1024]{2,1,0:T(8,128)(2,1)S(1)} %get-tuple-element.50), channel_id=1, source_target_pairs={{0,6},{2,0},{4,2},{6,4},{1,7},{3,1},{5,3},{7,5},{8,14},{10,8},{12,... | collective-permute-start | bytes 294920 | tf_op jit(solution)/shard_map/ppermute | solution.py:17
  213.2 16.3 %collective-permute-start.41 = (bf16[128,1024]{1,0:T(8,128)(2,1)S(1)}, bf16[128,1024]{1,0:T(8,128)(2,1)S(1)}, u32[]{:S(2)}, u32[]{:S(2)}) collective-permute-start(bf16[128,1024]{1,0:T(8,128)(2,1)S(1)} %fusion.62), channel_id=1, source_target_pairs={{0,8},{8,16},{16,24},{24,0},{1,9},{9,17},{17,25},{25,1},{2,10},{10... | collective-permute-start | bytes 786440 | tf_op jit(solution)/shard_map/ppermute | solution.py:17
  214.8 6.5 %collective-permute-start.50 = (bf16[1,48,1024]{2,1,0:T(8,128)(2,1)S(1)}, bf16[1,48,1024]{2,1,0:T(8,128)(2,1)S(1)}, u32[]{:S(2)}, u32[]{:S(2)}) collective-permute-start(bf16[1,48,1024]{2,1,0:T(8,128)(2,1)S(1)} %slice_bitcast_fusion.19), channel_id=1, source_target_pairs={{0,2},{2,4},{4,6},{6,0},{1,3},{3,5},{5,7},{7,1},{8,10},{10,12},{12... | collective-permute-start | bytes 294920 | tf_op jit(solution)/shard_map/ppermute | solution.py:17
  218.4 8.0 %collective-permute-start.49 = (bf16[1,48,1024]{2,1,0:T(8,128)(2,1)S(1)}, bf16[1,48,1024]{2,1,0:T(8,128)(2,1)S(1)}, u32[]{:S(2)}, u32[]{:S(2)}) collective-permute-start(bf16[1,48,1024]{2,1,0:T(8,128)(2,1)S(1)} %get-tuple-element.42), channel_id=1, source_target_pairs={{0,4},{2,6},{4,0},{6,2},{1,5},{3,7},{5,1},{7,3},{8,12},{10,14},{12... | collective-permute-start | bytes 294920 | tf_op jit(solution)/shard_map/ppermute | solution.py:17
  219.3 8.1 %collective-permute-start.48 = (bf16[1,48,1024]{2,1,0:T(8,128)(2,1)S(1)}, bf16[1,48,1024]{2,1,0:T(8,128)(2,1)S(1)}, u32[]{:S(2)}, u32[]{:S(2)}) collective-permute-start(bf16[1,48,1024]{2,1,0:T(8,128)(2,1)S(1)} %get-tuple-element.43), channel_id=1, source_target_pairs={{0,6},{2,0},{4,2},{6,4},{1,7},{3,1},{5,3},{7,5},{8,14},{10,8},{12,... | collective-permute-start | bytes 294920 | tf_op jit(solution)/shard_map/ppermute | solution.py:17
  221.4 10.4 %collective-permute-start.56 = (bf16[128,1024]{1,0:T(8,128)(2,1)S(1)}, bf16[128,1024]{1,0:T(8,128)(2,1)S(1)}, u32[]{:S(2)}, u32[]{:S(2)}) collective-permute-start(bf16[128,1024]{1,0:T(8,128)(2,1)S(1)} %fusion.59), channel_id=1, source_target_pairs={{0,8},{8,16},{16,24},{24,0},{1,9},{9,17},{17,25},{25,1},{2,10},{10... | collective-permute-start | bytes 786440 | tf_op jit(solution)/shard_map/ppermute | solution.py:17
  227.7 8.7 %collective-permute-start.51 = (bf16[128,1024]{1,0:T(8,128)(2,1)S(1)}, bf16[128,1024]{1,0:T(8,128)(2,1)S(1)}, u32[]{:S(2)}, u32[]{:S(2)}) collective-permute-start(bf16[128,1024]{1,0:T(8,128)(2,1)S(1)} %fusion.60), channel_id=1, source_target_pairs={{0,8},{8,16},{16,24},{24,0},{1,9},{9,17},{17,25},{25,1},{2,10},{10... | collective-permute-start | bytes 786440 | tf_op jit(solution)/shard_map/ppermute | solution.py:17
  (15 other events, 44.1 us)

commit v3 on v1

--- a/solution.py
+++ b/solution.py
@@ -8,13 +8,15 @@
 QUERY_HEADS = 32
 KEY_VALUE_HEADS = 2
 HEAD_SIZE = 128
-DISPATCH_CHUNKS = 2
-RETURN_CHUNKS = 2
 
 
 def shift(value, axis, by):
     devices = lax.axis_size(axis)
     return lax.ppermute(value, axis, [(i, (i + by) % devices) for i in range(devices)])
+
+
+def after(value, *earlier):
+    return lax.optimization_barrier((value, *earlier))[0]
 
 
 def attend_block(query_block, key_rows, value_rows, row_ids, col_ids):
@@ -53,7 +55,10 @@
     for k in range(1, contexts):
         pairs.append(shift(pair_for((me + k) % contexts), "ctx", k))
     for k in range(1, contexts):
-        blocks.append(shift(queries_for((me + k) % contexts), "ctx", k))
+        outgoing = queries_for((me + k) % contexts)
+        if k > 1:
+            outgoing = after(outgoing, blocks[1])
+        blocks.append(shift(outgoing, "ctx", k))
     if exps == 2:
         weights = [out_weight, shift(out_weight, "exp", 1)]
         first = my_exp * (width // 2)
@@ -69,24 +74,28 @@
     origins = [(me - k) % contexts * rows for k in range(contexts)]
     col_ids = jnp.concatenate([origin + within for origin in origins])
 
-    held = [None, None]
+    held, terms = [None, None], []
     for k in [*range(1, contexts), 0]:
+        block = blocks[k] if k == 1 else after(blocks[k], *terms)
         attended = attend_block(
-            blocks[k].reshape(rows, local_heads, HEAD_SIZE),
+            block.reshape(rows, local_heads, HEAD_SIZE),
             key_rows,
             value_rows,
             origins[k] + within,
             col_ids,
         ).reshape(rows, group_width)
+        terms = []
         for half in range(2):
             term = jnp.dot(attended, weights[half], preferred_element_type=jnp.float32)
+            if k == 0:
+                own = lax.dynamic_slice_in_dim(residual, offsets[half], width // 2, 1)
+                term = term + own.astype(jnp.float32)
+            terms.append(lax.optimization_barrier(term))
+        for half in range(2):
+            term = terms[half]
             if held[half] is not None:
                 term = term + held[half].astype(jnp.float32)
-            if k == 0:
-                own = lax.dynamic_slice_in_dim(residual, offsets[half], width // 2, 1)
-                held[half] = term + own.astype(jnp.float32)
-            else:
-                held[half] = shift(term.astype(jnp.bfloat16), "ctx", 1)
+            held[half] = term if k == 0 else shift(term.astype(jnp.bfloat16), "ctx", 1)
     return held, first
 
 
@@ -141,6 +150,9 @@
         (slot_ids[:, None] == slot_index[None, :, r]).astype(jnp.bfloat16)
         for r in range(route_count)
     )
+    next_slots = shift(slot_index.astype(jnp.float32), "pipe", 1).astype(jnp.int32)
+    next_weights = shift(route_weight[0, 0], "pipe", 1)
+    next_mixed = shift(mixed_rows.astype(jnp.bfloat16), "pipe", 1)
     packed = jnp.dot(slot_match, normed, preferred_element_type=jnp.float32).astype(jnp.bfloat16)
     packed = packed.reshape(contexts, per_context, capacity, model_width)
 
@@ -149,33 +161,23 @@
             return arrived[:, 0]
         return lax.dynamic_index_in_dim(arrived, exp // group_size, 1, keepdims=False)
 
+    def exchange(arrived):
+        rows = [wanted_by(arrived, my_exp)]
+        for k in range(1, exps):
+            rows.append(shift(wanted_by(arrived, (my_exp + k) % exps), "exp", k))
+        return jnp.concatenate(rows, axis=0).reshape(-1, model_width)
+
     hidden_width = down_weight.shape[2]
-    gate_up = 0.0
-    step = model_width // DISPATCH_CHUNKS
-    for chunk in range(DISPATCH_CHUNKS):
-        part = packed[..., chunk * step : (chunk + 1) * step]
-        arrived = jnp.stack(
-            [part[0]] + [shift(part[k], "ctx", k) for k in range(1, contexts)], axis=0
+
+    def expert_part(slot_rows):
+        gate_up = jnp.dot(slot_rows, in_weight[0, 0], preferred_element_type=jnp.float32)
+        hidden = (jax.nn.silu(gate_up[:, :hidden_width]) * gate_up[:, hidden_width:]).astype(
+            jnp.bfloat16
         )
-        gathered = [wanted_by(arrived, my_exp)]
-        for k in range(1, exps):
-            gathered.append(shift(wanted_by(arrived, (my_exp + k) % exps), "exp", k))
-        slot_rows = jnp.concatenate(gathered, axis=0).reshape(-1, step)
-        gate_up = gate_up + jnp.dot(
-            slot_rows,
-            in_weight[0, 0, chunk * step : (chunk + 1) * step],
-            preferred_element_type=jnp.float32,
-        )
-    hidden = (jax.nn.silu(gate_up[:, :hidden_width]) * gate_up[:, hidden_width:]).astype(
-        jnp.bfloat16
-    )
-
-    step = model_width // RETURN_CHUNKS
-    outputs = []
-    for chunk in range(RETURN_CHUNKS):
-        columns = slice(chunk * step, (chunk + 1) * step)
-        part = jnp.dot(hidden, down_weight[0, 0, :, columns], preferred_element_type=jnp.float32)
-        part = part.reshape(exps, contexts, capacity, step)
+        return jnp.dot(hidden, down_weight[0, 0], preferred_element_type=jnp.float32)
+
+    def summed(part, count):
+        part = part.reshape(exps, count, capacity, model_width)
         sums = [0.0] * per_context
         for k in range(exps):
             back = part[k]
@@ -186,17 +188,45 @@
             else:
                 place = (my_exp + k) % exps // group_size
                 sums = [s + jnp.where(place == i, back, 0.0) for i, s in enumerate(sums)]
-        total = jnp.stack(sums, axis=1).astype(jnp.bfloat16)
-        returned = jnp.concatenate(
-            [total[0]] + [shift(total[k], "ctx", -k) for k in range(1, contexts)], axis=0
-        ).reshape(slots, step)
-        layer = mixed_rows[:, columns]
+        return jnp.stack(sums, axis=1).astype(jnp.bfloat16)
+
+    def to_next_owner(rows, k):
+        pipes = lax.axis_size("pipe")
+        pairs = [
+            (p * contexts + c, (p + 1) % pipes * contexts + (c - k) % contexts)
+            for p in range(pipes)
+            for c in range(contexts)
+        ]
+        return lax.ppermute(rows, ("pipe", "ctx"), pairs)
+
+    order = sorted(range(1, contexts), key=lambda k: min(k, contexts - k))
+    groups = [[0, order[0]]] + [[k] for k in order[1:]]
+    arrived, returned = {0: packed[0]}, {}
+    for place, k in enumerate(order):
+        rows = packed[k]
+        if place >= 2:
+            rows = after(rows, arrived[order[place - 2]])
+        arrived[k] = shift(rows, "ctx", k)
+    part = None
+    for group in groups:
+        slot_rows = exchange(jnp.stack([arrived[k] for k in group], axis=0))
+        if part is not None:
+            slot_rows = after(slot_rows, part)
+        part = expert_part(slot_rows)
+        total = summed(part, len(group))
+        for i, k in enumerate(group):
+            returned[k] = to_next_owner(total[i], k)
+
+    layer = next_mixed.astype(jnp.float32)
+    width = per_context * capacity
+    for k in [0, *order]:
+        ids = slot_ids[k * width : (k + 1) * width]
+        rows = returned[k].reshape(width, model_width)
         for r in range(route_count):
-            match = (slot_ids[None, :] == slot_index[:, r, None]).astype(jnp.bfloat16)
-            picked = jnp.dot(match, returned, preferred_element_type=jnp.float32)
-            layer = layer + picked * route_weight[0, 0, :, r, None]
-        outputs.append(shift(layer.astype(jnp.bfloat16), "pipe", 1))
-    return jnp.concatenate(outputs, axis=1).reshape(1, 1, token_rows, model_width)
+            match = (ids[None, :] == next_slots[:, r, None]).astype(jnp.bfloat16)
+            picked = jnp.dot(match, rows, preferred_element_type=jnp.float32)
+            layer = layer + picked * next_weights[:, r, None]
+    return layer.astype(jnp.bfloat16).reshape(1, 1, token_rows, model_width)
 
 
 def solution(mesh):

time: 224 us -> 215 us (0.960)
  the two profiles are of different devices: /device:TPU:12 before, /device:TPU:0 now
where the time goes in v3:
time: 215 us; the launch traced here: 214 us
  waiting for transfers between devices  121 us (56%)
  matrix products  49.7 us (23%)
  starting transfers between devices  31 us (14%)
  other arithmetic  6.61 us (3%)
  local copies, waits for them, and re-layouts  4.99 us (2%)
    ppermute x25, waiting for transfers between devices, shift(): lax.ppermute(value, axis, [(i, (i + by) % devices) for i in range(devices)])  89.9 us
    ppermute x4, waiting for transfers between devices, to_next_owner(): return lax.ppermute(rows, ('pipe', 'ctx'), pairs)  30.9 us
    ppermute x25, starting transfers between devices, shift(): lax.ppermute(value, axis, [(i, (i + by) % devices) for i in range(devices)])  24.3 us
    dot_general x8, matrix products, mixed_halves(): term = jnp.dot(attended, weights[half], preferred_element_type=jnp.float32)  24.3 us
    dot_general x3, matrix products, expert_part(): jnp.dot(slot_rows, in_weight[0, 0], preferred_element_type=jnp.float32)  6.78 us
    ppermute x4, starting transfers between devices, to_next_owner(): return lax.ppermute(rows, ('pipe', 'ctx'), pairs)  6.69 us
    dot_general x4, matrix products, attend_block(): jnp.einsum('hqk,kd->qhd', attention_weights, value_rows, preferred_elemen...  6.19 us
    sub x4, matrix products, attend_block(): attention_weights = jax.nn.softmax(scores, axis=-1).astype(jnp.bfloat16)  5.04 us
  transfers between devices with their start and end apart: 29, of which 13 were waited for; matrix products, arithmetic and copies ran while one was open for 27% of the time, Pallas kernels for 0%

profile of v3, /device:TPU:0, one launch (start us, length us, event | category | flops | bytes accessed | tf_op | source)
XLA Modules:
  0.0 213.9 jit_solution(1973988083340036445)
XLA Ops:
  0.0 0.5 collective-permute-start.6
  0.5 1.0 dynamic-slice_bitcast_fusion.7
  1.4 4.7 %collective-permute-start.2 = (bf16[128,256]{1,0:T(8,128)(2,1)S(1)}, bf16[128,256]{1,0:T(8,128)(2,1)S(1)}, u32[]{:S(2)}, u32[]{:S(2)}) collective-permute-start(bf16[128,256]{1,0:T(8,128)(2,1)S(1)} %pad_maximum_fusion.6), channel_id=1, source_target_pairs={{0,6},{2,0},{4,2},{6,4},{1,7},{3,1},{5,3},{7,5},{8,14},{10,8},{12,... | collective-permute-start | bytes 196616 | tf_op jit(solution)/shard_map/ppermute | solution.py:15
  6.2 1.1 collective-permute-start.1
  7.3 1.3 constant_dynamic-slice_fusion
  8.7 3.4 %collective-permute-start.3 = (bf16[128,1024]{0,1:T(8,128)(2,1)S(1)}, bf16[128,1024]{0,1:T(8,128)(2,1)S(1)}, u32[]{:S(2)}, u32[]{:S(2)}) collective-permute-start(bf16[128,1024]{0,1:T(8,128)(2,1)S(1)} %bitcast.255), channel_id=1, source_target_pairs={{0,2},{2,4},{4,6},{6,0},{1,3},{3,5},{5,7},{7,1},{8,10},{10,12},{12... | collective-permute-start | bytes 786440 | tf_op jit(solution)/shard_map/ppermute | solution.py:15
  13.2 0.9 copy.18
  14.1 5.8 %collective-permute-done.1 = bf16[128,256]{1,0:T(8,128)(2,1)S(1)} collective-permute-done((bf16[128,256]{1,0:T(8,128)(2,1)S(1)}, bf16[128,256]{1,0:T(8,128)(2,1)S(1)}, u32[]{:S(2)}, u32[]{:S(2)}) %collective-permute-start.1) | collective-permute-done | bytes 65568 | tf_op jit(solution)/shard_map/ppermute | solution.py:15
  19.9 0.9 collective-permute-start.4
  20.8 0.6 collective-permute-start.5
  21.4 0.8 fusion.120
  22.2 1.0 convolution_convert_fusion.4
  23.3 2.9 %fusion.102 = bf16[128,2048]{1,0:T(8,128)(2,1)S(1)} fusion(bf16[128,1024]{0,1:T(8,128)(2,1)S(1)} %bitcast.247, bf16[1,1024,2048]{2,1,0:T(8,128)(2,1)} %param.12), kind=kOutput, calls=%fused_computation.179 | convolution fusion | flops 536870912 | bytes 4980736 | tf_op jit(solution)/shard_map/dot_general | solution.py:89
  26.2 1.6 collective-permute-start.7
  27.8 3.7 %fusion.124 = bf16[128,2048]{1,0:T(8,128)(2,1)} fusion(bf16[128,1024]{0,1:T(8,128)(2,1)S(1)} %bitcast.248, bf16[1024,2048]{1,0:T(8,128)(2,1)} %collective-permute-done.6), kind=kOutput, calls=%fused_computation.197 | convolution fusion | flops 536870912 | bytes 4980736 | tf_op jit(solution)/shard_map/dot_general | solution.py:89
  31.5 1.4 collective-permute-start.10
  32.9 27.9 %collective-permute-done.5 = bf16[128,1024]{0,1:T(8,128)(2,1)S(1)} collective-permute-done((bf16[128,1024]{0,1:T(8,128)(2,1)S(1)}, bf16[128,1024]{0,1:T(8,128)(2,1)S(1)}, u32[]{:S(2)}, u32[]{:S(2)}) %collective-permute-start.5) | collective-permute-done | bytes 262176 | tf_op jit(solution)/shard_map/ppermute | solution.py:15
  60.8 0.8 fusion.121
  61.5 1.0 convolution_convert_fusion.3
  62.6 2.9 %fusion.100 = f32[128,2048]{1,0:T(8,128)S(1)} fusion(bf16[128,1024]{0,1:T(8,128)(2,1)S(1)} %bitcast.251, bf16[1,1024,2048]{2,1,0:T(8,128)(2,1)} %param.12), kind=kOutput, calls=%fused_computation.177 | convolution fusion | flops 536870912 | bytes 5505024 | tf_op jit(solution)/shard_map/dot_general | solution.py:89
  65.5 2.9 %fusion.125 = f32[128,2048]{1,0:T(8,128)S(1)} fusion(bf16[128,1024]{0,1:T(8,128)(2,1)S(1)} %bitcast.252, bf16[1024,2048]{1,0:T(8,128)(2,1)} %collective-permute-done.6), kind=kOutput, calls=%fused_computation.198 | convolution fusion | flops 536870912 | bytes 5505024 | tf_op jit(solution)/shard_map/dot_general | solution.py:89
  68.5 1.7 fusion.122
  70.2 2.0 convolution_convert_fusion.2
  72.2 1.9 add_convert_fusion.5
  74.1 2.9 %fusion.98 = f32[128,2048]{1,0:T(8,128)S(1)} fusion(bf16[128,1024]{0,1:T(8,128)(2,1)S(1)} %bitcast.249, bf16[1,1024,2048]{2,1,0:T(8,128)(2,1)} %param.12), kind=kOutput, calls=%fused_computation.175 | convolution fusion | flops 536870912 | bytes 5505024 | tf_op jit(solution)/shard_map/dot_general | solution.py:89
  77.1 2.9 %fusion.126 = f32[128,2048]{1,0:T(8,128)S(1)} fusion(bf16[128,1024]{0,1:T(8,128)(2,1)S(1)} %bitcast.250, bf16[1024,2048]{1,0:T(8,128)(2,1)} %collective-permute-done.6), kind=kOutput, calls=%fused_computation.199 | convolution fusion | flops 536870912 | bytes 5505024 | tf_op jit(solution)/shard_map/dot_general | solution.py:89
  80.0 1.8 fusion.123
  81.8 2.1 convolution_convert_fusion.1
  83.9 1.2 add_convert_fusion.3
  85.3 2.9 %convolution_add_fusion.1 = f32[128,2048]{1,0:T(8,128)S(1)} fusion(bf16[128,1024]{0,1:T(8,128)(2,1)S(1)} %bitcast.245, bf16[1,1,128,4096]{3,2,1,0:T(8,128)(2,1)S(1)} %copy-done.1, s32[]{:T(128)S(6)} %select_n.178, bf16[1,1024,2048]{2,1,0:T(8,128)(2,1)} %param.12), kind=kOutput, calls=%fused_computation.22 | convolution fusion | flops 537395200 | bytes 6029316 | tf_op jit(solution)/shard_map/dot_general | solution.py:89
  88.3 0.6 collective-permute-done.8
  88.9 1.1 add_convert_fusion.4
  90.1 11.8 %collective-permute-done.11 = bf16[128,2048]{1,0:T(8,128)(2,1)S(1)} collective-permute-done((bf16[128,2048]{1,0:T(8,128)(2,1)S(1)}, bf16[128,2048]{1,0:T(8,128)(2,1)S(1)}, u32[]{:S(2)}, u32[]{:S(2)}) %collective-permute-start.11) | collective-permute-done | bytes 524320 | tf_op jit(solution)/shard_map/ppermute | solution.py:15
  102.1 2.9 %convolution_add_fusion = f32[128,2048]{1,0:T(8,128)S(1)} fusion(bf16[128,1024]{0,1:T(8,128)(2,1)S(1)} %bitcast.246, bf16[1024,2048]{1,0:T(8,128)(2,1)} %collective-permute-done.6, bf16[1,1,128,4096]{3,2,1,0:T(8,128)(2,1)S(1)} %copy-done.1, s32[]{:T(128)S(6)} %select_n.179), kind=kOutput, calls=%fused_computation.21 | convolution fusion | flops 537395200 | bytes 6029316 | tf_op jit(solution)/shard_map/dot_general | solution.py:89
  105.0 8.1 %collective-permute-done.9 = bf16[128,2048]{1,0:T(8,128)(2,1)S(1)} collective-permute-done((bf16[128,2048]{1,0:T(8,128)(2,1)S(1)}, bf16[128,2048]{1,0:T(8,128)(2,1)S(1)}, u32[]{:S(2)}, u32[]{:S(2)}) %collective-permute-start.9) | collective-permute-done | bytes 524320 | tf_op jit(solution)/shard_map/ppermute | solution.py:15
  113.3 8.9 %collective-permute-done.12 = bf16[128,2048]{1,0:T(8,128)(2,1)S(1)} collective-permute-done((bf16[128,2048]{1,0:T(8,128)(2,1)S(1)}, bf16[128,2048]{1,0:T(8,128)(2,1)S(1)}, u32[]{:S(2)}, u32[]{:S(2)}) %collective-permute-start.12) | collective-permute-done | bytes 524320 | tf_op jit(solution)/shard_map/ppermute | solution.py:15
  122.3 0.3 multiply_reduce_fusion
  122.7 0.7 convolution_convert_fusion
  123.6 1.5 collective-permute-start.14
  125.1 1.5 collective-permute-start.19
  126.8 1.2 collective-permute-done.14
  128.1 3.8 %collective-permute-start.21 = (bf16[1,48,4096]{2,1,0:T(8,128)(2,1)S(1)}, bf16[1,48,4096]{2,1,0:T(8,128)(2,1)S(1)}, u32[]{:S(2)}, u32[]{:S(2)}) collective-permute-start(bf16[1,48,4096]{2,1,0:T(8,128)(2,1)S(1)} %get-tuple-element.22), channel_id=1, source_target_pairs={{0,6},{2,0},{4,2},{6,4},{1,7},{3,1},{5,3},{7,5},{8,14},{10,8},{12,... | collective-permute-start | bytes 1179656 | tf_op jit(solution)/shard_map/ppermute | solution.py:15
  131.9 5.5 %collective-permute-done.15 = bf16[1,48,4096]{2,1,0:T(8,128)(2,1)S(1)} collective-permute-done((bf16[1,48,4096]{2,1,0:T(8,128)(2,1)S(1)}, bf16[1,48,4096]{2,1,0:T(8,128)(2,1)S(1)}, u32[]{:S(2)}, u32[]{:S(2)}) %collective-permute-start.15) | collective-permute-done | bytes 393248 | tf_op jit(solution)/shard_map/ppermute | solution.py:15
  137.6 5.2 %collective-permute-done.21 = bf16[1,48,4096]{2,1,0:T(8,128)(2,1)S(1)} collective-permute-done((bf16[1,48,4096]{2,1,0:T(8,128)(2,1)S(1)}, bf16[1,48,4096]{2,1,0:T(8,128)(2,1)S(1)}, u32[]{:S(2)}, u32[]{:S(2)}) %collective-permute-start.21) | collective-permute-done | bytes 393248 | tf_op jit(solution)/shard_map/ppermute | solution.py:15
  143.0 1.7 collective-permute-start.13
  144.7 14.8 %collective-permute-done.25 = bf16[1,48,4096]{2,1,0:T(8,128)(2,1)S(1)} collective-permute-done((bf16[1,48,4096]{2,1,0:T(8,128)(2,1)S(1)}, bf16[1,48,4096]{2,1,0:T(8,128)(2,1)S(1)}, u32[]{:S(2)}, u32[]{:S(2)}) %collective-permute-start.25) | collective-permute-done | bytes 393248 | tf_op jit(solution)/shard_map/ppermute | solution.py:15
  159.9 2.6 %fusion.8 = f32[192,1536]{1,0:T(8,128)S(1)} fusion(bf16[192,4096]{1,0:T(8,128)(2,1)S(1)} %bitcast.244, bf16[1,1,4096,1536]{3,2,1,0:T(8,128)(2,1)S(1)} %bitcast.237), kind=kOutput, calls=%fused_computation.8 | convolution fusion | flops 2415919104 | bytes 15335424 | tf_op jit(solution)/shard_map/dot_general | solution.py:173
  162.6 1.4 fusion.14
  164.1 2.1 fusion.6
  166.2 0.6 collective-permute-start.17
  166.8 1.1 fusion.12
  168.0 2.1 fusion.4
  170.2 1.1 fusion.10
  171.4 0.6 collective-permute-start.27
  172.1 0.7 slice-done.5
  173.0 5.0 %collective-permute-start.20 = (bf16[1,48,4096]{2,1,0:T(8,128)(2,1)S(1)}, bf16[1,48,4096]{2,1,0:T(8,128)(2,1)S(1)}, u32[]{:S(2)}, u32[]{:S(2)}) collective-permute-start(bf16[1,48,4096]{2,1,0:T(8,128)(2,1)S(1)} %get-tuple-element.30), channel_id=1, source_target_pairs={{0,14},{2,8},{4,10},{6,12},{8,22},{10,16},{12,18},{14,20},{16,30},... | collective-permute-start | bytes 1179656 | tf_op jit(solution)/shard_map/ppermute | solution.py:200
  178.2 1.5 collective-permute-start.18
  179.7 8.0 %collective-permute-done.24 = bf16[1,48,4096]{2,1,0:T(8,128)(2,1)S(1)} collective-permute-done((bf16[1,48,4096]{2,1,0:T(8,128)(2,1)S(1)}, bf16[1,48,4096]{2,1,0:T(8,128)(2,1)S(1)}, u32[]{:S(2)}, u32[]{:S(2)}) %collective-permute-start.24) | collective-permute-done | bytes 393248 | tf_op jit(solution)/shard_map/ppermute | solution.py:200
  187.7 0.5 convolution_multiply_fusion.1
  188.2 7.8 %collective-permute-done.20 = bf16[1,48,4096]{2,1,0:T(8,128)(2,1)S(1)} collective-permute-done((bf16[1,48,4096]{2,1,0:T(8,128)(2,1)S(1)}, bf16[1,48,4096]{2,1,0:T(8,128)(2,1)S(1)}, u32[]{:S(2)}, u32[]{:S(2)}) %collective-permute-start.20) | collective-permute-done | bytes 393248 | tf_op jit(solution)/shard_map/ppermute | solution.py:200
  196.0 0.5 convolution_multiply_fusion.2
  196.5 15.2 %collective-permute-done.18 = bf16[1,48,4096]{2,1,0:T(8,128)(2,1)S(1)} collective-permute-done((bf16[1,48,4096]{2,1,0:T(8,128)(2,1)S(1)}, bf16[1,48,4096]{2,1,0:T(8,128)(2,1)S(1)}, u32[]{:S(2)}, u32[]{:S(2)}) %collective-permute-start.18) | collective-permute-done | bytes 393248 | tf_op jit(solution)/shard_map/ppermute | solution.py:200
  211.6 0.5 convolution_multiply_fusion.3
  212.1 1.7 fusion.20
  (99 shorter events, 4.0 us)
Async XLA Ops:
  0.0 12.2 %copy-start.3 = (s32[1,1,128,1]{2,3,1,0:T(1,128)S(1)}, s32[1,1,128,1]{2,3,1,0:T(1,128)}, u32[]{:S(2)}) copy-start(s32[1,1,128,1]{2,3,1,0:T(1,128)} %param.16) | copy-start | bytes 1540
  0.0 27.8 %collective-permute-start.6 = (bf16[1024,2048]{1,0:T(8,128)(2,1)}, bf16[1024,2048]{1,0:T(8,128)(2,1)}, u32[]{:S(2)}, u32[]{:S(2)}) collective-permute-start(bf16[1024,2048]{1,0:T(8,128)(2,1)} %bitcast.240), channel_id=1, source_target_pairs={{0,1},{1,0},{2,3},{3,2},{4,5},{5,4},{6,7},{7,6},{8,9},{9,8},{10,11... | collective-permute-start | bytes 12582920 | tf_op jit(solution)/shard_map/ppermute | solution.py:15
  1.4 12.7 %collective-permute-start.2 = (bf16[128,256]{1,0:T(8,128)(2,1)S(1)}, bf16[128,256]{1,0:T(8,128)(2,1)S(1)}, u32[]{:S(2)}, u32[]{:S(2)}) collective-permute-start(bf16[128,256]{1,0:T(8,128)(2,1)S(1)} %pad_maximum_fusion.6), channel_id=1, source_target_pairs={{0,6},{2,0},{4,2},{6,4},{1,7},{3,1},{5,3},{7,5},{8,14},{10,8},{12,... | collective-permute-start | bytes 196616 | tf_op jit(solution)/shard_map/ppermute | solution.py:15
  6.1 7.9 %collective-permute-start = (bf16[128,256]{1,0:T(8,128)(2,1)S(1)}, bf16[128,256]{1,0:T(8,128)(2,1)S(1)}, u32[]{:S(2)}, u32[]{:S(2)}) collective-permute-start(bf16[128,256]{1,0:T(8,128)(2,1)S(1)} %pad_maximum_fusion.4), channel_id=1, source_target_pairs={{0,2},{2,4},{4,6},{6,0},{1,3},{3,5},{5,7},{7,1},{8,10},{10,12},{12... | collective-permute-start | bytes 196616 | tf_op jit(solution)/shard_map/ppermute | solution.py:15
  6.2 13.7 %collective-permute-start.1 = (bf16[128,256]{1,0:T(8,128)(2,1)S(1)}, bf16[128,256]{1,0:T(8,128)(2,1)S(1)}, u32[]{:S(2)}, u32[]{:S(2)}) collective-permute-start(bf16[128,256]{1,0:T(8,128)(2,1)S(1)} %pad_maximum_fusion.5), channel_id=1, source_target_pairs={{0,4},{2,6},{4,0},{6,2},{1,5},{3,7},{5,1},{7,3},{8,12},{10,14},{12... | collective-permute-start | bytes 196616 | tf_op jit(solution)/shard_map/ppermute | solution.py:15
  8.7 11.2 %collective-permute-start.3 = (bf16[128,1024]{0,1:T(8,128)(2,1)S(1)}, bf16[128,1024]{0,1:T(8,128)(2,1)S(1)}, u32[]{:S(2)}, u32[]{:S(2)}) collective-permute-start(bf16[128,1024]{0,1:T(8,128)(2,1)S(1)} %bitcast.255), channel_id=1, source_target_pairs={{0,2},{2,4},{4,6},{6,0},{1,3},{3,5},{5,7},{7,1},{8,10},{10,12},{12... | collective-permute-start | bytes 786440 | tf_op jit(solution)/shard_map/ppermute | solution.py:15
  19.9 50.3 %copy-start.2 = (bf16[512,256]{1,0:T(8,128)(2,1)}, bf16[512,256]{1,0:T(8,128)(2,1)S(1)}, u32[]{:S(2)}) copy-start(bf16[512,256]{1,0:T(8,128)(2,1)S(1)} %pad_maximum_fusion.3) | copy-start | bytes 786436
  19.9 48.5 %collective-permute-start.4 = (bf16[128,1024]{0,1:T(8,128)(2,1)S(1)}, bf16[128,1024]{0,1:T(8,128)(2,1)}, u32[]{:S(2)}, u32[]{:S(2)}) collective-permute-start(bf16[128,1024]{0,1:T(8,128)(2,1)S(1)} %bitcast.258), channel_id=1, source_target_pairs={{0,6},{2,0},{4,2},{6,4},{1,7},{3,1},{5,3},{7,5},{8,14},{10,8},{12,... | collective-permute-start | bytes 786440 | tf_op jit(solution)/shard_map/ppermute | solution.py:15
  20.8 39.9 %collective-permute-start.5 = (bf16[128,1024]{0,1:T(8,128)(2,1)S(1)}, bf16[128,1024]{0,1:T(8,128)(2,1)S(1)}, u32[]{:S(2)}, u32[]{:S(2)}) collective-permute-start(bf16[128,1024]{0,1:T(8,128)(2,1)S(1)} %bitcast.259), channel_id=1, source_target_pairs={{0,4},{2,6},{4,0},{6,2},{1,5},{3,7},{5,1},{7,3},{8,12},{10,14},{12... | collective-permute-start | bytes 786440 | tf_op jit(solution)/shard_map/ppermute | solution.py:15
  26.2 46.0 %collective-permute-start.7 = (bf16[128,2048]{1,0:T(8,128)(2,1)S(1)}, bf16[128,2048]{1,0:T(8,128)(2,1)}, u32[]{:S(2)}, u32[]{:S(2)}) collective-permute-start(bf16[128,2048]{1,0:T(8,128)(2,1)S(1)} %fusion.102), channel_id=1, source_target_pairs={{0,2},{2,4},{4,6},{6,0},{1,3},{3,5},{5,7},{7,1},{8,10},{10,12},{12... | collective-permute-start | bytes 1572872 | tf_op jit(solution)/shard_map/ppermute | solution.py:15
  31.5 52.4 %collective-permute-start.10 = (bf16[128,2048]{1,0:T(8,128)(2,1)}, bf16[128,2048]{1,0:T(8,128)(2,1)}, u32[]{:S(2)}, u32[]{:S(2)}) collective-permute-start(bf16[128,2048]{1,0:T(8,128)(2,1)} %fusion.124), channel_id=1, source_target_pairs={{0,2},{2,4},{4,6},{6,0},{1,3},{3,5},{5,7},{7,1},{8,10},{10,12},{12... | collective-permute-start | bytes 1572872 | tf_op jit(solution)/shard_map/ppermute | solution.py:15
  74.1 14.7 %collective-permute-start.8 = (bf16[128,2048]{1,0:T(8,128)(2,1)}, bf16[128,2048]{1,0:T(8,128)(2,1)}, u32[]{:S(2)}, u32[]{:S(2)}) collective-permute-start(bf16[128,2048]{1,0:T(8,128)(2,1)} %add_convert_fusion.5), channel_id=1, source_target_pairs={{0,2},{2,4},{4,6},{6,0},{1,3},{3,5},{5,7},{7,1},{8,10},{10,12},{12... | collective-permute-start | bytes 1572872 | tf_op jit(solution)/shard_map/ppermute | solution.py:15
  83.9 1.4 copy-start.1
  85.2 16.7 %collective-permute-start.11 = (bf16[128,2048]{1,0:T(8,128)(2,1)S(1)}, bf16[128,2048]{1,0:T(8,128)(2,1)S(1)}, u32[]{:S(2)}, u32[]{:S(2)}) collective-permute-start(bf16[128,2048]{1,0:T(8,128)(2,1)S(1)} %add_convert_fusion.3), channel_id=1, source_target_pairs={{0,2},{2,4},{4,6},{6,0},{1,3},{3,5},{5,7},{7,1},{8,10},{10,12},{12... | collective-permute-start | bytes 1572872 | tf_op jit(solution)/shard_map/ppermute | solution.py:15
  90.0 23.1 %collective-permute-start.9 = (bf16[128,2048]{1,0:T(8,128)(2,1)S(1)}, bf16[128,2048]{1,0:T(8,128)(2,1)S(1)}, u32[]{:S(2)}, u32[]{:S(2)}) collective-permute-start(bf16[128,2048]{1,0:T(8,128)(2,1)S(1)} %add_convert_fusion.4), channel_id=1, source_target_pairs={{0,2},{2,4},{4,6},{6,0},{1,3},{3,5},{5,7},{7,1},{8,10},{10,12},{12... | collective-permute-start | bytes 1572872 | tf_op jit(solution)/shard_map/ppermute | solution.py:15
  102.0 20.2 %collective-permute-start.12 = (bf16[128,2048]{1,0:T(8,128)(2,1)S(1)}, bf16[128,2048]{1,0:T(8,128)(2,1)S(1)}, u32[]{:S(2)}, u32[]{:S(2)}) collective-permute-start(bf16[128,2048]{1,0:T(8,128)(2,1)S(1)} %add_convert_fusion.2), channel_id=1, source_target_pairs={{0,2},{2,4},{4,6},{6,0},{1,3},{3,5},{5,7},{7,1},{8,10},{10,12},{12... | collective-permute-start | bytes 1572872 | tf_op jit(solution)/shard_map/ppermute | solution.py:15
  113.3 9.4 %copy-start.5 = (f32[1,4096]{1,0:T(1,128)S(1)}, f32[1,4096]{1,0:T(1,128)}, u32[]{:S(2)}) copy-start(f32[1,4096]{1,0:T(1,128)} %param.13) | copy-start | bytes 49156
  122.2 37.6 %slice-start = ((s8[12582912]{0:T(1024)(128)(4,1)}), s8[4194304]{0:T(1024)(128)(4,1)S(1)}, s32[]{:S(2)}) async-start(s8[12582912]{0:T(1024)(128)(4,1)} %bitcast.236), calls=%async_computation | async-start | bytes 8388608
  122.6 37.2 %slice-start.1 = ((s8[12582912]{0:T(1024)(128)(4,1)}), s8[4194304]{0:T(1024)(128)(4,1)S(1)}, s32[]{:S(2)}) async-start(s8[12582912]{0:T(1024)(128)(4,1)} %bitcast.236), calls=%async_computation.1 | async-start | bytes 8388608
  123.3 1.8 copy-start.6
  123.5 13.9 %collective-permute-start.15 = (bf16[1,48,4096]{2,1,0:T(8,128)(2,1)S(1)}, bf16[1,48,4096]{2,1,0:T(8,128)(2,1)S(1)}, u32[]{:S(2)}, u32[]{:S(2)}) collective-permute-start(bf16[1,48,4096]{2,1,0:T(8,128)(2,1)S(1)} %get-tuple-element.23), channel_id=1, source_target_pairs={{0,2},{2,4},{4,6},{6,0},{1,3},{3,5},{5,7},{7,1},{8,10},{10,12},{12... | collective-permute-start | bytes 1179656 | tf_op jit(solution)/shard_map/ppermute | solution.py:15
  123.6 4.5 %collective-permute-start.14 = (f32[128,1]{0,1:T(1,128)S(1)}, f32[128,1]{0,1:T(1,128)S(1)}, u32[]{:S(2)}, u32[]{:S(2)}) collective-permute-start(f32[128,1]{0,1:T(1,128)S(1)} %fusion.96), channel_id=1, source_target_pairs={{0,8},{8,16},{16,24},{24,0},{1,9},{9,17},{17,25},{25,1},{2,10},{10... | collective-permute-start | bytes 1544 | tf_op jit(solution)/shard_map/ppermute | solution.py:15
  125.1 53.1 %collective-permute-start.19 = (f32[128,1]{0,1:T(1,128)S(1)}, f32[128,1]{0,1:T(1,128)S(1)}, u32[]{:S(2)}, u32[]{:S(2)}) collective-permute-start(f32[128,1]{0,1:T(1,128)S(1)} %bitcast.271), channel_id=1, source_target_pairs={{0,8},{8,16},{16,24},{24,0},{1,9},{9,17},{17,25},{25,1},{2,10},{10... | collective-permute-start | bytes 1544 | tf_op jit(solution)/shard_map/ppermute | solution.py:15
  126.8 16.1 %copy-start.4 = (s32[192]{0:T(256)}, s32[192]{0:T(256)S(1)}, u32[]{:S(2)}) copy-start(s32[192]{0:T(256)S(1)} %iota.37) | copy-start | bytes 2308
  128.1 14.7 %collective-permute-start.21 = (bf16[1,48,4096]{2,1,0:T(8,128)(2,1)S(1)}, bf16[1,48,4096]{2,1,0:T(8,128)(2,1)S(1)}, u32[]{:S(2)}, u32[]{:S(2)}) collective-permute-start(bf16[1,48,4096]{2,1,0:T(8,128)(2,1)S(1)} %get-tuple-element.22), channel_id=1, source_target_pairs={{0,6},{2,0},{4,2},{6,4},{1,7},{3,1},{5,3},{7,5},{8,14},{10,8},{12,... | collective-permute-start | bytes 1179656 | tf_op jit(solution)/shard_map/ppermute | solution.py:15
  137.4 22.2 %collective-permute-start.25 = (bf16[1,48,4096]{2,1,0:T(8,128)(2,1)S(1)}, bf16[1,48,4096]{2,1,0:T(8,128)(2,1)S(1)}, u32[]{:S(2)}, u32[]{:S(2)}) collective-permute-start(bf16[1,48,4096]{2,1,0:T(8,128)(2,1)S(1)} %get-tuple-element.19), channel_id=1, source_target_pairs={{0,4},{2,6},{4,0},{6,2},{1,5},{3,7},{5,1},{7,3},{8,12},{10,14},{12... | collective-permute-start | bytes 1179656 | tf_op jit(solution)/shard_map/ppermute | solution.py:15
  137.5 22.4 %slice-start.2 = ((s8[12582912]{0:T(1024)(128)(4,1)}), s8[4194304]{0:T(1024)(128)(4,1)S(1)}, s32[]{:S(2)}) async-start(s8[12582912]{0:T(1024)(128)(4,1)} %bitcast.236), calls=%async_computation.2 | async-start | bytes 8388608
  137.5 22.2 %collective-permute-start.16 = (bf16[2,48,4096]{2,1,0:T(8,128)(2,1)S(1)}, bf16[2,48,4096]{2,1,0:T(8,128)(2,1)S(1)}, u32[]{:S(2)}, u32[]{:S(2)}) collective-permute-start(bf16[2,48,4096]{2,1,0:T(8,128)(2,1)S(1)} %maximum_bitcast_fusion), channel_id=1, source_target_pairs={{0,1},{1,0},{2,3},{3,2},{4,5},{5,4},{6,7},{7,6},{8,9},{9,8},{10,11... | collective-permute-start | bytes 2359304 | tf_op jit(solution)/shard_map/ppermute | solution.py:15
  142.8 16.8 %collective-permute-start.22 = (bf16[1,48,4096]{2,1,0:T(8,128)(2,1)S(1)}, bf16[1,48,4096]{2,1,0:T(8,128)(2,1)S(1)}, u32[]{:S(2)}, u32[]{:S(2)}) collective-permute-start(bf16[1,48,4096]{2,1,0:T(8,128)(2,1)S(1)} %collective-permute-done.21), channel_id=1, source_target_pairs={{0,1},{1,0},{2,3},{3,2},{4,5},{5,4},{6,7},{7,6},{8,9},{9,8},{10,11... | collective-permute-start | bytes 1179656 | tf_op jit(solution)/shard_map/ppermute | solution.py:15
  143.0 69.2 %collective-permute-start.13 = (bf16[128,4096]{1,0:T(8,128)(2,1)S(1)}, bf16[128,4096]{1,0:T(8,128)(2,1)S(1)}, u32[]{:S(2)}, u32[]{:S(2)}) collective-permute-start(bf16[128,4096]{1,0:T(8,128)(2,1)S(1)} %fusion.46), channel_id=1, source_target_pairs={{0,8},{8,16},{16,24},{24,0},{1,9},{9,17},{17,25},{25,1},{2,10},{10... | collective-permute-start | bytes 3145736 | tf_op jit(solution)/shard_map/ppermute | solution.py:15
  159.6 8.4 %collective-permute-start.26 = (bf16[1,48,4096]{2,1,0:T(8,128)(2,1)S(1)}, bf16[1,48,4096]{2,1,0:T(8,128)(2,1)S(1)}, u32[]{:S(2)}, u32[]{:S(2)}) collective-permute-start(bf16[1,48,4096]{2,1,0:T(8,128)(2,1)S(1)} %collective-permute-done.25), channel_id=1, source_target_pairs={{0,1},{1,0},{2,3},{3,2},{4,5},{5,4},{6,7},{7,6},{8,9},{9,8},{10,11... | collective-permute-start | bytes 1179656 | tf_op jit(solution)/shard_map/ppermute | solution.py:15
  159.6 2.8 %slice-start.3 = ((s8[6291456]{0:T(1024)(128)(4,1)}), s8[4194304]{0:T(1024)(128)(4,1)S(1)}, s32[]{:S(2)}) async-start(s8[6291456]{0:T(1024)(128)(4,1)} %bitcast.238), calls=%async_computation.3 | async-start | bytes 8388608
  159.8 2.7 %slice-start.4 = ((s8[6291456]{0:T(1024)(128)(4,1)}), s8[2097152]{0:T(1024)(128)(4,1)S(1)}, s32[]{:S(2)}) async-start(s8[6291456]{0:T(1024)(128)(4,1)} %bitcast.238), calls=%async_computation.4 | async-start | bytes 4194304
  164.0 3.9 %copy-start = (f32[192,4096]{1,0:T(8,128)}, f32[192,4096]{1,0:T(8,128)S(1)}, u32[]{:S(2)}) copy-start(f32[192,4096]{1,0:T(8,128)S(1)} %fusion.14) | copy-start | bytes 9437188
  166.2 5.9 %collective-permute-start.17 = (bf16[2,48,4096]{2,1,0:T(8,128)(2,1)S(1)}, bf16[2,48,4096]{2,1,0:T(8,128)(2,1)S(1)}, u32[]{:S(2)}, u32[]{:S(2)}) collective-permute-start(bf16[2,48,4096]{2,1,0:T(8,128)(2,1)S(1)} %bitcast.253), channel_id=1, source_target_pairs={{0,1},{1,0},{2,3},{3,2},{4,5},{5,4},{6,7},{7,6},{8,9},{9,8},{10,11... | collective-permute-start | bytes 2359304 | tf_op jit(solution)/shard_map/ppermute | solution.py:15
  170.1 1.8 collective-permute-start.23
  171.3 1.4 slice-start.5
  171.4 6.7 %collective-permute-start.27 = (bf16[1,48,4096]{2,1,0:T(8,128)(2,1)S(1)}, bf16[1,48,4096]{2,1,0:T(8,128)(2,1)S(1)}, u32[]{:S(2)}, u32[]{:S(2)}) collective-permute-start(bf16[1,48,4096]{2,1,0:T(8,128)(2,1)S(1)} %fusion.41), channel_id=1, source_target_pairs={{0,1},{1,0},{2,3},{3,2},{4,5},{5,4},{6,7},{7,6},{8,9},{9,8},{10,11... | collective-permute-start | bytes 1179656 | tf_op jit(solution)/shard_map/ppermute | solution.py:15
  172.0 15.7 %collective-permute-start.24 = (bf16[1,48,4096]{2,1,0:T(8,128)(2,1)S(1)}, bf16[1,48,4096]{2,1,0:T(8,128)(2,1)S(1)}, u32[]{:S(2)}, u32[]{:S(2)}) collective-permute-start(bf16[1,48,4096]{2,1,0:T(8,128)(2,1)S(1)} %fusion.38), channel_id=1, source_target_pairs={{0,10},{2,12},{4,14},{6,8},{8,18},{10,20},{12,22},{14,16},{16,26},... | collective-permute-start | bytes 1179656 | tf_op jit(solution)/shard_map/ppermute | solution.py:200
  173.0 23.0 %collective-permute-start.20 = (bf16[1,48,4096]{2,1,0:T(8,128)(2,1)S(1)}, bf16[1,48,4096]{2,1,0:T(8,128)(2,1)S(1)}, u32[]{:S(2)}, u32[]{:S(2)}) collective-permute-start(bf16[1,48,4096]{2,1,0:T(8,128)(2,1)S(1)} %get-tuple-element.30), channel_id=1, source_target_pairs={{0,14},{2,8},{4,10},{6,12},{8,22},{10,16},{12,18},{14,20},{16,30},... | collective-permute-start | bytes 1179656 | tf_op jit(solution)/shard_map/ppermute | solution.py:200
  178.1 34.0 %collective-permute-start.28 = (bf16[1,48,4096]{2,1,0:T(8,128)(2,1)S(1)}, bf16[1,48,4096]{2,1,0:T(8,128)(2,1)S(1)}, u32[]{:S(2)}, u32[]{:S(2)}) collective-permute-start(bf16[1,48,4096]{2,1,0:T(8,128)(2,1)S(1)} %fusion.36), channel_id=1, source_target_pairs={{0,12},{2,14},{4,8},{6,10},{8,20},{10,22},{12,16},{14,18},{16,28},... | collective-permute-start | bytes 1179656 | tf_op jit(solution)/shard_map/ppermute | solution.py:200
  178.2 33.4 %collective-permute-start.18 = (bf16[1,48,4096]{2,1,0:T(8,128)(2,1)S(1)}, bf16[1,48,4096]{2,1,0:T(8,128)(2,1)S(1)}, u32[]{:S(2)}, u32[]{:S(2)}) collective-permute-start(bf16[1,48,4096]{2,1,0:T(8,128)(2,1)S(1)} %get-tuple-element.29), channel_id=1, source_target_pairs={{0,8},{2,10},{4,12},{6,14},{8,16},{10,18},{12,20},{14,22},{16,24},... | collective-permute-start | bytes 1179656 | tf_op jit(solution)/shard_map/ppermute | solution.py:200
  187.7 23.9 %slice-start.6 = ((s32[192]{0:T(256)}), s32[48]{0:T(128)S(1)}, s32[]{:S(2)}) async-start(s32[192]{0:T(256)} %copy-done.4), calls=%async_computation.6 | async-start | bytes 1024 | tf_op jit(solution)/shard_map/slice | solution.py:223

commit v4 on v3

--- a/solution.py
+++ b/solution.py
@@ -31,7 +31,7 @@
     return attended.astype(jnp.bfloat16)
 
 
-def mixed_halves(queries, keys_values, residual, out_weight):
+def mixed_halves(queries, keys_values, residual, out_weight, finish):
     contexts, exps = lax.axis_size("ctx"), lax.axis_size("exp")
     me, my_exp = lax.axis_index("ctx"), lax.axis_index("exp")
     rows = queries.shape[0]
@@ -74,9 +74,11 @@
     origins = [(me - k) % contexts * rows for k in range(contexts)]
     col_ids = jnp.concatenate([origin + within for origin in origins])
 
-    held, terms = [None, None], []
+    held, sent = [None, None], []
     for k in [*range(1, contexts), 0]:
-        block = blocks[k] if k == 1 else after(blocks[k], *terms)
+        block = blocks[k] if k == 1 else after(blocks[k], *sent)
+        if k == 0:
+            block = after(block, finish)
         attended = attend_block(
             block.reshape(rows, local_heads, HEAD_SIZE),
             key_rows,
@@ -84,7 +86,7 @@
             origins[k] + within,
             col_ids,
         ).reshape(rows, group_width)
-        terms = []
+        terms, sent = [], []
         for half in range(2):
             term = jnp.dot(attended, weights[half], preferred_element_type=jnp.float32)
             if k == 0:
@@ -95,7 +97,11 @@
             term = terms[half]
             if held[half] is not None:
                 term = term + held[half].astype(jnp.float32)
-            held[half] = term if k == 0 else shift(term.astype(jnp.bfloat16), "ctx", 1)
+            if k == 0:
+                held[half] = term
+            else:
+                sent.append(term.astype(jnp.bfloat16))
+                held[half] = shift(sent[half], "ctx", 1)
     return held, first
 
 
@@ -114,16 +120,6 @@
     me, my_exp = lax.axis_index("ctx"), lax.axis_index("exp")
     token_rows = queries.shape[2]
     model_width = residual.shape[3]
-    halves, first = mixed_halves(
-        queries[0, 0], rotated_keys_values[0, 0], residual[0, 0], out_weight[0]
-    )
-    mixed_rows = jnp.concatenate(halves, axis=1)
-    if exps == 2:
-        mixed_rows = jnp.where(first == 0, mixed_rows, jnp.concatenate(halves[::-1], axis=1))
-
-    mean_square = jnp.mean(mixed_rows * mixed_rows, axis=-1, keepdims=True)
-    normed = (mixed_rows * lax.rsqrt(mean_square + 1e-06) * norm_gain[0]).astype(jnp.bfloat16)
-
     route_count = routes.shape[3]
     group_size = min(4, exps)
     per_context = exps // group_size
@@ -150,8 +146,20 @@
         (slot_ids[:, None] == slot_index[None, :, r]).astype(jnp.bfloat16)
         for r in range(route_count)
     )
-    next_slots = shift(slot_index.astype(jnp.float32), "pipe", 1).astype(jnp.int32)
-    next_weights = shift(route_weight[0, 0], "pipe", 1)
+    finish = jnp.concatenate([slot_index.astype(jnp.float32).T, route_weight[0, 0].T], axis=0)
+    finish = shift(finish, "pipe", 1)
+    next_slots = finish[:route_count].astype(jnp.int32)
+    next_weights = finish[route_count:]
+
+    halves, first = mixed_halves(
+        queries[0, 0], rotated_keys_values[0, 0], residual[0, 0], out_weight[0], finish
+    )
+    mixed_rows = jnp.concatenate(halves, axis=1)
+    if exps == 2:
+        mixed_rows = jnp.where(first == 0, mixed_rows, jnp.concatenate(halves[::-1], axis=1))
+
+    mean_square = jnp.mean(mixed_rows * mixed_rows, axis=-1, keepdims=True)
+    normed = (mixed_rows * lax.rsqrt(mean_square + 1e-06) * norm_gain[0]).astype(jnp.bfloat16)
     next_mixed = shift(mixed_rows.astype(jnp.bfloat16), "pipe", 1)
     packed = jnp.dot(slot_match, normed, preferred_element_type=jnp.float32).astype(jnp.bfloat16)
     packed = packed.reshape(contexts, per_context, capacity, model_width)
@@ -199,33 +207,34 @@
         ]
         return lax.ppermute(rows, ("pipe", "ctx"), pairs)
 
-    order = sorted(range(1, contexts), key=lambda k: min(k, contexts - k))
-    groups = [[0, order[0]]] + [[k] for k in order[1:]]
+    order = list(range(1, contexts))
+    groups = [[0, *order[:-1]], order[-1:]]
     arrived, returned = {0: packed[0]}, {}
-    for place, k in enumerate(order):
+    for k in order:
         rows = packed[k]
-        if place >= 2:
-            rows = after(rows, arrived[order[place - 2]])
+        if k == order[-1]:
+            rows = after(rows, arrived[order[0]])
         arrived[k] = shift(rows, "ctx", k)
-    part = None
+    total = None
     for group in groups:
-        slot_rows = exchange(jnp.stack([arrived[k] for k in group], axis=0))
-        if part is not None:
-            slot_rows = after(slot_rows, part)
-        part = expert_part(slot_rows)
-        total = summed(part, len(group))
+        rows = jnp.stack([arrived[k] for k in group], axis=0)
+        if total is not None:
+            rows = after(rows, total, next_mixed)
+        total = summed(expert_part(exchange(rows)), len(group))
         for i, k in enumerate(group):
             returned[k] = to_next_owner(total[i], k)
 
     layer = next_mixed.astype(jnp.float32)
     width = per_context * capacity
     for k in [0, *order]:
+        if k == order[-1]:
+            layer = lax.optimization_barrier(layer)
         ids = slot_ids[k * width : (k + 1) * width]
         rows = returned[k].reshape(width, model_width)
         for r in range(route_count):
-            match = (ids[None, :] == next_slots[:, r, None]).astype(jnp.bfloat16)
+            match = (ids[None, :] == next_slots[r, :, None]).astype(jnp.bfloat16)
             picked = jnp.dot(match, rows, preferred_element_type=jnp.float32)
-            layer = layer + picked * next_weights[:, r, None]
+            layer = layer + picked * next_weights[r, :, None]
     return layer.astype(jnp.bfloat16).reshape(1, 1, token_rows, model_width)
 
 

time: 215 us -> 213 us (level)
  waiting for transfers between devices: 121 us -> 134 us
  starting transfers between devices: 31 us -> 20.8 us
    ppermute x25 -> x22, waiting for transfers between devices: 89.9 us -> 101 us  [shift(): lax.ppermute(value, axis, [(i, (i + by) % devices) for i in range(devices)])]
    ppermute x25 -> x22, starting transfers between devices: 24.3 us -> 16.5 us  [shift(): lax.ppermute(value, axis, [(i, (i + by) % devices) for i in range(devices)])]
    convert_element_type x4, other arithmetic: 4.44 us -> 1.54 us  [mixed_halves(): sent.append(term.astype(jnp.bfloat16))]
    ppermute x4, starting transfers between devices: 6.69 us -> 4.28 us  [to_next_owner(): return lax.ppermute(rows, ('pipe', 'ctx'), pairs)]
    dot_general x3 -> x2, matrix products: 6.78 us -> 5.98 us  [expert_part(): jnp.dot(slot_rows, in_weight[0, 0], preferred_element_type=jnp.float32)]
  transfers between devices with their start and end apart: 29 -> 26, of which waited for: 13 -> 15; matrix products, arithmetic and copies ran while one was open for 27% -> 25% of each run, Pallas kernels for 0% -> 0%
where the time goes in v4:
time: 213 us; the launch traced here: 212 us
  waiting for transfers between devices  134 us (63%)
  matrix products  47.6 us (22%)
  starting transfers between devices  20.8 us (10%)
  other arithmetic  5.67 us (3%)
  local copies, waits for them, and re-layouts  3.69 us (2%)
    ppermute x22, waiting for transfers between devices, shift(): lax.ppermute(value, axis, [(i, (i + by) % devices) for i in range(devices)])  101 us
    ppermute x4, waiting for transfers between devices, to_next_owner(): return lax.ppermute(rows, ('pipe', 'ctx'), pairs)  32.8 us
    dot_general x8, matrix products, mixed_halves(): term = jnp.dot(attended, weights[half], preferred_element_type=jnp.float32)  23.5 us
    ppermute x22, starting transfers between devices, shift(): lax.ppermute(value, axis, [(i, (i + by) % devices) for i in range(devices)])  16.5 us
    dot_general x4, matrix products, attend_block(): jnp.einsum('hqk,kd->qhd', attention_weights, value_rows, preferred_elemen...  7.23 us
    dot_general x2, matrix products, expert_part(): jnp.dot(slot_rows, in_weight[0, 0], preferred_element_type=jnp.float32)  5.98 us
    sub x4, matrix products, attend_block(): attention_weights = jax.nn.softmax(scores, axis=-1).astype(jnp.bfloat16)  4.97 us
    ppermute x4, starting transfers between devices, to_next_owner(): return lax.ppermute(rows, ('pipe', 'ctx'), pairs)  4.28 us
  transfers between devices with their start and end apart: 26, of which 15 were waited for; matrix products, arithmetic and copies ran while one was open for 25% of the time, Pallas kernels for 0%

profile of v4, /device:TPU:0, one launch (start us, length us, event | category | flops | bytes accessed | tf_op | source)
XLA Modules:
  0.0 212.2 jit_solution(986549252645948935)
XLA Ops:
  0.0 0.5 collective-permute-start.6
  0.5 1.3 constant_dynamic-slice_fusion
  1.9 2.7 %collective-permute-start.3 = (bf16[128,1024]{0,1:T(8,128)(2,1)S(1)}, bf16[128,1024]{0,1:T(8,128)(2,1)S(1)}, u32[]{:S(2)}, u32[]{:S(2)}) collective-permute-start(bf16[128,1024]{0,1:T(8,128)(2,1)S(1)} %bitcast.245), channel_id=1, source_target_pairs={{0,2},{2,4},{4,6},{6,0},{1,3},{3,5},{5,7},{7,1},{8,10},{10,12},{12... | collective-permute-start | bytes 786440 | tf_op jit(solution)/shard_map/ppermute | solution.py:15
  4.7 2.2 %collective-permute-start.2 = (bf16[128,256]{1,0:T(8,128)(2,1)S(1)}, bf16[128,256]{1,0:T(8,128)(2,1)S(1)}, u32[]{:S(2)}, u32[]{:S(2)}) collective-permute-start(bf16[128,256]{1,0:T(8,128)(2,1)S(1)} %pad_maximum_fusion.5), channel_id=1, source_target_pairs={{0,6},{2,0},{4,2},{6,4},{1,7},{3,1},{5,3},{7,5},{8,14},{10,8},{12,... | collective-permute-start | bytes 196616 | tf_op jit(solution)/shard_map/ppermute | solution.py:15
  6.9 0.9 collective-permute-start.1
  7.9 1.6 collective-permute-start
  10.0 0.9 broadcast_compare_fusion
  11.2 0.2 copy.21
  11.4 3.1 %collective-permute-done.2 = bf16[128,256]{1,0:T(8,128)(2,1)S(1)} collective-permute-done((bf16[128,256]{1,0:T(8,128)(2,1)S(1)}, bf16[128,256]{1,0:T(8,128)(2,1)S(1)}, u32[]{:S(2)}, u32[]{:S(2)}) %collective-permute-start.2) | collective-permute-done | bytes 65568 | tf_op jit(solution)/shard_map/ppermute | solution.py:15
  14.5 1.5 collective-permute-start.11
  16.0 3.2 %collective-permute-done.1 = bf16[128,256]{1,0:T(8,128)(2,1)S(1)} collective-permute-done((bf16[128,256]{1,0:T(8,128)(2,1)S(1)}, bf16[128,256]{1,0:T(8,128)(2,1)S(1)}, u32[]{:S(2)}, u32[]{:S(2)}) %collective-permute-start.1) | collective-permute-done | bytes 65568 | tf_op jit(solution)/shard_map/ppermute | solution.py:15
  19.2 0.7 collective-permute-start.4
  20.1 0.8 fusion.109
  20.8 1.0 convolution_convert_fusion.4
  21.9 2.9 %fusion.92 = bf16[128,2048]{1,0:T(8,128)(2,1)S(1)} fusion(bf16[128,1024]{0,1:T(8,128)(2,1)S(1)} %bitcast.235, bf16[1,1024,2048]{2,1,0:T(8,128)(2,1)} %param.12), kind=kOutput, calls=%fused_computation.169 | convolution fusion | flops 536870912 | bytes 4980736 | tf_op jit(solution)/shard_map/dot_general | solution.py:91
  24.8 2.0 collective-permute-start.7
  26.8 2.9 %fusion.113 = bf16[128,2048]{1,0:T(8,128)(2,1)S(1)} fusion(bf16[128,1024]{0,1:T(8,128)(2,1)S(1)} %bitcast.236, bf16[1024,2048]{1,0:T(8,128)(2,1)} %collective-permute-done.6), kind=kOutput, calls=%fused_computation.186 | convolution fusion | flops 536870912 | bytes 4980736 | tf_op jit(solution)/shard_map/dot_general | solution.py:91
  29.8 1.5 collective-permute-start.8
  31.2 28.7 %collective-permute-done.5 = bf16[128,1024]{0,1:T(8,128)(2,1)} collective-permute-done((bf16[128,1024]{0,1:T(8,128)(2,1)S(1)}, bf16[128,1024]{0,1:T(8,128)(2,1)}, u32[]{:S(2)}, u32[]{:S(2)}) %collective-permute-start.5) | collective-permute-done | bytes 262176 | tf_op jit(solution)/shard_map/ppermute | solution.py:15
  59.9 1.7 fusion.110
  61.6 2.0 convolution_convert_fusion.3
  63.6 2.9 %fusion.90 = f32[128,2048]{1,0:T(8,128)S(1)} fusion(bf16[128,1024]{0,1:T(8,128)(2,1)S(1)} %bitcast.239, bf16[1,1024,2048]{2,1,0:T(8,128)(2,1)} %param.12), kind=kOutput, calls=%fused_computation.167 | convolution fusion | flops 536870912 | bytes 5505024 | tf_op jit(solution)/shard_map/dot_general | solution.py:91
  66.6 2.9 %fusion.114 = f32[128,2048]{1,0:T(8,128)S(1)} fusion(bf16[128,1024]{0,1:T(8,128)(2,1)S(1)} %bitcast.240, bf16[1024,2048]{1,0:T(8,128)(2,1)} %collective-permute-done.6), kind=kOutput, calls=%fused_computation.187 | convolution fusion | flops 536870912 | bytes 5505024 | tf_op jit(solution)/shard_map/dot_general | solution.py:91
  69.9 1.7 fusion.111
  71.6 2.0 convolution_convert_fusion.2
  73.6 2.9 %fusion.88 = f32[128,2048]{1,0:T(8,128)S(1)} fusion(bf16[128,1024]{0,1:T(8,128)(2,1)S(1)} %bitcast.241, bf16[1,1024,2048]{2,1,0:T(8,128)(2,1)} %param.12), kind=kOutput, calls=%fused_computation.165 | convolution fusion | flops 536870912 | bytes 5505024 | tf_op jit(solution)/shard_map/dot_general | solution.py:91
  76.6 2.9 %fusion.115 = f32[128,2048]{1,0:T(8,128)S(1)} fusion(bf16[128,1024]{0,1:T(8,128)(2,1)S(1)} %bitcast.242, bf16[1024,2048]{1,0:T(8,128)(2,1)} %collective-permute-done.6), kind=kOutput, calls=%fused_computation.188 | convolution fusion | flops 536870912 | bytes 5505024 | tf_op jit(solution)/shard_map/dot_general | solution.py:91
  79.5 6.8 %collective-permute-done.9 = bf16[128,2048]{1,0:T(8,128)(2,1)S(1)} collective-permute-done((bf16[128,2048]{1,0:T(8,128)(2,1)S(1)}, bf16[128,2048]{1,0:T(8,128)(2,1)S(1)}, u32[]{:S(2)}, u32[]{:S(2)}) %collective-permute-start.9) | collective-permute-done | bytes 524320 | tf_op jit(solution)/shard_map/ppermute | solution.py:15
  86.5 0.2 collective-permute-start.12
  86.7 11.0 %collective-permute-done.10 = bf16[128,2048]{1,0:T(8,128)(2,1)} collective-permute-done((bf16[128,2048]{1,0:T(8,128)(2,1)S(1)}, bf16[128,2048]{1,0:T(8,128)(2,1)}, u32[]{:S(2)}, u32[]{:S(2)}) %collective-permute-start.10) | collective-permute-done | bytes 524320 | tf_op jit(solution)/shard_map/ppermute | solution.py:15
  97.7 1.2 add_convert_fusion.2
  99.0 0.8 fusion.112
  99.7 2.2 %convolution_convert_fusion.1 = bf16[128,8,128]{2,0,1:T(8,128)(2,1)S(1)} fusion(f32[8,128]{1,0:T(8,128)S(1)} %fusion.112, bf16[512,256]{1,0:T(8,128)(2,1)} %copy-done.3, pred[128,512]{0,1:T(8,128)(4,1)S(1)} %get-tuple-element.43, bf16[128,8,128]{0,2,1:T(8,128)(2,1)} %bitcast.247), kind=kOutput, calls=%fused_computation.43 | convolution fusion | flops 271189504 | bytes 856064 | tf_op jit(solution)/shard_map/hqk,kd->qhd/dot_general | solution.py:28
  102.0 2.9 %convolution_add_fusion.1 = f32[128,2048]{1,0:T(8,128)S(1)} fusion(bf16[128,1024]{0,1:T(8,128)(2,1)S(1)} %bitcast.237, bf16[1,1,128,4096]{3,2,1,0:T(8,128)(2,1)S(1)} %copy-done, s32[]{:T(128)S(6)} %select_n.181, bf16[1,1024,2048]{2,1,0:T(8,128)(2,1)} %param.12), kind=kOutput, calls=%fused_computation.18 | convolution fusion | flops 537395200 | bytes 6029316 | tf_op jit(solution)/shard_map/dot_general | solution.py:91
  104.9 2.9 %convolution_add_fusion = f32[128,2048]{1,0:T(8,128)S(1)} fusion(bf16[128,1024]{0,1:T(8,128)(2,1)S(1)} %bitcast.238, bf16[1024,2048]{1,0:T(8,128)(2,1)} %collective-permute-done.6, bf16[1,1,128,4096]{3,2,1,0:T(8,128)(2,1)S(1)} %copy-done, s32[]{:T(128)S(6)} %select_n.182), kind=kOutput, calls=%fused_computation.17 | convolution fusion | flops 537395200 | bytes 6029316 | tf_op jit(solution)/shard_map/dot_general | solution.py:91
  107.9 1.0 collective-permute-done.12
  108.9 9.1 %collective-permute-done.13 = bf16[128,2048]{1,0:T(8,128)(2,1)S(1)} collective-permute-done((bf16[128,2048]{1,0:T(8,128)(2,1)S(1)}, bf16[128,2048]{1,0:T(8,128)(2,1)S(1)}, u32[]{:S(2)}, u32[]{:S(2)}) %collective-permute-start.13) | collective-permute-done | bytes 524320 | tf_op jit(solution)/shard_map/ppermute | solution.py:15
  118.2 0.3 multiply_reduce_fusion
  118.5 0.2 fusion.41
  118.8 1.5 collective-permute-start.14
  120.3 0.7 convolution_convert_fusion
  121.2 13.3 %collective-permute-done.15 = bf16[1,48,4096]{2,1,0:T(8,128)(2,1)S(1)} collective-permute-done((bf16[1,48,4096]{2,1,0:T(8,128)(2,1)S(1)}, bf16[1,48,4096]{2,1,0:T(8,128)(2,1)S(1)}, u32[]{:S(2)}, u32[]{:S(2)}) %collective-permute-start.15) | collective-permute-done | bytes 393248 | tf_op jit(solution)/shard_map/ppermute | solution.py:15
  134.4 8.4 %collective-permute-done.22 = bf16[1,48,4096]{2,1,0:T(8,128)(2,1)S(1)} collective-permute-done((bf16[1,48,4096]{2,1,0:T(8,128)(2,1)S(1)}, bf16[1,48,4096]{2,1,0:T(8,128)(2,1)S(1)}, u32[]{:S(2)}, u32[]{:S(2)}) %collective-permute-start.22) | collective-permute-done | bytes 393248 | tf_op jit(solution)/shard_map/ppermute | solution.py:15
  142.9 14.4 %collective-permute-done.16 = bf16[1,48,4096]{2,1,0:T(8,128)(2,1)S(1)} collective-permute-done((bf16[1,48,4096]{2,1,0:T(8,128)(2,1)S(1)}, bf16[1,48,4096]{2,1,0:T(8,128)(2,1)S(1)}, u32[]{:S(2)}, u32[]{:S(2)}) %collective-permute-start.16) | collective-permute-done | bytes 393248 | tf_op jit(solution)/shard_map/ppermute | solution.py:15
  157.6 2.1 fusion.4
  159.8 0.6 slice-done.4
  160.4 1.1 fusion.8
  161.6 0.5 collective-permute-start.24
  162.1 0.2 pad_maximum_fusion
  162.3 3.9 %fusion.6 = f32[288,1536]{1,0:T(8,128)S(1)} fusion(bf16[288,4096]{1,0:T(8,128)(2,1)S(1)} %bitcast.233, bf16[1,1,4096,1536]{3,2,1,0:T(8,128)(2,1)S(1)} %bitcast.228), kind=kOutput, calls=%fused_computation.6 | convolution fusion | flops 3623878656 | bytes 16711680 | tf_op jit(solution)/shard_map/dot_general | solution.py:181
  166.2 2.1 fusion.10
  168.9 0.2 copy-done.6
  169.3 2.0 collective-permute-done.18
  171.3 0.3 add_convert_fusion
  171.7 3.7 %collective-permute-start.20 = (bf16[1,48,4096]{2,1,0:T(8,128)(2,1)S(1)}, bf16[1,48,4096]{2,1,0:T(8,128)(2,1)S(1)}, u32[]{:S(2)}, u32[]{:S(2)}) collective-permute-start(bf16[1,48,4096]{2,1,0:T(8,128)(2,1)S(1)} %get-tuple-element.26), channel_id=1, source_target_pairs={{0,14},{2,8},{4,10},{6,12},{8,22},{10,16},{12,18},{14,20},{16,30},... | collective-permute-start | bytes 1179656 | tf_op jit(solution)/shard_map/ppermute | solution.py:208
  175.4 0.5 collective-permute-start.19
  175.9 9.1 %collective-permute-done.25 = bf16[1,48,4096]{2,1,0:T(8,128)(2,1)S(1)} collective-permute-done((bf16[1,48,4096]{2,1,0:T(8,128)(2,1)S(1)}, bf16[1,48,4096]{2,1,0:T(8,128)(2,1)S(1)}, u32[]{:S(2)}, u32[]{:S(2)}) %collective-permute-start.25) | collective-permute-done | bytes 393248 | tf_op jit(solution)/shard_map/ppermute | solution.py:208
  185.0 0.5 convolution_multiply_fusion
  185.6 8.8 %collective-permute-done.20 = bf16[1,48,4096]{2,1,0:T(8,128)(2,1)S(1)} collective-permute-done((bf16[1,48,4096]{2,1,0:T(8,128)(2,1)S(1)}, bf16[1,48,4096]{2,1,0:T(8,128)(2,1)S(1)}, u32[]{:S(2)}, u32[]{:S(2)}) %collective-permute-start.20) | collective-permute-done | bytes 393248 | tf_op jit(solution)/shard_map/ppermute | solution.py:208
  194.4 0.5 convolution_multiply_fusion.2
  194.8 14.9 %collective-permute-done.19 = bf16[1,48,4096]{2,1,0:T(8,128)(2,1)S(1)} collective-permute-done((bf16[1,48,4096]{2,1,0:T(8,128)(2,1)S(1)}, bf16[1,48,4096]{2,1,0:T(8,128)(2,1)S(1)}, u32[]{:S(2)}, u32[]{:S(2)}) %collective-permute-start.19) | collective-permute-done | bytes 393248 | tf_op jit(solution)/shard_map/ppermute | solution.py:208
  209.8 0.5 convolution_multiply_fusion.3
  210.3 0.7 add_add_fusion
  211.0 1.2 fusion.16
  (93 shorter events, 3.6 us)
Async XLA Ops:
  0.0 4.6 %copy-start.1 = (bf16[1,1,128,512]{3,2,1,0:T(8,128)(2,1)S(1)}, bf16[1,1,128,512]{3,2,1,0:T(8,128)(2,1)}, u32[]{:S(2)}) copy-start(bf16[1,1,128,512]{3,2,1,0:T(8,128)(2,1)} %param.10) | copy-start | bytes 393220
  0.0 9.5 %copy-start.5 = (s32[1,1,128,1]{2,3,1,0:T(1,128)S(1)}, s32[1,1,128,1]{2,3,1,0:T(1,128)}, u32[]{:S(2)}) copy-start(s32[1,1,128,1]{2,3,1,0:T(1,128)} %param.16) | copy-start | bytes 1540
  0.0 26.8 %collective-permute-start.6 = (bf16[1024,2048]{1,0:T(8,128)(2,1)}, bf16[1024,2048]{1,0:T(8,128)(2,1)}, u32[]{:S(2)}, u32[]{:S(2)}) collective-permute-start(bf16[1024,2048]{1,0:T(8,128)(2,1)} %bitcast.226), channel_id=1, source_target_pairs={{0,1},{1,0},{2,3},{3,2},{4,5},{5,4},{6,7},{7,6},{8,9},{9,8},{10,11... | collective-permute-start | bytes 12582920 | tf_op jit(solution)/shard_map/ppermute | solution.py:15
  1.7 9.7 %copy-start.7 = (f32[1,1,128,1]{2,3,1,0:T(1,128)S(1)}, f32[1,1,128,1]{2,3,1,0:T(1,128)}, u32[]{:S(2)}) copy-start(f32[1,1,128,1]{2,3,1,0:T(1,128)} %param.17) | copy-start | bytes 1540
  1.9 17.3 %collective-permute-start.3 = (bf16[128,1024]{0,1:T(8,128)(2,1)S(1)}, bf16[128,1024]{0,1:T(8,128)(2,1)S(1)}, u32[]{:S(2)}, u32[]{:S(2)}) collective-permute-start(bf16[128,1024]{0,1:T(8,128)(2,1)S(1)} %bitcast.245), channel_id=1, source_target_pairs={{0,2},{2,4},{4,6},{6,0},{1,3},{3,5},{5,7},{7,1},{8,10},{10,12},{12... | collective-permute-start | bytes 786440 | tf_op jit(solution)/shard_map/ppermute | solution.py:15
  4.7 9.8 %collective-permute-start.2 = (bf16[128,256]{1,0:T(8,128)(2,1)S(1)}, bf16[128,256]{1,0:T(8,128)(2,1)S(1)}, u32[]{:S(2)}, u32[]{:S(2)}) collective-permute-start(bf16[128,256]{1,0:T(8,128)(2,1)S(1)} %pad_maximum_fusion.5), channel_id=1, source_target_pairs={{0,6},{2,0},{4,2},{6,4},{1,7},{3,1},{5,3},{7,5},{8,14},{10,8},{12,... | collective-permute-start | bytes 196616 | tf_op jit(solution)/shard_map/ppermute | solution.py:15
  6.9 12.2 %collective-permute-start.1 = (bf16[128,256]{1,0:T(8,128)(2,1)S(1)}, bf16[128,256]{1,0:T(8,128)(2,1)S(1)}, u32[]{:S(2)}, u32[]{:S(2)}) collective-permute-start(bf16[128,256]{1,0:T(8,128)(2,1)S(1)} %pad_maximum_fusion.4), channel_id=1, source_target_pairs={{0,4},{2,6},{4,0},{6,2},{1,5},{3,7},{5,1},{7,3},{8,12},{10,14},{12... | collective-permute-start | bytes 196616 | tf_op jit(solution)/shard_map/ppermute | solution.py:15
  7.9 11.3 %collective-permute-start = (bf16[128,256]{1,0:T(8,128)(2,1)S(1)}, bf16[128,256]{1,0:T(8,128)(2,1)S(1)}, u32[]{:S(2)}, u32[]{:S(2)}) collective-permute-start(bf16[128,256]{1,0:T(8,128)(2,1)S(1)} %pad_maximum_fusion.3), channel_id=1, source_target_pairs={{0,2},{2,4},{4,6},{6,0},{1,3},{3,5},{5,7},{7,1},{8,10},{10,12},{12... | collective-permute-start | bytes 196616 | tf_op jit(solution)/shard_map/ppermute | solution.py:15
  11.1 87.9 %copy-start.2 = (bf16[1,1,128,1024]{2,3,1,0:T(8,128)(2,1)}, bf16[1,1,128,1024]{2,3,1,0:T(8,128)(2,1)S(1)}, u32[]{:S(2)}) copy-start(bf16[1,1,128,1024]{2,3,1,0:T(8,128)(2,1)S(1)} %copy.18) | copy-start | bytes 786436
  14.5 84.4 %collective-permute-start.11 = (f32[2,128]{1,0:T(2,128)S(1)}, f32[2,128]{1,0:T(2,128)S(1)}, u32[]{:S(2)}, u32[]{:S(2)}) collective-permute-start(f32[2,128]{1,0:T(2,128)S(1)} %pad_maximum_fusion.6), channel_id=1, source_target_pairs={{0,8},{8,16},{16,24},{24,0},{1,9},{9,17},{17,25},{25,1},{2,10},{10... | collective-permute-start | bytes 3080 | tf_op jit(solution)/shard_map/ppermute | solution.py:15
  19.2 79.8 %copy-start.3 = (bf16[512,256]{1,0:T(8,128)(2,1)}, bf16[512,256]{1,0:T(8,128)(2,1)S(1)}, u32[]{:S(2)}) copy-start(bf16[512,256]{1,0:T(8,128)(2,1)S(1)} %pad_maximum_fusion.2) | copy-start | bytes 786436
  19.2 50.7 %collective-permute-start.4 = (bf16[128,1024]{0,1:T(8,128)(2,1)S(1)}, bf16[128,1024]{0,1:T(8,128)(2,1)}, u32[]{:S(2)}, u32[]{:S(2)}) collective-permute-start(bf16[128,1024]{0,1:T(8,128)(2,1)S(1)} %bitcast.248), channel_id=1, source_target_pairs={{0,6},{2,0},{4,2},{6,4},{1,7},{3,1},{5,3},{7,5},{8,14},{10,8},{12,... | collective-permute-start | bytes 786440 | tf_op jit(solution)/shard_map/ppermute | solution.py:15
  19.9 40.0 %collective-permute-start.5 = (bf16[128,1024]{0,1:T(8,128)(2,1)S(1)}, bf16[128,1024]{0,1:T(8,128)(2,1)}, u32[]{:S(2)}, u32[]{:S(2)}) collective-permute-start(bf16[128,1024]{0,1:T(8,128)(2,1)S(1)} %bitcast.249), channel_id=1, source_target_pairs={{0,4},{2,6},{4,0},{6,2},{1,5},{3,7},{5,1},{7,3},{8,12},{10,14},{12... | collective-permute-start | bytes 786440 | tf_op jit(solution)/shard_map/ppermute | solution.py:15
  24.8 35.1 %copy-start.4 = (pred[128,512]{0,1:T(8,128)(4,1)S(1)}, pred[128,512]{0,1:T(8,128)(4,1)}, u32[]{:S(2)}) copy-start(pred[128,512]{0,1:T(8,128)(4,1)} %get-tuple-element.42) | copy-start | bytes 196612
  24.8 44.7 %collective-permute-start.7 = (bf16[128,2048]{1,0:T(8,128)(2,1)S(1)}, bf16[128,2048]{1,0:T(8,128)(2,1)S(1)}, u32[]{:S(2)}, u32[]{:S(2)}) collective-permute-start(bf16[128,2048]{1,0:T(8,128)(2,1)S(1)} %fusion.92), channel_id=1, source_target_pairs={{0,2},{2,4},{4,6},{6,0},{1,3},{3,5},{5,7},{7,1},{8,10},{10,12},{12... | collective-permute-start | bytes 1572872 | tf_op jit(solution)/shard_map/ppermute | solution.py:15
  29.8 40.0 %collective-permute-start.8 = (bf16[128,2048]{1,0:T(8,128)(2,1)S(1)}, bf16[128,2048]{1,0:T(8,128)(2,1)S(1)}, u32[]{:S(2)}, u32[]{:S(2)}) collective-permute-start(bf16[128,2048]{1,0:T(8,128)(2,1)S(1)} %fusion.113), channel_id=1, source_target_pairs={{0,2},{2,4},{4,6},{6,0},{1,3},{3,5},{5,7},{7,1},{8,10},{10,12},{12... | collective-permute-start | bytes 1572872 | tf_op jit(solution)/shard_map/ppermute | solution.py:15
  69.6 16.7 %collective-permute-start.9 = (bf16[128,2048]{1,0:T(8,128)(2,1)S(1)}, bf16[128,2048]{1,0:T(8,128)(2,1)S(1)}, u32[]{:S(2)}, u32[]{:S(2)}) collective-permute-start(bf16[128,2048]{1,0:T(8,128)(2,1)S(1)} %add_convert_fusion.5), channel_id=1, source_target_pairs={{0,2},{2,4},{4,6},{6,0},{1,3},{3,5},{5,7},{7,1},{8,10},{10,12},{12... | collective-permute-start | bytes 1572872 | tf_op jit(solution)/shard_map/ppermute | solution.py:15
  69.9 27.8 %collective-permute-start.10 = (bf16[128,2048]{1,0:T(8,128)(2,1)S(1)}, bf16[128,2048]{1,0:T(8,128)(2,1)}, u32[]{:S(2)}, u32[]{:S(2)}) collective-permute-start(bf16[128,2048]{1,0:T(8,128)(2,1)S(1)} %add_convert_fusion.4), channel_id=1, source_target_pairs={{0,2},{2,4},{4,6},{6,0},{1,3},{3,5},{5,7},{7,1},{8,10},{10,12},{12... | collective-permute-start | bytes 1572872 | tf_op jit(solution)/shard_map/ppermute | solution.py:15
  86.5 22.3 %collective-permute-start.12 = (bf16[128,2048]{1,0:T(8,128)(2,1)S(1)}, bf16[128,2048]{1,0:T(8,128)(2,1)S(1)}, u32[]{:S(2)}, u32[]{:S(2)}) collective-permute-start(bf16[128,2048]{1,0:T(8,128)(2,1)S(1)} %add_convert_fusion.3), channel_id=1, source_target_pairs={{0,2},{2,4},{4,6},{6,0},{1,3},{3,5},{5,7},{7,1},{8,10},{10,12},{12... | collective-permute-start | bytes 1572872 | tf_op jit(solution)/shard_map/ppermute | solution.py:15
  98.9 19.2 %collective-permute-start.13 = (bf16[128,2048]{1,0:T(8,128)(2,1)S(1)}, bf16[128,2048]{1,0:T(8,128)(2,1)S(1)}, u32[]{:S(2)}, u32[]{:S(2)}) collective-permute-start(bf16[128,2048]{1,0:T(8,128)(2,1)S(1)} %add_convert_fusion.2), channel_id=1, source_target_pairs={{0,2},{2,4},{4,6},{6,0},{1,3},{3,5},{5,7},{7,1},{8,10},{10,12},{12... | collective-permute-start | bytes 1572872 | tf_op jit(solution)/shard_map/ppermute | solution.py:15
  99.7 2.2 %copy-start = (bf16[1,1,128,4096]{3,2,1,0:T(8,128)(2,1)S(1)}, bf16[1,1,128,4096]{3,2,1,0:T(8,128)(2,1)}, u32[]{:S(2)}) copy-start(bf16[1,1,128,4096]{3,2,1,0:T(8,128)(2,1)} %param.11) | copy-start | bytes 3145732
  108.8 48.8 %slice-start = ((s8[12582912]{0:T(1024)(128)(4,1)}), s8[4194304]{0:T(1024)(128)(4,1)S(1)}, s32[]{:S(2)}) async-start(s8[12582912]{0:T(1024)(128)(4,1)} %bitcast.227), calls=%async_computation | async-start | bytes 8388608
  118.2 2.1 copy-start.8
  118.5 39.1 %slice-start.1 = ((s8[12582912]{0:T(1024)(128)(4,1)}), s8[4194304]{0:T(1024)(128)(4,1)S(1)}, s32[]{:S(2)}) async-start(s8[12582912]{0:T(1024)(128)(4,1)} %bitcast.227), calls=%async_computation.1 | async-start | bytes 8388608
  118.8 24.2 %collective-permute-start.14 = (bf16[128,4096]{1,0:T(8,128)(2,1)S(1)}, bf16[128,4096]{1,0:T(8,128)(2,1)S(1)}, u32[]{:S(2)}, u32[]{:S(2)}) collective-permute-start(bf16[128,4096]{1,0:T(8,128)(2,1)S(1)} %fusion.41), channel_id=1, source_target_pairs={{0,8},{8,16},{16,24},{24,0},{1,9},{9,17},{17,25},{25,1},{2,10},{10... | collective-permute-start | bytes 3145736 | tf_op jit(solution)/shard_map/ppermute | solution.py:15
  120.3 37.3 %slice-start.2 = ((s8[12582912]{0:T(1024)(128)(4,1)}), s8[4194304]{0:T(1024)(128)(4,1)S(1)}, s32[]{:S(2)}) async-start(s8[12582912]{0:T(1024)(128)(4,1)} %bitcast.227), calls=%async_computation.2 | async-start | bytes 8388608
  121.1 13.3 %collective-permute-start.15 = (bf16[1,48,4096]{2,1,0:T(8,128)(2,1)S(1)}, bf16[1,48,4096]{2,1,0:T(8,128)(2,1)S(1)}, u32[]{:S(2)}, u32[]{:S(2)}) collective-permute-start(bf16[1,48,4096]{2,1,0:T(8,128)(2,1)S(1)} %get-tuple-element.23), channel_id=1, source_target_pairs={{0,2},{2,4},{4,6},{6,0},{1,3},{3,5},{5,7},{7,1},{8,10},{10,12},{12... | collective-permute-start | bytes 1179656 | tf_op jit(solution)/shard_map/ppermute | solution.py:15
  134.4 8.4 %collective-permute-start.22 = (bf16[1,48,4096]{2,1,0:T(8,128)(2,1)S(1)}, bf16[1,48,4096]{2,1,0:T(8,128)(2,1)S(1)}, u32[]{:S(2)}, u32[]{:S(2)}) collective-permute-start(bf16[1,48,4096]{2,1,0:T(8,128)(2,1)S(1)} %get-tuple-element.19), channel_id=1, source_target_pairs={{0,6},{2,0},{4,2},{6,4},{1,7},{3,1},{5,3},{7,5},{8,14},{10,8},{12,... | collective-permute-start | bytes 1179656 | tf_op jit(solution)/shard_map/ppermute | solution.py:15
  134.4 22.8 %collective-permute-start.16 = (bf16[1,48,4096]{2,1,0:T(8,128)(2,1)S(1)}, bf16[1,48,4096]{2,1,0:T(8,128)(2,1)S(1)}, u32[]{:S(2)}, u32[]{:S(2)}) collective-permute-start(bf16[1,48,4096]{2,1,0:T(8,128)(2,1)S(1)} %get-tuple-element.22), channel_id=1, source_target_pairs={{0,4},{2,6},{4,0},{6,2},{1,5},{3,7},{5,1},{7,3},{8,12},{10,14},{12... | collective-permute-start | bytes 1179656 | tf_op jit(solution)/shard_map/ppermute | solution.py:15
  142.9 14.6 %collective-permute-start.23 = (bf16[1,48,4096]{2,1,0:T(8,128)(2,1)S(1)}, bf16[1,48,4096]{2,1,0:T(8,128)(2,1)S(1)}, u32[]{:S(2)}, u32[]{:S(2)}) collective-permute-start(bf16[1,48,4096]{2,1,0:T(8,128)(2,1)S(1)} %collective-permute-done.22), channel_id=1, source_target_pairs={{0,1},{1,0},{2,3},{3,2},{4,5},{5,4},{6,7},{7,6},{8,9},{9,8},{10,11... | collective-permute-start | bytes 1179656 | tf_op jit(solution)/shard_map/ppermute | solution.py:15
  157.4 4.7 %collective-permute-start.17 = (bf16[3,48,4096]{2,1,0:T(8,128)(2,1)S(1)}, bf16[3,48,4096]{2,1,0:T(8,128)(2,1)S(1)}, u32[]{:S(2)}, u32[]{:S(2)}) collective-permute-start(bf16[3,48,4096]{2,1,0:T(8,128)(2,1)S(1)} %maximum_bitcast_fusion), channel_id=1, source_target_pairs={{0,1},{1,0},{2,3},{3,2},{4,5},{5,4},{6,7},{7,6},{8,9},{9,8},{10,11... | collective-permute-start | bytes 3538952 | tf_op jit(solution)/shard_map/ppermute | solution.py:15
  157.5 2.3 %slice-start.3 = ((s8[6291456]{0:T(1024)(128)(4,1)}), s8[4194304]{0:T(1024)(128)(4,1)S(1)}, s32[]{:S(2)}) async-start(s8[6291456]{0:T(1024)(128)(4,1)} %bitcast.229), calls=%async_computation.3 | async-start | bytes 8388608
  157.6 2.8 %slice-start.4 = ((s8[6291456]{0:T(1024)(128)(4,1)}), s8[2097152]{0:T(1024)(128)(4,1)S(1)}, s32[]{:S(2)}) async-start(s8[6291456]{0:T(1024)(128)(4,1)} %bitcast.229), calls=%async_computation.4 | async-start | bytes 4194304
  161.6 7.6 %collective-permute-start.24 = (bf16[1,48,4096]{2,1,0:T(8,128)(2,1)S(1)}, bf16[1,48,4096]{2,1,0:T(8,128)(2,1)S(1)}, u32[]{:S(2)}, u32[]{:S(2)}) collective-permute-start(bf16[1,48,4096]{2,1,0:T(8,128)(2,1)S(1)} %fusion.36), channel_id=1, source_target_pairs={{0,1},{1,0},{2,3},{3,2},{4,5},{5,4},{6,7},{7,6},{8,9},{9,8},{10,11... | collective-permute-start | bytes 1179656 | tf_op jit(solution)/shard_map/ppermute | solution.py:15
  168.4 2.9 %collective-permute-start.18 = (bf16[3,48,4096]{2,1,0:T(8,128)(2,1)S(1)}, bf16[3,48,4096]{2,1,0:T(8,128)(2,1)S(1)}, u32[]{:S(2)}, u32[]{:S(2)}) collective-permute-start(bf16[3,48,4096]{2,1,0:T(8,128)(2,1)S(1)} %bitcast.234), channel_id=1, source_target_pairs={{0,1},{1,0},{2,3},{3,2},{4,5},{5,4},{6,7},{7,6},{8,9},{9,8},{10,11... | collective-permute-start | bytes 3538952 | tf_op jit(solution)/shard_map/ppermute | solution.py:15
  168.6 0.6 copy-start.6
  169.2 15.8 %collective-permute-start.25 = (bf16[1,48,4096]{2,1,0:T(8,128)(2,1)S(1)}, bf16[1,48,4096]{2,1,0:T(8,128)(2,1)S(1)}, u32[]{:S(2)}, u32[]{:S(2)}) collective-permute-start(bf16[1,48,4096]{2,1,0:T(8,128)(2,1)S(1)} %fusion.33), channel_id=1, source_target_pairs={{0,10},{2,12},{4,14},{6,8},{8,18},{10,20},{12,22},{14,16},{16,26},... | collective-permute-start | bytes 1179656 | tf_op jit(solution)/shard_map/ppermute | solution.py:208
  171.7 22.6 %collective-permute-start.20 = (bf16[1,48,4096]{2,1,0:T(8,128)(2,1)S(1)}, bf16[1,48,4096]{2,1,0:T(8,128)(2,1)S(1)}, u32[]{:S(2)}, u32[]{:S(2)}) collective-permute-start(bf16[1,48,4096]{2,1,0:T(8,128)(2,1)S(1)} %get-tuple-element.26), channel_id=1, source_target_pairs={{0,14},{2,8},{4,10},{6,12},{8,22},{10,16},{12,18},{14,20},{16,30},... | collective-permute-start | bytes 1179656 | tf_op jit(solution)/shard_map/ppermute | solution.py:208
  175.4 34.4 %collective-permute-start.19 = (bf16[1,48,4096]{2,1,0:T(8,128)(2,1)S(1)}, bf16[1,48,4096]{2,1,0:T(8,128)(2,1)S(1)}, u32[]{:S(2)}, u32[]{:S(2)}) collective-permute-start(bf16[1,48,4096]{2,1,0:T(8,128)(2,1)S(1)} %get-tuple-element.27), channel_id=1, source_target_pairs={{0,8},{2,10},{4,12},{6,14},{8,16},{10,18},{12,20},{14,22},{16,24},... | collective-permute-start | bytes 1179656 | tf_op jit(solution)/shard_map/ppermute | solution.py:208
  185.0 24.8 %slice-start.5 = ((s32[192]{0:T(256)}), s32[48]{0:T(128)S(1)}, s32[]{:S(2)}) async-start(s32[192]{0:T(256)} %copy-done.6), calls=%async_computation.5 | async-start | bytes 1024 | tf_op jit(solution)/shard_map/slice | solution.py:232
  185.5 24.8 %collective-permute-start.21 = (bf16[1,48,4096]{2,1,0:T(8,128)(2,1)S(1)}, bf16[1,48,4096]{2,1,0:T(8,128)(2,1)S(1)}, u32[]{:S(2)}, u32[]{:S(2)}) collective-permute-start(bf16[1,48,4096]{2,1,0:T(8,128)(2,1)S(1)} %get-tuple-element.25), channel_id=1, source_target_pairs={{0,12},{2,14},{4,8},{6,10},{8,20},{10,22},{12,16},{14,18},{16,28},... | collective-permute-start | bytes 1179656 | tf_op jit(solution)/shard_map/ppermute | solution.py:208

commit v5 on v4

--- a/solution.py
+++ b/solution.py
@@ -16,7 +16,8 @@
 
 
 def after(value, *earlier):
-    return lax.optimization_barrier((value, *earlier))[0]
+    zero = sum(array.reshape(-1)[0].astype(jnp.float32) * 0.0 for array in earlier)
+    return value + zero.astype(value.dtype)
 
 
 def attend_block(query_block, key_rows, value_rows, row_ids, col_ids):
@@ -56,8 +57,6 @@
         pairs.append(shift(pair_for((me + k) % contexts), "ctx", k))
     for k in range(1, contexts):
         outgoing = queries_for((me + k) % contexts)
-        if k > 1:
-            outgoing = after(outgoing, blocks[1])
         blocks.append(shift(outgoing, "ctx", k))
     if exps == 2:
         weights = [out_weight, shift(out_weight, "exp", 1)]
@@ -208,21 +207,20 @@
         return lax.ppermute(rows, ("pipe", "ctx"), pairs)
 
     order = list(range(1, contexts))
-    groups = [[0, *order[:-1]], order[-1:]]
-    arrived, returned = {0: packed[0]}, {}
-    for k in order:
-        rows = packed[k]
-        if k == order[-1]:
-            rows = after(rows, arrived[order[0]])
-        arrived[k] = shift(rows, "ctx", k)
-    total = None
-    for group in groups:
+    groups = [[0], order[:-1], order[-1:]]
+    arrived, returned, totals = {0: packed[0]}, {}, []
+    for k in order[:-1]:
+        arrived[k] = shift(packed[k], "ctx", k)
+    for place, group in enumerate(groups):
+        if place == 1:
+            last = after(packed[order[-1]], arrived[1], totals[0])
+            arrived[order[-1]] = shift(last, "ctx", order[-1])
         rows = jnp.stack([arrived[k] for k in group], axis=0)
-        if total is not None:
-            rows = after(rows, total, next_mixed)
-        total = summed(expert_part(exchange(rows)), len(group))
+        if place:
+            rows = after(rows, totals[-1], next_mixed)
+        totals.append(summed(expert_part(exchange(rows)), len(group)))
         for i, k in enumerate(group):
-            returned[k] = to_next_owner(total[i], k)
+            returned[k] = to_next_owner(totals[-1][i], k)
 
     layer = next_mixed.astype(jnp.float32)
     width = per_context * capacity

time: 213 us -> 215 us (level)
  waiting for transfers between devices: 134 us -> 104 us
  starting transfers between devices: 20.8 us -> 35 us
  local copies, waits for them, and re-layouts: 3.69 us -> 11.1 us
  between operations: 0.67 us -> 7.87 us
  other arithmetic: 5.67 us -> 8.89 us
    ppermute x22 -> x24, waiting for transfers between devices: 101 us -> 73.6 us  [shift(): lax.ppermute(value, axis, [(i, (i + by) % devices) for i in range(devices)])]
    ppermute x22 -> x24, starting transfers between devices: 16.5 us -> 29.2 us  [shift(): lax.ppermute(value, axis, [(i, (i + by) % devices) for i in range(devices)])]
    slice x1 -> x12, local copies, waits for them, and re-layouts: 0.08 us -> 5.96 us  [the longest x11 5.91 us: after(): array.reshape(-1)[0].astype(jnp.float32) * 0.0]
    ppermute x4, waiting for transfers between devices: 32.8 us -> 30.2 us  [to_next_owner(): return lax.ppermute(rows, ('pipe', 'ctx'), pairs)]
    dot_general x2 -> x3, matrix products: 5.98 us -> 6.79 us  [expert_part(): jnp.dot(slot_rows, in_weight[0, 0], preferred_element_type=jnp.float32)]
  transfers between devices with their start and end apart: 26 -> 28, of which waited for: 15 -> 13; matrix products, arithmetic and copies ran while one was open for 25% -> 28% of each run, Pallas kernels for 0% -> 0%
where the time goes in v5:
time: 215 us
  waiting for transfers between devices  104 us (48%)
  matrix products  48 us (22%)
  starting transfers between devices  35 us (16%)
  local copies, waits for them, and re-layouts  11.1 us (5%)
  other arithmetic  8.89 us (4%)
  between operations  7.87 us (4%)
    ppermute x24, waiting for transfers between devices, shift(): lax.ppermute(value, axis, [(i, (i + by) % devices) for i in range(devices)])  73.6 us
    ppermute x4, waiting for transfers between devices, to_next_owner(): return lax.ppermute(rows, ('pipe', 'ctx'), pairs)  30.2 us
    ppermute x24, starting transfers between devices, shift(): lax.ppermute(value, axis, [(i, (i + by) % devices) for i in range(devices)])  29.2 us
    dot_general x8, matrix products, mixed_halves(): term = jnp.dot(attended, weights[half], preferred_element_type=jnp.float32)  23.8 us
    dot_general x3, matrix products, expert_part(): jnp.dot(slot_rows, in_weight[0, 0], preferred_element_type=jnp.float32)  6.79 us
    dot_general x4, matrix products, attend_block(): jnp.einsum('hqk,kd->qhd', attention_weights, value_rows, preferred_elemen...  6.16 us
    slice x11, local copies, waits for them, and re-layouts, after(): array.reshape(-1)[0].astype(jnp.float32) * 0.0  5.91 us
    ppermute x4, starting transfers between devices, to_next_owner(): return lax.ppermute(rows, ('pipe', 'ctx'), pairs)  5.78 us
  transfers between devices with their start and end apart: 28, of which 13 were waited for; matrix products, arithmetic and copies ran while one was open for 28% of the time, Pallas kernels for 0%

profile of v5, /device:TPU:0, one launch (start us, length us, event | category | flops | bytes accessed | tf_op | source)
XLA Modules:
  0.0 214.6 jit_solution(9253647570733362861)
XLA Ops:
  0.5 0.7 fusion.64
  1.4 0.8 select_reduce_fusion
  2.2 0.7 fusion.97
  2.9 0.7 pad_maximum_fusion.7
  3.5 2.5 %collective-permute-start.11 = (f32[2,128]{1,0:T(2,128)S(1)}, f32[2,128]{1,0:T(2,128)S(1)}, u32[]{:S(2)}, u32[]{:S(2)}) collective-permute-start(f32[2,128]{1,0:T(2,128)S(1)} %pad_maximum_fusion.7), channel_id=1, source_target_pairs={{0,8},{8,16},{16,24},{24,0},{1,9},{9,17},{17,25},{25,1},{2,10},{10... | collective-permute-start | bytes 3080 | tf_op jit(solution)/shard_map/ppermute | solution.py:15
  6.1 1.3 constant_dynamic-slice_fusion
  7.5 1.6 collective-permute-start.5
  9.2 2.3 %collective-permute-start.2 = (bf16[128,256]{1,0:T(8,128)(2,1)S(1)}, bf16[128,256]{1,0:T(8,128)(2,1)S(1)}, u32[]{:S(2)}, u32[]{:S(2)}) collective-permute-start(bf16[128,256]{1,0:T(8,128)(2,1)S(1)} %pad_maximum_fusion.6), channel_id=1, source_target_pairs={{0,6},{2,0},{4,2},{6,4},{1,7},{3,1},{5,3},{7,5},{8,14},{10,8},{12,... | collective-permute-start | bytes 196616 | tf_op jit(solution)/shard_map/ppermute | solution.py:15
  11.5 0.9 collective-permute-start.1
  12.4 0.8 broadcast_compare_fusion
  13.3 1.6 collective-permute-start
  15.1 0.8 copy.19
  16.1 0.6 slice.136
  17.4 1.4 collective-permute-done.2
  18.8 2.8 %collective-permute-start.3 = (bf16[128,1024]{0,1:T(8,128)(2,1)}, bf16[128,1024]{0,1:T(8,128)(2,1)}, u32[]{:S(2)}, u32[]{:S(2)}) collective-permute-start(bf16[128,1024]{0,1:T(8,128)(2,1)} %bitcast.11), channel_id=1, source_target_pairs={{0,6},{2,0},{4,2},{6,4},{1,7},{3,1},{5,3},{7,5},{8,14},{10,8},{12,... | collective-permute-start | bytes 786440 | tf_op jit(solution)/shard_map/ppermute | solution.py:15
  21.6 2.0 collective-permute-done.1
  23.8 0.8 fusion.121
  24.5 1.0 convolution_convert_fusion.4
  25.6 2.9 %fusion.103 = bf16[128,2048]{1,0:T(8,128)(2,1)S(1)} fusion(bf16[128,1024]{0,1:T(8,128)(2,1)S(1)} %bitcast.280, bf16[1,1024,2048]{2,1,0:T(8,128)(2,1)} %param.12), kind=kOutput, calls=%fused_computation.187 | convolution fusion | flops 536870912 | bytes 4980736 | tf_op jit(solution)/shard_map/dot_general | solution.py:90
  28.5 8.9 %collective-permute-start.7 = (bf16[128,2048]{1,0:T(8,128)(2,1)S(1)}, bf16[128,2048]{1,0:T(8,128)(2,1)S(1)}, u32[]{:S(2)}, u32[]{:S(2)}) collective-permute-start(bf16[128,2048]{1,0:T(8,128)(2,1)S(1)} %fusion.103), channel_id=1, source_target_pairs={{0,2},{2,4},{4,6},{6,0},{1,3},{3,5},{5,7},{7,1},{8,10},{10,12},{12... | collective-permute-start | bytes 1572872 | tf_op jit(solution)/shard_map/ppermute | solution.py:15
  38.1 2.9 %fusion.125 = bf16[128,2048]{1,0:T(8,128)(2,1)S(1)} fusion(bf16[128,1024]{0,1:T(8,128)(2,1)S(1)} %bitcast.281, bf16[1024,2048]{1,0:T(8,128)(2,1)} %collective-permute-done.6), kind=kOutput, calls=%fused_computation.205 | convolution fusion | flops 536870912 | bytes 4980736 | tf_op jit(solution)/shard_map/dot_general | solution.py:90
  41.1 3.0 %collective-permute-start.8 = (bf16[128,2048]{1,0:T(8,128)(2,1)S(1)}, bf16[128,2048]{1,0:T(8,128)(2,1)S(1)}, u32[]{:S(2)}, u32[]{:S(2)}) collective-permute-start(bf16[128,2048]{1,0:T(8,128)(2,1)S(1)} %fusion.125), channel_id=1, source_target_pairs={{0,2},{2,4},{4,6},{6,0},{1,3},{3,5},{5,7},{7,1},{8,10},{10,12},{12... | collective-permute-start | bytes 1572872 | tf_op jit(solution)/shard_map/ppermute | solution.py:15
  44.2 0.6 slice.168
  46.0 16.8 %collective-permute-done.4 = bf16[128,1024]{0,1:T(8,128)(2,1)S(1)} collective-permute-done((bf16[128,1024]{0,1:T(8,128)(2,1)S(1)}, bf16[128,1024]{0,1:T(8,128)(2,1)S(1)}, u32[]{:S(2)}, u32[]{:S(2)}) %collective-permute-start.4) | collective-permute-done | bytes 262176 | tf_op jit(solution)/shard_map/ppermute | solution.py:15
  62.8 1.6 fusion.122
  64.4 1.9 convolution_convert_fusion.3
  66.3 2.9 %fusion.101 = f32[128,2048]{1,0:T(8,128)S(1)} fusion(bf16[128,1024]{0,1:T(8,128)(2,1)S(1)} %bitcast.285, bf16[1,1024,2048]{2,1,0:T(8,128)(2,1)} %param.12), kind=kOutput, calls=%fused_computation.185 | convolution fusion | flops 536870912 | bytes 5505024 | tf_op jit(solution)/shard_map/dot_general | solution.py:90
  69.6 0.6 slice.169
  70.1 2.9 %fusion.126 = f32[128,2048]{1,0:T(8,128)S(1)} fusion(bf16[128,1024]{0,1:T(8,128)(2,1)S(1)} %bitcast.286, bf16[1024,2048]{1,0:T(8,128)(2,1)} %collective-permute-done.6), kind=kOutput, calls=%fused_computation.206 | convolution fusion | flops 536870912 | bytes 5505024 | tf_op jit(solution)/shard_map/dot_general | solution.py:90
  75.2 1.0 broadcast_add_fusion.1
  76.2 0.8 fusion.123
  77.0 1.0 convolution_convert_fusion.2
  78.0 2.9 %fusion.99 = f32[128,2048]{1,0:T(8,128)S(1)} fusion(bf16[128,1024]{0,1:T(8,128)(2,1)S(1)} %bitcast.287, bf16[1,1024,2048]{2,1,0:T(8,128)(2,1)} %param.12), kind=kOutput, calls=%fused_computation.183 | convolution fusion | flops 536870912 | bytes 5505024 | tf_op jit(solution)/shard_map/dot_general | solution.py:90
  81.0 5.1 %collective-permute-done.9 = bf16[128,2048]{1,0:T(8,128)(2,1)S(1)} collective-permute-done((bf16[128,2048]{1,0:T(8,128)(2,1)S(1)}, bf16[128,2048]{1,0:T(8,128)(2,1)S(1)}, u32[]{:S(2)}, u32[]{:S(2)}) %collective-permute-start.9) | collective-permute-done | bytes 524320 | tf_op jit(solution)/shard_map/ppermute | solution.py:15
  87.1 2.9 %fusion.127 = f32[128,2048]{1,0:T(8,128)S(1)} fusion(bf16[128,1024]{0,1:T(8,128)(2,1)S(1)} %bitcast.288, bf16[1024,2048]{1,0:T(8,128)(2,1)} %collective-permute-done.6), kind=kOutput, calls=%fused_computation.207 | convolution fusion | flops 536870912 | bytes 5505024 | tf_op jit(solution)/shard_map/dot_general | solution.py:90
  90.0 7.3 %collective-permute-done.10 = bf16[128,2048]{1,0:T(8,128)(2,1)S(1)} collective-permute-done((bf16[128,2048]{1,0:T(8,128)(2,1)S(1)}, bf16[128,2048]{1,0:T(8,128)(2,1)S(1)}, u32[]{:S(2)}, u32[]{:S(2)}) %collective-permute-start.10) | collective-permute-done | bytes 524320 | tf_op jit(solution)/shard_map/ppermute | solution.py:15
  97.7 0.6 slice.172
  99.5 0.7 add_add_fusion.1
  100.2 1.7 fusion.124
  102.0 2.2 %convolution_convert_fusion.1 = bf16[128,8,128]{2,0,1:T(8,128)(2,1)S(1)} fusion(f32[8,128]{1,0:T(8,128)S(1)} %fusion.124, bf16[512,256]{1,0:T(8,128)(2,1)} %copy-done.2, pred[128,512]{0,1:T(8,128)(4,1)S(1)} %get-tuple-element.26, bf16[128,8,128]{0,2,1:T(8,128)(2,1)} %bitcast.41), kind=kOutput, calls=%fused_computation.47 | convolution fusion | flops 271189504 | bytes 856064 | tf_op jit(solution)/shard_map/hqk,kd->qhd/dot_general | solution.py:29
  104.2 3.1 %convolution_add_fusion.1 = f32[128,2048]{1,0:T(8,128)S(1)} fusion(bf16[128,1024]{0,1:T(8,128)(2,1)S(1)} %bitcast.282, bf16[1,1,128,4096]{3,2,1,0:T(8,128)(2,1)S(1)} %copy-done, s32[]{:T(128)S(6)} %select_n.181, bf16[1,1024,2048]{2,1,0:T(8,128)(2,1)} %param.12), kind=kOutput, calls=%fused_computation.22 | convolution fusion | flops 537395200 | bytes 6029316 | tf_op jit(solution)/shard_map/dot_general | solution.py:90
  107.3 3.1 %convolution_add_fusion = f32[128,2048]{1,0:T(8,128)S(1)} fusion(bf16[128,1024]{0,1:T(8,128)(2,1)S(1)} %bitcast.283, bf16[1024,2048]{1,0:T(8,128)(2,1)} %collective-permute-done.6, bf16[1,1,128,4096]{3,2,1,0:T(8,128)(2,1)S(1)} %copy-done, s32[]{:T(128)S(6)} %select_n.182), kind=kOutput, calls=%fused_computation.21 | convolution fusion | flops 537395200 | bytes 6029316 | tf_op jit(solution)/shard_map/dot_general | solution.py:90
  110.5 6.3 %collective-permute-done.13 = bf16[128,2048]{1,0:T(8,128)(2,1)S(1)} collective-permute-done((bf16[128,2048]{1,0:T(8,128)(2,1)S(1)}, bf16[128,2048]{1,0:T(8,128)(2,1)S(1)}, u32[]{:S(2)}, u32[]{:S(2)}) %collective-permute-start.13) | collective-permute-done | bytes 524320 | tf_op jit(solution)/shard_map/ppermute | solution.py:15
  117.3 0.7 convolution_convert_fusion
  118.2 1.6 collective-permute-done.15
  119.9 2.1 fusion.8
  122.0 0.7 slice-done.4
  122.7 1.1 fusion.14
  124.3 1.8 collective-permute-start.14
  126.1 5.4 %collective-permute-done.18 = bf16[1,48,4096]{2,1,0:T(8,128)(2,1)S(1)} collective-permute-done((bf16[1,48,4096]{2,1,0:T(8,128)(2,1)S(1)}, bf16[1,48,4096]{2,1,0:T(8,128)(2,1)S(1)}, u32[]{:S(2)}, u32[]{:S(2)}) %collective-permute-start.18) | collective-permute-done | bytes 393248 | tf_op jit(solution)/shard_map/ppermute | solution.py:15
  134.1 17.5 %collective-permute-done.14 = bf16[128,4096]{1,0:T(8,128)(2,1)S(1)} collective-permute-done((bf16[128,4096]{1,0:T(8,128)(2,1)S(1)}, bf16[128,4096]{1,0:T(8,128)(2,1)S(1)}, u32[]{:S(2)}, u32[]{:S(2)}) %collective-permute-start.14) | collective-permute-done | bytes 1048608 | tf_op jit(solution)/shard_map/ppermute | solution.py:15
  153.3 2.3 %collective-permute-done.20 = bf16[2,48,4096]{2,1,0:T(8,128)(2,1)S(1)} collective-permute-done((bf16[2,48,4096]{2,1,0:T(8,128)(2,1)S(1)}, bf16[2,48,4096]{2,1,0:T(8,128)(2,1)S(1)}, u32[]{:S(2)}, u32[]{:S(2)}) %collective-permute-start.20) | collective-permute-done | bytes 786464 | tf_op jit(solution)/shard_map/ppermute | solution.py:15
  155.7 2.6 %fusion.6 = f32[192,1536]{1,0:T(8,128)S(1)} fusion(bf16[192,4096]{1,0:T(8,128)(2,1)S(1)} %bitcast.277, bf16[1,1,4096,1536]{3,2,1,0:T(8,128)(2,1)S(1)} %bitcast.262), kind=kOutput, calls=%fused_computation.6 | convolution fusion | flops 2415919104 | bytes 15335424 | tf_op jit(solution)/shard_map/dot_general | solution.py:180
  158.3 1.4 fusion.12
  160.3 0.6 collective-permute-start.17
  160.9 1.6 collective-permute-start.24
  164.2 7.8 %collective-permute-done.24 = bf16[1,48,4096]{2,1,0:T(8,128)(2,1)S(1)} collective-permute-done((bf16[1,48,4096]{2,1,0:T(8,128)(2,1)S(1)}, bf16[1,48,4096]{2,1,0:T(8,128)(2,1)S(1)}, u32[]{:S(2)}, u32[]{:S(2)}) %collective-permute-start.24) | collective-permute-done | bytes 393248 | tf_op jit(solution)/shard_map/ppermute | solution.py:15
  172.2 5.0 %collective-permute-start.22 = (bf16[1,48,4096]{2,1,0:T(8,128)(2,1)S(1)}, bf16[1,48,4096]{2,1,0:T(8,128)(2,1)S(1)}, u32[]{:S(2)}, u32[]{:S(2)}) collective-permute-start(bf16[1,48,4096]{2,1,0:T(8,128)(2,1)S(1)} %get-tuple-element.14), channel_id=1, source_target_pairs={{0,14},{2,8},{4,10},{6,12},{8,22},{10,16},{12,18},{14,20},{16,30},... | collective-permute-start | bytes 1179656 | tf_op jit(solution)/shard_map/ppermute | solution.py:207
  177.3 2.1 fusion.4
  179.4 1.1 fusion.10
  181.4 5.3 %collective-permute-done.22 = bf16[1,48,4096]{2,1,0:T(8,128)(2,1)S(1)} collective-permute-done((bf16[1,48,4096]{2,1,0:T(8,128)(2,1)S(1)}, bf16[1,48,4096]{2,1,0:T(8,128)(2,1)S(1)}, u32[]{:S(2)}, u32[]{:S(2)}) %collective-permute-start.22) | collective-permute-done | bytes 393248 | tf_op jit(solution)/shard_map/ppermute | solution.py:207
  187.3 24.9 %collective-permute-done.23 = bf16[1,48,4096]{2,1,0:T(8,128)(2,1)S(1)} collective-permute-done((bf16[1,48,4096]{2,1,0:T(8,128)(2,1)S(1)}, bf16[1,48,4096]{2,1,0:T(8,128)(2,1)S(1)}, u32[]{:S(2)}, u32[]{:S(2)}) %collective-permute-start.23) | collective-permute-done | bytes 393248 | tf_op jit(solution)/shard_map/ppermute | solution.py:207
  212.2 0.6 add_add_fusion
  213.4 1.2 fusion.20
  (122 shorter events, 12.0 us)
Async XLA Ops:
  0.0 9.1 %copy-start.1 = (bf16[1,1,128,512]{3,2,1,0:T(8,128)(2,1)S(1)}, bf16[1,1,128,512]{3,2,1,0:T(8,128)(2,1)}, u32[]{:S(2)}) copy-start(bf16[1,1,128,512]{3,2,1,0:T(8,128)(2,1)} %param.10) | copy-start | bytes 393220
  0.0 38.1 %collective-permute-start.6 = (bf16[1024,2048]{1,0:T(8,128)(2,1)}, bf16[1024,2048]{1,0:T(8,128)(2,1)}, u32[]{:S(2)}, u32[]{:S(2)}) collective-permute-start(bf16[1024,2048]{1,0:T(8,128)(2,1)} %bitcast.265), channel_id=1, source_target_pairs={{0,1},{1,0},{2,3},{3,2},{4,5},{5,4},{6,7},{7,6},{8,9},{9,8},{10,11... | collective-permute-start | bytes 12582920 | tf_op jit(solution)/shard_map/ppermute | solution.py:15
  3.5 9.7 %collective-permute-start.11 = (f32[2,128]{1,0:T(2,128)S(1)}, f32[2,128]{1,0:T(2,128)S(1)}, u32[]{:S(2)}, u32[]{:S(2)}) collective-permute-start(f32[2,128]{1,0:T(2,128)S(1)} %pad_maximum_fusion.7), channel_id=1, source_target_pairs={{0,8},{8,16},{16,24},{24,0},{1,9},{9,17},{17,25},{25,1},{2,10},{10... | collective-permute-start | bytes 3080 | tf_op jit(solution)/shard_map/ppermute | solution.py:15
  6.1 8.8 %copy-start.3 = (s32[1,1,128,1]{2,3,1,0:T(1,128)S(1)}, s32[1,1,128,1]{2,3,1,0:T(1,128)}, u32[]{:S(2)}) copy-start(s32[1,1,128,1]{2,3,1,0:T(1,128)} %param.16) | copy-start | bytes 1540
  7.5 16.2 %collective-permute-start.5 = (bf16[128,1024]{0,1:T(8,128)(2,1)S(1)}, bf16[128,1024]{0,1:T(8,128)(2,1)S(1)}, u32[]{:S(2)}, u32[]{:S(2)}) collective-permute-start(bf16[128,1024]{0,1:T(8,128)(2,1)S(1)} %bitcast.303), channel_id=1, source_target_pairs={{0,2},{2,4},{4,6},{6,0},{1,3},{3,5},{5,7},{7,1},{8,10},{10,12},{12... | collective-permute-start | bytes 786440 | tf_op jit(solution)/shard_map/ppermute | solution.py:15
  9.2 9.6 %collective-permute-start.2 = (bf16[128,256]{1,0:T(8,128)(2,1)S(1)}, bf16[128,256]{1,0:T(8,128)(2,1)S(1)}, u32[]{:S(2)}, u32[]{:S(2)}) collective-permute-start(bf16[128,256]{1,0:T(8,128)(2,1)S(1)} %pad_maximum_fusion.6), channel_id=1, source_target_pairs={{0,6},{2,0},{4,2},{6,4},{1,7},{3,1},{5,3},{7,5},{8,14},{10,8},{12,... | collective-permute-start | bytes 196616 | tf_op jit(solution)/shard_map/ppermute | solution.py:15
  11.5 12.0 %collective-permute-start.1 = (bf16[128,256]{1,0:T(8,128)(2,1)S(1)}, bf16[128,256]{1,0:T(8,128)(2,1)S(1)}, u32[]{:S(2)}, u32[]{:S(2)}) collective-permute-start(bf16[128,256]{1,0:T(8,128)(2,1)S(1)} %pad_maximum_fusion.5), channel_id=1, source_target_pairs={{0,4},{2,6},{4,0},{6,2},{1,5},{3,7},{5,1},{7,3},{8,12},{10,14},{12... | collective-permute-start | bytes 196616 | tf_op jit(solution)/shard_map/ppermute | solution.py:15
  13.3 10.5 %collective-permute-start = (bf16[128,256]{1,0:T(8,128)(2,1)S(1)}, bf16[128,256]{1,0:T(8,128)(2,1)S(1)}, u32[]{:S(2)}, u32[]{:S(2)}) collective-permute-start(bf16[128,256]{1,0:T(8,128)(2,1)S(1)} %pad_maximum_fusion.4), channel_id=1, source_target_pairs={{0,2},{2,4},{4,6},{6,0},{1,3},{3,5},{5,7},{7,1},{8,10},{10,12},{12... | collective-permute-start | bytes 196616 | tf_op jit(solution)/shard_map/ppermute | solution.py:15
  18.8 56.4 %collective-permute-start.3 = (bf16[128,1024]{0,1:T(8,128)(2,1)}, bf16[128,1024]{0,1:T(8,128)(2,1)}, u32[]{:S(2)}, u32[]{:S(2)}) collective-permute-start(bf16[128,1024]{0,1:T(8,128)(2,1)} %bitcast.11), channel_id=1, source_target_pairs={{0,6},{2,0},{4,2},{6,4},{1,7},{3,1},{5,3},{7,5},{8,14},{10,8},{12,... | collective-permute-start | bytes 786440 | tf_op jit(solution)/shard_map/ppermute | solution.py:15
  23.6 39.2 %collective-permute-start.4 = (bf16[128,1024]{0,1:T(8,128)(2,1)S(1)}, bf16[128,1024]{0,1:T(8,128)(2,1)S(1)}, u32[]{:S(2)}, u32[]{:S(2)}) collective-permute-start(bf16[128,1024]{0,1:T(8,128)(2,1)S(1)} %bitcast.304), channel_id=1, source_target_pairs={{0,4},{2,6},{4,0},{6,2},{1,5},{3,7},{5,1},{7,3},{8,12},{10,14},{12... | collective-permute-start | bytes 786440 | tf_op jit(solution)/shard_map/ppermute | solution.py:15
  23.7 76.5 %copy-start.2 = (bf16[512,256]{1,0:T(8,128)(2,1)}, bf16[512,256]{1,0:T(8,128)(2,1)S(1)}, u32[]{:S(2)}) copy-start(bf16[512,256]{1,0:T(8,128)(2,1)S(1)} %pad_maximum_fusion.3) | copy-start | bytes 786436
  28.5 40.7 %collective-permute-start.7 = (bf16[128,2048]{1,0:T(8,128)(2,1)S(1)}, bf16[128,2048]{1,0:T(8,128)(2,1)S(1)}, u32[]{:S(2)}, u32[]{:S(2)}) collective-permute-start(bf16[128,2048]{1,0:T(8,128)(2,1)S(1)} %fusion.103), channel_id=1, source_target_pairs={{0,2},{2,4},{4,6},{6,0},{1,3},{3,5},{5,7},{7,1},{8,10},{10,12},{12... | collective-permute-start | bytes 1572872 | tf_op jit(solution)/shard_map/ppermute | solution.py:15
  41.1 32.0 %collective-permute-start.8 = (bf16[128,2048]{1,0:T(8,128)(2,1)S(1)}, bf16[128,2048]{1,0:T(8,128)(2,1)S(1)}, u32[]{:S(2)}, u32[]{:S(2)}) collective-permute-start(bf16[128,2048]{1,0:T(8,128)(2,1)S(1)} %fusion.125), channel_id=1, source_target_pairs={{0,2},{2,4},{4,6},{6,0},{1,3},{3,5},{5,7},{7,1},{8,10},{10,12},{12... | collective-permute-start | bytes 1572872 | tf_op jit(solution)/shard_map/ppermute | solution.py:15
  69.4 16.7 %collective-permute-start.9 = (bf16[128,2048]{1,0:T(8,128)(2,1)S(1)}, bf16[128,2048]{1,0:T(8,128)(2,1)S(1)}, u32[]{:S(2)}, u32[]{:S(2)}) collective-permute-start(bf16[128,2048]{1,0:T(8,128)(2,1)S(1)} %add_convert_fusion.5), channel_id=1, source_target_pairs={{0,2},{2,4},{4,6},{6,0},{1,3},{3,5},{5,7},{7,1},{8,10},{10,12},{12... | collective-permute-start | bytes 1572872 | tf_op jit(solution)/shard_map/ppermute | solution.py:15
  73.2 24.1 %collective-permute-start.10 = (bf16[128,2048]{1,0:T(8,128)(2,1)S(1)}, bf16[128,2048]{1,0:T(8,128)(2,1)S(1)}, u32[]{:S(2)}, u32[]{:S(2)}) collective-permute-start(bf16[128,2048]{1,0:T(8,128)(2,1)S(1)} %add_convert_fusion.4), channel_id=1, source_target_pairs={{0,2},{2,4},{4,6},{6,0},{1,3},{3,5},{5,7},{7,1},{8,10},{10,12},{12... | collective-permute-start | bytes 1572872 | tf_op jit(solution)/shard_map/ppermute | solution.py:15
  86.2 24.2 %collective-permute-start.12 = (bf16[128,2048]{1,0:T(8,128)(2,1)S(1)}, bf16[128,2048]{1,0:T(8,128)(2,1)S(1)}, u32[]{:S(2)}, u32[]{:S(2)}) collective-permute-start(bf16[128,2048]{1,0:T(8,128)(2,1)S(1)} %add_convert_fusion.3), channel_id=1, source_target_pairs={{0,2},{2,4},{4,6},{6,0},{1,3},{3,5},{5,7},{7,1},{8,10},{10,12},{12... | collective-permute-start | bytes 1572872 | tf_op jit(solution)/shard_map/ppermute | solution.py:15
  97.5 19.4 %collective-permute-start.13 = (bf16[128,2048]{1,0:T(8,128)(2,1)S(1)}, bf16[128,2048]{1,0:T(8,128)(2,1)S(1)}, u32[]{:S(2)}, u32[]{:S(2)}) collective-permute-start(bf16[128,2048]{1,0:T(8,128)(2,1)S(1)} %add_convert_fusion.2), channel_id=1, source_target_pairs={{0,2},{2,4},{4,6},{6,0},{1,3},{3,5},{5,7},{7,1},{8,10},{10,12},{12... | collective-permute-start | bytes 1572872 | tf_op jit(solution)/shard_map/ppermute | solution.py:15
  102.0 2.2 %copy-start = (bf16[1,1,128,4096]{3,2,1,0:T(8,128)(2,1)S(1)}, bf16[1,1,128,4096]{3,2,1,0:T(8,128)(2,1)}, u32[]{:S(2)}) copy-start(bf16[1,1,128,4096]{3,2,1,0:T(8,128)(2,1)} %param.11) | copy-start | bytes 3145732
  104.2 15.7 %slice-start = ((s8[12582912]{0:T(1024)(128)(4,1)}), s8[4194304]{0:T(1024)(128)(4,1)S(1)}, s32[]{:S(2)}) async-start(s8[12582912]{0:T(1024)(128)(4,1)} %bitcast.261), calls=%async_computation | async-start | bytes 8388608
  107.3 12.6 %slice-start.1 = ((s8[12582912]{0:T(1024)(128)(4,1)}), s8[4194304]{0:T(1024)(128)(4,1)S(1)}, s32[]{:S(2)}) async-start(s8[12582912]{0:T(1024)(128)(4,1)} %bitcast.261), calls=%async_computation.1 | async-start | bytes 8388608
  110.5 6.8 %copy-start.5 = (f32[1,4096]{1,0:T(1,128)S(1)}, f32[1,4096]{1,0:T(1,128)}, u32[]{:S(2)}) copy-start(f32[1,4096]{1,0:T(1,128)} %param.13) | copy-start | bytes 49156
  116.9 3.0 %slice-start.2 = ((s8[12582912]{0:T(1024)(128)(4,1)}), s8[4194304]{0:T(1024)(128)(4,1)S(1)}, s32[]{:S(2)}) async-start(s8[12582912]{0:T(1024)(128)(4,1)} %bitcast.261), calls=%async_computation.2 | async-start | bytes 8388608
  118.0 1.8 collective-permute-start.15
  118.1 13.3 %collective-permute-start.18 = (bf16[1,48,4096]{2,1,0:T(8,128)(2,1)S(1)}, bf16[1,48,4096]{2,1,0:T(8,128)(2,1)S(1)}, u32[]{:S(2)}, u32[]{:S(2)}) collective-permute-start(bf16[1,48,4096]{2,1,0:T(8,128)(2,1)S(1)} %get-tuple-element.8), channel_id=1, source_target_pairs={{0,2},{2,4},{4,6},{6,0},{1,3},{3,5},{5,7},{7,1},{8,10},{10,12},{12... | collective-permute-start | bytes 1179656 | tf_op jit(solution)/shard_map/ppermute | solution.py:15
  119.8 2.2 %slice-start.3 = ((s8[6291456]{0:T(1024)(128)(4,1)}), s8[4194304]{0:T(1024)(128)(4,1)S(1)}, s32[]{:S(2)}) async-start(s8[6291456]{0:T(1024)(128)(4,1)} %bitcast.263), calls=%async_computation.3 | async-start | bytes 8388608
  119.9 2.8 %slice-start.4 = ((s8[6291456]{0:T(1024)(128)(4,1)}), s8[2097152]{0:T(1024)(128)(4,1)S(1)}, s32[]{:S(2)}) async-start(s8[6291456]{0:T(1024)(128)(4,1)} %bitcast.263), calls=%async_computation.4 | async-start | bytes 4194304
  123.9 8.8 %collective-permute-start.16 = (bf16[1,48,4096]{2,1,0:T(8,128)(2,1)S(1)}, bf16[1,48,4096]{2,1,0:T(8,128)(2,1)S(1)}, u32[]{:S(2)}, u32[]{:S(2)}) collective-permute-start(bf16[1,48,4096]{2,1,0:T(8,128)(2,1)S(1)} %fusion.40), channel_id=1, source_target_pairs={{0,1},{1,0},{2,3},{3,2},{4,5},{5,4},{6,7},{7,6},{8,9},{9,8},{10,11... | collective-permute-start | bytes 1179656 | tf_op jit(solution)/shard_map/ppermute | solution.py:15
  124.3 27.4 %collective-permute-start.14 = (bf16[128,4096]{1,0:T(8,128)(2,1)S(1)}, bf16[128,4096]{1,0:T(8,128)(2,1)S(1)}, u32[]{:S(2)}, u32[]{:S(2)}) collective-permute-start(bf16[128,4096]{1,0:T(8,128)(2,1)S(1)} %fusion.47), channel_id=1, source_target_pairs={{0,8},{8,16},{16,24},{24,0},{1,9},{9,17},{17,25},{25,1},{2,10},{10... | collective-permute-start | bytes 3145736 | tf_op jit(solution)/shard_map/ppermute | solution.py:15
  134.0 19.1 %collective-permute-start.19 = (bf16[1,48,4096]{2,1,0:T(8,128)(2,1)S(1)}, bf16[1,48,4096]{2,1,0:T(8,128)(2,1)S(1)}, u32[]{:S(2)}, u32[]{:S(2)}) collective-permute-start(bf16[1,48,4096]{2,1,0:T(8,128)(2,1)S(1)} %get-tuple-element.6), channel_id=1, source_target_pairs={{0,4},{2,6},{4,0},{6,2},{1,5},{3,7},{5,1},{7,3},{8,12},{10,14},{12... | collective-permute-start | bytes 1179656 | tf_op jit(solution)/shard_map/ppermute | solution.py:15
  153.2 2.4 %collective-permute-start.20 = (bf16[2,48,4096]{2,1,0:T(8,128)(2,1)S(1)}, bf16[2,48,4096]{2,1,0:T(8,128)(2,1)S(1)}, u32[]{:S(2)}, u32[]{:S(2)}) collective-permute-start(bf16[2,48,4096]{2,1,0:T(8,128)(2,1)S(1)} %maximum_add_fusion), channel_id=1, source_target_pairs={{0,1},{1,0},{2,3},{3,2},{4,5},{5,4},{6,7},{7,6},{8,9},{9,8},{10,11... | collective-permute-start | bytes 2359304 | tf_op jit(solution)/shard_map/ppermute | solution.py:15
  159.8 2.8 %collective-permute-start.21 = (bf16[2,48,4096]{2,1,0:T(8,128)(2,1)S(1)}, bf16[2,48,4096]{2,1,0:T(8,128)(2,1)S(1)}, u32[]{:S(2)}, u32[]{:S(2)}) collective-permute-start(bf16[2,48,4096]{2,1,0:T(8,128)(2,1)S(1)} %bitcast.289), channel_id=1, source_target_pairs={{0,1},{1,0},{2,3},{3,2},{4,5},{5,4},{6,7},{7,6},{8,9},{9,8},{10,11... | collective-permute-start | bytes 2359304 | tf_op jit(solution)/shard_map/ppermute | solution.py:15
  160.1 2.7 %copy-start.4 = (s32[192]{0:T(256)}, s32[192]{0:T(256)S(1)}, u32[]{:S(2)}) copy-start(s32[192]{0:T(256)S(1)} %iota.37) | copy-start | bytes 2308
  160.3 20.6 %collective-permute-start.17 = (bf16[1,48,4096]{2,1,0:T(8,128)(2,1)S(1)}, bf16[1,48,4096]{2,1,0:T(8,128)(2,1)S(1)}, u32[]{:S(2)}, u32[]{:S(2)}) collective-permute-start(bf16[1,48,4096]{2,1,0:T(8,128)(2,1)S(1)} %fusion.38), channel_id=1, source_target_pairs={{0,8},{2,10},{4,12},{6,14},{8,16},{10,18},{12,20},{14,22},{16,24},... | collective-permute-start | bytes 1179656 | tf_op jit(solution)/shard_map/ppermute | solution.py:207
  160.9 11.1 %collective-permute-start.24 = (bf16[1,48,4096]{2,1,0:T(8,128)(2,1)S(1)}, bf16[1,48,4096]{2,1,0:T(8,128)(2,1)S(1)}, u32[]{:S(2)}, u32[]{:S(2)}) collective-permute-start(bf16[1,48,4096]{2,1,0:T(8,128)(2,1)S(1)} %get-tuple-element.5), channel_id=1, source_target_pairs={{0,6},{2,0},{4,2},{6,4},{1,7},{3,1},{5,3},{7,5},{8,14},{10,8},{12,... | collective-permute-start | bytes 1179656 | tf_op jit(solution)/shard_map/ppermute | solution.py:15
  172.0 5.2 %collective-permute-start.25 = (bf16[1,48,4096]{2,1,0:T(8,128)(2,1)S(1)}, bf16[1,48,4096]{2,1,0:T(8,128)(2,1)S(1)}, u32[]{:S(2)}, u32[]{:S(2)}) collective-permute-start(bf16[1,48,4096]{2,1,0:T(8,128)(2,1)S(1)} %broadcast_add_fusion), channel_id=1, source_target_pairs={{0,1},{1,0},{2,3},{3,2},{4,5},{5,4},{6,7},{7,6},{8,9},{9,8},{10,11... | collective-permute-start | bytes 1179656 | tf_op jit(solution)/shard_map/ppermute | solution.py:15
  172.2 14.5 %collective-permute-start.22 = (bf16[1,48,4096]{2,1,0:T(8,128)(2,1)S(1)}, bf16[1,48,4096]{2,1,0:T(8,128)(2,1)S(1)}, u32[]{:S(2)}, u32[]{:S(2)}) collective-permute-start(bf16[1,48,4096]{2,1,0:T(8,128)(2,1)S(1)} %get-tuple-element.14), channel_id=1, source_target_pairs={{0,14},{2,8},{4,10},{6,12},{8,22},{10,16},{12,18},{14,20},{16,30},... | collective-permute-start | bytes 1179656 | tf_op jit(solution)/shard_map/ppermute | solution.py:207
  179.4 1.5 slice-start.5
  180.6 6.6 %collective-permute-start.26 = (bf16[1,48,4096]{2,1,0:T(8,128)(2,1)S(1)}, bf16[1,48,4096]{2,1,0:T(8,128)(2,1)S(1)}, u32[]{:S(2)}, u32[]{:S(2)}) collective-permute-start(bf16[1,48,4096]{2,1,0:T(8,128)(2,1)S(1)} %fusion.41), channel_id=1, source_target_pairs={{0,1},{1,0},{2,3},{3,2},{4,5},{5,4},{6,7},{7,6},{8,9},{9,8},{10,11... | collective-permute-start | bytes 1179656 | tf_op jit(solution)/shard_map/ppermute | solution.py:15
  181.3 30.9 %collective-permute-start.23 = (bf16[1,48,4096]{2,1,0:T(8,128)(2,1)S(1)}, bf16[1,48,4096]{2,1,0:T(8,128)(2,1)S(1)}, u32[]{:S(2)}, u32[]{:S(2)}) collective-permute-start(bf16[1,48,4096]{2,1,0:T(8,128)(2,1)S(1)} %get-tuple-element.13), channel_id=1, source_target_pairs={{0,12},{2,14},{4,8},{6,10},{8,20},{10,22},{12,16},{14,18},{16,28},... | collective-permute-start | bytes 1179656 | tf_op jit(solution)/shard_map/ppermute | solution.py:207
  187.2 25.7 %collective-permute-start.27 = (bf16[1,48,4096]{2,1,0:T(8,128)(2,1)S(1)}, bf16[1,48,4096]{2,1,0:T(8,128)(2,1)S(1)}, u32[]{:S(2)}, u32[]{:S(2)}) collective-permute-start(bf16[1,48,4096]{2,1,0:T(8,128)(2,1)S(1)} %fusion.36), channel_id=1, source_target_pairs={{0,10},{2,12},{4,14},{6,8},{8,18},{10,20},{12,22},{14,16},{16,26},... | collective-permute-start | bytes 1179656 | tf_op jit(solution)/shard_map/ppermute | solution.py:207

commit v6 on v5

--- a/solution.py
+++ b/solution.py
@@ -16,8 +16,14 @@
 
 
 def after(value, *earlier):
-    zero = sum(array.reshape(-1)[0].astype(jnp.float32) * 0.0 for array in earlier)
-    return value + zero.astype(value.dtype)
+    blocks = value.reshape(-1, *value.shape[-2:])
+    first = blocks[0]
+    for array in earlier:
+        block = array[(0,) * (array.ndim - 2)][: first.shape[0]]
+        zero = block.astype(value.dtype) * 0.0
+        rows = zero.shape[0]
+        first = jnp.concatenate([first[:rows] + zero, first[rows:]], axis=0)
+    return jnp.concatenate([first[None], blocks[1:]], axis=0).reshape(value.shape)
 
 
 def attend_block(query_block, key_rows, value_rows, row_ids, col_ids):
@@ -73,11 +79,11 @@
     origins = [(me - k) % contexts * rows for k in range(contexts)]
     col_ids = jnp.concatenate([origin + within for origin in origins])
 
-    held, sent = [None, None], []
+    held = [None, None]
     for k in [*range(1, contexts), 0]:
-        block = blocks[k] if k == 1 else after(blocks[k], *sent)
+        block = blocks[k]
         if k == 0:
-            block = after(block, finish)
+            block = block + (finish[0, 0] * 0.0).astype(block.dtype)
         attended = attend_block(
             block.reshape(rows, local_heads, HEAD_SIZE),
             key_rows,
@@ -85,7 +91,7 @@
             origins[k] + within,
             col_ids,
         ).reshape(rows, group_width)
-        terms, sent = [], []
+        terms = []
         for half in range(2):
             term = jnp.dot(attended, weights[half], preferred_element_type=jnp.float32)
             if k == 0:
@@ -96,11 +102,7 @@
             term = terms[half]
             if held[half] is not None:
                 term = term + held[half].astype(jnp.float32)
-            if k == 0:
-                held[half] = term
-            else:
-                sent.append(term.astype(jnp.bfloat16))
-                held[half] = shift(sent[half], "ctx", 1)
+            held[half] = term if k == 0 else shift(term.astype(jnp.bfloat16), "ctx", 1)
     return held, first
 
 
@@ -159,7 +161,11 @@
 
     mean_square = jnp.mean(mixed_rows * mixed_rows, axis=-1, keepdims=True)
     normed = (mixed_rows * lax.rsqrt(mean_square + 1e-06) * norm_gain[0]).astype(jnp.bfloat16)
-    next_mixed = shift(mixed_rows.astype(jnp.bfloat16), "pipe", 1)
+    cuts = [0, token_rows * 3 // 8, token_rows * 3 // 4, token_rows]
+    next_mixed = [
+        shift(mixed_rows[start:stop].astype(jnp.bfloat16), "pipe", 1)
+        for start, stop in zip(cuts, cuts[1:])
+    ]
     packed = jnp.dot(slot_match, normed, preferred_element_type=jnp.float32).astype(jnp.bfloat16)
     packed = packed.reshape(contexts, per_context, capacity, model_width)
 
@@ -183,13 +189,14 @@
         )
         return jnp.dot(hidden, down_weight[0, 0], preferred_element_type=jnp.float32)
 
-    def summed(part, count):
+    def summed(part, count, *earlier):
         part = part.reshape(exps, count, capacity, model_width)
         sums = [0.0] * per_context
         for k in range(exps):
             back = part[k]
             if k:
-                back = shift(back.astype(jnp.bfloat16), "exp", -k).astype(jnp.float32)
+                back = after(back.astype(jnp.bfloat16), *earlier)
+                back = shift(back, "exp", -k).astype(jnp.float32)
             if per_context == 1:
                 sums[0] = sums[0] + back
             else:
@@ -207,22 +214,24 @@
         return lax.ppermute(rows, ("pipe", "ctx"), pairs)
 
     order = list(range(1, contexts))
+    arrived = {0: packed[0]} | {k: shift(packed[k], "ctx", k) for k in order}
     groups = [[0], order[:-1], order[-1:]]
-    arrived, returned, totals = {0: packed[0]}, {}, []
-    for k in order[:-1]:
-        arrived[k] = shift(packed[k], "ctx", k)
+    returned, total = {}, None
     for place, group in enumerate(groups):
-        if place == 1:
-            last = after(packed[order[-1]], arrived[1], totals[0])
-            arrived[order[-1]] = shift(last, "ctx", order[-1])
         rows = jnp.stack([arrived[k] for k in group], axis=0)
-        if place:
-            rows = after(rows, totals[-1], next_mixed)
-        totals.append(summed(expert_part(exchange(rows)), len(group)))
+        if place == 0:
+            earlier = [arrived[1], next_mixed[0]]
+        elif place == 1:
+            rows = after(rows, returned[0], next_mixed[1])
+            earlier = [arrived[order[-1]], next_mixed[2]]
+        else:
+            rows = after(rows, total)
+            earlier = [returned[1]]
+        total = summed(expert_part(exchange(rows)), len(group), *earlier)
         for i, k in enumerate(group):
-            returned[k] = to_next_owner(totals[-1][i], k)
-
-    layer = next_mixed.astype(jnp.float32)
+            returned[k] = to_next_owner(total[i], k)
+
+    layer = jnp.concatenate(next_mixed, axis=0).astype(jnp.float32)
     width = per_context * capacity
     for k in [0, *order]:
         if k == order[-1]:

time: 215 us -> 226 us (1.051)
  starting transfers between devices: 35 us -> 54.1 us
  between operations: 7.87 us -> 1.25 us
  local copies, waits for them, and re-layouts: 11.1 us -> 4.87 us
  waiting for transfers between devices: 104 us -> 107 us
    ppermute x24 -> x26, starting transfers between devices: 29.2 us -> 44.6 us  [shift(): lax.ppermute(value, axis, [(i, (i + by) % devices) for i in range(devices)])]
    ppermute x4, waiting for transfers between devices: 30.2 us -> 39.5 us  [to_next_owner(): return lax.ppermute(rows, ('pipe', 'ctx'), pairs)]
    ppermute x24 -> x26, waiting for transfers between devices: 73.6 us -> 67.2 us  [shift(): lax.ppermute(value, axis, [(i, (i + by) % devices) for i in range(devices)])]
    slice x12 -> x4, local copies, waits for them, and re-layouts: 5.96 us -> 0.6 us  [the longest x1 0.52 us: mixed_halves(): block = block + (finish[0, 0] * 0.0).astype(block.dtype)]
    ppermute x4, starting transfers between devices: 5.78 us -> 9.5 us  [to_next_owner(): return lax.ppermute(rows, ('pipe', 'ctx'), pairs)]
  transfers between devices with their start and end apart: 28 -> 30, of which waited for: 13 -> 18; matrix products, arithmetic and copies ran while one was open for 28% -> 25% of each run, Pallas kernels for 0% -> 0%
where the time goes in v6:
time: 226 us; the launch traced here: 225 us
  waiting for transfers between devices  107 us (47%)
  starting transfers between devices  54.1 us (24%)
  matrix products  48.5 us (21%)
  other arithmetic  9.69 us (4%)
  local copies, waits for them, and re-layouts  4.87 us (2%)
    ppermute x26, waiting for transfers between devices, shift(): lax.ppermute(value, axis, [(i, (i + by) % devices) for i in range(devices)])  67.2 us
    ppermute x26, starting transfers between devices, shift(): lax.ppermute(value, axis, [(i, (i + by) % devices) for i in range(devices)])  44.6 us
    ppermute x4, waiting for transfers between devices, to_next_owner(): return lax.ppermute(rows, ('pipe', 'ctx'), pairs)  39.5 us
    dot_general x8, matrix products, mixed_halves(): term = jnp.dot(attended, weights[half], preferred_element_type=jnp.float32)  22.3 us
    ppermute x4, starting transfers between devices, to_next_owner(): return lax.ppermute(rows, ('pipe', 'ctx'), pairs)  9.5 us
    dot_general x4, matrix products, attend_block(): jnp.einsum('hqk,kd->qhd', attention_weights, value_rows, preferred_elemen...  7.01 us
    dot_general x3, matrix products, expert_part(): jnp.dot(slot_rows, in_weight[0, 0], preferred_element_type=jnp.float32)  6.77 us
    sub x4, matrix products, attend_block(): attention_weights = jax.nn.softmax(scores, axis=-1).astype(jnp.bfloat16)  5.92 us
  transfers between devices with their start and end apart: 30, of which 18 were waited for; matrix products, arithmetic and copies ran while one was open for 25% of the time, Pallas kernels for 0%

profile of v6, /device:TPU:0, one launch (start us, length us, event | category | flops | bytes accessed | tf_op | source)
XLA Modules:
  0.0 225.0 jit_solution(18384310741608647906)
XLA Ops:
  0.0 1.0 dynamic-slice_bitcast_fusion.7
  1.0 3.1 %collective-permute-start = (bf16[128,256]{1,0:T(8,128)(2,1)S(1)}, bf16[128,256]{1,0:T(8,128)(2,1)}, u32[]{:S(2)}, u32[]{:S(2)}) collective-permute-start(bf16[128,256]{1,0:T(8,128)(2,1)S(1)} %pad_maximum_fusion.6), channel_id=1, source_target_pairs={{0,2},{2,4},{4,6},{6,0},{1,3},{3,5},{5,7},{7,1},{8,10},{10,12},{12... | collective-permute-start | bytes 196616 | tf_op jit(solution)/shard_map/ppermute | solution.py:15
  4.1 2.7 %collective-permute-start.1 = (bf16[128,256]{1,0:T(8,128)(2,1)S(1)}, bf16[128,256]{1,0:T(8,128)(2,1)}, u32[]{:S(2)}, u32[]{:S(2)}) collective-permute-start(bf16[128,256]{1,0:T(8,128)(2,1)S(1)} %pad_maximum_fusion.7), channel_id=1, source_target_pairs={{0,4},{2,6},{4,0},{6,2},{1,5},{3,7},{5,1},{7,3},{8,12},{10,14},{12... | collective-permute-start | bytes 196616 | tf_op jit(solution)/shard_map/ppermute | solution.py:15
  6.8 1.4 collective-permute-start.2
  8.2 0.7 fusion.69
  9.1 0.8 select_reduce_fusion
  9.9 0.7 fusion.102
  11.3 1.5 collective-permute-start.3
  12.9 0.8 broadcast_compare_fusion
  14.5 1.2 collective-permute-done.3
  15.7 0.7 collective-permute-start.6
  18.0 2.9 %collective-permute-start.4 = (bf16[128,1024]{0,1:T(8,128)(2,1)S(1)}, bf16[128,1024]{0,1:T(8,128)(2,1)}, u32[]{:S(2)}, u32[]{:S(2)}) collective-permute-start(bf16[128,1024]{0,1:T(8,128)(2,1)S(1)} %bitcast.276), channel_id=1, source_target_pairs={{0,6},{2,0},{4,2},{6,4},{1,7},{3,1},{5,3},{7,5},{8,14},{10,8},{12,... | collective-permute-start | bytes 786440 | tf_op jit(solution)/shard_map/ppermute | solution.py:15
  21.5 0.9 pad_maximum_fusion.5
  22.5 0.8 fusion.126
  23.2 1.0 convolution_convert_fusion.4
  24.4 2.9 %convolution_add_fusion.1 = f32[128,2048]{1,0:T(8,128)S(1)} fusion(bf16[128,1024]{0,1:T(8,128)(2,1)S(1)} %bitcast.266, bf16[1,1,128,4096]{3,2,1,0:T(8,128)(2,1)S(1)} %copy-done.1, s32[]{:T(128)S(6)} %select_n.175, bf16[1,1024,2048]{2,1,0:T(8,128)(2,1)} %param.12), kind=kOutput, calls=%fused_computation.22 | convolution fusion | flops 537395200 | bytes 6029316 | tf_op jit(solution)/shard_map/dot_general | solution.py:96
  27.4 1.7 fusion.129
  29.1 2.0 convolution_convert_fusion.1
  31.1 3.7 %fusion.103 = bf16[128,2048]{1,0:T(8,128)(2,1)} fusion(bf16[128,1024]{0,1:T(8,128)(2,1)S(1)} %bitcast.268, bf16[1,1024,2048]{2,1,0:T(8,128)(2,1)} %param.12), kind=kOutput, calls=%fused_computation.191 | convolution fusion | flops 536870912 | bytes 4980736 | tf_op jit(solution)/shard_map/dot_general | solution.py:96
  35.3 1.2 collective-permute-done.5
  36.6 1.7 fusion.128
  38.3 1.7 fusion.127
  40.0 2.0 convolution_convert_fusion.2
  42.0 2.0 convolution_convert_fusion.3
  44.0 3.1 %fusion.105 = f32[128,2048]{1,0:T(8,128)S(1)} fusion(bf16[128,1024]{0,1:T(8,128)(2,1)S(1)} %bitcast.272, bf16[1,1024,2048]{2,1,0:T(8,128)(2,1)} %param.12), kind=kOutput, calls=%fused_computation.193 | convolution fusion | flops 536870912 | bytes 5505024 | tf_op jit(solution)/shard_map/dot_general | solution.py:96
  47.5 0.7 fusion.107
  48.2 2.9 %fusion.133 = bf16[128,2048]{1,0:T(8,128)(2,1)S(1)} fusion(bf16[128,1024]{0,1:T(8,128)(2,1)S(1)} %bitcast.269, bf16[1024,2048]{1,0:T(8,128)(2,1)} %collective-permute-done.10), kind=kOutput, calls=%fused_computation.217 | convolution fusion | flops 536870912 | bytes 4980736 | tf_op jit(solution)/shard_map/dot_general | solution.py:96
  51.1 15.7 %collective-permute-start.11 = (bf16[128,2048]{1,0:T(8,128)(2,1)S(1)}, bf16[128,2048]{1,0:T(8,128)(2,1)S(1)}, u32[]{:S(2)}, u32[]{:S(2)}) collective-permute-start(bf16[128,2048]{1,0:T(8,128)(2,1)S(1)} %fusion.133), channel_id=1, source_target_pairs={{0,2},{2,4},{4,6},{6,0},{1,3},{3,5},{5,7},{7,1},{8,10},{10,12},{12... | collective-permute-start | bytes 1572872 | tf_op jit(solution)/shard_map/ppermute | solution.py:15
  66.8 1.2 add_convert_fusion.5
  68.0 2.9 %fusion.132 = f32[128,2048]{1,0:T(8,128)S(1)} fusion(bf16[128,1024]{0,1:T(8,128)(2,1)S(1)} %bitcast.273, bf16[1024,2048]{1,0:T(8,128)(2,1)} %collective-permute-done.10), kind=kOutput, calls=%fused_computation.216 | convolution fusion | flops 536870912 | bytes 5505024 | tf_op jit(solution)/shard_map/dot_general | solution.py:96
  71.0 8.1 %collective-permute-done.11 = bf16[128,2048]{1,0:T(8,128)(2,1)S(1)} collective-permute-done((bf16[128,2048]{1,0:T(8,128)(2,1)S(1)}, bf16[128,2048]{1,0:T(8,128)(2,1)S(1)}, u32[]{:S(2)}, u32[]{:S(2)}) %collective-permute-start.11) | collective-permute-done | bytes 524320 | tf_op jit(solution)/shard_map/ppermute | solution.py:15
  79.2 2.5 %collective-permute-start.12 = (bf16[128,2048]{1,0:T(8,128)(2,1)S(1)}, bf16[128,2048]{1,0:T(8,128)(2,1)S(1)}, u32[]{:S(2)}, u32[]{:S(2)}) collective-permute-start(bf16[128,2048]{1,0:T(8,128)(2,1)S(1)} %add_convert_fusion.3), channel_id=1, source_target_pairs={{0,2},{2,4},{4,6},{6,0},{1,3},{3,5},{5,7},{7,1},{8,10},{10,12},{12... | collective-permute-start | bytes 1572872 | tf_op jit(solution)/shard_map/ppermute | solution.py:15
  81.7 8.6 %collective-permute-done.8 = bf16[128,2048]{1,0:T(8,128)(2,1)S(1)} collective-permute-done((bf16[128,2048]{1,0:T(8,128)(2,1)S(1)}, bf16[128,2048]{1,0:T(8,128)(2,1)S(1)}, u32[]{:S(2)}, u32[]{:S(2)}) %collective-permute-start.8) | collective-permute-done | bytes 524320 | tf_op jit(solution)/shard_map/ppermute | solution.py:15
  90.4 2.5 %collective-permute-start.9 = (bf16[128,2048]{1,0:T(8,128)(2,1)S(1)}, bf16[128,2048]{1,0:T(8,128)(2,1)S(1)}, u32[]{:S(2)}, u32[]{:S(2)}) collective-permute-start(bf16[128,2048]{1,0:T(8,128)(2,1)S(1)} %add_convert_fusion.4), channel_id=1, source_target_pairs={{0,2},{2,4},{4,6},{6,0},{1,3},{3,5},{5,7},{7,1},{8,10},{10,12},{12... | collective-permute-start | bytes 1572872 | tf_op jit(solution)/shard_map/ppermute | solution.py:15
  93.0 2.9 %fusion.131 = f32[128,2048]{1,0:T(8,128)S(1)} fusion(bf16[128,1024]{0,1:T(8,128)(2,1)S(1)} %bitcast.271, bf16[1024,2048]{1,0:T(8,128)(2,1)} %collective-permute-done.10), kind=kOutput, calls=%fused_computation.215 | convolution fusion | flops 536870912 | bytes 5505024 | tf_op jit(solution)/shard_map/dot_general | solution.py:96
  95.9 5.7 %collective-permute-done.12 = bf16[128,2048]{1,0:T(8,128)(2,1)S(1)} collective-permute-done((bf16[128,2048]{1,0:T(8,128)(2,1)S(1)}, bf16[128,2048]{1,0:T(8,128)(2,1)S(1)}, u32[]{:S(2)}, u32[]{:S(2)}) %collective-permute-start.12) | collective-permute-done | bytes 524320 | tf_op jit(solution)/shard_map/ppermute | solution.py:15
  101.7 2.5 %collective-permute-start.13 = (bf16[128,2048]{1,0:T(8,128)(2,1)S(1)}, bf16[128,2048]{1,0:T(8,128)(2,1)S(1)}, u32[]{:S(2)}, u32[]{:S(2)}) collective-permute-start(bf16[128,2048]{1,0:T(8,128)(2,1)S(1)} %add_convert_fusion.2), channel_id=1, source_target_pairs={{0,2},{2,4},{4,6},{6,0},{1,3},{3,5},{5,7},{7,1},{8,10},{10,12},{12... | collective-permute-start | bytes 1572872 | tf_op jit(solution)/shard_map/ppermute | solution.py:15
  104.2 8.6 %collective-permute-done.9 = bf16[128,2048]{1,0:T(8,128)(2,1)S(1)} collective-permute-done((bf16[128,2048]{1,0:T(8,128)(2,1)S(1)}, bf16[128,2048]{1,0:T(8,128)(2,1)S(1)}, u32[]{:S(2)}, u32[]{:S(2)}) %collective-permute-start.9) | collective-permute-done | bytes 524320 | tf_op jit(solution)/shard_map/ppermute | solution.py:15
  113.0 3.1 %convolution_add_fusion = f32[128,2048]{1,0:T(8,128)S(1)} fusion(bf16[128,1024]{0,1:T(8,128)(2,1)S(1)} %bitcast.267, bf16[1024,2048]{1,0:T(8,128)(2,1)} %collective-permute-done.10, bf16[1,1,128,4096]{3,2,1,0:T(8,128)(2,1)S(1)} %copy-done.1, s32[]{:T(128)S(6)} %select_n.182), kind=kOutput, calls=%fused_computation.21 | convolution fusion | flops 537395200 | bytes 6029316 | tf_op jit(solution)/shard_map/dot_general | solution.py:96
  116.1 7.0 %collective-permute-done.13 = bf16[128,2048]{1,0:T(8,128)(2,1)S(1)} collective-permute-done((bf16[128,2048]{1,0:T(8,128)(2,1)S(1)}, bf16[128,2048]{1,0:T(8,128)(2,1)S(1)}, u32[]{:S(2)}, u32[]{:S(2)}) %collective-permute-start.13) | collective-permute-done | bytes 524320 | tf_op jit(solution)/shard_map/ppermute | solution.py:15
  124.9 1.2 collective-permute-start.14
  126.1 2.5 %collective-permute-start.18 = (bf16[1,48,4096]{2,1,0:T(8,128)(2,1)S(1)}, bf16[1,48,4096]{2,1,0:T(8,128)(2,1)S(1)}, u32[]{:S(2)}, u32[]{:S(2)}) collective-permute-start(bf16[1,48,4096]{2,1,0:T(8,128)(2,1)S(1)} %get-tuple-element.9), channel_id=1, source_target_pairs={{0,2},{2,4},{4,6},{6,0},{1,3},{3,5},{5,7},{7,1},{8,10},{10,12},{12... | collective-permute-start | bytes 1179656 | tf_op jit(solution)/shard_map/ppermute | solution.py:15
  128.7 2.1 fusion.8
  130.8 0.7 slice-done.4
  131.5 1.1 fusion.14
  132.6 4.7 %collective-permute-done.14 = bf16[48,4096]{1,0:T(8,128)(2,1)S(1)} collective-permute-done((bf16[48,4096]{1,0:T(8,128)(2,1)S(1)}, bf16[48,4096]{1,0:T(8,128)(2,1)S(1)}, u32[]{:S(2)}, u32[]{:S(2)}) %collective-permute-start.14) | collective-permute-done | bytes 393248 | tf_op jit(solution)/shard_map/ppermute | solution.py:15
  137.3 1.8 collective-permute-done.18
  139.3 1.9 collective-permute-start.15
  141.3 1.7 collective-permute-start.20
  143.4 8.8 %collective-permute-done.15 = bf16[48,4096]{1,0:T(8,128)(2,1)S(1)} collective-permute-done((bf16[48,4096]{1,0:T(8,128)(2,1)S(1)}, bf16[48,4096]{1,0:T(8,128)(2,1)S(1)}, u32[]{:S(2)}, u32[]{:S(2)}) %collective-permute-start.15) | collective-permute-done | bytes 393248 | tf_op jit(solution)/shard_map/ppermute | solution.py:15
  152.2 8.0 %collective-permute-done.20 = bf16[1,48,4096]{2,1,0:T(8,128)(2,1)S(1)} collective-permute-done((bf16[1,48,4096]{2,1,0:T(8,128)(2,1)S(1)}, bf16[1,48,4096]{2,1,0:T(8,128)(2,1)S(1)}, u32[]{:S(2)}, u32[]{:S(2)}) %collective-permute-start.20) | collective-permute-done | bytes 393248 | tf_op jit(solution)/shard_map/ppermute | solution.py:214
  160.2 3.0 %collective-permute-done.21 = bf16[1,48,4096]{2,1,0:T(8,128)(2,1)S(1)} collective-permute-done((bf16[1,48,4096]{2,1,0:T(8,128)(2,1)S(1)}, bf16[1,48,4096]{2,1,0:T(8,128)(2,1)S(1)}, u32[]{:S(2)}, u32[]{:S(2)}) %collective-permute-start.21) | collective-permute-done | bytes 393248 | tf_op jit(solution)/shard_map/ppermute | solution.py:15
  163.8 1.2 collective-permute-start.16
  165.8 2.6 %fusion.6 = f32[192,1536]{1,0:T(8,128)S(1)} fusion(bf16[192,4096]{1,0:T(8,128)(2,1)S(1)} %bitcast.265, bf16[1,1,4096,1536]{3,2,1,0:T(8,128)(2,1)S(1)} %bitcast.258), kind=kOutput, calls=%fused_computation.6 | convolution fusion | flops 2415919104 | bytes 15335424 | tf_op jit(solution)/shard_map/dot_general | solution.py:186
  168.4 1.4 fusion.130
  169.8 5.1 %collective-permute-done.23 = bf16[1,48,4096]{2,1,0:T(8,128)(2,1)S(1)} collective-permute-done((bf16[1,48,4096]{2,1,0:T(8,128)(2,1)S(1)}, bf16[1,48,4096]{2,1,0:T(8,128)(2,1)S(1)}, u32[]{:S(2)}, u32[]{:S(2)}) %collective-permute-start.23) | collective-permute-done | bytes 393248 | tf_op jit(solution)/shard_map/ppermute | solution.py:15
  175.4 2.2 collective-permute-done.24
  178.3 2.8 %collective-permute-start.25 = (bf16[1,48,4096]{2,1,0:T(8,128)(2,1)S(1)}, bf16[1,48,4096]{2,1,0:T(8,128)(2,1)S(1)}, u32[]{:S(2)}, u32[]{:S(2)}) collective-permute-start(bf16[1,48,4096]{2,1,0:T(8,128)(2,1)S(1)} %get-tuple-element.19), channel_id=1, source_target_pairs={{0,14},{2,8},{4,10},{6,12},{8,22},{10,16},{12,18},{14,20},{16,30},... | collective-permute-start | bytes 1179656 | tf_op jit(solution)/shard_map/ppermute | solution.py:214
  181.2 2.1 fusion.4
  183.3 1.1 fusion.10
  184.5 7.1 %collective-permute-done.25 = bf16[1,48,4096]{2,1,0:T(8,128)(2,1)S(1)} collective-permute-done((bf16[1,48,4096]{2,1,0:T(8,128)(2,1)S(1)}, bf16[1,48,4096]{2,1,0:T(8,128)(2,1)S(1)}, u32[]{:S(2)}, u32[]{:S(2)}) %collective-permute-start.25) | collective-permute-done | bytes 393248 | tf_op jit(solution)/shard_map/ppermute | solution.py:214
  193.5 4.8 %collective-permute-start.29 = (bf16[1,48,4096]{2,1,0:T(8,128)(2,1)S(1)}, bf16[1,48,4096]{2,1,0:T(8,128)(2,1)S(1)}, u32[]{:S(2)}, u32[]{:S(2)}) collective-permute-start(bf16[1,48,4096]{2,1,0:T(8,128)(2,1)S(1)} %fusion.36), channel_id=1, source_target_pairs={{0,10},{2,12},{4,14},{6,8},{8,18},{10,20},{12,22},{14,16},{16,26},... | collective-permute-start | bytes 1179656 | tf_op jit(solution)/shard_map/ppermute | solution.py:214
  198.3 24.4 %collective-permute-done.26 = bf16[1,48,4096]{2,1,0:T(8,128)(2,1)S(1)} collective-permute-done((bf16[1,48,4096]{2,1,0:T(8,128)(2,1)S(1)}, bf16[1,48,4096]{2,1,0:T(8,128)(2,1)S(1)}, u32[]{:S(2)}, u32[]{:S(2)}) %collective-permute-start.26) | collective-permute-done | bytes 393248 | tf_op jit(solution)/shard_map/ppermute | solution.py:214
  223.8 1.2 fusion.20
  (108 shorter events, 13.1 us)
Async XLA Ops:
  0.0 12.9 %copy-start.4 = (s32[1,1,128,1]{2,3,1,0:T(1,128)S(1)}, s32[1,1,128,1]{2,3,1,0:T(1,128)}, u32[]{:S(2)}) copy-start(s32[1,1,128,1]{2,3,1,0:T(1,128)} %param.16) | copy-start | bytes 1540
  0.0 12.8 %copy-start.2 = (bf16[1,1,128,4096]{3,2,1,0:T(8,128)(2,1)S(1)}, bf16[1,1,128,4096]{3,2,1,0:T(8,128)(2,1)}, u32[]{:S(2)}) copy-start(bf16[1,1,128,4096]{3,2,1,0:T(8,128)(2,1)} %param.9) | copy-start | bytes 3145732
  1.0 16.6 %collective-permute-start = (bf16[128,256]{1,0:T(8,128)(2,1)S(1)}, bf16[128,256]{1,0:T(8,128)(2,1)}, u32[]{:S(2)}, u32[]{:S(2)}) collective-permute-start(bf16[128,256]{1,0:T(8,128)(2,1)S(1)} %pad_maximum_fusion.6), channel_id=1, source_target_pairs={{0,2},{2,4},{4,6},{6,0},{1,3},{3,5},{5,7},{7,1},{8,10},{10,12},{12... | collective-permute-start | bytes 196616 | tf_op jit(solution)/shard_map/ppermute | solution.py:15
  4.1 13.9 %collective-permute-start.1 = (bf16[128,256]{1,0:T(8,128)(2,1)S(1)}, bf16[128,256]{1,0:T(8,128)(2,1)}, u32[]{:S(2)}, u32[]{:S(2)}) collective-permute-start(bf16[128,256]{1,0:T(8,128)(2,1)S(1)} %pad_maximum_fusion.7), channel_id=1, source_target_pairs={{0,4},{2,6},{4,0},{6,2},{1,5},{3,7},{5,1},{7,3},{8,12},{10,14},{12... | collective-permute-start | bytes 196616 | tf_op jit(solution)/shard_map/ppermute | solution.py:15
  6.8 14.1 %collective-permute-start.2 = (bf16[128,256]{1,0:T(8,128)(2,1)S(1)}, bf16[128,256]{1,0:T(8,128)(2,1)S(1)}, u32[]{:S(2)}, u32[]{:S(2)}) collective-permute-start(bf16[128,256]{1,0:T(8,128)(2,1)S(1)} %pad_maximum_fusion.8), channel_id=1, source_target_pairs={{0,6},{2,0},{4,2},{6,4},{1,7},{3,1},{5,3},{7,5},{8,14},{10,8},{12,... | collective-permute-start | bytes 196616 | tf_op jit(solution)/shard_map/ppermute | solution.py:15
  8.2 40.0 %collective-permute-start.10 = (bf16[1024,2048]{1,0:T(8,128)(2,1)}, bf16[1024,2048]{1,0:T(8,128)(2,1)}, u32[]{:S(2)}, u32[]{:S(2)}) collective-permute-start(bf16[1024,2048]{1,0:T(8,128)(2,1)} %bitcast.261), channel_id=1, source_target_pairs={{0,1},{1,0},{2,3},{3,2},{4,5},{5,4},{6,7},{7,6},{8,9},{9,8},{10,11... | collective-permute-start | bytes 12582920 | tf_op jit(solution)/shard_map/ppermute | solution.py:15
  11.3 4.5 %collective-permute-start.3 = (f32[2,128]{1,0:T(2,128)S(1)}, f32[2,128]{1,0:T(2,128)S(1)}, u32[]{:S(2)}, u32[]{:S(2)}) collective-permute-start(f32[2,128]{1,0:T(2,128)S(1)} %pad_maximum_fusion.9), channel_id=1, source_target_pairs={{0,8},{8,16},{16,24},{24,0},{1,9},{9,17},{17,25},{25,1},{2,10},{10... | collective-permute-start | bytes 3080 | tf_op jit(solution)/shard_map/ppermute | solution.py:15
  15.7 11.7 %collective-permute-start.6 = (bf16[128,1024]{0,1:T(8,128)(2,1)S(1)}, bf16[128,1024]{0,1:T(8,128)(2,1)}, u32[]{:S(2)}, u32[]{:S(2)}) collective-permute-start(bf16[128,1024]{0,1:T(8,128)(2,1)S(1)} %bitcast.278), channel_id=1, source_target_pairs={{0,2},{2,4},{4,6},{6,0},{1,3},{3,5},{5,7},{7,1},{8,10},{10,12},{12... | collective-permute-start | bytes 786440 | tf_op jit(solution)/shard_map/ppermute | solution.py:15
  17.6 19.0 %collective-permute-start.5 = (bf16[128,1024]{0,1:T(8,128)(2,1)S(1)}, bf16[128,1024]{0,1:T(8,128)(2,1)}, u32[]{:S(2)}, u32[]{:S(2)}) collective-permute-start(bf16[128,1024]{0,1:T(8,128)(2,1)S(1)} %bitcast.277), channel_id=1, source_target_pairs={{0,4},{2,6},{4,0},{6,2},{1,5},{3,7},{5,1},{7,3},{8,12},{10,14},{12... | collective-permute-start | bytes 786440 | tf_op jit(solution)/shard_map/ppermute | solution.py:15
  18.0 20.3 %collective-permute-start.4 = (bf16[128,1024]{0,1:T(8,128)(2,1)S(1)}, bf16[128,1024]{0,1:T(8,128)(2,1)}, u32[]{:S(2)}, u32[]{:S(2)}) collective-permute-start(bf16[128,1024]{0,1:T(8,128)(2,1)S(1)} %bitcast.276), channel_id=1, source_target_pairs={{0,6},{2,0},{4,2},{6,4},{1,7},{3,1},{5,3},{7,5},{8,14},{10,8},{12,... | collective-permute-start | bytes 786440 | tf_op jit(solution)/shard_map/ppermute | solution.py:15
  20.9 0.6 copy-start.3
  23.2 1.2 copy-start.1
  34.9 31.9 %collective-permute-start.7 = (bf16[128,2048]{1,0:T(8,128)(2,1)}, bf16[128,2048]{1,0:T(8,128)(2,1)}, u32[]{:S(2)}, u32[]{:S(2)}) collective-permute-start(bf16[128,2048]{1,0:T(8,128)(2,1)} %fusion.103), channel_id=1, source_target_pairs={{0,2},{2,4},{4,6},{6,0},{1,3},{3,5},{5,7},{7,1},{8,10},{10,12},{12... | collective-permute-start | bytes 1572872 | tf_op jit(solution)/shard_map/ppermute | solution.py:15
  44.0 3.5 %copy-start = (bf16[1,1024,2048]{2,1,0:T(8,128)(2,1)S(1)}, bf16[1,1024,2048]{2,1,0:T(8,128)(2,1)}, u32[]{:S(2)}) copy-start(bf16[1,1024,2048]{2,1,0:T(8,128)(2,1)} %param.12) | copy-start | bytes 12582916
  51.1 28.0 %collective-permute-start.11 = (bf16[128,2048]{1,0:T(8,128)(2,1)S(1)}, bf16[128,2048]{1,0:T(8,128)(2,1)S(1)}, u32[]{:S(2)}, u32[]{:S(2)}) collective-permute-start(bf16[128,2048]{1,0:T(8,128)(2,1)S(1)} %fusion.133), channel_id=1, source_target_pairs={{0,2},{2,4},{4,6},{6,0},{1,3},{3,5},{5,7},{7,1},{8,10},{10,12},{12... | collective-permute-start | bytes 1572872 | tf_op jit(solution)/shard_map/ppermute | solution.py:15
  68.0 22.4 %collective-permute-start.8 = (bf16[128,2048]{1,0:T(8,128)(2,1)S(1)}, bf16[128,2048]{1,0:T(8,128)(2,1)S(1)}, u32[]{:S(2)}, u32[]{:S(2)}) collective-permute-start(bf16[128,2048]{1,0:T(8,128)(2,1)S(1)} %add_convert_fusion.5), channel_id=1, source_target_pairs={{0,2},{2,4},{4,6},{6,0},{1,3},{3,5},{5,7},{7,1},{8,10},{10,12},{12... | collective-permute-start | bytes 1572872 | tf_op jit(solution)/shard_map/ppermute | solution.py:15
  79.2 22.4 %collective-permute-start.12 = (bf16[128,2048]{1,0:T(8,128)(2,1)S(1)}, bf16[128,2048]{1,0:T(8,128)(2,1)S(1)}, u32[]{:S(2)}, u32[]{:S(2)}) collective-permute-start(bf16[128,2048]{1,0:T(8,128)(2,1)S(1)} %add_convert_fusion.3), channel_id=1, source_target_pairs={{0,2},{2,4},{4,6},{6,0},{1,3},{3,5},{5,7},{7,1},{8,10},{10,12},{12... | collective-permute-start | bytes 1572872 | tf_op jit(solution)/shard_map/ppermute | solution.py:15
  90.4 22.4 %collective-permute-start.9 = (bf16[128,2048]{1,0:T(8,128)(2,1)S(1)}, bf16[128,2048]{1,0:T(8,128)(2,1)S(1)}, u32[]{:S(2)}, u32[]{:S(2)}) collective-permute-start(bf16[128,2048]{1,0:T(8,128)(2,1)S(1)} %add_convert_fusion.4), channel_id=1, source_target_pairs={{0,2},{2,4},{4,6},{6,0},{1,3},{3,5},{5,7},{7,1},{8,10},{10,12},{12... | collective-permute-start | bytes 1572872 | tf_op jit(solution)/shard_map/ppermute | solution.py:15
  101.7 21.4 %collective-permute-start.13 = (bf16[128,2048]{1,0:T(8,128)(2,1)S(1)}, bf16[128,2048]{1,0:T(8,128)(2,1)S(1)}, u32[]{:S(2)}, u32[]{:S(2)}) collective-permute-start(bf16[128,2048]{1,0:T(8,128)(2,1)S(1)} %add_convert_fusion.2), channel_id=1, source_target_pairs={{0,2},{2,4},{4,6},{6,0},{1,3},{3,5},{5,7},{7,1},{8,10},{10,12},{12... | collective-permute-start | bytes 1572872 | tf_op jit(solution)/shard_map/ppermute | solution.py:15
  112.9 15.7 %slice-start = ((s8[12582912]{0:T(1024)(128)(4,1)}), s8[4194304]{0:T(1024)(128)(4,1)S(1)}, s32[]{:S(2)}) async-start(s8[12582912]{0:T(1024)(128)(4,1)} %bitcast.257), calls=%async_computation | async-start | bytes 8388608
  116.0 12.6 %slice-start.1 = ((s8[12582912]{0:T(1024)(128)(4,1)}), s8[4194304]{0:T(1024)(128)(4,1)S(1)}, s32[]{:S(2)}) async-start(s8[12582912]{0:T(1024)(128)(4,1)} %bitcast.257), calls=%async_computation.1 | async-start | bytes 8388608
  123.2 0.7 copy-start.5
  123.9 4.7 %slice-start.2 = ((s8[12582912]{0:T(1024)(128)(4,1)}), s8[4194304]{0:T(1024)(128)(4,1)S(1)}, s32[]{:S(2)}) async-start(s8[12582912]{0:T(1024)(128)(4,1)} %bitcast.257), calls=%async_computation.2 | async-start | bytes 8388608
  124.7 3.9 %collective-permute-start.17 = (bf16[1,48,4096]{2,1,0:T(8,128)(2,1)S(1)}, bf16[1,48,4096]{2,1,0:T(8,128)(2,1)S(1)}, u32[]{:S(2)}, u32[]{:S(2)}) collective-permute-start(bf16[1,48,4096]{2,1,0:T(8,128)(2,1)S(1)} %get-tuple-element.10), channel_id=1, source_target_pairs={{0,1},{1,0},{2,3},{3,2},{4,5},{5,4},{6,7},{7,6},{8,9},{9,8},{10,11... | collective-permute-start | bytes 1179656 | tf_op jit(solution)/shard_map/ppermute | solution.py:15
  124.9 12.5 %collective-permute-start.14 = (bf16[48,4096]{1,0:T(8,128)(2,1)S(1)}, bf16[48,4096]{1,0:T(8,128)(2,1)S(1)}, u32[]{:S(2)}, u32[]{:S(2)}) collective-permute-start(bf16[48,4096]{1,0:T(8,128)(2,1)S(1)} %get-tuple-element.12), channel_id=1, source_target_pairs={{0,8},{8,16},{16,24},{24,0},{1,9},{9,17},{17,25},{25,1},{2,10},{10... | collective-permute-start | bytes 1179656 | tf_op jit(solution)/shard_map/ppermute | solution.py:15
  126.1 13.0 %collective-permute-start.18 = (bf16[1,48,4096]{2,1,0:T(8,128)(2,1)S(1)}, bf16[1,48,4096]{2,1,0:T(8,128)(2,1)S(1)}, u32[]{:S(2)}, u32[]{:S(2)}) collective-permute-start(bf16[1,48,4096]{2,1,0:T(8,128)(2,1)S(1)} %get-tuple-element.9), channel_id=1, source_target_pairs={{0,2},{2,4},{4,6},{6,0},{1,3},{3,5},{5,7},{7,1},{8,10},{10,12},{12... | collective-permute-start | bytes 1179656 | tf_op jit(solution)/shard_map/ppermute | solution.py:15
  128.6 2.2 slice-start.3
  128.7 2.8 %slice-start.4 = ((s8[6291456]{0:T(1024)(128)(4,1)}), s8[2097152]{0:T(1024)(128)(4,1)S(1)}, s32[]{:S(2)}) async-start(s8[6291456]{0:T(1024)(128)(4,1)} %bitcast.259), calls=%async_computation.4 | async-start | bytes 4194304
  139.3 1.9 collective-permute-start.19
  139.3 12.9 %collective-permute-start.15 = (bf16[48,4096]{1,0:T(8,128)(2,1)S(1)}, bf16[48,4096]{1,0:T(8,128)(2,1)S(1)}, u32[]{:S(2)}, u32[]{:S(2)}) collective-permute-start(bf16[48,4096]{1,0:T(8,128)(2,1)S(1)} %get-tuple-element.11), channel_id=1, source_target_pairs={{0,8},{8,16},{16,24},{24,0},{1,9},{9,17},{17,25},{25,1},{2,10},{10... | collective-permute-start | bytes 1179656 | tf_op jit(solution)/shard_map/ppermute | solution.py:15
  141.3 18.9 %collective-permute-start.20 = (bf16[1,48,4096]{2,1,0:T(8,128)(2,1)S(1)}, bf16[1,48,4096]{2,1,0:T(8,128)(2,1)S(1)}, u32[]{:S(2)}, u32[]{:S(2)}) collective-permute-start(bf16[1,48,4096]{2,1,0:T(8,128)(2,1)S(1)} %fusion.38), channel_id=1, source_target_pairs={{0,8},{2,10},{4,12},{6,14},{8,16},{10,18},{12,20},{14,22},{16,24},... | collective-permute-start | bytes 1179656 | tf_op jit(solution)/shard_map/ppermute | solution.py:214
  143.0 20.2 %collective-permute-start.21 = (bf16[1,48,4096]{2,1,0:T(8,128)(2,1)S(1)}, bf16[1,48,4096]{2,1,0:T(8,128)(2,1)S(1)}, u32[]{:S(2)}, u32[]{:S(2)}) collective-permute-start(bf16[1,48,4096]{2,1,0:T(8,128)(2,1)S(1)} %get-tuple-element.8), channel_id=1, source_target_pairs={{0,4},{2,6},{4,0},{6,2},{1,5},{3,7},{5,1},{7,3},{8,12},{10,14},{12... | collective-permute-start | bytes 1179656 | tf_op jit(solution)/shard_map/ppermute | solution.py:15
  163.3 2.4 %collective-permute-start.22 = (bf16[2,48,4096]{2,1,0:T(8,128)(2,1)S(1)}, bf16[2,48,4096]{2,1,0:T(8,128)(2,1)S(1)}, u32[]{:S(2)}, u32[]{:S(2)}) collective-permute-start(bf16[2,48,4096]{2,1,0:T(8,128)(2,1)S(1)} %pad_maximum_fusion.2), channel_id=1, source_target_pairs={{0,1},{1,0},{2,3},{3,2},{4,5},{5,4},{6,7},{7,6},{8,9},{9,8},{10,11... | collective-permute-start | bytes 2359304 | tf_op jit(solution)/shard_map/ppermute | solution.py:15
  163.4 11.6 %collective-permute-start.23 = (bf16[1,48,4096]{2,1,0:T(8,128)(2,1)S(1)}, bf16[1,48,4096]{2,1,0:T(8,128)(2,1)S(1)}, u32[]{:S(2)}, u32[]{:S(2)}) collective-permute-start(bf16[1,48,4096]{2,1,0:T(8,128)(2,1)S(1)} %get-tuple-element.7), channel_id=1, source_target_pairs={{0,6},{2,0},{4,2},{6,4},{1,7},{3,1},{5,3},{7,5},{8,14},{10,8},{12,... | collective-permute-start | bytes 1179656 | tf_op jit(solution)/shard_map/ppermute | solution.py:15
  163.8 11.2 %collective-permute-start.16 = (bf16[32,4096]{1,0:T(8,128)(2,1)S(1)}, bf16[32,4096]{1,0:T(8,128)(2,1)S(1)}, u32[]{:S(2)}, u32[]{:S(2)}) collective-permute-start(bf16[32,4096]{1,0:T(8,128)(2,1)S(1)} %slice.167), channel_id=1, source_target_pairs={{0,8},{8,16},{16,24},{24,0},{1,9},{9,17},{17,25},{25,1},{2,10},{10... | collective-permute-start | bytes 786440 | tf_op jit(solution)/shard_map/ppermute | solution.py:15
  175.2 2.4 %collective-permute-start.24 = (bf16[2,48,4096]{2,1,0:T(8,128)(2,1)S(1)}, bf16[2,48,4096]{2,1,0:T(8,128)(2,1)S(1)}, u32[]{:S(2)}, u32[]{:S(2)}) collective-permute-start(bf16[2,48,4096]{2,1,0:T(8,128)(2,1)S(1)} %pad_maximum_fusion.3), channel_id=1, source_target_pairs={{0,1},{1,0},{2,3},{3,2},{4,5},{5,4},{6,7},{7,6},{8,9},{9,8},{10,11... | collective-permute-start | bytes 2359304 | tf_op jit(solution)/shard_map/ppermute | solution.py:15
  177.9 3.3 %collective-permute-start.27 = (bf16[1,48,4096]{2,1,0:T(8,128)(2,1)S(1)}, bf16[1,48,4096]{2,1,0:T(8,128)(2,1)S(1)}, u32[]{:S(2)}, u32[]{:S(2)}) collective-permute-start(bf16[1,48,4096]{2,1,0:T(8,128)(2,1)S(1)} %get-tuple-element.17), channel_id=1, source_target_pairs={{0,1},{1,0},{2,3},{3,2},{4,5},{5,4},{6,7},{7,6},{8,9},{9,8},{10,11... | collective-permute-start | bytes 1179656 | tf_op jit(solution)/shard_map/ppermute | solution.py:15
  178.3 13.2 %collective-permute-start.25 = (bf16[1,48,4096]{2,1,0:T(8,128)(2,1)S(1)}, bf16[1,48,4096]{2,1,0:T(8,128)(2,1)S(1)}, u32[]{:S(2)}, u32[]{:S(2)}) collective-permute-start(bf16[1,48,4096]{2,1,0:T(8,128)(2,1)S(1)} %get-tuple-element.19), channel_id=1, source_target_pairs={{0,14},{2,8},{4,10},{6,12},{8,22},{10,16},{12,18},{14,20},{16,30},... | collective-permute-start | bytes 1179656 | tf_op jit(solution)/shard_map/ppermute | solution.py:214
  191.6 1.8 collective-permute-start.28
  192.2 30.5 %collective-permute-start.26 = (bf16[1,48,4096]{2,1,0:T(8,128)(2,1)S(1)}, bf16[1,48,4096]{2,1,0:T(8,128)(2,1)S(1)}, u32[]{:S(2)}, u32[]{:S(2)}) collective-permute-start(bf16[1,48,4096]{2,1,0:T(8,128)(2,1)S(1)} %get-tuple-element.18), channel_id=1, source_target_pairs={{0,12},{2,14},{4,8},{6,10},{8,20},{10,22},{12,16},{14,18},{16,28},... | collective-permute-start | bytes 1179656 | tf_op jit(solution)/shard_map/ppermute | solution.py:214
  193.5 29.9 %collective-permute-start.29 = (bf16[1,48,4096]{2,1,0:T(8,128)(2,1)S(1)}, bf16[1,48,4096]{2,1,0:T(8,128)(2,1)S(1)}, u32[]{:S(2)}, u32[]{:S(2)}) collective-permute-start(bf16[1,48,4096]{2,1,0:T(8,128)(2,1)S(1)} %fusion.36), channel_id=1, source_target_pairs={{0,10},{2,12},{4,14},{6,8},{8,18},{10,20},{12,22},{14,16},{16,26},... | collective-permute-start | bytes 1179656 | tf_op jit(solution)/shard_map/ppermute | solution.py:214

commit v7 on v5

v7 whole, which is shorter than its diff:
```python
import math

import jax
import jax.numpy as jnp
from jax import lax
from jax.sharding import PartitionSpec as P

QUERY_HEADS = 32
KEY_VALUE_HEADS = 2
HEAD_SIZE = 128


def shift(value, axis, by):
    devices = lax.axis_size(axis)
    return lax.ppermute(value, axis, [(i, (i + by) % devices) for i in range(devices)])


def attend_block(query_block, key_rows, value_rows, row_ids, col_ids):
    scores = jnp.einsum(
        "qhd,kd->hqk", query_block, key_rows, preferred_element_type=jnp.float32
    ) * (1.0 / math.sqrt(HEAD_SIZE))
    scores = jnp.where((col_ids[None, :] <= row_ids[:, None])[None, :, :], scores, -jnp.inf)
    attention_weights = jax.nn.softmax(scores, axis=-1).astype(jnp.bfloat16)
    attended = jnp.einsum(
        "hqk,kd->qhd", attention_weights, value_rows, preferred_element_type=jnp.float32
    )
    return attended.astype(jnp.bfloat16)


def mixed_halves(queries, keys_values, residual, out_weight, notes, slots_here):
    contexts, exps = lax.axis_size("ctx"), lax.axis_size("exp")
    me, my_exp = lax.axis_index("ctx"), lax.axis_index("exp")
    rows = queries.shape[0]
    width = residual.shape[1]
    local_heads = QUERY_HEADS // contexts
    group_width = local_heads * HEAD_SIZE

    note_rows = -(-len(notes[0]) // 16) * 16

    def pair_for(owner, k):
        head = owner * local_heads // (QUERY_HEADS // KEY_VALUE_HEADS)
        key = lax.dynamic_slice_in_dim(keys_values, head * HEAD_SIZE, HEAD_SIZE, 1)
        value = lax.dynamic_slice_in_dim(
            keys_values, (KEY_VALUE_HEADS + head) * HEAD_SIZE, HEAD_SIZE, 1
        )
        pair = jnp.concatenate([key, value], axis=1)
        note = jnp.pad(notes[k], ((0, note_rows - len(notes[k])), (0, 2 * HEAD_SIZE - rows)))
        return jnp.concatenate([pair, note], axis=0)

    def queries_for(owner):
        return lax.dynamic_slice_in_dim(queries, owner * group_width, group_width, 1)

    pairs = [pair_for(me, 0)]
    blocks = [queries_for(me)]
    for k in range(1, contexts):
        pairs.append(shift(pair_for((me + k) % contexts, k), "ctx", k))
    for k in range(1, contexts):
        outgoing = queries_for((me + k) % contexts)
        blocks.append(shift(outgoing, "ctx", k))
    if exps == 2:
        weights = [out_weight, shift(out_weight, "exp", 1)]
        first = my_exp * (width // 2)
    else:
        gathered = lax.all_gather(out_weight, "exp", axis=1, tiled=True)
        weights = [gathered[:, : width // 2], gathered[:, width // 2 :]]
        first = 0
    offsets = [first, width // 2 - first]

    arrived_notes = [pair[rows : rows + len(notes[0]), :rows] for pair in pairs]
    pair_rows = jnp.concatenate([pair[:rows] for pair in pairs], axis=0)
    key_rows, value_rows = pair_rows[:, :HEAD_SIZE], pair_rows[:, HEAD_SIZE:]
    within = jnp.arange(rows, dtype=jnp.int32)
    origins = [(me - k) % contexts * rows for k in range(contexts)]
    col_ids = jnp.concatenate([origin + within for origin in origins])

    held, next_slots = [None, None], None
    for k in [*range(1, contexts), 0]:
        attended = attend_block(
            blocks[k].reshape(rows, local_heads, HEAD_SIZE),
            key_rows,
            value_rows,
            origins[k] + within,
            col_ids,
        ).reshape(rows, group_width)
        if k == contexts - 1:
            follows = slots_here + held[0][0, 0].astype(jnp.float32) * 0.0
            next_slots = shift(follows, "pipe", 1)
        terms = []
        for half in range(2):
            term = jnp.dot(attended, weights[half], preferred_element_type=jnp.float32)
            if k == 0:
                own = lax.dynamic_slice_in_dim(residual, offsets[half], width // 2, 1)
                term = term + own.astype(jnp.float32)
            terms.append(lax.optimization_barrier(term))
        for half in range(2):
            term = terms[half]
            if held[half] is not None:
                term = term + held[half].astype(jnp.float32)
            if k == 0:
                held[half] = term + next_slots[0, 0] * 0.0
            else:
                held[half] = shift(term.astype(jnp.bfloat16), "ctx", 1)
    return held, first, arrived_notes, next_slots.astype(jnp.int32)


def on_device(
    queries,
    rotated_keys_values,
    residual,
    out_weight,
    norm_gain,
    in_weight,
    down_weight,
    routes,
    route_weight,
):
    contexts, exps = lax.axis_size("ctx"), lax.axis_size("exp")
    me, my_exp = lax.axis_index("ctx"), lax.axis_index("exp")
    token_rows = queries.shape[2]
    model_width = residual.shape[3]
    group_size = min(4, exps)
    per_context = exps // group_size
    experts = contexts * per_context
    capacity = min(
        token_rows,
        group_size
        * ((3 * token_rows + 2 * experts * group_size - 1) // (2 * experts * group_size)),
    )
    slots = experts * capacity
    expert_ids = routes[0, 0, :, 0]
    expert_hits = (expert_ids[:, None] == jnp.arange(experts, dtype=jnp.int32)[None, :]).astype(
        jnp.int32
    )
    position = jnp.sum((jnp.cumsum(expert_hits, axis=0) - 1) * expert_hits, axis=1)
    distance = (expert_ids // per_context - me) % contexts
    slot_index = (distance * per_context + expert_ids % per_context) * capacity + position
    slot_ids = jnp.arange(slots, dtype=jnp.int32)
    slot_match = (slot_ids[:, None] == slot_index[None, :]).astype(jnp.bfloat16)
    weights = route_weight[0, 0, :, 0]
    coarse = lax.reduce_precision(weights, exponent_bits=8, mantissa_bits=7)
    notes = []
    for k in range(contexts):
        local = slot_index - k * per_context * capacity
        local = jnp.where((local >= 0) & (local < per_context * capacity), local, -1)
        note = jnp.stack([coarse, weights - coarse, local.astype(jnp.float32)], axis=0)
        notes.append(note.astype(jnp.bfloat16))

    halves, first, arrived_notes, next_slots = mixed_halves(
        queries[0, 0],
        rotated_keys_values[0, 0],
        residual[0, 0],
        out_weight[0],
        notes,
        slot_index.astype(jnp.float32)[None, :],
    )
    mixed_rows = jnp.concatenate(halves, axis=1)
    if exps == 2:
        mixed_rows = jnp.where(first == 0, mixed_rows, jnp.concatenate(halves[::-1], axis=1))

    gain = norm_gain[0]
    scaled = (mixed_rows * gain).astype(jnp.bfloat16)
    packed = jnp.dot(slot_match, scaled, preferred_element_type=jnp.float32).astype(jnp.bfloat16)
    packed = packed.reshape(contexts, per_context, capacity, model_width)
    arrived = jnp.stack(
        [packed[0]] + [shift(packed[k], "ctx", k) for k in range(1, contexts)], axis=0
    )

    here = jnp.arange(per_context * capacity, dtype=jnp.float32)
    slot_weights = []
    for note in arrived_notes:
        note = note.astype(jnp.float32)
        hits = note[2][None, :] == here[:, None]
        slot_weights.append(jnp.sum(jnp.where(hits, note[0] + note[1], 0.0), axis=1))
    slot_weights = jnp.stack(slot_weights, axis=0).reshape(contexts, per_context, capacity, 1)

    def wanted_by(blocks, exp):
        if per_context == 1:
            return blocks[:, 0]
        return lax.dynamic_index_in_dim(blocks, exp // group_size, 1, keepdims=False)

    hidden_width = down_weight.shape[2]

    def expert_part(rows):
        rows = rows.reshape(-1, model_width)
        unscaled = rows.astype(jnp.float32) / gain
        mean_square = jnp.mean(unscaled * unscaled, axis=-1, keepdims=True)
        gate_up = jnp.dot(rows, in_weight[0, 0], preferred_element_type=jnp.float32)
        gate_up = gate_up * lax.rsqrt(mean_square + 1e-06)
        hidden = (jax.nn.silu(gate_up[:, :hidden_width]) * gate_up[:, hidden_width:]).astype(
            jnp.bfloat16
        )
        return jnp.dot(hidden, down_weight[0, 0], preferred_element_type=jnp.float32)

    others = [
        shift(wanted_by(arrived, (my_exp + k) % exps), "exp", k) for k in range(1, exps)
    ]
    own_part = expert_part(wanted_by(arrived, my_exp)).reshape(contexts, capacity, model_width)
    other_parts = expert_part(jnp.concatenate(others, axis=0)).astype(jnp.bfloat16)
    other_parts = other_parts.reshape(exps - 1, contexts, capacity, model_width)
    sums = [0.0] * per_context
    for k in range(exps):
        back = shift(other_parts[k - 1], "exp", -k).astype(jnp.float32) if k else own_part
        if per_context == 1:
            sums[0] = sums[0] + back
        else:
            place = (my_exp + k) % exps // group_size
            sums = [s + jnp.where(place == i, back, 0.0) for i, s in enumerate(sums)]
    finished = (
        arrived.astype(jnp.float32) / gain + slot_weights * jnp.stack(sums, axis=1)
    ).astype(jnp.bfloat16)

    def to_next_owner(rows, k):
        pipes = lax.axis_size("pipe")
        pairs = [
            (p * contexts + c, (p + 1) % pipes * contexts + (c - k) % contexts)
            for p in range(pipes)
            for c in range(contexts)
        ]
        return lax.ppermute(rows, ("pipe", "ctx"), pairs)

    returned = jnp.concatenate(
        [to_next_owner(finished[k], k).reshape(-1, model_width) for k in range(contexts)], axis=0
    )
    next_match = (slot_ids[None, :] == next_slots[0][:, None]).astype(jnp.bfloat16)
    layer = jnp.dot(next_match, returned, preferred_element_type=jnp.float32)
    return layer.astype(jnp.bfloat16).reshape(1, 1, token_rows, model_width)


def solution(mesh):
    placed = (
        P("pipe", "exp", "ctx", None),
        P("pipe", "exp", "ctx", None),
        P("pipe", "exp", "ctx", None),
        P("pipe", "ctx", "exp"),
        P("pipe", None),
        P("pipe", ("ctx", "exp"), None, None),
        P("pipe", ("ctx", "exp"), None, None),
        P("pipe", "exp", "ctx", None),
        P("pipe", "exp", "ctx", None),
    )
    return jax.shard_map(
        on_device,
        mesh=mesh,
        in_specs=placed,
        out_specs=P("pipe", "exp", "ctx", None),
        check_vma=False,
    )
```

time: 215 us -> 230 us (1.070)
  matrix products: 48 us -> 62.8 us
  starting transfers between devices: 35 us -> 41.6 us
  between operations: 7.87 us -> 1.36 us
  local copies, waits for them, and re-layouts: 11.1 us -> 5.5 us
  other arithmetic: 8.89 us -> 14.3 us
    dot_general x3 -> x2, matrix products: 3.65 us -> 10.3 us  [expert_part(): jnp.dot(hidden, down_weight[0, 0], preferred_element_type=jnp.float32)]
    ppermute x4, starting transfers between devices: 5.78 us -> 12.3 us  [to_next_owner(): return lax.ppermute(rows, ('pipe', 'ctx'), pairs)]
    slice x19 -> x5, local copies, waits for them, and re-layouts: 6.38 us -> 0.63 us  [the longest x1 0.51 us: mixed_halves(): follows = slots_here + held[0][0, 0].astype(jnp.float32) * 0.0]
    dot_general x8 -> x4, matrix products: 9.54 us -> 14.2 us  [the longest x2 12.1 us: expert_part(): gate_up = jnp.dot(rows, in_weight[0, 0], preferred_element_type=jnp.float32)]
    reduce_sum x1 -> x6, other arithmetic: 0.31 us -> 3.71 us  [the longest x4 2.07 us: on_device(): jnp.sum(jnp.where(hits, note[0] + note[1], 0.0), axis=1)]
    ppermute x24 -> x19, waiting for transfers between devices: 73.6 us -> 70.2 us  [shift(): lax.ppermute(value, axis, [(i, (i + by) % devices) for i in range(devices)])]
    convert_element_type x9, other arithmetic: 1.7 us -> 5.07 us  [the longest x4 2.62 us: on_device(): note = note.astype(jnp.float32)]
    ppermute x4, waiting for transfers between devices: 30.2 us -> 33.4 us  [to_next_owner(): return lax.ppermute(rows, ('pipe', 'ctx'), pairs)]
  transfers between devices with their start and end apart: 28 -> 23, of which waited for: 13 -> 10; matrix products, arithmetic and copies ran while one was open for 28% -> 23% of each run, Pallas kernels for 0% -> 0%
where the time goes in v7:
time: 230 us; the launch traced here: 229 us
  waiting for transfers between devices  104 us (45%)
  matrix products  62.8 us (27%)
  starting transfers between devices  41.6 us (18%)
  other arithmetic  14.3 us (6%)
  local copies, waits for them, and re-layouts  5.5 us (2%)
    ppermute x19, waiting for transfers between devices, shift(): lax.ppermute(value, axis, [(i, (i + by) % devices) for i in range(devices)])  70.2 us
    ppermute x4, waiting for transfers between devices, to_next_owner(): return lax.ppermute(rows, ('pipe', 'ctx'), pairs)  33.4 us
    ppermute x19, starting transfers between devices, shift(): lax.ppermute(value, axis, [(i, (i + by) % devices) for i in range(devices)])  29.3 us
    dot_general x8, matrix products, mixed_halves(): term = jnp.dot(attended, weights[half], preferred_element_type=jnp.float32)  24.5 us
    ppermute x4, starting transfers between devices, to_next_owner(): return lax.ppermute(rows, ('pipe', 'ctx'), pairs)  12.3 us
    dot_general x2, matrix products, expert_part(): gate_up = jnp.dot(rows, in_weight[0, 0], preferred_element_type=jnp.float32)  12.1 us
    dot_general x2, matrix products, expert_part(): jnp.dot(hidden, down_weight[0, 0], preferred_element_type=jnp.float32)  10.3 us
    dot_general x4, matrix products, attend_block(): jnp.einsum('hqk,kd->qhd', attention_weights, value_rows, preferred_elemen...  7.84 us
  transfers between devices with their start and end apart: 23, of which 10 were waited for; matrix products, arithmetic and copies ran while one was open for 23% of the time, Pallas kernels for 0%

profile of v7, /device:TPU:0, one launch (start us, length us, event | category | flops | bytes accessed | tf_op | source)
XLA Modules:
  0.0 229.2 jit_solution(14008532550607863435)
XLA Ops:
  0.0 0.8 fusion.69
  1.0 0.8 select_reduce_fusion
  1.8 0.7 fusion.96
  2.5 0.7 reduce-precision_convert_fusion
  3.2 0.6 maximum_convert_fusion
  3.8 1.0 dynamic-slice_bitcast_fusion.7
  4.8 3.1 %collective-permute-start = (bf16[144,256]{1,0:T(8,128)(2,1)S(1)}, bf16[144,256]{1,0:T(8,128)(2,1)S(1)}, u32[]{:S(2)}, u32[]{:S(2)}) collective-permute-start(bf16[144,256]{1,0:T(8,128)(2,1)S(1)} %fusion.65), channel_id=1, source_target_pairs={{0,2},{2,4},{4,6},{6,0},{1,3},{3,5},{5,7},{7,1},{8,10},{10,12},{12... | collective-permute-start | bytes 221192 | tf_op jit(solution)/shard_map/ppermute | solution.py:15
  7.9 2.7 %collective-permute-start.1 = (bf16[144,256]{1,0:T(8,128)(2,1)S(1)}, bf16[144,256]{1,0:T(8,128)(2,1)S(1)}, u32[]{:S(2)}, u32[]{:S(2)}) collective-permute-start(bf16[144,256]{1,0:T(8,128)(2,1)S(1)} %fusion.66), channel_id=1, source_target_pairs={{0,4},{2,6},{4,0},{6,2},{1,5},{3,7},{5,1},{7,3},{8,12},{10,14},{12... | collective-permute-start | bytes 221192 | tf_op jit(solution)/shard_map/ppermute | solution.py:15
  10.5 1.4 collective-permute-start.2
  12.2 0.7 collective-permute-start.4
  13.2 0.6 fusion.94
  14.0 0.9 copy.46
  15.0 1.2 collective-permute-start.3
  16.2 3.4 %collective-permute-start.8 = (bf16[128,1024]{0,1:T(8,128)(2,1)}, bf16[128,1024]{0,1:T(8,128)(2,1)}, u32[]{:S(2)}, u32[]{:S(2)}) collective-permute-start(bf16[128,1024]{0,1:T(8,128)(2,1)} %bitcast.35), channel_id=1, source_target_pairs={{0,6},{2,0},{4,2},{6,4},{1,7},{3,1},{5,3},{7,5},{8,14},{10,8},{12,... | collective-permute-start | bytes 786440 | tf_op jit(solution)/shard_map/ppermute | solution.py:15
  19.7 0.6 copy-done.13
  20.3 0.8 fusion.122
  21.1 1.0 convolution_convert_fusion.3
  22.3 2.9 %convolution_add_fusion.1 = f32[128,2048]{1,0:T(8,128)S(1)} fusion(bf16[128,1024]{0,1:T(8,128)(2,1)S(1)} %bitcast.245, bf16[1,1,128,4096]{3,2,1,0:T(8,128)(2,1)S(1)} %copy-done, s32[]{:T(128)S(6)} %select_n.266, bf16[1,1024,2048]{2,1,0:T(8,128)(2,1)} %param.12), kind=kOutput, calls=%fused_computation.22 | convolution fusion | flops 537395200 | bytes 6029316 | tf_op jit(solution)/shard_map/dot_general | solution.py:90
  25.3 1.7 fusion.125
  27.0 2.0 convolution_convert_fusion.4
  29.0 3.8 %fusion.103 = bf16[128,2048]{1,0:T(8,128)(2,1)} fusion(bf16[128,1024]{0,1:T(8,128)(2,1)S(1)} %bitcast.247, bf16[1,1024,2048]{2,1,0:T(8,128)(2,1)} %param.12), kind=kOutput, calls=%fused_computation.195 | convolution fusion | flops 536870912 | bytes 4980736 | tf_op jit(solution)/shard_map/dot_general | solution.py:90
  32.8 8.8 %collective-permute-start.5 = (bf16[128,2048]{1,0:T(8,128)(2,1)}, bf16[128,2048]{1,0:T(8,128)(2,1)}, u32[]{:S(2)}, u32[]{:S(2)}) collective-permute-start(bf16[128,2048]{1,0:T(8,128)(2,1)} %fusion.103), channel_id=1, source_target_pairs={{0,2},{2,4},{4,6},{6,0},{1,3},{3,5},{5,7},{7,1},{8,10},{10,12},{12... | collective-permute-start | bytes 1572872 | tf_op jit(solution)/shard_map/ppermute | solution.py:15
  41.6 1.7 fusion.124
  43.3 2.7 %convolution_convert_fusion.5 = bf16[128,8,128]{2,0,1:T(8,128)(2,1)} fusion(f32[8,128]{1,0:T(8,128)S(1)} %fusion.124, bf16[512,256]{1,0:T(8,128)(2,1)S(1)} %pad_maximum_fusion.1, pred[128,512]{0,1:T(8,128)(4,1)S(1)} %get-tuple-element.41, bf16[128,8,128]{0,2,1:T(8,128)(2,1)} %bitcast.15), kind=kOutput, calls=%fused_computation.53 | convolution fusion | flops 271189504 | bytes 856064 | tf_op jit(solution)/shard_map/hqk,kd->qhd/dot_general | solution.py:24
  46.0 3.0 %fusion.105 = f32[128,2048]{1,0:T(8,128)S(1)} fusion(bf16[128,1024]{0,1:T(8,128)(2,1)} %bitcast.251, bf16[1,1024,2048]{2,1,0:T(8,128)(2,1)} %param.12), kind=kOutput, calls=%fused_computation.197 | convolution fusion | flops 536870912 | bytes 5505024 | tf_op jit(solution)/shard_map/dot_general | solution.py:90
  49.1 1.8 fusion.123
  50.8 2.3 collective-permute-done.5
  53.1 1.9 add_convert_fusion.4
  55.0 2.5 %collective-permute-start.6 = (bf16[128,2048]{1,0:T(8,128)(2,1)}, bf16[128,2048]{1,0:T(8,128)(2,1)S(1)}, u32[]{:S(2)}, u32[]{:S(2)}) collective-permute-start(bf16[128,2048]{1,0:T(8,128)(2,1)} %add_convert_fusion.4), channel_id=1, source_target_pairs={{0,2},{2,4},{4,6},{6,0},{1,3},{3,5},{5,7},{7,1},{8,10},{10,12},{12... | collective-permute-start | bytes 1572872 | tf_op jit(solution)/shard_map/ppermute | solution.py:15
  57.5 2.1 convolution_convert_fusion.2
  59.7 3.0 %fusion.100 = f32[128,2048]{1,0:T(8,128)S(1)} fusion(bf16[128,1024]{0,1:T(8,128)(2,1)S(1)} %bitcast.249, bf16[1,1024,2048]{2,1,0:T(8,128)(2,1)} %param.12), kind=kOutput, calls=%fused_computation.192 | convolution fusion | flops 536870912 | bytes 5505024 | tf_op jit(solution)/shard_map/dot_general | solution.py:90
  62.6 7.2 %collective-permute-done.6 = bf16[128,2048]{1,0:T(8,128)(2,1)S(1)} collective-permute-done((bf16[128,2048]{1,0:T(8,128)(2,1)}, bf16[128,2048]{1,0:T(8,128)(2,1)S(1)}, u32[]{:S(2)}, u32[]{:S(2)}) %collective-permute-start.6) | collective-permute-done | bytes 524320 | tf_op jit(solution)/shard_map/ppermute | solution.py:15
  71.0 3.0 %fusion.128 = bf16[128,2048]{1,0:T(8,128)(2,1)S(1)} fusion(bf16[128,1024]{0,1:T(8,128)(2,1)S(1)} %bitcast.248, bf16[1024,2048]{1,0:T(8,128)(2,1)} %collective-permute-done.10), kind=kOutput, calls=%fused_computation.215 | convolution fusion | flops 536870912 | bytes 4980736 | tf_op jit(solution)/shard_map/dot_general | solution.py:90
  74.0 0.7 collective-permute-start.11
  75.1 2.9 %fusion.127 = f32[128,2048]{1,0:T(8,128)S(1)} fusion(bf16[128,1024]{0,1:T(8,128)(2,1)S(1)} %bitcast.252, bf16[1024,2048]{1,0:T(8,128)(2,1)} %collective-permute-done.10), kind=kOutput, calls=%fused_computation.214 | convolution fusion | flops 536870912 | bytes 5505024 | tf_op jit(solution)/shard_map/dot_general | solution.py:90
  78.0 9.7 %collective-permute-done.11 = bf16[128,2048]{1,0:T(8,128)(2,1)S(1)} collective-permute-done((bf16[128,2048]{1,0:T(8,128)(2,1)S(1)}, bf16[128,2048]{1,0:T(8,128)(2,1)S(1)}, u32[]{:S(2)}, u32[]{:S(2)}) %collective-permute-start.11) | collective-permute-done | bytes 524320 | tf_op jit(solution)/shard_map/ppermute | solution.py:15
  88.2 2.9 %fusion.126 = f32[128,2048]{1,0:T(8,128)S(1)} fusion(bf16[128,1024]{0,1:T(8,128)(2,1)S(1)} %bitcast.250, bf16[1024,2048]{1,0:T(8,128)(2,1)} %collective-permute-done.10), kind=kOutput, calls=%fused_computation.213 | convolution fusion | flops 536870912 | bytes 5505024 | tf_op jit(solution)/shard_map/dot_general | solution.py:90
  91.1 13.4 %collective-permute-done.12 = bf16[128,2048]{1,0:T(8,128)(2,1)S(1)} collective-permute-done((bf16[128,2048]{1,0:T(8,128)(2,1)S(1)}, bf16[128,2048]{1,0:T(8,128)(2,1)S(1)}, u32[]{:S(2)}, u32[]{:S(2)}) %collective-permute-start.12) | collective-permute-done | bytes 524320 | tf_op jit(solution)/shard_map/ppermute | solution.py:15
  104.7 11.1 %collective-permute-done.9 = bf16[128,2048]{1,0:T(8,128)(2,1)S(1)} collective-permute-done((bf16[128,2048]{1,0:T(8,128)(2,1)S(1)}, bf16[128,2048]{1,0:T(8,128)(2,1)S(1)}, u32[]{:S(2)}, u32[]{:S(2)}) %collective-permute-start.9) | collective-permute-done | bytes 524320 | tf_op jit(solution)/shard_map/ppermute | solution.py:15
  115.9 2.9 %convolution_add_fusion = f32[128,2048]{1,0:T(8,128)S(1)} fusion(bf16[128,1024]{0,1:T(8,128)(2,1)S(1)} %bitcast.246, bf16[1024,2048]{1,0:T(8,128)(2,1)} %collective-permute-done.10, bf16[1,1,128,4096]{3,2,1,0:T(8,128)(2,1)S(1)} %copy-done, s32[]{:T(128)S(6)} %select_n.269), kind=kOutput, calls=%fused_computation.21 | convolution fusion | flops 537395200 | bytes 6029316 | tf_op jit(solution)/shard_map/dot_general | solution.py:90
  118.9 4.2 %collective-permute-done.13 = bf16[128,2048]{1,0:T(8,128)(2,1)S(1)} collective-permute-done((bf16[128,2048]{1,0:T(8,128)(2,1)S(1)}, bf16[128,2048]{1,0:T(8,128)(2,1)S(1)}, u32[]{:S(2)}, u32[]{:S(2)}) %collective-permute-start.13) | collective-permute-done | bytes 524320 | tf_op jit(solution)/shard_map/ppermute | solution.py:15
  123.3 0.6 convolution_convert_fusion
  124.2 3.7 %collective-permute-start.16 = (bf16[1,48,4096]{2,1,0:T(8,128)(2,1)S(1)}, bf16[1,48,4096]{2,1,0:T(8,128)(2,1)S(1)}, u32[]{:S(2)}, u32[]{:S(2)}) collective-permute-start(bf16[1,48,4096]{2,1,0:T(8,128)(2,1)S(1)} %get-tuple-element.15), channel_id=1, source_target_pairs={{0,6},{2,0},{4,2},{6,4},{1,7},{3,1},{5,3},{7,5},{8,14},{10,8},{12,... | collective-permute-start | bytes 1179656 | tf_op jit(solution)/shard_map/ppermute | solution.py:15
  127.9 10.1 %collective-permute-done.14 = bf16[1,48,4096]{2,1,0:T(8,128)(2,1)S(1)} collective-permute-done((bf16[1,48,4096]{2,1,0:T(8,128)(2,1)S(1)}, bf16[1,48,4096]{2,1,0:T(8,128)(2,1)S(1)}, u32[]{:S(2)}, u32[]{:S(2)}) %collective-permute-start.14) | collective-permute-done | bytes 393248 | tf_op jit(solution)/shard_map/ppermute | solution.py:15
  138.0 12.2 %collective-permute-done.15 = bf16[1,48,4096]{2,1,0:T(8,128)(2,1)S(1)} collective-permute-done((bf16[1,48,4096]{2,1,0:T(8,128)(2,1)S(1)}, bf16[1,48,4096]{2,1,0:T(8,128)(2,1)S(1)}, u32[]{:S(2)}, u32[]{:S(2)}) %collective-permute-start.15) | collective-permute-done | bytes 393248 | tf_op jit(solution)/shard_map/ppermute | solution.py:15
  150.2 1.1 multiply_reduce_fusion.1
  151.4 0.7 select_reduce_fusion.4
  152.1 0.7 slice_convert_fusion.2
  152.8 0.7 select_reduce_fusion.3
  153.4 0.7 slice_convert_fusion.1
  154.1 0.6 select_reduce_fusion.2
  154.7 0.7 slice_convert_fusion
  156.5 0.6 add_rsqrt_fusion
  157.1 1.3 rsqrt.25
  158.4 6.0 %fusion.19 = f32[192,1536]{1,0:T(8,128)S(1)} fusion(bf16[192,4096]{1,0:T(8,128)(2,1)S(1)} %bitcast.242, bf16[1,1,4096,1536]{3,2,1,0:T(8,128)(2,1)} %param.14, f32[192]{0:T(256)} %rsqrt.25), kind=kOutput, calls=%fused_computation.20 | convolution fusion | flops 2416214016 | bytes 15336192 | tf_op jit(solution)/shard_map/dot_general | solution.py:187
  164.5 5.4 %fusion.12 = bf16[192,4096]{1,0:T(8,128)(2,1)} fusion(bf16[1,1,768,4096]{3,2,1,0:T(8,128)(2,1)} %param.15, f32[192,1536]{1,0:T(8,128)S(1)} %fusion.19), kind=kOutput, calls=%fused_computation.12 | convolution fusion | flops 1209630720 | bytes 9043968 | tf_op jit(solution)/shard_map/dot_general | solution.py:192
  170.6 6.1 %fusion.16 = f32[192,1536]{1,0:T(8,128)S(1)} fusion(bf16[192,4096]{1,0:T(8,128)(2,1)S(1)} %bitcast.244, bf16[1,1,4096,1536]{3,2,1,0:T(8,128)(2,1)} %param.14, f32[192]{0:T(256)S(1)} %rsqrt.23), kind=kOutput, calls=%fused_computation.19 | convolution fusion | flops 2416214016 | bytes 15336192 | tf_op jit(solution)/shard_map/dot_general | solution.py:187
  177.0 4.9 %add_convert_fusion = bf16[4,48,4096]{2,1,0:T(8,128)(2,1)S(1)} fusion(bf16[4,48,4096]{2,1,0:T(8,128)(2,1)} %collective-permute-done.18, bf16[1,48,4096]{2,1,0:T(8,128)(2,1)S(1)} %copy-done.10, bf16[1,48,4096]{2,1,0:T(8,128)(2,1)S(1)} %copy-done.8, bf16[1,48,4096]{2,1,0:T(8,128)(2,1)S(1)} %copy-done.6, bf16[1,48,4096]{2,1,0:T(8,128)(2,1)S(1)} %get-tuple-element.13, ...), kind=kOutput, calls=%fused_computation.16 | convolution fusion | flops 1215823872 | bytes 11322112 | tf_op jit(solution)/shard_map/dot_general | solution.py:192
  182.1 5.4 %collective-permute-start.20 = (bf16[1,48,4096]{2,1,0:T(8,128)(2,1)S(1)}, bf16[1,48,4096]{2,1,0:T(8,128)(2,1)S(1)}, u32[]{:S(2)}, u32[]{:S(2)}) collective-permute-start(bf16[1,48,4096]{2,1,0:T(8,128)(2,1)S(1)} %get-tuple-element.12), channel_id=1, source_target_pairs={{0,14},{2,8},{4,10},{6,12},{8,22},{10,16},{12,18},{14,20},{16,30},... | collective-permute-start | bytes 1179656 | tf_op jit(solution)/shard_map/ppermute | solution.py:219
  187.5 3.8 %collective-permute-start.21 = (bf16[1,48,4096]{2,1,0:T(8,128)(2,1)S(1)}, bf16[1,48,4096]{2,1,0:T(8,128)(2,1)S(1)}, u32[]{:S(2)}, u32[]{:S(2)}) collective-permute-start(bf16[1,48,4096]{2,1,0:T(8,128)(2,1)S(1)} %get-tuple-element.11), channel_id=1, source_target_pairs={{0,12},{2,14},{4,8},{6,10},{8,20},{10,22},{12,16},{14,18},{16,28},... | collective-permute-start | bytes 1179656 | tf_op jit(solution)/shard_map/ppermute | solution.py:219
  191.4 3.0 %collective-permute-start.22 = (bf16[1,48,4096]{2,1,0:T(8,128)(2,1)S(1)}, bf16[1,48,4096]{2,1,0:T(8,128)(2,1)S(1)}, u32[]{:S(2)}, u32[]{:S(2)}) collective-permute-start(bf16[1,48,4096]{2,1,0:T(8,128)(2,1)S(1)} %get-tuple-element.10), channel_id=1, source_target_pairs={{0,10},{2,12},{4,14},{6,8},{8,18},{10,20},{12,22},{14,16},{16,26},... | collective-permute-start | bytes 1179656 | tf_op jit(solution)/shard_map/ppermute | solution.py:219
  194.4 8.1 %collective-permute-done.19 = bf16[1,48,4096]{2,1,0:T(8,128)(2,1)S(1)} collective-permute-done((bf16[1,48,4096]{2,1,0:T(8,128)(2,1)S(1)}, bf16[1,48,4096]{2,1,0:T(8,128)(2,1)S(1)}, u32[]{:S(2)}, u32[]{:S(2)}) %collective-permute-start.19) | collective-permute-done | bytes 393248 | tf_op jit(solution)/shard_map/ppermute | solution.py:219
  202.5 25.3 %collective-permute-done.21 = bf16[1,48,4096]{2,1,0:T(8,128)(2,1)S(1)} collective-permute-done((bf16[1,48,4096]{2,1,0:T(8,128)(2,1)S(1)}, bf16[1,48,4096]{2,1,0:T(8,128)(2,1)S(1)}, u32[]{:S(2)}, u32[]{:S(2)}) %collective-permute-start.21) | collective-permute-done | bytes 393248 | tf_op jit(solution)/shard_map/ppermute | solution.py:219
  227.8 1.5 fusion.15
  (113 shorter events, 5.5 us)
Async XLA Ops:
  0.0 11.9 %copy-start.3 = (bf16[1,1,128,4096]{3,2,1,0:T(8,128)(2,1)S(1)}, bf16[1,1,128,4096]{3,2,1,0:T(8,128)(2,1)}, u32[]{:S(2)}) copy-start(bf16[1,1,128,4096]{3,2,1,0:T(8,128)(2,1)} %param.9) | copy-start | bytes 3145732
  0.8 12.4 %copy-start.16 = (s32[1,1,128,1]{2,3,1,0:T(1,128)S(1)}, s32[1,1,128,1]{2,3,1,0:T(1,128)}, u32[]{:S(2)}) copy-start(s32[1,1,128,1]{2,3,1,0:T(1,128)} %param.16) | copy-start | bytes 1540
  4.8 10.2 %collective-permute-start = (bf16[144,256]{1,0:T(8,128)(2,1)S(1)}, bf16[144,256]{1,0:T(8,128)(2,1)S(1)}, u32[]{:S(2)}, u32[]{:S(2)}) collective-permute-start(bf16[144,256]{1,0:T(8,128)(2,1)S(1)} %fusion.65), channel_id=1, source_target_pairs={{0,2},{2,4},{4,6},{6,0},{1,3},{3,5},{5,7},{7,1},{8,10},{10,12},{12... | collective-permute-start | bytes 221192 | tf_op jit(solution)/shard_map/ppermute | solution.py:15
  7.9 8.3 %collective-permute-start.1 = (bf16[144,256]{1,0:T(8,128)(2,1)S(1)}, bf16[144,256]{1,0:T(8,128)(2,1)S(1)}, u32[]{:S(2)}, u32[]{:S(2)}) collective-permute-start(bf16[144,256]{1,0:T(8,128)(2,1)S(1)} %fusion.66), channel_id=1, source_target_pairs={{0,4},{2,6},{4,0},{6,2},{1,5},{3,7},{5,1},{7,3},{8,12},{10,14},{12... | collective-permute-start | bytes 221192 | tf_op jit(solution)/shard_map/ppermute | solution.py:15
  10.5 9.1 %collective-permute-start.2 = (bf16[144,256]{1,0:T(8,128)(2,1)S(1)}, bf16[144,256]{1,0:T(8,128)(2,1)S(1)}, u32[]{:S(2)}, u32[]{:S(2)}) collective-permute-start(bf16[144,256]{1,0:T(8,128)(2,1)S(1)} %fusion.67), channel_id=1, source_target_pairs={{0,6},{2,0},{4,2},{6,4},{1,7},{3,1},{5,3},{7,5},{8,14},{10,8},{12,... | collective-permute-start | bytes 221192 | tf_op jit(solution)/shard_map/ppermute | solution.py:15
  12.2 13.1 %collective-permute-start.4 = (bf16[128,1024]{0,1:T(8,128)(2,1)S(1)}, bf16[128,1024]{0,1:T(8,128)(2,1)}, u32[]{:S(2)}, u32[]{:S(2)}) collective-permute-start(bf16[128,1024]{0,1:T(8,128)(2,1)S(1)} %bitcast.257), channel_id=1, source_target_pairs={{0,2},{2,4},{4,6},{6,0},{1,3},{3,5},{5,7},{7,1},{8,10},{10,12},{12... | collective-permute-start | bytes 786440 | tf_op jit(solution)/shard_map/ppermute | solution.py:15
  12.9 58.1 %collective-permute-start.10 = (bf16[1024,2048]{1,0:T(8,128)(2,1)}, bf16[1024,2048]{1,0:T(8,128)(2,1)}, u32[]{:S(2)}, u32[]{:S(2)}) collective-permute-start(bf16[1024,2048]{1,0:T(8,128)(2,1)} %bitcast.241), channel_id=1, source_target_pairs={{0,1},{1,0},{2,3},{3,2},{4,5},{5,4},{6,7},{7,6},{8,9},{9,8},{10,11... | collective-permute-start | bytes 12582920 | tf_op jit(solution)/shard_map/ppermute | solution.py:15
  15.0 6.1 %copy-start.15 = (bf16[144,256]{1,0:T(8,128)(2,1)}, bf16[144,256]{1,0:T(8,128)(2,1)S(1)}, u32[]{:S(2)}) copy-start(bf16[144,256]{1,0:T(8,128)(2,1)S(1)} %collective-permute-done) | copy-start | bytes 221188
  15.0 26.6 %collective-permute-start.3 = (bf16[128,1024]{0,1:T(8,128)(2,1)S(1)}, bf16[128,1024]{0,1:T(8,128)(2,1)}, u32[]{:S(2)}, u32[]{:S(2)}) collective-permute-start(bf16[128,1024]{0,1:T(8,128)(2,1)S(1)} %bitcast.258), channel_id=1, source_target_pairs={{0,4},{2,6},{4,0},{6,2},{1,5},{3,7},{5,1},{7,3},{8,12},{10,14},{12... | collective-permute-start | bytes 786440 | tf_op jit(solution)/shard_map/ppermute | solution.py:15
  16.2 3.5 %copy-start.14 = (bf16[144,256]{1,0:T(8,128)(2,1)}, bf16[144,256]{1,0:T(8,128)(2,1)S(1)}, u32[]{:S(2)}) copy-start(bf16[144,256]{1,0:T(8,128)(2,1)S(1)} %collective-permute-done.1) | copy-start | bytes 221188
  16.2 32.8 %collective-permute-start.8 = (bf16[128,1024]{0,1:T(8,128)(2,1)}, bf16[128,1024]{0,1:T(8,128)(2,1)}, u32[]{:S(2)}, u32[]{:S(2)}) collective-permute-start(bf16[128,1024]{0,1:T(8,128)(2,1)} %bitcast.35), channel_id=1, source_target_pairs={{0,6},{2,0},{4,2},{6,4},{1,7},{3,1},{5,3},{7,5},{8,14},{10,8},{12,... | collective-permute-start | bytes 786440 | tf_op jit(solution)/shard_map/ppermute | solution.py:15
  19.7 0.6 copy-start.13
  20.3 23.0 %copy-start.11 = (bf16[512,256]{1,0:T(8,128)(2,1)}, bf16[512,256]{1,0:T(8,128)(2,1)S(1)}, u32[]{:S(2)}) copy-start(bf16[512,256]{1,0:T(8,128)(2,1)S(1)} %pad_maximum_fusion.1) | copy-start | bytes 786436
  21.1 1.2 copy-start
  29.0 3.8 %copy-start.1 = (bf16[128,8,128]{2,0,1:T(8,128)(2,1)}, bf16[128,8,128]{2,0,1:T(8,128)(2,1)S(1)}, u32[]{:S(2)}) copy-start(bf16[128,8,128]{2,0,1:T(8,128)(2,1)S(1)} %convolution_convert_fusion.4) | copy-start | bytes 786436
  32.8 20.3 %collective-permute-start.5 = (bf16[128,2048]{1,0:T(8,128)(2,1)}, bf16[128,2048]{1,0:T(8,128)(2,1)}, u32[]{:S(2)}, u32[]{:S(2)}) collective-permute-start(bf16[128,2048]{1,0:T(8,128)(2,1)} %fusion.103), channel_id=1, source_target_pairs={{0,2},{2,4},{4,6},{6,0},{1,3},{3,5},{5,7},{7,1},{8,10},{10,12},{12... | collective-permute-start | bytes 1572872 | tf_op jit(solution)/shard_map/ppermute | solution.py:15
  55.0 14.8 %collective-permute-start.6 = (bf16[128,2048]{1,0:T(8,128)(2,1)}, bf16[128,2048]{1,0:T(8,128)(2,1)S(1)}, u32[]{:S(2)}, u32[]{:S(2)}) collective-permute-start(bf16[128,2048]{1,0:T(8,128)(2,1)} %add_convert_fusion.4), channel_id=1, source_target_pairs={{0,2},{2,4},{4,6},{6,0},{1,3},{3,5},{5,7},{7,1},{8,10},{10,12},{12... | collective-permute-start | bytes 1572872 | tf_op jit(solution)/shard_map/ppermute | solution.py:15
  59.7 11.4 %copy-start.2 = (bf16[128,8,128]{2,0,1:T(8,128)(2,1)S(1)}, bf16[128,8,128]{2,0,1:T(8,128)(2,1)}, u32[]{:S(2)}) copy-start(bf16[128,8,128]{2,0,1:T(8,128)(2,1)} %copy-done.1) | copy-start | bytes 786436
  71.0 4.1 %copy-start.4 = (bf16[128,8,128]{2,0,1:T(8,128)(2,1)S(1)}, bf16[128,8,128]{2,0,1:T(8,128)(2,1)}, u32[]{:S(2)}) copy-start(bf16[128,8,128]{2,0,1:T(8,128)(2,1)} %convolution_convert_fusion.5) | copy-start | bytes 786436
  74.0 13.7 %collective-permute-start.11 = (bf16[128,2048]{1,0:T(8,128)(2,1)S(1)}, bf16[128,2048]{1,0:T(8,128)(2,1)S(1)}, u32[]{:S(2)}, u32[]{:S(2)}) collective-permute-start(bf16[128,2048]{1,0:T(8,128)(2,1)S(1)} %fusion.128), channel_id=1, source_target_pairs={{0,2},{2,4},{4,6},{6,0},{1,3},{3,5},{5,7},{7,1},{8,10},{10,12},{12... | collective-permute-start | bytes 1572872 | tf_op jit(solution)/shard_map/ppermute | solution.py:15
  74.8 13.4 %collective-permute-start.7 = (f32[1,128]{1,0:T(1,128)S(1)}, f32[1,128]{1,0:T(1,128)S(1)}, u32[]{:S(2)}, u32[]{:S(2)}) collective-permute-start(f32[1,128]{1,0:T(1,128)S(1)} %convert_add_fusion), channel_id=1, source_target_pairs={{0,8},{8,16},{16,24},{24,0},{1,9},{9,17},{17,25},{25,1},{2,10},{10... | collective-permute-start | bytes 1544 | tf_op jit(solution)/shard_map/ppermute | solution.py:15
  87.8 16.7 %collective-permute-start.12 = (bf16[128,2048]{1,0:T(8,128)(2,1)S(1)}, bf16[128,2048]{1,0:T(8,128)(2,1)S(1)}, u32[]{:S(2)}, u32[]{:S(2)}) collective-permute-start(bf16[128,2048]{1,0:T(8,128)(2,1)S(1)} %add_convert_fusion.2), channel_id=1, source_target_pairs={{0,2},{2,4},{4,6},{6,0},{1,3},{3,5},{5,7},{7,1},{8,10},{10,12},{12... | collective-permute-start | bytes 1572872 | tf_op jit(solution)/shard_map/ppermute | solution.py:15
  88.0 27.7 %collective-permute-start.9 = (bf16[128,2048]{1,0:T(8,128)(2,1)S(1)}, bf16[128,2048]{1,0:T(8,128)(2,1)S(1)}, u32[]{:S(2)}, u32[]{:S(2)}) collective-permute-start(bf16[128,2048]{1,0:T(8,128)(2,1)S(1)} %add_convert_fusion.3), channel_id=1, source_target_pairs={{0,2},{2,4},{4,6},{6,0},{1,3},{3,5},{5,7},{7,1},{8,10},{10,12},{12... | collective-permute-start | bytes 1572872 | tf_op jit(solution)/shard_map/ppermute | solution.py:15
  88.1 3.0 %copy-start.25 = (f32[1,128]{1,0:T(1,128)}, f32[1,128]{1,0:T(1,128)S(1)}, u32[]{:S(2)}) copy-start(f32[1,128]{1,0:T(1,128)S(1)} %collective-permute-done.7) | copy-start | bytes 1540
  104.7 18.4 %collective-permute-start.13 = (bf16[128,2048]{1,0:T(8,128)(2,1)S(1)}, bf16[128,2048]{1,0:T(8,128)(2,1)S(1)}, u32[]{:S(2)}, u32[]{:S(2)}) collective-permute-start(bf16[128,2048]{1,0:T(8,128)(2,1)S(1)} %add_convert_fusion.1), channel_id=1, source_target_pairs={{0,2},{2,4},{4,6},{6,0},{1,3},{3,5},{5,7},{7,1},{8,10},{10,12},{12... | collective-permute-start | bytes 1572872 | tf_op jit(solution)/shard_map/ppermute | solution.py:15
  118.9 4.4 %copy-start.12 = (f32[1,4096]{1,0:T(1,128)S(1)}, f32[1,4096]{1,0:T(1,128)}, u32[]{:S(2)}) copy-start(f32[1,4096]{1,0:T(1,128)} %param.13) | copy-start | bytes 49156
  118.9 4.4 %copy-start.21 = (s32[128]{0:T(128)S(1)}, s32[128]{0:T(128)}, u32[]{:S(2)}) copy-start(s32[128]{0:T(128)} %fusion.94) | copy-start | bytes 1540
  123.9 4.1 %copy-start.18 = (f32[3,128]{1,0:T(4,128)S(1)}, f32[3,128]{1,0:T(4,128)}, u32[]{:S(2)}) copy-start(f32[3,128]{1,0:T(4,128)} %get-tuple-element.42) | copy-start | bytes 4612
  124.0 14.0 %collective-permute-start.14 = (bf16[1,48,4096]{2,1,0:T(8,128)(2,1)S(1)}, bf16[1,48,4096]{2,1,0:T(8,128)(2,1)S(1)}, u32[]{:S(2)}, u32[]{:S(2)}) collective-permute-start(bf16[1,48,4096]{2,1,0:T(8,128)(2,1)S(1)} %get-tuple-element.17), channel_id=1, source_target_pairs={{0,2},{2,4},{4,6},{6,0},{1,3},{3,5},{5,7},{7,1},{8,10},{10,12},{12... | collective-permute-start | bytes 1179656 | tf_op jit(solution)/shard_map/ppermute | solution.py:15
  124.1 26.1 %collective-permute-start.15 = (bf16[1,48,4096]{2,1,0:T(8,128)(2,1)S(1)}, bf16[1,48,4096]{2,1,0:T(8,128)(2,1)S(1)}, u32[]{:S(2)}, u32[]{:S(2)}) collective-permute-start(bf16[1,48,4096]{2,1,0:T(8,128)(2,1)S(1)} %get-tuple-element.16), channel_id=1, source_target_pairs={{0,4},{2,6},{4,0},{6,2},{1,5},{3,7},{5,1},{7,3},{8,12},{10,14},{12... | collective-permute-start | bytes 1179656 | tf_op jit(solution)/shard_map/ppermute | solution.py:15
  124.2 26.0 %collective-permute-start.16 = (bf16[1,48,4096]{2,1,0:T(8,128)(2,1)S(1)}, bf16[1,48,4096]{2,1,0:T(8,128)(2,1)S(1)}, u32[]{:S(2)}, u32[]{:S(2)}) collective-permute-start(bf16[1,48,4096]{2,1,0:T(8,128)(2,1)S(1)} %get-tuple-element.15), channel_id=1, source_target_pairs={{0,6},{2,0},{4,2},{6,4},{1,7},{3,1},{5,3},{7,5},{8,14},{10,8},{12,... | collective-permute-start | bytes 1179656 | tf_op jit(solution)/shard_map/ppermute | solution.py:15
  138.0 13.3 %copy-start.5 = (bf16[1,48,4096]{2,1,0:T(8,128)(2,1)}, bf16[1,48,4096]{2,1,0:T(8,128)(2,1)S(1)}, u32[]{:S(2)}) copy-start(bf16[1,48,4096]{2,1,0:T(8,128)(2,1)S(1)} %collective-permute-done.14) | copy-start | bytes 1179652
  150.2 1.2 copy-start.7
  150.2 1.2 copy-start.9
  151.4 4.6 %collective-permute-start.17 = (bf16[4,48,4096]{2,1,0:T(8,128)(2,1)S(1)}, bf16[4,48,4096]{2,1,0:T(8,128)(2,1)S(1)}, u32[]{:S(2)}, u32[]{:S(2)}) collective-permute-start(bf16[4,48,4096]{2,1,0:T(8,128)(2,1)S(1)} %bitcast.243), channel_id=1, source_target_pairs={{0,1},{1,0},{2,3},{3,2},{4,5},{5,4},{6,7},{7,6},{8,9},{9,8},{10,11... | collective-permute-start | bytes 4718600 | tf_op jit(solution)/shard_map/ppermute | solution.py:15
  164.4 5.9 %copy-start.19 = (f32[128]{0:T(128)S(1)}, f32[128]{0:T(128)}, u32[]{:S(2)}) copy-start(f32[128]{0:T(128)} %get-tuple-element.36) | copy-start | bytes 1540
  164.4 5.9 %copy-start.20 = (f32[128]{0:T(128)S(1)}, f32[128]{0:T(128)}, u32[]{:S(2)}) copy-start(f32[128]{0:T(128)} %get-tuple-element.37) | copy-start | bytes 1540
  164.4 6.0 %copy-start.22 = (f32[48]{0:T(128)S(1)}, f32[48]{0:T(128)}, u32[]{:S(2)}) copy-start(f32[48]{0:T(128)} %select_reduce_fusion.4) | copy-start | bytes 580
  164.5 6.0 %copy-start.23 = (f32[48]{0:T(128)S(1)}, f32[48]{0:T(128)}, u32[]{:S(2)}) copy-start(f32[48]{0:T(128)} %select_reduce_fusion.3) | copy-start | bytes 580
  164.5 6.0 %copy-start.24 = (f32[48]{0:T(128)S(1)}, f32[48]{0:T(128)}, u32[]{:S(2)}) copy-start(f32[48]{0:T(128)} %select_reduce_fusion.2) | copy-start | bytes 580
  164.5 6.0 %copy-start.17 = (f32[4,48]{1,0:T(4,128)S(1)}, f32[4,48]{1,0:T(4,128)}, u32[]{:S(2)}) copy-start(f32[4,48]{1,0:T(4,128)} %get-tuple-element.7) | copy-start | bytes 2308
  169.9 7.1 %collective-permute-start.18 = (bf16[4,48,4096]{2,1,0:T(8,128)(2,1)}, bf16[4,48,4096]{2,1,0:T(8,128)(2,1)}, u32[]{:S(2)}, u32[]{:S(2)}) collective-permute-start(bf16[4,48,4096]{2,1,0:T(8,128)(2,1)} %bitcast.74), channel_id=1, source_target_pairs={{0,1},{1,0},{2,3},{3,2},{4,5},{5,4},{6,7},{7,6},{8,9},{9,8},{10,11... | collective-permute-start | bytes 4718600 | tf_op jit(solution)/shard_map/ppermute | solution.py:15
  170.6 6.3 %copy-start.6 = (bf16[1,48,4096]{2,1,0:T(8,128)(2,1)S(1)}, bf16[1,48,4096]{2,1,0:T(8,128)(2,1)}, u32[]{:S(2)}) copy-start(bf16[1,48,4096]{2,1,0:T(8,128)(2,1)} %copy-done.5) | copy-start | bytes 1179652
  170.6 6.3 %copy-start.8 = (bf16[1,48,4096]{2,1,0:T(8,128)(2,1)S(1)}, bf16[1,48,4096]{2,1,0:T(8,128)(2,1)}, u32[]{:S(2)}) copy-start(bf16[1,48,4096]{2,1,0:T(8,128)(2,1)} %copy-done.7) | copy-start | bytes 1179652
  170.6 6.3 %copy-start.10 = (bf16[1,48,4096]{2,1,0:T(8,128)(2,1)S(1)}, bf16[1,48,4096]{2,1,0:T(8,128)(2,1)}, u32[]{:S(2)}) copy-start(bf16[1,48,4096]{2,1,0:T(8,128)(2,1)} %copy-done.9) | copy-start | bytes 1179652
  181.9 12.5 %copy-start.26 = (f32[1,128]{1,0:T(1,128)S(1)}, f32[1,128]{1,0:T(1,128)}, u32[]{:S(2)}) copy-start(f32[1,128]{1,0:T(1,128)} %copy-done.25) | copy-start | bytes 1540
  182.0 20.4 %collective-permute-start.19 = (bf16[1,48,4096]{2,1,0:T(8,128)(2,1)S(1)}, bf16[1,48,4096]{2,1,0:T(8,128)(2,1)S(1)}, u32[]{:S(2)}, u32[]{:S(2)}) collective-permute-start(bf16[1,48,4096]{2,1,0:T(8,128)(2,1)S(1)} %get-tuple-element.9), channel_id=1, source_target_pairs={{0,8},{2,10},{4,12},{6,14},{8,16},{10,18},{12,20},{14,22},{16,24},... | collective-permute-start | bytes 1179656 | tf_op jit(solution)/shard_map/ppermute | solution.py:219
  182.1 20.4 %collective-permute-start.20 = (bf16[1,48,4096]{2,1,0:T(8,128)(2,1)S(1)}, bf16[1,48,4096]{2,1,0:T(8,128)(2,1)S(1)}, u32[]{:S(2)}, u32[]{:S(2)}) collective-permute-start(bf16[1,48,4096]{2,1,0:T(8,128)(2,1)S(1)} %get-tuple-element.12), channel_id=1, source_target_pairs={{0,14},{2,8},{4,10},{6,12},{8,22},{10,16},{12,18},{14,20},{16,30},... | collective-permute-start | bytes 1179656 | tf_op jit(solution)/shard_map/ppermute | solution.py:219
  187.5 40.2 %collective-permute-start.21 = (bf16[1,48,4096]{2,1,0:T(8,128)(2,1)S(1)}, bf16[1,48,4096]{2,1,0:T(8,128)(2,1)S(1)}, u32[]{:S(2)}, u32[]{:S(2)}) collective-permute-start(bf16[1,48,4096]{2,1,0:T(8,128)(2,1)S(1)} %get-tuple-element.11), channel_id=1, source_target_pairs={{0,12},{2,14},{4,8},{6,10},{8,20},{10,22},{12,16},{14,18},{16,28},... | collective-permute-start | bytes 1179656 | tf_op jit(solution)/shard_map/ppermute | solution.py:219
  191.4 36.4 %collective-permute-start.22 = (bf16[1,48,4096]{2,1,0:T(8,128)(2,1)S(1)}, bf16[1,48,4096]{2,1,0:T(8,128)(2,1)S(1)}, u32[]{:S(2)}, u32[]{:S(2)}) collective-permute-start(bf16[1,48,4096]{2,1,0:T(8,128)(2,1)S(1)} %get-tuple-element.10), channel_id=1, source_target_pairs={{0,10},{2,12},{4,14},{6,8},{8,18},{10,20},{12,22},{14,16},{16,26},... | collective-permute-start | bytes 1179656 | tf_op jit(solution)/shard_map/ppermute | solution.py:219

commit v8 on v7

v8 whole, which is shorter than its diff:
```python
import functools
import math

import jax
import jax.numpy as jnp
from jax import lax
from jax.experimental import pallas as pl
from jax.experimental.pallas import tpu as pltpu
from jax.sharding import PartitionSpec as P

QUERY_HEADS = 32
KEY_VALUE_HEADS = 2
HEAD_SIZE = 128


def shift(value, axis, by):
    devices = lax.axis_size(axis)
    return lax.ppermute(value, axis, [(i, (i + by) % devices) for i in range(devices)])


IN_VMEM = pl.BlockSpec(memory_space=pltpu.VMEM)
ANYWHERE = pl.BlockSpec(memory_space=pl.ANY)


def attend_kernel(heads, origins, queries, pairs, *rest):
    out = rest[-1]
    rows = queries.shape[0]
    blocks = pairs.shape[0] // rows
    row_ids = origins[0] + lax.broadcasted_iota(jnp.int32, (rows, rows), 0)
    within = lax.broadcasted_iota(jnp.int32, (rows, rows), 1)
    seen = [origins[1 + block] + within <= row_ids for block in range(blocks)]
    seen = jnp.concatenate([one.astype(jnp.float32) for one in seen], axis=1) > 0.5
    for head in range(heads):
        columns = slice(head * HEAD_SIZE, (head + 1) * HEAD_SIZE)
        scores = lax.dot_general(
            queries[:, columns],
            pairs[:, :HEAD_SIZE],
            (((1,), (1,)), ((), ())),
            preferred_element_type=jnp.float32,
        ) * (1.0 / math.sqrt(HEAD_SIZE))
        scores = jnp.where(seen, scores, -jnp.inf)
        weights = jnp.exp(scores - jnp.max(scores, axis=1, keepdims=True))
        weights = weights / jnp.sum(weights, axis=1, keepdims=True)
        out[:, columns] = jnp.dot(
            weights.astype(jnp.bfloat16),
            pairs[:, HEAD_SIZE:],
            preferred_element_type=jnp.float32,
        ).astype(jnp.bfloat16)


def attend(queries, pairs, origins, heads, *earlier):
    rows, keys = queries.shape[0], pairs.shape[0]
    return pl.pallas_call(
        functools.partial(attend_kernel, heads),
        out_shape=jax.ShapeDtypeStruct(queries.shape, jnp.bfloat16),
        in_specs=[pl.BlockSpec(memory_space=pltpu.SMEM), IN_VMEM, IN_VMEM]
        + [ANYWHERE] * len(earlier),
        out_specs=IN_VMEM,
        cost_estimate=pl.CostEstimate(
            flops=4 * heads * rows * keys * HEAD_SIZE,
            bytes_accessed=4 * queries.size + 2 * pairs.size,
            transcendentals=heads * rows * keys,
        ),
        name="attend",
    )(origins, queries, pairs, *earlier)


def hidden_kernel(rows, into, inverse_gain, *rest):
    out = rest[-1]
    depth, width = rows.shape[1], out.shape[1]
    squares = jnp.zeros((rows.shape[0], 128), jnp.float32)
    for start in range(0, depth, 128):
        columns = slice(start, start + 128)
        mixed = rows[:, columns].astype(jnp.float32) * inverse_gain[:, columns]
        squares = squares + mixed * mixed
    scale = lax.rsqrt(jnp.sum(squares, axis=1, keepdims=True) / depth + 1e-06)
    tile = 256 if width % 256 == 0 else 128

    @pl.loop(0, width // tile)
    def _(j):
        gates = pl.ds(pl.multiple_of(j * tile, tile), tile)
        ups = pl.ds(pl.multiple_of(width + j * tile, tile), tile)
        gate = jnp.dot(rows[...], into[:, gates], preferred_element_type=jnp.float32) * scale
        up = jnp.dot(rows[...], into[:, ups], preferred_element_type=jnp.float32) * scale
        out[:, gates] = (gate / (1.0 + jnp.exp(-gate)) * up).astype(jnp.bfloat16)


def hidden_units(rows, into, inverse_gain, *earlier):
    count, depth, width = rows.shape[0], into.shape[0], into.shape[1] // 2
    return pl.pallas_call(
        hidden_kernel,
        out_shape=jax.ShapeDtypeStruct((count, width), jnp.bfloat16),
        in_specs=[IN_VMEM] * 3 + [ANYWHERE] * len(earlier),
        out_specs=IN_VMEM,
        cost_estimate=pl.CostEstimate(
            flops=4 * count * depth * width,
            bytes_accessed=2 * (rows.size + into.size),
            transcendentals=count * width,
        ),
        name="hidden_units",
    )(rows, into, inverse_gain, *earlier)


def down_kernel(hidden, down, out):
    tile = 512

    @pl.loop(0, out.shape[1] // tile)
    def _(j):
        columns = pl.ds(pl.multiple_of(j * tile, tile), tile)
        out[:, columns] = jnp.dot(
            hidden[...], down[:, columns], preferred_element_type=jnp.float32
        ).astype(out.dtype)


def down_part(hidden, down, kind):
    count, depth, width = hidden.shape[0], *down.shape
    return pl.pallas_call(
        down_kernel,
        out_shape=jax.ShapeDtypeStruct((count, width), kind),
        in_specs=[IN_VMEM] * 2,
        out_specs=IN_VMEM,
        cost_estimate=pl.CostEstimate(
            flops=2 * count * depth * width, bytes_accessed=2 * down.size, transcendentals=0
        ),
        name="down_part",
    )(hidden, down)


def mixed_halves(queries, keys_values, residual, out_weight, slot_weights, slots_here):
    contexts, exps = lax.axis_size("ctx"), lax.axis_size("exp")
    me, my_exp = lax.axis_index("ctx"), lax.axis_index("exp")
    rows = queries.shape[0]
    width = residual.shape[1]
    local_heads = QUERY_HEADS // contexts
    group_width = local_heads * HEAD_SIZE

    def pair_for(owner):
        head = owner * local_heads // (QUERY_HEADS // KEY_VALUE_HEADS)
        key = lax.dynamic_slice_in_dim(keys_values, head * HEAD_SIZE, HEAD_SIZE, 1)
        value = lax.dynamic_slice_in_dim(
            keys_values, (KEY_VALUE_HEADS + head) * HEAD_SIZE, HEAD_SIZE, 1
        )
        return jnp.concatenate([key, value], axis=1)

    def queries_for(owner):
        return lax.dynamic_slice_in_dim(queries, owner * group_width, group_width, 1)

    pairs = [pair_for(me)]
    blocks = [queries_for(me)]
    for k in range(1, contexts):
        pairs.append(shift(pair_for((me + k) % contexts), "ctx", k))
    for k in range(1, contexts):
        outgoing = queries_for((me + k) % contexts)
        blocks.append(shift(outgoing, "ctx", k))
    if exps == 2:
        weights = [out_weight, shift(out_weight, "exp", 1)]
        first = my_exp * (width // 2)
    else:
        gathered = lax.all_gather(out_weight, "exp", axis=1, tiled=True)
        weights = [gathered[:, : width // 2], gathered[:, width // 2 :]]
        first = 0
    offsets = [first, width // 2 - first]

    pair_rows = jnp.concatenate(pairs, axis=0)
    origins = [(me - k) % contexts * rows for k in range(contexts)]

    held, sent, weights_here, next_slots = [None, None], [], [slot_weights[0]], None
    for k in [*range(1, contexts), 0]:
        block_origins = jnp.stack([origins[k], *origins]).astype(jnp.int32)
        attended = attend(blocks[k], pair_rows, block_origins, local_heads, *sent)
        if k == contexts - 1:
            behind = sent[1][0, 0].astype(jnp.float32) * 0.0
            next_slots = shift(slots_here + behind, "pipe", 1)
            for j in range(1, contexts):
                weights_here.append(shift(slot_weights[j] + behind, "ctx", j))
        terms = []
        for half in range(2):
            term = jnp.dot(attended, weights[half], preferred_element_type=jnp.float32)
            if k == 0:
                own = lax.dynamic_slice_in_dim(residual, offsets[half], width // 2, 1)
                term = term + own.astype(jnp.float32)
            terms.append(lax.optimization_barrier(term))
        sent = []
        for half in range(2):
            term = terms[half]
            if held[half] is not None:
                term = term + held[half].astype(jnp.float32)
            if k == 0:
                held[half] = term
            else:
                sent.append(term.astype(jnp.bfloat16))
                held[half] = shift(sent[half], "ctx", 1)
    return held, first, jnp.concatenate(weights_here, axis=0), next_slots


def on_device(
    queries,
    rotated_keys_values,
    residual,
    out_weight,
    norm_gain,
    in_weight,
    down_weight,
    routes,
    route_weight,
):
    contexts, exps = lax.axis_size("ctx"), lax.axis_size("exp")
    me, my_exp = lax.axis_index("ctx"), lax.axis_index("exp")
    token_rows = queries.shape[2]
    model_width = residual.shape[3]
    group_size = min(4, exps)
    per_context = exps // group_size
    experts = contexts * per_context
    capacity = min(
        token_rows,
        group_size
        * ((3 * token_rows + 2 * experts * group_size - 1) // (2 * experts * group_size)),
    )
    slots = experts * capacity
    expert_ids = routes[0, 0, :, 0]
    expert_hits = (expert_ids[:, None] == jnp.arange(experts, dtype=jnp.int32)[None, :]).astype(
        jnp.int32
    )
    position = jnp.sum((jnp.cumsum(expert_hits, axis=0) - 1) * expert_hits, axis=1)
    distance = (expert_ids // per_context - me) % contexts
    slot_index = (distance * per_context + expert_ids % per_context) * capacity + position
    slot_ids = jnp.arange(slots, dtype=jnp.int32)
    slot_match = (slot_ids[:, None] == slot_index[None, :]).astype(jnp.bfloat16)
    hits = slot_ids[:, None] == slot_index[None, :]
    slot_weights = jnp.sum(jnp.where(hits, route_weight[0, 0, :, 0], 0.0), axis=1)
    halves, first, arrived_weights, next_slots = mixed_halves(
        queries[0, 0],
        rotated_keys_values[0, 0],
        residual[0, 0],
        out_weight[0],
        slot_weights.reshape(contexts, 1, per_context * capacity),
        slot_index.astype(jnp.float32)[None, :],
    )
    mixed_rows = jnp.concatenate(halves, axis=1)
    if exps == 2:
        mixed_rows = jnp.where(first == 0, mixed_rows, jnp.concatenate(halves[::-1], axis=1))

    gain = norm_gain
    inverse_gain = 1.0 / gain
    beside = sum(arrived_weights[k, 0] for k in range(contexts)) + next_slots[0, 0]
    scaled = (mixed_rows * (gain + beside * 0.0)).astype(jnp.bfloat16)
    packed = jnp.dot(slot_match, scaled, preferred_element_type=jnp.float32).astype(jnp.bfloat16)
    packed = packed.reshape(contexts, per_context, capacity, model_width)
    arrived = jnp.stack(
        [packed[0]] + [shift(packed[k], "ctx", k) for k in range(1, contexts)], axis=0
    )

    def wanted_by(blocks, exp):
        if per_context == 1:
            return blocks[:, 0]
        return lax.dynamic_index_in_dim(blocks, exp // group_size, 1, keepdims=False)

    own_rows = wanted_by(arrived, my_exp).reshape(-1, model_width)
    other_rows = jnp.concatenate(
        [shift(wanted_by(arrived, (my_exp + k) % exps), "exp", k) for k in range(1, exps)], axis=0
    ).reshape(-1, model_width)
    own_hidden = hidden_units(own_rows, in_weight[0, 0], inverse_gain)
    other_hidden = hidden_units(other_rows, in_weight[0, 0], inverse_gain, own_hidden)
    other_parts = down_part(other_hidden, down_weight[0, 0], jnp.bfloat16)
    other_parts = other_parts.reshape(exps - 1, contexts, capacity, model_width)
    own_part = down_part(own_hidden, down_weight[0, 0], jnp.float32)
    own_part = own_part.reshape(contexts, capacity, model_width)
    sums = [0.0] * per_context
    for k in range(exps):
        back = shift(other_parts[k - 1], "exp", -k).astype(jnp.float32) if k else own_part
        if per_context == 1:
            sums[0] = sums[0] + back
        else:
            place = (my_exp + k) % exps // group_size
            sums = [s + jnp.where(place == i, back, 0.0) for i, s in enumerate(sums)]
    weights = arrived_weights.reshape(contexts, per_context, capacity, 1)
    finished = arrived.astype(jnp.float32) * inverse_gain[0] + weights * jnp.stack(sums, axis=1)
    finished = finished.astype(jnp.bfloat16)

    def to_next_owner(rows, k):
        pipes = lax.axis_size("pipe")
        pairs = [
            (p * contexts + c, (p + 1) % pipes * contexts + (c - k) % contexts)
            for p in range(pipes)
            for c in range(contexts)
        ]
        return lax.ppermute(rows, ("pipe", "ctx"), pairs)

    returned = jnp.concatenate(
        [to_next_owner(finished[k], k).reshape(-1, model_width) for k in range(contexts)], axis=0
    )
    next_match = slot_ids[None, :] == next_slots[0].astype(jnp.int32)[:, None]
    layer = jnp.dot(next_match.astype(jnp.bfloat16), returned, preferred_element_type=jnp.float32)
    return layer.astype(jnp.bfloat16).reshape(1, 1, token_rows, model_width)


def solution(mesh):
    placed = (
        P("pipe", "exp", "ctx", None),
        P("pipe", "exp", "ctx", None),
        P("pipe", "exp", "ctx", None),
        P("pipe", "ctx", "exp"),
        P("pipe", None),
        P("pipe", ("ctx", "exp"), None, None),
        P("pipe", ("ctx", "exp"), None, None),
        P("pipe", "exp", "ctx", None),
        P("pipe", "exp", "ctx", None),
    )
    return jax.shard_map(
        on_device,
        mesh=mesh,
        in_specs=placed,
        out_specs=P("pipe", "exp", "ctx", None),
        check_vma=False,
    )
```

time: 230 us -> 235 us (1.022)
  Pallas kernels: 0 us -> 51.2 us
  matrix products: 62.8 us -> 26.2 us
  waiting for transfers between devices: 104 us -> 72.8 us
  starting transfers between devices: 41.6 us -> 68.1 us
  other arithmetic: 14.3 us -> 6.87 us
    pallas_call x0 -> x8, Pallas kernels: none -> 51.2 us  [the longest x2 18.7 us: hidden_units(): pl.pallas_call(hidden_kernel, out_shape=jax.ShapeDtypeStruct((count, widt...]
    ppermute x19 -> x22, waiting for transfers between devices: 70.2 us -> 38.2 us  [shift(): lax.ppermute(value, axis, [(i, (i + by) % devices) for i in range(devices)])]
    dot_general x9 -> x1, matrix products: 31.7 us -> 1.46 us  [on_device(): jnp.dot(next_match.astype(jnp.bfloat16), returned, preferred_element_type...]
    ppermute x19 -> x22, starting transfers between devices: 29.3 us -> 54.9 us  [shift(): lax.ppermute(value, axis, [(i, (i + by) % devices) for i in range(devices)])]
    sub x4 -> x0, matrix products: 5.99 us -> none  [attend_block(): attention_weights = jax.nn.softmax(scores, axis=-1).astype(jnp.bfloat16)]
    reduce_sum x6 -> x1, other arithmetic: 3.71 us -> 0.11 us  [on_device(): jnp.sum(jnp.where(hits, route_weight[0, 0, :, 0], 0.0), axis=1)]
    another operation x0 -> x4, local copies, waits for them, and re-layouts: none -> 2.58 us  [mixed_halves(): block_origins = jnp.stack([origins[k], *origins]).astype(jnp.int32)]
    convert_element_type x9 -> x6, other arithmetic: 5.07 us -> 3.15 us  [the longest x1 2.65 us: on_device(): finished = finished.astype(jnp.bfloat16)]
  transfers between devices with their start and end apart: 23 -> 26, of which waited for: 10 -> 7; matrix products, arithmetic and copies ran while one was open for 23% -> 14% of each run, Pallas kernels for 0% -> 15%
where the time goes in v8:
time: 235 us; the launch traced here: 234 us
  waiting for transfers between devices  72.8 us (31%)
  starting transfers between devices  68.1 us (29%)
  Pallas kernels  51.2 us (22%)
  matrix products  26.2 us (11%)
  local copies, waits for them, and re-layouts  7.84 us (3%)
  other arithmetic  6.87 us (3%)
    ppermute x22, starting transfers between devices, shift(): lax.ppermute(value, axis, [(i, (i + by) % devices) for i in range(devices)])  54.9 us
    ppermute x22, waiting for transfers between devices, shift(): lax.ppermute(value, axis, [(i, (i + by) % devices) for i in range(devices)])  38.2 us
    ppermute x4, waiting for transfers between devices, to_next_owner(): return lax.ppermute(rows, ('pipe', 'ctx'), pairs)  34.5 us
    dot_general x8, matrix products, mixed_halves(): term = jnp.dot(attended, weights[half], preferred_element_type=jnp.float32)  24.1 us
    pallas_call x2, Pallas kernels, hidden_units(): pl.pallas_call(hidden_kernel, out_shape=jax.ShapeDtypeStruct((count, widt...  18.7 us
    pallas_call x4, Pallas kernels, attend(): pl.pallas_call(functools.partial(attend_kernel, heads), out_shape=jax.Sha...  18.5 us
    pallas_call x2, Pallas kernels, down_part(): pl.pallas_call(down_kernel, out_shape=jax.ShapeDtypeStruct((count, width)...  14 us
    ppermute x4, starting transfers between devices, to_next_owner(): return lax.ppermute(rows, ('pipe', 'ctx'), pairs)  13.2 us
  transfers between devices with their start and end apart: 26, of which 7 were waited for; matrix products, arithmetic and copies ran while one was open for 14% of the time, Pallas kernels for 15%

profile of v8, /device:TPU:0, one launch (start us, length us, event | category | flops | bytes accessed | tf_op | source)
XLA Modules:
  0.0 234.2 jit_solution(2557329217924423797)
XLA Ops:
  0.0 0.5 collective-permute-start.5
  0.5 1.0 dynamic-slice_bitcast_fusion.11
  1.4 2.8 %collective-permute-start.1 = (bf16[128,256]{1,0:T(8,128)(2,1)S(1)}, bf16[128,256]{1,0:T(8,128)(2,1)S(1)}, u32[]{:S(2)}, u32[]{:S(2)}) collective-permute-start(bf16[128,256]{1,0:T(8,128)(2,1)S(1)} %pad_maximum_fusion.2), channel_id=1, source_target_pairs={{0,2},{2,4},{4,6},{6,0},{1,3},{3,5},{5,7},{7,1},{8,10},{10,12},{12... | collective-permute-start | bytes 196616 | tf_op jit(solution)/shard_map/ppermute | solution.py:18
  4.3 2.7 %collective-permute-start.2 = (bf16[128,256]{1,0:T(8,128)(2,1)S(1)}, bf16[128,256]{1,0:T(8,128)(2,1)S(1)}, u32[]{:S(2)}, u32[]{:S(2)}) collective-permute-start(bf16[128,256]{1,0:T(8,128)(2,1)S(1)} %pad_maximum_fusion.3), channel_id=1, source_target_pairs={{0,4},{2,6},{4,0},{6,2},{1,5},{3,7},{5,1},{7,3},{8,12},{10,14},{12... | collective-permute-start | bytes 196616 | tf_op jit(solution)/shard_map/ppermute | solution.py:18
  6.9 1.4 collective-permute-start.3
  8.3 2.0 dynamic-slice_bitcast_fusion.2
  10.3 0.7 collective-permute-start.4
  11.1 0.2 reduce_window_sum.11
  11.2 0.2 select_reduce_fusion.1
  11.5 0.6 stack.62.origins
  12.1 0.7 stack.61.origins
  12.8 0.7 stack.64.origins
  13.5 0.6 stack.63.origins
  14.2 0.4 collective-permute-start
  14.6 2.9 %collective-permute-start.8 = (bf16[128,1024]{1,0:T(8,128)(2,1)S(1)}, bf16[128,1024]{1,0:T(8,128)(2,1)S(1)}, u32[]{:S(2)}, u32[]{:S(2)}) collective-permute-start(bf16[128,1024]{1,0:T(8,128)(2,1)S(1)} %get-tuple-element.18), channel_id=1, source_target_pairs={{0,6},{2,0},{4,2},{6,4},{1,7},{3,1},{5,3},{7,5},{8,14},{10,8},{12,... | collective-permute-start | bytes 786440 | tf_op jit(solution)/shard_map/ppermute | solution.py:18
  17.5 0.7 pad_maximum_fusion.1.pairs
  18.2 3.2 %collective-permute-done.4.queries = bf16[128,1024]{1,0:T(8,128)(2,1)S(1)} collective-permute-done((bf16[128,1024]{1,0:T(8,128)(2,1)S(1)}, bf16[128,1024]{1,0:T(8,128)(2,1)S(1)}, u32[]{:S(2)}, u32[]{:S(2)}) %collective-permute-start.4) | collective-permute-done | bytes 262176 | tf_op jit(solution)/shard_map/ppermute | solution.py:18
  21.4 0.7 copy-done.17
  22.1 4.6 %attend.4 = bf16[128,1024]{1,0:T(8,128)(2,1)} custom-call(s32[5]{0:T(128)} %stack.62.origins, bf16[128,1024]{1,0:T(8,128)(2,1)} %copy-done.17, bf16[512,256]{1,0:T(8,128)(2,1)} %pad_maximum_fusion.1.pairs), custom_call_target="tpu_custom_call" | custom-call | flops 268435456 | bytes 786432 | tf_op jit(solution)/shard_map/attend/pallas_call | solution.py:53
  26.8 3.0 %fusion.29.rest_0_ = bf16[128,2048]{1,0:T(8,128)(2,1)S(1)} fusion(bf16[128,1024]{1,0:T(8,128)(2,1)} %attend.4, bf16[1,1024,2048]{2,1,0:T(8,128)(2,1)} %param.12), kind=kOutput, calls=%fused_computation.82 | convolution fusion | flops 536870912 | bytes 4980736 | tf_op jit(solution)/shard_map/dot_general | solution.py:178
  29.9 3.0 %fusion.33.rest_1_ = bf16[128,2048]{1,0:T(8,128)(2,1)S(1)} fusion(bf16[128,1024]{1,0:T(8,128)(2,1)S(1)} %copy-done.10, bf16[1024,2048]{1,0:T(8,128)(2,1)} %collective-permute-done.5), kind=kOutput, calls=%fused_computation.86 | convolution fusion | flops 536870912 | bytes 4980736 | tf_op jit(solution)/shard_map/dot_general | solution.py:178
  33.0 9.8 %collective-permute-start.6 = (bf16[128,2048]{1,0:T(8,128)(2,1)S(1)}, bf16[128,2048]{1,0:T(8,128)(2,1)S(1)}, u32[]{:S(2)}, u32[]{:S(2)}) collective-permute-start(bf16[128,2048]{1,0:T(8,128)(2,1)S(1)} %fusion.33.rest_1_), channel_id=1, source_target_pairs={{0,2},{2,4},{4,6},{6,0},{1,3},{3,5},{5,7},{7,1},{8,10},{10,12},{12... | collective-permute-start | bytes 1572872 | tf_op jit(solution)/shard_map/ppermute | solution.py:18
  42.8 0.7 copy-done.12
  43.5 4.6 %attend.5 = bf16[128,1024]{1,0:T(8,128)(2,1)} custom-call(s32[5]{0:T(128)} %stack.61.origins, bf16[128,1024]{1,0:T(8,128)(2,1)} %copy-done.12, bf16[512,256]{1,0:T(8,128)(2,1)} %pad_maximum_fusion.1.pairs, bf16[128,2048]{1,0:T(8,128)(2,1)} %copy-done.4, bf16[128,2048]{1,0:T(8,128)(2,1)} %copy-done.3), custom_call_target="tpu_custom_call" | custom-call | flops 268435456 | bytes 786432 | tf_op jit(solution)/shard_map/attend/pallas_call | solution.py:53
  48.1 3.0 %fusion.27 = f32[128,2048]{1,0:T(8,128)S(1)} fusion(bf16[128,1024]{1,0:T(8,128)(2,1)} %attend.5, bf16[1,1024,2048]{2,1,0:T(8,128)(2,1)} %param.12), kind=kOutput, calls=%fused_computation.80 | convolution fusion | flops 536870912 | bytes 5505024 | tf_op jit(solution)/shard_map/dot_general | solution.py:178
  51.2 2.9 %fusion.34 = f32[128,2048]{1,0:T(8,128)S(1)} fusion(bf16[128,1024]{1,0:T(8,128)(2,1)S(1)} %copy-done.2, bf16[1024,2048]{1,0:T(8,128)(2,1)} %collective-permute-done.5), kind=kOutput, calls=%fused_computation.87 | convolution fusion | flops 536870912 | bytes 5505024 | tf_op jit(solution)/shard_map/dot_general | solution.py:178
  54.2 0.8 collective-permute-start.10
  55.0 2.8 %collective-permute-done.6 = bf16[128,2048]{1,0:T(8,128)(2,1)S(1)} collective-permute-done((bf16[128,2048]{1,0:T(8,128)(2,1)S(1)}, bf16[128,2048]{1,0:T(8,128)(2,1)S(1)}, u32[]{:S(2)}, u32[]{:S(2)}) %collective-permute-start.6) | collective-permute-done | bytes 524320 | tf_op jit(solution)/shard_map/ppermute | solution.py:18
  58.0 0.6 slice.87
  58.5 5.6 %collective-permute-start.11 = (bf16[128,2048]{1,0:T(8,128)(2,1)S(1)}, bf16[128,2048]{1,0:T(8,128)(2,1)S(1)}, u32[]{:S(2)}, u32[]{:S(2)}) collective-permute-start(bf16[128,2048]{1,0:T(8,128)(2,1)S(1)} %add_convert_fusion.4.rest_1_), channel_id=1, source_target_pairs={{0,2},{2,4},{4,6},{6,0},{1,3},{3,5},{5,7},{7,1},{8,10},{10,12},{12... | collective-permute-start | bytes 1572872 | tf_op jit(solution)/shard_map/ppermute | solution.py:18
  64.8 2.5 %collective-permute-start.14 = (f32[1,48]{1,0:T(1,128)S(1)}, f32[1,48]{1,0:T(1,128)S(1)}, u32[]{:S(2)}, u32[]{:S(2)}) collective-permute-start(f32[1,48]{1,0:T(1,128)S(1)} %get-tuple-element.32), channel_id=1, source_target_pairs={{0,2},{2,4},{4,6},{6,0},{1,3},{3,5},{5,7},{7,1},{8,10},{10,12},{12... | collective-permute-start | bytes 584 | tf_op jit(solution)/shard_map/ppermute | solution.py:18
  67.3 2.4 %collective-permute-start.16 = (f32[1,48]{1,0:T(1,128)S(1)}, f32[1,48]{1,0:T(1,128)S(1)}, u32[]{:S(2)}, u32[]{:S(2)}) collective-permute-start(f32[1,48]{1,0:T(1,128)S(1)} %get-tuple-element.30), channel_id=1, source_target_pairs={{0,6},{2,0},{4,2},{6,4},{1,7},{3,1},{5,3},{7,5},{8,14},{10,8},{12,... | collective-permute-start | bytes 584 | tf_op jit(solution)/shard_map/ppermute | solution.py:18
  69.8 4.6 %attend.6 = bf16[128,1024]{1,0:T(8,128)(2,1)} custom-call(s32[5]{0:T(128)} %stack.64.origins, bf16[128,1024]{1,0:T(8,128)(2,1)} %copy-done.11, bf16[512,256]{1,0:T(8,128)(2,1)} %pad_maximum_fusion.1.pairs, bf16[128,2048]{1,0:T(8,128)(2,1)} %copy-done.7, bf16[128,2048]{1,0:T(8,128)(2,1)} %copy-done.5), custom_call_target="tpu_custom_call" | custom-call | flops 268435456 | bytes 786432 | tf_op jit(solution)/shard_map/attend/pallas_call | solution.py:53
  74.4 3.0 %fusion.25 = f32[128,2048]{1,0:T(8,128)S(1)} fusion(bf16[128,1024]{1,0:T(8,128)(2,1)} %attend.6, bf16[1,1024,2048]{2,1,0:T(8,128)(2,1)} %param.12), kind=kOutput, calls=%fused_computation.78 | convolution fusion | flops 536870912 | bytes 5505024 | tf_op jit(solution)/shard_map/dot_general | solution.py:178
  77.5 1.9 collective-permute-start.7
  79.5 3.1 %fusion.35 = f32[128,2048]{1,0:T(8,128)S(1)} fusion(bf16[128,1024]{1,0:T(8,128)(2,1)S(1)} %copy-done.1, bf16[1024,2048]{1,0:T(8,128)(2,1)} %collective-permute-done.5), kind=kOutput, calls=%fused_computation.88 | convolution fusion | flops 536870912 | bytes 5505024 | tf_op jit(solution)/shard_map/dot_general | solution.py:178
  82.6 12.8 %collective-permute-start.12 = (bf16[128,2048]{1,0:T(8,128)(2,1)S(1)}, bf16[128,2048]{1,0:T(8,128)(2,1)S(1)}, u32[]{:S(2)}, u32[]{:S(2)}) collective-permute-start(bf16[128,2048]{1,0:T(8,128)(2,1)S(1)} %add_convert_fusion.2.rest_0_), channel_id=1, source_target_pairs={{0,2},{2,4},{4,6},{6,0},{1,3},{3,5},{5,7},{7,1},{8,10},{10,12},{12... | collective-permute-start | bytes 1572872 | tf_op jit(solution)/shard_map/ppermute | solution.py:18
  95.7 0.6 broadcast_divide_fusion
  96.4 1.6 collective-permute-start.13
  98.0 4.6 %attend.7 = bf16[128,1024]{1,0:T(8,128)(2,1)} custom-call(s32[5]{0:T(128)} %stack.63.origins, bf16[128,1024]{1,0:T(8,128)(2,1)} %get-tuple-element.19.queries, bf16[512,256]{1,0:T(8,128)(2,1)} %pad_maximum_fusion.1.pairs, bf16[128,2048]{1,0:T(8,128)(2,1)} %copy-done.6, bf16[128,2048]{1,0:T(8,128)(2,1)} %copy-done.8), custom_call_target="tpu_custom_call" | custom-call | flops 268435456 | bytes 786432 | tf_op jit(solution)/shard_map/attend/pallas_call | solution.py:53
  102.7 3.0 %convolution_add_fusion.1 = f32[128,2048]{1,0:T(8,128)S(1)} fusion(bf16[128,1024]{1,0:T(8,128)(2,1)} %attend.7, bf16[1,1,128,4096]{3,2,1,0:T(8,128)(2,1)S(1)} %copy-done.9, s32[]{:T(128)S(6)} %select_n.166, bf16[1,1024,2048]{2,1,0:T(8,128)(2,1)} %param.12), kind=kOutput, calls=%fused_computation.5 | convolution fusion | flops 537395200 | bytes 6029316 | tf_op jit(solution)/shard_map/dot_general | solution.py:178
  105.7 2.9 %convolution_add_fusion = f32[128,2048]{1,0:T(8,128)S(1)} fusion(bf16[128,1024]{1,0:T(8,128)(2,1)S(1)} %copy-done, bf16[1024,2048]{1,0:T(8,128)(2,1)} %collective-permute-done.5, bf16[1,1,128,4096]{3,2,1,0:T(8,128)(2,1)S(1)} %copy-done.9, s32[]{:T(128)S(6)} %select_n.167), kind=kOutput, calls=%fused_computation.4 | convolution fusion | flops 537395200 | bytes 6029316 | tf_op jit(solution)/shard_map/dot_general | solution.py:178
  108.8 9.2 %collective-permute-done.13 = bf16[128,2048]{1,0:T(8,128)(2,1)S(1)} collective-permute-done((bf16[128,2048]{1,0:T(8,128)(2,1)S(1)}, bf16[128,2048]{1,0:T(8,128)(2,1)S(1)}, u32[]{:S(2)}, u32[]{:S(2)}) %collective-permute-start.13) | collective-permute-done | bytes 524320 | tf_op jit(solution)/shard_map/ppermute | solution.py:18
  118.1 0.6 convolution_convert_fusion
  118.7 0.2 slice_bitcast_fusion.4
  118.9 2.3 collective-permute-start.17
  121.2 0.8 collective-permute-start.18
  122.0 2.6 %collective-permute-start.19 = (bf16[1,48,4096]{2,1,0:T(8,128)(2,1)S(1)}, bf16[1,48,4096]{2,1,0:T(8,128)(2,1)S(1)}, u32[]{:S(2)}, u32[]{:S(2)}) collective-permute-start(bf16[1,48,4096]{2,1,0:T(8,128)(2,1)S(1)} %get-tuple-element.11), channel_id=1, source_target_pairs={{0,6},{2,0},{4,2},{6,4},{1,7},{3,1},{5,3},{7,5},{8,14},{10,8},{12,... | collective-permute-start | bytes 1179656 | tf_op jit(solution)/shard_map/ppermute | solution.py:18
  124.7 8.3 %collective-permute-done.17 = bf16[1,48,4096]{2,1,0:T(8,128)(2,1)S(1)} collective-permute-done((bf16[1,48,4096]{2,1,0:T(8,128)(2,1)S(1)}, bf16[1,48,4096]{2,1,0:T(8,128)(2,1)S(1)}, u32[]{:S(2)}, u32[]{:S(2)}) %collective-permute-start.17) | collective-permute-done | bytes 393248 | tf_op jit(solution)/shard_map/ppermute | solution.py:18
  133.0 14.7 %collective-permute-done.18 = bf16[1,48,4096]{2,1,0:T(8,128)(2,1)S(1)} collective-permute-done((bf16[1,48,4096]{2,1,0:T(8,128)(2,1)S(1)}, bf16[1,48,4096]{2,1,0:T(8,128)(2,1)S(1)}, u32[]{:S(2)}, u32[]{:S(2)}) %collective-permute-start.18) | collective-permute-done | bytes 393248 | tf_op jit(solution)/shard_map/ppermute | solution.py:18
  147.6 1.4 fusion.31
  149.1 9.4 %hidden_units.2.hidden.rest_0_ = bf16[192,768]{1,0:T(8,128)(2,1)} custom-call(bf16[192,4096]{1,0:T(8,128)(2,1)} %bitcast.118, bf16[4096,1536]{1,0:T(8,128)(2,1)} %bitcast.113, f32[1,4096]{1,0:T(1,128)} %get-tuple-element.28.inverse_gain), custom_call_target="tpu_custom_call" | custom-call | flops 2415919104 | bytes 14155776 | tf_op jit(solution)/shard_map/hidden_units/pallas_call | solution.py:90
  158.4 9.3 %hidden_units.3.hidden = bf16[192,768]{1,0:T(8,128)(2,1)} custom-call(bf16[192,4096]{1,0:T(8,128)(2,1)} %bitcast.45.rows, bf16[4096,1536]{1,0:T(8,128)(2,1)} %bitcast.114, f32[1,4096]{1,0:T(1,128)} %get-tuple-element.28.inverse_gain, bf16[192,768]{1,0:T(8,128)(2,1)} %hidden_units.2.hidden.rest_0_), custom_call_target="tpu_custom_call" | custom-call | flops 2415919104 | bytes 14155776 | tf_op jit(solution)/shard_map/hidden_units/pallas_call | solution.py:90
  167.7 6.7 %down_part.3 = bf16[192,4096]{1,0:T(8,128)(2,1)} custom-call(bf16[192,768]{1,0:T(8,128)(2,1)} %hidden_units.3.hidden, bf16[768,4096]{1,0:T(8,128)(2,1)} %bitcast.115), custom_call_target="tpu_custom_call" | custom-call | flops 1207959552 | bytes 6291456 | tf_op jit(solution)/shard_map/down_part/pallas_call | solution.py:117
  174.5 0.5 collective-permute-start.21
  175.0 7.3 %down_part.2 = f32[192,4096]{1,0:T(8,128)} custom-call(bf16[192,768]{1,0:T(8,128)(2,1)} %hidden_units.2.hidden.rest_0_, bf16[768,4096]{1,0:T(8,128)(2,1)} %bitcast.116), custom_call_target="tpu_custom_call" | custom-call | flops 1207959552 | bytes 6291456 | tf_op jit(solution)/shard_map/down_part/pallas_call | solution.py:117
  182.2 2.6 %add_convert_fusion = bf16[4,48,4096]{2,1,0:T(8,128)(2,1)S(1)} fusion(f32[4,48,4096]{2,1,0:T(8,128)} %bitcast.117, bf16[4,48,4096]{2,1,0:T(8,128)(2,1)S(1)} %collective-permute-done.21, bf16[1,48,4096]{2,1,0:T(8,128)(2,1)S(1)} %collective-permute-done.19, bf16[1,48,4096]{2,1,0:T(8,128)(2,1)S(1)} %collective-permute-done.18, ...), kind=kLoop, calls=%fused_computation.3 | loop fusion | flops 7864320 | bytes 7881472 | tf_op jit(solution)/shard_map/convert_element_type | solution.py:278
  185.0 1.5 collective-permute-start.22
  186.6 10.8 %collective-permute-start.23 = (bf16[1,48,4096]{2,1,0:T(8,128)(2,1)S(1)}, bf16[1,48,4096]{2,1,0:T(8,128)(2,1)S(1)}, u32[]{:S(2)}, u32[]{:S(2)}) collective-permute-start(bf16[1,48,4096]{2,1,0:T(8,128)(2,1)S(1)} %get-tuple-element.8), channel_id=1, source_target_pairs={{0,14},{2,8},{4,10},{6,12},{8,22},{10,16},{12,18},{14,20},{16,30},... | collective-permute-start | bytes 1179656 | tf_op jit(solution)/shard_map/ppermute | solution.py:287
  197.3 0.4 collective-permute-start.24
  197.7 0.5 collective-permute-start.25
  198.2 8.7 %collective-permute-done.23 = bf16[1,48,4096]{2,1,0:T(8,128)(2,1)S(1)} collective-permute-done((bf16[1,48,4096]{2,1,0:T(8,128)(2,1)S(1)}, bf16[1,48,4096]{2,1,0:T(8,128)(2,1)S(1)}, u32[]{:S(2)}, u32[]{:S(2)}) %collective-permute-start.23) | collective-permute-done | bytes 393248 | tf_op jit(solution)/shard_map/ppermute | solution.py:287
  207.0 25.8 %collective-permute-done.24 = bf16[1,48,4096]{2,1,0:T(8,128)(2,1)S(1)} collective-permute-done((bf16[1,48,4096]{2,1,0:T(8,128)(2,1)S(1)}, bf16[1,48,4096]{2,1,0:T(8,128)(2,1)S(1)}, u32[]{:S(2)}, u32[]{:S(2)}) %collective-permute-start.24) | collective-permute-done | bytes 393248 | tf_op jit(solution)/shard_map/ppermute | solution.py:287
  232.8 1.5 fusion
  (73 shorter events, 1.4 us)
Async XLA Ops:
  0.0 11.0 %copy-start.15 = (s32[1,1,128,1]{2,3,1,0:T(1,128)S(1)}, s32[1,1,128,1]{2,3,1,0:T(1,128)}, u32[]{:S(2)}) copy-start(s32[1,1,128,1]{2,3,1,0:T(1,128)} %param.16) | copy-start | bytes 1540
  0.0 14.1 %copy-start.16 = (f32[1,1,128,1]{2,3,1,0:T(1,128)S(1)}, f32[1,1,128,1]{2,3,1,0:T(1,128)}, u32[]{:S(2)}) copy-start(f32[1,1,128,1]{2,3,1,0:T(1,128)} %param.17) | copy-start | bytes 1540
  0.0 29.9 %collective-permute-start.5 = (bf16[1024,2048]{1,0:T(8,128)(2,1)}, bf16[1024,2048]{1,0:T(8,128)(2,1)}, u32[]{:S(2)}, u32[]{:S(2)}) collective-permute-start(bf16[1024,2048]{1,0:T(8,128)(2,1)} %bitcast.112), channel_id=1, source_target_pairs={{0,1},{1,0},{2,3},{3,2},{4,5},{5,4},{6,7},{7,6},{8,9},{9,8},{10,11... | collective-permute-start | bytes 12582920 | tf_op jit(solution)/shard_map/ppermute | solution.py:18
  1.4 12.8 %collective-permute-start.1 = (bf16[128,256]{1,0:T(8,128)(2,1)S(1)}, bf16[128,256]{1,0:T(8,128)(2,1)S(1)}, u32[]{:S(2)}, u32[]{:S(2)}) collective-permute-start(bf16[128,256]{1,0:T(8,128)(2,1)S(1)} %pad_maximum_fusion.2), channel_id=1, source_target_pairs={{0,2},{2,4},{4,6},{6,0},{1,3},{3,5},{5,7},{7,1},{8,10},{10,12},{12... | collective-permute-start | bytes 196616 | tf_op jit(solution)/shard_map/ppermute | solution.py:18
  4.3 10.3 %collective-permute-start.2 = (bf16[128,256]{1,0:T(8,128)(2,1)S(1)}, bf16[128,256]{1,0:T(8,128)(2,1)S(1)}, u32[]{:S(2)}, u32[]{:S(2)}) collective-permute-start(bf16[128,256]{1,0:T(8,128)(2,1)S(1)} %pad_maximum_fusion.3), channel_id=1, source_target_pairs={{0,4},{2,6},{4,0},{6,2},{1,5},{3,7},{5,1},{7,3},{8,12},{10,14},{12... | collective-permute-start | bytes 196616 | tf_op jit(solution)/shard_map/ppermute | solution.py:18
  6.9 10.6 %collective-permute-start.3 = (bf16[128,256]{1,0:T(8,128)(2,1)S(1)}, bf16[128,256]{1,0:T(8,128)(2,1)S(1)}, u32[]{:S(2)}, u32[]{:S(2)}) collective-permute-start(bf16[128,256]{1,0:T(8,128)(2,1)S(1)} %pad_maximum_fusion.4), channel_id=1, source_target_pairs={{0,6},{2,0},{4,2},{6,4},{1,7},{3,1},{5,3},{7,5},{8,14},{10,8},{12,... | collective-permute-start | bytes 196616 | tf_op jit(solution)/shard_map/ppermute | solution.py:18
  10.3 11.1 %collective-permute-start.4 = (bf16[128,1024]{1,0:T(8,128)(2,1)S(1)}, bf16[128,1024]{1,0:T(8,128)(2,1)S(1)}, u32[]{:S(2)}, u32[]{:S(2)}) collective-permute-start(bf16[128,1024]{1,0:T(8,128)(2,1)S(1)} %get-tuple-element.16), channel_id=1, source_target_pairs={{0,2},{2,4},{4,6},{6,0},{1,3},{3,5},{5,7},{7,1},{8,10},{10,12},{12... | collective-permute-start | bytes 786440 | tf_op jit(solution)/shard_map/ppermute | solution.py:18
  14.2 28.6 %collective-permute-start = (bf16[128,1024]{1,0:T(8,128)(2,1)S(1)}, bf16[128,1024]{1,0:T(8,128)(2,1)S(1)}, u32[]{:S(2)}, u32[]{:S(2)}) collective-permute-start(bf16[128,1024]{1,0:T(8,128)(2,1)S(1)} %get-tuple-element.17), channel_id=1, source_target_pairs={{0,4},{2,6},{4,0},{6,2},{1,5},{3,7},{5,1},{7,3},{8,12},{10,14},{12... | collective-permute-start | bytes 786440 | tf_op jit(solution)/shard_map/ppermute | solution.py:18
  14.6 52.7 %collective-permute-start.8 = (bf16[128,1024]{1,0:T(8,128)(2,1)S(1)}, bf16[128,1024]{1,0:T(8,128)(2,1)S(1)}, u32[]{:S(2)}, u32[]{:S(2)}) collective-permute-start(bf16[128,1024]{1,0:T(8,128)(2,1)S(1)} %get-tuple-element.18), channel_id=1, source_target_pairs={{0,6},{2,0},{4,2},{6,4},{1,7},{3,1},{5,3},{7,5},{8,14},{10,8},{12,... | collective-permute-start | bytes 786440 | tf_op jit(solution)/shard_map/ppermute | solution.py:18
  21.4 0.7 copy-start.17
  26.8 3.1 %copy-start.10 = (bf16[128,1024]{1,0:T(8,128)(2,1)S(1)}, bf16[128,1024]{1,0:T(8,128)(2,1)}, u32[]{:S(2)}) copy-start(bf16[128,1024]{1,0:T(8,128)(2,1)} %attend.4) | copy-start | bytes 786436
  29.8 13.0 %copy-start.4 = (bf16[128,2048]{1,0:T(8,128)(2,1)}, bf16[128,2048]{1,0:T(8,128)(2,1)S(1)}, u32[]{:S(2)}) copy-start(bf16[128,2048]{1,0:T(8,128)(2,1)S(1)} %fusion.29.rest_0_) | copy-start | bytes 1572868
  29.8 24.3 %collective-permute-start.9 = (bf16[128,2048]{1,0:T(8,128)(2,1)S(1)}, bf16[128,2048]{1,0:T(8,128)(2,1)S(1)}, u32[]{:S(2)}, u32[]{:S(2)}) collective-permute-start(bf16[128,2048]{1,0:T(8,128)(2,1)S(1)} %fusion.29.rest_0_), channel_id=1, source_target_pairs={{0,2},{2,4},{4,6},{6,0},{1,3},{3,5},{5,7},{7,1},{8,10},{10,12},{12... | collective-permute-start | bytes 1572872 | tf_op jit(solution)/shard_map/ppermute | solution.py:18
  33.0 9.8 %copy-start.3 = (bf16[128,2048]{1,0:T(8,128)(2,1)}, bf16[128,2048]{1,0:T(8,128)(2,1)S(1)}, u32[]{:S(2)}) copy-start(bf16[128,2048]{1,0:T(8,128)(2,1)S(1)} %fusion.33.rest_1_) | copy-start | bytes 1572868
  33.0 24.9 %collective-permute-start.6 = (bf16[128,2048]{1,0:T(8,128)(2,1)S(1)}, bf16[128,2048]{1,0:T(8,128)(2,1)S(1)}, u32[]{:S(2)}, u32[]{:S(2)}) collective-permute-start(bf16[128,2048]{1,0:T(8,128)(2,1)S(1)} %fusion.33.rest_1_), channel_id=1, source_target_pairs={{0,2},{2,4},{4,6},{6,0},{1,3},{3,5},{5,7},{7,1},{8,10},{10,12},{12... | collective-permute-start | bytes 1572872 | tf_op jit(solution)/shard_map/ppermute | solution.py:18
  42.8 0.7 copy-start.12
  48.1 3.0 %copy-start.2 = (bf16[128,1024]{1,0:T(8,128)(2,1)S(1)}, bf16[128,1024]{1,0:T(8,128)(2,1)}, u32[]{:S(2)}) copy-start(bf16[128,1024]{1,0:T(8,128)(2,1)} %attend.5) | copy-start | bytes 786436
  54.2 15.5 %copy-start.7 = (bf16[128,2048]{1,0:T(8,128)(2,1)}, bf16[128,2048]{1,0:T(8,128)(2,1)S(1)}, u32[]{:S(2)}) copy-start(bf16[128,2048]{1,0:T(8,128)(2,1)S(1)} %add_convert_fusion.3.rest_0_) | copy-start | bytes 1572868
  54.2 23.2 %collective-permute-start.10 = (bf16[128,2048]{1,0:T(8,128)(2,1)S(1)}, bf16[128,2048]{1,0:T(8,128)(2,1)S(1)}, u32[]{:S(2)}, u32[]{:S(2)}) collective-permute-start(bf16[128,2048]{1,0:T(8,128)(2,1)S(1)} %add_convert_fusion.3.rest_0_), channel_id=1, source_target_pairs={{0,2},{2,4},{4,6},{6,0},{1,3},{3,5},{5,7},{7,1},{8,10},{10,12},{12... | collective-permute-start | bytes 1572872 | tf_op jit(solution)/shard_map/ppermute | solution.py:18
  58.0 11.8 %copy-start.5 = (bf16[128,2048]{1,0:T(8,128)(2,1)}, bf16[128,2048]{1,0:T(8,128)(2,1)S(1)}, u32[]{:S(2)}) copy-start(bf16[128,2048]{1,0:T(8,128)(2,1)S(1)} %add_convert_fusion.4.rest_1_) | copy-start | bytes 1572868
  58.5 37.7 %collective-permute-start.11 = (bf16[128,2048]{1,0:T(8,128)(2,1)S(1)}, bf16[128,2048]{1,0:T(8,128)(2,1)S(1)}, u32[]{:S(2)}, u32[]{:S(2)}) collective-permute-start(bf16[128,2048]{1,0:T(8,128)(2,1)S(1)} %add_convert_fusion.4.rest_1_), channel_id=1, source_target_pairs={{0,2},{2,4},{4,6},{6,0},{1,3},{3,5},{5,7},{7,1},{8,10},{10,12},{12... | collective-permute-start | bytes 1572872 | tf_op jit(solution)/shard_map/ppermute | solution.py:18
  64.8 17.8 %collective-permute-start.14 = (f32[1,48]{1,0:T(1,128)S(1)}, f32[1,48]{1,0:T(1,128)S(1)}, u32[]{:S(2)}, u32[]{:S(2)}) collective-permute-start(f32[1,48]{1,0:T(1,128)S(1)} %get-tuple-element.32), channel_id=1, source_target_pairs={{0,2},{2,4},{4,6},{6,0},{1,3},{3,5},{5,7},{7,1},{8,10},{10,12},{12... | collective-permute-start | bytes 584 | tf_op jit(solution)/shard_map/ppermute | solution.py:18
  67.3 28.2 %collective-permute-start.15 = (f32[1,48]{1,0:T(1,128)S(1)}, f32[1,48]{1,0:T(1,128)S(1)}, u32[]{:S(2)}, u32[]{:S(2)}) collective-permute-start(f32[1,48]{1,0:T(1,128)S(1)} %get-tuple-element.31), channel_id=1, source_target_pairs={{0,4},{2,6},{4,0},{6,2},{1,5},{3,7},{5,1},{7,3},{8,12},{10,14},{12... | collective-permute-start | bytes 584 | tf_op jit(solution)/shard_map/ppermute | solution.py:18
  67.3 2.4 %copy-start.11 = (bf16[128,1024]{1,0:T(8,128)(2,1)}, bf16[128,1024]{1,0:T(8,128)(2,1)S(1)}, u32[]{:S(2)}) copy-start(bf16[128,1024]{1,0:T(8,128)(2,1)S(1)} %collective-permute-done.8.queries) | copy-start | bytes 786436
  67.3 28.2 %collective-permute-start.16 = (f32[1,48]{1,0:T(1,128)S(1)}, f32[1,48]{1,0:T(1,128)S(1)}, u32[]{:S(2)}, u32[]{:S(2)}) collective-permute-start(f32[1,48]{1,0:T(1,128)S(1)} %get-tuple-element.30), channel_id=1, source_target_pairs={{0,6},{2,0},{4,2},{6,4},{1,7},{3,1},{5,3},{7,5},{8,14},{10,8},{12,... | collective-permute-start | bytes 584 | tf_op jit(solution)/shard_map/ppermute | solution.py:18
  74.4 5.1 %copy-start.1 = (bf16[128,1024]{1,0:T(8,128)(2,1)S(1)}, bf16[128,1024]{1,0:T(8,128)(2,1)}, u32[]{:S(2)}) copy-start(bf16[128,1024]{1,0:T(8,128)(2,1)} %attend.6) | copy-start | bytes 786436
  77.5 18.1 %collective-permute-start.7 = (f32[1,128]{1,0:T(1,128)S(1)}, f32[1,128]{1,0:T(1,128)S(1)}, u32[]{:S(2)}, u32[]{:S(2)}) collective-permute-start(f32[1,128]{1,0:T(1,128)S(1)} %convert_add_fusion.2), channel_id=1, source_target_pairs={{0,8},{8,16},{16,24},{24,0},{1,9},{9,17},{17,25},{25,1},{2,10},{10... | collective-permute-start | bytes 1544 | tf_op jit(solution)/shard_map/ppermute | solution.py:18
  79.5 17.0 %copy-start.6 = (bf16[128,2048]{1,0:T(8,128)(2,1)}, bf16[128,2048]{1,0:T(8,128)(2,1)S(1)}, u32[]{:S(2)}) copy-start(bf16[128,2048]{1,0:T(8,128)(2,1)S(1)} %add_convert_fusion.2.rest_0_) | copy-start | bytes 1572868
  79.5 16.2 %copy-start.14 = (f32[1,4096]{1,0:T(1,128)S(1)}, f32[1,4096]{1,0:T(1,128)}, u32[]{:S(2)}) copy-start(f32[1,4096]{1,0:T(1,128)} %param.13) | copy-start | bytes 49156
  82.6 20.0 %copy-start.9 = (bf16[1,1,128,4096]{3,2,1,0:T(8,128)(2,1)S(1)}, bf16[1,1,128,4096]{3,2,1,0:T(8,128)(2,1)}, u32[]{:S(2)}) copy-start(bf16[1,1,128,4096]{3,2,1,0:T(8,128)(2,1)} %param.11) | copy-start | bytes 3145732
  82.6 26.0 %collective-permute-start.12 = (bf16[128,2048]{1,0:T(8,128)(2,1)S(1)}, bf16[128,2048]{1,0:T(8,128)(2,1)S(1)}, u32[]{:S(2)}, u32[]{:S(2)}) collective-permute-start(bf16[128,2048]{1,0:T(8,128)(2,1)S(1)} %add_convert_fusion.2.rest_0_), channel_id=1, source_target_pairs={{0,2},{2,4},{4,6},{6,0},{1,3},{3,5},{5,7},{7,1},{8,10},{10,12},{12... | collective-permute-start | bytes 1572872 | tf_op jit(solution)/shard_map/ppermute | solution.py:18
  96.4 1.6 copy-start.8
  96.4 21.6 %collective-permute-start.13 = (bf16[128,2048]{1,0:T(8,128)(2,1)S(1)}, bf16[128,2048]{1,0:T(8,128)(2,1)S(1)}, u32[]{:S(2)}, u32[]{:S(2)}) collective-permute-start(bf16[128,2048]{1,0:T(8,128)(2,1)S(1)} %add_convert_fusion.1.rest_1_), channel_id=1, source_target_pairs={{0,2},{2,4},{4,6},{6,0},{1,3},{3,5},{5,7},{7,1},{8,10},{10,12},{12... | collective-permute-start | bytes 1572872 | tf_op jit(solution)/shard_map/ppermute | solution.py:18
  102.7 3.0 %copy-start = (bf16[128,1024]{1,0:T(8,128)(2,1)S(1)}, bf16[128,1024]{1,0:T(8,128)(2,1)}, u32[]{:S(2)}) copy-start(bf16[128,1024]{1,0:T(8,128)(2,1)} %attend.7) | copy-start | bytes 786436
  118.9 14.0 %collective-permute-start.17 = (bf16[1,48,4096]{2,1,0:T(8,128)(2,1)S(1)}, bf16[1,48,4096]{2,1,0:T(8,128)(2,1)S(1)}, u32[]{:S(2)}, u32[]{:S(2)}) collective-permute-start(bf16[1,48,4096]{2,1,0:T(8,128)(2,1)S(1)} %get-tuple-element.13), channel_id=1, source_target_pairs={{0,2},{2,4},{4,6},{6,0},{1,3},{3,5},{5,7},{7,1},{8,10},{10,12},{12... | collective-permute-start | bytes 1179656 | tf_op jit(solution)/shard_map/ppermute | solution.py:18
  121.2 26.4 %collective-permute-start.18 = (bf16[1,48,4096]{2,1,0:T(8,128)(2,1)S(1)}, bf16[1,48,4096]{2,1,0:T(8,128)(2,1)S(1)}, u32[]{:S(2)}, u32[]{:S(2)}) collective-permute-start(bf16[1,48,4096]{2,1,0:T(8,128)(2,1)S(1)} %get-tuple-element.12), channel_id=1, source_target_pairs={{0,4},{2,6},{4,0},{6,2},{1,5},{3,7},{5,1},{7,3},{8,12},{10,14},{12... | collective-permute-start | bytes 1179656 | tf_op jit(solution)/shard_map/ppermute | solution.py:18
  122.0 25.6 %collective-permute-start.19 = (bf16[1,48,4096]{2,1,0:T(8,128)(2,1)S(1)}, bf16[1,48,4096]{2,1,0:T(8,128)(2,1)S(1)}, u32[]{:S(2)}, u32[]{:S(2)}) collective-permute-start(bf16[1,48,4096]{2,1,0:T(8,128)(2,1)S(1)} %get-tuple-element.11), channel_id=1, source_target_pairs={{0,6},{2,0},{4,2},{6,4},{1,7},{3,1},{5,3},{7,5},{8,14},{10,8},{12,... | collective-permute-start | bytes 1179656 | tf_op jit(solution)/shard_map/ppermute | solution.py:18
  149.0 9.4 %collective-permute-start.20 = (bf16[4,48,4096]{2,1,0:T(8,128)(2,1)S(1)}, bf16[4,48,4096]{2,1,0:T(8,128)(2,1)}, u32[]{:S(2)}, u32[]{:S(2)}) collective-permute-start(bf16[4,48,4096]{2,1,0:T(8,128)(2,1)S(1)} %get-tuple-element.14), channel_id=1, source_target_pairs={{0,1},{1,0},{2,3},{3,2},{4,5},{5,4},{6,7},{7,6},{8,9},{9,8},{10,11... | collective-permute-start | bytes 4718600 | tf_op jit(solution)/shard_map/ppermute | solution.py:18
  174.5 7.8 %collective-permute-start.21 = (bf16[4,48,4096]{2,1,0:T(8,128)(2,1)}, bf16[4,48,4096]{2,1,0:T(8,128)(2,1)S(1)}, u32[]{:S(2)}, u32[]{:S(2)}) collective-permute-start(bf16[4,48,4096]{2,1,0:T(8,128)(2,1)} %bitcast.122), channel_id=1, source_target_pairs={{0,1},{1,0},{2,3},{3,2},{4,5},{5,4},{6,7},{7,6},{8,9},{9,8},{10,11... | collective-permute-start | bytes 4718600 | tf_op jit(solution)/shard_map/ppermute | solution.py:18
  175.0 7.3 %copy-start.13 = (f32[1,4096]{1,0:T(1,128)S(1)}, f32[1,4096]{1,0:T(1,128)}, u32[]{:S(2)}) copy-start(f32[1,4096]{1,0:T(1,128)} %get-tuple-element.28.inverse_gain) | copy-start | bytes 49156
  185.0 13.2 %collective-permute-start.22 = (bf16[1,48,4096]{2,1,0:T(8,128)(2,1)S(1)}, bf16[1,48,4096]{2,1,0:T(8,128)(2,1)S(1)}, u32[]{:S(2)}, u32[]{:S(2)}) collective-permute-start(bf16[1,48,4096]{2,1,0:T(8,128)(2,1)S(1)} %get-tuple-element.5), channel_id=1, source_target_pairs={{0,8},{2,10},{4,12},{6,14},{8,16},{10,18},{12,20},{14,22},{16,24},... | collective-permute-start | bytes 1179656 | tf_op jit(solution)/shard_map/ppermute | solution.py:287
  186.6 20.4 %collective-permute-start.23 = (bf16[1,48,4096]{2,1,0:T(8,128)(2,1)S(1)}, bf16[1,48,4096]{2,1,0:T(8,128)(2,1)S(1)}, u32[]{:S(2)}, u32[]{:S(2)}) collective-permute-start(bf16[1,48,4096]{2,1,0:T(8,128)(2,1)S(1)} %get-tuple-element.8), channel_id=1, source_target_pairs={{0,14},{2,8},{4,10},{6,12},{8,22},{10,16},{12,18},{14,20},{16,30},... | collective-permute-start | bytes 1179656 | tf_op jit(solution)/shard_map/ppermute | solution.py:287
  197.3 35.4 %collective-permute-start.24 = (bf16[1,48,4096]{2,1,0:T(8,128)(2,1)S(1)}, bf16[1,48,4096]{2,1,0:T(8,128)(2,1)S(1)}, u32[]{:S(2)}, u32[]{:S(2)}) collective-permute-start(bf16[1,48,4096]{2,1,0:T(8,128)(2,1)S(1)} %get-tuple-element.7), channel_id=1, source_target_pairs={{0,12},{2,14},{4,8},{6,10},{8,20},{10,22},{12,16},{14,18},{16,28},... | collective-permute-start | bytes 1179656 | tf_op jit(solution)/shard_map/ppermute | solution.py:287
  197.7 35.0 %collective-permute-start.25 = (bf16[1,48,4096]{2,1,0:T(8,128)(2,1)S(1)}, bf16[1,48,4096]{2,1,0:T(8,128)(2,1)S(1)}, u32[]{:S(2)}, u32[]{:S(2)}) collective-permute-start(bf16[1,48,4096]{2,1,0:T(8,128)(2,1)S(1)} %get-tuple-element.6), channel_id=1, source_target_pairs={{0,10},{2,12},{4,14},{6,8},{8,18},{10,20},{12,22},{14,16},{16,26},... | collective-permute-start | bytes 1179656 | tf_op jit(solution)/shard_map/ppermute | solution.py:287

commit v9 on v7

--- a/solution.py
+++ b/solution.py
@@ -13,6 +13,10 @@
 def shift(value, axis, by):
     devices = lax.axis_size(axis)
     return lax.ppermute(value, axis, [(i, (i + by) % devices) for i in range(devices)])
+
+
+def after(value, *earlier):
+    return lax.optimization_barrier((value, *earlier))[0]
 
 
 def attend_block(query_block, key_rows, value_rows, row_ids, col_ids):
@@ -27,7 +31,7 @@
     return attended.astype(jnp.bfloat16)
 
 
-def mixed_halves(queries, keys_values, residual, out_weight, notes, slots_here):
+def mixed_halves(queries, keys_values, residual, out_weight):
     contexts, exps = lax.axis_size("ctx"), lax.axis_size("exp")
     me, my_exp = lax.axis_index("ctx"), lax.axis_index("exp")
     rows = queries.shape[0]
@@ -35,27 +39,25 @@
     local_heads = QUERY_HEADS // contexts
     group_width = local_heads * HEAD_SIZE
 
-    note_rows = -(-len(notes[0]) // 16) * 16
-
-    def pair_for(owner, k):
+    def pair_for(owner):
         head = owner * local_heads // (QUERY_HEADS // KEY_VALUE_HEADS)
         key = lax.dynamic_slice_in_dim(keys_values, head * HEAD_SIZE, HEAD_SIZE, 1)
         value = lax.dynamic_slice_in_dim(
             keys_values, (KEY_VALUE_HEADS + head) * HEAD_SIZE, HEAD_SIZE, 1
         )
-        pair = jnp.concatenate([key, value], axis=1)
-        note = jnp.pad(notes[k], ((0, note_rows - len(notes[k])), (0, 2 * HEAD_SIZE - rows)))
-        return jnp.concatenate([pair, note], axis=0)
+        return jnp.concatenate([key, value], axis=1)
 
     def queries_for(owner):
         return lax.dynamic_slice_in_dim(queries, owner * group_width, group_width, 1)
 
-    pairs = [pair_for(me, 0)]
+    pairs = [pair_for(me)]
     blocks = [queries_for(me)]
     for k in range(1, contexts):
-        pairs.append(shift(pair_for((me + k) % contexts, k), "ctx", k))
+        pairs.append(shift(pair_for((me + k) % contexts), "ctx", k))
     for k in range(1, contexts):
         outgoing = queries_for((me + k) % contexts)
+        if k > 1:
+            outgoing = after(outgoing, blocks[1])
         blocks.append(shift(outgoing, "ctx", k))
     if exps == 2:
         weights = [out_weight, shift(out_weight, "exp", 1)]
@@ -66,26 +68,23 @@
         first = 0
     offsets = [first, width // 2 - first]
 
-    arrived_notes = [pair[rows : rows + len(notes[0]), :rows] for pair in pairs]
-    pair_rows = jnp.concatenate([pair[:rows] for pair in pairs], axis=0)
+    pair_rows = jnp.concatenate(pairs, axis=0)
     key_rows, value_rows = pair_rows[:, :HEAD_SIZE], pair_rows[:, HEAD_SIZE:]
     within = jnp.arange(rows, dtype=jnp.int32)
     origins = [(me - k) % contexts * rows for k in range(contexts)]
     col_ids = jnp.concatenate([origin + within for origin in origins])
 
-    held, next_slots = [None, None], None
+    held, sent = [None, None], []
     for k in [*range(1, contexts), 0]:
+        block = blocks[k] if k == 1 else after(blocks[k], *sent)
         attended = attend_block(
-            blocks[k].reshape(rows, local_heads, HEAD_SIZE),
+            block.reshape(rows, local_heads, HEAD_SIZE),
             key_rows,
             value_rows,
             origins[k] + within,
             col_ids,
         ).reshape(rows, group_width)
-        if k == contexts - 1:
-            follows = slots_here + held[0][0, 0].astype(jnp.float32) * 0.0
-            next_slots = shift(follows, "pipe", 1)
-        terms = []
+        terms, sent = [], []
         for half in range(2):
             term = jnp.dot(attended, weights[half], preferred_element_type=jnp.float32)
             if k == 0:
@@ -97,10 +96,11 @@
             if held[half] is not None:
                 term = term + held[half].astype(jnp.float32)
             if k == 0:
-                held[half] = term + next_slots[0, 0] * 0.0
+                held[half] = term
             else:
-                held[half] = shift(term.astype(jnp.bfloat16), "ctx", 1)
-    return held, first, arrived_notes, next_slots.astype(jnp.int32)
+                sent.append(term.astype(jnp.bfloat16))
+                held[half] = shift(sent[half], "ctx", 1)
+    return held, first
 
 
 def on_device(
@@ -136,42 +136,36 @@
     slot_index = (distance * per_context + expert_ids % per_context) * capacity + position
     slot_ids = jnp.arange(slots, dtype=jnp.int32)
     slot_match = (slot_ids[:, None] == slot_index[None, :]).astype(jnp.bfloat16)
-    weights = route_weight[0, 0, :, 0]
-    coarse = lax.reduce_precision(weights, exponent_bits=8, mantissa_bits=7)
-    notes = []
-    for k in range(contexts):
-        local = slot_index - k * per_context * capacity
-        local = jnp.where((local >= 0) & (local < per_context * capacity), local, -1)
-        note = jnp.stack([coarse, weights - coarse, local.astype(jnp.float32)], axis=0)
-        notes.append(note.astype(jnp.bfloat16))
-
-    halves, first, arrived_notes, next_slots = mixed_halves(
-        queries[0, 0],
-        rotated_keys_values[0, 0],
-        residual[0, 0],
-        out_weight[0],
-        notes,
-        slot_index.astype(jnp.float32)[None, :],
+    hits = slot_ids[:, None] == slot_index[None, :]
+    slot_weights = jnp.sum(jnp.where(hits, route_weight[0, 0, :, 0], 0.0), axis=1)
+    told = jnp.concatenate([slot_weights, slot_index.astype(jnp.float32)])
+    told = lax.all_gather(told, ("pipe", "ctx"))
+    pipes, my_pipe = lax.axis_size("pipe"), lax.axis_index("pipe")
+    width = per_context * capacity
+    arrived_weights = [
+        lax.dynamic_slice(told, (my_pipe * contexts + (me - k) % contexts, k * width), (1, width))
+        for k in range(contexts)
+    ]
+    next_slots = lax.dynamic_slice(
+        told, ((my_pipe - 1) % pipes * contexts + me, slots), (1, token_rows)
+    )[0].astype(jnp.int32)
+
+    halves, first = mixed_halves(
+        queries[0, 0], rotated_keys_values[0, 0], residual[0, 0], out_weight[0]
     )
     mixed_rows = jnp.concatenate(halves, axis=1)
     if exps == 2:
         mixed_rows = jnp.where(first == 0, mixed_rows, jnp.concatenate(halves[::-1], axis=1))
 
-    gain = norm_gain[0]
-    scaled = (mixed_rows * gain).astype(jnp.bfloat16)
+    gain, inverse_gain = norm_gain[0], 1.0 / norm_gain[0]
+    beside = next_slots[0].astype(jnp.float32) + sum(w[0, 0] for w in arrived_weights)
+    scaled = (mixed_rows * (gain + beside * 0.0)).astype(jnp.bfloat16)
     packed = jnp.dot(slot_match, scaled, preferred_element_type=jnp.float32).astype(jnp.bfloat16)
     packed = packed.reshape(contexts, per_context, capacity, model_width)
     arrived = jnp.stack(
         [packed[0]] + [shift(packed[k], "ctx", k) for k in range(1, contexts)], axis=0
     )
-
-    here = jnp.arange(per_context * capacity, dtype=jnp.float32)
-    slot_weights = []
-    for note in arrived_notes:
-        note = note.astype(jnp.float32)
-        hits = note[2][None, :] == here[:, None]
-        slot_weights.append(jnp.sum(jnp.where(hits, note[0] + note[1], 0.0), axis=1))
-    slot_weights = jnp.stack(slot_weights, axis=0).reshape(contexts, per_context, capacity, 1)
+    arrived = lax.optimization_barrier(arrived)
 
     def wanted_by(blocks, exp):
         if per_context == 1:
@@ -182,7 +176,7 @@
 
     def expert_part(rows):
         rows = rows.reshape(-1, model_width)
-        unscaled = rows.astype(jnp.float32) / gain
+        unscaled = rows.astype(jnp.float32) * inverse_gain
         mean_square = jnp.mean(unscaled * unscaled, axis=-1, keepdims=True)
         gate_up = jnp.dot(rows, in_weight[0, 0], preferred_element_type=jnp.float32)
         gate_up = gate_up * lax.rsqrt(mean_square + 1e-06)
@@ -194,7 +188,8 @@
     others = [
         shift(wanted_by(arrived, (my_exp + k) % exps), "exp", k) for k in range(1, exps)
     ]
-    own_part = expert_part(wanted_by(arrived, my_exp)).reshape(contexts, capacity, model_width)
+    own_part = lax.optimization_barrier(expert_part(wanted_by(arrived, my_exp)))
+    own_part = own_part.reshape(contexts, capacity, model_width)
     other_parts = expert_part(jnp.concatenate(others, axis=0)).astype(jnp.bfloat16)
     other_parts = other_parts.reshape(exps - 1, contexts, capacity, model_width)
     sums = [0.0] * per_context
@@ -205,9 +200,9 @@
         else:
             place = (my_exp + k) % exps // group_size
             sums = [s + jnp.where(place == i, back, 0.0) for i, s in enumerate(sums)]
-    finished = (
-        arrived.astype(jnp.float32) / gain + slot_weights * jnp.stack(sums, axis=1)
-    ).astype(jnp.bfloat16)
+    weights = jnp.stack(arrived_weights, axis=0).reshape(contexts, per_context, capacity, 1)
+    finished = arrived.astype(jnp.float32) * inverse_gain + weights * jnp.stack(sums, axis=1)
+    finished = finished.astype(jnp.bfloat16)
 
     def to_next_owner(rows, k):
         pipes = lax.axis_size("pipe")
@@ -221,7 +216,7 @@
     returned = jnp.concatenate(
         [to_next_owner(finished[k], k).reshape(-1, model_width) for k in range(contexts)], axis=0
     )
-    next_match = (slot_ids[None, :] == next_slots[0][:, None]).astype(jnp.bfloat16)
+    next_match = (slot_ids[None, :] == next_slots[:, None]).astype(jnp.bfloat16)
     layer = jnp.dot(next_match, returned, preferred_element_type=jnp.float32)
     return layer.astype(jnp.bfloat16).reshape(1, 1, token_rows, model_width)
 

time: 230 us -> 271 us (1.18)
  blocking collectives: 0 us -> 76.5 us
  starting transfers between devices: 41.6 us -> 26.3 us
  other arithmetic: 14.3 us -> 6.13 us
  waiting for transfers between devices: 104 us -> 97.2 us
  matrix products: 62.8 us -> 58.1 us
    unnamed x0 -> x1, blocking collectives: none -> 76.5 us
    ppermute x19 -> x18, starting transfers between devices: 29.3 us -> 18.7 us  [shift(): lax.ppermute(value, axis, [(i, (i + by) % devices) for i in range(devices)])]
    ppermute x4, starting transfers between devices: 12.3 us -> 7.55 us  [to_next_owner(): return lax.ppermute(rows, ('pipe', 'ctx'), pairs)]
    ppermute x19 -> x18, waiting for transfers between devices: 70.2 us -> 66.9 us  [shift(): lax.ppermute(value, axis, [(i, (i + by) % devices) for i in range(devices)])]
    ppermute x4, waiting for transfers between devices: 33.4 us -> 30.3 us  [to_next_owner(): return lax.ppermute(rows, ('pipe', 'ctx'), pairs)]
  transfers between devices with their start and end apart: 23 -> 22, of which waited for: 10 -> 10; matrix products, arithmetic and copies ran while one was open for 23% -> 19% of each run, Pallas kernels for 0% -> 0%
where the time goes in v9:
time: 271 us; the launch traced here: 270 us
  waiting for transfers between devices  97.2 us (36%)
  blocking collectives  76.5 us (28%)
  matrix products  58.1 us (21%)
  starting transfers between devices  26.3 us (10%)
  other arithmetic  6.13 us (2%)
  local copies, waits for them, and re-layouts  4.51 us (2%)
    unnamed x1, blocking collectives  76.5 us
    ppermute x18, waiting for transfers between devices, shift(): lax.ppermute(value, axis, [(i, (i + by) % devices) for i in range(devices)])  66.9 us
    ppermute x4, waiting for transfers between devices, to_next_owner(): return lax.ppermute(rows, ('pipe', 'ctx'), pairs)  30.3 us
    dot_general x8, matrix products, mixed_halves(): term = jnp.dot(attended, weights[half], preferred_element_type=jnp.float32)  23.4 us
    ppermute x18, starting transfers between devices, shift(): lax.ppermute(value, axis, [(i, (i + by) % devices) for i in range(devices)])  18.7 us
    dot_general x2, matrix products, expert_part(): gate_up = jnp.dot(rows, in_weight[0, 0], preferred_element_type=jnp.float32)  12 us
    dot_general x2, matrix products, expert_part(): jnp.dot(hidden, down_weight[0, 0], preferred_element_type=jnp.float32)  9.57 us
    ppermute x4, starting transfers between devices, to_next_owner(): return lax.ppermute(rows, ('pipe', 'ctx'), pairs)  7.55 us
  transfers between devices with their start and end apart: 22, of which 10 were waited for; matrix products, arithmetic and copies ran while one was open for 19% of the time, Pallas kernels for 0%

profile of v9, /device:TPU:0, one launch (start us, length us, event | category | flops | bytes accessed | tf_op | source)
XLA Modules:
  0.0 270.2 jit_solution(12461715156829222030)
XLA Ops:
  0.0 0.5 collective-permute-start.6
  0.5 1.3 constant_dynamic-slice_fusion.1
  1.9 2.7 collective-permute-start.3
  4.7 2.2 collective-permute-start.2
  7.0 0.9 collective-permute-start.1
  7.9 1.6 collective-permute-start
  9.6 0.2 reduce_window_sum.11
  9.8 0.6 dynamic-slice.14
  11.0 0.2 select_reduce_fusion.1
  11.4 0.2 maximum_dynamic-update-slice_fusion
  11.6 76.5 %all-reduce = f32[5120]{0:T(1024)S(1)} all-reduce(f32[5120]{0:T(1024)S(1)} %maximum_dynamic-update-slice_fusion), channel_id=2, replica_groups=mesh['pipe'=4,'ctx'=4,'exp'=2] {'pipe','ctx'}, use_global_device_ids=true, to_apply=%add | all-reduce | flops 5120 | bytes 40960
  88.5 0.2 copy-done.7
  89.0 0.6 broadcast_divide_fusion
  89.6 0.2 broadcast_compare_fusion
  89.8 0.8 copy.34
  90.8 0.2 copy.37
  91.2 0.8 fusion.108
  92.0 1.0 convolution_convert_fusion.5
  93.0 2.9 %fusion.90 = bf16[128,2048]{1,0:T(8,128)(2,1)S(1)} fusion(bf16[128,1024]{0,1:T(8,128)(2,1)S(1)} %bitcast.235, bf16[1,1024,2048]{2,1,0:T(8,128)(2,1)} %param.12), kind=kOutput, calls=%fused_computation.161 | convolution fusion | flops 536870912 | bytes 4980736 | tf_op jit(solution)/shard_map/dot_general | solution.py:89
  96.0 2.0 collective-permute-start.7
  98.0 2.9 %fusion.112 = bf16[128,2048]{1,0:T(8,128)(2,1)S(1)} fusion(bf16[128,1024]{0,1:T(8,128)(2,1)S(1)} %bitcast.236, bf16[1024,2048]{1,0:T(8,128)(2,1)} %collective-permute-done.6), kind=kOutput, calls=%fused_computation.178 | convolution fusion | flops 536870912 | bytes 4980736 | tf_op jit(solution)/shard_map/dot_general | solution.py:89
  100.9 1.6 collective-permute-start.8
  102.5 36.4 %collective-permute-done.5 = bf16[128,1024]{0,1:T(8,128)(2,1)} collective-permute-done((bf16[128,1024]{0,1:T(8,128)(2,1)S(1)}, bf16[128,1024]{0,1:T(8,128)(2,1)}, u32[]{:S(2)}, u32[]{:S(2)}) %collective-permute-start.5) | collective-permute-done | bytes 262176 | tf_op jit(solution)/shard_map/ppermute | solution.py:15
  138.9 1.7 fusion.109
  140.6 2.0 convolution_convert_fusion.4
  142.6 2.9 %fusion.88 = f32[128,2048]{1,0:T(8,128)S(1)} fusion(bf16[128,1024]{0,1:T(8,128)(2,1)S(1)} %bitcast.239, bf16[1,1024,2048]{2,1,0:T(8,128)(2,1)} %param.12), kind=kOutput, calls=%fused_computation.159 | convolution fusion | flops 536870912 | bytes 5505024 | tf_op jit(solution)/shard_map/dot_general | solution.py:89
  145.6 2.9 %fusion.113 = f32[128,2048]{1,0:T(8,128)S(1)} fusion(bf16[128,1024]{0,1:T(8,128)(2,1)S(1)} %bitcast.240, bf16[1024,2048]{1,0:T(8,128)(2,1)} %collective-permute-done.6), kind=kOutput, calls=%fused_computation.179 | convolution fusion | flops 536870912 | bytes 5505024 | tf_op jit(solution)/shard_map/dot_general | solution.py:89
  148.8 0.2 collective-permute-start.10
  149.1 1.7 fusion.110
  150.8 2.0 convolution_convert_fusion.3
  152.8 2.9 %fusion.86 = f32[128,2048]{1,0:T(8,128)S(1)} fusion(bf16[128,1024]{0,1:T(8,128)(2,1)S(1)} %bitcast.241, bf16[1,1024,2048]{2,1,0:T(8,128)(2,1)} %param.12), kind=kOutput, calls=%fused_computation.157 | convolution fusion | flops 536870912 | bytes 5505024 | tf_op jit(solution)/shard_map/dot_general | solution.py:89
  155.8 2.9 %fusion.114 = f32[128,2048]{1,0:T(8,128)S(1)} fusion(bf16[128,1024]{0,1:T(8,128)(2,1)S(1)} %bitcast.242, bf16[1024,2048]{1,0:T(8,128)(2,1)} %collective-permute-done.6), kind=kOutput, calls=%fused_computation.180 | convolution fusion | flops 536870912 | bytes 5505024 | tf_op jit(solution)/shard_map/dot_general | solution.py:89
  158.7 4.1 %collective-permute-done.9 = bf16[128,2048]{1,0:T(8,128)(2,1)S(1)} collective-permute-done((bf16[128,2048]{1,0:T(8,128)(2,1)S(1)}, bf16[128,2048]{1,0:T(8,128)(2,1)S(1)}, u32[]{:S(2)}, u32[]{:S(2)}) %collective-permute-start.9) | collective-permute-done | bytes 524320 | tf_op jit(solution)/shard_map/ppermute | solution.py:15
  163.0 5.4 %collective-permute-done.10 = bf16[128,2048]{1,0:T(8,128)(2,1)S(1)} collective-permute-done((bf16[128,2048]{1,0:T(8,128)(2,1)S(1)}, bf16[128,2048]{1,0:T(8,128)(2,1)S(1)}, u32[]{:S(2)}, u32[]{:S(2)}) %collective-permute-start.10) | collective-permute-done | bytes 524320 | tf_op jit(solution)/shard_map/ppermute | solution.py:15
  168.5 0.9 add_convert_fusion
  169.4 1.7 collective-permute-start.12
  171.1 0.8 fusion.111
  171.9 1.0 convolution_convert_fusion.2
  173.0 0.2 copy-done
  173.2 2.9 %convolution_add_fusion.1 = f32[128,2048]{1,0:T(8,128)S(1)} fusion(bf16[128,1024]{0,1:T(8,128)(2,1)S(1)} %bitcast.237, bf16[1,1,128,4096]{3,2,1,0:T(8,128)(2,1)S(1)} %copy-done, s32[]{:T(128)S(6)} %select_n.201, bf16[1,1024,2048]{2,1,0:T(8,128)(2,1)} %param.12), kind=kOutput, calls=%fused_computation.24 | convolution fusion | flops 537395200 | bytes 6029316 | tf_op jit(solution)/shard_map/dot_general | solution.py:89
  176.1 2.9 %convolution_add_fusion = f32[128,2048]{1,0:T(8,128)S(1)} fusion(bf16[128,1024]{0,1:T(8,128)(2,1)S(1)} %bitcast.238, bf16[1024,2048]{1,0:T(8,128)(2,1)} %collective-permute-done.6, bf16[1,1,128,4096]{3,2,1,0:T(8,128)(2,1)S(1)} %copy-done, s32[]{:T(128)S(6)} %select_n.202), kind=kOutput, calls=%fused_computation.23 | convolution fusion | flops 537395200 | bytes 6029316 | tf_op jit(solution)/shard_map/dot_general | solution.py:89
  179.2 1.5 collective-permute-done.12
  180.8 0.6 convolution_convert_fusion
  181.6 1.3 collective-permute-start.15
  182.9 1.7 collective-permute-start.14
  184.5 1.8 collective-permute-start.13
  186.4 3.1 %collective-permute-done.15 = bf16[1,48,4096]{2,1,0:T(8,128)(2,1)S(1)} collective-permute-done((bf16[1,48,4096]{2,1,0:T(8,128)(2,1)S(1)}, bf16[1,48,4096]{2,1,0:T(8,128)(2,1)S(1)}, u32[]{:S(2)}, u32[]{:S(2)}) %collective-permute-start.15) | collective-permute-done | bytes 393248 | tf_op jit(solution)/shard_map/ppermute | solution.py:15
  189.4 13.5 %collective-permute-done.14 = bf16[1,48,4096]{2,1,0:T(8,128)(2,1)S(1)} collective-permute-done((bf16[1,48,4096]{2,1,0:T(8,128)(2,1)S(1)}, bf16[1,48,4096]{2,1,0:T(8,128)(2,1)S(1)}, u32[]{:S(2)}, u32[]{:S(2)}) %collective-permute-start.14) | collective-permute-done | bytes 393248 | tf_op jit(solution)/shard_map/ppermute | solution.py:15
  202.9 0.2 pad_maximum_fusion
  203.3 0.5 multiply_reduce_fusion.1
  203.8 2.8 %collective-permute-done.16 = bf16[4,48,4096]{2,1,0:T(8,128)(2,1)S(1)} collective-permute-done((bf16[4,48,4096]{2,1,0:T(8,128)(2,1)S(1)}, bf16[4,48,4096]{2,1,0:T(8,128)(2,1)S(1)}, u32[]{:S(2)}, u32[]{:S(2)}) %collective-permute-start.16) | collective-permute-done | bytes 1572896 | tf_op jit(solution)/shard_map/ppermute | solution.py:15
  206.6 0.5 multiply_reduce_fusion
  207.2 6.0 %fusion.20 = f32[192,1536]{1,0:T(8,128)S(1)} fusion(bf16[192,4096]{1,0:T(8,128)(2,1)S(1)} %bitcast.234, bf16[1,1,4096,1536]{3,2,1,0:T(8,128)(2,1)} %param.14, f32[192]{0:T(256)S(1)} %rsqrt.25), kind=kOutput, calls=%fused_computation.22 | convolution fusion | flops 2416214016 | bytes 15336192 | tf_op jit(solution)/shard_map/dot_general | solution.py:181
  213.2 5.4 %fusion.12 = bf16[192,4096]{1,0:T(8,128)(2,1)} fusion(bf16[1,1,768,4096]{3,2,1,0:T(8,128)(2,1)} %param.15, f32[192,1536]{1,0:T(8,128)S(1)} %fusion.20), kind=kOutput, calls=%fused_computation.12 | convolution fusion | flops 1209630720 | bytes 9043968 | tf_op jit(solution)/shard_map/dot_general | solution.py:186
  218.8 6.0 %fusion.17 = f32[192,1536]{1,0:T(8,128)S(1)} fusion(bf16[192,4096]{1,0:T(8,128)(2,1)S(1)} %bitcast.232, bf16[1,1,4096,1536]{3,2,1,0:T(8,128)(2,1)} %param.14, f32[192]{0:T(256)S(1)} %rsqrt.23), kind=kOutput, calls=%fused_computation.21 | convolution fusion | flops 2416214016 | bytes 15336192 | tf_op jit(solution)/shard_map/dot_general | solution.py:181
  224.8 4.2 %fusion.10 = f32[192,4096]{1,0:T(8,128)S(1)} fusion(bf16[1,1,768,4096]{3,2,1,0:T(8,128)(2,1)} %param.15, f32[192,1536]{1,0:T(8,128)S(1)} %fusion.17), kind=kOutput, calls=%fused_computation.10 | convolution fusion | flops 1208844288 | bytes 10616832 | tf_op jit(solution)/shard_map/dot_general | solution.py:186
  229.1 0.9 fusion.16
  230.2 4.7 %collective-permute-start.19 = (bf16[1,48,4096]{2,1,0:T(8,128)(2,1)S(1)}, bf16[1,48,4096]{2,1,0:T(8,128)(2,1)S(1)}, u32[]{:S(2)}, u32[]{:S(2)}) collective-permute-start(bf16[1,48,4096]{2,1,0:T(8,128)(2,1)S(1)} %get-tuple-element.20), channel_id=1, source_target_pairs={{0,14},{2,8},{4,10},{6,12},{8,22},{10,16},{12,18},{14,20},{16,30},... | collective-permute-start | bytes 1179656 | tf_op jit(solution)/shard_map/ppermute | solution.py:214
  234.8 2.8 %collective-permute-start.18 = (bf16[1,48,4096]{2,1,0:T(8,128)(2,1)S(1)}, bf16[1,48,4096]{2,1,0:T(8,128)(2,1)S(1)}, u32[]{:S(2)}, u32[]{:S(2)}) collective-permute-start(bf16[1,48,4096]{2,1,0:T(8,128)(2,1)S(1)} %get-tuple-element.17), channel_id=1, source_target_pairs={{0,8},{2,10},{4,12},{6,14},{8,16},{10,18},{12,20},{14,22},{16,24},... | collective-permute-start | bytes 1179656 | tf_op jit(solution)/shard_map/ppermute | solution.py:214
  237.6 0.8 fusion.137
  238.4 7.5 %collective-permute-done.21 = bf16[1,48,4096]{2,1,0:T(8,128)(2,1)S(1)} collective-permute-done((bf16[1,48,4096]{2,1,0:T(8,128)(2,1)S(1)}, bf16[1,48,4096]{2,1,0:T(8,128)(2,1)S(1)}, u32[]{:S(2)}, u32[]{:S(2)}) %collective-permute-start.21) | collective-permute-done | bytes 393248 | tf_op jit(solution)/shard_map/ppermute | solution.py:214
  245.9 15.9 %collective-permute-done.20 = bf16[1,48,4096]{2,1,0:T(8,128)(2,1)S(1)} collective-permute-done((bf16[1,48,4096]{2,1,0:T(8,128)(2,1)S(1)}, bf16[1,48,4096]{2,1,0:T(8,128)(2,1)S(1)}, u32[]{:S(2)}, u32[]{:S(2)}) %collective-permute-start.20) | collective-permute-done | bytes 393248 | tf_op jit(solution)/shard_map/ppermute | solution.py:214
  261.7 7.0 %collective-permute-done.18 = bf16[1,48,4096]{2,1,0:T(8,128)(2,1)S(1)} collective-permute-done((bf16[1,48,4096]{2,1,0:T(8,128)(2,1)S(1)}, bf16[1,48,4096]{2,1,0:T(8,128)(2,1)S(1)}, u32[]{:S(2)}, u32[]{:S(2)}) %collective-permute-start.18) | collective-permute-done | bytes 393248 | tf_op jit(solution)/shard_map/ppermute | solution.py:214
  268.7 1.5 fusion.15
  (93 shorter events, 2.9 us)
Async XLA Ops:
  0.0 4.6 %copy-start.1 = (bf16[1,1,128,512]{3,2,1,0:T(8,128)(2,1)S(1)}, bf16[1,1,128,512]{3,2,1,0:T(8,128)(2,1)}, u32[]{:S(2)}) copy-start(bf16[1,1,128,512]{3,2,1,0:T(8,128)(2,1)} %param.10) | copy-start | bytes 393220
  0.0 9.5 %copy-start.10 = (s32[1,1,128,1]{2,3,1,0:T(1,128)S(1)}, s32[1,1,128,1]{2,3,1,0:T(1,128)}, u32[]{:S(2)}) copy-start(s32[1,1,128,1]{2,3,1,0:T(1,128)} %param.16) | copy-start | bytes 1540
  0.0 98.0 %collective-permute-start.6 = (bf16[1024,2048]{1,0:T(8,128)(2,1)}, bf16[1024,2048]{1,0:T(8,128)(2,1)}, u32[]{:S(2)}, u32[]{:S(2)}) collective-permute-start(bf16[1024,2048]{1,0:T(8,128)(2,1)} %bitcast.230), channel_id=1, source_target_pairs={{0,1},{1,0},{2,3},{3,2},{4,5},{5,4},{6,7},{7,6},{8,9},{9,8},{10,11... | collective-permute-start | bytes 12582920 | tf_op jit(solution)/shard_map/ppermute | solution.py:15
  0.5 9.3 %copy-start.22 = (u32[32]{0:T(128)S(1)}, u32[32]{0:T(128)}, u32[]{:S(2)}) copy-start(u32[32]{0:T(128)} %constant.218) | copy-start | bytes 388
  0.5 10.8 %copy-start.21 = (f32[1,1,128,1]{2,3,1,0:T(1,128)S(1)}, f32[1,1,128,1]{2,3,1,0:T(1,128)}, u32[]{:S(2)}) copy-start(f32[1,1,128,1]{2,3,1,0:T(1,128)} %param.17) | copy-start | bytes 1540
  0.5 88.5 %copy-start.8 = (f32[1,4096]{1,0:T(1,128)S(1)}, f32[1,4096]{1,0:T(1,128)}, u32[]{:S(2)}) copy-start(f32[1,4096]{1,0:T(1,128)} %param.13) | copy-start | bytes 49156
  1.9 89.1 %collective-permute-start.3 = (bf16[128,1024]{0,1:T(8,128)(2,1)S(1)}, bf16[128,1024]{0,1:T(8,128)(2,1)S(1)}, u32[]{:S(2)}, u32[]{:S(2)}) collective-permute-start(bf16[128,1024]{0,1:T(8,128)(2,1)S(1)} %bitcast.249), channel_id=1, source_target_pairs={{0,2},{2,4},{4,6},{6,0},{1,3},{3,5},{5,7},{7,1},{8,10},{10,12},{12... | collective-permute-start | bytes 786440 | tf_op jit(solution)/shard_map/ppermute | solution.py:15
  4.7 86.3 %collective-permute-start.2 = (bf16[128,256]{1,0:T(8,128)(2,1)S(1)}, bf16[128,256]{1,0:T(8,128)(2,1)S(1)}, u32[]{:S(2)}, u32[]{:S(2)}) collective-permute-start(bf16[128,256]{1,0:T(8,128)(2,1)S(1)} %pad_maximum_fusion.4), channel_id=1, source_target_pairs={{0,6},{2,0},{4,2},{6,4},{1,7},{3,1},{5,3},{7,5},{8,14},{10,8},{12,... | collective-permute-start | bytes 196616 | tf_op jit(solution)/shard_map/ppermute | solution.py:15
  7.0 84.0 %collective-permute-start.1 = (bf16[128,256]{1,0:T(8,128)(2,1)S(1)}, bf16[128,256]{1,0:T(8,128)(2,1)S(1)}, u32[]{:S(2)}, u32[]{:S(2)}) collective-permute-start(bf16[128,256]{1,0:T(8,128)(2,1)S(1)} %pad_maximum_fusion.3), channel_id=1, source_target_pairs={{0,4},{2,6},{4,0},{6,2},{1,5},{3,7},{5,1},{7,3},{8,12},{10,14},{12... | collective-permute-start | bytes 196616 | tf_op jit(solution)/shard_map/ppermute | solution.py:15
  7.9 83.1 %collective-permute-start = (bf16[128,256]{1,0:T(8,128)(2,1)S(1)}, bf16[128,256]{1,0:T(8,128)(2,1)S(1)}, u32[]{:S(2)}, u32[]{:S(2)}) collective-permute-start(bf16[128,256]{1,0:T(8,128)(2,1)S(1)} %pad_maximum_fusion.2), channel_id=1, source_target_pairs={{0,2},{2,4},{4,6},{6,0},{1,3},{3,5},{5,7},{7,1},{8,10},{10,12},{12... | collective-permute-start | bytes 196616 | tf_op jit(solution)/shard_map/ppermute | solution.py:15
  11.2 77.3 %copy-start.11 = (s32[128]{0:T(128)}, s32[128]{0:T(128)S(1)}, u32[]{:S(2)}) copy-start(s32[128]{0:T(128)S(1)} %get-tuple-element.16) | copy-start | bytes 1540
  88.1 0.6 copy-start.7
  88.3 0.5 copy-start.13
  88.3 0.6 copy-start.15
  88.3 0.6 copy-start.17
  88.3 0.6 copy-start.19
  91.0 59.8 %copy-start.4 = (bf16[512,256]{1,0:T(8,128)(2,1)}, bf16[512,256]{1,0:T(8,128)(2,1)S(1)}, u32[]{:S(2)}) copy-start(bf16[512,256]{1,0:T(8,128)(2,1)S(1)} %pad_maximum_fusion.1) | copy-start | bytes 786436
  91.1 58.0 %collective-permute-start.4 = (bf16[128,1024]{0,1:T(8,128)(2,1)S(1)}, bf16[128,1024]{0,1:T(8,128)(2,1)}, u32[]{:S(2)}, u32[]{:S(2)}) collective-permute-start(bf16[128,1024]{0,1:T(8,128)(2,1)S(1)} %bitcast.252), channel_id=1, source_target_pairs={{0,6},{2,0},{4,2},{6,4},{1,7},{3,1},{5,3},{7,5},{8,14},{10,8},{12,... | collective-permute-start | bytes 786440 | tf_op jit(solution)/shard_map/ppermute | solution.py:15
  91.1 47.8 %collective-permute-start.5 = (bf16[128,1024]{0,1:T(8,128)(2,1)S(1)}, bf16[128,1024]{0,1:T(8,128)(2,1)}, u32[]{:S(2)}, u32[]{:S(2)}) collective-permute-start(bf16[128,1024]{0,1:T(8,128)(2,1)S(1)} %bitcast.253), channel_id=1, source_target_pairs={{0,4},{2,6},{4,0},{6,2},{1,5},{3,7},{5,1},{7,3},{8,12},{10,14},{12... | collective-permute-start | bytes 786440 | tf_op jit(solution)/shard_map/ppermute | solution.py:15
  96.0 52.5 %collective-permute-start.7 = (bf16[128,2048]{1,0:T(8,128)(2,1)S(1)}, bf16[128,2048]{1,0:T(8,128)(2,1)S(1)}, u32[]{:S(2)}, u32[]{:S(2)}) collective-permute-start(bf16[128,2048]{1,0:T(8,128)(2,1)S(1)} %fusion.90), channel_id=1, source_target_pairs={{0,2},{2,4},{4,6},{6,0},{1,3},{3,5},{5,7},{7,1},{8,10},{10,12},{12... | collective-permute-start | bytes 1572872 | tf_op jit(solution)/shard_map/ppermute | solution.py:15
  100.9 47.8 %collective-permute-start.8 = (bf16[128,2048]{1,0:T(8,128)(2,1)S(1)}, bf16[128,2048]{1,0:T(8,128)(2,1)S(1)}, u32[]{:S(2)}, u32[]{:S(2)}) collective-permute-start(bf16[128,2048]{1,0:T(8,128)(2,1)S(1)} %fusion.112), channel_id=1, source_target_pairs={{0,2},{2,4},{4,6},{6,0},{1,3},{3,5},{5,7},{7,1},{8,10},{10,12},{12... | collective-permute-start | bytes 1572872 | tf_op jit(solution)/shard_map/ppermute | solution.py:15
  148.6 14.2 %collective-permute-start.9 = (bf16[128,2048]{1,0:T(8,128)(2,1)S(1)}, bf16[128,2048]{1,0:T(8,128)(2,1)S(1)}, u32[]{:S(2)}, u32[]{:S(2)}) collective-permute-start(bf16[128,2048]{1,0:T(8,128)(2,1)S(1)} %add_convert_fusion.3), channel_id=1, source_target_pairs={{0,2},{2,4},{4,6},{6,0},{1,3},{3,5},{5,7},{7,1},{8,10},{10,12},{12... | collective-permute-start | bytes 1572872 | tf_op jit(solution)/shard_map/ppermute | solution.py:15
  148.8 19.6 %collective-permute-start.10 = (bf16[128,2048]{1,0:T(8,128)(2,1)S(1)}, bf16[128,2048]{1,0:T(8,128)(2,1)S(1)}, u32[]{:S(2)}, u32[]{:S(2)}) collective-permute-start(bf16[128,2048]{1,0:T(8,128)(2,1)S(1)} %add_convert_fusion.2), channel_id=1, source_target_pairs={{0,2},{2,4},{4,6},{6,0},{1,3},{3,5},{5,7},{7,1},{8,10},{10,12},{12... | collective-permute-start | bytes 1572872 | tf_op jit(solution)/shard_map/ppermute | solution.py:15
  158.7 12.4 %copy-start.2 = (bf16[1,1,128,1024]{2,3,1,0:T(8,128)(2,1)S(1)}, bf16[1,1,128,1024]{2,3,1,0:T(8,128)(2,1)}, u32[]{:S(2)}) copy-start(bf16[1,1,128,1024]{2,3,1,0:T(8,128)(2,1)} %copy.34) | copy-start | bytes 786436
  162.8 8.3 %copy-start.5 = (bf16[512,256]{1,0:T(8,128)(2,1)S(1)}, bf16[512,256]{1,0:T(8,128)(2,1)}, u32[]{:S(2)}) copy-start(bf16[512,256]{1,0:T(8,128)(2,1)} %copy-done.4) | copy-start | bytes 786436
  163.0 16.1 %collective-permute-start.11 = (bf16[128,2048]{1,0:T(8,128)(2,1)S(1)}, bf16[128,2048]{1,0:T(8,128)(2,1)S(1)}, u32[]{:S(2)}, u32[]{:S(2)}) collective-permute-start(bf16[128,2048]{1,0:T(8,128)(2,1)S(1)} %add_convert_fusion.1), channel_id=1, source_target_pairs={{0,2},{2,4},{4,6},{6,0},{1,3},{3,5},{5,7},{7,1},{8,10},{10,12},{12... | collective-permute-start | bytes 1572872 | tf_op jit(solution)/shard_map/ppermute | solution.py:15
  169.4 2.5 copy-start.3
  169.4 2.5 copy-start.6
  169.4 11.3 %collective-permute-start.12 = (bf16[128,2048]{1,0:T(8,128)(2,1)}, bf16[128,2048]{1,0:T(8,128)(2,1)S(1)}, u32[]{:S(2)}, u32[]{:S(2)}) collective-permute-start(bf16[128,2048]{1,0:T(8,128)(2,1)} %add_convert_fusion), channel_id=1, source_target_pairs={{0,2},{2,4},{4,6},{6,0},{1,3},{3,5},{5,7},{7,1},{8,10},{10,12},{12... | collective-permute-start | bytes 1572872 | tf_op jit(solution)/shard_map/ppermute | solution.py:15
  171.9 1.2 copy-start
  179.0 1.8 copy-start.9
  179.0 1.8 copy-start.12
  181.6 21.6 %copy-start.14 = (f32[1,48]{1,0:T(1,128)S(1)}, f32[1,48]{1,0:T(1,128)}, u32[]{:S(2)}) copy-start(f32[1,48]{1,0:T(1,128)} %copy-done.13) | copy-start | bytes 580
  181.6 21.6 %copy-start.16 = (f32[1,48]{1,0:T(1,128)S(1)}, f32[1,48]{1,0:T(1,128)}, u32[]{:S(2)}) copy-start(f32[1,48]{1,0:T(1,128)} %copy-done.15) | copy-start | bytes 580
  181.6 21.6 %copy-start.18 = (f32[1,48]{1,0:T(1,128)S(1)}, f32[1,48]{1,0:T(1,128)}, u32[]{:S(2)}) copy-start(f32[1,48]{1,0:T(1,128)} %copy-done.17) | copy-start | bytes 580
  181.6 21.6 %copy-start.20 = (f32[1,48]{1,0:T(1,128)S(1)}, f32[1,48]{1,0:T(1,128)}, u32[]{:S(2)}) copy-start(f32[1,48]{1,0:T(1,128)} %copy-done.19) | copy-start | bytes 580
  181.6 7.8 %collective-permute-start.15 = (bf16[1,48,4096]{2,1,0:T(8,128)(2,1)S(1)}, bf16[1,48,4096]{2,1,0:T(8,128)(2,1)S(1)}, u32[]{:S(2)}, u32[]{:S(2)}) collective-permute-start(bf16[1,48,4096]{2,1,0:T(8,128)(2,1)S(1)} %get-tuple-element.22), channel_id=1, source_target_pairs={{0,6},{2,0},{4,2},{6,4},{1,7},{3,1},{5,3},{7,5},{8,14},{10,8},{12,... | collective-permute-start | bytes 1179656 | tf_op jit(solution)/shard_map/ppermute | solution.py:15
  182.9 20.1 %collective-permute-start.14 = (bf16[1,48,4096]{2,1,0:T(8,128)(2,1)S(1)}, bf16[1,48,4096]{2,1,0:T(8,128)(2,1)S(1)}, u32[]{:S(2)}, u32[]{:S(2)}) collective-permute-start(bf16[1,48,4096]{2,1,0:T(8,128)(2,1)S(1)} %get-tuple-element.23), channel_id=1, source_target_pairs={{0,4},{2,6},{4,0},{6,2},{1,5},{3,7},{5,1},{7,3},{8,12},{10,14},{12... | collective-permute-start | bytes 1179656 | tf_op jit(solution)/shard_map/ppermute | solution.py:15
  184.5 18.4 %collective-permute-start.13 = (bf16[1,48,4096]{2,1,0:T(8,128)(2,1)S(1)}, bf16[1,48,4096]{2,1,0:T(8,128)(2,1)S(1)}, u32[]{:S(2)}, u32[]{:S(2)}) collective-permute-start(bf16[1,48,4096]{2,1,0:T(8,128)(2,1)S(1)} %get-tuple-element.24), channel_id=1, source_target_pairs={{0,2},{2,4},{4,6},{6,0},{1,3},{3,5},{5,7},{7,1},{8,10},{10,12},{12... | collective-permute-start | bytes 1179656 | tf_op jit(solution)/shard_map/ppermute | solution.py:15
  203.1 3.5 %collective-permute-start.16 = (bf16[4,48,4096]{2,1,0:T(8,128)(2,1)S(1)}, bf16[4,48,4096]{2,1,0:T(8,128)(2,1)S(1)}, u32[]{:S(2)}, u32[]{:S(2)}) collective-permute-start(bf16[4,48,4096]{2,1,0:T(8,128)(2,1)S(1)} %bitcast.231), channel_id=1, source_target_pairs={{0,1},{1,0},{2,3},{3,2},{4,5},{5,4},{6,7},{7,6},{8,9},{9,8},{10,11... | collective-permute-start | bytes 4718600 | tf_op jit(solution)/shard_map/ppermute | solution.py:15
  218.6 10.5 %collective-permute-start.17 = (bf16[4,48,4096]{2,1,0:T(8,128)(2,1)}, bf16[4,48,4096]{2,1,0:T(8,128)(2,1)S(1)}, u32[]{:S(2)}, u32[]{:S(2)}) collective-permute-start(bf16[4,48,4096]{2,1,0:T(8,128)(2,1)} %bitcast.65), channel_id=1, source_target_pairs={{0,1},{1,0},{2,3},{3,2},{4,5},{5,4},{6,7},{7,6},{8,9},{9,8},{10,11... | collective-permute-start | bytes 4718600 | tf_op jit(solution)/shard_map/ppermute | solution.py:15
  230.0 15.8 %collective-permute-start.21 = (bf16[1,48,4096]{2,1,0:T(8,128)(2,1)S(1)}, bf16[1,48,4096]{2,1,0:T(8,128)(2,1)S(1)}, u32[]{:S(2)}, u32[]{:S(2)}) collective-permute-start(bf16[1,48,4096]{2,1,0:T(8,128)(2,1)S(1)} %get-tuple-element.18), channel_id=1, source_target_pairs={{0,10},{2,12},{4,14},{6,8},{8,18},{10,20},{12,22},{14,16},{16,26},... | collective-permute-start | bytes 1179656 | tf_op jit(solution)/shard_map/ppermute | solution.py:214
  230.1 31.6 %collective-permute-start.20 = (bf16[1,48,4096]{2,1,0:T(8,128)(2,1)S(1)}, bf16[1,48,4096]{2,1,0:T(8,128)(2,1)S(1)}, u32[]{:S(2)}, u32[]{:S(2)}) collective-permute-start(bf16[1,48,4096]{2,1,0:T(8,128)(2,1)S(1)} %get-tuple-element.19), channel_id=1, source_target_pairs={{0,12},{2,14},{4,8},{6,10},{8,20},{10,22},{12,16},{14,18},{16,28},... | collective-permute-start | bytes 1179656 | tf_op jit(solution)/shard_map/ppermute | solution.py:214
  230.2 31.6 %collective-permute-start.19 = (bf16[1,48,4096]{2,1,0:T(8,128)(2,1)S(1)}, bf16[1,48,4096]{2,1,0:T(8,128)(2,1)S(1)}, u32[]{:S(2)}, u32[]{:S(2)}) collective-permute-start(bf16[1,48,4096]{2,1,0:T(8,128)(2,1)S(1)} %get-tuple-element.20), channel_id=1, source_target_pairs={{0,14},{2,8},{4,10},{6,12},{8,22},{10,16},{12,18},{14,20},{16,30},... | collective-permute-start | bytes 1179656 | tf_op jit(solution)/shard_map/ppermute | solution.py:214
  234.8 33.9 %collective-permute-start.18 = (bf16[1,48,4096]{2,1,0:T(8,128)(2,1)S(1)}, bf16[1,48,4096]{2,1,0:T(8,128)(2,1)S(1)}, u32[]{:S(2)}, u32[]{:S(2)}) collective-permute-start(bf16[1,48,4096]{2,1,0:T(8,128)(2,1)S(1)} %get-tuple-element.17), channel_id=1, source_target_pairs={{0,8},{2,10},{4,12},{6,14},{8,16},{10,18},{12,20},{14,22},{16,24},... | collective-permute-start | bytes 1179656 | tf_op jit(solution)/shard_map/ppermute | solution.py:214

commit v10 on v9

--- a/solution.py
+++ b/solution.py
@@ -136,20 +136,6 @@
     slot_index = (distance * per_context + expert_ids % per_context) * capacity + position
     slot_ids = jnp.arange(slots, dtype=jnp.int32)
     slot_match = (slot_ids[:, None] == slot_index[None, :]).astype(jnp.bfloat16)
-    hits = slot_ids[:, None] == slot_index[None, :]
-    slot_weights = jnp.sum(jnp.where(hits, route_weight[0, 0, :, 0], 0.0), axis=1)
-    told = jnp.concatenate([slot_weights, slot_index.astype(jnp.float32)])
-    told = lax.all_gather(told, ("pipe", "ctx"))
-    pipes, my_pipe = lax.axis_size("pipe"), lax.axis_index("pipe")
-    width = per_context * capacity
-    arrived_weights = [
-        lax.dynamic_slice(told, (my_pipe * contexts + (me - k) % contexts, k * width), (1, width))
-        for k in range(contexts)
-    ]
-    next_slots = lax.dynamic_slice(
-        told, ((my_pipe - 1) % pipes * contexts + me, slots), (1, token_rows)
-    )[0].astype(jnp.int32)
-
     halves, first = mixed_halves(
         queries[0, 0], rotated_keys_values[0, 0], residual[0, 0], out_weight[0]
     )
@@ -158,13 +144,16 @@
         mixed_rows = jnp.where(first == 0, mixed_rows, jnp.concatenate(halves[::-1], axis=1))
 
     gain, inverse_gain = norm_gain[0], 1.0 / norm_gain[0]
-    beside = next_slots[0].astype(jnp.float32) + sum(w[0, 0] for w in arrived_weights)
-    scaled = (mixed_rows * (gain + beside * 0.0)).astype(jnp.bfloat16)
+    weights = route_weight[0, 0]
+    coarse = lax.reduce_precision(weights, exponent_bits=8, mantissa_bits=7)
+    beside = jnp.pad(jnp.concatenate([coarse, weights - coarse], axis=1), ((0, 0), (0, 126)))
+    scaled = jnp.concatenate([mixed_rows * gain, beside], axis=1).astype(jnp.bfloat16)
     packed = jnp.dot(slot_match, scaled, preferred_element_type=jnp.float32).astype(jnp.bfloat16)
-    packed = packed.reshape(contexts, per_context, capacity, model_width)
-    arrived = jnp.stack(
-        [packed[0]] + [shift(packed[k], "ctx", k) for k in range(1, contexts)], axis=0
-    )
+    packed = packed.reshape(contexts, per_context, capacity, model_width + 128)
+    blocks = [packed[0]] + [shift(packed[k], "ctx", k) for k in range(1, contexts)]
+    arrived = jnp.stack([block[..., :model_width] for block in blocks], axis=0)
+    weights = jnp.stack([block[..., model_width:] for block in blocks], axis=0)
+    weights = weights[..., 0:1].astype(jnp.float32) + weights[..., 1:2].astype(jnp.float32)
     arrived = lax.optimization_barrier(arrived)
 
     def wanted_by(blocks, exp):
@@ -175,7 +164,7 @@
     hidden_width = down_weight.shape[2]
 
     def expert_part(rows):
-        rows = rows.reshape(-1, model_width)
+        rows = lax.optimization_barrier(rows.reshape(-1, model_width))
         unscaled = rows.astype(jnp.float32) * inverse_gain
         mean_square = jnp.mean(unscaled * unscaled, axis=-1, keepdims=True)
         gate_up = jnp.dot(rows, in_weight[0, 0], preferred_element_type=jnp.float32)
@@ -200,7 +189,6 @@
         else:
             place = (my_exp + k) % exps // group_size
             sums = [s + jnp.where(place == i, back, 0.0) for i, s in enumerate(sums)]
-    weights = jnp.stack(arrived_weights, axis=0).reshape(contexts, per_context, capacity, 1)
     finished = arrived.astype(jnp.float32) * inverse_gain + weights * jnp.stack(sums, axis=1)
     finished = finished.astype(jnp.bfloat16)
 
@@ -213,10 +201,11 @@
         ]
         return lax.ppermute(rows, ("pipe", "ctx"), pairs)
 
-    returned = jnp.concatenate(
-        [to_next_owner(finished[k], k).reshape(-1, model_width) for k in range(contexts)], axis=0
-    )
+    returned = [to_next_owner(finished[k], k).reshape(-1, model_width) for k in range(contexts)]
+    next_slots = slot_index.astype(jnp.float32) + returned[0][0, 0].astype(jnp.float32) * 0.0
+    next_slots = shift(next_slots[None, :], "pipe", 1)[0].astype(jnp.int32)
     next_match = (slot_ids[None, :] == next_slots[:, None]).astype(jnp.bfloat16)
+    returned = jnp.concatenate(returned, axis=0)
     layer = jnp.dot(next_match, returned, preferred_element_type=jnp.float32)
     return layer.astype(jnp.bfloat16).reshape(1, 1, token_rows, model_width)
 

time: 271 us -> 230 us (0.85)
  blocking collectives: 76.5 us -> 0 us
  starting transfers between devices: 26.3 us -> 61 us
  waiting for transfers between devices: 97.2 us -> 113 us
  matrix products: 58.1 us -> 45.8 us
    unnamed x1 -> x0, blocking collectives: 76.5 us -> none
    ppermute x18 -> x19, starting transfers between devices: 18.7 us -> 55.5 us  [shift(): lax.ppermute(value, axis, [(i, (i + by) % devices) for i in range(devices)])]
    ppermute x18 -> x19, waiting for transfers between devices: 66.9 us -> 80.9 us  [shift(): lax.ppermute(value, axis, [(i, (i + by) % devices) for i in range(devices)])]
    dot_general x2, matrix products: 12 us -> 5.25 us  [expert_part(): gate_up = jnp.dot(rows, in_weight[0, 0], preferred_element_type=jnp.float32)]
    dot_general x2, matrix products: 9.57 us -> 2.89 us  [expert_part(): jnp.dot(hidden, down_weight[0, 0], preferred_element_type=jnp.float32)]
  transfers between devices with their start and end apart: 22 -> 23, of which waited for: 10 -> 10; matrix products, arithmetic and copies ran while one was open for 19% -> 20% of each run, Pallas kernels for 0% -> 0%
where the time goes in v10:
time: 230 us
  waiting for transfers between devices  113 us (49%)
  starting transfers between devices  61 us (27%)
  matrix products  45.8 us (20%)
  local copies, waits for them, and re-layouts  4.62 us (2%)
  other arithmetic  3.91 us (2%)
    ppermute x19, waiting for transfers between devices, shift(): lax.ppermute(value, axis, [(i, (i + by) % devices) for i in range(devices)])  80.9 us
    ppermute x19, starting transfers between devices, shift(): lax.ppermute(value, axis, [(i, (i + by) % devices) for i in range(devices)])  55.5 us
    ppermute x4, waiting for transfers between devices, to_next_owner(): return lax.ppermute(rows, ('pipe', 'ctx'), pairs)  32.1 us
    dot_general x8, matrix products, mixed_halves(): term = jnp.dot(attended, weights[half], preferred_element_type=jnp.float32)  23.5 us
    dot_general x4, matrix products, attend_block(): jnp.einsum('hqk,kd->qhd', attention_weights, value_rows, preferred_elemen...  7.23 us
    ppermute x4, starting transfers between devices, to_next_owner(): return lax.ppermute(rows, ('pipe', 'ctx'), pairs)  5.55 us
    dot_general x2, matrix products, expert_part(): gate_up = jnp.dot(rows, in_weight[0, 0], preferred_element_type=jnp.float32)  5.25 us
    sub x4, matrix products, attend_block(): attention_weights = jax.nn.softmax(scores, axis=-1).astype(jnp.bfloat16)  4.97 us
  transfers between devices with their start and end apart: 23, of which 10 were waited for; matrix products, arithmetic and copies ran while one was open for 20% of the time, Pallas kernels for 0%

profile of v10, /device:TPU:0, one launch (start us, length us, event | category | flops | bytes accessed | tf_op | source)
XLA Modules:
  0.0 229.7 jit_solution(15906515390253031553)
XLA Ops:
  0.0 0.5 collective-permute-start.6
  0.5 1.0 dynamic-slice_bitcast_fusion.7
  1.4 2.7 %collective-permute-start = (bf16[128,256]{1,0:T(8,128)(2,1)S(1)}, bf16[128,256]{1,0:T(8,128)(2,1)S(1)}, u32[]{:S(2)}, u32[]{:S(2)}) collective-permute-start(bf16[128,256]{1,0:T(8,128)(2,1)S(1)} %pad_maximum_fusion.2), channel_id=1, source_target_pairs={{0,2},{2,4},{4,6},{6,0},{1,3},{3,5},{5,7},{7,1},{8,10},{10,12},{12... | collective-permute-start | bytes 196616 | tf_op jit(solution)/shard_map/ppermute | solution.py:15
  4.1 2.7 %collective-permute-start.1 = (bf16[128,256]{1,0:T(8,128)(2,1)S(1)}, bf16[128,256]{1,0:T(8,128)(2,1)S(1)}, u32[]{:S(2)}, u32[]{:S(2)}) collective-permute-start(bf16[128,256]{1,0:T(8,128)(2,1)S(1)} %pad_maximum_fusion.3), channel_id=1, source_target_pairs={{0,4},{2,6},{4,0},{6,2},{1,5},{3,7},{5,1},{7,3},{8,12},{10,14},{12... | collective-permute-start | bytes 196616 | tf_op jit(solution)/shard_map/ppermute | solution.py:15
  6.8 1.4 collective-permute-start.2
  8.2 1.3 constant_dynamic-slice_fusion
  9.6 0.7 collective-permute-start.3
  10.5 0.2 reduce_window_sum.11
  10.7 0.2 select_reduce_fusion
  10.9 0.2 broadcast_compare_fusion
  11.3 0.2 copy.39
  11.5 0.8 copy.38
  12.5 6.8 %collective-permute-done.3 = bf16[128,1024]{0,1:T(8,128)(2,1)S(1)} collective-permute-done((bf16[128,1024]{0,1:T(8,128)(2,1)S(1)}, bf16[128,1024]{0,1:T(8,128)(2,1)S(1)}, u32[]{:S(2)}, u32[]{:S(2)}) %collective-permute-start.3) | collective-permute-done | bytes 262176 | tf_op jit(solution)/shard_map/ppermute | solution.py:15
  19.3 0.8 fusion.116
  20.1 1.0 convolution_convert_fusion.5
  21.1 2.9 %fusion.99 = bf16[128,2048]{1,0:T(8,128)(2,1)S(1)} fusion(bf16[128,1024]{0,1:T(8,128)(2,1)S(1)} %bitcast.248, bf16[1,1024,2048]{2,1,0:T(8,128)(2,1)} %param.12), kind=kOutput, calls=%fused_computation.180 | convolution fusion | flops 536870912 | bytes 4980736 | tf_op jit(solution)/shard_map/dot_general | solution.py:89
  24.1 0.2 collective-permute-start.5
  24.3 0.9 collective-permute-start.7
  25.2 2.9 %collective-permute-start.4 = (bf16[128,1024]{0,1:T(8,128)(2,1)S(1)}, bf16[128,1024]{0,1:T(8,128)(2,1)}, u32[]{:S(2)}, u32[]{:S(2)}) collective-permute-start(bf16[128,1024]{0,1:T(8,128)(2,1)S(1)} %bitcast.259), channel_id=1, source_target_pairs={{0,6},{2,0},{4,2},{6,4},{1,7},{3,1},{5,3},{7,5},{8,14},{10,8},{12,... | collective-permute-start | bytes 786440 | tf_op jit(solution)/shard_map/ppermute | solution.py:15
  28.1 2.9 %fusion.120 = bf16[128,2048]{1,0:T(8,128)(2,1)S(1)} fusion(bf16[128,1024]{0,1:T(8,128)(2,1)S(1)} %bitcast.249, bf16[1024,2048]{1,0:T(8,128)(2,1)} %collective-permute-done.6), kind=kOutput, calls=%fused_computation.197 | convolution fusion | flops 536870912 | bytes 4980736 | tf_op jit(solution)/shard_map/dot_general | solution.py:89
  31.1 18.6 %collective-permute-done.5 = bf16[128,1024]{0,1:T(8,128)(2,1)} collective-permute-done((bf16[128,1024]{0,1:T(8,128)(2,1)S(1)}, bf16[128,1024]{0,1:T(8,128)(2,1)}, u32[]{:S(2)}, u32[]{:S(2)}) %collective-permute-start.5) | collective-permute-done | bytes 262176 | tf_op jit(solution)/shard_map/ppermute | solution.py:15
  49.7 1.7 fusion.117
  51.4 2.0 convolution_convert_fusion.4
  53.4 2.9 %fusion.97 = f32[128,2048]{1,0:T(8,128)S(1)} fusion(bf16[128,1024]{0,1:T(8,128)(2,1)S(1)} %bitcast.252, bf16[1,1024,2048]{2,1,0:T(8,128)(2,1)} %param.12), kind=kOutput, calls=%fused_computation.178 | convolution fusion | flops 536870912 | bytes 5505024 | tf_op jit(solution)/shard_map/dot_general | solution.py:89
  56.4 2.9 %fusion.121 = f32[128,2048]{1,0:T(8,128)S(1)} fusion(bf16[128,1024]{0,1:T(8,128)(2,1)S(1)} %bitcast.253, bf16[1024,2048]{1,0:T(8,128)(2,1)} %collective-permute-done.6), kind=kOutput, calls=%fused_computation.198 | convolution fusion | flops 536870912 | bytes 5505024 | tf_op jit(solution)/shard_map/dot_general | solution.py:89
  59.7 5.7 %collective-permute-start.10 = (bf16[128,2048]{1,0:T(8,128)(2,1)S(1)}, bf16[128,2048]{1,0:T(8,128)(2,1)S(1)}, u32[]{:S(2)}, u32[]{:S(2)}) collective-permute-start(bf16[128,2048]{1,0:T(8,128)(2,1)S(1)} %add_convert_fusion.2), channel_id=1, source_target_pairs={{0,2},{2,4},{4,6},{6,0},{1,3},{3,5},{5,7},{7,1},{8,10},{10,12},{12... | collective-permute-start | bytes 1572872 | tf_op jit(solution)/shard_map/ppermute | solution.py:15
  65.3 1.7 fusion.118
  67.1 2.0 convolution_convert_fusion.3
  69.1 2.9 %fusion.95 = f32[128,2048]{1,0:T(8,128)S(1)} fusion(bf16[128,1024]{0,1:T(8,128)(2,1)S(1)} %bitcast.254, bf16[1,1024,2048]{2,1,0:T(8,128)(2,1)} %param.12), kind=kOutput, calls=%fused_computation.176 | convolution fusion | flops 536870912 | bytes 5505024 | tf_op jit(solution)/shard_map/dot_general | solution.py:89
  72.0 2.9 %fusion.122 = f32[128,2048]{1,0:T(8,128)S(1)} fusion(bf16[128,1024]{0,1:T(8,128)(2,1)S(1)} %bitcast.255, bf16[1024,2048]{1,0:T(8,128)(2,1)} %collective-permute-done.6), kind=kOutput, calls=%fused_computation.199 | convolution fusion | flops 536870912 | bytes 5505024 | tf_op jit(solution)/shard_map/dot_general | solution.py:89
  74.9 1.2 collective-permute-done.9
  76.3 32.3 %collective-permute-start.11 = (bf16[128,2048]{1,0:T(8,128)(2,1)S(1)}, bf16[128,2048]{1,0:T(8,128)(2,1)S(1)}, u32[]{:S(2)}, u32[]{:S(2)}) collective-permute-start(bf16[128,2048]{1,0:T(8,128)(2,1)S(1)} %add_convert_fusion.1), channel_id=1, source_target_pairs={{0,2},{2,4},{4,6},{6,0},{1,3},{3,5},{5,7},{7,1},{8,10},{10,12},{12... | collective-permute-start | bytes 1572872 | tf_op jit(solution)/shard_map/ppermute | solution.py:15
  108.7 0.3 collective-permute-start.12
  109.0 0.8 fusion.119
  109.8 2.2 convolution_convert_fusion.2
  112.0 2.9 %convolution_add_fusion.1 = f32[128,2048]{1,0:T(8,128)S(1)} fusion(bf16[128,1024]{0,1:T(8,128)(2,1)S(1)} %bitcast.250, bf16[1,1,128,4096]{3,2,1,0:T(8,128)(2,1)S(1)} %copy-done, s32[]{:T(128)S(6)} %select_n.179, bf16[1,1024,2048]{2,1,0:T(8,128)(2,1)} %param.12), kind=kOutput, calls=%fused_computation.23 | convolution fusion | flops 537395200 | bytes 6029316 | tf_op jit(solution)/shard_map/dot_general | solution.py:89
  114.9 2.9 %convolution_add_fusion = f32[128,2048]{1,0:T(8,128)S(1)} fusion(bf16[128,1024]{0,1:T(8,128)(2,1)S(1)} %bitcast.251, bf16[1024,2048]{1,0:T(8,128)(2,1)} %collective-permute-done.6, bf16[1,1,128,4096]{3,2,1,0:T(8,128)(2,1)S(1)} %copy-done, s32[]{:T(128)S(6)} %select_n.180), kind=kOutput, calls=%fused_computation.22 | convolution fusion | flops 537395200 | bytes 6029316 | tf_op jit(solution)/shard_map/dot_general | solution.py:89
  117.9 3.0 %collective-permute-done.11 = bf16[128,2048]{1,0:T(8,128)(2,1)S(1)} collective-permute-done((bf16[128,2048]{1,0:T(8,128)(2,1)S(1)}, bf16[128,2048]{1,0:T(8,128)(2,1)S(1)}, u32[]{:S(2)}, u32[]{:S(2)}) %collective-permute-start.11) | collective-permute-done | bytes 524320 | tf_op jit(solution)/shard_map/ppermute | solution.py:15
  121.0 10.2 %collective-permute-done.12 = bf16[128,2048]{1,0:T(8,128)(2,1)S(1)} collective-permute-done((bf16[128,2048]{1,0:T(8,128)(2,1)S(1)}, bf16[128,2048]{1,0:T(8,128)(2,1)S(1)}, u32[]{:S(2)}, u32[]{:S(2)}) %collective-permute-start.12) | collective-permute-done | bytes 524320 | tf_op jit(solution)/shard_map/ppermute | solution.py:15
  131.4 0.2 fusion.25
  131.6 0.6 convolution_convert_fusion
  132.3 1.0 collective-permute-start.15
  133.3 3.0 %collective-permute-start.14 = (bf16[1,48,4224]{2,1,0:T(8,128)(2,1)S(1)}, bf16[1,48,4224]{2,1,0:T(8,128)(2,1)S(1)}, u32[]{:S(2)}, u32[]{:S(2)}) collective-permute-start(bf16[1,48,4224]{2,1,0:T(8,128)(2,1)S(1)} %get-tuple-element.19), channel_id=1, source_target_pairs={{0,4},{2,6},{4,0},{6,2},{1,5},{3,7},{5,1},{7,3},{8,12},{10,14},{12... | collective-permute-start | bytes 1216520 | tf_op jit(solution)/shard_map/ppermute | solution.py:15
  136.3 0.3 collective-permute-start.13
  136.7 25.6 %collective-permute-done.13 = bf16[1,48,4224]{2,1,0:T(8,128)(2,1)S(1)} collective-permute-done((bf16[1,48,4224]{2,1,0:T(8,128)(2,1)S(1)}, bf16[1,48,4224]{2,1,0:T(8,128)(2,1)S(1)}, u32[]{:S(2)}, u32[]{:S(2)}) %collective-permute-start.13) | collective-permute-done | bytes 405536 | tf_op jit(solution)/shard_map/ppermute | solution.py:15
  162.3 8.5 %collective-permute-done.14 = bf16[1,48,4224]{2,1,0:T(8,128)(2,1)S(1)} collective-permute-done((bf16[1,48,4224]{2,1,0:T(8,128)(2,1)S(1)}, bf16[1,48,4224]{2,1,0:T(8,128)(2,1)S(1)}, u32[]{:S(2)}, u32[]{:S(2)}) %collective-permute-start.14) | collective-permute-done | bytes 405536 | tf_op jit(solution)/shard_map/ppermute | solution.py:15
  170.9 0.2 pad_maximum_fusion
  171.2 0.2 add_reduce_fusion
  171.4 3.1 %collective-permute-done.16 = bf16[4,48,4096]{2,1,0:T(8,128)(2,1)S(1)} collective-permute-done((bf16[4,48,4096]{2,1,0:T(8,128)(2,1)S(1)}, bf16[4,48,4096]{2,1,0:T(8,128)(2,1)S(1)}, u32[]{:S(2)}, u32[]{:S(2)}) %collective-permute-start.16) | collective-permute-done | bytes 1572896 | tf_op jit(solution)/shard_map/ppermute | solution.py:15
  174.5 0.9 multiply_reduce_fusion
  175.5 2.6 %fusion.20 = f32[192,1536]{1,0:T(8,128)S(1)} fusion(bf16[192,4096]{1,0:T(8,128)(2,1)S(1)} %bitcast.247, bf16[1,1,4096,1536]{3,2,1,0:T(8,128)(2,1)S(1)} %bitcast.267, f32[192]{0:T(256)S(1)} %add_rsqrt_fusion), kind=kOutput, calls=%fused_computation.21 | convolution fusion | flops 2416214016 | bytes 15336192 | tf_op jit(solution)/shard_map/dot_general | solution.py:170
  178.1 1.4 fusion.12
  179.6 0.2 collective-permute-start.17
  179.8 2.6 %fusion.17 = f32[192,1536]{1,0:T(8,128)S(1)} fusion(bf16[192,4096]{1,0:T(8,128)(2,1)S(1)} %bitcast.244, bf16[1,1,4096,1536]{3,2,1,0:T(8,128)(2,1)S(1)} %bitcast.267, f32[192]{0:T(256)S(1)} %add_rsqrt_fusion.1), kind=kOutput, calls=%fused_computation.20 | convolution fusion | flops 2416214016 | bytes 15336192 | tf_op jit(solution)/shard_map/dot_general | solution.py:170
  182.5 1.4 fusion.10
  183.9 0.8 fusion.16
  184.8 1.5 collective-permute-start.18
  186.4 1.6 collective-permute-start.21
  188.0 2.4 %collective-permute-start.22 = (bf16[1,48,4096]{2,1,0:T(8,128)(2,1)S(1)}, bf16[1,48,4096]{2,1,0:T(8,128)(2,1)S(1)}, u32[]{:S(2)}, u32[]{:S(2)}) collective-permute-start(bf16[1,48,4096]{2,1,0:T(8,128)(2,1)S(1)} %get-tuple-element.22), channel_id=1, source_target_pairs={{0,10},{2,12},{4,14},{6,8},{8,18},{10,20},{12,22},{14,16},{16,26},... | collective-permute-start | bytes 1179656 | tf_op jit(solution)/shard_map/ppermute | solution.py:202
  190.4 32.1 %collective-permute-done.18 = bf16[1,48,4096]{2,1,0:T(8,128)(2,1)S(1)} collective-permute-done((bf16[1,48,4096]{2,1,0:T(8,128)(2,1)S(1)}, bf16[1,48,4096]{2,1,0:T(8,128)(2,1)S(1)}, u32[]{:S(2)}, u32[]{:S(2)}) %collective-permute-start.18) | collective-permute-done | bytes 393248 | tf_op jit(solution)/shard_map/ppermute | solution.py:202
  222.5 0.5 slice.125
  223.7 0.6 collective-permute-start.19
  224.3 3.9 %collective-permute-done.19 = f32[1,128]{1,0:T(1,128)S(1)} collective-permute-done((f32[1,128]{1,0:T(1,128)S(1)}, f32[1,128]{1,0:T(1,128)S(1)}, u32[]{:S(2)}, u32[]{:S(2)}) %collective-permute-start.19) | collective-permute-done | bytes 544 | tf_op jit(solution)/shard_map/ppermute | solution.py:15
  228.2 1.5 fusion.15
  (80 shorter events, 2.1 us)
Async XLA Ops:
  0.0 10.4 %copy-start.5 = (s32[1,1,128,1]{2,3,1,0:T(1,128)S(1)}, s32[1,1,128,1]{2,3,1,0:T(1,128)}, u32[]{:S(2)}) copy-start(s32[1,1,128,1]{2,3,1,0:T(1,128)} %param.16) | copy-start | bytes 1540
  0.0 28.1 %collective-permute-start.6 = (bf16[1024,2048]{1,0:T(8,128)(2,1)}, bf16[1024,2048]{1,0:T(8,128)(2,1)}, u32[]{:S(2)}, u32[]{:S(2)}) collective-permute-start(bf16[1024,2048]{1,0:T(8,128)(2,1)} %bitcast.241), channel_id=1, source_target_pairs={{0,1},{1,0},{2,3},{3,2},{4,5},{5,4},{6,7},{7,6},{8,9},{9,8},{10,11... | collective-permute-start | bytes 12582920 | tf_op jit(solution)/shard_map/ppermute | solution.py:15
  0.5 10.6 %copy-start.6 = (f32[1,1,128,1]{2,3,1,0:T(1,128)S(1)}, f32[1,1,128,1]{2,3,1,0:T(1,128)}, u32[]{:S(2)}) copy-start(f32[1,1,128,1]{2,3,1,0:T(1,128)} %param.17) | copy-start | bytes 1540
  1.4 11.0 %collective-permute-start = (bf16[128,256]{1,0:T(8,128)(2,1)S(1)}, bf16[128,256]{1,0:T(8,128)(2,1)S(1)}, u32[]{:S(2)}, u32[]{:S(2)}) collective-permute-start(bf16[128,256]{1,0:T(8,128)(2,1)S(1)} %pad_maximum_fusion.2), channel_id=1, source_target_pairs={{0,2},{2,4},{4,6},{6,0},{1,3},{3,5},{5,7},{7,1},{8,10},{10,12},{12... | collective-permute-start | bytes 196616 | tf_op jit(solution)/shard_map/ppermute | solution.py:15
  4.1 8.3 %collective-permute-start.1 = (bf16[128,256]{1,0:T(8,128)(2,1)S(1)}, bf16[128,256]{1,0:T(8,128)(2,1)S(1)}, u32[]{:S(2)}, u32[]{:S(2)}) collective-permute-start(bf16[128,256]{1,0:T(8,128)(2,1)S(1)} %pad_maximum_fusion.3), channel_id=1, source_target_pairs={{0,4},{2,6},{4,0},{6,2},{1,5},{3,7},{5,1},{7,3},{8,12},{10,14},{12... | collective-permute-start | bytes 196616 | tf_op jit(solution)/shard_map/ppermute | solution.py:15
  6.8 5.7 %collective-permute-start.2 = (bf16[128,256]{1,0:T(8,128)(2,1)S(1)}, bf16[128,256]{1,0:T(8,128)(2,1)S(1)}, u32[]{:S(2)}, u32[]{:S(2)}) collective-permute-start(bf16[128,256]{1,0:T(8,128)(2,1)S(1)} %pad_maximum_fusion.4), channel_id=1, source_target_pairs={{0,6},{2,0},{4,2},{6,4},{1,7},{3,1},{5,3},{7,5},{8,14},{10,8},{12,... | collective-permute-start | bytes 196616 | tf_op jit(solution)/shard_map/ppermute | solution.py:15
  9.6 9.7 %collective-permute-start.3 = (bf16[128,1024]{0,1:T(8,128)(2,1)S(1)}, bf16[128,1024]{0,1:T(8,128)(2,1)S(1)}, u32[]{:S(2)}, u32[]{:S(2)}) collective-permute-start(bf16[128,1024]{0,1:T(8,128)(2,1)S(1)} %bitcast.256), channel_id=1, source_target_pairs={{0,2},{2,4},{4,6},{6,0},{1,3},{3,5},{5,7},{7,1},{8,10},{10,12},{12... | collective-permute-start | bytes 786440 | tf_op jit(solution)/shard_map/ppermute | solution.py:15
  12.5 54.5 %copy-start.2 = (bf16[512,256]{1,0:T(8,128)(2,1)}, bf16[512,256]{1,0:T(8,128)(2,1)S(1)}, u32[]{:S(2)}) copy-start(bf16[512,256]{1,0:T(8,128)(2,1)S(1)} %pad_maximum_fusion.1) | copy-start | bytes 786436
  24.1 25.6 %collective-permute-start.5 = (bf16[128,1024]{0,1:T(8,128)(2,1)S(1)}, bf16[128,1024]{0,1:T(8,128)(2,1)}, u32[]{:S(2)}, u32[]{:S(2)}) collective-permute-start(bf16[128,1024]{0,1:T(8,128)(2,1)S(1)} %bitcast.260), channel_id=1, source_target_pairs={{0,4},{2,6},{4,0},{6,2},{1,5},{3,7},{5,1},{7,3},{8,12},{10,14},{12... | collective-permute-start | bytes 786440 | tf_op jit(solution)/shard_map/ppermute | solution.py:15
  24.3 35.0 %collective-permute-start.7 = (bf16[128,2048]{1,0:T(8,128)(2,1)S(1)}, bf16[128,2048]{1,0:T(8,128)(2,1)S(1)}, u32[]{:S(2)}, u32[]{:S(2)}) collective-permute-start(bf16[128,2048]{1,0:T(8,128)(2,1)S(1)} %fusion.99), channel_id=1, source_target_pairs={{0,2},{2,4},{4,6},{6,0},{1,3},{3,5},{5,7},{7,1},{8,10},{10,12},{12... | collective-permute-start | bytes 1572872 | tf_op jit(solution)/shard_map/ppermute | solution.py:15
  25.2 40.1 %collective-permute-start.4 = (bf16[128,1024]{0,1:T(8,128)(2,1)S(1)}, bf16[128,1024]{0,1:T(8,128)(2,1)}, u32[]{:S(2)}, u32[]{:S(2)}) collective-permute-start(bf16[128,1024]{0,1:T(8,128)(2,1)S(1)} %bitcast.259), channel_id=1, source_target_pairs={{0,6},{2,0},{4,2},{6,4},{1,7},{3,1},{5,3},{7,5},{8,14},{10,8},{12,... | collective-permute-start | bytes 786440 | tf_op jit(solution)/shard_map/ppermute | solution.py:15
  31.0 28.5 %collective-permute-start.8 = (bf16[128,2048]{1,0:T(8,128)(2,1)S(1)}, bf16[128,2048]{1,0:T(8,128)(2,1)S(1)}, u32[]{:S(2)}, u32[]{:S(2)}) collective-permute-start(bf16[128,2048]{1,0:T(8,128)(2,1)S(1)} %fusion.120), channel_id=1, source_target_pairs={{0,2},{2,4},{4,6},{6,0},{1,3},{3,5},{5,7},{7,1},{8,10},{10,12},{12... | collective-permute-start | bytes 1572872 | tf_op jit(solution)/shard_map/ppermute | solution.py:15
  59.4 16.7 %collective-permute-start.9 = (bf16[128,2048]{1,0:T(8,128)(2,1)S(1)}, bf16[128,2048]{1,0:T(8,128)(2,1)S(1)}, u32[]{:S(2)}, u32[]{:S(2)}) collective-permute-start(bf16[128,2048]{1,0:T(8,128)(2,1)S(1)} %add_convert_fusion.3), channel_id=1, source_target_pairs={{0,2},{2,4},{4,6},{6,0},{1,3},{3,5},{5,7},{7,1},{8,10},{10,12},{12... | collective-permute-start | bytes 1572872 | tf_op jit(solution)/shard_map/ppermute | solution.py:15
  59.7 49.0 %collective-permute-start.10 = (bf16[128,2048]{1,0:T(8,128)(2,1)S(1)}, bf16[128,2048]{1,0:T(8,128)(2,1)S(1)}, u32[]{:S(2)}, u32[]{:S(2)}) collective-permute-start(bf16[128,2048]{1,0:T(8,128)(2,1)S(1)} %add_convert_fusion.2), channel_id=1, source_target_pairs={{0,2},{2,4},{4,6},{6,0},{1,3},{3,5},{5,7},{7,1},{8,10},{10,12},{12... | collective-permute-start | bytes 1572872 | tf_op jit(solution)/shard_map/ppermute | solution.py:15
  74.9 34.1 %copy-start.1 = (bf16[1,1,128,1024]{2,3,1,0:T(8,128)(2,1)S(1)}, bf16[1,1,128,1024]{2,3,1,0:T(8,128)(2,1)}, u32[]{:S(2)}) copy-start(bf16[1,1,128,1024]{2,3,1,0:T(8,128)(2,1)} %copy.38) | copy-start | bytes 786436
  76.2 32.8 %copy-start.3 = (bf16[512,256]{1,0:T(8,128)(2,1)S(1)}, bf16[512,256]{1,0:T(8,128)(2,1)}, u32[]{:S(2)}) copy-start(bf16[512,256]{1,0:T(8,128)(2,1)} %copy-done.2) | copy-start | bytes 786436
  76.3 44.6 %collective-permute-start.11 = (bf16[128,2048]{1,0:T(8,128)(2,1)S(1)}, bf16[128,2048]{1,0:T(8,128)(2,1)S(1)}, u32[]{:S(2)}, u32[]{:S(2)}) collective-permute-start(bf16[128,2048]{1,0:T(8,128)(2,1)S(1)} %add_convert_fusion.1), channel_id=1, source_target_pairs={{0,2},{2,4},{4,6},{6,0},{1,3},{3,5},{5,7},{7,1},{8,10},{10,12},{12... | collective-permute-start | bytes 1572872 | tf_op jit(solution)/shard_map/ppermute | solution.py:15
  108.7 22.5 %collective-permute-start.12 = (bf16[128,2048]{1,0:T(8,128)(2,1)S(1)}, bf16[128,2048]{1,0:T(8,128)(2,1)S(1)}, u32[]{:S(2)}, u32[]{:S(2)}) collective-permute-start(bf16[128,2048]{1,0:T(8,128)(2,1)S(1)} %add_convert_fusion), channel_id=1, source_target_pairs={{0,2},{2,4},{4,6},{6,0},{1,3},{3,5},{5,7},{7,1},{8,10},{10,12},{12... | collective-permute-start | bytes 1572872 | tf_op jit(solution)/shard_map/ppermute | solution.py:15
  109.8 2.2 copy-start
  117.9 13.5 %copy-start.4 = (f32[1,4096]{1,0:T(1,128)S(1)}, f32[1,4096]{1,0:T(1,128)}, u32[]{:S(2)}) copy-start(f32[1,4096]{1,0:T(1,128)} %param.13) | copy-start | bytes 49156
  120.9 54.5 %slice-start = ((s8[12582912]{0:T(1024)(128)(4,1)}), s8[4194304]{0:T(1024)(128)(4,1)S(1)}, s32[]{:S(2)}) async-start(s8[12582912]{0:T(1024)(128)(4,1)} %bitcast.266), calls=%async_computation | async-start | bytes 8388608
  131.4 44.1 %slice-start.1 = ((s8[12582912]{0:T(1024)(128)(4,1)}), s8[4194304]{0:T(1024)(128)(4,1)S(1)}, s32[]{:S(2)}) async-start(s8[12582912]{0:T(1024)(128)(4,1)} %bitcast.266), calls=%async_computation.1 | async-start | bytes 8388608
  132.3 30.0 %collective-permute-start.15 = (bf16[1,48,4224]{2,1,0:T(8,128)(2,1)S(1)}, bf16[1,48,4224]{2,1,0:T(8,128)(2,1)S(1)}, u32[]{:S(2)}, u32[]{:S(2)}) collective-permute-start(bf16[1,48,4224]{2,1,0:T(8,128)(2,1)S(1)} %get-tuple-element.18), channel_id=1, source_target_pairs={{0,6},{2,0},{4,2},{6,4},{1,7},{3,1},{5,3},{7,5},{8,14},{10,8},{12,... | collective-permute-start | bytes 1216520 | tf_op jit(solution)/shard_map/ppermute | solution.py:15
  133.3 37.5 %collective-permute-start.14 = (bf16[1,48,4224]{2,1,0:T(8,128)(2,1)S(1)}, bf16[1,48,4224]{2,1,0:T(8,128)(2,1)S(1)}, u32[]{:S(2)}, u32[]{:S(2)}) collective-permute-start(bf16[1,48,4224]{2,1,0:T(8,128)(2,1)S(1)} %get-tuple-element.19), channel_id=1, source_target_pairs={{0,4},{2,6},{4,0},{6,2},{1,5},{3,7},{5,1},{7,3},{8,12},{10,14},{12... | collective-permute-start | bytes 1216520 | tf_op jit(solution)/shard_map/ppermute | solution.py:15
  136.3 26.0 %collective-permute-start.13 = (bf16[1,48,4224]{2,1,0:T(8,128)(2,1)S(1)}, bf16[1,48,4224]{2,1,0:T(8,128)(2,1)S(1)}, u32[]{:S(2)}, u32[]{:S(2)}) collective-permute-start(bf16[1,48,4224]{2,1,0:T(8,128)(2,1)S(1)} %get-tuple-element.20), channel_id=1, source_target_pairs={{0,2},{2,4},{4,6},{6,0},{1,3},{3,5},{5,7},{7,1},{8,10},{10,12},{12... | collective-permute-start | bytes 1216520 | tf_op jit(solution)/shard_map/ppermute | solution.py:15
  136.6 38.8 %slice-start.2 = ((s8[12582912]{0:T(1024)(128)(4,1)}), s8[4194304]{0:T(1024)(128)(4,1)S(1)}, s32[]{:S(2)}) async-start(s8[12582912]{0:T(1024)(128)(4,1)} %bitcast.266), calls=%async_computation.2 | async-start | bytes 8388608
  171.1 3.5 %collective-permute-start.16 = (bf16[4,48,4096]{2,1,0:T(8,128)(2,1)S(1)}, bf16[4,48,4096]{2,1,0:T(8,128)(2,1)S(1)}, u32[]{:S(2)}, u32[]{:S(2)}) collective-permute-start(bf16[4,48,4096]{2,1,0:T(8,128)(2,1)S(1)} %bitcast.242), channel_id=1, source_target_pairs={{0,1},{1,0},{2,3},{3,2},{4,5},{5,4},{6,7},{7,6},{8,9},{9,8},{10,11... | collective-permute-start | bytes 4718600 | tf_op jit(solution)/shard_map/ppermute | solution.py:15
  174.5 3.6 %slice-start.3 = ((s8[6291456]{0:T(1024)(128)(4,1)}), s8[4194304]{0:T(1024)(128)(4,1)S(1)}, s32[]{:S(2)}) async-start(s8[6291456]{0:T(1024)(128)(4,1)} %bitcast.268), calls=%async_computation.3 | async-start | bytes 8388608
  175.5 2.6 %slice-start.4 = ((s8[6291456]{0:T(1024)(128)(4,1)}), s8[2097152]{0:T(1024)(128)(4,1)S(1)}, s32[]{:S(2)}) async-start(s8[6291456]{0:T(1024)(128)(4,1)} %bitcast.268), calls=%async_computation.4 | async-start | bytes 4194304
  179.6 4.3 %collective-permute-start.17 = (bf16[4,48,4096]{2,1,0:T(8,128)(2,1)S(1)}, bf16[4,48,4096]{2,1,0:T(8,128)(2,1)S(1)}, u32[]{:S(2)}, u32[]{:S(2)}) collective-permute-start(bf16[4,48,4096]{2,1,0:T(8,128)(2,1)S(1)} %bitcast.270), channel_id=1, source_target_pairs={{0,1},{1,0},{2,3},{3,2},{4,5},{5,4},{6,7},{7,6},{8,9},{9,8},{10,11... | collective-permute-start | bytes 4718600 | tf_op jit(solution)/shard_map/ppermute | solution.py:15
  184.8 37.6 %collective-permute-start.18 = (bf16[1,48,4096]{2,1,0:T(8,128)(2,1)S(1)}, bf16[1,48,4096]{2,1,0:T(8,128)(2,1)S(1)}, u32[]{:S(2)}, u32[]{:S(2)}) collective-permute-start(bf16[1,48,4096]{2,1,0:T(8,128)(2,1)S(1)} %get-tuple-element.21), channel_id=1, source_target_pairs={{0,8},{2,10},{4,12},{6,14},{8,16},{10,18},{12,20},{14,22},{16,24},... | collective-permute-start | bytes 1179656 | tf_op jit(solution)/shard_map/ppermute | solution.py:202
  186.4 41.8 %collective-permute-start.20 = (bf16[1,48,4096]{2,1,0:T(8,128)(2,1)S(1)}, bf16[1,48,4096]{2,1,0:T(8,128)(2,1)S(1)}, u32[]{:S(2)}, u32[]{:S(2)}) collective-permute-start(bf16[1,48,4096]{2,1,0:T(8,128)(2,1)S(1)} %get-tuple-element.24), channel_id=1, source_target_pairs={{0,14},{2,8},{4,10},{6,12},{8,22},{10,16},{12,18},{14,20},{16,30},... | collective-permute-start | bytes 1179656 | tf_op jit(solution)/shard_map/ppermute | solution.py:202
  186.4 41.8 %collective-permute-start.21 = (bf16[1,48,4096]{2,1,0:T(8,128)(2,1)S(1)}, bf16[1,48,4096]{2,1,0:T(8,128)(2,1)S(1)}, u32[]{:S(2)}, u32[]{:S(2)}) collective-permute-start(bf16[1,48,4096]{2,1,0:T(8,128)(2,1)S(1)} %get-tuple-element.23), channel_id=1, source_target_pairs={{0,12},{2,14},{4,8},{6,10},{8,20},{10,22},{12,16},{14,18},{16,28},... | collective-permute-start | bytes 1179656 | tf_op jit(solution)/shard_map/ppermute | solution.py:202
  188.0 40.2 %collective-permute-start.22 = (bf16[1,48,4096]{2,1,0:T(8,128)(2,1)S(1)}, bf16[1,48,4096]{2,1,0:T(8,128)(2,1)S(1)}, u32[]{:S(2)}, u32[]{:S(2)}) collective-permute-start(bf16[1,48,4096]{2,1,0:T(8,128)(2,1)S(1)} %get-tuple-element.22), channel_id=1, source_target_pairs={{0,10},{2,12},{4,14},{6,8},{8,18},{10,20},{12,22},{14,16},{16,26},... | collective-permute-start | bytes 1179656 | tf_op jit(solution)/shard_map/ppermute | solution.py:202
  223.7 4.5 %collective-permute-start.19 = (f32[1,128]{1,0:T(1,128)S(1)}, f32[1,128]{1,0:T(1,128)S(1)}, u32[]{:S(2)}, u32[]{:S(2)}) collective-permute-start(f32[1,128]{1,0:T(1,128)S(1)} %convert_add_fusion.2), channel_id=1, source_target_pairs={{0,8},{8,16},{16,24},{24,0},{1,9},{9,17},{17,25},{25,1},{2,10},{10... | collective-permute-start | bytes 1544 | tf_op jit(solution)/shard_map/ppermute | solution.py:15

commit v11 on v10

--- a/solution.py
+++ b/solution.py
@@ -31,7 +31,7 @@
     return attended.astype(jnp.bfloat16)
 
 
-def mixed_halves(queries, keys_values, residual, out_weight):
+def mixed_halves(queries, keys_values, residual, out_weight, slots_here):
     contexts, exps = lax.axis_size("ctx"), lax.axis_size("exp")
     me, my_exp = lax.axis_index("ctx"), lax.axis_index("exp")
     rows = queries.shape[0]
@@ -74,33 +74,36 @@
     origins = [(me - k) % contexts * rows for k in range(contexts)]
     col_ids = jnp.concatenate([origin + within for origin in origins])
 
-    held, sent = [None, None], []
+    held, sent, next_slots = [None, None], [], shift(slots_here, "pipe", 1)
     for k in [*range(1, contexts), 0]:
-        block = blocks[k] if k == 1 else after(blocks[k], *sent)
+        behind = sum(block[0, 0] * 0.0 for block in sent)
         attended = attend_block(
-            block.reshape(rows, local_heads, HEAD_SIZE),
+            (blocks[k] + behind).reshape(rows, local_heads, HEAD_SIZE),
             key_rows,
             value_rows,
             origins[k] + within,
             col_ids,
         ).reshape(rows, group_width)
-        terms, sent = [], []
+        sent = []
+        terms = []
         for half in range(2):
             term = jnp.dot(attended, weights[half], preferred_element_type=jnp.float32)
             if k == 0:
                 own = lax.dynamic_slice_in_dim(residual, offsets[half], width // 2, 1)
                 term = term + own.astype(jnp.float32)
+            if k == 1 and half == 0:
+                term = term + weights[1][0, 0].astype(jnp.float32) * 0.0
             terms.append(lax.optimization_barrier(term))
         for half in range(2):
             term = terms[half]
             if held[half] is not None:
                 term = term + held[half].astype(jnp.float32)
             if k == 0:
-                held[half] = term
+                held[half] = term + next_slots[0, 0] * 0.0
             else:
                 sent.append(term.astype(jnp.bfloat16))
                 held[half] = shift(sent[half], "ctx", 1)
-    return held, first
+    return held, first, next_slots[0].astype(jnp.int32)
 
 
 def on_device(
@@ -136,8 +139,12 @@
     slot_index = (distance * per_context + expert_ids % per_context) * capacity + position
     slot_ids = jnp.arange(slots, dtype=jnp.int32)
     slot_match = (slot_ids[:, None] == slot_index[None, :]).astype(jnp.bfloat16)
-    halves, first = mixed_halves(
-        queries[0, 0], rotated_keys_values[0, 0], residual[0, 0], out_weight[0]
+    halves, first, next_slots = mixed_halves(
+        queries[0, 0],
+        rotated_keys_values[0, 0],
+        residual[0, 0],
+        out_weight[0],
+        slot_index.astype(jnp.float32)[None, :],
     )
     mixed_rows = jnp.concatenate(halves, axis=1)
     if exps == 2:
@@ -163,12 +170,14 @@
 
     hidden_width = down_weight.shape[2]
 
-    def expert_part(rows):
+    def gate_and_up(rows, behind):
         rows = lax.optimization_barrier(rows.reshape(-1, model_width))
-        unscaled = rows.astype(jnp.float32) * inverse_gain
+        unscaled = rows.astype(jnp.float32) * inverse_gain + behind
         mean_square = jnp.mean(unscaled * unscaled, axis=-1, keepdims=True)
         gate_up = jnp.dot(rows, in_weight[0, 0], preferred_element_type=jnp.float32)
-        gate_up = gate_up * lax.rsqrt(mean_square + 1e-06)
+        return gate_up * lax.rsqrt(mean_square + 1e-06)
+
+    def down_part(gate_up):
         hidden = (jax.nn.silu(gate_up[:, :hidden_width]) * gate_up[:, hidden_width:]).astype(
             jnp.bfloat16
         )
@@ -177,9 +186,11 @@
     others = [
         shift(wanted_by(arrived, (my_exp + k) % exps), "exp", k) for k in range(1, exps)
     ]
-    own_part = lax.optimization_barrier(expert_part(wanted_by(arrived, my_exp)))
+    own_gate_up = lax.optimization_barrier(gate_and_up(wanted_by(arrived, my_exp), 0.0))
+    other_gate_up = gate_and_up(jnp.concatenate(others, axis=0), own_gate_up[0, 0] * 0.0)
+    other_parts = down_part(other_gate_up).astype(jnp.bfloat16)
+    own_part = lax.optimization_barrier(down_part(own_gate_up))
     own_part = own_part.reshape(contexts, capacity, model_width)
-    other_parts = expert_part(jnp.concatenate(others, axis=0)).astype(jnp.bfloat16)
     other_parts = other_parts.reshape(exps - 1, contexts, capacity, model_width)
     sums = [0.0] * per_context
     for k in range(exps):
@@ -202,8 +213,6 @@
         return lax.ppermute(rows, ("pipe", "ctx"), pairs)
 
     returned = [to_next_owner(finished[k], k).reshape(-1, model_width) for k in range(contexts)]
-    next_slots = slot_index.astype(jnp.float32) + returned[0][0, 0].astype(jnp.float32) * 0.0
-    next_slots = shift(next_slots[None, :], "pipe", 1)[0].astype(jnp.int32)
     next_match = (slot_ids[None, :] == next_slots[:, None]).astype(jnp.bfloat16)
     returned = jnp.concatenate(returned, axis=0)
     layer = jnp.dot(next_match, returned, preferred_element_type=jnp.float32)

time: 230 us -> 213 us (0.926); the launches traced: 230 us -> 210 us
  starting transfers between devices: 61 us -> 26.2 us
  local copies, waits for them, and re-layouts: 4.62 us -> 10.2 us
  waiting for transfers between devices: 113 us -> 118 us
  between operations: 1.29 us -> 6 us
  other arithmetic: 3.91 us -> 7.59 us
  matrix products: 45.8 us -> 42.2 us
    ppermute x19, starting transfers between devices: 55.5 us -> 17.8 us  [shift(): lax.ppermute(value, axis, [(i, (i + by) % devices) for i in range(devices)])]
    ppermute x19, waiting for transfers between devices: 80.9 us -> 88.8 us  [shift(): lax.ppermute(value, axis, [(i, (i + by) % devices) for i in range(devices)])]
    slice x1 -> x8, local copies, waits for them, and re-layouts: 0.51 us -> 5.72 us  [the longest x6 4.01 us: mixed_halves(): behind = sum((block[0, 0] * 0.0 for block in sent))]
    ppermute x4, waiting for transfers between devices: 32.1 us -> 29.3 us  [to_next_owner(): return lax.ppermute(rows, ('pipe', 'ctx'), pairs)]
    ppermute x4, starting transfers between devices: 5.55 us -> 8.37 us  [to_next_owner(): return lax.ppermute(rows, ('pipe', 'ctx'), pairs)]
  transfers between devices with their start and end apart: 23 -> 23, of which waited for: 10 -> 9; matrix products, arithmetic and copies ran while one was open for 20% -> 24% of each run, Pallas kernels for 0% -> 0%
where the time goes in v11:
time: 213 us; the launch traced here: 210 us
  waiting for transfers between devices  118 us (55%)
  matrix products  42.2 us (20%)
  starting transfers between devices  26.2 us (12%)
  local copies, waits for them, and re-layouts  10.2 us (5%)
  other arithmetic  7.59 us (4%)
  between operations  6 us (3%)
    ppermute x19, waiting for transfers between devices, shift(): lax.ppermute(value, axis, [(i, (i + by) % devices) for i in range(devices)])  88.8 us
    ppermute x4, waiting for transfers between devices, to_next_owner(): return lax.ppermute(rows, ('pipe', 'ctx'), pairs)  29.3 us
    dot_general x8, matrix products, mixed_halves(): term = jnp.dot(attended, weights[half], preferred_element_type=jnp.float32)  21.4 us
    ppermute x19, starting transfers between devices, shift(): lax.ppermute(value, axis, [(i, (i + by) % devices) for i in range(devices)])  17.8 us
    ppermute x4, starting transfers between devices, to_next_owner(): return lax.ppermute(rows, ('pipe', 'ctx'), pairs)  8.37 us
    dot_general x4, matrix products, attend_block(): jnp.einsum('hqk,kd->qhd', attention_weights, value_rows, preferred_elemen...  5.84 us
    dot_general x2, matrix products, gate_and_up(): gate_up = jnp.dot(rows, in_weight[0, 0], preferred_element_type=jnp.float32)  5.21 us
    sub x4, matrix products, attend_block(): attention_weights = jax.nn.softmax(scores, axis=-1).astype(jnp.bfloat16)  4.85 us
  transfers between devices with their start and end apart: 23, of which 9 were waited for; matrix products, arithmetic and copies ran while one was open for 24% of the time, Pallas kernels for 0%

profile of v11, /device:TPU:0, one launch (start us, length us, event | category | flops | bytes accessed | tf_op | source)
XLA Modules:
  0.0 210.2 jit_solution(12679883581474093733)
XLA Ops:
  0.0 0.5 collective-permute-start.7
  0.5 0.7 fusion.70
  1.4 0.8 select_reduce_fusion
  2.2 0.7 fusion.91
  2.9 2.6 %collective-permute-start = (f32[1,128]{1,0:T(1,128)S(1)}, f32[1,128]{1,0:T(1,128)S(1)}, u32[]{:S(2)}, u32[]{:S(2)}) collective-permute-start(f32[1,128]{1,0:T(1,128)S(1)} %fusion.91), channel_id=1, source_target_pairs={{0,8},{8,16},{16,24},{24,0},{1,9},{9,17},{17,25},{25,1},{2,10},{10... | collective-permute-start | bytes 1544 | tf_op jit(solution)/shard_map/ppermute | solution.py:15
  5.4 1.0 dynamic-slice_bitcast_fusion.7
  6.4 3.7 %collective-permute-start.3 = (bf16[128,256]{1,0:T(8,128)(2,1)S(1)}, bf16[128,256]{1,0:T(8,128)(2,1)S(1)}, u32[]{:S(2)}, u32[]{:S(2)}) collective-permute-start(bf16[128,256]{1,0:T(8,128)(2,1)S(1)} %pad_maximum_fusion.4), channel_id=1, source_target_pairs={{0,6},{2,0},{4,2},{6,4},{1,7},{3,1},{5,3},{7,5},{8,14},{10,8},{12,... | collective-permute-start | bytes 196616 | tf_op jit(solution)/shard_map/ppermute | solution.py:15
  10.2 1.3 constant_dynamic-slice_fusion
  11.9 0.9 broadcast_compare_fusion
  12.8 4.3 %collective-permute-start.2 = (bf16[128,256]{1,0:T(8,128)(2,1)S(1)}, bf16[128,256]{1,0:T(8,128)(2,1)S(1)}, u32[]{:S(2)}, u32[]{:S(2)}) collective-permute-start(bf16[128,256]{1,0:T(8,128)(2,1)S(1)} %pad_maximum_fusion.3), channel_id=1, source_target_pairs={{0,4},{2,6},{4,0},{6,2},{1,5},{3,7},{5,1},{7,3},{8,12},{10,14},{12... | collective-permute-start | bytes 196616 | tf_op jit(solution)/shard_map/ppermute | solution.py:15
  17.4 0.8 copy.39
  18.5 6.1 %collective-permute-done.2 = bf16[128,256]{1,0:T(8,128)(2,1)S(1)} collective-permute-done((bf16[128,256]{1,0:T(8,128)(2,1)S(1)}, bf16[128,256]{1,0:T(8,128)(2,1)S(1)}, u32[]{:S(2)}, u32[]{:S(2)}) %collective-permute-start.2) | collective-permute-done | bytes 65568 | tf_op jit(solution)/shard_map/ppermute | solution.py:15
  24.8 0.7 collective-permute-start.6
  25.5 0.8 fusion.119
  26.2 1.0 convolution_convert_fusion.5
  27.3 3.1 %fusion.123 = bf16[128,2048]{1,0:T(8,128)(2,1)S(1)} fusion(bf16[128,1024]{0,1:T(8,128)(2,1)S(1)} %bitcast.255, bf16[1024,2048]{1,0:T(8,128)(2,1)} %collective-permute-done.7), kind=kOutput, calls=%fused_computation.201 | convolution fusion | flops 536870912 | bytes 4980736 | tf_op jit(solution)/shard_map/dot_general | solution.py:90
  30.4 0.6 slice.141
  31.0 1.3 collective-permute-start.9
  32.3 1.2 slice.139
  34.1 0.7 broadcast_add_fusion
  34.9 0.5 slice.140
  35.4 1.5 collective-permute-start.8
  38.2 26.4 %collective-permute-done.6 = bf16[128,1024]{0,1:T(8,128)(2,1)S(1)} collective-permute-done((bf16[128,1024]{0,1:T(8,128)(2,1)S(1)}, bf16[128,1024]{0,1:T(8,128)(2,1)S(1)}, u32[]{:S(2)}, u32[]{:S(2)}) %collective-permute-start.6) | collective-permute-done | bytes 262176 | tf_op jit(solution)/shard_map/ppermute | solution.py:15
  64.7 1.6 fusion.120
  66.3 1.9 convolution_convert_fusion.4
  68.2 2.9 %fusion.98 = f32[128,2048]{1,0:T(8,128)S(1)} fusion(bf16[128,1024]{0,1:T(8,128)(2,1)S(1)} %bitcast.259, bf16[1,1024,2048]{2,1,0:T(8,128)(2,1)} %param.12), kind=kOutput, calls=%fused_computation.182 | convolution fusion | flops 536870912 | bytes 5505024 | tf_op jit(solution)/shard_map/dot_general | solution.py:90
  71.1 2.9 %fusion.124 = f32[128,2048]{1,0:T(8,128)S(1)} fusion(bf16[128,1024]{0,1:T(8,128)(2,1)S(1)} %bitcast.260, bf16[1024,2048]{1,0:T(8,128)(2,1)} %collective-permute-done.7), kind=kOutput, calls=%fused_computation.202 | convolution fusion | flops 536870912 | bytes 5505024 | tf_op jit(solution)/shard_map/dot_general | solution.py:90
  74.2 0.6 slice.143
  74.9 0.5 slice.142
  76.9 1.7 fusion.121
  78.6 1.9 convolution_convert_fusion.3
  80.5 2.9 %fusion.96 = f32[128,2048]{1,0:T(8,128)S(1)} fusion(bf16[128,1024]{0,1:T(8,128)(2,1)S(1)} %bitcast.261, bf16[1,1024,2048]{2,1,0:T(8,128)(2,1)} %param.12), kind=kOutput, calls=%fused_computation.180 | convolution fusion | flops 536870912 | bytes 5505024 | tf_op jit(solution)/shard_map/dot_general | solution.py:90
  83.5 2.9 %fusion.125 = f32[128,2048]{1,0:T(8,128)S(1)} fusion(bf16[128,1024]{0,1:T(8,128)(2,1)S(1)} %bitcast.262, bf16[1024,2048]{1,0:T(8,128)(2,1)} %collective-permute-done.7), kind=kOutput, calls=%fused_computation.203 | convolution fusion | flops 536870912 | bytes 5505024 | tf_op jit(solution)/shard_map/dot_general | solution.py:90
  86.4 5.1 %collective-permute-done.11 = bf16[128,2048]{1,0:T(8,128)(2,1)S(1)} collective-permute-done((bf16[128,2048]{1,0:T(8,128)(2,1)S(1)}, bf16[128,2048]{1,0:T(8,128)(2,1)S(1)}, u32[]{:S(2)}, u32[]{:S(2)}) %collective-permute-start.11) | collective-permute-done | bytes 524320 | tf_op jit(solution)/shard_map/ppermute | solution.py:15
  91.6 0.6 slice.145
  92.2 10.5 %collective-permute-done.10 = bf16[128,2048]{1,0:T(8,128)(2,1)S(1)} collective-permute-done((bf16[128,2048]{1,0:T(8,128)(2,1)S(1)}, bf16[128,2048]{1,0:T(8,128)(2,1)S(1)}, u32[]{:S(2)}, u32[]{:S(2)}) %collective-permute-start.10) | collective-permute-done | bytes 524320 | tf_op jit(solution)/shard_map/ppermute | solution.py:15
  102.7 0.9 add_convert_fusion.1
  103.6 1.2 slice.144
  106.1 0.8 fusion.122
  107.1 1.0 convolution_convert_fusion.2
  108.3 2.9 %convolution_add_fusion.1 = f32[128,2048]{1,0:T(8,128)S(1)} fusion(bf16[128,1024]{0,1:T(8,128)(2,1)S(1)} %bitcast.257, bf16[1,1,128,4096]{3,2,1,0:T(8,128)(2,1)S(1)} %copy-done.1, s32[]{:T(128)S(6)} %select_n.179, bf16[1,1024,2048]{2,1,0:T(8,128)(2,1)} %param.12), kind=kOutput, calls=%fused_computation.23 | convolution fusion | flops 537395200 | bytes 6029316 | tf_op jit(solution)/shard_map/dot_general | solution.py:90
  111.2 2.9 %convolution_add_fusion = f32[128,2048]{1,0:T(8,128)S(1)} fusion(bf16[128,1024]{0,1:T(8,128)(2,1)S(1)} %bitcast.258, bf16[1024,2048]{1,0:T(8,128)(2,1)} %collective-permute-done.7, bf16[1,1,128,4096]{3,2,1,0:T(8,128)(2,1)S(1)} %copy-done.1, s32[]{:T(128)S(6)} %select_n.180), kind=kOutput, calls=%fused_computation.22 | convolution fusion | flops 537395200 | bytes 6029316 | tf_op jit(solution)/shard_map/dot_general | solution.py:90
  114.3 9.0 %collective-permute-done.12 = bf16[128,2048]{1,0:T(8,128)(2,1)S(1)} collective-permute-done((bf16[128,2048]{1,0:T(8,128)(2,1)}, bf16[128,2048]{1,0:T(8,128)(2,1)S(1)}, u32[]{:S(2)}, u32[]{:S(2)}) %collective-permute-start.12) | collective-permute-done | bytes 524320 | tf_op jit(solution)/shard_map/ppermute | solution.py:15
  123.5 0.2 fusion.25
  123.7 0.6 convolution_convert_fusion
  124.6 2.3 %collective-permute-start.14 = (bf16[1,48,4224]{2,1,0:T(8,128)(2,1)S(1)}, bf16[1,48,4224]{2,1,0:T(8,128)(2,1)S(1)}, u32[]{:S(2)}, u32[]{:S(2)}) collective-permute-start(bf16[1,48,4224]{2,1,0:T(8,128)(2,1)S(1)} %get-tuple-element.12), channel_id=1, source_target_pairs={{0,2},{2,4},{4,6},{6,0},{1,3},{3,5},{5,7},{7,1},{8,10},{10,12},{12... | collective-permute-start | bytes 1216520 | tf_op jit(solution)/shard_map/ppermute | solution.py:15
  126.9 7.5 %collective-permute-done.16 = bf16[1,48,4224]{2,1,0:T(8,128)(2,1)S(1)} collective-permute-done((bf16[1,48,4224]{2,1,0:T(8,128)(2,1)S(1)}, bf16[1,48,4224]{2,1,0:T(8,128)(2,1)S(1)}, u32[]{:S(2)}, u32[]{:S(2)}) %collective-permute-start.16) | collective-permute-done | bytes 405536 | tf_op jit(solution)/shard_map/ppermute | solution.py:15
  134.4 22.8 %collective-permute-done.15 = bf16[1,48,4224]{2,1,0:T(8,128)(2,1)S(1)} collective-permute-done((bf16[1,48,4224]{2,1,0:T(8,128)(2,1)S(1)}, bf16[1,48,4224]{2,1,0:T(8,128)(2,1)S(1)}, u32[]{:S(2)}, u32[]{:S(2)}) %collective-permute-start.15) | collective-permute-done | bytes 405536 | tf_op jit(solution)/shard_map/ppermute | solution.py:15
  157.6 0.5 multiply_reduce_fusion.1
  158.1 2.6 %fusion.17 = f32[192,1536]{1,0:T(8,128)S(1)} fusion(bf16[192,4096]{1,0:T(8,128)(2,1)S(1)} %bitcast.251, bf16[1,1,4096,1536]{3,2,1,0:T(8,128)(2,1)S(1)} %bitcast.278, f32[192]{0:T(256)S(1)} %add_rsqrt_fusion.1), kind=kOutput, calls=%fused_computation.20 | convolution fusion | flops 2416214016 | bytes 15336192 | tf_op jit(solution)/shard_map/dot_general | solution.py:177
  160.8 0.5 slice.162
  161.9 0.6 multiply_reduce_fusion
  162.6 2.6 %fusion.20 = f32[192,1536]{1,0:T(8,128)S(1)} fusion(bf16[192,4096]{1,0:T(8,128)(2,1)S(1)} %bitcast.254, bf16[1,1,4096,1536]{3,2,1,0:T(8,128)(2,1)S(1)} %bitcast.278, f32[192]{0:T(256)S(1)} %add_rsqrt_fusion), kind=kOutput, calls=%fused_computation.21 | convolution fusion | flops 2416214016 | bytes 15336192 | tf_op jit(solution)/shard_map/dot_general | solution.py:177
  165.2 1.5 fusion.12
  166.7 0.6 collective-permute-start.18
  167.2 1.4 fusion.10
  168.9 1.4 collective-permute-done.18
  170.3 0.8 fusion.16
  171.1 1.6 collective-permute-start.19
  172.7 1.1 collective-permute-start.22
  173.8 1.9 collective-permute-start.21
  175.7 3.8 %collective-permute-start.20 = (bf16[1,48,4096]{2,1,0:T(8,128)(2,1)S(1)}, bf16[1,48,4096]{2,1,0:T(8,128)(2,1)S(1)}, u32[]{:S(2)}, u32[]{:S(2)}) collective-permute-start(bf16[1,48,4096]{2,1,0:T(8,128)(2,1)S(1)} %get-tuple-element.16), channel_id=1, source_target_pairs={{0,14},{2,8},{4,10},{6,12},{8,22},{10,16},{12,18},{14,20},{16,30},... | collective-permute-start | bytes 1179656 | tf_op jit(solution)/shard_map/ppermute | solution.py:213
  179.5 29.2 %collective-permute-done.19 = bf16[1,48,4096]{2,1,0:T(8,128)(2,1)S(1)} collective-permute-done((bf16[1,48,4096]{2,1,0:T(8,128)(2,1)S(1)}, bf16[1,48,4096]{2,1,0:T(8,128)(2,1)S(1)}, u32[]{:S(2)}, u32[]{:S(2)}) %collective-permute-start.19) | collective-permute-done | bytes 393248 | tf_op jit(solution)/shard_map/ppermute | solution.py:213
  208.8 1.5 fusion.15
  (93 shorter events, 3.4 us)
Async XLA Ops:
  0.0 11.8 %copy-start.6 = (s32[1,1,128,1]{2,3,1,0:T(1,128)S(1)}, s32[1,1,128,1]{2,3,1,0:T(1,128)}, u32[]{:S(2)}) copy-start(s32[1,1,128,1]{2,3,1,0:T(1,128)} %param.16) | copy-start | bytes 1540
  0.0 11.8 %copy-start.7 = (f32[1,1,128,1]{2,3,1,0:T(1,128)S(1)}, f32[1,1,128,1]{2,3,1,0:T(1,128)}, u32[]{:S(2)}) copy-start(f32[1,1,128,1]{2,3,1,0:T(1,128)} %param.17) | copy-start | bytes 1540
  0.0 27.3 %collective-permute-start.7 = (bf16[1024,2048]{1,0:T(8,128)(2,1)}, bf16[1024,2048]{1,0:T(8,128)(2,1)}, u32[]{:S(2)}, u32[]{:S(2)}) collective-permute-start(bf16[1024,2048]{1,0:T(8,128)(2,1)} %bitcast.248), channel_id=1, source_target_pairs={{0,1},{1,0},{2,3},{3,2},{4,5},{5,4},{6,7},{7,6},{8,9},{9,8},{10,11... | collective-permute-start | bytes 12582920 | tf_op jit(solution)/shard_map/ppermute | solution.py:15
  1.4 11.4 %copy-start.5 = (f32[1,4096]{1,0:T(1,128)S(1)}, f32[1,4096]{1,0:T(1,128)}, u32[]{:S(2)}) copy-start(f32[1,4096]{1,0:T(1,128)} %param.13) | copy-start | bytes 49156
  2.9 9.9 %collective-permute-start = (f32[1,128]{1,0:T(1,128)S(1)}, f32[1,128]{1,0:T(1,128)S(1)}, u32[]{:S(2)}, u32[]{:S(2)}) collective-permute-start(f32[1,128]{1,0:T(1,128)S(1)} %fusion.91), channel_id=1, source_target_pairs={{0,8},{8,16},{16,24},{24,0},{1,9},{9,17},{17,25},{25,1},{2,10},{10... | collective-permute-start | bytes 1544 | tf_op jit(solution)/shard_map/ppermute | solution.py:15
  6.4 12.1 %collective-permute-start.3 = (bf16[128,256]{1,0:T(8,128)(2,1)S(1)}, bf16[128,256]{1,0:T(8,128)(2,1)S(1)}, u32[]{:S(2)}, u32[]{:S(2)}) collective-permute-start(bf16[128,256]{1,0:T(8,128)(2,1)S(1)} %pad_maximum_fusion.4), channel_id=1, source_target_pairs={{0,6},{2,0},{4,2},{6,4},{1,7},{3,1},{5,3},{7,5},{8,14},{10,8},{12,... | collective-permute-start | bytes 196616 | tf_op jit(solution)/shard_map/ppermute | solution.py:15
  10.1 8.4 %collective-permute-start.1 = (bf16[128,256]{1,0:T(8,128)(2,1)S(1)}, bf16[128,256]{1,0:T(8,128)(2,1)S(1)}, u32[]{:S(2)}, u32[]{:S(2)}) collective-permute-start(bf16[128,256]{1,0:T(8,128)(2,1)S(1)} %pad_maximum_fusion.2), channel_id=1, source_target_pairs={{0,2},{2,4},{4,6},{6,0},{1,3},{3,5},{5,7},{7,1},{8,10},{10,12},{12... | collective-permute-start | bytes 196616 | tf_op jit(solution)/shard_map/ppermute | solution.py:15
  11.6 13.0 %collective-permute-start.4 = (bf16[128,1024]{0,1:T(8,128)(2,1)S(1)}, bf16[128,1024]{0,1:T(8,128)(2,1)S(1)}, u32[]{:S(2)}, u32[]{:S(2)}) collective-permute-start(bf16[128,1024]{0,1:T(8,128)(2,1)S(1)} %bitcast.269), channel_id=1, source_target_pairs={{0,2},{2,4},{4,6},{6,0},{1,3},{3,5},{5,7},{7,1},{8,10},{10,12},{12... | collective-permute-start | bytes 786440 | tf_op jit(solution)/shard_map/ppermute | solution.py:15
  12.8 11.8 %collective-permute-start.2 = (bf16[128,256]{1,0:T(8,128)(2,1)S(1)}, bf16[128,256]{1,0:T(8,128)(2,1)S(1)}, u32[]{:S(2)}, u32[]{:S(2)}) collective-permute-start(bf16[128,256]{1,0:T(8,128)(2,1)S(1)} %pad_maximum_fusion.3), channel_id=1, source_target_pairs={{0,4},{2,6},{4,0},{6,2},{1,5},{3,7},{5,1},{7,3},{8,12},{10,14},{12... | collective-permute-start | bytes 196616 | tf_op jit(solution)/shard_map/ppermute | solution.py:15
  24.7 41.7 %copy-start.2 = (bf16[512,256]{1,0:T(8,128)(2,1)}, bf16[512,256]{1,0:T(8,128)(2,1)S(1)}, u32[]{:S(2)}) copy-start(bf16[512,256]{1,0:T(8,128)(2,1)S(1)} %pad_maximum_fusion.1) | copy-start | bytes 786436
  24.7 52.2 %collective-permute-start.5 = (bf16[128,1024]{0,1:T(8,128)(2,1)}, bf16[128,1024]{0,1:T(8,128)(2,1)S(1)}, u32[]{:S(2)}, u32[]{:S(2)}) collective-permute-start(bf16[128,1024]{0,1:T(8,128)(2,1)} %bitcast.15), channel_id=1, source_target_pairs={{0,6},{2,0},{4,2},{6,4},{1,7},{3,1},{5,3},{7,5},{8,14},{10,8},{12,... | collective-permute-start | bytes 786440 | tf_op jit(solution)/shard_map/ppermute | solution.py:15
  24.8 39.9 %collective-permute-start.6 = (bf16[128,1024]{0,1:T(8,128)(2,1)S(1)}, bf16[128,1024]{0,1:T(8,128)(2,1)S(1)}, u32[]{:S(2)}, u32[]{:S(2)}) collective-permute-start(bf16[128,1024]{0,1:T(8,128)(2,1)S(1)} %bitcast.270), channel_id=1, source_target_pairs={{0,4},{2,6},{4,0},{6,2},{1,5},{3,7},{5,1},{7,3},{8,12},{10,14},{12... | collective-permute-start | bytes 786440 | tf_op jit(solution)/shard_map/ppermute | solution.py:15
  27.3 6.8 %copy-start = (bf16[1,1024,2048]{2,1,0:T(8,128)(2,1)S(1)}, bf16[1,1024,2048]{2,1,0:T(8,128)(2,1)}, u32[]{:S(2)}) copy-start(bf16[1,1024,2048]{2,1,0:T(8,128)(2,1)} %param.12) | copy-start | bytes 12582916
  31.0 43.1 %collective-permute-start.9 = (bf16[128,2048]{1,0:T(8,128)(2,1)S(1)}, bf16[128,2048]{1,0:T(8,128)(2,1)S(1)}, u32[]{:S(2)}, u32[]{:S(2)}) collective-permute-start(bf16[128,2048]{1,0:T(8,128)(2,1)S(1)} %fusion.123), channel_id=1, source_target_pairs={{0,2},{2,4},{4,6},{6,0},{1,3},{3,5},{5,7},{7,1},{8,10},{10,12},{12... | collective-permute-start | bytes 1572872 | tf_op jit(solution)/shard_map/ppermute | solution.py:15
  35.4 39.4 %collective-permute-start.8 = (bf16[128,2048]{1,0:T(8,128)(2,1)S(1)}, bf16[128,2048]{1,0:T(8,128)(2,1)S(1)}, u32[]{:S(2)}, u32[]{:S(2)}) collective-permute-start(bf16[128,2048]{1,0:T(8,128)(2,1)S(1)} %broadcast_add_fusion), channel_id=1, source_target_pairs={{0,2},{2,4},{4,6},{6,0},{1,3},{3,5},{5,7},{7,1},{8,10},{10,12},{12... | collective-permute-start | bytes 1572872 | tf_op jit(solution)/shard_map/ppermute | solution.py:15
  74.8 16.7 %collective-permute-start.11 = (bf16[128,2048]{1,0:T(8,128)(2,1)S(1)}, bf16[128,2048]{1,0:T(8,128)(2,1)S(1)}, u32[]{:S(2)}, u32[]{:S(2)}) collective-permute-start(bf16[128,2048]{1,0:T(8,128)(2,1)S(1)} %add_convert_fusion.2), channel_id=1, source_target_pairs={{0,2},{2,4},{4,6},{6,0},{1,3},{3,5},{5,7},{7,1},{8,10},{10,12},{12... | collective-permute-start | bytes 1572872 | tf_op jit(solution)/shard_map/ppermute | solution.py:15
  75.5 27.2 %collective-permute-start.10 = (bf16[128,2048]{1,0:T(8,128)(2,1)S(1)}, bf16[128,2048]{1,0:T(8,128)(2,1)S(1)}, u32[]{:S(2)}, u32[]{:S(2)}) collective-permute-start(bf16[128,2048]{1,0:T(8,128)(2,1)S(1)} %add_convert_fusion.3), channel_id=1, source_target_pairs={{0,2},{2,4},{4,6},{6,0},{1,3},{3,5},{5,7},{7,1},{8,10},{10,12},{12... | collective-permute-start | bytes 1572872 | tf_op jit(solution)/shard_map/ppermute | solution.py:15
  76.9 1.8 copy-start.3
  92.2 22.0 %collective-permute-start.13 = (bf16[128,2048]{1,0:T(8,128)(2,1)S(1)}, bf16[128,2048]{1,0:T(8,128)(2,1)S(1)}, u32[]{:S(2)}, u32[]{:S(2)}) collective-permute-start(bf16[128,2048]{1,0:T(8,128)(2,1)S(1)} %add_convert_fusion), channel_id=1, source_target_pairs={{0,2},{2,4},{4,6},{6,0},{1,3},{3,5},{5,7},{7,1},{8,10},{10,12},{12... | collective-permute-start | bytes 1572872 | tf_op jit(solution)/shard_map/ppermute | solution.py:15
  104.8 18.5 %collective-permute-start.12 = (bf16[128,2048]{1,0:T(8,128)(2,1)}, bf16[128,2048]{1,0:T(8,128)(2,1)S(1)}, u32[]{:S(2)}, u32[]{:S(2)}) collective-permute-start(bf16[128,2048]{1,0:T(8,128)(2,1)} %add_convert_fusion.1), channel_id=1, source_target_pairs={{0,2},{2,4},{4,6},{6,0},{1,3},{3,5},{5,7},{7,1},{8,10},{10,12},{12... | collective-permute-start | bytes 1572872 | tf_op jit(solution)/shard_map/ppermute | solution.py:15
  106.1 1.0 copy-start.4
  107.1 1.2 copy-start.1
  114.2 43.9 %slice-start = ((s8[12582912]{0:T(1024)(128)(4,1)}), s8[4194304]{0:T(1024)(128)(4,1)S(1)}, s32[]{:S(2)}) async-start(s8[12582912]{0:T(1024)(128)(4,1)} %bitcast.277), calls=%async_computation | async-start | bytes 8388608
  123.5 34.6 %slice-start.1 = ((s8[12582912]{0:T(1024)(128)(4,1)}), s8[4194304]{0:T(1024)(128)(4,1)S(1)}, s32[]{:S(2)}) async-start(s8[12582912]{0:T(1024)(128)(4,1)} %bitcast.277), calls=%async_computation.1 | async-start | bytes 8388608
  124.4 9.9 %collective-permute-start.16 = (bf16[1,48,4224]{2,1,0:T(8,128)(2,1)S(1)}, bf16[1,48,4224]{2,1,0:T(8,128)(2,1)S(1)}, u32[]{:S(2)}, u32[]{:S(2)}) collective-permute-start(bf16[1,48,4224]{2,1,0:T(8,128)(2,1)S(1)} %get-tuple-element.10), channel_id=1, source_target_pairs={{0,6},{2,0},{4,2},{6,4},{1,7},{3,1},{5,3},{7,5},{8,14},{10,8},{12,... | collective-permute-start | bytes 1216520 | tf_op jit(solution)/shard_map/ppermute | solution.py:15
  124.5 33.6 %slice-start.2 = ((s8[12582912]{0:T(1024)(128)(4,1)}), s8[4194304]{0:T(1024)(128)(4,1)S(1)}, s32[]{:S(2)}) async-start(s8[12582912]{0:T(1024)(128)(4,1)} %bitcast.277), calls=%async_computation.2 | async-start | bytes 8388608
  124.5 32.7 %collective-permute-start.15 = (bf16[1,48,4224]{2,1,0:T(8,128)(2,1)S(1)}, bf16[1,48,4224]{2,1,0:T(8,128)(2,1)S(1)}, u32[]{:S(2)}, u32[]{:S(2)}) collective-permute-start(bf16[1,48,4224]{2,1,0:T(8,128)(2,1)S(1)} %get-tuple-element.11), channel_id=1, source_target_pairs={{0,4},{2,6},{4,0},{6,2},{1,5},{3,7},{5,1},{7,3},{8,12},{10,14},{12... | collective-permute-start | bytes 1216520 | tf_op jit(solution)/shard_map/ppermute | solution.py:15
  124.6 32.6 %collective-permute-start.14 = (bf16[1,48,4224]{2,1,0:T(8,128)(2,1)S(1)}, bf16[1,48,4224]{2,1,0:T(8,128)(2,1)S(1)}, u32[]{:S(2)}, u32[]{:S(2)}) collective-permute-start(bf16[1,48,4224]{2,1,0:T(8,128)(2,1)S(1)} %get-tuple-element.12), channel_id=1, source_target_pairs={{0,2},{2,4},{4,6},{6,0},{1,3},{3,5},{5,7},{7,1},{8,10},{10,12},{12... | collective-permute-start | bytes 1216520 | tf_op jit(solution)/shard_map/ppermute | solution.py:15
  157.5 4.4 %collective-permute-start.17 = (bf16[4,48,4096]{2,1,0:T(8,128)(2,1)S(1)}, bf16[4,48,4096]{2,1,0:T(8,128)(2,1)S(1)}, u32[]{:S(2)}, u32[]{:S(2)}) collective-permute-start(bf16[4,48,4096]{2,1,0:T(8,128)(2,1)S(1)} %bitcast.249), channel_id=1, source_target_pairs={{0,1},{1,0},{2,3},{3,2},{4,5},{5,4},{6,7},{7,6},{8,9},{9,8},{10,11... | collective-permute-start | bytes 4718600 | tf_op jit(solution)/shard_map/ppermute | solution.py:15
  158.1 7.0 %slice-start.3 = ((s8[6291456]{0:T(1024)(128)(4,1)}), s8[4194304]{0:T(1024)(128)(4,1)S(1)}, s32[]{:S(2)}) async-start(s8[6291456]{0:T(1024)(128)(4,1)} %bitcast.279), calls=%async_computation.3 | async-start | bytes 8388608
  161.9 3.2 %slice-start.4 = ((s8[6291456]{0:T(1024)(128)(4,1)}), s8[2097152]{0:T(1024)(128)(4,1)S(1)}, s32[]{:S(2)}) async-start(s8[6291456]{0:T(1024)(128)(4,1)} %bitcast.279), calls=%async_computation.4 | async-start | bytes 4194304
  166.7 3.6 %collective-permute-start.18 = (bf16[4,48,4096]{2,1,0:T(8,128)(2,1)S(1)}, bf16[4,48,4096]{2,1,0:T(8,128)(2,1)S(1)}, u32[]{:S(2)}, u32[]{:S(2)}) collective-permute-start(bf16[4,48,4096]{2,1,0:T(8,128)(2,1)S(1)} %bitcast.281), channel_id=1, source_target_pairs={{0,1},{1,0},{2,3},{3,2},{4,5},{5,4},{6,7},{7,6},{8,9},{9,8},{10,11... | collective-permute-start | bytes 4718600 | tf_op jit(solution)/shard_map/ppermute | solution.py:15
  171.1 37.6 %collective-permute-start.19 = (bf16[1,48,4096]{2,1,0:T(8,128)(2,1)S(1)}, bf16[1,48,4096]{2,1,0:T(8,128)(2,1)S(1)}, u32[]{:S(2)}, u32[]{:S(2)}) collective-permute-start(bf16[1,48,4096]{2,1,0:T(8,128)(2,1)S(1)} %get-tuple-element.13), channel_id=1, source_target_pairs={{0,8},{2,10},{4,12},{6,14},{8,16},{10,18},{12,20},{14,22},{16,24},... | collective-permute-start | bytes 1179656 | tf_op jit(solution)/shard_map/ppermute | solution.py:213
  172.7 36.1 %collective-permute-start.22 = (bf16[1,48,4096]{2,1,0:T(8,128)(2,1)S(1)}, bf16[1,48,4096]{2,1,0:T(8,128)(2,1)S(1)}, u32[]{:S(2)}, u32[]{:S(2)}) collective-permute-start(bf16[1,48,4096]{2,1,0:T(8,128)(2,1)S(1)} %get-tuple-element.14), channel_id=1, source_target_pairs={{0,10},{2,12},{4,14},{6,8},{8,18},{10,20},{12,22},{14,16},{16,26},... | collective-permute-start | bytes 1179656 | tf_op jit(solution)/shard_map/ppermute | solution.py:213
  173.8 34.9 %collective-permute-start.21 = (bf16[1,48,4096]{2,1,0:T(8,128)(2,1)S(1)}, bf16[1,48,4096]{2,1,0:T(8,128)(2,1)S(1)}, u32[]{:S(2)}, u32[]{:S(2)}) collective-permute-start(bf16[1,48,4096]{2,1,0:T(8,128)(2,1)S(1)} %get-tuple-element.15), channel_id=1, source_target_pairs={{0,12},{2,14},{4,8},{6,10},{8,20},{10,22},{12,16},{14,18},{16,28},... | collective-permute-start | bytes 1179656 | tf_op jit(solution)/shard_map/ppermute | solution.py:213
  175.7 33.0 %collective-permute-start.20 = (bf16[1,48,4096]{2,1,0:T(8,128)(2,1)S(1)}, bf16[1,48,4096]{2,1,0:T(8,128)(2,1)S(1)}, u32[]{:S(2)}, u32[]{:S(2)}) collective-permute-start(bf16[1,48,4096]{2,1,0:T(8,128)(2,1)S(1)} %get-tuple-element.16), channel_id=1, source_target_pairs={{0,14},{2,8},{4,10},{6,12},{8,22},{10,16},{12,18},{14,20},{16,30},... | collective-permute-start | bytes 1179656 | tf_op jit(solution)/shard_map/ppermute | solution.py:213

commit v12 on v11

--- a/solution.py
+++ b/solution.py
@@ -74,7 +74,7 @@
     origins = [(me - k) % contexts * rows for k in range(contexts)]
     col_ids = jnp.concatenate([origin + within for origin in origins])
 
-    held, sent, next_slots = [None, None], [], shift(slots_here, "pipe", 1)
+    held, sent, next_slots = [None, None], [], None
     for k in [*range(1, contexts), 0]:
         behind = sum(block[0, 0] * 0.0 for block in sent)
         attended = attend_block(
@@ -84,6 +84,8 @@
             origins[k] + within,
             col_ids,
         ).reshape(rows, group_width)
+        if k == contexts - 1:
+            next_slots = shift(slots_here + behind, "pipe", 1)
         sent = []
         terms = []
         for half in range(2):

time: 213 us -> 200 us (0.939)
  waiting for transfers between devices: 118 us -> 105 us
  starting transfers between devices: 26.2 us -> 29.2 us
    ppermute x19, waiting for transfers between devices: 88.8 us -> 73.6 us  [shift(): lax.ppermute(value, axis, [(i, (i + by) % devices) for i in range(devices)])]
    ppermute x19, starting transfers between devices: 17.8 us -> 23 us  [shift(): lax.ppermute(value, axis, [(i, (i + by) % devices) for i in range(devices)])]
    ppermute x4, starting transfers between devices: 8.37 us -> 6.22 us  [to_next_owner(): return lax.ppermute(rows, ('pipe', 'ctx'), pairs)]
    ppermute x4, waiting for transfers between devices: 29.3 us -> 31.4 us  [to_next_owner(): return lax.ppermute(rows, ('pipe', 'ctx'), pairs)]
  transfers between devices with their start and end apart: 23 -> 23, of which waited for: 9 -> 9; matrix products, arithmetic and copies ran while one was open for 24% -> 25% of each run, Pallas kernels for 0% -> 0%
where the time goes in v12:
time: 200 us; the launch traced here: 199 us
  waiting for transfers between devices  105 us (52%)
  matrix products  42.2 us (21%)
  starting transfers between devices  29.2 us (15%)
  local copies, waits for them, and re-layouts  10.8 us (5%)
  between operations  6.05 us (3%)
  other arithmetic  5.62 us (3%)
    ppermute x19, waiting for transfers between devices, shift(): lax.ppermute(value, axis, [(i, (i + by) % devices) for i in range(devices)])  73.6 us
    ppermute x4, waiting for transfers between devices, to_next_owner(): return lax.ppermute(rows, ('pipe', 'ctx'), pairs)  31.4 us
    ppermute x19, starting transfers between devices, shift(): lax.ppermute(value, axis, [(i, (i + by) % devices) for i in range(devices)])  23 us
    dot_general x8, matrix products, mixed_halves(): term = jnp.dot(attended, weights[half], preferred_element_type=jnp.float32)  21.4 us
    ppermute x4, starting transfers between devices, to_next_owner(): return lax.ppermute(rows, ('pipe', 'ctx'), pairs)  6.22 us
    dot_general x4, matrix products, attend_block(): jnp.einsum('hqk,kd->qhd', attention_weights, value_rows, preferred_elemen...  5.84 us
    dot_general x2, matrix products, gate_and_up(): gate_up = jnp.dot(rows, in_weight[0, 0], preferred_element_type=jnp.float32)  5.21 us
    sub x4, matrix products, attend_block(): attention_weights = jax.nn.softmax(scores, axis=-1).astype(jnp.bfloat16)  4.85 us
  transfers between devices with their start and end apart: 23, of which 9 were waited for; matrix products, arithmetic and copies ran while one was open for 25% of the time, Pallas kernels for 0%

profile of v12, /device:TPU:0, one launch (start us, length us, event | category | flops | bytes accessed | tf_op | source)
XLA Modules:
  0.0 198.9 jit_solution(469277967466904295)
XLA Ops:
  0.0 0.5 collective-permute-start.5
  0.5 1.0 dynamic-slice_bitcast_fusion.7
  1.4 4.8 %collective-permute-start.2 = (bf16[128,256]{1,0:T(8,128)(2,1)S(1)}, bf16[128,256]{1,0:T(8,128)(2,1)S(1)}, u32[]{:S(2)}, u32[]{:S(2)}) collective-permute-start(bf16[128,256]{1,0:T(8,128)(2,1)S(1)} %pad_maximum_fusion.4), channel_id=1, source_target_pairs={{0,6},{2,0},{4,2},{6,4},{1,7},{3,1},{5,3},{7,5},{8,14},{10,8},{12,... | collective-permute-start | bytes 196616 | tf_op jit(solution)/shard_map/ppermute | solution.py:15
  6.3 1.1 collective-permute-start.1
  7.4 1.3 constant_dynamic-slice_fusion.3
  8.8 3.4 %collective-permute-start.3 = (bf16[128,1024]{0,1:T(8,128)(2,1)S(1)}, bf16[128,1024]{0,1:T(8,128)(2,1)S(1)}, u32[]{:S(2)}, u32[]{:S(2)}) collective-permute-start(bf16[128,1024]{0,1:T(8,128)(2,1)S(1)} %bitcast.269), channel_id=1, source_target_pairs={{0,2},{2,4},{4,6},{6,0},{1,3},{3,5},{5,7},{7,1},{8,10},{10,12},{12... | collective-permute-start | bytes 786440 | tf_op jit(solution)/shard_map/ppermute | solution.py:15
  12.8 0.9 broadcast_compare_fusion.2
  13.8 0.8 copy.38
  14.7 0.8 copy.47
  15.7 4.2 %collective-permute-done.1 = bf16[128,256]{1,0:T(8,128)(2,1)S(1)} collective-permute-done((bf16[128,256]{1,0:T(8,128)(2,1)S(1)}, bf16[128,256]{1,0:T(8,128)(2,1)S(1)}, u32[]{:S(2)}, u32[]{:S(2)}) %collective-permute-start.1) | collective-permute-done | bytes 65568 | tf_op jit(solution)/shard_map/ppermute | solution.py:15
  19.9 0.9 collective-permute-start.4
  20.9 1.5 collective-permute-start.9
  22.3 0.8 fusion.118
  23.1 1.0 convolution_convert_fusion.5
  24.2 3.1 %fusion.122 = bf16[128,2048]{1,0:T(8,128)(2,1)S(1)} fusion(bf16[128,1024]{0,1:T(8,128)(2,1)S(1)} %bitcast.255, bf16[1024,2048]{1,0:T(8,128)(2,1)} %collective-permute-done.5), kind=kOutput, calls=%fused_computation.201 | convolution fusion | flops 536870912 | bytes 4980736 | tf_op jit(solution)/shard_map/dot_general | solution.py:92
  27.3 0.6 slice.141
  27.8 0.6 collective-permute-start.7
  28.4 1.3 slice.139
  30.4 0.7 broadcast_add_fusion
  31.2 0.6 slice.140
  31.7 0.6 collective-permute-start.6
  33.7 27.5 %collective-permute-done.4 = bf16[128,1024]{0,1:T(8,128)(2,1)S(1)} collective-permute-done((bf16[128,1024]{0,1:T(8,128)(2,1)}, bf16[128,1024]{0,1:T(8,128)(2,1)S(1)}, u32[]{:S(2)}, u32[]{:S(2)}) %collective-permute-start.4) | collective-permute-done | bytes 262176 | tf_op jit(solution)/shard_map/ppermute | solution.py:15
  61.2 1.6 fusion.119
  62.8 1.9 convolution_convert_fusion.4
  64.7 2.9 %fusion.97 = f32[128,2048]{1,0:T(8,128)S(1)} fusion(bf16[128,1024]{0,1:T(8,128)(2,1)S(1)} %bitcast.261, bf16[1,1024,2048]{2,1,0:T(8,128)(2,1)} %param.12), kind=kOutput, calls=%fused_computation.182 | convolution fusion | flops 536870912 | bytes 5505024 | tf_op jit(solution)/shard_map/dot_general | solution.py:92
  67.7 2.9 %fusion.123 = f32[128,2048]{1,0:T(8,128)S(1)} fusion(bf16[128,1024]{0,1:T(8,128)(2,1)S(1)} %bitcast.262, bf16[1024,2048]{1,0:T(8,128)(2,1)} %collective-permute-done.5), kind=kOutput, calls=%fused_computation.202 | convolution fusion | flops 536870912 | bytes 5505024 | tf_op jit(solution)/shard_map/dot_general | solution.py:92
  70.7 0.6 slice.143
  71.5 0.5 slice.142
  73.4 1.7 fusion.120
  75.1 1.9 convolution_convert_fusion.3
  77.0 1.7 collective-permute-start.8
  78.7 2.9 %fusion.95 = f32[128,2048]{1,0:T(8,128)S(1)} fusion(bf16[128,1024]{0,1:T(8,128)(2,1)S(1)} %bitcast.259, bf16[1,1024,2048]{2,1,0:T(8,128)(2,1)} %param.12), kind=kOutput, calls=%fused_computation.180 | convolution fusion | flops 536870912 | bytes 5505024 | tf_op jit(solution)/shard_map/dot_general | solution.py:92
  81.6 2.9 %fusion.124 = f32[128,2048]{1,0:T(8,128)S(1)} fusion(bf16[128,1024]{0,1:T(8,128)(2,1)S(1)} %bitcast.260, bf16[1024,2048]{1,0:T(8,128)(2,1)} %collective-permute-done.5), kind=kOutput, calls=%fused_computation.203 | convolution fusion | flops 536870912 | bytes 5505024 | tf_op jit(solution)/shard_map/dot_general | solution.py:92
  84.6 3.2 %collective-permute-done.11 = bf16[128,2048]{1,0:T(8,128)(2,1)S(1)} collective-permute-done((bf16[128,2048]{1,0:T(8,128)(2,1)S(1)}, bf16[128,2048]{1,0:T(8,128)(2,1)S(1)}, u32[]{:S(2)}, u32[]{:S(2)}) %collective-permute-start.11) | collective-permute-done | bytes 524320 | tf_op jit(solution)/shard_map/ppermute | solution.py:15
  88.0 0.6 slice.145
  88.6 7.2 %collective-permute-done.10 = bf16[128,2048]{1,0:T(8,128)(2,1)S(1)} collective-permute-done((bf16[128,2048]{1,0:T(8,128)(2,1)S(1)}, bf16[128,2048]{1,0:T(8,128)(2,1)S(1)}, u32[]{:S(2)}, u32[]{:S(2)}) %collective-permute-start.10) | collective-permute-done | bytes 524320 | tf_op jit(solution)/shard_map/ppermute | solution.py:15
  95.8 0.9 add_convert_fusion.1
  96.7 1.2 slice.144
  99.3 0.8 fusion.121
  100.1 1.0 convolution_convert_fusion.2
  101.3 2.9 %convolution_add_fusion.1 = f32[128,2048]{1,0:T(8,128)S(1)} fusion(bf16[128,1024]{0,1:T(8,128)(2,1)S(1)} %bitcast.257, bf16[1,1,128,4096]{3,2,1,0:T(8,128)(2,1)S(1)} %copy-done.1, s32[]{:T(128)S(6)} %select_n.179, bf16[1,1024,2048]{2,1,0:T(8,128)(2,1)} %param.12), kind=kOutput, calls=%fused_computation.23 | convolution fusion | flops 537395200 | bytes 6029316 | tf_op jit(solution)/shard_map/dot_general | solution.py:92
  104.2 2.9 %convolution_add_fusion = f32[128,2048]{1,0:T(8,128)S(1)} fusion(bf16[128,1024]{0,1:T(8,128)(2,1)S(1)} %bitcast.258, bf16[1024,2048]{1,0:T(8,128)(2,1)} %collective-permute-done.5, bf16[1,1,128,4096]{3,2,1,0:T(8,128)(2,1)S(1)} %copy-done.1, s32[]{:T(128)S(6)} %select_n.180), kind=kOutput, calls=%fused_computation.22 | convolution fusion | flops 537395200 | bytes 6029316 | tf_op jit(solution)/shard_map/dot_general | solution.py:92
  107.4 7.0 %collective-permute-done.12 = bf16[128,2048]{1,0:T(8,128)(2,1)S(1)} collective-permute-done((bf16[128,2048]{1,0:T(8,128)(2,1)}, bf16[128,2048]{1,0:T(8,128)(2,1)S(1)}, u32[]{:S(2)}, u32[]{:S(2)}) %collective-permute-start.12) | collective-permute-done | bytes 524320 | tf_op jit(solution)/shard_map/ppermute | solution.py:15
  114.5 0.2 fusion.25
  114.7 0.6 convolution_convert_fusion
  115.6 5.2 %collective-permute-start.15 = (bf16[1,48,4224]{2,1,0:T(8,128)(2,1)S(1)}, bf16[1,48,4224]{2,1,0:T(8,128)(2,1)S(1)}, u32[]{:S(2)}, u32[]{:S(2)}) collective-permute-start(bf16[1,48,4224]{2,1,0:T(8,128)(2,1)S(1)} %get-tuple-element.11), channel_id=1, source_target_pairs={{0,4},{2,6},{4,0},{6,2},{1,5},{3,7},{5,1},{7,3},{8,12},{10,14},{12... | collective-permute-start | bytes 1216520 | tf_op jit(solution)/shard_map/ppermute | solution.py:15
  120.7 2.0 %collective-permute-start.14 = (bf16[1,48,4224]{2,1,0:T(8,128)(2,1)S(1)}, bf16[1,48,4224]{2,1,0:T(8,128)(2,1)S(1)}, u32[]{:S(2)}, u32[]{:S(2)}) collective-permute-start(bf16[1,48,4224]{2,1,0:T(8,128)(2,1)S(1)} %get-tuple-element.12), channel_id=1, source_target_pairs={{0,2},{2,4},{4,6},{6,0},{1,3},{3,5},{5,7},{7,1},{8,10},{10,12},{12... | collective-permute-start | bytes 1216520 | tf_op jit(solution)/shard_map/ppermute | solution.py:15
  122.7 6.6 %collective-permute-done.16 = bf16[1,48,4224]{2,1,0:T(8,128)(2,1)S(1)} collective-permute-done((bf16[1,48,4224]{2,1,0:T(8,128)(2,1)S(1)}, bf16[1,48,4224]{2,1,0:T(8,128)(2,1)S(1)}, u32[]{:S(2)}, u32[]{:S(2)}) %collective-permute-start.16) | collective-permute-done | bytes 405536 | tf_op jit(solution)/shard_map/ppermute | solution.py:15
  129.4 16.5 %collective-permute-done.15 = bf16[1,48,4224]{2,1,0:T(8,128)(2,1)S(1)} collective-permute-done((bf16[1,48,4224]{2,1,0:T(8,128)(2,1)S(1)}, bf16[1,48,4224]{2,1,0:T(8,128)(2,1)S(1)}, u32[]{:S(2)}, u32[]{:S(2)}) %collective-permute-start.15) | collective-permute-done | bytes 405536 | tf_op jit(solution)/shard_map/ppermute | solution.py:15
  146.3 0.5 multiply_reduce_fusion.1
  146.8 2.6 %fusion.17 = f32[192,1536]{1,0:T(8,128)S(1)} fusion(bf16[192,4096]{1,0:T(8,128)(2,1)S(1)} %bitcast.251, bf16[1,1,4096,1536]{3,2,1,0:T(8,128)(2,1)S(1)} %bitcast.277, f32[192]{0:T(256)S(1)} %add_rsqrt_fusion.1), kind=kOutput, calls=%fused_computation.20 | convolution fusion | flops 2416214016 | bytes 15336192 | tf_op jit(solution)/shard_map/dot_general | solution.py:179
  149.4 0.5 slice.162
  150.6 0.6 multiply_reduce_fusion
  151.2 2.6 %fusion.20 = f32[192,1536]{1,0:T(8,128)S(1)} fusion(bf16[192,4096]{1,0:T(8,128)(2,1)S(1)} %bitcast.254, bf16[1,1,4096,1536]{3,2,1,0:T(8,128)(2,1)S(1)} %bitcast.277, f32[192]{0:T(256)S(1)} %add_rsqrt_fusion), kind=kOutput, calls=%fused_computation.21 | convolution fusion | flops 2416214016 | bytes 15336192 | tf_op jit(solution)/shard_map/dot_general | solution.py:179
  153.9 1.5 fusion.12
  155.3 0.6 collective-permute-start.18
  155.9 1.4 fusion.10
  157.6 1.4 collective-permute-done.18
  158.9 0.8 fusion.16
  159.8 1.5 collective-permute-start.19
  161.4 0.5 collective-permute-start.21
  161.9 4.2 %collective-permute-start.20 = (bf16[1,48,4096]{2,1,0:T(8,128)(2,1)S(1)}, bf16[1,48,4096]{2,1,0:T(8,128)(2,1)S(1)}, u32[]{:S(2)}, u32[]{:S(2)}) collective-permute-start(bf16[1,48,4096]{2,1,0:T(8,128)(2,1)S(1)} %get-tuple-element.16), channel_id=1, source_target_pairs={{0,14},{2,8},{4,10},{6,12},{8,22},{10,16},{12,18},{14,20},{16,30},... | collective-permute-start | bytes 1179656 | tf_op jit(solution)/shard_map/ppermute | solution.py:215
  166.1 31.4 %collective-permute-done.19 = bf16[1,48,4096]{2,1,0:T(8,128)(2,1)S(1)} collective-permute-done((bf16[1,48,4096]{2,1,0:T(8,128)(2,1)S(1)}, bf16[1,48,4096]{2,1,0:T(8,128)(2,1)S(1)}, u32[]{:S(2)}, u32[]{:S(2)}) %collective-permute-start.19) | collective-permute-done | bytes 393248 | tf_op jit(solution)/shard_map/ppermute | solution.py:215
  197.5 1.5 fusion.15
  (91 shorter events, 3.0 us)
Async XLA Ops:
  0.0 12.3 %copy-start.5 = (s32[1,1,128,1]{2,3,1,0:T(1,128)S(1)}, s32[1,1,128,1]{2,3,1,0:T(1,128)}, u32[]{:S(2)}) copy-start(s32[1,1,128,1]{2,3,1,0:T(1,128)} %param.16) | copy-start | bytes 1540
  0.0 24.2 %collective-permute-start.5 = (bf16[1024,2048]{1,0:T(8,128)(2,1)}, bf16[1024,2048]{1,0:T(8,128)(2,1)}, u32[]{:S(2)}, u32[]{:S(2)}) collective-permute-start(bf16[1024,2048]{1,0:T(8,128)(2,1)} %bitcast.248), channel_id=1, source_target_pairs={{0,1},{1,0},{2,3},{3,2},{4,5},{5,4},{6,7},{7,6},{8,9},{9,8},{10,11... | collective-permute-start | bytes 12582920 | tf_op jit(solution)/shard_map/ppermute | solution.py:15
  0.5 12.3 %copy-start.6 = (f32[1,1,128,1]{2,3,1,0:T(1,128)S(1)}, f32[1,1,128,1]{2,3,1,0:T(1,128)}, u32[]{:S(2)}) copy-start(f32[1,1,128,1]{2,3,1,0:T(1,128)} %param.17) | copy-start | bytes 1540
  0.5 13.2 %copy-start.4 = (f32[1,4096]{1,0:T(1,128)S(1)}, f32[1,4096]{1,0:T(1,128)}, u32[]{:S(2)}) copy-start(f32[1,4096]{1,0:T(1,128)} %param.13) | copy-start | bytes 49156
  1.4 14.3 %collective-permute-start.2 = (bf16[128,256]{1,0:T(8,128)(2,1)S(1)}, bf16[128,256]{1,0:T(8,128)(2,1)S(1)}, u32[]{:S(2)}, u32[]{:S(2)}) collective-permute-start(bf16[128,256]{1,0:T(8,128)(2,1)S(1)} %pad_maximum_fusion.4), channel_id=1, source_target_pairs={{0,6},{2,0},{4,2},{6,4},{1,7},{3,1},{5,3},{7,5},{8,14},{10,8},{12,... | collective-permute-start | bytes 196616 | tf_op jit(solution)/shard_map/ppermute | solution.py:15
  6.3 9.4 %collective-permute-start = (bf16[128,256]{1,0:T(8,128)(2,1)S(1)}, bf16[128,256]{1,0:T(8,128)(2,1)S(1)}, u32[]{:S(2)}, u32[]{:S(2)}) collective-permute-start(bf16[128,256]{1,0:T(8,128)(2,1)S(1)} %pad_maximum_fusion.2), channel_id=1, source_target_pairs={{0,2},{2,4},{4,6},{6,0},{1,3},{3,5},{5,7},{7,1},{8,10},{10,12},{12... | collective-permute-start | bytes 196616 | tf_op jit(solution)/shard_map/ppermute | solution.py:15
  6.3 13.6 %collective-permute-start.1 = (bf16[128,256]{1,0:T(8,128)(2,1)S(1)}, bf16[128,256]{1,0:T(8,128)(2,1)S(1)}, u32[]{:S(2)}, u32[]{:S(2)}) collective-permute-start(bf16[128,256]{1,0:T(8,128)(2,1)S(1)} %pad_maximum_fusion.3), channel_id=1, source_target_pairs={{0,4},{2,6},{4,0},{6,2},{1,5},{3,7},{5,1},{7,3},{8,12},{10,14},{12... | collective-permute-start | bytes 196616 | tf_op jit(solution)/shard_map/ppermute | solution.py:15
  8.8 11.1 %collective-permute-start.3 = (bf16[128,1024]{0,1:T(8,128)(2,1)S(1)}, bf16[128,1024]{0,1:T(8,128)(2,1)S(1)}, u32[]{:S(2)}, u32[]{:S(2)}) collective-permute-start(bf16[128,1024]{0,1:T(8,128)(2,1)S(1)} %bitcast.269), channel_id=1, source_target_pairs={{0,2},{2,4},{4,6},{6,0},{1,3},{3,5},{5,7},{7,1},{8,10},{10,12},{12... | collective-permute-start | bytes 786440 | tf_op jit(solution)/shard_map/ppermute | solution.py:15
  19.9 42.9 %copy-start.2 = (bf16[512,256]{1,0:T(8,128)(2,1)}, bf16[512,256]{1,0:T(8,128)(2,1)S(1)}, u32[]{:S(2)}) copy-start(bf16[512,256]{1,0:T(8,128)(2,1)S(1)} %pad_maximum_fusion.1) | copy-start | bytes 786436
  19.9 41.3 %collective-permute-start.4 = (bf16[128,1024]{0,1:T(8,128)(2,1)}, bf16[128,1024]{0,1:T(8,128)(2,1)S(1)}, u32[]{:S(2)}, u32[]{:S(2)}) collective-permute-start(bf16[128,1024]{0,1:T(8,128)(2,1)} %bitcast.13), channel_id=1, source_target_pairs={{0,4},{2,6},{4,0},{6,2},{1,5},{3,7},{5,1},{7,3},{8,12},{10,14},{12... | collective-permute-start | bytes 786440 | tf_op jit(solution)/shard_map/ppermute | solution.py:15
  20.9 52.4 %collective-permute-start.9 = (bf16[128,1024]{0,1:T(8,128)(2,1)}, bf16[128,1024]{0,1:T(8,128)(2,1)S(1)}, u32[]{:S(2)}, u32[]{:S(2)}) collective-permute-start(bf16[128,1024]{0,1:T(8,128)(2,1)} %bitcast.33), channel_id=1, source_target_pairs={{0,6},{2,0},{4,2},{6,4},{1,7},{3,1},{5,3},{7,5},{8,14},{10,8},{12,... | collective-permute-start | bytes 786440 | tf_op jit(solution)/shard_map/ppermute | solution.py:15
  24.2 6.2 %copy-start = (bf16[1,1024,2048]{2,1,0:T(8,128)(2,1)S(1)}, bf16[1,1024,2048]{2,1,0:T(8,128)(2,1)}, u32[]{:S(2)}) copy-start(bf16[1,1024,2048]{2,1,0:T(8,128)(2,1)} %param.12) | copy-start | bytes 12582916
  27.8 42.8 %collective-permute-start.7 = (bf16[128,2048]{1,0:T(8,128)(2,1)S(1)}, bf16[128,2048]{1,0:T(8,128)(2,1)S(1)}, u32[]{:S(2)}, u32[]{:S(2)}) collective-permute-start(bf16[128,2048]{1,0:T(8,128)(2,1)S(1)} %fusion.122), channel_id=1, source_target_pairs={{0,2},{2,4},{4,6},{6,0},{1,3},{3,5},{5,7},{7,1},{8,10},{10,12},{12... | collective-permute-start | bytes 1572872 | tf_op jit(solution)/shard_map/ppermute | solution.py:15
  31.7 39.6 %collective-permute-start.6 = (bf16[128,2048]{1,0:T(8,128)(2,1)S(1)}, bf16[128,2048]{1,0:T(8,128)(2,1)S(1)}, u32[]{:S(2)}, u32[]{:S(2)}) collective-permute-start(bf16[128,2048]{1,0:T(8,128)(2,1)S(1)} %broadcast_add_fusion), channel_id=1, source_target_pairs={{0,2},{2,4},{4,6},{6,0},{1,3},{3,5},{5,7},{7,1},{8,10},{10,12},{12... | collective-permute-start | bytes 1572872 | tf_op jit(solution)/shard_map/ppermute | solution.py:15
  71.3 16.5 %collective-permute-start.11 = (bf16[128,2048]{1,0:T(8,128)(2,1)S(1)}, bf16[128,2048]{1,0:T(8,128)(2,1)S(1)}, u32[]{:S(2)}, u32[]{:S(2)}) collective-permute-start(bf16[128,2048]{1,0:T(8,128)(2,1)S(1)} %add_convert_fusion.2), channel_id=1, source_target_pairs={{0,2},{2,4},{4,6},{6,0},{1,3},{3,5},{5,7},{7,1},{8,10},{10,12},{12... | collective-permute-start | bytes 1572872 | tf_op jit(solution)/shard_map/ppermute | solution.py:15
  72.0 23.8 %collective-permute-start.10 = (bf16[128,2048]{1,0:T(8,128)(2,1)S(1)}, bf16[128,2048]{1,0:T(8,128)(2,1)S(1)}, u32[]{:S(2)}, u32[]{:S(2)}) collective-permute-start(bf16[128,2048]{1,0:T(8,128)(2,1)S(1)} %add_convert_fusion.3), channel_id=1, source_target_pairs={{0,2},{2,4},{4,6},{6,0},{1,3},{3,5},{5,7},{7,1},{8,10},{10,12},{12... | collective-permute-start | bytes 1572872 | tf_op jit(solution)/shard_map/ppermute | solution.py:15
  73.3 1.8 copy-start.3
  77.0 7.6 %collective-permute-start.8 = (f32[1,128]{1,0:T(1,128)S(1)}, f32[1,128]{1,0:T(1,128)S(1)}, u32[]{:S(2)}, u32[]{:S(2)}) collective-permute-start(f32[1,128]{1,0:T(1,128)S(1)} %convert_add_fusion), channel_id=1, source_target_pairs={{0,8},{8,16},{16,24},{24,0},{1,9},{9,17},{17,25},{25,1},{2,10},{10... | collective-permute-start | bytes 1544 | tf_op jit(solution)/shard_map/ppermute | solution.py:15
  88.6 18.6 %collective-permute-start.13 = (bf16[128,2048]{1,0:T(8,128)(2,1)S(1)}, bf16[128,2048]{1,0:T(8,128)(2,1)S(1)}, u32[]{:S(2)}, u32[]{:S(2)}) collective-permute-start(bf16[128,2048]{1,0:T(8,128)(2,1)S(1)} %add_convert_fusion), channel_id=1, source_target_pairs={{0,2},{2,4},{4,6},{6,0},{1,3},{3,5},{5,7},{7,1},{8,10},{10,12},{12... | collective-permute-start | bytes 1572872 | tf_op jit(solution)/shard_map/ppermute | solution.py:15
  97.9 16.4 %collective-permute-start.12 = (bf16[128,2048]{1,0:T(8,128)(2,1)}, bf16[128,2048]{1,0:T(8,128)(2,1)S(1)}, u32[]{:S(2)}, u32[]{:S(2)}) collective-permute-start(bf16[128,2048]{1,0:T(8,128)(2,1)} %add_convert_fusion.1), channel_id=1, source_target_pairs={{0,2},{2,4},{4,6},{6,0},{1,3},{3,5},{5,7},{7,1},{8,10},{10,12},{12... | collective-permute-start | bytes 1572872 | tf_op jit(solution)/shard_map/ppermute | solution.py:15
  100.1 1.2 copy-start.1
  107.2 39.6 %slice-start = ((s8[12582912]{0:T(1024)(128)(4,1)}), s8[4194304]{0:T(1024)(128)(4,1)S(1)}, s32[]{:S(2)}) async-start(s8[12582912]{0:T(1024)(128)(4,1)} %bitcast.276), calls=%async_computation | async-start | bytes 8388608
  114.5 32.3 %slice-start.1 = ((s8[12582912]{0:T(1024)(128)(4,1)}), s8[4194304]{0:T(1024)(128)(4,1)S(1)}, s32[]{:S(2)}) async-start(s8[12582912]{0:T(1024)(128)(4,1)} %bitcast.276), calls=%async_computation.1 | async-start | bytes 8388608
  115.4 13.9 %collective-permute-start.16 = (bf16[1,48,4224]{2,1,0:T(8,128)(2,1)S(1)}, bf16[1,48,4224]{2,1,0:T(8,128)(2,1)S(1)}, u32[]{:S(2)}, u32[]{:S(2)}) collective-permute-start(bf16[1,48,4224]{2,1,0:T(8,128)(2,1)S(1)} %get-tuple-element.10), channel_id=1, source_target_pairs={{0,6},{2,0},{4,2},{6,4},{1,7},{3,1},{5,3},{7,5},{8,14},{10,8},{12,... | collective-permute-start | bytes 1216520 | tf_op jit(solution)/shard_map/ppermute | solution.py:15
  115.5 31.3 %slice-start.2 = ((s8[12582912]{0:T(1024)(128)(4,1)}), s8[4194304]{0:T(1024)(128)(4,1)S(1)}, s32[]{:S(2)}) async-start(s8[12582912]{0:T(1024)(128)(4,1)} %bitcast.276), calls=%async_computation.2 | async-start | bytes 8388608
  115.6 30.3 %collective-permute-start.15 = (bf16[1,48,4224]{2,1,0:T(8,128)(2,1)S(1)}, bf16[1,48,4224]{2,1,0:T(8,128)(2,1)S(1)}, u32[]{:S(2)}, u32[]{:S(2)}) collective-permute-start(bf16[1,48,4224]{2,1,0:T(8,128)(2,1)S(1)} %get-tuple-element.11), channel_id=1, source_target_pairs={{0,4},{2,6},{4,0},{6,2},{1,5},{3,7},{5,1},{7,3},{8,12},{10,14},{12... | collective-permute-start | bytes 1216520 | tf_op jit(solution)/shard_map/ppermute | solution.py:15
  120.7 25.2 %collective-permute-start.14 = (bf16[1,48,4224]{2,1,0:T(8,128)(2,1)S(1)}, bf16[1,48,4224]{2,1,0:T(8,128)(2,1)S(1)}, u32[]{:S(2)}, u32[]{:S(2)}) collective-permute-start(bf16[1,48,4224]{2,1,0:T(8,128)(2,1)S(1)} %get-tuple-element.12), channel_id=1, source_target_pairs={{0,2},{2,4},{4,6},{6,0},{1,3},{3,5},{5,7},{7,1},{8,10},{10,12},{12... | collective-permute-start | bytes 1216520 | tf_op jit(solution)/shard_map/ppermute | solution.py:15
  146.2 4.4 %collective-permute-start.17 = (bf16[4,48,4096]{2,1,0:T(8,128)(2,1)S(1)}, bf16[4,48,4096]{2,1,0:T(8,128)(2,1)S(1)}, u32[]{:S(2)}, u32[]{:S(2)}) collective-permute-start(bf16[4,48,4096]{2,1,0:T(8,128)(2,1)S(1)} %bitcast.249), channel_id=1, source_target_pairs={{0,1},{1,0},{2,3},{3,2},{4,5},{5,4},{6,7},{7,6},{8,9},{9,8},{10,11... | collective-permute-start | bytes 4718600 | tf_op jit(solution)/shard_map/ppermute | solution.py:15
  146.8 7.0 %slice-start.3 = ((s8[6291456]{0:T(1024)(128)(4,1)}), s8[4194304]{0:T(1024)(128)(4,1)S(1)}, s32[]{:S(2)}) async-start(s8[6291456]{0:T(1024)(128)(4,1)} %bitcast.278), calls=%async_computation.3 | async-start | bytes 8388608
  150.6 3.2 %slice-start.4 = ((s8[6291456]{0:T(1024)(128)(4,1)}), s8[2097152]{0:T(1024)(128)(4,1)S(1)}, s32[]{:S(2)}) async-start(s8[6291456]{0:T(1024)(128)(4,1)} %bitcast.278), calls=%async_computation.4 | async-start | bytes 4194304
  155.3 3.6 %collective-permute-start.18 = (bf16[4,48,4096]{2,1,0:T(8,128)(2,1)S(1)}, bf16[4,48,4096]{2,1,0:T(8,128)(2,1)S(1)}, u32[]{:S(2)}, u32[]{:S(2)}) collective-permute-start(bf16[4,48,4096]{2,1,0:T(8,128)(2,1)S(1)} %bitcast.280), channel_id=1, source_target_pairs={{0,1},{1,0},{2,3},{3,2},{4,5},{5,4},{6,7},{7,6},{8,9},{9,8},{10,11... | collective-permute-start | bytes 4718600 | tf_op jit(solution)/shard_map/ppermute | solution.py:15
  159.8 37.6 %collective-permute-start.19 = (bf16[1,48,4096]{2,1,0:T(8,128)(2,1)S(1)}, bf16[1,48,4096]{2,1,0:T(8,128)(2,1)S(1)}, u32[]{:S(2)}, u32[]{:S(2)}) collective-permute-start(bf16[1,48,4096]{2,1,0:T(8,128)(2,1)S(1)} %get-tuple-element.13), channel_id=1, source_target_pairs={{0,8},{2,10},{4,12},{6,14},{8,16},{10,18},{12,20},{14,22},{16,24},... | collective-permute-start | bytes 1179656 | tf_op jit(solution)/shard_map/ppermute | solution.py:215
  161.4 36.1 %collective-permute-start.22 = (bf16[1,48,4096]{2,1,0:T(8,128)(2,1)S(1)}, bf16[1,48,4096]{2,1,0:T(8,128)(2,1)S(1)}, u32[]{:S(2)}, u32[]{:S(2)}) collective-permute-start(bf16[1,48,4096]{2,1,0:T(8,128)(2,1)S(1)} %get-tuple-element.14), channel_id=1, source_target_pairs={{0,10},{2,12},{4,14},{6,8},{8,18},{10,20},{12,22},{14,16},{16,26},... | collective-permute-start | bytes 1179656 | tf_op jit(solution)/shard_map/ppermute | solution.py:215
  161.4 36.1 %collective-permute-start.21 = (bf16[1,48,4096]{2,1,0:T(8,128)(2,1)S(1)}, bf16[1,48,4096]{2,1,0:T(8,128)(2,1)S(1)}, u32[]{:S(2)}, u32[]{:S(2)}) collective-permute-start(bf16[1,48,4096]{2,1,0:T(8,128)(2,1)S(1)} %get-tuple-element.15), channel_id=1, source_target_pairs={{0,12},{2,14},{4,8},{6,10},{8,20},{10,22},{12,16},{14,18},{16,28},... | collective-permute-start | bytes 1179656 | tf_op jit(solution)/shard_map/ppermute | solution.py:215
  161.9 35.6 %collective-permute-start.20 = (bf16[1,48,4096]{2,1,0:T(8,128)(2,1)S(1)}, bf16[1,48,4096]{2,1,0:T(8,128)(2,1)S(1)}, u32[]{:S(2)}, u32[]{:S(2)}) collective-permute-start(bf16[1,48,4096]{2,1,0:T(8,128)(2,1)S(1)} %get-tuple-element.16), channel_id=1, source_target_pairs={{0,14},{2,8},{4,10},{6,12},{8,22},{10,16},{12,18},{14,20},{16,30},... | collective-permute-start | bytes 1179656 | tf_op jit(solution)/shard_map/ppermute | solution.py:215

commit v13 on v12

--- a/solution.py
+++ b/solution.py
@@ -93,8 +93,8 @@
             if k == 0:
                 own = lax.dynamic_slice_in_dim(residual, offsets[half], width // 2, 1)
                 term = term + own.astype(jnp.float32)
-            if k == 1 and half == 0:
-                term = term + weights[1][0, 0].astype(jnp.float32) * 0.0
+            if k == 1 and half == 1 and contexts > 2:
+                term = term + blocks[2][0, 0].astype(jnp.float32) * 0.0
             terms.append(lax.optimization_barrier(term))
         for half in range(2):
             term = terms[half]

time: 200 us -> 201 us (level)
  matrix products: 42.2 us -> 45.4 us
  local copies, waits for them, and re-layouts: 10.8 us -> 8.45 us
    ppermute x19, starting transfers between devices: 23 us -> 19.2 us  [shift(): lax.ppermute(value, axis, [(i, (i + by) % devices) for i in range(devices)])]
    ppermute x4, starting transfers between devices: 6.22 us -> 9.2 us  [to_next_owner(): return lax.ppermute(rows, ('pipe', 'ctx'), pairs)]
    ppermute x4, waiting for transfers between devices: 31.4 us -> 28.4 us  [to_next_owner(): return lax.ppermute(rows, ('pipe', 'ctx'), pairs)]
    ppermute x19, waiting for transfers between devices: 73.6 us -> 76 us  [shift(): lax.ppermute(value, axis, [(i, (i + by) % devices) for i in range(devices)])]
    dot_general x8, matrix products: 21.4 us -> 23.4 us  [mixed_halves(): term = jnp.dot(attended, weights[half], preferred_element_type=jnp.float32)]
  transfers between devices with their start and end apart: 23 -> 23, of which waited for: 9 -> 10; matrix products, arithmetic and copies ran while one was open for 25% -> 25% of each run, Pallas kernels for 0% -> 0%
where the time goes in v13:
time: 201 us; the launch traced here: 198 us
  waiting for transfers between devices  104 us (52%)
  matrix products  45.4 us (23%)
  starting transfers between devices  28.4 us (14%)
  local copies, waits for them, and re-layouts  8.45 us (4%)
  between operations  5.84 us (3%)
  other arithmetic  5.76 us (3%)
    ppermute x19, waiting for transfers between devices, shift(): lax.ppermute(value, axis, [(i, (i + by) % devices) for i in range(devices)])  76 us
    ppermute x4, waiting for transfers between devices, to_next_owner(): return lax.ppermute(rows, ('pipe', 'ctx'), pairs)  28.4 us
    dot_general x8, matrix products, mixed_halves(): term = jnp.dot(attended, weights[half], preferred_element_type=jnp.float32)  23.4 us
    ppermute x19, starting transfers between devices, shift(): lax.ppermute(value, axis, [(i, (i + by) % devices) for i in range(devices)])  19.2 us
    ppermute x4, starting transfers between devices, to_next_owner(): return lax.ppermute(rows, ('pipe', 'ctx'), pairs)  9.2 us
    dot_general x4, matrix products, attend_block(): jnp.einsum('hqk,kd->qhd', attention_weights, value_rows, preferred_elemen...  7.01 us
    dot_general x2, matrix products, gate_and_up(): gate_up = jnp.dot(rows, in_weight[0, 0], preferred_element_type=jnp.float32)  5.22 us
    sub x4, matrix products, attend_block(): attention_weights = jax.nn.softmax(scores, axis=-1).astype(jnp.bfloat16)  4.75 us
  transfers between devices with their start and end apart: 23, of which 10 were waited for; matrix products, arithmetic and copies ran while one was open for 25% of the time, Pallas kernels for 0%

profile of v13, /device:TPU:0, one launch (start us, length us, event | category | flops | bytes accessed | tf_op | source)
XLA Modules:
  0.0 198.3 jit_solution(1762004837502985580)
XLA Ops:
  0.0 0.5 collective-permute-start.5
  0.5 1.0 dynamic-slice_bitcast_fusion.8
  1.4 4.8 %collective-permute-start.2 = (bf16[128,256]{1,0:T(8,128)(2,1)S(1)}, bf16[128,256]{1,0:T(8,128)(2,1)S(1)}, u32[]{:S(2)}, u32[]{:S(2)}) collective-permute-start(bf16[128,256]{1,0:T(8,128)(2,1)S(1)} %pad_maximum_fusion.4), channel_id=1, source_target_pairs={{0,6},{2,0},{4,2},{6,4},{1,7},{3,1},{5,3},{7,5},{8,14},{10,8},{12,... | collective-permute-start | bytes 196616 | tf_op jit(solution)/shard_map/ppermute | solution.py:15
  6.3 1.1 collective-permute-start.1
  7.4 1.3 dynamic-slice_bitcast_fusion
  8.8 3.4 %collective-permute-start.3 = (bf16[128,1024]{0,1:T(8,128)(2,1)S(1)}, bf16[128,1024]{0,1:T(8,128)(2,1)S(1)}, u32[]{:S(2)}, u32[]{:S(2)}) collective-permute-start(bf16[128,1024]{0,1:T(8,128)(2,1)S(1)} %bitcast.266), channel_id=1, source_target_pairs={{0,2},{2,4},{4,6},{6,0},{1,3},{3,5},{5,7},{7,1},{8,10},{10,12},{12... | collective-permute-start | bytes 786440 | tf_op jit(solution)/shard_map/ppermute | solution.py:15
  12.8 0.9 broadcast_compare_fusion.2
  14.2 5.7 %collective-permute-done.1 = bf16[128,256]{1,0:T(8,128)(2,1)S(1)} collective-permute-done((bf16[128,256]{1,0:T(8,128)(2,1)S(1)}, bf16[128,256]{1,0:T(8,128)(2,1)S(1)}, u32[]{:S(2)}, u32[]{:S(2)}) %collective-permute-start.1) | collective-permute-done | bytes 65568 | tf_op jit(solution)/shard_map/ppermute | solution.py:15
  19.9 0.9 collective-permute-start.4
  20.9 0.8 fusion.116
  21.7 1.0 convolution_convert_fusion.5
  22.7 2.9 %fusion.99 = bf16[128,2048]{1,0:T(8,128)(2,1)S(1)} fusion(bf16[128,1024]{0,1:T(8,128)(2,1)S(1)} %bitcast.254, bf16[1,1024,2048]{2,1,0:T(8,128)(2,1)} %param.12), kind=kOutput, calls=%fused_computation.184 | convolution fusion | flops 536870912 | bytes 4980736 | tf_op jit(solution)/shard_map/dot_general | solution.py:92
  25.6 0.5 slice.139
  26.2 0.5 collective-permute-start.6
  26.7 3.3 %collective-permute-start.9 = (bf16[128,1024]{0,1:T(8,128)(2,1)S(1)}, bf16[128,1024]{0,1:T(8,128)(2,1)}, u32[]{:S(2)}, u32[]{:S(2)}) collective-permute-start(bf16[128,1024]{0,1:T(8,128)(2,1)S(1)} %bitcast.267), channel_id=1, source_target_pairs={{0,6},{2,0},{4,2},{6,4},{1,7},{3,1},{5,3},{7,5},{8,14},{10,8},{12,... | collective-permute-start | bytes 786440 | tf_op jit(solution)/shard_map/ppermute | solution.py:15
  30.0 14.1 %collective-permute-done.4 = bf16[128,1024]{1,0:T(8,128)(2,1)S(1)} collective-permute-done((bf16[128,1024]{1,0:T(8,128)(2,1)S(1)}, bf16[128,1024]{1,0:T(8,128)(2,1)S(1)}, u32[]{:S(2)}, u32[]{:S(2)}) %collective-permute-start.4) | collective-permute-done | bytes 262176 | tf_op jit(solution)/shard_map/ppermute | solution.py:15
  44.1 0.6 slice.140
  45.4 2.9 %convolution_add_fusion.2 = bf16[128,2048]{1,0:T(8,128)(2,1)S(1)} fusion(bf16[128,1024]{0,1:T(8,128)(2,1)S(1)} %bitcast.255, bf16[1024,2048]{1,0:T(8,128)(2,1)} %collective-permute-done.5, f32[]{:T(128)} %bitcast.22), kind=kOutput, calls=%fused_computation.24 | convolution fusion | flops 537395200 | bytes 4980740 | tf_op jit(solution)/shard_map/dot_general | solution.py:92
  48.3 0.6 slice.141
  50.4 1.6 fusion.117
  52.0 1.9 convolution_convert_fusion.4
  53.9 2.9 %fusion.97 = f32[128,2048]{1,0:T(8,128)S(1)} fusion(bf16[128,1024]{0,1:T(8,128)(2,1)S(1)} %bitcast.260, bf16[1,1024,2048]{2,1,0:T(8,128)(2,1)} %param.12), kind=kOutput, calls=%fused_computation.182 | convolution fusion | flops 536870912 | bytes 5505024 | tf_op jit(solution)/shard_map/dot_general | solution.py:92
  56.9 0.5 slice.142
  57.6 2.9 %fusion.120 = f32[128,2048]{1,0:T(8,128)S(1)} fusion(bf16[128,1024]{0,1:T(8,128)(2,1)S(1)} %bitcast.261, bf16[1024,2048]{1,0:T(8,128)(2,1)} %collective-permute-done.5), kind=kOutput, calls=%fused_computation.201 | convolution fusion | flops 536870912 | bytes 5505024 | tf_op jit(solution)/shard_map/dot_general | solution.py:92
  60.5 5.0 %collective-permute-done.7 = bf16[128,2048]{1,0:T(8,128)(2,1)S(1)} collective-permute-done((bf16[128,2048]{1,0:T(8,128)(2,1)S(1)}, bf16[128,2048]{1,0:T(8,128)(2,1)S(1)}, u32[]{:S(2)}, u32[]{:S(2)}) %collective-permute-start.7) | collective-permute-done | bytes 524320 | tf_op jit(solution)/shard_map/ppermute | solution.py:15
  65.6 0.6 slice.143
  67.5 1.0 broadcast_add_fusion.1
  68.5 1.6 fusion.118
  70.1 1.9 convolution_convert_fusion.3
  72.0 2.9 %fusion.95 = f32[128,2048]{1,0:T(8,128)S(1)} fusion(bf16[128,1024]{0,1:T(8,128)(2,1)S(1)} %bitcast.258, bf16[1,1024,2048]{2,1,0:T(8,128)(2,1)} %param.12), kind=kOutput, calls=%fused_computation.180 | convolution fusion | flops 536870912 | bytes 5505024 | tf_op jit(solution)/shard_map/dot_general | solution.py:92
  74.9 1.8 collective-permute-done.10
  76.9 0.5 slice.144
  77.4 1.7 collective-permute-start.8
  79.1 2.9 %fusion.121 = f32[128,2048]{1,0:T(8,128)S(1)} fusion(bf16[128,1024]{0,1:T(8,128)(2,1)S(1)} %bitcast.259, bf16[1024,2048]{1,0:T(8,128)(2,1)} %collective-permute-done.5), kind=kOutput, calls=%fused_computation.202 | convolution fusion | flops 536870912 | bytes 5505024 | tf_op jit(solution)/shard_map/dot_general | solution.py:92
  82.1 5.9 %collective-permute-done.11 = bf16[128,2048]{1,0:T(8,128)(2,1)S(1)} collective-permute-done((bf16[128,2048]{1,0:T(8,128)(2,1)S(1)}, bf16[128,2048]{1,0:T(8,128)(2,1)S(1)}, u32[]{:S(2)}, u32[]{:S(2)}) %collective-permute-start.11) | collective-permute-done | bytes 524320 | tf_op jit(solution)/shard_map/ppermute | solution.py:15
  88.1 0.5 slice.145
  89.9 0.7 copy-done.1
  90.6 0.8 fusion.119
  91.4 2.2 %convolution_convert_fusion.2 = bf16[128,8,128]{2,0,1:T(8,128)(2,1)S(1)} fusion(f32[8,128]{1,0:T(8,128)S(1)} %fusion.119, bf16[512,256]{1,0:T(8,128)(2,1)} %copy-done.2, pred[128,512]{0,1:T(8,128)(4,1)S(1)} %get-tuple-element.30, bf16[128,8,128]{0,2,1:T(8,128)(2,1)} %bitcast.263), kind=kOutput, calls=%fused_computation.54 | convolution fusion | flops 271189504 | bytes 856064 | tf_op jit(solution)/shard_map/hqk,kd->qhd/dot_general | solution.py:28
  93.6 2.9 %convolution_add_fusion.1 = f32[128,2048]{1,0:T(8,128)S(1)} fusion(bf16[128,1024]{0,1:T(8,128)(2,1)S(1)} %bitcast.256, bf16[1,1,128,4096]{3,2,1,0:T(8,128)(2,1)S(1)} %copy-done, s32[]{:T(128)S(6)} %select_n.179, bf16[1,1024,2048]{2,1,0:T(8,128)(2,1)} %param.12), kind=kOutput, calls=%fused_computation.23 | convolution fusion | flops 537395200 | bytes 6029316 | tf_op jit(solution)/shard_map/dot_general | solution.py:92
  96.6 2.9 %convolution_add_fusion = f32[128,2048]{1,0:T(8,128)S(1)} fusion(bf16[128,1024]{0,1:T(8,128)(2,1)S(1)} %bitcast.257, bf16[1024,2048]{1,0:T(8,128)(2,1)} %collective-permute-done.5, bf16[1,1,128,4096]{3,2,1,0:T(8,128)(2,1)S(1)} %copy-done, s32[]{:T(128)S(6)} %select_n.180), kind=kOutput, calls=%fused_computation.22 | convolution fusion | flops 537395200 | bytes 6029316 | tf_op jit(solution)/shard_map/dot_general | solution.py:92
  99.7 9.7 %collective-permute-done.13 = bf16[128,2048]{1,0:T(8,128)(2,1)S(1)} collective-permute-done((bf16[128,2048]{1,0:T(8,128)(2,1)S(1)}, bf16[128,2048]{1,0:T(8,128)(2,1)S(1)}, u32[]{:S(2)}, u32[]{:S(2)}) %collective-permute-start.13) | collective-permute-done | bytes 524320 | tf_op jit(solution)/shard_map/ppermute | solution.py:15
  109.6 0.2 fusion.25
  109.8 0.6 convolution_convert_fusion
  110.7 2.0 %collective-permute-start.14 = (bf16[1,48,4224]{2,1,0:T(8,128)(2,1)S(1)}, bf16[1,48,4224]{2,1,0:T(8,128)(2,1)S(1)}, u32[]{:S(2)}, u32[]{:S(2)}) collective-permute-start(bf16[1,48,4224]{2,1,0:T(8,128)(2,1)S(1)} %get-tuple-element.12), channel_id=1, source_target_pairs={{0,2},{2,4},{4,6},{6,0},{1,3},{3,5},{5,7},{7,1},{8,10},{10,12},{12... | collective-permute-start | bytes 1216520 | tf_op jit(solution)/shard_map/ppermute | solution.py:15
  112.8 8.8 %collective-permute-done.16 = bf16[1,48,4224]{2,1,0:T(8,128)(2,1)S(1)} collective-permute-done((bf16[1,48,4224]{2,1,0:T(8,128)(2,1)S(1)}, bf16[1,48,4224]{2,1,0:T(8,128)(2,1)S(1)}, u32[]{:S(2)}, u32[]{:S(2)}) %collective-permute-start.16) | collective-permute-done | bytes 405536 | tf_op jit(solution)/shard_map/ppermute | solution.py:15
  121.6 23.6 %collective-permute-done.15 = bf16[1,48,4224]{2,1,0:T(8,128)(2,1)S(1)} collective-permute-done((bf16[1,48,4224]{2,1,0:T(8,128)(2,1)S(1)}, bf16[1,48,4224]{2,1,0:T(8,128)(2,1)S(1)}, u32[]{:S(2)}, u32[]{:S(2)}) %collective-permute-start.15) | collective-permute-done | bytes 405536 | tf_op jit(solution)/shard_map/ppermute | solution.py:15
  145.3 0.2 pad_maximum_fusion
  145.6 0.5 multiply_reduce_fusion.1
  146.2 2.6 %fusion.17 = f32[192,1536]{1,0:T(8,128)S(1)} fusion(bf16[192,4096]{1,0:T(8,128)(2,1)S(1)} %bitcast.250, bf16[1,1,4096,1536]{3,2,1,0:T(8,128)(2,1)S(1)} %bitcast.277, f32[192]{0:T(256)S(1)} %add_rsqrt_fusion.1), kind=kOutput, calls=%fused_computation.20 | convolution fusion | flops 2416214016 | bytes 15336192 | tf_op jit(solution)/shard_map/dot_general | solution.py:179
  148.8 0.5 slice.162
  150.0 0.6 multiply_reduce_fusion
  150.6 2.6 %fusion.20 = f32[192,1536]{1,0:T(8,128)S(1)} fusion(bf16[192,4096]{1,0:T(8,128)(2,1)S(1)} %bitcast.253, bf16[1,1,4096,1536]{3,2,1,0:T(8,128)(2,1)S(1)} %bitcast.277, f32[192]{0:T(256)S(1)} %add_rsqrt_fusion), kind=kOutput, calls=%fused_computation.21 | convolution fusion | flops 2416214016 | bytes 15336192 | tf_op jit(solution)/shard_map/dot_general | solution.py:179
  153.2 1.5 fusion.12
  154.7 0.6 collective-permute-start.18
  155.2 1.4 fusion.10
  156.9 1.4 collective-permute-done.18
  158.3 0.8 fusion.16
  159.2 1.5 collective-permute-start.19
  160.7 2.0 collective-permute-start.22
  162.7 1.9 collective-permute-start.21
  164.6 3.8 %collective-permute-start.20 = (bf16[1,48,4096]{2,1,0:T(8,128)(2,1)S(1)}, bf16[1,48,4096]{2,1,0:T(8,128)(2,1)S(1)}, u32[]{:S(2)}, u32[]{:S(2)}) collective-permute-start(bf16[1,48,4096]{2,1,0:T(8,128)(2,1)S(1)} %get-tuple-element.16), channel_id=1, source_target_pairs={{0,14},{2,8},{4,10},{6,12},{8,22},{10,16},{12,18},{14,20},{16,30},... | collective-permute-start | bytes 1179656 | tf_op jit(solution)/shard_map/ppermute | solution.py:215
  168.4 28.4 %collective-permute-done.19 = bf16[1,48,4096]{2,1,0:T(8,128)(2,1)S(1)} collective-permute-done((bf16[1,48,4096]{2,1,0:T(8,128)(2,1)S(1)}, bf16[1,48,4096]{2,1,0:T(8,128)(2,1)S(1)}, u32[]{:S(2)}, u32[]{:S(2)}) %collective-permute-start.19) | collective-permute-done | bytes 393248 | tf_op jit(solution)/shard_map/ppermute | solution.py:215
  196.8 1.5 fusion.15
  (89 shorter events, 3.2 us)
Async XLA Ops:
  0.0 12.3 %copy-start.4 = (s32[1,1,128,1]{2,3,1,0:T(1,128)S(1)}, s32[1,1,128,1]{2,3,1,0:T(1,128)}, u32[]{:S(2)}) copy-start(s32[1,1,128,1]{2,3,1,0:T(1,128)} %param.16) | copy-start | bytes 1540
  0.0 45.4 %collective-permute-start.5 = (bf16[1024,2048]{1,0:T(8,128)(2,1)}, bf16[1024,2048]{1,0:T(8,128)(2,1)}, u32[]{:S(2)}, u32[]{:S(2)}) collective-permute-start(bf16[1024,2048]{1,0:T(8,128)(2,1)} %bitcast.247), channel_id=1, source_target_pairs={{0,1},{1,0},{2,3},{3,2},{4,5},{5,4},{6,7},{7,6},{8,9},{9,8},{10,11... | collective-permute-start | bytes 12582920 | tf_op jit(solution)/shard_map/ppermute | solution.py:15
  0.5 12.3 %copy-start.5 = (f32[1,1,128,1]{2,3,1,0:T(1,128)S(1)}, f32[1,1,128,1]{2,3,1,0:T(1,128)}, u32[]{:S(2)}) copy-start(f32[1,1,128,1]{2,3,1,0:T(1,128)} %param.17) | copy-start | bytes 1540
  0.5 13.2 %copy-start.3 = (f32[1,4096]{1,0:T(1,128)S(1)}, f32[1,4096]{1,0:T(1,128)}, u32[]{:S(2)}) copy-start(f32[1,4096]{1,0:T(1,128)} %param.13) | copy-start | bytes 49156
  1.4 12.8 %collective-permute-start.2 = (bf16[128,256]{1,0:T(8,128)(2,1)S(1)}, bf16[128,256]{1,0:T(8,128)(2,1)S(1)}, u32[]{:S(2)}, u32[]{:S(2)}) collective-permute-start(bf16[128,256]{1,0:T(8,128)(2,1)S(1)} %pad_maximum_fusion.4), channel_id=1, source_target_pairs={{0,6},{2,0},{4,2},{6,4},{1,7},{3,1},{5,3},{7,5},{8,14},{10,8},{12,... | collective-permute-start | bytes 196616 | tf_op jit(solution)/shard_map/ppermute | solution.py:15
  6.3 7.9 %collective-permute-start = (bf16[128,256]{1,0:T(8,128)(2,1)S(1)}, bf16[128,256]{1,0:T(8,128)(2,1)S(1)}, u32[]{:S(2)}, u32[]{:S(2)}) collective-permute-start(bf16[128,256]{1,0:T(8,128)(2,1)S(1)} %pad_maximum_fusion.2), channel_id=1, source_target_pairs={{0,2},{2,4},{4,6},{6,0},{1,3},{3,5},{5,7},{7,1},{8,10},{10,12},{12... | collective-permute-start | bytes 196616 | tf_op jit(solution)/shard_map/ppermute | solution.py:15
  6.3 13.6 %collective-permute-start.1 = (bf16[128,256]{1,0:T(8,128)(2,1)S(1)}, bf16[128,256]{1,0:T(8,128)(2,1)S(1)}, u32[]{:S(2)}, u32[]{:S(2)}) collective-permute-start(bf16[128,256]{1,0:T(8,128)(2,1)S(1)} %pad_maximum_fusion.3), channel_id=1, source_target_pairs={{0,4},{2,6},{4,0},{6,2},{1,5},{3,7},{5,1},{7,3},{8,12},{10,14},{12... | collective-permute-start | bytes 196616 | tf_op jit(solution)/shard_map/ppermute | solution.py:15
  8.8 11.1 %collective-permute-start.3 = (bf16[128,1024]{0,1:T(8,128)(2,1)S(1)}, bf16[128,1024]{0,1:T(8,128)(2,1)S(1)}, u32[]{:S(2)}, u32[]{:S(2)}) collective-permute-start(bf16[128,1024]{0,1:T(8,128)(2,1)S(1)} %bitcast.266), channel_id=1, source_target_pairs={{0,2},{2,4},{4,6},{6,0},{1,3},{3,5},{5,7},{7,1},{8,10},{10,12},{12... | collective-permute-start | bytes 786440 | tf_op jit(solution)/shard_map/ppermute | solution.py:15
  19.9 70.0 %copy-start.2 = (bf16[512,256]{1,0:T(8,128)(2,1)}, bf16[512,256]{1,0:T(8,128)(2,1)S(1)}, u32[]{:S(2)}) copy-start(bf16[512,256]{1,0:T(8,128)(2,1)S(1)} %pad_maximum_fusion.1) | copy-start | bytes 786436
  19.9 24.2 %collective-permute-start.4 = (bf16[128,1024]{1,0:T(8,128)(2,1)S(1)}, bf16[128,1024]{1,0:T(8,128)(2,1)S(1)}, u32[]{:S(2)}, u32[]{:S(2)}) collective-permute-start(bf16[128,1024]{1,0:T(8,128)(2,1)S(1)} %get-tuple-element.7), channel_id=1, source_target_pairs={{0,4},{2,6},{4,0},{6,2},{1,5},{3,7},{5,1},{7,3},{8,12},{10,14},{12... | collective-permute-start | bytes 786440 | tf_op jit(solution)/shard_map/ppermute | solution.py:15
  26.2 30.7 %collective-permute-start.6 = (bf16[128,2048]{1,0:T(8,128)(2,1)S(1)}, bf16[128,2048]{1,0:T(8,128)(2,1)S(1)}, u32[]{:S(2)}, u32[]{:S(2)}) collective-permute-start(bf16[128,2048]{1,0:T(8,128)(2,1)S(1)} %fusion.99), channel_id=1, source_target_pairs={{0,2},{2,4},{4,6},{6,0},{1,3},{3,5},{5,7},{7,1},{8,10},{10,12},{12... | collective-permute-start | bytes 1572872 | tf_op jit(solution)/shard_map/ppermute | solution.py:15
  26.7 40.9 %collective-permute-start.9 = (bf16[128,1024]{0,1:T(8,128)(2,1)S(1)}, bf16[128,1024]{0,1:T(8,128)(2,1)}, u32[]{:S(2)}, u32[]{:S(2)}) collective-permute-start(bf16[128,1024]{0,1:T(8,128)(2,1)S(1)} %bitcast.267), channel_id=1, source_target_pairs={{0,6},{2,0},{4,2},{6,4},{1,7},{3,1},{5,3},{7,5},{8,14},{10,8},{12,... | collective-permute-start | bytes 786440 | tf_op jit(solution)/shard_map/ppermute | solution.py:15
  48.9 16.6 %collective-permute-start.7 = (bf16[128,2048]{1,0:T(8,128)(2,1)S(1)}, bf16[128,2048]{1,0:T(8,128)(2,1)S(1)}, u32[]{:S(2)}, u32[]{:S(2)}) collective-permute-start(bf16[128,2048]{1,0:T(8,128)(2,1)S(1)} %convolution_add_fusion.2), channel_id=1, source_target_pairs={{0,2},{2,4},{4,6},{6,0},{1,3},{3,5},{5,7},{7,1},{8,10},{10,12},{12... | collective-permute-start | bytes 1572872 | tf_op jit(solution)/shard_map/ppermute | solution.py:15
  57.5 19.3 %collective-permute-start.10 = (bf16[128,2048]{1,0:T(8,128)(2,1)S(1)}, bf16[128,2048]{1,0:T(8,128)(2,1)S(1)}, u32[]{:S(2)}, u32[]{:S(2)}) collective-permute-start(bf16[128,2048]{1,0:T(8,128)(2,1)S(1)} %add_convert_fusion.3), channel_id=1, source_target_pairs={{0,2},{2,4},{4,6},{6,0},{1,3},{3,5},{5,7},{7,1},{8,10},{10,12},{12... | collective-permute-start | bytes 1572872 | tf_op jit(solution)/shard_map/ppermute | solution.py:15
  66.2 21.8 %collective-permute-start.11 = (bf16[128,2048]{1,0:T(8,128)(2,1)S(1)}, bf16[128,2048]{1,0:T(8,128)(2,1)S(1)}, u32[]{:S(2)}, u32[]{:S(2)}) collective-permute-start(bf16[128,2048]{1,0:T(8,128)(2,1)S(1)} %add_convert_fusion.2), channel_id=1, source_target_pairs={{0,2},{2,4},{4,6},{6,0},{1,3},{3,5},{5,7},{7,1},{8,10},{10,12},{12... | collective-permute-start | bytes 1572872 | tf_op jit(solution)/shard_map/ppermute | solution.py:15
  77.4 22.1 %collective-permute-start.12 = (bf16[128,2048]{1,0:T(8,128)(2,1)S(1)}, bf16[128,2048]{1,0:T(8,128)(2,1)S(1)}, u32[]{:S(2)}, u32[]{:S(2)}) collective-permute-start(bf16[128,2048]{1,0:T(8,128)(2,1)S(1)} %add_convert_fusion.1), channel_id=1, source_target_pairs={{0,2},{2,4},{4,6},{6,0},{1,3},{3,5},{5,7},{7,1},{8,10},{10,12},{12... | collective-permute-start | bytes 1572872 | tf_op jit(solution)/shard_map/ppermute | solution.py:15
  77.4 4.7 %collective-permute-start.8 = (f32[1,128]{1,0:T(1,128)S(1)}, f32[1,128]{1,0:T(1,128)S(1)}, u32[]{:S(2)}, u32[]{:S(2)}) collective-permute-start(f32[1,128]{1,0:T(1,128)S(1)} %convert_add_fusion), channel_id=1, source_target_pairs={{0,8},{8,16},{16,24},{24,0},{1,9},{9,17},{17,25},{25,1},{2,10},{10... | collective-permute-start | bytes 1544 | tf_op jit(solution)/shard_map/ppermute | solution.py:15
  88.7 20.7 %collective-permute-start.13 = (bf16[128,2048]{1,0:T(8,128)(2,1)S(1)}, bf16[128,2048]{1,0:T(8,128)(2,1)S(1)}, u32[]{:S(2)}, u32[]{:S(2)}) collective-permute-start(bf16[128,2048]{1,0:T(8,128)(2,1)S(1)} %add_convert_fusion), channel_id=1, source_target_pairs={{0,2},{2,4},{4,6},{6,0},{1,3},{3,5},{5,7},{7,1},{8,10},{10,12},{12... | collective-permute-start | bytes 1572872 | tf_op jit(solution)/shard_map/ppermute | solution.py:15
  89.9 0.7 copy-start.1
  91.4 2.2 %copy-start = (bf16[1,1,128,4096]{3,2,1,0:T(8,128)(2,1)S(1)}, bf16[1,1,128,4096]{3,2,1,0:T(8,128)(2,1)}, u32[]{:S(2)}) copy-start(bf16[1,1,128,4096]{3,2,1,0:T(8,128)(2,1)} %param.11) | copy-start | bytes 3145732
  99.5 46.6 %slice-start = ((s8[12582912]{0:T(1024)(128)(4,1)}), s8[4194304]{0:T(1024)(128)(4,1)S(1)}, s32[]{:S(2)}) async-start(s8[12582912]{0:T(1024)(128)(4,1)} %bitcast.276), calls=%async_computation | async-start | bytes 8388608
  109.6 36.6 %slice-start.1 = ((s8[12582912]{0:T(1024)(128)(4,1)}), s8[4194304]{0:T(1024)(128)(4,1)S(1)}, s32[]{:S(2)}) async-start(s8[12582912]{0:T(1024)(128)(4,1)} %bitcast.276), calls=%async_computation.1 | async-start | bytes 8388608
  110.5 11.1 %collective-permute-start.16 = (bf16[1,48,4224]{2,1,0:T(8,128)(2,1)S(1)}, bf16[1,48,4224]{2,1,0:T(8,128)(2,1)S(1)}, u32[]{:S(2)}, u32[]{:S(2)}) collective-permute-start(bf16[1,48,4224]{2,1,0:T(8,128)(2,1)S(1)} %get-tuple-element.10), channel_id=1, source_target_pairs={{0,6},{2,0},{4,2},{6,4},{1,7},{3,1},{5,3},{7,5},{8,14},{10,8},{12,... | collective-permute-start | bytes 1216520 | tf_op jit(solution)/shard_map/ppermute | solution.py:15
  110.6 35.5 %slice-start.2 = ((s8[12582912]{0:T(1024)(128)(4,1)}), s8[4194304]{0:T(1024)(128)(4,1)S(1)}, s32[]{:S(2)}) async-start(s8[12582912]{0:T(1024)(128)(4,1)} %bitcast.276), calls=%async_computation.2 | async-start | bytes 8388608
  110.6 34.6 %collective-permute-start.15 = (bf16[1,48,4224]{2,1,0:T(8,128)(2,1)S(1)}, bf16[1,48,4224]{2,1,0:T(8,128)(2,1)S(1)}, u32[]{:S(2)}, u32[]{:S(2)}) collective-permute-start(bf16[1,48,4224]{2,1,0:T(8,128)(2,1)S(1)} %get-tuple-element.11), channel_id=1, source_target_pairs={{0,4},{2,6},{4,0},{6,2},{1,5},{3,7},{5,1},{7,3},{8,12},{10,14},{12... | collective-permute-start | bytes 1216520 | tf_op jit(solution)/shard_map/ppermute | solution.py:15
  110.7 34.5 %collective-permute-start.14 = (bf16[1,48,4224]{2,1,0:T(8,128)(2,1)S(1)}, bf16[1,48,4224]{2,1,0:T(8,128)(2,1)S(1)}, u32[]{:S(2)}, u32[]{:S(2)}) collective-permute-start(bf16[1,48,4224]{2,1,0:T(8,128)(2,1)S(1)} %get-tuple-element.12), channel_id=1, source_target_pairs={{0,2},{2,4},{4,6},{6,0},{1,3},{3,5},{5,7},{7,1},{8,10},{10,12},{12... | collective-permute-start | bytes 1216520 | tf_op jit(solution)/shard_map/ppermute | solution.py:15
  145.5 4.4 %collective-permute-start.17 = (bf16[4,48,4096]{2,1,0:T(8,128)(2,1)S(1)}, bf16[4,48,4096]{2,1,0:T(8,128)(2,1)S(1)}, u32[]{:S(2)}, u32[]{:S(2)}) collective-permute-start(bf16[4,48,4096]{2,1,0:T(8,128)(2,1)S(1)} %bitcast.248), channel_id=1, source_target_pairs={{0,1},{1,0},{2,3},{3,2},{4,5},{5,4},{6,7},{7,6},{8,9},{9,8},{10,11... | collective-permute-start | bytes 4718600 | tf_op jit(solution)/shard_map/ppermute | solution.py:15
  146.1 7.0 %slice-start.3 = ((s8[6291456]{0:T(1024)(128)(4,1)}), s8[4194304]{0:T(1024)(128)(4,1)S(1)}, s32[]{:S(2)}) async-start(s8[6291456]{0:T(1024)(128)(4,1)} %bitcast.278), calls=%async_computation.3 | async-start | bytes 8388608
  150.0 3.2 %slice-start.4 = ((s8[6291456]{0:T(1024)(128)(4,1)}), s8[2097152]{0:T(1024)(128)(4,1)S(1)}, s32[]{:S(2)}) async-start(s8[6291456]{0:T(1024)(128)(4,1)} %bitcast.278), calls=%async_computation.4 | async-start | bytes 4194304
  154.7 3.6 %collective-permute-start.18 = (bf16[4,48,4096]{2,1,0:T(8,128)(2,1)S(1)}, bf16[4,48,4096]{2,1,0:T(8,128)(2,1)S(1)}, u32[]{:S(2)}, u32[]{:S(2)}) collective-permute-start(bf16[4,48,4096]{2,1,0:T(8,128)(2,1)S(1)} %bitcast.280), channel_id=1, source_target_pairs={{0,1},{1,0},{2,3},{3,2},{4,5},{5,4},{6,7},{7,6},{8,9},{9,8},{10,11... | collective-permute-start | bytes 4718600 | tf_op jit(solution)/shard_map/ppermute | solution.py:15
  159.2 37.6 %collective-permute-start.19 = (bf16[1,48,4096]{2,1,0:T(8,128)(2,1)S(1)}, bf16[1,48,4096]{2,1,0:T(8,128)(2,1)S(1)}, u32[]{:S(2)}, u32[]{:S(2)}) collective-permute-start(bf16[1,48,4096]{2,1,0:T(8,128)(2,1)S(1)} %get-tuple-element.13), channel_id=1, source_target_pairs={{0,8},{2,10},{4,12},{6,14},{8,16},{10,18},{12,20},{14,22},{16,24},... | collective-permute-start | bytes 1179656 | tf_op jit(solution)/shard_map/ppermute | solution.py:215
  160.7 36.1 %collective-permute-start.22 = (bf16[1,48,4096]{2,1,0:T(8,128)(2,1)S(1)}, bf16[1,48,4096]{2,1,0:T(8,128)(2,1)S(1)}, u32[]{:S(2)}, u32[]{:S(2)}) collective-permute-start(bf16[1,48,4096]{2,1,0:T(8,128)(2,1)S(1)} %get-tuple-element.14), channel_id=1, source_target_pairs={{0,10},{2,12},{4,14},{6,8},{8,18},{10,20},{12,22},{14,16},{16,26},... | collective-permute-start | bytes 1179656 | tf_op jit(solution)/shard_map/ppermute | solution.py:215
  162.7 34.1 %collective-permute-start.21 = (bf16[1,48,4096]{2,1,0:T(8,128)(2,1)S(1)}, bf16[1,48,4096]{2,1,0:T(8,128)(2,1)S(1)}, u32[]{:S(2)}, u32[]{:S(2)}) collective-permute-start(bf16[1,48,4096]{2,1,0:T(8,128)(2,1)S(1)} %get-tuple-element.15), channel_id=1, source_target_pairs={{0,12},{2,14},{4,8},{6,10},{8,20},{10,22},{12,16},{14,18},{16,28},... | collective-permute-start | bytes 1179656 | tf_op jit(solution)/shard_map/ppermute | solution.py:215
  164.6 32.2 %collective-permute-start.20 = (bf16[1,48,4096]{2,1,0:T(8,128)(2,1)S(1)}, bf16[1,48,4096]{2,1,0:T(8,128)(2,1)S(1)}, u32[]{:S(2)}, u32[]{:S(2)}) collective-permute-start(bf16[1,48,4096]{2,1,0:T(8,128)(2,1)S(1)} %get-tuple-element.16), channel_id=1, source_target_pairs={{0,14},{2,8},{4,10},{6,12},{8,22},{10,16},{12,18},{14,20},{16,30},... | collective-permute-start | bytes 1179656 | tf_op jit(solution)/shard_map/ppermute | solution.py:215

commit v14 on v13

--- a/solution.py
+++ b/solution.py
@@ -172,38 +172,29 @@
 
     hidden_width = down_weight.shape[2]
 
-    def gate_and_up(rows, behind):
+    def gate_and_up(rows, behind=None):
         rows = lax.optimization_barrier(rows.reshape(-1, model_width))
-        unscaled = rows.astype(jnp.float32) * inverse_gain + behind
+        unscaled = rows.astype(jnp.float32) * inverse_gain
+        if behind is not None:
+            lead = behind.shape[0]
+            behind = jnp.pad(behind * 0.0, ((0, 0), (0, model_width - behind.shape[1])))
+            unscaled = jnp.concatenate([unscaled[:lead] + behind, unscaled[lead:]], axis=0)
         mean_square = jnp.mean(unscaled * unscaled, axis=-1, keepdims=True)
         gate_up = jnp.dot(rows, in_weight[0, 0], preferred_element_type=jnp.float32)
         return gate_up * lax.rsqrt(mean_square + 1e-06)
 
-    def down_part(gate_up):
+    def down_part(gate_up, columns):
         hidden = (jax.nn.silu(gate_up[:, :hidden_width]) * gate_up[:, hidden_width:]).astype(
             jnp.bfloat16
         )
-        return jnp.dot(hidden, down_weight[0, 0], preferred_element_type=jnp.float32)
+        return jnp.dot(hidden, down_weight[0, 0, :, columns], preferred_element_type=jnp.float32)
 
     others = [
         shift(wanted_by(arrived, (my_exp + k) % exps), "exp", k) for k in range(1, exps)
     ]
-    own_gate_up = lax.optimization_barrier(gate_and_up(wanted_by(arrived, my_exp), 0.0))
-    other_gate_up = gate_and_up(jnp.concatenate(others, axis=0), own_gate_up[0, 0] * 0.0)
-    other_parts = down_part(other_gate_up).astype(jnp.bfloat16)
-    own_part = lax.optimization_barrier(down_part(own_gate_up))
-    own_part = own_part.reshape(contexts, capacity, model_width)
-    other_parts = other_parts.reshape(exps - 1, contexts, capacity, model_width)
-    sums = [0.0] * per_context
-    for k in range(exps):
-        back = shift(other_parts[k - 1], "exp", -k).astype(jnp.float32) if k else own_part
-        if per_context == 1:
-            sums[0] = sums[0] + back
-        else:
-            place = (my_exp + k) % exps // group_size
-            sums = [s + jnp.where(place == i, back, 0.0) for i, s in enumerate(sums)]
-    finished = arrived.astype(jnp.float32) * inverse_gain + weights * jnp.stack(sums, axis=1)
-    finished = finished.astype(jnp.bfloat16)
+    own_gate_up = lax.optimization_barrier(gate_and_up(wanted_by(arrived, my_exp)))
+    other_gate_up = gate_and_up(jnp.concatenate(others, axis=0), own_gate_up)
+    other_gate_up = lax.optimization_barrier(other_gate_up)
 
     def to_next_owner(rows, k):
         pipes = lax.axis_size("pipe")
@@ -214,11 +205,29 @@
         ]
         return lax.ppermute(rows, ("pipe", "ctx"), pairs)
 
-    returned = [to_next_owner(finished[k], k).reshape(-1, model_width) for k in range(contexts)]
     next_match = (slot_ids[None, :] == next_slots[:, None]).astype(jnp.bfloat16)
-    returned = jnp.concatenate(returned, axis=0)
-    layer = jnp.dot(next_match, returned, preferred_element_type=jnp.float32)
-    return layer.astype(jnp.bfloat16).reshape(1, 1, token_rows, model_width)
+    half = model_width // 2
+    halves = []
+    for columns in (slice(0, half), slice(half, model_width)):
+        other_parts = down_part(other_gate_up, columns).astype(jnp.bfloat16)
+        other_parts = other_parts.reshape(exps - 1, contexts, capacity, half)
+        own_part = lax.optimization_barrier(down_part(own_gate_up, columns))
+        own_part = own_part.reshape(contexts, capacity, half)
+        sums = [0.0] * per_context
+        for k in range(exps):
+            back = shift(other_parts[k - 1], "exp", -k).astype(jnp.float32) if k else own_part
+            if per_context == 1:
+                sums[0] = sums[0] + back
+            else:
+                place = (my_exp + k) % exps // group_size
+                sums = [s + jnp.where(place == i, back, 0.0) for i, s in enumerate(sums)]
+        mixed = arrived[..., columns].astype(jnp.float32) * inverse_gain[columns]
+        finished = (mixed + weights * jnp.stack(sums, axis=1)).astype(jnp.bfloat16)
+        returned = [to_next_owner(finished[k], k).reshape(-1, half) for k in range(contexts)]
+        returned = jnp.concatenate(returned, axis=0)
+        layer = jnp.dot(next_match, returned, preferred_element_type=jnp.float32)
+        halves.append(layer.astype(jnp.bfloat16))
+    return jnp.concatenate(halves, axis=1).reshape(1, 1, token_rows, model_width)
 
 
 def solution(mesh):

time: 201 us -> 200 us (level)
  waiting for transfers between devices: 104 us -> 92.7 us
  starting transfers between devices: 28.4 us -> 37.9 us
  other arithmetic: 5.76 us -> 8.38 us
    ppermute x4 -> x8, starting transfers between devices: 9.2 us -> 18.6 us  [to_next_owner(): return lax.ppermute(rows, ('pipe', 'ctx'), pairs)]
    ppermute x4 -> x8, waiting for transfers between devices: 28.4 us -> 19.9 us  [to_next_owner(): return lax.ppermute(rows, ('pipe', 'ctx'), pairs)]
    ppermute x19 -> x20, waiting for transfers between devices: 76 us -> 72.9 us  [shift(): lax.ppermute(value, axis, [(i, (i + by) % devices) for i in range(devices)])]
    ppermute x19 -> x20, starting transfers between devices: 19.2 us -> 19.3 us  [shift(): lax.ppermute(value, axis, [(i, (i + by) % devices) for i in range(devices)])]
  transfers between devices with their start and end apart: 23 -> 28, of which waited for: 10 -> 11; matrix products, arithmetic and copies ran while one was open for 25% -> 27% of each run, Pallas kernels for 0% -> 0%
where the time goes in v14:
time: 200 us; the launch traced here: 199 us
  waiting for transfers between devices  92.7 us (46%)
  matrix products  46.1 us (23%)
  starting transfers between devices  37.9 us (19%)
  local copies, waits for them, and re-layouts  8.47 us (4%)
  other arithmetic  8.38 us (4%)
  between operations  5.37 us (3%)
    ppermute x20, waiting for transfers between devices, shift(): lax.ppermute(value, axis, [(i, (i + by) % devices) for i in range(devices)])  72.9 us
    dot_general x8, matrix products, mixed_halves(): term = jnp.dot(attended, weights[half], preferred_element_type=jnp.float32)  23.4 us
    ppermute x8, waiting for transfers between devices, to_next_owner(): return lax.ppermute(rows, ('pipe', 'ctx'), pairs)  19.9 us
    ppermute x20, starting transfers between devices, shift(): lax.ppermute(value, axis, [(i, (i + by) % devices) for i in range(devices)])  19.3 us
    ppermute x8, starting transfers between devices, to_next_owner(): return lax.ppermute(rows, ('pipe', 'ctx'), pairs)  18.6 us
    dot_general x4, matrix products, attend_block(): jnp.einsum('hqk,kd->qhd', attention_weights, value_rows, preferred_elemen...  7 us
    sub x4, matrix products, attend_block(): attention_weights = jax.nn.softmax(scores, axis=-1).astype(jnp.bfloat16)  5.94 us
    dot_general x2, matrix products, gate_and_up(): gate_up = jnp.dot(rows, in_weight[0, 0], preferred_element_type=jnp.float32)  5.22 us
  transfers between devices with their start and end apart: 28, of which 11 were waited for; matrix products, arithmetic and copies ran while one was open for 27% of the time, Pallas kernels for 0%

profile of v14, /device:TPU:0, one launch (start us, length us, event | category | flops | bytes accessed | tf_op | source)
XLA Modules:
  0.0 198.9 jit_solution(10285862522839980015)
XLA Ops:
  0.5 1.0 dynamic-slice_bitcast_fusion.8
  1.4 4.8 %collective-permute-start.2 = (bf16[128,256]{1,0:T(8,128)(2,1)S(1)}, bf16[128,256]{1,0:T(8,128)(2,1)S(1)}, u32[]{:S(2)}, u32[]{:S(2)}) collective-permute-start(bf16[128,256]{1,0:T(8,128)(2,1)S(1)} %pad_maximum_fusion.4), channel_id=1, source_target_pairs={{0,6},{2,0},{4,2},{6,4},{1,7},{3,1},{5,3},{7,5},{8,14},{10,8},{12,... | collective-permute-start | bytes 196616 | tf_op jit(solution)/shard_map/ppermute | solution.py:15
  6.3 1.1 collective-permute-start.1
  7.4 1.3 dynamic-slice_bitcast_fusion
  8.8 3.4 %collective-permute-start.3 = (bf16[128,1024]{0,1:T(8,128)(2,1)S(1)}, bf16[128,1024]{0,1:T(8,128)(2,1)S(1)}, u32[]{:S(2)}, u32[]{:S(2)}) collective-permute-start(bf16[128,1024]{0,1:T(8,128)(2,1)S(1)} %bitcast.301), channel_id=1, source_target_pairs={{0,2},{2,4},{4,6},{6,0},{1,3},{3,5},{5,7},{7,1},{8,10},{10,12},{12... | collective-permute-start | bytes 786440 | tf_op jit(solution)/shard_map/ppermute | solution.py:15
  12.8 0.9 broadcast_compare_fusion.2
  13.7 0.6 fusion.103
  14.8 5.1 %collective-permute-done.1 = bf16[128,256]{1,0:T(8,128)(2,1)S(1)} collective-permute-done((bf16[128,256]{1,0:T(8,128)(2,1)S(1)}, bf16[128,256]{1,0:T(8,128)(2,1)S(1)}, u32[]{:S(2)}, u32[]{:S(2)}) %collective-permute-start.1) | collective-permute-done | bytes 65568 | tf_op jit(solution)/shard_map/ppermute | solution.py:15
  19.9 0.9 collective-permute-start.4
  20.9 0.8 fusion.131
  21.7 1.0 convolution_convert_fusion.6
  22.7 2.9 %fusion.115 = bf16[128,2048]{1,0:T(8,128)(2,1)S(1)} fusion(bf16[128,1024]{0,1:T(8,128)(2,1)S(1)} %bitcast.289, bf16[1,1024,2048]{2,1,0:T(8,128)(2,1)} %param.12), kind=kOutput, calls=%fused_computation.208 | convolution fusion | flops 536870912 | bytes 4980736 | tf_op jit(solution)/shard_map/dot_general | solution.py:92
  25.6 0.6 slice.181
  26.7 3.3 %collective-permute-start.9 = (bf16[128,1024]{0,1:T(8,128)(2,1)S(1)}, bf16[128,1024]{0,1:T(8,128)(2,1)}, u32[]{:S(2)}, u32[]{:S(2)}) collective-permute-start(bf16[128,1024]{0,1:T(8,128)(2,1)S(1)} %bitcast.302), channel_id=1, source_target_pairs={{0,6},{2,0},{4,2},{6,4},{1,7},{3,1},{5,3},{7,5},{8,14},{10,8},{12,... | collective-permute-start | bytes 786440 | tf_op jit(solution)/shard_map/ppermute | solution.py:15
  30.0 14.1 %collective-permute-done.4 = bf16[128,1024]{1,0:T(8,128)(2,1)S(1)} collective-permute-done((bf16[128,1024]{1,0:T(8,128)(2,1)S(1)}, bf16[128,1024]{1,0:T(8,128)(2,1)S(1)}, u32[]{:S(2)}, u32[]{:S(2)}) %collective-permute-start.4) | collective-permute-done | bytes 262176 | tf_op jit(solution)/shard_map/ppermute | solution.py:15
  44.1 0.6 slice.182
  45.3 2.9 %convolution_add_fusion.2 = bf16[128,2048]{1,0:T(8,128)(2,1)S(1)} fusion(bf16[128,1024]{0,1:T(8,128)(2,1)S(1)} %bitcast.290, bf16[1024,2048]{1,0:T(8,128)(2,1)} %collective-permute-done.5, f32[]{:T(128)} %bitcast.22), kind=kOutput, calls=%fused_computation.29 | convolution fusion | flops 537395200 | bytes 4980740 | tf_op jit(solution)/shard_map/dot_general | solution.py:92
  48.3 0.6 slice.183
  50.3 2.2 %fusion.132 = f32[8,128]{1,0:T(8,128)} fusion(pred[128,512]{0,1:T(8,128)(4,1)} %get-tuple-element.37, bf16[128,8,128]{0,2,1:T(8,128)(2,1)S(1)} %bitcast.303, bf16[512,256]{1,0:T(8,128)(2,1)S(1)} %pad_maximum_fusion.1), kind=kOutput, calls=%fused_computation.221 | convolution fusion | flops 136315392 | bytes 462848 | tf_op jit(solution)/shard_map/sub | solution.py:27
  52.5 1.9 convolution_convert_fusion.5
  54.4 2.9 %fusion.113 = f32[128,2048]{1,0:T(8,128)S(1)} fusion(bf16[128,1024]{0,1:T(8,128)(2,1)S(1)} %bitcast.295, bf16[1,1024,2048]{2,1,0:T(8,128)(2,1)} %param.12), kind=kOutput, calls=%fused_computation.206 | convolution fusion | flops 536870912 | bytes 5505024 | tf_op jit(solution)/shard_map/dot_general | solution.py:92
  57.5 0.5 slice.184
  58.1 2.9 %fusion.135 = f32[128,2048]{1,0:T(8,128)S(1)} fusion(bf16[128,1024]{0,1:T(8,128)(2,1)S(1)} %bitcast.296, bf16[1024,2048]{1,0:T(8,128)(2,1)} %collective-permute-done.5), kind=kOutput, calls=%fused_computation.224 | convolution fusion | flops 536870912 | bytes 5505024 | tf_op jit(solution)/shard_map/dot_general | solution.py:92
  61.1 4.4 %collective-permute-done.7 = bf16[128,2048]{1,0:T(8,128)(2,1)S(1)} collective-permute-done((bf16[128,2048]{1,0:T(8,128)(2,1)S(1)}, bf16[128,2048]{1,0:T(8,128)(2,1)S(1)}, u32[]{:S(2)}, u32[]{:S(2)}) %collective-permute-start.7) | collective-permute-done | bytes 524320 | tf_op jit(solution)/shard_map/ppermute | solution.py:15
  65.6 0.6 slice.185
  67.5 1.0 broadcast_add_fusion.1
  68.5 1.6 fusion.133
  70.1 1.9 convolution_convert_fusion.4
  72.0 2.9 %fusion.111 = f32[128,2048]{1,0:T(8,128)S(1)} fusion(bf16[128,1024]{0,1:T(8,128)(2,1)S(1)} %bitcast.293, bf16[1,1024,2048]{2,1,0:T(8,128)(2,1)} %param.12), kind=kOutput, calls=%fused_computation.204 | convolution fusion | flops 536870912 | bytes 5505024 | tf_op jit(solution)/shard_map/dot_general | solution.py:92
  74.9 1.7 collective-permute-done.10
  76.8 0.6 slice.186
  77.4 1.7 collective-permute-start.8
  79.1 2.9 %fusion.136 = f32[128,2048]{1,0:T(8,128)S(1)} fusion(bf16[128,1024]{0,1:T(8,128)(2,1)S(1)} %bitcast.294, bf16[1024,2048]{1,0:T(8,128)(2,1)} %collective-permute-done.5), kind=kOutput, calls=%fused_computation.225 | convolution fusion | flops 536870912 | bytes 5505024 | tf_op jit(solution)/shard_map/dot_general | solution.py:92
  82.1 0.5 convert_bitcast_fusion
  82.6 5.3 %collective-permute-done.11 = bf16[128,2048]{1,0:T(8,128)(2,1)S(1)} collective-permute-done((bf16[128,2048]{1,0:T(8,128)(2,1)S(1)}, bf16[128,2048]{1,0:T(8,128)(2,1)S(1)}, u32[]{:S(2)}, u32[]{:S(2)}) %collective-permute-start.11) | collective-permute-done | bytes 524320 | tf_op jit(solution)/shard_map/ppermute | solution.py:15
  88.0 0.5 slice.187
  89.9 0.7 copy-done.1
  90.6 1.4 fusion.134
  91.9 2.2 %convolution_convert_fusion.3 = bf16[128,8,128]{2,0,1:T(8,128)(2,1)S(1)} fusion(f32[8,128]{1,0:T(8,128)} %fusion.134, bf16[512,256]{1,0:T(8,128)(2,1)} %copy-done.2, pred[128,512]{0,1:T(8,128)(4,1)S(1)} %get-tuple-element.35, bf16[128,8,128]{0,2,1:T(8,128)(2,1)} %bitcast.298), kind=kOutput, calls=%fused_computation.58 | convolution fusion | flops 271189504 | bytes 856064 | tf_op jit(solution)/shard_map/hqk,kd->qhd/dot_general | solution.py:28
  94.2 2.9 %convolution_add_fusion.1 = f32[128,2048]{1,0:T(8,128)S(1)} fusion(bf16[128,1024]{0,1:T(8,128)(2,1)S(1)} %bitcast.291, bf16[1,1,128,4096]{3,2,1,0:T(8,128)(2,1)S(1)} %copy-done, s32[]{:T(128)S(6)} %select_n.179, bf16[1,1024,2048]{2,1,0:T(8,128)(2,1)} %param.12), kind=kOutput, calls=%fused_computation.28 | convolution fusion | flops 537395200 | bytes 6029316 | tf_op jit(solution)/shard_map/dot_general | solution.py:92
  97.1 2.9 %convolution_add_fusion = f32[128,2048]{1,0:T(8,128)S(1)} fusion(bf16[128,1024]{0,1:T(8,128)(2,1)S(1)} %bitcast.292, bf16[1024,2048]{1,0:T(8,128)(2,1)} %collective-permute-done.5, bf16[1,1,128,4096]{3,2,1,0:T(8,128)(2,1)S(1)} %copy-done, s32[]{:T(128)S(6)} %select_n.180), kind=kOutput, calls=%fused_computation.27 | convolution fusion | flops 537395200 | bytes 6029316 | tf_op jit(solution)/shard_map/dot_general | solution.py:92
  100.2 9.1 %collective-permute-done.13 = bf16[128,2048]{1,0:T(8,128)(2,1)S(1)} collective-permute-done((bf16[128,2048]{1,0:T(8,128)(2,1)S(1)}, bf16[128,2048]{1,0:T(8,128)(2,1)S(1)}, u32[]{:S(2)}, u32[]{:S(2)}) %collective-permute-start.13) | collective-permute-done | bytes 524320 | tf_op jit(solution)/shard_map/ppermute | solution.py:15
  110.1 0.6 convolution_convert_fusion
  111.0 2.0 %collective-permute-start.14 = (bf16[1,48,4224]{2,1,0:T(8,128)(2,1)S(1)}, bf16[1,48,4224]{2,1,0:T(8,128)(2,1)S(1)}, u32[]{:S(2)}, u32[]{:S(2)}) collective-permute-start(bf16[1,48,4224]{2,1,0:T(8,128)(2,1)S(1)} %get-tuple-element.12), channel_id=1, source_target_pairs={{0,2},{2,4},{4,6},{6,0},{1,3},{3,5},{5,7},{7,1},{8,10},{10,12},{12... | collective-permute-start | bytes 1216520 | tf_op jit(solution)/shard_map/ppermute | solution.py:15
  113.1 8.8 %collective-permute-done.16 = bf16[1,48,4224]{2,1,0:T(8,128)(2,1)S(1)} collective-permute-done((bf16[1,48,4224]{2,1,0:T(8,128)(2,1)S(1)}, bf16[1,48,4224]{2,1,0:T(8,128)(2,1)S(1)}, u32[]{:S(2)}, u32[]{:S(2)}) %collective-permute-start.16) | collective-permute-done | bytes 405536 | tf_op jit(solution)/shard_map/ppermute | solution.py:15
  121.9 23.6 %collective-permute-done.15 = bf16[1,48,4224]{2,1,0:T(8,128)(2,1)S(1)} collective-permute-done((bf16[1,48,4224]{2,1,0:T(8,128)(2,1)S(1)}, bf16[1,48,4224]{2,1,0:T(8,128)(2,1)S(1)}, u32[]{:S(2)}, u32[]{:S(2)}) %collective-permute-start.15) | collective-permute-done | bytes 405536 | tf_op jit(solution)/shard_map/ppermute | solution.py:15
  146.5 2.6 %fusion.20 = f32[192,1536]{1,0:T(8,128)S(1)} fusion(bf16[192,4096]{1,0:T(8,128)(2,1)S(1)} %bitcast.282, bf16[1,1,4096,1536]{3,2,1,0:T(8,128)(2,1)S(1)} %bitcast.312, f32[192]{0:T(256)S(1)} %add_rsqrt_fusion.1), kind=kOutput, calls=%fused_computation.23 | convolution fusion | flops 2416214016 | bytes 15336192 | tf_op jit(solution)/shard_map/dot_general | solution.py:183
  149.3 0.8 fusion.10
  150.1 0.8 fusion.14
  151.1 0.6 multiply_reduce_fusion
  151.6 2.6 %fusion.23 = f32[192,1536]{1,0:T(8,128)S(1)} fusion(bf16[192,4096]{1,0:T(8,128)(2,1)S(1)} %bitcast.288, bf16[1,1,4096,1536]{3,2,1,0:T(8,128)(2,1)S(1)} %bitcast.312, f32[192]{0:T(256)S(1)} %add_rsqrt_fusion), kind=kOutput, calls=%fused_computation.24 | convolution fusion | flops 2416214016 | bytes 15336192 | tf_op jit(solution)/shard_map/dot_general | solution.py:183
  154.4 0.8 fusion.26
  155.2 0.5 collective-permute-start.18
  156.0 0.8 fusion.29
  156.9 0.8 collective-permute-done.18
  158.1 2.0 %collective-permute-start.22 = (bf16[1,48,2048]{2,1,0:T(8,128)(2,1)S(1)}, bf16[1,48,2048]{2,1,0:T(8,128)(2,1)S(1)}, u32[]{:S(2)}, u32[]{:S(2)}) collective-permute-start(bf16[1,48,2048]{2,1,0:T(8,128)(2,1)S(1)} %slice_bitcast_fusion.12), channel_id=1, source_target_pairs={{0,10},{2,12},{4,14},{6,8},{8,18},{10,20},{12,22},{14,16},{16,26},... | collective-permute-start | bytes 589832 | tf_op jit(solution)/shard_map/ppermute | solution.py:206
  160.2 1.5 collective-permute-start.19
  161.7 1.9 collective-permute-start.21
  163.7 3.8 %collective-permute-start.20 = (bf16[1,48,2048]{2,1,0:T(8,128)(2,1)S(1)}, bf16[1,48,2048]{2,1,0:T(8,128)(2,1)S(1)}, u32[]{:S(2)}, u32[]{:S(2)}) collective-permute-start(bf16[1,48,2048]{2,1,0:T(8,128)(2,1)S(1)} %get-tuple-element.19), channel_id=1, source_target_pairs={{0,14},{2,8},{4,10},{6,12},{8,22},{10,16},{12,18},{14,20},{16,30},... | collective-permute-start | bytes 589832 | tf_op jit(solution)/shard_map/ppermute | solution.py:206
  167.9 1.5 collective-permute-start.24
  169.4 7.8 %collective-permute-start.27 = (bf16[1,48,2048]{2,1,0:T(8,128)(2,1)S(1)}, bf16[1,48,2048]{2,1,0:T(8,128)(2,1)S(1)}, u32[]{:S(2)}, u32[]{:S(2)}) collective-permute-start(bf16[1,48,2048]{2,1,0:T(8,128)(2,1)S(1)} %get-tuple-element.21), channel_id=1, source_target_pairs={{0,10},{2,12},{4,14},{6,8},{8,18},{10,20},{12,22},{14,16},{16,26},... | collective-permute-start | bytes 589832 | tf_op jit(solution)/shard_map/ppermute | solution.py:206
  177.3 8.5 %collective-permute-done.19 = bf16[1,48,2048]{2,1,0:T(8,128)(2,1)S(1)} collective-permute-done((bf16[1,48,2048]{2,1,0:T(8,128)(2,1)S(1)}, bf16[1,48,2048]{2,1,0:T(8,128)(2,1)S(1)}, u32[]{:S(2)}, u32[]{:S(2)}) %collective-permute-start.19) | collective-permute-done | bytes 196640 | tf_op jit(solution)/shard_map/ppermute | solution.py:206
  186.1 11.4 %collective-permute-done.24 = bf16[1,48,2048]{2,1,0:T(8,128)(2,1)S(1)} collective-permute-done((bf16[1,48,2048]{2,1,0:T(8,128)(2,1)S(1)}, bf16[1,48,2048]{2,1,0:T(8,128)(2,1)S(1)}, u32[]{:S(2)}, u32[]{:S(2)}) %collective-permute-start.24) | collective-permute-done | bytes 196640 | tf_op jit(solution)/shard_map/ppermute | solution.py:206
  197.9 1.1 maximum_bitcast_fusion
  (119 shorter events, 7.7 us)
Async XLA Ops:
  0.0 12.3 %copy-start.4 = (s32[1,1,128,1]{2,3,1,0:T(1,128)S(1)}, s32[1,1,128,1]{2,3,1,0:T(1,128)}, u32[]{:S(2)}) copy-start(s32[1,1,128,1]{2,3,1,0:T(1,128)} %param.16) | copy-start | bytes 1540
  0.0 45.3 %collective-permute-start.5 = (bf16[1024,2048]{1,0:T(8,128)(2,1)}, bf16[1024,2048]{1,0:T(8,128)(2,1)}, u32[]{:S(2)}, u32[]{:S(2)}) collective-permute-start(bf16[1024,2048]{1,0:T(8,128)(2,1)} %bitcast.279), channel_id=1, source_target_pairs={{0,1},{1,0},{2,3},{3,2},{4,5},{5,4},{6,7},{7,6},{8,9},{9,8},{10,11... | collective-permute-start | bytes 12582920 | tf_op jit(solution)/shard_map/ppermute | solution.py:15
  0.5 12.3 %copy-start.9 = (f32[1,1,128,1]{2,3,1,0:T(1,128)S(1)}, f32[1,1,128,1]{2,3,1,0:T(1,128)}, u32[]{:S(2)}) copy-start(f32[1,1,128,1]{2,3,1,0:T(1,128)} %param.17) | copy-start | bytes 1540
  0.5 12.3 %copy-start.3 = (f32[1,4096]{1,0:T(1,128)S(1)}, f32[1,4096]{1,0:T(1,128)}, u32[]{:S(2)}) copy-start(f32[1,4096]{1,0:T(1,128)} %param.13) | copy-start | bytes 49156
  1.4 13.4 %collective-permute-start.2 = (bf16[128,256]{1,0:T(8,128)(2,1)S(1)}, bf16[128,256]{1,0:T(8,128)(2,1)S(1)}, u32[]{:S(2)}, u32[]{:S(2)}) collective-permute-start(bf16[128,256]{1,0:T(8,128)(2,1)S(1)} %pad_maximum_fusion.4), channel_id=1, source_target_pairs={{0,6},{2,0},{4,2},{6,4},{1,7},{3,1},{5,3},{7,5},{8,14},{10,8},{12,... | collective-permute-start | bytes 196616 | tf_op jit(solution)/shard_map/ppermute | solution.py:15
  6.3 8.6 %collective-permute-start = (bf16[128,256]{1,0:T(8,128)(2,1)S(1)}, bf16[128,256]{1,0:T(8,128)(2,1)S(1)}, u32[]{:S(2)}, u32[]{:S(2)}) collective-permute-start(bf16[128,256]{1,0:T(8,128)(2,1)S(1)} %pad_maximum_fusion.2), channel_id=1, source_target_pairs={{0,2},{2,4},{4,6},{6,0},{1,3},{3,5},{5,7},{7,1},{8,10},{10,12},{12... | collective-permute-start | bytes 196616 | tf_op jit(solution)/shard_map/ppermute | solution.py:15
  6.3 13.6 %collective-permute-start.1 = (bf16[128,256]{1,0:T(8,128)(2,1)S(1)}, bf16[128,256]{1,0:T(8,128)(2,1)S(1)}, u32[]{:S(2)}, u32[]{:S(2)}) collective-permute-start(bf16[128,256]{1,0:T(8,128)(2,1)S(1)} %pad_maximum_fusion.3), channel_id=1, source_target_pairs={{0,4},{2,6},{4,0},{6,2},{1,5},{3,7},{5,1},{7,3},{8,12},{10,14},{12... | collective-permute-start | bytes 196616 | tf_op jit(solution)/shard_map/ppermute | solution.py:15
  8.8 11.1 %collective-permute-start.3 = (bf16[128,1024]{0,1:T(8,128)(2,1)S(1)}, bf16[128,1024]{0,1:T(8,128)(2,1)S(1)}, u32[]{:S(2)}, u32[]{:S(2)}) collective-permute-start(bf16[128,1024]{0,1:T(8,128)(2,1)S(1)} %bitcast.301), channel_id=1, source_target_pairs={{0,2},{2,4},{4,6},{6,0},{1,3},{3,5},{5,7},{7,1},{8,10},{10,12},{12... | collective-permute-start | bytes 786440 | tf_op jit(solution)/shard_map/ppermute | solution.py:15
  12.8 8.9 %copy-start.6 = (s32[128]{0:T(128)}, s32[128]{0:T(128)S(1)}, u32[]{:S(2)}) copy-start(s32[128]{0:T(128)S(1)} %select_reduce_fusion) | copy-start | bytes 1540
  19.9 70.0 %copy-start.2 = (bf16[512,256]{1,0:T(8,128)(2,1)}, bf16[512,256]{1,0:T(8,128)(2,1)S(1)}, u32[]{:S(2)}) copy-start(bf16[512,256]{1,0:T(8,128)(2,1)S(1)} %pad_maximum_fusion.1) | copy-start | bytes 786436
  19.9 24.2 %collective-permute-start.4 = (bf16[128,1024]{1,0:T(8,128)(2,1)S(1)}, bf16[128,1024]{1,0:T(8,128)(2,1)S(1)}, u32[]{:S(2)}, u32[]{:S(2)}) collective-permute-start(bf16[128,1024]{1,0:T(8,128)(2,1)S(1)} %get-tuple-element.7), channel_id=1, source_target_pairs={{0,4},{2,6},{4,0},{6,2},{1,5},{3,7},{5,1},{7,3},{8,12},{10,14},{12... | collective-permute-start | bytes 786440 | tf_op jit(solution)/shard_map/ppermute | solution.py:15
  26.2 31.1 %collective-permute-start.6 = (bf16[128,2048]{1,0:T(8,128)(2,1)S(1)}, bf16[128,2048]{1,0:T(8,128)(2,1)S(1)}, u32[]{:S(2)}, u32[]{:S(2)}) collective-permute-start(bf16[128,2048]{1,0:T(8,128)(2,1)S(1)} %fusion.115), channel_id=1, source_target_pairs={{0,2},{2,4},{4,6},{6,0},{1,3},{3,5},{5,7},{7,1},{8,10},{10,12},{12... | collective-permute-start | bytes 1572872 | tf_op jit(solution)/shard_map/ppermute | solution.py:15
  26.7 40.7 %collective-permute-start.9 = (bf16[128,1024]{0,1:T(8,128)(2,1)S(1)}, bf16[128,1024]{0,1:T(8,128)(2,1)}, u32[]{:S(2)}, u32[]{:S(2)}) collective-permute-start(bf16[128,1024]{0,1:T(8,128)(2,1)S(1)} %bitcast.302), channel_id=1, source_target_pairs={{0,6},{2,0},{4,2},{6,4},{1,7},{3,1},{5,3},{7,5},{8,14},{10,8},{12,... | collective-permute-start | bytes 786440 | tf_op jit(solution)/shard_map/ppermute | solution.py:15
  48.8 16.6 %collective-permute-start.7 = (bf16[128,2048]{1,0:T(8,128)(2,1)S(1)}, bf16[128,2048]{1,0:T(8,128)(2,1)S(1)}, u32[]{:S(2)}, u32[]{:S(2)}) collective-permute-start(bf16[128,2048]{1,0:T(8,128)(2,1)S(1)} %convolution_add_fusion.2), channel_id=1, source_target_pairs={{0,2},{2,4},{4,6},{6,0},{1,3},{3,5},{5,7},{7,1},{8,10},{10,12},{12... | collective-permute-start | bytes 1572872 | tf_op jit(solution)/shard_map/ppermute | solution.py:15
  58.0 18.6 %collective-permute-start.10 = (bf16[128,2048]{1,0:T(8,128)(2,1)S(1)}, bf16[128,2048]{1,0:T(8,128)(2,1)S(1)}, u32[]{:S(2)}, u32[]{:S(2)}) collective-permute-start(bf16[128,2048]{1,0:T(8,128)(2,1)S(1)} %add_convert_fusion.3), channel_id=1, source_target_pairs={{0,2},{2,4},{4,6},{6,0},{1,3},{3,5},{5,7},{7,1},{8,10},{10,12},{12... | collective-permute-start | bytes 1572872 | tf_op jit(solution)/shard_map/ppermute | solution.py:15
  66.1 21.8 %collective-permute-start.11 = (bf16[128,2048]{1,0:T(8,128)(2,1)S(1)}, bf16[128,2048]{1,0:T(8,128)(2,1)S(1)}, u32[]{:S(2)}, u32[]{:S(2)}) collective-permute-start(bf16[128,2048]{1,0:T(8,128)(2,1)S(1)} %add_convert_fusion.2), channel_id=1, source_target_pairs={{0,2},{2,4},{4,6},{6,0},{1,3},{3,5},{5,7},{7,1},{8,10},{10,12},{12... | collective-permute-start | bytes 1572872 | tf_op jit(solution)/shard_map/ppermute | solution.py:15
  74.9 2.5 %copy-start.5 = (s32[1,1,128,1]{2,3,1,0:T(1,128)S(1)}, s32[1,1,128,1]{2,3,1,0:T(1,128)}, u32[]{:S(2)}) copy-start(s32[1,1,128,1]{2,3,1,0:T(1,128)} %param.16) | copy-start | bytes 1540
  74.9 2.5 %copy-start.7 = (s32[128]{0:T(128)S(1)}, s32[128]{0:T(128)}, u32[]{:S(2)}) copy-start(s32[128]{0:T(128)} %copy-done.6) | copy-start | bytes 1540
  77.4 22.7 %collective-permute-start.12 = (bf16[128,2048]{1,0:T(8,128)(2,1)S(1)}, bf16[128,2048]{1,0:T(8,128)(2,1)S(1)}, u32[]{:S(2)}, u32[]{:S(2)}) collective-permute-start(bf16[128,2048]{1,0:T(8,128)(2,1)S(1)} %add_convert_fusion.1), channel_id=1, source_target_pairs={{0,2},{2,4},{4,6},{6,0},{1,3},{3,5},{5,7},{7,1},{8,10},{10,12},{12... | collective-permute-start | bytes 1572872 | tf_op jit(solution)/shard_map/ppermute | solution.py:15
  77.4 4.7 %collective-permute-start.8 = (f32[1,128]{1,0:T(1,128)S(1)}, f32[1,128]{1,0:T(1,128)S(1)}, u32[]{:S(2)}, u32[]{:S(2)}) collective-permute-start(f32[1,128]{1,0:T(1,128)S(1)} %convert_add_fusion), channel_id=1, source_target_pairs={{0,8},{8,16},{16,24},{24,0},{1,9},{9,17},{17,25},{25,1},{2,10},{10... | collective-permute-start | bytes 1544 | tf_op jit(solution)/shard_map/ppermute | solution.py:15
  88.6 20.8 %collective-permute-start.13 = (bf16[128,2048]{1,0:T(8,128)(2,1)S(1)}, bf16[128,2048]{1,0:T(8,128)(2,1)S(1)}, u32[]{:S(2)}, u32[]{:S(2)}) collective-permute-start(bf16[128,2048]{1,0:T(8,128)(2,1)S(1)} %add_convert_fusion), channel_id=1, source_target_pairs={{0,2},{2,4},{4,6},{6,0},{1,3},{3,5},{5,7},{7,1},{8,10},{10,12},{12... | collective-permute-start | bytes 1572872 | tf_op jit(solution)/shard_map/ppermute | solution.py:15
  89.9 0.7 copy-start.1
  91.9 2.2 %copy-start = (bf16[1,1,128,4096]{3,2,1,0:T(8,128)(2,1)S(1)}, bf16[1,1,128,4096]{3,2,1,0:T(8,128)(2,1)}, u32[]{:S(2)}) copy-start(bf16[1,1,128,4096]{3,2,1,0:T(8,128)(2,1)} %param.11) | copy-start | bytes 3145732
  100.1 46.4 %slice-start = ((s8[12582912]{0:T(1024)(128)(4,1)}), s8[4194304]{0:T(1024)(128)(4,1)S(1)}, s32[]{:S(2)}) async-start(s8[12582912]{0:T(1024)(128)(4,1)} %bitcast.311), calls=%async_computation | async-start | bytes 8388608
  109.5 0.7 copy-start.8
  109.5 37.0 %slice-start.1 = ((s8[12582912]{0:T(1024)(128)(4,1)}), s8[4194304]{0:T(1024)(128)(4,1)S(1)}, s32[]{:S(2)}) async-start(s8[12582912]{0:T(1024)(128)(4,1)} %bitcast.311), calls=%async_computation.1 | async-start | bytes 8388608
  110.8 11.1 %collective-permute-start.16 = (bf16[1,48,4224]{2,1,0:T(8,128)(2,1)S(1)}, bf16[1,48,4224]{2,1,0:T(8,128)(2,1)S(1)}, u32[]{:S(2)}, u32[]{:S(2)}) collective-permute-start(bf16[1,48,4224]{2,1,0:T(8,128)(2,1)S(1)} %get-tuple-element.10), channel_id=1, source_target_pairs={{0,6},{2,0},{4,2},{6,4},{1,7},{3,1},{5,3},{7,5},{8,14},{10,8},{12,... | collective-permute-start | bytes 1216520 | tf_op jit(solution)/shard_map/ppermute | solution.py:15
  110.9 35.6 %slice-start.2 = ((s8[12582912]{0:T(1024)(128)(4,1)}), s8[4194304]{0:T(1024)(128)(4,1)S(1)}, s32[]{:S(2)}) async-start(s8[12582912]{0:T(1024)(128)(4,1)} %bitcast.311), calls=%async_computation.2 | async-start | bytes 8388608
  111.0 34.6 %collective-permute-start.15 = (bf16[1,48,4224]{2,1,0:T(8,128)(2,1)S(1)}, bf16[1,48,4224]{2,1,0:T(8,128)(2,1)S(1)}, u32[]{:S(2)}, u32[]{:S(2)}) collective-permute-start(bf16[1,48,4224]{2,1,0:T(8,128)(2,1)S(1)} %get-tuple-element.11), channel_id=1, source_target_pairs={{0,4},{2,6},{4,0},{6,2},{1,5},{3,7},{5,1},{7,3},{8,12},{10,14},{12... | collective-permute-start | bytes 1216520 | tf_op jit(solution)/shard_map/ppermute | solution.py:15
  111.0 34.6 %collective-permute-start.14 = (bf16[1,48,4224]{2,1,0:T(8,128)(2,1)S(1)}, bf16[1,48,4224]{2,1,0:T(8,128)(2,1)S(1)}, u32[]{:S(2)}, u32[]{:S(2)}) collective-permute-start(bf16[1,48,4224]{2,1,0:T(8,128)(2,1)S(1)} %get-tuple-element.12), channel_id=1, source_target_pairs={{0,2},{2,4},{4,6},{6,0},{1,3},{3,5},{5,7},{7,1},{8,10},{10,12},{12... | collective-permute-start | bytes 1216520 | tf_op jit(solution)/shard_map/ppermute | solution.py:15
  146.3 2.9 %slice-start.3 = ((s8[6291456]{0:T(1024)(128)(4,1)}), s8[4194304]{0:T(1024)(128)(4,1)S(1)}, s32[]{:S(2)}) async-start(s8[6291456]{0:T(1024)(128)(4,1)} %bitcast.313), calls=%async_computation.3 | async-start | bytes 8388608
  146.4 2.9 %slice-start.4 = ((s8[6291456]{0:T(1024)(128)(4,1)}), s8[2097152]{0:T(1024)(128)(4,1)S(1)}, s32[]{:S(2)}) async-start(s8[6291456]{0:T(1024)(128)(4,1)} %bitcast.313), calls=%async_computation.4 | async-start | bytes 4194304
  146.4 4.7 %collective-permute-start.17 = (bf16[4,48,4096]{2,1,0:T(8,128)(2,1)S(1)}, bf16[4,48,4096]{2,1,0:T(8,128)(2,1)S(1)}, u32[]{:S(2)}, u32[]{:S(2)}) collective-permute-start(bf16[4,48,4096]{2,1,0:T(8,128)(2,1)S(1)} %bitcast.281), channel_id=1, source_target_pairs={{0,1},{1,0},{2,3},{3,2},{4,5},{5,4},{6,7},{7,6},{8,9},{9,8},{10,11... | collective-permute-start | bytes 4718600 | tf_op jit(solution)/shard_map/ppermute | solution.py:15
  155.2 2.4 %collective-permute-start.18 = (bf16[4,48,2048]{2,1,0:T(8,128)(2,1)S(1)}, bf16[4,48,2048]{2,1,0:T(8,128)(2,1)S(1)}, u32[]{:S(2)}, u32[]{:S(2)}) collective-permute-start(bf16[4,48,2048]{2,1,0:T(8,128)(2,1)S(1)} %bitcast.316), channel_id=1, source_target_pairs={{0,1},{1,0},{2,3},{3,2},{4,5},{5,4},{6,7},{7,6},{8,9},{9,8},{10,11... | collective-permute-start | bytes 2359304 | tf_op jit(solution)/shard_map/ppermute | solution.py:15
  156.8 10.6 %collective-permute-start.23 = (bf16[4,48,2048]{2,1,0:T(8,128)(2,1)S(1)}, bf16[4,48,2048]{2,1,0:T(8,128)(2,1)S(1)}, u32[]{:S(2)}, u32[]{:S(2)}) collective-permute-start(bf16[4,48,2048]{2,1,0:T(8,128)(2,1)S(1)} %bitcast.315), channel_id=1, source_target_pairs={{0,1},{1,0},{2,3},{3,2},{4,5},{5,4},{6,7},{7,6},{8,9},{9,8},{10,11... | collective-permute-start | bytes 2359304 | tf_op jit(solution)/shard_map/ppermute | solution.py:15
  158.1 11.3 %collective-permute-start.22 = (bf16[1,48,2048]{2,1,0:T(8,128)(2,1)S(1)}, bf16[1,48,2048]{2,1,0:T(8,128)(2,1)S(1)}, u32[]{:S(2)}, u32[]{:S(2)}) collective-permute-start(bf16[1,48,2048]{2,1,0:T(8,128)(2,1)S(1)} %slice_bitcast_fusion.12), channel_id=1, source_target_pairs={{0,10},{2,12},{4,14},{6,8},{8,18},{10,20},{12,22},{14,16},{16,26},... | collective-permute-start | bytes 589832 | tf_op jit(solution)/shard_map/ppermute | solution.py:206
  160.2 25.6 %collective-permute-start.19 = (bf16[1,48,2048]{2,1,0:T(8,128)(2,1)S(1)}, bf16[1,48,2048]{2,1,0:T(8,128)(2,1)S(1)}, u32[]{:S(2)}, u32[]{:S(2)}) collective-permute-start(bf16[1,48,2048]{2,1,0:T(8,128)(2,1)S(1)} %get-tuple-element.17), channel_id=1, source_target_pairs={{0,8},{2,10},{4,12},{6,14},{8,16},{10,18},{12,20},{14,22},{16,24},... | collective-permute-start | bytes 589832 | tf_op jit(solution)/shard_map/ppermute | solution.py:206
  161.7 24.0 %collective-permute-start.21 = (bf16[1,48,2048]{2,1,0:T(8,128)(2,1)S(1)}, bf16[1,48,2048]{2,1,0:T(8,128)(2,1)S(1)}, u32[]{:S(2)}, u32[]{:S(2)}) collective-permute-start(bf16[1,48,2048]{2,1,0:T(8,128)(2,1)S(1)} %get-tuple-element.18), channel_id=1, source_target_pairs={{0,12},{2,14},{4,8},{6,10},{8,20},{10,22},{12,16},{14,18},{16,28},... | collective-permute-start | bytes 589832 | tf_op jit(solution)/shard_map/ppermute | solution.py:206
  163.7 22.1 %collective-permute-start.20 = (bf16[1,48,2048]{2,1,0:T(8,128)(2,1)S(1)}, bf16[1,48,2048]{2,1,0:T(8,128)(2,1)S(1)}, u32[]{:S(2)}, u32[]{:S(2)}) collective-permute-start(bf16[1,48,2048]{2,1,0:T(8,128)(2,1)S(1)} %get-tuple-element.19), channel_id=1, source_target_pairs={{0,14},{2,8},{4,10},{6,12},{8,22},{10,16},{12,18},{14,20},{16,30},... | collective-permute-start | bytes 589832 | tf_op jit(solution)/shard_map/ppermute | solution.py:206
  167.4 18.4 %copy-start.10 = (s32[128]{0:T(128)S(1)}, s32[128]{0:T(128)}, u32[]{:S(2)}) copy-start(s32[128]{0:T(128)} %convert_bitcast_fusion) | copy-start | bytes 1540
  167.9 29.6 %collective-permute-start.24 = (bf16[1,48,2048]{2,1,0:T(8,128)(2,1)S(1)}, bf16[1,48,2048]{2,1,0:T(8,128)(2,1)S(1)}, u32[]{:S(2)}, u32[]{:S(2)}) collective-permute-start(bf16[1,48,2048]{2,1,0:T(8,128)(2,1)S(1)} %get-tuple-element.20), channel_id=1, source_target_pairs={{0,8},{2,10},{4,12},{6,14},{8,16},{10,18},{12,20},{14,22},{16,24},... | collective-permute-start | bytes 589832 | tf_op jit(solution)/shard_map/ppermute | solution.py:206
  169.4 28.1 %collective-permute-start.27 = (bf16[1,48,2048]{2,1,0:T(8,128)(2,1)S(1)}, bf16[1,48,2048]{2,1,0:T(8,128)(2,1)S(1)}, u32[]{:S(2)}, u32[]{:S(2)}) collective-permute-start(bf16[1,48,2048]{2,1,0:T(8,128)(2,1)S(1)} %get-tuple-element.21), channel_id=1, source_target_pairs={{0,10},{2,12},{4,14},{6,8},{8,18},{10,20},{12,22},{14,16},{16,26},... | collective-permute-start | bytes 589832 | tf_op jit(solution)/shard_map/ppermute | solution.py:206
  185.7 11.8 %collective-permute-start.26 = (bf16[1,48,2048]{2,1,0:T(8,128)(2,1)S(1)}, bf16[1,48,2048]{2,1,0:T(8,128)(2,1)S(1)}, u32[]{:S(2)}, u32[]{:S(2)}) collective-permute-start(bf16[1,48,2048]{2,1,0:T(8,128)(2,1)S(1)} %get-tuple-element.22), channel_id=1, source_target_pairs={{0,12},{2,14},{4,8},{6,10},{8,20},{10,22},{12,16},{14,18},{16,28},... | collective-permute-start | bytes 589832 | tf_op jit(solution)/shard_map/ppermute | solution.py:206
  185.8 11.8 %collective-permute-start.25 = (bf16[1,48,2048]{2,1,0:T(8,128)(2,1)S(1)}, bf16[1,48,2048]{2,1,0:T(8,128)(2,1)S(1)}, u32[]{:S(2)}, u32[]{:S(2)}) collective-permute-start(bf16[1,48,2048]{2,1,0:T(8,128)(2,1)S(1)} %get-tuple-element.23), channel_id=1, source_target_pairs={{0,14},{2,8},{4,10},{6,12},{8,22},{10,16},{12,18},{14,20},{16,30},... | collective-permute-start | bytes 589832 | tf_op jit(solution)/shard_map/ppermute | solution.py:206

commit v15 on v14

--- a/solution.py
+++ b/solution.py
@@ -207,7 +207,7 @@
 
     next_match = (slot_ids[None, :] == next_slots[:, None]).astype(jnp.bfloat16)
     half = model_width // 2
-    halves = []
+    returned = []
     for columns in (slice(0, half), slice(half, model_width)):
         other_parts = down_part(other_gate_up, columns).astype(jnp.bfloat16)
         other_parts = other_parts.reshape(exps - 1, contexts, capacity, half)
@@ -223,11 +223,13 @@
                 sums = [s + jnp.where(place == i, back, 0.0) for i, s in enumerate(sums)]
         mixed = arrived[..., columns].astype(jnp.float32) * inverse_gain[columns]
         finished = (mixed + weights * jnp.stack(sums, axis=1)).astype(jnp.bfloat16)
-        returned = [to_next_owner(finished[k], k).reshape(-1, half) for k in range(contexts)]
-        returned = jnp.concatenate(returned, axis=0)
-        layer = jnp.dot(next_match, returned, preferred_element_type=jnp.float32)
-        halves.append(layer.astype(jnp.bfloat16))
-    return jnp.concatenate(halves, axis=1).reshape(1, 1, token_rows, model_width)
+        returned.append([to_next_owner(finished[k], k) for k in range(contexts)])
+    returned = jnp.concatenate(
+        [jnp.concatenate(pair, axis=-1).reshape(-1, model_width) for pair in zip(*returned)], axis=0
+    )
+    returned = lax.optimization_barrier(returned)
+    layer = jnp.dot(next_match, returned, preferred_element_type=jnp.float32)
+    return layer.astype(jnp.bfloat16).reshape(1, 1, token_rows, model_width)
 
 
 def solution(mesh):

time: 200 us -> 206 us (1.030)
  starting transfers between devices: 37.9 us -> 43 us
    ppermute x8, starting transfers between devices: 18.6 us -> 23.7 us  [to_next_owner(): return lax.ppermute(rows, ('pipe', 'ctx'), pairs)]
    ppermute x20, waiting for transfers between devices: 72.9 us -> 75.9 us  [shift(): lax.ppermute(value, axis, [(i, (i + by) % devices) for i in range(devices)])]
  transfers between devices with their start and end apart: 28 -> 28, of which waited for: 11 -> 13; matrix products, arithmetic and copies ran while one was open for 27% -> 25% of each run, Pallas kernels for 0% -> 0%
where the time goes in v15:
time: 206 us; the launch traced here: 205 us
  waiting for transfers between devices  94.2 us (46%)
  matrix products  47 us (23%)
  starting transfers between devices  43 us (21%)
  local copies, waits for them, and re-layouts  8.15 us (4%)
  other arithmetic  7.2 us (3%)
  between operations  5.06 us (2%)
    ppermute x20, waiting for transfers between devices, shift(): lax.ppermute(value, axis, [(i, (i + by) % devices) for i in range(devices)])  75.9 us
    ppermute x8, starting transfers between devices, to_next_owner(): return lax.ppermute(rows, ('pipe', 'ctx'), pairs)  23.7 us
    dot_general x8, matrix products, mixed_halves(): term = jnp.dot(attended, weights[half], preferred_element_type=jnp.float32)  23.5 us
    ppermute x20, starting transfers between devices, shift(): lax.ppermute(value, axis, [(i, (i + by) % devices) for i in range(devices)])  19.3 us
    ppermute x8, waiting for transfers between devices, to_next_owner(): return lax.ppermute(rows, ('pipe', 'ctx'), pairs)  18.3 us
    dot_general x4, matrix products, attend_block(): jnp.einsum('hqk,kd->qhd', attention_weights, value_rows, preferred_elemen...  7 us
    sub x4, matrix products, attend_block(): attention_weights = jax.nn.softmax(scores, axis=-1).astype(jnp.bfloat16)  5.94 us
    dot_general x2, matrix products, gate_and_up(): gate_up = jnp.dot(rows, in_weight[0, 0], preferred_element_type=jnp.float32)  5.31 us
  transfers between devices with their start and end apart: 28, of which 13 were waited for; matrix products, arithmetic and copies ran while one was open for 25% of the time, Pallas kernels for 0%

profile of v15, /device:TPU:0, one launch (start us, length us, event | category | flops | bytes accessed | tf_op | source)
XLA Modules:
  0.0 204.5 jit_solution(1458982387728593323)
XLA Ops:
  0.5 1.0 dynamic-slice_bitcast_fusion.8
  1.4 4.8 %collective-permute-start.2 = (bf16[128,256]{1,0:T(8,128)(2,1)S(1)}, bf16[128,256]{1,0:T(8,128)(2,1)S(1)}, u32[]{:S(2)}, u32[]{:S(2)}) collective-permute-start(bf16[128,256]{1,0:T(8,128)(2,1)S(1)} %pad_maximum_fusion.5), channel_id=1, source_target_pairs={{0,6},{2,0},{4,2},{6,4},{1,7},{3,1},{5,3},{7,5},{8,14},{10,8},{12,... | collective-permute-start | bytes 196616 | tf_op jit(solution)/shard_map/ppermute | solution.py:15
  6.3 1.1 collective-permute-start.1
  7.4 1.3 dynamic-slice_bitcast_fusion
  8.8 3.4 %collective-permute-start.3 = (bf16[128,1024]{0,1:T(8,128)(2,1)S(1)}, bf16[128,1024]{0,1:T(8,128)(2,1)S(1)}, u32[]{:S(2)}, u32[]{:S(2)}) collective-permute-start(bf16[128,1024]{0,1:T(8,128)(2,1)S(1)} %bitcast.298), channel_id=1, source_target_pairs={{0,2},{2,4},{4,6},{6,0},{1,3},{3,5},{5,7},{7,1},{8,10},{10,12},{12... | collective-permute-start | bytes 786440 | tf_op jit(solution)/shard_map/ppermute | solution.py:15
  12.8 0.9 broadcast_compare_fusion.2
  13.7 0.6 fusion.89
  14.8 5.1 %collective-permute-done.1 = bf16[128,256]{1,0:T(8,128)(2,1)S(1)} collective-permute-done((bf16[128,256]{1,0:T(8,128)(2,1)S(1)}, bf16[128,256]{1,0:T(8,128)(2,1)S(1)}, u32[]{:S(2)}, u32[]{:S(2)}) %collective-permute-start.1) | collective-permute-done | bytes 65568 | tf_op jit(solution)/shard_map/ppermute | solution.py:15
  19.9 0.9 collective-permute-start.4
  20.9 0.8 fusion.115
  21.7 1.0 convolution_convert_fusion.5
  22.7 2.9 %fusion.99 = bf16[128,2048]{1,0:T(8,128)(2,1)S(1)} fusion(bf16[128,1024]{0,1:T(8,128)(2,1)S(1)} %bitcast.286, bf16[1,1024,2048]{2,1,0:T(8,128)(2,1)} %param.12), kind=kOutput, calls=%fused_computation.195 | convolution fusion | flops 536870912 | bytes 4980736 | tf_op jit(solution)/shard_map/dot_general | solution.py:92
  26.7 3.3 %collective-permute-start.9 = (bf16[128,1024]{0,1:T(8,128)(2,1)S(1)}, bf16[128,1024]{0,1:T(8,128)(2,1)}, u32[]{:S(2)}, u32[]{:S(2)}) collective-permute-start(bf16[128,1024]{0,1:T(8,128)(2,1)S(1)} %bitcast.299), channel_id=1, source_target_pairs={{0,6},{2,0},{4,2},{6,4},{1,7},{3,1},{5,3},{7,5},{8,14},{10,8},{12,... | collective-permute-start | bytes 786440 | tf_op jit(solution)/shard_map/ppermute | solution.py:15
  30.0 14.1 %collective-permute-done.4 = bf16[128,1024]{1,0:T(8,128)(2,1)S(1)} collective-permute-done((bf16[128,1024]{1,0:T(8,128)(2,1)S(1)}, bf16[128,1024]{1,0:T(8,128)(2,1)S(1)}, u32[]{:S(2)}, u32[]{:S(2)}) %collective-permute-start.4) | collective-permute-done | bytes 262176 | tf_op jit(solution)/shard_map/ppermute | solution.py:15
  44.1 0.5 slice.182
  45.3 2.9 %convolution_add_fusion.2 = bf16[128,2048]{1,0:T(8,128)(2,1)S(1)} fusion(bf16[128,1024]{0,1:T(8,128)(2,1)S(1)} %bitcast.287, bf16[1024,2048]{1,0:T(8,128)(2,1)} %collective-permute-done.5, f32[]{:T(128)} %bitcast.22), kind=kOutput, calls=%fused_computation.31 | convolution fusion | flops 537395200 | bytes 4980740 | tf_op jit(solution)/shard_map/dot_general | solution.py:92
  48.2 0.5 slice.183
  50.2 2.2 %fusion.116 = f32[8,128]{1,0:T(8,128)} fusion(pred[128,512]{0,1:T(8,128)(4,1)} %get-tuple-element.40, bf16[128,8,128]{0,2,1:T(8,128)(2,1)S(1)} %bitcast.300, bf16[512,256]{1,0:T(8,128)(2,1)S(1)} %pad_maximum_fusion.2), kind=kOutput, calls=%fused_computation.208 | convolution fusion | flops 136315392 | bytes 462848 | tf_op jit(solution)/shard_map/sub | solution.py:27
  52.4 1.9 convolution_convert_fusion.4
  54.3 2.9 %fusion.97 = f32[128,2048]{1,0:T(8,128)S(1)} fusion(bf16[128,1024]{0,1:T(8,128)(2,1)S(1)} %bitcast.292, bf16[1,1024,2048]{2,1,0:T(8,128)(2,1)} %param.12), kind=kOutput, calls=%fused_computation.193 | convolution fusion | flops 536870912 | bytes 5505024 | tf_op jit(solution)/shard_map/dot_general | solution.py:92
  58.0 2.9 %fusion.119 = f32[128,2048]{1,0:T(8,128)S(1)} fusion(bf16[128,1024]{0,1:T(8,128)(2,1)S(1)} %bitcast.293, bf16[1024,2048]{1,0:T(8,128)(2,1)} %collective-permute-done.5), kind=kOutput, calls=%fused_computation.211 | convolution fusion | flops 536870912 | bytes 5505024 | tf_op jit(solution)/shard_map/dot_general | solution.py:92
  60.9 4.5 %collective-permute-done.7 = bf16[128,2048]{1,0:T(8,128)(2,1)S(1)} collective-permute-done((bf16[128,2048]{1,0:T(8,128)(2,1)S(1)}, bf16[128,2048]{1,0:T(8,128)(2,1)S(1)}, u32[]{:S(2)}, u32[]{:S(2)}) %collective-permute-start.7) | collective-permute-done | bytes 524320 | tf_op jit(solution)/shard_map/ppermute | solution.py:15
  67.1 1.0 broadcast_add_fusion.1
  68.1 1.6 fusion.117
  69.7 1.9 convolution_convert_fusion.3
  71.6 2.9 %fusion.95 = f32[128,2048]{1,0:T(8,128)S(1)} fusion(bf16[128,1024]{0,1:T(8,128)(2,1)S(1)} %bitcast.290, bf16[1,1024,2048]{2,1,0:T(8,128)(2,1)} %param.12), kind=kOutput, calls=%fused_computation.191 | convolution fusion | flops 536870912 | bytes 5505024 | tf_op jit(solution)/shard_map/dot_general | solution.py:92
  74.6 2.1 %collective-permute-done.10 = bf16[128,2048]{1,0:T(8,128)(2,1)S(1)} collective-permute-done((bf16[128,2048]{1,0:T(8,128)(2,1)S(1)}, bf16[128,2048]{1,0:T(8,128)(2,1)S(1)}, u32[]{:S(2)}, u32[]{:S(2)}) %collective-permute-start.10) | collective-permute-done | bytes 524320 | tf_op jit(solution)/shard_map/ppermute | solution.py:15
  76.7 0.6 slice.186
  77.4 1.7 collective-permute-start.8
  79.1 2.9 %fusion.120 = f32[128,2048]{1,0:T(8,128)S(1)} fusion(bf16[128,1024]{0,1:T(8,128)(2,1)S(1)} %bitcast.291, bf16[1024,2048]{1,0:T(8,128)(2,1)} %collective-permute-done.5), kind=kOutput, calls=%fused_computation.212 | convolution fusion | flops 536870912 | bytes 5505024 | tf_op jit(solution)/shard_map/dot_general | solution.py:92
  82.1 5.8 %collective-permute-done.11 = bf16[128,2048]{1,0:T(8,128)(2,1)S(1)} collective-permute-done((bf16[128,2048]{1,0:T(8,128)(2,1)S(1)}, bf16[128,2048]{1,0:T(8,128)(2,1)S(1)}, u32[]{:S(2)}, u32[]{:S(2)}) %collective-permute-start.11) | collective-permute-done | bytes 524320 | tf_op jit(solution)/shard_map/ppermute | solution.py:15
  89.8 0.7 copy-done.1
  90.5 1.4 fusion.118
  91.8 2.2 %convolution_convert_fusion.2 = bf16[128,8,128]{2,0,1:T(8,128)(2,1)S(1)} fusion(f32[8,128]{1,0:T(8,128)} %fusion.118, bf16[512,256]{1,0:T(8,128)(2,1)} %copy-done.2, pred[128,512]{0,1:T(8,128)(4,1)S(1)} %get-tuple-element.38, bf16[128,8,128]{0,2,1:T(8,128)(2,1)} %bitcast.295), kind=kOutput, calls=%fused_computation.59 | convolution fusion | flops 271189504 | bytes 856064 | tf_op jit(solution)/shard_map/hqk,kd->qhd/dot_general | solution.py:28
  94.1 2.9 %convolution_add_fusion.1 = f32[128,2048]{1,0:T(8,128)S(1)} fusion(bf16[128,1024]{0,1:T(8,128)(2,1)S(1)} %bitcast.288, bf16[1,1,128,4096]{3,2,1,0:T(8,128)(2,1)S(1)} %copy-done, s32[]{:T(128)S(6)} %select_n.179, bf16[1,1024,2048]{2,1,0:T(8,128)(2,1)} %param.12), kind=kOutput, calls=%fused_computation.30 | convolution fusion | flops 537395200 | bytes 6029316 | tf_op jit(solution)/shard_map/dot_general | solution.py:92
  97.0 2.9 %convolution_add_fusion = f32[128,2048]{1,0:T(8,128)S(1)} fusion(bf16[128,1024]{0,1:T(8,128)(2,1)S(1)} %bitcast.289, bf16[1024,2048]{1,0:T(8,128)(2,1)} %collective-permute-done.5, bf16[1,1,128,4096]{3,2,1,0:T(8,128)(2,1)S(1)} %copy-done, s32[]{:T(128)S(6)} %select_n.180), kind=kOutput, calls=%fused_computation.29 | convolution fusion | flops 537395200 | bytes 6029316 | tf_op jit(solution)/shard_map/dot_general | solution.py:92
  100.1 9.1 %collective-permute-done.13 = bf16[128,2048]{1,0:T(8,128)(2,1)S(1)} collective-permute-done((bf16[128,2048]{1,0:T(8,128)(2,1)S(1)}, bf16[128,2048]{1,0:T(8,128)(2,1)S(1)}, u32[]{:S(2)}, u32[]{:S(2)}) %collective-permute-start.13) | collective-permute-done | bytes 524320 | tf_op jit(solution)/shard_map/ppermute | solution.py:15
  110.1 0.6 convolution_convert_fusion
  111.0 2.0 %collective-permute-start.14 = (bf16[1,48,4224]{2,1,0:T(8,128)(2,1)S(1)}, bf16[1,48,4224]{2,1,0:T(8,128)(2,1)S(1)}, u32[]{:S(2)}, u32[]{:S(2)}) collective-permute-start(bf16[1,48,4224]{2,1,0:T(8,128)(2,1)S(1)} %get-tuple-element.12), channel_id=1, source_target_pairs={{0,2},{2,4},{4,6},{6,0},{1,3},{3,5},{5,7},{7,1},{8,10},{10,12},{12... | collective-permute-start | bytes 1216520 | tf_op jit(solution)/shard_map/ppermute | solution.py:15
  113.0 8.8 %collective-permute-done.16 = bf16[1,48,4224]{2,1,0:T(8,128)(2,1)S(1)} collective-permute-done((bf16[1,48,4224]{2,1,0:T(8,128)(2,1)S(1)}, bf16[1,48,4224]{2,1,0:T(8,128)(2,1)S(1)}, u32[]{:S(2)}, u32[]{:S(2)}) %collective-permute-start.16) | collective-permute-done | bytes 405536 | tf_op jit(solution)/shard_map/ppermute | solution.py:15
  121.9 23.6 %collective-permute-done.15 = bf16[1,48,4224]{2,1,0:T(8,128)(2,1)S(1)} collective-permute-done((bf16[1,48,4224]{2,1,0:T(8,128)(2,1)S(1)}, bf16[1,48,4224]{2,1,0:T(8,128)(2,1)S(1)}, u32[]{:S(2)}, u32[]{:S(2)}) %collective-permute-start.15) | collective-permute-done | bytes 405536 | tf_op jit(solution)/shard_map/ppermute | solution.py:15
  146.4 2.7 %fusion.21 = f32[192,1536]{1,0:T(8,128)S(1)} fusion(bf16[192,4096]{1,0:T(8,128)(2,1)S(1)} %bitcast.281, bf16[1,1,4096,1536]{3,2,1,0:T(8,128)(2,1)S(1)} %bitcast.309, f32[192]{0:T(256)S(1)} %add_rsqrt_fusion.1), kind=kOutput, calls=%fused_computation.25 | convolution fusion | flops 2416214016 | bytes 15336192 | tf_op jit(solution)/shard_map/dot_general | solution.py:183
  149.3 0.8 fusion.11
  150.1 0.8 fusion.15
  151.0 0.6 multiply_reduce_fusion
  151.6 2.7 %fusion.24 = f32[192,1536]{1,0:T(8,128)S(1)} fusion(bf16[192,4096]{1,0:T(8,128)(2,1)S(1)} %bitcast.283, bf16[1,1,4096,1536]{3,2,1,0:T(8,128)(2,1)S(1)} %bitcast.309, f32[192]{0:T(256)S(1)} %add_rsqrt_fusion), kind=kOutput, calls=%fused_computation.26 | convolution fusion | flops 2416214016 | bytes 15336192 | tf_op jit(solution)/shard_map/dot_general | solution.py:183
  154.4 0.8 fusion.30
  155.2 0.8 fusion.27
  156.1 0.5 collective-permute-start.18
  156.9 1.6 collective-permute-done.18
  158.5 1.1 collective-permute-done.20
  159.6 1.0 fusion.41
  160.7 1.6 collective-permute-start.19
  162.3 1.5 collective-permute-start.21
  163.8 2.0 collective-permute-start.26
  165.8 2.0 collective-permute-start.24
  167.8 3.7 %collective-permute-start.22 = (bf16[1,48,2048]{2,1,0:T(8,128)(2,1)S(1)}, bf16[1,48,2048]{2,1,0:T(8,128)(2,1)S(1)}, u32[]{:S(2)}, u32[]{:S(2)}) collective-permute-start(bf16[1,48,2048]{2,1,0:T(8,128)(2,1)S(1)} %get-tuple-element.22), channel_id=1, source_target_pairs={{0,14},{2,8},{4,10},{6,12},{8,22},{10,16},{12,18},{14,20},{16,30},... | collective-permute-start | bytes 589832 | tf_op jit(solution)/shard_map/ppermute | solution.py:206
  171.5 5.6 %collective-permute-start.27 = (bf16[1,48,2048]{2,1,0:T(8,128)(2,1)S(1)}, bf16[1,48,2048]{2,1,0:T(8,128)(2,1)S(1)}, u32[]{:S(2)}, u32[]{:S(2)}) collective-permute-start(bf16[1,48,2048]{2,1,0:T(8,128)(2,1)S(1)} %get-tuple-element.24), channel_id=1, source_target_pairs={{0,10},{2,12},{4,14},{6,8},{8,18},{10,20},{12,22},{14,16},{16,26},... | collective-permute-start | bytes 589832 | tf_op jit(solution)/shard_map/ppermute | solution.py:206
  177.1 12.8 %collective-permute-done.21 = bf16[1,48,2048]{2,1,0:T(8,128)(2,1)S(1)} collective-permute-done((bf16[1,48,2048]{2,1,0:T(8,128)(2,1)S(1)}, bf16[1,48,2048]{2,1,0:T(8,128)(2,1)S(1)}, u32[]{:S(2)}, u32[]{:S(2)}) %collective-permute-start.21) | collective-permute-done | bytes 196640 | tf_op jit(solution)/shard_map/ppermute | solution.py:206
  189.9 2.1 %collective-permute-start.25 = (bf16[1,48,2048]{2,1,0:T(8,128)(2,1)S(1)}, bf16[1,48,2048]{2,1,0:T(8,128)(2,1)S(1)}, u32[]{:S(2)}, u32[]{:S(2)}) collective-permute-start(bf16[1,48,2048]{2,1,0:T(8,128)(2,1)S(1)} %get-tuple-element.25), channel_id=1, source_target_pairs={{0,12},{2,14},{4,8},{6,10},{8,20},{10,22},{12,16},{14,18},{16,28},... | collective-permute-start | bytes 589832 | tf_op jit(solution)/shard_map/ppermute | solution.py:206
  192.0 5.3 %collective-permute-start.23 = (bf16[1,48,2048]{2,1,0:T(8,128)(2,1)S(1)}, bf16[1,48,2048]{2,1,0:T(8,128)(2,1)S(1)}, u32[]{:S(2)}, u32[]{:S(2)}) collective-permute-start(bf16[1,48,2048]{2,1,0:T(8,128)(2,1)S(1)} %get-tuple-element.26), channel_id=1, source_target_pairs={{0,14},{2,8},{4,10},{6,12},{8,22},{10,16},{12,18},{14,20},{16,30},... | collective-permute-start | bytes 589832 | tf_op jit(solution)/shard_map/ppermute | solution.py:206
  197.3 4.3 %collective-permute-done.25 = bf16[1,48,2048]{2,1,0:T(8,128)(2,1)S(1)} collective-permute-done((bf16[1,48,2048]{2,1,0:T(8,128)(2,1)S(1)}, bf16[1,48,2048]{2,1,0:T(8,128)(2,1)S(1)}, u32[]{:S(2)}, u32[]{:S(2)}) %collective-permute-start.25) | collective-permute-done | bytes 196640 | tf_op jit(solution)/shard_map/ppermute | solution.py:206
  201.7 1.2 collective-permute-done.23
  203.1 1.5 fusion.8
  (122 shorter events, 8.3 us)
Async XLA Ops:
  0.0 12.3 %copy-start.4 = (s32[1,1,128,1]{2,3,1,0:T(1,128)S(1)}, s32[1,1,128,1]{2,3,1,0:T(1,128)}, u32[]{:S(2)}) copy-start(s32[1,1,128,1]{2,3,1,0:T(1,128)} %param.16) | copy-start | bytes 1540
  0.0 45.3 %collective-permute-start.5 = (bf16[1024,2048]{1,0:T(8,128)(2,1)}, bf16[1024,2048]{1,0:T(8,128)(2,1)}, u32[]{:S(2)}, u32[]{:S(2)}) collective-permute-start(bf16[1024,2048]{1,0:T(8,128)(2,1)} %bitcast.278), channel_id=1, source_target_pairs={{0,1},{1,0},{2,3},{3,2},{4,5},{5,4},{6,7},{7,6},{8,9},{9,8},{10,11... | collective-permute-start | bytes 12582920 | tf_op jit(solution)/shard_map/ppermute | solution.py:15
  0.5 12.3 %copy-start.9 = (f32[1,1,128,1]{2,3,1,0:T(1,128)S(1)}, f32[1,1,128,1]{2,3,1,0:T(1,128)}, u32[]{:S(2)}) copy-start(f32[1,1,128,1]{2,3,1,0:T(1,128)} %param.17) | copy-start | bytes 1540
  0.5 12.3 %copy-start.3 = (f32[1,4096]{1,0:T(1,128)S(1)}, f32[1,4096]{1,0:T(1,128)}, u32[]{:S(2)}) copy-start(f32[1,4096]{1,0:T(1,128)} %param.13) | copy-start | bytes 49156
  1.4 13.4 %collective-permute-start.2 = (bf16[128,256]{1,0:T(8,128)(2,1)S(1)}, bf16[128,256]{1,0:T(8,128)(2,1)S(1)}, u32[]{:S(2)}, u32[]{:S(2)}) collective-permute-start(bf16[128,256]{1,0:T(8,128)(2,1)S(1)} %pad_maximum_fusion.5), channel_id=1, source_target_pairs={{0,6},{2,0},{4,2},{6,4},{1,7},{3,1},{5,3},{7,5},{8,14},{10,8},{12,... | collective-permute-start | bytes 196616 | tf_op jit(solution)/shard_map/ppermute | solution.py:15
  6.3 8.6 %collective-permute-start = (bf16[128,256]{1,0:T(8,128)(2,1)S(1)}, bf16[128,256]{1,0:T(8,128)(2,1)S(1)}, u32[]{:S(2)}, u32[]{:S(2)}) collective-permute-start(bf16[128,256]{1,0:T(8,128)(2,1)S(1)} %pad_maximum_fusion.3), channel_id=1, source_target_pairs={{0,2},{2,4},{4,6},{6,0},{1,3},{3,5},{5,7},{7,1},{8,10},{10,12},{12... | collective-permute-start | bytes 196616 | tf_op jit(solution)/shard_map/ppermute | solution.py:15
  6.3 13.6 %collective-permute-start.1 = (bf16[128,256]{1,0:T(8,128)(2,1)S(1)}, bf16[128,256]{1,0:T(8,128)(2,1)S(1)}, u32[]{:S(2)}, u32[]{:S(2)}) collective-permute-start(bf16[128,256]{1,0:T(8,128)(2,1)S(1)} %pad_maximum_fusion.4), channel_id=1, source_target_pairs={{0,4},{2,6},{4,0},{6,2},{1,5},{3,7},{5,1},{7,3},{8,12},{10,14},{12... | collective-permute-start | bytes 196616 | tf_op jit(solution)/shard_map/ppermute | solution.py:15
  8.8 11.1 %collective-permute-start.3 = (bf16[128,1024]{0,1:T(8,128)(2,1)S(1)}, bf16[128,1024]{0,1:T(8,128)(2,1)S(1)}, u32[]{:S(2)}, u32[]{:S(2)}) collective-permute-start(bf16[128,1024]{0,1:T(8,128)(2,1)S(1)} %bitcast.298), channel_id=1, source_target_pairs={{0,2},{2,4},{4,6},{6,0},{1,3},{3,5},{5,7},{7,1},{8,10},{10,12},{12... | collective-permute-start | bytes 786440 | tf_op jit(solution)/shard_map/ppermute | solution.py:15
  12.8 1.5 copy-start.6
  19.9 69.9 %copy-start.2 = (bf16[512,256]{1,0:T(8,128)(2,1)}, bf16[512,256]{1,0:T(8,128)(2,1)S(1)}, u32[]{:S(2)}) copy-start(bf16[512,256]{1,0:T(8,128)(2,1)S(1)} %pad_maximum_fusion.2) | copy-start | bytes 786436
  19.9 24.2 %collective-permute-start.4 = (bf16[128,1024]{1,0:T(8,128)(2,1)S(1)}, bf16[128,1024]{1,0:T(8,128)(2,1)S(1)}, u32[]{:S(2)}, u32[]{:S(2)}) collective-permute-start(bf16[128,1024]{1,0:T(8,128)(2,1)S(1)} %get-tuple-element.7), channel_id=1, source_target_pairs={{0,4},{2,6},{4,0},{6,2},{1,5},{3,7},{5,1},{7,3},{8,12},{10,14},{12... | collective-permute-start | bytes 786440 | tf_op jit(solution)/shard_map/ppermute | solution.py:15
  26.1 31.1 %collective-permute-start.6 = (bf16[128,2048]{1,0:T(8,128)(2,1)S(1)}, bf16[128,2048]{1,0:T(8,128)(2,1)S(1)}, u32[]{:S(2)}, u32[]{:S(2)}) collective-permute-start(bf16[128,2048]{1,0:T(8,128)(2,1)S(1)} %fusion.99), channel_id=1, source_target_pairs={{0,2},{2,4},{4,6},{6,0},{1,3},{3,5},{5,7},{7,1},{8,10},{10,12},{12... | collective-permute-start | bytes 1572872 | tf_op jit(solution)/shard_map/ppermute | solution.py:15
  26.7 40.5 %collective-permute-start.9 = (bf16[128,1024]{0,1:T(8,128)(2,1)S(1)}, bf16[128,1024]{0,1:T(8,128)(2,1)}, u32[]{:S(2)}, u32[]{:S(2)}) collective-permute-start(bf16[128,1024]{0,1:T(8,128)(2,1)S(1)} %bitcast.299), channel_id=1, source_target_pairs={{0,6},{2,0},{4,2},{6,4},{1,7},{3,1},{5,3},{7,5},{8,14},{10,8},{12,... | collective-permute-start | bytes 786440 | tf_op jit(solution)/shard_map/ppermute | solution.py:15
  48.8 16.6 %collective-permute-start.7 = (bf16[128,2048]{1,0:T(8,128)(2,1)S(1)}, bf16[128,2048]{1,0:T(8,128)(2,1)S(1)}, u32[]{:S(2)}, u32[]{:S(2)}) collective-permute-start(bf16[128,2048]{1,0:T(8,128)(2,1)S(1)} %convolution_add_fusion.2), channel_id=1, source_target_pairs={{0,2},{2,4},{4,6},{6,0},{1,3},{3,5},{5,7},{7,1},{8,10},{10,12},{12... | collective-permute-start | bytes 1572872 | tf_op jit(solution)/shard_map/ppermute | solution.py:15
  57.9 18.7 %collective-permute-start.10 = (bf16[128,2048]{1,0:T(8,128)(2,1)S(1)}, bf16[128,2048]{1,0:T(8,128)(2,1)S(1)}, u32[]{:S(2)}, u32[]{:S(2)}) collective-permute-start(bf16[128,2048]{1,0:T(8,128)(2,1)S(1)} %add_convert_fusion.3), channel_id=1, source_target_pairs={{0,2},{2,4},{4,6},{6,0},{1,3},{3,5},{5,7},{7,1},{8,10},{10,12},{12... | collective-permute-start | bytes 1572872 | tf_op jit(solution)/shard_map/ppermute | solution.py:15
  66.0 21.9 %collective-permute-start.11 = (bf16[128,2048]{1,0:T(8,128)(2,1)S(1)}, bf16[128,2048]{1,0:T(8,128)(2,1)S(1)}, u32[]{:S(2)}, u32[]{:S(2)}) collective-permute-start(bf16[128,2048]{1,0:T(8,128)(2,1)S(1)} %add_convert_fusion.2), channel_id=1, source_target_pairs={{0,2},{2,4},{4,6},{6,0},{1,3},{3,5},{5,7},{7,1},{8,10},{10,12},{12... | collective-permute-start | bytes 1572872 | tf_op jit(solution)/shard_map/ppermute | solution.py:15
  74.5 2.8 %copy-start.5 = (s32[1,1,128,1]{2,3,1,0:T(1,128)S(1)}, s32[1,1,128,1]{2,3,1,0:T(1,128)}, u32[]{:S(2)}) copy-start(s32[1,1,128,1]{2,3,1,0:T(1,128)} %param.16) | copy-start | bytes 1540
  74.5 2.8 %copy-start.7 = (s32[128]{0:T(128)S(1)}, s32[128]{0:T(128)}, u32[]{:S(2)}) copy-start(s32[128]{0:T(128)} %copy-done.6) | copy-start | bytes 1540
  77.3 22.6 %collective-permute-start.12 = (bf16[128,2048]{1,0:T(8,128)(2,1)S(1)}, bf16[128,2048]{1,0:T(8,128)(2,1)S(1)}, u32[]{:S(2)}, u32[]{:S(2)}) collective-permute-start(bf16[128,2048]{1,0:T(8,128)(2,1)S(1)} %add_convert_fusion.1), channel_id=1, source_target_pairs={{0,2},{2,4},{4,6},{6,0},{1,3},{3,5},{5,7},{7,1},{8,10},{10,12},{12... | collective-permute-start | bytes 1572872 | tf_op jit(solution)/shard_map/ppermute | solution.py:15
  77.4 4.7 %collective-permute-start.8 = (f32[1,128]{1,0:T(1,128)S(1)}, f32[1,128]{1,0:T(1,128)S(1)}, u32[]{:S(2)}, u32[]{:S(2)}) collective-permute-start(f32[1,128]{1,0:T(1,128)S(1)} %convert_add_fusion), channel_id=1, source_target_pairs={{0,8},{8,16},{16,24},{24,0},{1,9},{9,17},{17,25},{25,1},{2,10},{10... | collective-permute-start | bytes 1544 | tf_op jit(solution)/shard_map/ppermute | solution.py:15
  82.0 7.8 %copy-start.10 = (f32[1,128]{1,0:T(1,128)}, f32[1,128]{1,0:T(1,128)S(1)}, u32[]{:S(2)}) copy-start(f32[1,128]{1,0:T(1,128)S(1)} %collective-permute-done.8) | copy-start | bytes 1540
  88.5 20.8 %collective-permute-start.13 = (bf16[128,2048]{1,0:T(8,128)(2,1)S(1)}, bf16[128,2048]{1,0:T(8,128)(2,1)S(1)}, u32[]{:S(2)}, u32[]{:S(2)}) collective-permute-start(bf16[128,2048]{1,0:T(8,128)(2,1)S(1)} %add_convert_fusion), channel_id=1, source_target_pairs={{0,2},{2,4},{4,6},{6,0},{1,3},{3,5},{5,7},{7,1},{8,10},{10,12},{12... | collective-permute-start | bytes 1572872 | tf_op jit(solution)/shard_map/ppermute | solution.py:15
  89.8 0.7 copy-start.1
  91.8 2.2 %copy-start = (bf16[1,1,128,4096]{3,2,1,0:T(8,128)(2,1)S(1)}, bf16[1,1,128,4096]{3,2,1,0:T(8,128)(2,1)}, u32[]{:S(2)}) copy-start(bf16[1,1,128,4096]{3,2,1,0:T(8,128)(2,1)} %param.11) | copy-start | bytes 3145732
  100.0 46.4 %slice-start = ((s8[12582912]{0:T(1024)(128)(4,1)}), s8[4194304]{0:T(1024)(128)(4,1)S(1)}, s32[]{:S(2)}) async-start(s8[12582912]{0:T(1024)(128)(4,1)} %bitcast.308), calls=%async_computation | async-start | bytes 8388608
  109.4 0.7 copy-start.8
  109.4 37.0 %slice-start.1 = ((s8[12582912]{0:T(1024)(128)(4,1)}), s8[4194304]{0:T(1024)(128)(4,1)S(1)}, s32[]{:S(2)}) async-start(s8[12582912]{0:T(1024)(128)(4,1)} %bitcast.308), calls=%async_computation.1 | async-start | bytes 8388608
  110.8 11.1 %collective-permute-start.16 = (bf16[1,48,4224]{2,1,0:T(8,128)(2,1)S(1)}, bf16[1,48,4224]{2,1,0:T(8,128)(2,1)S(1)}, u32[]{:S(2)}, u32[]{:S(2)}) collective-permute-start(bf16[1,48,4224]{2,1,0:T(8,128)(2,1)S(1)} %get-tuple-element.10), channel_id=1, source_target_pairs={{0,6},{2,0},{4,2},{6,4},{1,7},{3,1},{5,3},{7,5},{8,14},{10,8},{12,... | collective-permute-start | bytes 1216520 | tf_op jit(solution)/shard_map/ppermute | solution.py:15
  110.8 35.6 %slice-start.2 = ((s8[12582912]{0:T(1024)(128)(4,1)}), s8[4194304]{0:T(1024)(128)(4,1)S(1)}, s32[]{:S(2)}) async-start(s8[12582912]{0:T(1024)(128)(4,1)} %bitcast.308), calls=%async_computation.2 | async-start | bytes 8388608
  110.9 34.6 %collective-permute-start.15 = (bf16[1,48,4224]{2,1,0:T(8,128)(2,1)S(1)}, bf16[1,48,4224]{2,1,0:T(8,128)(2,1)S(1)}, u32[]{:S(2)}, u32[]{:S(2)}) collective-permute-start(bf16[1,48,4224]{2,1,0:T(8,128)(2,1)S(1)} %get-tuple-element.11), channel_id=1, source_target_pairs={{0,4},{2,6},{4,0},{6,2},{1,5},{3,7},{5,1},{7,3},{8,12},{10,14},{12... | collective-permute-start | bytes 1216520 | tf_op jit(solution)/shard_map/ppermute | solution.py:15
  111.0 34.5 %collective-permute-start.14 = (bf16[1,48,4224]{2,1,0:T(8,128)(2,1)S(1)}, bf16[1,48,4224]{2,1,0:T(8,128)(2,1)S(1)}, u32[]{:S(2)}, u32[]{:S(2)}) collective-permute-start(bf16[1,48,4224]{2,1,0:T(8,128)(2,1)S(1)} %get-tuple-element.12), channel_id=1, source_target_pairs={{0,2},{2,4},{4,6},{6,0},{1,3},{3,5},{5,7},{7,1},{8,10},{10,12},{12... | collective-permute-start | bytes 1216520 | tf_op jit(solution)/shard_map/ppermute | solution.py:15
  146.3 3.0 %slice-start.3 = ((s8[6291456]{0:T(1024)(128)(4,1)}), s8[4194304]{0:T(1024)(128)(4,1)S(1)}, s32[]{:S(2)}) async-start(s8[6291456]{0:T(1024)(128)(4,1)} %bitcast.310), calls=%async_computation.3 | async-start | bytes 8388608
  146.3 3.0 %slice-start.4 = ((s8[6291456]{0:T(1024)(128)(4,1)}), s8[2097152]{0:T(1024)(128)(4,1)S(1)}, s32[]{:S(2)}) async-start(s8[6291456]{0:T(1024)(128)(4,1)} %bitcast.310), calls=%async_computation.4 | async-start | bytes 4194304
  146.3 4.7 %collective-permute-start.17 = (bf16[4,48,4096]{2,1,0:T(8,128)(2,1)S(1)}, bf16[4,48,4096]{2,1,0:T(8,128)(2,1)S(1)}, u32[]{:S(2)}, u32[]{:S(2)}) collective-permute-start(bf16[4,48,4096]{2,1,0:T(8,128)(2,1)S(1)} %bitcast.280), channel_id=1, source_target_pairs={{0,1},{1,0},{2,3},{3,2},{4,5},{5,4},{6,7},{7,6},{8,9},{9,8},{10,11... | collective-permute-start | bytes 4718600 | tf_op jit(solution)/shard_map/ppermute | solution.py:15
  156.1 2.4 %collective-permute-start.18 = (bf16[4,48,2048]{2,1,0:T(8,128)(2,1)S(1)}, bf16[4,48,2048]{2,1,0:T(8,128)(2,1)S(1)}, u32[]{:S(2)}, u32[]{:S(2)}) collective-permute-start(bf16[4,48,2048]{2,1,0:T(8,128)(2,1)S(1)} %bitcast.313), channel_id=1, source_target_pairs={{0,1},{1,0},{2,3},{3,2},{4,5},{5,4},{6,7},{7,6},{8,9},{9,8},{10,11... | collective-permute-start | bytes 2359304 | tf_op jit(solution)/shard_map/ppermute | solution.py:15
  156.6 3.0 %collective-permute-start.20 = (bf16[4,48,2048]{2,1,0:T(8,128)(2,1)S(1)}, bf16[4,48,2048]{2,1,0:T(8,128)(2,1)S(1)}, u32[]{:S(2)}, u32[]{:S(2)}) collective-permute-start(bf16[4,48,2048]{2,1,0:T(8,128)(2,1)S(1)} %bitcast.312), channel_id=1, source_target_pairs={{0,1},{1,0},{2,3},{3,2},{4,5},{5,4},{6,7},{7,6},{8,9},{9,8},{10,11... | collective-permute-start | bytes 2359304 | tf_op jit(solution)/shard_map/ppermute | solution.py:15
  160.6 3.2 %copy-start.11 = (f32[1,128]{1,0:T(1,128)S(1)}, f32[1,128]{1,0:T(1,128)}, u32[]{:S(2)}) copy-start(f32[1,128]{1,0:T(1,128)} %copy-done.10) | copy-start | bytes 1540
  160.7 10.8 %collective-permute-start.19 = (bf16[1,48,2048]{2,1,0:T(8,128)(2,1)S(1)}, bf16[1,48,2048]{2,1,0:T(8,128)(2,1)S(1)}, u32[]{:S(2)}, u32[]{:S(2)}) collective-permute-start(bf16[1,48,2048]{2,1,0:T(8,128)(2,1)S(1)} %get-tuple-element.19), channel_id=1, source_target_pairs={{0,8},{2,10},{4,12},{6,14},{8,16},{10,18},{12,20},{14,22},{16,24},... | collective-permute-start | bytes 589832 | tf_op jit(solution)/shard_map/ppermute | solution.py:206
  162.3 27.6 %collective-permute-start.21 = (bf16[1,48,2048]{2,1,0:T(8,128)(2,1)S(1)}, bf16[1,48,2048]{2,1,0:T(8,128)(2,1)S(1)}, u32[]{:S(2)}, u32[]{:S(2)}) collective-permute-start(bf16[1,48,2048]{2,1,0:T(8,128)(2,1)S(1)} %get-tuple-element.23), channel_id=1, source_target_pairs={{0,8},{2,10},{4,12},{6,14},{8,16},{10,18},{12,20},{14,22},{16,24},... | collective-permute-start | bytes 589832 | tf_op jit(solution)/shard_map/ppermute | solution.py:206
  163.8 28.1 %collective-permute-start.26 = (bf16[1,48,2048]{2,1,0:T(8,128)(2,1)S(1)}, bf16[1,48,2048]{2,1,0:T(8,128)(2,1)S(1)}, u32[]{:S(2)}, u32[]{:S(2)}) collective-permute-start(bf16[1,48,2048]{2,1,0:T(8,128)(2,1)S(1)} %get-tuple-element.20), channel_id=1, source_target_pairs={{0,10},{2,12},{4,14},{6,8},{8,18},{10,20},{12,22},{14,16},{16,26},... | collective-permute-start | bytes 589832 | tf_op jit(solution)/shard_map/ppermute | solution.py:206
  165.8 31.5 %collective-permute-start.24 = (bf16[1,48,2048]{2,1,0:T(8,128)(2,1)S(1)}, bf16[1,48,2048]{2,1,0:T(8,128)(2,1)S(1)}, u32[]{:S(2)}, u32[]{:S(2)}) collective-permute-start(bf16[1,48,2048]{2,1,0:T(8,128)(2,1)S(1)} %get-tuple-element.21), channel_id=1, source_target_pairs={{0,12},{2,14},{4,8},{6,10},{8,20},{10,22},{12,16},{14,18},{16,28},... | collective-permute-start | bytes 589832 | tf_op jit(solution)/shard_map/ppermute | solution.py:206
  167.8 33.9 %collective-permute-start.22 = (bf16[1,48,2048]{2,1,0:T(8,128)(2,1)S(1)}, bf16[1,48,2048]{2,1,0:T(8,128)(2,1)S(1)}, u32[]{:S(2)}, u32[]{:S(2)}) collective-permute-start(bf16[1,48,2048]{2,1,0:T(8,128)(2,1)S(1)} %get-tuple-element.22), channel_id=1, source_target_pairs={{0,14},{2,8},{4,10},{6,12},{8,22},{10,16},{12,18},{14,20},{16,30},... | collective-permute-start | bytes 589832 | tf_op jit(solution)/shard_map/ppermute | solution.py:206
  171.5 25.8 %collective-permute-start.27 = (bf16[1,48,2048]{2,1,0:T(8,128)(2,1)S(1)}, bf16[1,48,2048]{2,1,0:T(8,128)(2,1)S(1)}, u32[]{:S(2)}, u32[]{:S(2)}) collective-permute-start(bf16[1,48,2048]{2,1,0:T(8,128)(2,1)S(1)} %get-tuple-element.24), channel_id=1, source_target_pairs={{0,10},{2,12},{4,14},{6,8},{8,18},{10,20},{12,22},{14,16},{16,26},... | collective-permute-start | bytes 589832 | tf_op jit(solution)/shard_map/ppermute | solution.py:206
  189.9 11.8 %collective-permute-start.25 = (bf16[1,48,2048]{2,1,0:T(8,128)(2,1)S(1)}, bf16[1,48,2048]{2,1,0:T(8,128)(2,1)S(1)}, u32[]{:S(2)}, u32[]{:S(2)}) collective-permute-start(bf16[1,48,2048]{2,1,0:T(8,128)(2,1)S(1)} %get-tuple-element.25), channel_id=1, source_target_pairs={{0,12},{2,14},{4,8},{6,10},{8,20},{10,22},{12,16},{14,18},{16,28},... | collective-permute-start | bytes 589832 | tf_op jit(solution)/shard_map/ppermute | solution.py:206
  192.0 10.9 %collective-permute-start.23 = (bf16[1,48,2048]{2,1,0:T(8,128)(2,1)S(1)}, bf16[1,48,2048]{2,1,0:T(8,128)(2,1)S(1)}, u32[]{:S(2)}, u32[]{:S(2)}) collective-permute-start(bf16[1,48,2048]{2,1,0:T(8,128)(2,1)S(1)} %get-tuple-element.26), channel_id=1, source_target_pairs={{0,14},{2,8},{4,10},{6,12},{8,22},{10,16},{12,18},{14,20},{16,30},... | collective-permute-start | bytes 589832 | tf_op jit(solution)/shard_map/ppermute | solution.py:206

commit v16 on v13

--- a/solution.py
+++ b/solution.py
@@ -172,9 +172,13 @@
 
     hidden_width = down_weight.shape[2]
 
-    def gate_and_up(rows, behind):
+    def gate_and_up(rows, behind=None):
         rows = lax.optimization_barrier(rows.reshape(-1, model_width))
-        unscaled = rows.astype(jnp.float32) * inverse_gain + behind
+        unscaled = rows.astype(jnp.float32) * inverse_gain
+        if behind is not None:
+            lead = behind.shape[0]
+            behind = jnp.pad(behind * 0.0, ((0, 0), (0, model_width - behind.shape[1])))
+            unscaled = jnp.concatenate([unscaled[:lead] + behind, unscaled[lead:]], axis=0)
         mean_square = jnp.mean(unscaled * unscaled, axis=-1, keepdims=True)
         gate_up = jnp.dot(rows, in_weight[0, 0], preferred_element_type=jnp.float32)
         return gate_up * lax.rsqrt(mean_square + 1e-06)
@@ -188,8 +192,8 @@
     others = [
         shift(wanted_by(arrived, (my_exp + k) % exps), "exp", k) for k in range(1, exps)
     ]
-    own_gate_up = lax.optimization_barrier(gate_and_up(wanted_by(arrived, my_exp), 0.0))
-    other_gate_up = gate_and_up(jnp.concatenate(others, axis=0), own_gate_up[0, 0] * 0.0)
+    own_gate_up = lax.optimization_barrier(gate_and_up(wanted_by(arrived, my_exp)))
+    other_gate_up = gate_and_up(jnp.concatenate(others, axis=0), own_gate_up[:, :128])
     other_parts = down_part(other_gate_up).astype(jnp.bfloat16)
     own_part = lax.optimization_barrier(down_part(own_gate_up))
     own_part = own_part.reshape(contexts, capacity, model_width)

time: 201 us -> 200 us (level)
  transfers between devices with their start and end apart: 23 -> 23, of which waited for: 10 -> 11; matrix products, arithmetic and copies ran while one was open for 25% -> 26% of each run, Pallas kernels for 0% -> 0%
where the time goes in v16:
time: 200 us; the launch traced here: 197 us
  waiting for transfers between devices  103 us (52%)
  matrix products  46.5 us (23%)
  starting transfers between devices  28.2 us (14%)
  local copies, waits for them, and re-layouts  8.51 us (4%)
  other arithmetic  6.28 us (3%)
  between operations  5.44 us (3%)
    ppermute x19, waiting for transfers between devices, shift(): lax.ppermute(value, axis, [(i, (i + by) % devices) for i in range(devices)])  74.2 us
    ppermute x4, waiting for transfers between devices, to_next_owner(): return lax.ppermute(rows, ('pipe', 'ctx'), pairs)  28.4 us
    dot_general x8, matrix products, mixed_halves(): term = jnp.dot(attended, weights[half], preferred_element_type=jnp.float32)  23.4 us
    ppermute x19, starting transfers between devices, shift(): lax.ppermute(value, axis, [(i, (i + by) % devices) for i in range(devices)])  19 us
    ppermute x4, starting transfers between devices, to_next_owner(): return lax.ppermute(rows, ('pipe', 'ctx'), pairs)  9.17 us
    dot_general x4, matrix products, attend_block(): jnp.einsum('hqk,kd->qhd', attention_weights, value_rows, preferred_elemen...  6.99 us
    sub x4, matrix products, attend_block(): attention_weights = jax.nn.softmax(scores, axis=-1).astype(jnp.bfloat16)  5.94 us
    dot_general x2, matrix products, gate_and_up(): gate_up = jnp.dot(rows, in_weight[0, 0], preferred_element_type=jnp.float32)  5.21 us
  transfers between devices with their start and end apart: 23, of which 11 were waited for; matrix products, arithmetic and copies ran while one was open for 26% of the time, Pallas kernels for 0%

profile of v16, /device:TPU:0, one launch (start us, length us, event | category | flops | bytes accessed | tf_op | source)
XLA Modules:
  0.0 197.4 jit_solution(14266375647739230385)
XLA Ops:
  0.0 0.5 collective-permute-start.5
  0.5 1.0 dynamic-slice_bitcast_fusion.8
  1.4 4.8 %collective-permute-start.2 = (bf16[128,256]{1,0:T(8,128)(2,1)S(1)}, bf16[128,256]{1,0:T(8,128)(2,1)S(1)}, u32[]{:S(2)}, u32[]{:S(2)}) collective-permute-start(bf16[128,256]{1,0:T(8,128)(2,1)S(1)} %pad_maximum_fusion.4), channel_id=1, source_target_pairs={{0,6},{2,0},{4,2},{6,4},{1,7},{3,1},{5,3},{7,5},{8,14},{10,8},{12,... | collective-permute-start | bytes 196616 | tf_op jit(solution)/shard_map/ppermute | solution.py:15
  6.3 1.1 collective-permute-start.1
  7.4 1.3 dynamic-slice_bitcast_fusion
  8.8 3.4 %collective-permute-start.3 = (bf16[128,1024]{0,1:T(8,128)(2,1)S(1)}, bf16[128,1024]{0,1:T(8,128)(2,1)S(1)}, u32[]{:S(2)}, u32[]{:S(2)}) collective-permute-start(bf16[128,1024]{0,1:T(8,128)(2,1)S(1)} %bitcast.265), channel_id=1, source_target_pairs={{0,2},{2,4},{4,6},{6,0},{1,3},{3,5},{5,7},{7,1},{8,10},{10,12},{12... | collective-permute-start | bytes 786440 | tf_op jit(solution)/shard_map/ppermute | solution.py:15
  12.8 0.9 broadcast_compare_fusion.2
  13.7 0.6 fusion.88
  14.8 5.1 %collective-permute-done.1 = bf16[128,256]{1,0:T(8,128)(2,1)S(1)} collective-permute-done((bf16[128,256]{1,0:T(8,128)(2,1)S(1)}, bf16[128,256]{1,0:T(8,128)(2,1)S(1)}, u32[]{:S(2)}, u32[]{:S(2)}) %collective-permute-start.1) | collective-permute-done | bytes 65568 | tf_op jit(solution)/shard_map/ppermute | solution.py:15
  19.9 0.9 collective-permute-start.4
  20.9 0.8 fusion.116
  21.7 1.0 convolution_convert_fusion.5
  22.7 2.9 %fusion.99 = bf16[128,2048]{1,0:T(8,128)(2,1)S(1)} fusion(bf16[128,1024]{0,1:T(8,128)(2,1)S(1)} %bitcast.253, bf16[1,1024,2048]{2,1,0:T(8,128)(2,1)} %param.12), kind=kOutput, calls=%fused_computation.185 | convolution fusion | flops 536870912 | bytes 4980736 | tf_op jit(solution)/shard_map/dot_general | solution.py:92
  25.6 0.6 slice.139
  26.2 0.5 collective-permute-start.6
  26.7 3.3 %collective-permute-start.9 = (bf16[128,1024]{0,1:T(8,128)(2,1)S(1)}, bf16[128,1024]{0,1:T(8,128)(2,1)}, u32[]{:S(2)}, u32[]{:S(2)}) collective-permute-start(bf16[128,1024]{0,1:T(8,128)(2,1)S(1)} %bitcast.266), channel_id=1, source_target_pairs={{0,6},{2,0},{4,2},{6,4},{1,7},{3,1},{5,3},{7,5},{8,14},{10,8},{12,... | collective-permute-start | bytes 786440 | tf_op jit(solution)/shard_map/ppermute | solution.py:15
  30.0 14.1 %collective-permute-done.4 = bf16[128,1024]{1,0:T(8,128)(2,1)S(1)} collective-permute-done((bf16[128,1024]{1,0:T(8,128)(2,1)S(1)}, bf16[128,1024]{1,0:T(8,128)(2,1)S(1)}, u32[]{:S(2)}, u32[]{:S(2)}) %collective-permute-start.4) | collective-permute-done | bytes 262176 | tf_op jit(solution)/shard_map/ppermute | solution.py:15
  44.1 0.6 slice.140
  45.4 2.9 %convolution_add_fusion.2 = bf16[128,2048]{1,0:T(8,128)(2,1)S(1)} fusion(bf16[128,1024]{0,1:T(8,128)(2,1)S(1)} %bitcast.254, bf16[1024,2048]{1,0:T(8,128)(2,1)} %collective-permute-done.5, f32[]{:T(128)} %bitcast.22), kind=kOutput, calls=%fused_computation.24 | convolution fusion | flops 537395200 | bytes 4980740 | tf_op jit(solution)/shard_map/dot_general | solution.py:92
  48.3 0.6 slice.141
  50.4 2.2 %fusion.117 = f32[8,128]{1,0:T(8,128)} fusion(pred[128,512]{0,1:T(8,128)(4,1)} %get-tuple-element.32, bf16[128,8,128]{0,2,1:T(8,128)(2,1)S(1)} %bitcast.267, bf16[512,256]{1,0:T(8,128)(2,1)S(1)} %pad_maximum_fusion.1), kind=kOutput, calls=%fused_computation.199 | convolution fusion | flops 136315392 | bytes 462848 | tf_op jit(solution)/shard_map/sub | solution.py:27
  52.7 1.9 convolution_convert_fusion.4
  54.5 2.9 %fusion.97 = f32[128,2048]{1,0:T(8,128)S(1)} fusion(bf16[128,1024]{0,1:T(8,128)(2,1)S(1)} %bitcast.259, bf16[1,1024,2048]{2,1,0:T(8,128)(2,1)} %param.12), kind=kOutput, calls=%fused_computation.183 | convolution fusion | flops 536870912 | bytes 5505024 | tf_op jit(solution)/shard_map/dot_general | solution.py:92
  57.6 0.6 slice.142
  58.3 2.9 %fusion.120 = f32[128,2048]{1,0:T(8,128)S(1)} fusion(bf16[128,1024]{0,1:T(8,128)(2,1)S(1)} %bitcast.260, bf16[1024,2048]{1,0:T(8,128)(2,1)} %collective-permute-done.5), kind=kOutput, calls=%fused_computation.202 | convolution fusion | flops 536870912 | bytes 5505024 | tf_op jit(solution)/shard_map/dot_general | solution.py:92
  61.3 4.3 %collective-permute-done.7 = bf16[128,2048]{1,0:T(8,128)(2,1)S(1)} collective-permute-done((bf16[128,2048]{1,0:T(8,128)(2,1)S(1)}, bf16[128,2048]{1,0:T(8,128)(2,1)S(1)}, u32[]{:S(2)}, u32[]{:S(2)}) %collective-permute-start.7) | collective-permute-done | bytes 524320 | tf_op jit(solution)/shard_map/ppermute | solution.py:15
  65.6 0.5 slice.143
  67.4 1.0 broadcast_add_fusion.1
  68.4 1.6 fusion.118
  70.0 1.9 convolution_convert_fusion.3
  71.9 2.9 %fusion.95 = f32[128,2048]{1,0:T(8,128)S(1)} fusion(bf16[128,1024]{0,1:T(8,128)(2,1)S(1)} %bitcast.257, bf16[1,1024,2048]{2,1,0:T(8,128)(2,1)} %param.12), kind=kOutput, calls=%fused_computation.181 | convolution fusion | flops 536870912 | bytes 5505024 | tf_op jit(solution)/shard_map/dot_general | solution.py:92
  74.9 1.9 collective-permute-done.10
  76.9 0.6 slice.144
  77.5 1.7 collective-permute-start.8
  79.2 2.9 %fusion.121 = f32[128,2048]{1,0:T(8,128)S(1)} fusion(bf16[128,1024]{0,1:T(8,128)(2,1)S(1)} %bitcast.258, bf16[1024,2048]{1,0:T(8,128)(2,1)} %collective-permute-done.5), kind=kOutput, calls=%fused_computation.203 | convolution fusion | flops 536870912 | bytes 5505024 | tf_op jit(solution)/shard_map/dot_general | solution.py:92
  82.2 5.8 %collective-permute-done.11 = bf16[128,2048]{1,0:T(8,128)(2,1)S(1)} collective-permute-done((bf16[128,2048]{1,0:T(8,128)(2,1)S(1)}, bf16[128,2048]{1,0:T(8,128)(2,1)S(1)}, u32[]{:S(2)}, u32[]{:S(2)}) %collective-permute-start.11) | collective-permute-done | bytes 524320 | tf_op jit(solution)/shard_map/ppermute | solution.py:15
  88.1 0.6 slice.145
  90.2 0.7 copy-done.1
  90.8 1.4 fusion.119
  92.2 2.2 %convolution_convert_fusion.2 = bf16[128,8,128]{2,0,1:T(8,128)(2,1)S(1)} fusion(f32[8,128]{1,0:T(8,128)} %fusion.119, bf16[512,256]{1,0:T(8,128)(2,1)} %copy-done.2, pred[128,512]{0,1:T(8,128)(4,1)S(1)} %get-tuple-element.30, bf16[128,8,128]{0,2,1:T(8,128)(2,1)} %bitcast.262), kind=kOutput, calls=%fused_computation.54 | convolution fusion | flops 271189504 | bytes 856064 | tf_op jit(solution)/shard_map/hqk,kd->qhd/dot_general | solution.py:28
  94.4 2.9 %convolution_add_fusion.1 = f32[128,2048]{1,0:T(8,128)S(1)} fusion(bf16[128,1024]{0,1:T(8,128)(2,1)S(1)} %bitcast.255, bf16[1,1,128,4096]{3,2,1,0:T(8,128)(2,1)S(1)} %copy-done, s32[]{:T(128)S(6)} %select_n.179, bf16[1,1024,2048]{2,1,0:T(8,128)(2,1)} %param.12), kind=kOutput, calls=%fused_computation.23 | convolution fusion | flops 537395200 | bytes 6029316 | tf_op jit(solution)/shard_map/dot_general | solution.py:92
  97.3 2.9 %convolution_add_fusion = f32[128,2048]{1,0:T(8,128)S(1)} fusion(bf16[128,1024]{0,1:T(8,128)(2,1)S(1)} %bitcast.256, bf16[1024,2048]{1,0:T(8,128)(2,1)} %collective-permute-done.5, bf16[1,1,128,4096]{3,2,1,0:T(8,128)(2,1)S(1)} %copy-done, s32[]{:T(128)S(6)} %select_n.180), kind=kOutput, calls=%fused_computation.22 | convolution fusion | flops 537395200 | bytes 6029316 | tf_op jit(solution)/shard_map/dot_general | solution.py:92
  100.5 8.9 %collective-permute-done.13 = bf16[128,2048]{1,0:T(8,128)(2,1)S(1)} collective-permute-done((bf16[128,2048]{1,0:T(8,128)(2,1)S(1)}, bf16[128,2048]{1,0:T(8,128)(2,1)S(1)}, u32[]{:S(2)}, u32[]{:S(2)}) %collective-permute-start.13) | collective-permute-done | bytes 524320 | tf_op jit(solution)/shard_map/ppermute | solution.py:15
  109.6 0.2 fusion.25
  109.8 0.4 copy-done.8
  110.2 0.6 convolution_convert_fusion
  111.1 2.0 %collective-permute-start.14 = (bf16[1,48,4224]{2,1,0:T(8,128)(2,1)S(1)}, bf16[1,48,4224]{2,1,0:T(8,128)(2,1)S(1)}, u32[]{:S(2)}, u32[]{:S(2)}) collective-permute-start(bf16[1,48,4224]{2,1,0:T(8,128)(2,1)S(1)} %get-tuple-element.12), channel_id=1, source_target_pairs={{0,2},{2,4},{4,6},{6,0},{1,3},{3,5},{5,7},{7,1},{8,10},{10,12},{12... | collective-permute-start | bytes 1216520 | tf_op jit(solution)/shard_map/ppermute | solution.py:15
  113.2 8.8 %collective-permute-done.16 = bf16[1,48,4224]{2,1,0:T(8,128)(2,1)S(1)} collective-permute-done((bf16[1,48,4224]{2,1,0:T(8,128)(2,1)S(1)}, bf16[1,48,4224]{2,1,0:T(8,128)(2,1)S(1)}, u32[]{:S(2)}, u32[]{:S(2)}) %collective-permute-start.16) | collective-permute-done | bytes 405536 | tf_op jit(solution)/shard_map/ppermute | solution.py:15
  122.0 23.6 %collective-permute-done.15 = bf16[1,48,4224]{2,1,0:T(8,128)(2,1)S(1)} collective-permute-done((bf16[1,48,4224]{2,1,0:T(8,128)(2,1)S(1)}, bf16[1,48,4224]{2,1,0:T(8,128)(2,1)S(1)}, u32[]{:S(2)}, u32[]{:S(2)}) %collective-permute-start.15) | collective-permute-done | bytes 405536 | tf_op jit(solution)/shard_map/ppermute | solution.py:15
  146.0 0.5 multiply_reduce_fusion.1
  146.6 2.6 %fusion.17 = f32[192,1536]{1,0:T(8,128)S(1)} fusion(bf16[192,4096]{1,0:T(8,128)(2,1)S(1)} %bitcast.249, bf16[1,1,4096,1536]{3,2,1,0:T(8,128)(2,1)S(1)} %bitcast.276, f32[192]{0:T(256)S(1)} %add_rsqrt_fusion.1), kind=kOutput, calls=%fused_computation.20 | convolution fusion | flops 2416214016 | bytes 15336192 | tf_op jit(solution)/shard_map/dot_general | solution.py:183
  149.4 0.5 multiply_reduce_fusion
  149.9 2.6 %fusion.20 = f32[192,1536]{1,0:T(8,128)S(1)} fusion(bf16[192,4096]{1,0:T(8,128)(2,1)S(1)} %bitcast.252, bf16[1,1,4096,1536]{3,2,1,0:T(8,128)(2,1)S(1)} %bitcast.276, f32[192]{0:T(256)S(1)} %add_rsqrt_fusion), kind=kOutput, calls=%fused_computation.21 | convolution fusion | flops 2416214016 | bytes 15336192 | tf_op jit(solution)/shard_map/dot_general | solution.py:183
  152.6 1.4 fusion.12
  154.0 0.4 collective-permute-start.18
  154.4 1.4 fusion.10
  156.0 1.5 collective-permute-done.18
  157.5 0.8 fusion.16
  158.4 1.5 collective-permute-start.19
  159.9 2.0 collective-permute-start.22
  161.9 1.9 collective-permute-start.21
  163.8 3.8 %collective-permute-start.20 = (bf16[1,48,4096]{2,1,0:T(8,128)(2,1)S(1)}, bf16[1,48,4096]{2,1,0:T(8,128)(2,1)S(1)}, u32[]{:S(2)}, u32[]{:S(2)}) collective-permute-start(bf16[1,48,4096]{2,1,0:T(8,128)(2,1)S(1)} %get-tuple-element.16), channel_id=1, source_target_pairs={{0,14},{2,8},{4,10},{6,12},{8,22},{10,16},{12,18},{14,20},{16,30},... | collective-permute-start | bytes 1179656 | tf_op jit(solution)/shard_map/ppermute | solution.py:219
  167.6 28.4 %collective-permute-done.19 = bf16[1,48,4096]{2,1,0:T(8,128)(2,1)S(1)} collective-permute-done((bf16[1,48,4096]{2,1,0:T(8,128)(2,1)S(1)}, bf16[1,48,4096]{2,1,0:T(8,128)(2,1)S(1)}, u32[]{:S(2)}, u32[]{:S(2)}) %collective-permute-start.19) | collective-permute-done | bytes 393248 | tf_op jit(solution)/shard_map/ppermute | solution.py:219
  195.9 1.5 fusion.15
  (101 shorter events, 3.7 us)
Async XLA Ops:
  0.0 12.3 %copy-start.4 = (s32[1,1,128,1]{2,3,1,0:T(1,128)S(1)}, s32[1,1,128,1]{2,3,1,0:T(1,128)}, u32[]{:S(2)}) copy-start(s32[1,1,128,1]{2,3,1,0:T(1,128)} %param.16) | copy-start | bytes 1540
  0.0 45.4 %collective-permute-start.5 = (bf16[1024,2048]{1,0:T(8,128)(2,1)}, bf16[1024,2048]{1,0:T(8,128)(2,1)}, u32[]{:S(2)}, u32[]{:S(2)}) collective-permute-start(bf16[1024,2048]{1,0:T(8,128)(2,1)} %bitcast.246), channel_id=1, source_target_pairs={{0,1},{1,0},{2,3},{3,2},{4,5},{5,4},{6,7},{7,6},{8,9},{9,8},{10,11... | collective-permute-start | bytes 12582920 | tf_op jit(solution)/shard_map/ppermute | solution.py:15
  0.5 12.3 %copy-start.9 = (f32[1,1,128,1]{2,3,1,0:T(1,128)S(1)}, f32[1,1,128,1]{2,3,1,0:T(1,128)}, u32[]{:S(2)}) copy-start(f32[1,1,128,1]{2,3,1,0:T(1,128)} %param.17) | copy-start | bytes 1540
  0.5 12.3 %copy-start.3 = (f32[1,4096]{1,0:T(1,128)S(1)}, f32[1,4096]{1,0:T(1,128)}, u32[]{:S(2)}) copy-start(f32[1,4096]{1,0:T(1,128)} %param.13) | copy-start | bytes 49156
  1.4 13.4 %collective-permute-start.2 = (bf16[128,256]{1,0:T(8,128)(2,1)S(1)}, bf16[128,256]{1,0:T(8,128)(2,1)S(1)}, u32[]{:S(2)}, u32[]{:S(2)}) collective-permute-start(bf16[128,256]{1,0:T(8,128)(2,1)S(1)} %pad_maximum_fusion.4), channel_id=1, source_target_pairs={{0,6},{2,0},{4,2},{6,4},{1,7},{3,1},{5,3},{7,5},{8,14},{10,8},{12,... | collective-permute-start | bytes 196616 | tf_op jit(solution)/shard_map/ppermute | solution.py:15
  6.3 8.6 %collective-permute-start = (bf16[128,256]{1,0:T(8,128)(2,1)S(1)}, bf16[128,256]{1,0:T(8,128)(2,1)S(1)}, u32[]{:S(2)}, u32[]{:S(2)}) collective-permute-start(bf16[128,256]{1,0:T(8,128)(2,1)S(1)} %pad_maximum_fusion.2), channel_id=1, source_target_pairs={{0,2},{2,4},{4,6},{6,0},{1,3},{3,5},{5,7},{7,1},{8,10},{10,12},{12... | collective-permute-start | bytes 196616 | tf_op jit(solution)/shard_map/ppermute | solution.py:15
  6.3 13.6 %collective-permute-start.1 = (bf16[128,256]{1,0:T(8,128)(2,1)S(1)}, bf16[128,256]{1,0:T(8,128)(2,1)S(1)}, u32[]{:S(2)}, u32[]{:S(2)}) collective-permute-start(bf16[128,256]{1,0:T(8,128)(2,1)S(1)} %pad_maximum_fusion.3), channel_id=1, source_target_pairs={{0,4},{2,6},{4,0},{6,2},{1,5},{3,7},{5,1},{7,3},{8,12},{10,14},{12... | collective-permute-start | bytes 196616 | tf_op jit(solution)/shard_map/ppermute | solution.py:15
  8.8 11.1 %collective-permute-start.3 = (bf16[128,1024]{0,1:T(8,128)(2,1)S(1)}, bf16[128,1024]{0,1:T(8,128)(2,1)S(1)}, u32[]{:S(2)}, u32[]{:S(2)}) collective-permute-start(bf16[128,1024]{0,1:T(8,128)(2,1)S(1)} %bitcast.265), channel_id=1, source_target_pairs={{0,2},{2,4},{4,6},{6,0},{1,3},{3,5},{5,7},{7,1},{8,10},{10,12},{12... | collective-permute-start | bytes 786440 | tf_op jit(solution)/shard_map/ppermute | solution.py:15
  12.8 8.9 %copy-start.6 = (s32[128]{0:T(128)}, s32[128]{0:T(128)S(1)}, u32[]{:S(2)}) copy-start(s32[128]{0:T(128)S(1)} %select_reduce_fusion) | copy-start | bytes 1540
  19.9 70.2 %copy-start.2 = (bf16[512,256]{1,0:T(8,128)(2,1)}, bf16[512,256]{1,0:T(8,128)(2,1)S(1)}, u32[]{:S(2)}) copy-start(bf16[512,256]{1,0:T(8,128)(2,1)S(1)} %pad_maximum_fusion.1) | copy-start | bytes 786436
  19.9 24.2 %collective-permute-start.4 = (bf16[128,1024]{1,0:T(8,128)(2,1)S(1)}, bf16[128,1024]{1,0:T(8,128)(2,1)S(1)}, u32[]{:S(2)}, u32[]{:S(2)}) collective-permute-start(bf16[128,1024]{1,0:T(8,128)(2,1)S(1)} %get-tuple-element.7), channel_id=1, source_target_pairs={{0,4},{2,6},{4,0},{6,2},{1,5},{3,7},{5,1},{7,3},{8,12},{10,14},{12... | collective-permute-start | bytes 786440 | tf_op jit(solution)/shard_map/ppermute | solution.py:15
  26.2 31.3 %collective-permute-start.6 = (bf16[128,2048]{1,0:T(8,128)(2,1)S(1)}, bf16[128,2048]{1,0:T(8,128)(2,1)S(1)}, u32[]{:S(2)}, u32[]{:S(2)}) collective-permute-start(bf16[128,2048]{1,0:T(8,128)(2,1)S(1)} %fusion.99), channel_id=1, source_target_pairs={{0,2},{2,4},{4,6},{6,0},{1,3},{3,5},{5,7},{7,1},{8,10},{10,12},{12... | collective-permute-start | bytes 1572872 | tf_op jit(solution)/shard_map/ppermute | solution.py:15
  26.7 40.7 %collective-permute-start.9 = (bf16[128,1024]{0,1:T(8,128)(2,1)S(1)}, bf16[128,1024]{0,1:T(8,128)(2,1)}, u32[]{:S(2)}, u32[]{:S(2)}) collective-permute-start(bf16[128,1024]{0,1:T(8,128)(2,1)S(1)} %bitcast.266), channel_id=1, source_target_pairs={{0,6},{2,0},{4,2},{6,4},{1,7},{3,1},{5,3},{7,5},{8,14},{10,8},{12,... | collective-permute-start | bytes 786440 | tf_op jit(solution)/shard_map/ppermute | solution.py:15
  48.9 16.6 %collective-permute-start.7 = (bf16[128,2048]{1,0:T(8,128)(2,1)S(1)}, bf16[128,2048]{1,0:T(8,128)(2,1)S(1)}, u32[]{:S(2)}, u32[]{:S(2)}) collective-permute-start(bf16[128,2048]{1,0:T(8,128)(2,1)S(1)} %convolution_add_fusion.2), channel_id=1, source_target_pairs={{0,2},{2,4},{4,6},{6,0},{1,3},{3,5},{5,7},{7,1},{8,10},{10,12},{12... | collective-permute-start | bytes 1572872 | tf_op jit(solution)/shard_map/ppermute | solution.py:15
  58.2 18.5 %collective-permute-start.10 = (bf16[128,2048]{1,0:T(8,128)(2,1)S(1)}, bf16[128,2048]{1,0:T(8,128)(2,1)S(1)}, u32[]{:S(2)}, u32[]{:S(2)}) collective-permute-start(bf16[128,2048]{1,0:T(8,128)(2,1)S(1)} %add_convert_fusion.3), channel_id=1, source_target_pairs={{0,2},{2,4},{4,6},{6,0},{1,3},{3,5},{5,7},{7,1},{8,10},{10,12},{12... | collective-permute-start | bytes 1572872 | tf_op jit(solution)/shard_map/ppermute | solution.py:15
  66.1 21.8 %collective-permute-start.11 = (bf16[128,2048]{1,0:T(8,128)(2,1)S(1)}, bf16[128,2048]{1,0:T(8,128)(2,1)S(1)}, u32[]{:S(2)}, u32[]{:S(2)}) collective-permute-start(bf16[128,2048]{1,0:T(8,128)(2,1)S(1)} %add_convert_fusion.2), channel_id=1, source_target_pairs={{0,2},{2,4},{4,6},{6,0},{1,3},{3,5},{5,7},{7,1},{8,10},{10,12},{12... | collective-permute-start | bytes 1572872 | tf_op jit(solution)/shard_map/ppermute | solution.py:15
  74.8 2.6 %copy-start.5 = (s32[1,1,128,1]{2,3,1,0:T(1,128)S(1)}, s32[1,1,128,1]{2,3,1,0:T(1,128)}, u32[]{:S(2)}) copy-start(s32[1,1,128,1]{2,3,1,0:T(1,128)} %param.16) | copy-start | bytes 1540
  74.9 2.6 %copy-start.7 = (s32[128]{0:T(128)S(1)}, s32[128]{0:T(128)}, u32[]{:S(2)}) copy-start(s32[128]{0:T(128)} %copy-done.6) | copy-start | bytes 1540
  77.5 22.8 %collective-permute-start.12 = (bf16[128,2048]{1,0:T(8,128)(2,1)S(1)}, bf16[128,2048]{1,0:T(8,128)(2,1)S(1)}, u32[]{:S(2)}, u32[]{:S(2)}) collective-permute-start(bf16[128,2048]{1,0:T(8,128)(2,1)S(1)} %add_convert_fusion.1), channel_id=1, source_target_pairs={{0,2},{2,4},{4,6},{6,0},{1,3},{3,5},{5,7},{7,1},{8,10},{10,12},{12... | collective-permute-start | bytes 1572872 | tf_op jit(solution)/shard_map/ppermute | solution.py:15
  77.5 4.7 %collective-permute-start.8 = (f32[1,128]{1,0:T(1,128)S(1)}, f32[1,128]{1,0:T(1,128)S(1)}, u32[]{:S(2)}, u32[]{:S(2)}) collective-permute-start(f32[1,128]{1,0:T(1,128)S(1)} %convert_add_fusion), channel_id=1, source_target_pairs={{0,8},{8,16},{16,24},{24,0},{1,9},{9,17},{17,25},{25,1},{2,10},{10... | collective-permute-start | bytes 1544 | tf_op jit(solution)/shard_map/ppermute | solution.py:15
  82.2 8.0 %copy-start.10 = (f32[1,128]{1,0:T(1,128)}, f32[1,128]{1,0:T(1,128)S(1)}, u32[]{:S(2)}) copy-start(f32[1,128]{1,0:T(1,128)S(1)} %collective-permute-done.8) | copy-start | bytes 1540
  88.7 20.7 %collective-permute-start.13 = (bf16[128,2048]{1,0:T(8,128)(2,1)S(1)}, bf16[128,2048]{1,0:T(8,128)(2,1)S(1)}, u32[]{:S(2)}, u32[]{:S(2)}) collective-permute-start(bf16[128,2048]{1,0:T(8,128)(2,1)S(1)} %add_convert_fusion), channel_id=1, source_target_pairs={{0,2},{2,4},{4,6},{6,0},{1,3},{3,5},{5,7},{7,1},{8,10},{10,12},{12... | collective-permute-start | bytes 1572872 | tf_op jit(solution)/shard_map/ppermute | solution.py:15
  90.1 0.7 copy-start.1
  92.2 2.2 %copy-start = (bf16[1,1,128,4096]{3,2,1,0:T(8,128)(2,1)S(1)}, bf16[1,1,128,4096]{3,2,1,0:T(8,128)(2,1)}, u32[]{:S(2)}) copy-start(bf16[1,1,128,4096]{3,2,1,0:T(8,128)(2,1)} %param.11) | copy-start | bytes 3145732
  100.3 46.2 %slice-start = ((s8[12582912]{0:T(1024)(128)(4,1)}), s8[4194304]{0:T(1024)(128)(4,1)S(1)}, s32[]{:S(2)}) async-start(s8[12582912]{0:T(1024)(128)(4,1)} %bitcast.275), calls=%async_computation | async-start | bytes 8388608
  109.6 0.7 copy-start.8
  109.6 37.0 %slice-start.1 = ((s8[12582912]{0:T(1024)(128)(4,1)}), s8[4194304]{0:T(1024)(128)(4,1)S(1)}, s32[]{:S(2)}) async-start(s8[12582912]{0:T(1024)(128)(4,1)} %bitcast.275), calls=%async_computation.1 | async-start | bytes 8388608
  110.9 11.1 %collective-permute-start.16 = (bf16[1,48,4224]{2,1,0:T(8,128)(2,1)S(1)}, bf16[1,48,4224]{2,1,0:T(8,128)(2,1)S(1)}, u32[]{:S(2)}, u32[]{:S(2)}) collective-permute-start(bf16[1,48,4224]{2,1,0:T(8,128)(2,1)S(1)} %get-tuple-element.10), channel_id=1, source_target_pairs={{0,6},{2,0},{4,2},{6,4},{1,7},{3,1},{5,3},{7,5},{8,14},{10,8},{12,... | collective-permute-start | bytes 1216520 | tf_op jit(solution)/shard_map/ppermute | solution.py:15
  111.0 35.5 %slice-start.2 = ((s8[12582912]{0:T(1024)(128)(4,1)}), s8[4194304]{0:T(1024)(128)(4,1)S(1)}, s32[]{:S(2)}) async-start(s8[12582912]{0:T(1024)(128)(4,1)} %bitcast.275), calls=%async_computation.2 | async-start | bytes 8388608
  111.0 34.6 %collective-permute-start.15 = (bf16[1,48,4224]{2,1,0:T(8,128)(2,1)S(1)}, bf16[1,48,4224]{2,1,0:T(8,128)(2,1)S(1)}, u32[]{:S(2)}, u32[]{:S(2)}) collective-permute-start(bf16[1,48,4224]{2,1,0:T(8,128)(2,1)S(1)} %get-tuple-element.11), channel_id=1, source_target_pairs={{0,4},{2,6},{4,0},{6,2},{1,5},{3,7},{5,1},{7,3},{8,12},{10,14},{12... | collective-permute-start | bytes 1216520 | tf_op jit(solution)/shard_map/ppermute | solution.py:15
  111.1 34.6 %collective-permute-start.14 = (bf16[1,48,4224]{2,1,0:T(8,128)(2,1)S(1)}, bf16[1,48,4224]{2,1,0:T(8,128)(2,1)S(1)}, u32[]{:S(2)}, u32[]{:S(2)}) collective-permute-start(bf16[1,48,4224]{2,1,0:T(8,128)(2,1)S(1)} %get-tuple-element.12), channel_id=1, source_target_pairs={{0,2},{2,4},{4,6},{6,0},{1,3},{3,5},{5,7},{7,1},{8,10},{10,12},{12... | collective-permute-start | bytes 1216520 | tf_op jit(solution)/shard_map/ppermute | solution.py:15
  145.9 3.5 %collective-permute-start.17 = (bf16[4,48,4096]{2,1,0:T(8,128)(2,1)S(1)}, bf16[4,48,4096]{2,1,0:T(8,128)(2,1)S(1)}, u32[]{:S(2)}, u32[]{:S(2)}) collective-permute-start(bf16[4,48,4096]{2,1,0:T(8,128)(2,1)S(1)} %bitcast.247), channel_id=1, source_target_pairs={{0,1},{1,0},{2,3},{3,2},{4,5},{5,4},{6,7},{7,6},{8,9},{9,8},{10,11... | collective-permute-start | bytes 4718600 | tf_op jit(solution)/shard_map/ppermute | solution.py:15
  149.2 3.4 %slice-start.3 = ((s8[6291456]{0:T(1024)(128)(4,1)}), s8[4194304]{0:T(1024)(128)(4,1)S(1)}, s32[]{:S(2)}) async-start(s8[6291456]{0:T(1024)(128)(4,1)} %bitcast.277), calls=%async_computation.3 | async-start | bytes 8388608
  149.9 2.6 %slice-start.4 = ((s8[6291456]{0:T(1024)(128)(4,1)}), s8[2097152]{0:T(1024)(128)(4,1)S(1)}, s32[]{:S(2)}) async-start(s8[6291456]{0:T(1024)(128)(4,1)} %bitcast.277), calls=%async_computation.4 | async-start | bytes 4194304
  154.0 3.5 %collective-permute-start.18 = (bf16[4,48,4096]{2,1,0:T(8,128)(2,1)S(1)}, bf16[4,48,4096]{2,1,0:T(8,128)(2,1)S(1)}, u32[]{:S(2)}, u32[]{:S(2)}) collective-permute-start(bf16[4,48,4096]{2,1,0:T(8,128)(2,1)S(1)} %bitcast.279), channel_id=1, source_target_pairs={{0,1},{1,0},{2,3},{3,2},{4,5},{5,4},{6,7},{7,6},{8,9},{9,8},{10,11... | collective-permute-start | bytes 4718600 | tf_op jit(solution)/shard_map/ppermute | solution.py:15
  158.3 9.3 %copy-start.11 = (f32[1,128]{1,0:T(1,128)S(1)}, f32[1,128]{1,0:T(1,128)}, u32[]{:S(2)}) copy-start(f32[1,128]{1,0:T(1,128)} %copy-done.10) | copy-start | bytes 1540
  158.4 37.5 %collective-permute-start.19 = (bf16[1,48,4096]{2,1,0:T(8,128)(2,1)S(1)}, bf16[1,48,4096]{2,1,0:T(8,128)(2,1)S(1)}, u32[]{:S(2)}, u32[]{:S(2)}) collective-permute-start(bf16[1,48,4096]{2,1,0:T(8,128)(2,1)S(1)} %get-tuple-element.13), channel_id=1, source_target_pairs={{0,8},{2,10},{4,12},{6,14},{8,16},{10,18},{12,20},{14,22},{16,24},... | collective-permute-start | bytes 1179656 | tf_op jit(solution)/shard_map/ppermute | solution.py:219
  159.9 36.0 %collective-permute-start.22 = (bf16[1,48,4096]{2,1,0:T(8,128)(2,1)S(1)}, bf16[1,48,4096]{2,1,0:T(8,128)(2,1)S(1)}, u32[]{:S(2)}, u32[]{:S(2)}) collective-permute-start(bf16[1,48,4096]{2,1,0:T(8,128)(2,1)S(1)} %get-tuple-element.14), channel_id=1, source_target_pairs={{0,10},{2,12},{4,14},{6,8},{8,18},{10,20},{12,22},{14,16},{16,26},... | collective-permute-start | bytes 1179656 | tf_op jit(solution)/shard_map/ppermute | solution.py:219
  161.9 34.1 %collective-permute-start.21 = (bf16[1,48,4096]{2,1,0:T(8,128)(2,1)S(1)}, bf16[1,48,4096]{2,1,0:T(8,128)(2,1)S(1)}, u32[]{:S(2)}, u32[]{:S(2)}) collective-permute-start(bf16[1,48,4096]{2,1,0:T(8,128)(2,1)S(1)} %get-tuple-element.15), channel_id=1, source_target_pairs={{0,12},{2,14},{4,8},{6,10},{8,20},{10,22},{12,16},{14,18},{16,28},... | collective-permute-start | bytes 1179656 | tf_op jit(solution)/shard_map/ppermute | solution.py:219
  163.8 32.2 %collective-permute-start.20 = (bf16[1,48,4096]{2,1,0:T(8,128)(2,1)S(1)}, bf16[1,48,4096]{2,1,0:T(8,128)(2,1)S(1)}, u32[]{:S(2)}, u32[]{:S(2)}) collective-permute-start(bf16[1,48,4096]{2,1,0:T(8,128)(2,1)S(1)} %get-tuple-element.16), channel_id=1, source_target_pairs={{0,14},{2,8},{4,10},{6,12},{8,22},{10,16},{12,18},{14,20},{16,30},... | collective-permute-start | bytes 1179656 | tf_op jit(solution)/shard_map/ppermute | solution.py:219

commit v17 on v16

--- a/solution.py
+++ b/solution.py
@@ -93,8 +93,8 @@
             if k == 0:
                 own = lax.dynamic_slice_in_dim(residual, offsets[half], width // 2, 1)
                 term = term + own.astype(jnp.float32)
-            if k == 1 and half == 1 and contexts > 2:
-                term = term + blocks[2][0, 0].astype(jnp.float32) * 0.0
+            if k == 1 and half == 0:
+                term = term + weights[1][0, 0].astype(jnp.float32) * 0.0
             terms.append(lax.optimization_barrier(term))
         for half in range(2):
             term = terms[half]

time: 200 us -> 199 us (level)
  waiting for transfers between devices: 103 us -> 108 us
  starting transfers between devices: 28.2 us -> 24.8 us
  matrix products: 46.5 us -> 44.1 us
    ppermute x19, waiting for transfers between devices: 74.2 us -> 76.9 us  [shift(): lax.ppermute(value, axis, [(i, (i + by) % devices) for i in range(devices)])]
    ppermute x4, waiting for transfers between devices: 28.4 us -> 30.7 us  [to_next_owner(): return lax.ppermute(rows, ('pipe', 'ctx'), pairs)]
    ppermute x4, starting transfers between devices: 9.17 us -> 6.84 us  [to_next_owner(): return lax.ppermute(rows, ('pipe', 'ctx'), pairs)]
    dot_general x8, matrix products: 23.4 us -> 21.4 us  [mixed_halves(): term = jnp.dot(attended, weights[half], preferred_element_type=jnp.float32)]
  transfers between devices with their start and end apart: 23 -> 23, of which waited for: 11 -> 10; matrix products, arithmetic and copies ran while one was open for 26% -> 26% of each run, Pallas kernels for 0% -> 0%
where the time goes in v17:
time: 199 us; the launch traced here: 198 us
  waiting for transfers between devices  108 us (54%)
  matrix products  44.1 us (22%)
  starting transfers between devices  24.8 us (12%)
  local copies, waits for them, and re-layouts  10.3 us (5%)
  other arithmetic  6 us (3%)
  between operations  5.28 us (3%)
    ppermute x19, waiting for transfers between devices, shift(): lax.ppermute(value, axis, [(i, (i + by) % devices) for i in range(devices)])  76.9 us
    ppermute x4, waiting for transfers between devices, to_next_owner(): return lax.ppermute(rows, ('pipe', 'ctx'), pairs)  30.7 us
    dot_general x8, matrix products, mixed_halves(): term = jnp.dot(attended, weights[half], preferred_element_type=jnp.float32)  21.4 us
    ppermute x19, starting transfers between devices, shift(): lax.ppermute(value, axis, [(i, (i + by) % devices) for i in range(devices)])  17.9 us
    ppermute x4, starting transfers between devices, to_next_owner(): return lax.ppermute(rows, ('pipe', 'ctx'), pairs)  6.84 us
    dot_general x4, matrix products, attend_block(): jnp.einsum('hqk,kd->qhd', attention_weights, value_rows, preferred_elemen...  6.6 us
    sub x4, matrix products, attend_block(): attention_weights = jax.nn.softmax(scores, axis=-1).astype(jnp.bfloat16)  6.02 us
    dot_general x2, matrix products, gate_and_up(): gate_up = jnp.dot(rows, in_weight[0, 0], preferred_element_type=jnp.float32)  5.21 us
  transfers between devices with their start and end apart: 23, of which 10 were waited for; matrix products, arithmetic and copies ran while one was open for 26% of the time, Pallas kernels for 0%

profile of v17, /device:TPU:0, one launch (start us, length us, event | category | flops | bytes accessed | tf_op | source)
XLA Modules:
  0.0 198.1 jit_solution(13216257398035087599)
XLA Ops:
  0.0 0.5 collective-permute-start.5
  0.5 1.0 dynamic-slice_bitcast_fusion.7
  1.4 4.8 %collective-permute-start.2 = (bf16[128,256]{1,0:T(8,128)(2,1)S(1)}, bf16[128,256]{1,0:T(8,128)(2,1)S(1)}, u32[]{:S(2)}, u32[]{:S(2)}) collective-permute-start(bf16[128,256]{1,0:T(8,128)(2,1)S(1)} %pad_maximum_fusion.4), channel_id=1, source_target_pairs={{0,6},{2,0},{4,2},{6,4},{1,7},{3,1},{5,3},{7,5},{8,14},{10,8},{12,... | collective-permute-start | bytes 196616 | tf_op jit(solution)/shard_map/ppermute | solution.py:15
  6.3 1.1 collective-permute-start.1
  7.4 1.3 constant_dynamic-slice_fusion.3
  8.8 3.4 %collective-permute-start.3 = (bf16[128,1024]{0,1:T(8,128)(2,1)S(1)}, bf16[128,1024]{0,1:T(8,128)(2,1)S(1)}, u32[]{:S(2)}, u32[]{:S(2)}) collective-permute-start(bf16[128,1024]{0,1:T(8,128)(2,1)S(1)} %bitcast.268), channel_id=1, source_target_pairs={{0,2},{2,4},{4,6},{6,0},{1,3},{3,5},{5,7},{7,1},{8,10},{10,12},{12... | collective-permute-start | bytes 786440 | tf_op jit(solution)/shard_map/ppermute | solution.py:15
  12.8 0.9 broadcast_compare_fusion.2
  13.7 0.5 fusion.88
  14.3 0.9 copy.38
  15.2 0.8 copy.47
  16.2 3.7 %collective-permute-done.1 = bf16[128,256]{1,0:T(8,128)(2,1)S(1)} collective-permute-done((bf16[128,256]{1,0:T(8,128)(2,1)S(1)}, bf16[128,256]{1,0:T(8,128)(2,1)S(1)}, u32[]{:S(2)}, u32[]{:S(2)}) %collective-permute-start.1) | collective-permute-done | bytes 65568 | tf_op jit(solution)/shard_map/ppermute | solution.py:15
  19.9 0.9 collective-permute-start.4
  20.9 1.5 collective-permute-start.9
  22.3 0.8 fusion.118
  23.1 1.0 convolution_convert_fusion.5
  24.2 3.1 %fusion.122 = bf16[128,2048]{1,0:T(8,128)(2,1)S(1)} fusion(bf16[128,1024]{0,1:T(8,128)(2,1)S(1)} %bitcast.254, bf16[1024,2048]{1,0:T(8,128)(2,1)} %collective-permute-done.5), kind=kOutput, calls=%fused_computation.202 | convolution fusion | flops 536870912 | bytes 4980736 | tf_op jit(solution)/shard_map/dot_general | solution.py:92
  27.3 0.5 slice.141
  27.8 0.6 collective-permute-start.7
  28.4 1.2 slice.139
  30.3 0.7 broadcast_add_fusion
  31.0 0.6 slice.140
  31.6 0.6 collective-permute-start.6
  33.5 27.7 %collective-permute-done.4 = bf16[128,1024]{0,1:T(8,128)(2,1)S(1)} collective-permute-done((bf16[128,1024]{0,1:T(8,128)(2,1)}, bf16[128,1024]{0,1:T(8,128)(2,1)S(1)}, u32[]{:S(2)}, u32[]{:S(2)}) %collective-permute-start.4) | collective-permute-done | bytes 262176 | tf_op jit(solution)/shard_map/ppermute | solution.py:15
  61.2 2.2 %fusion.119 = f32[8,128]{1,0:T(8,128)} fusion(pred[128,512]{0,1:T(8,128)(4,1)} %get-tuple-element.32, bf16[128,8,128]{0,2,1:T(8,128)(2,1)S(1)} %bitcast.264, bf16[512,256]{1,0:T(8,128)(2,1)S(1)} %pad_maximum_fusion.1), kind=kOutput, calls=%fused_computation.199 | convolution fusion | flops 136315392 | bytes 462848 | tf_op jit(solution)/shard_map/sub | solution.py:27
  63.4 1.9 convolution_convert_fusion.4
  65.3 2.9 %fusion.97 = f32[128,2048]{1,0:T(8,128)S(1)} fusion(bf16[128,1024]{0,1:T(8,128)(2,1)S(1)} %bitcast.260, bf16[1,1024,2048]{2,1,0:T(8,128)(2,1)} %param.12), kind=kOutput, calls=%fused_computation.183 | convolution fusion | flops 536870912 | bytes 5505024 | tf_op jit(solution)/shard_map/dot_general | solution.py:92
  68.2 2.9 %fusion.123 = f32[128,2048]{1,0:T(8,128)S(1)} fusion(bf16[128,1024]{0,1:T(8,128)(2,1)S(1)} %bitcast.261, bf16[1024,2048]{1,0:T(8,128)(2,1)} %collective-permute-done.5), kind=kOutput, calls=%fused_computation.203 | convolution fusion | flops 536870912 | bytes 5505024 | tf_op jit(solution)/shard_map/dot_general | solution.py:92
  71.3 0.6 slice.143
  72.1 0.6 slice.142
  74.1 1.7 fusion.120
  75.8 1.9 convolution_convert_fusion.3
  77.7 1.7 collective-permute-start.8
  79.5 2.9 %fusion.95 = f32[128,2048]{1,0:T(8,128)S(1)} fusion(bf16[128,1024]{0,1:T(8,128)(2,1)S(1)} %bitcast.258, bf16[1,1024,2048]{2,1,0:T(8,128)(2,1)} %param.12), kind=kOutput, calls=%fused_computation.181 | convolution fusion | flops 536870912 | bytes 5505024 | tf_op jit(solution)/shard_map/dot_general | solution.py:92
  82.4 2.9 %fusion.124 = f32[128,2048]{1,0:T(8,128)S(1)} fusion(bf16[128,1024]{0,1:T(8,128)(2,1)S(1)} %bitcast.259, bf16[1024,2048]{1,0:T(8,128)(2,1)} %collective-permute-done.5), kind=kOutput, calls=%fused_computation.204 | convolution fusion | flops 536870912 | bytes 5505024 | tf_op jit(solution)/shard_map/dot_general | solution.py:92
  85.4 2.6 %collective-permute-done.11 = bf16[128,2048]{1,0:T(8,128)(2,1)S(1)} collective-permute-done((bf16[128,2048]{1,0:T(8,128)(2,1)S(1)}, bf16[128,2048]{1,0:T(8,128)(2,1)S(1)}, u32[]{:S(2)}, u32[]{:S(2)}) %collective-permute-start.11) | collective-permute-done | bytes 524320 | tf_op jit(solution)/shard_map/ppermute | solution.py:15
  88.1 0.5 slice.145
  88.6 7.5 %collective-permute-done.10 = bf16[128,2048]{1,0:T(8,128)(2,1)S(1)} collective-permute-done((bf16[128,2048]{1,0:T(8,128)(2,1)S(1)}, bf16[128,2048]{1,0:T(8,128)(2,1)S(1)}, u32[]{:S(2)}, u32[]{:S(2)}) %collective-permute-start.10) | collective-permute-done | bytes 524320 | tf_op jit(solution)/shard_map/ppermute | solution.py:15
  96.2 0.9 add_convert_fusion.1
  97.1 1.2 slice.144
  99.5 1.4 fusion.121
  100.9 1.8 convolution_convert_fusion.2
  102.7 2.9 %convolution_add_fusion.1 = f32[128,2048]{1,0:T(8,128)S(1)} fusion(bf16[128,1024]{0,1:T(8,128)(2,1)S(1)} %bitcast.256, bf16[1,1,128,4096]{3,2,1,0:T(8,128)(2,1)S(1)} %copy-done.1, s32[]{:T(128)S(6)} %select_n.179, bf16[1,1024,2048]{2,1,0:T(8,128)(2,1)} %param.12), kind=kOutput, calls=%fused_computation.23 | convolution fusion | flops 537395200 | bytes 6029316 | tf_op jit(solution)/shard_map/dot_general | solution.py:92
  105.6 2.9 %convolution_add_fusion = f32[128,2048]{1,0:T(8,128)S(1)} fusion(bf16[128,1024]{0,1:T(8,128)(2,1)S(1)} %bitcast.257, bf16[1024,2048]{1,0:T(8,128)(2,1)} %collective-permute-done.5, bf16[1,1,128,4096]{3,2,1,0:T(8,128)(2,1)S(1)} %copy-done.1, s32[]{:T(128)S(6)} %select_n.180), kind=kOutput, calls=%fused_computation.22 | convolution fusion | flops 537395200 | bytes 6029316 | tf_op jit(solution)/shard_map/dot_general | solution.py:92
  108.8 6.5 %collective-permute-done.12 = bf16[128,2048]{1,0:T(8,128)(2,1)S(1)} collective-permute-done((bf16[128,2048]{1,0:T(8,128)(2,1)}, bf16[128,2048]{1,0:T(8,128)(2,1)S(1)}, u32[]{:S(2)}, u32[]{:S(2)}) %collective-permute-start.12) | collective-permute-done | bytes 524320 | tf_op jit(solution)/shard_map/ppermute | solution.py:15
  115.4 0.2 fusion.25
  115.7 0.3 copy-done.9
  116.0 0.6 convolution_convert_fusion
  116.9 2.3 %collective-permute-start.14 = (bf16[1,48,4224]{2,1,0:T(8,128)(2,1)S(1)}, bf16[1,48,4224]{2,1,0:T(8,128)(2,1)S(1)}, u32[]{:S(2)}, u32[]{:S(2)}) collective-permute-start(bf16[1,48,4224]{2,1,0:T(8,128)(2,1)S(1)} %get-tuple-element.12), channel_id=1, source_target_pairs={{0,2},{2,4},{4,6},{6,0},{1,3},{3,5},{5,7},{7,1},{8,10},{10,12},{12... | collective-permute-start | bytes 1216520 | tf_op jit(solution)/shard_map/ppermute | solution.py:15
  119.1 11.0 %collective-permute-done.16 = bf16[1,48,4224]{2,1,0:T(8,128)(2,1)S(1)} collective-permute-done((bf16[1,48,4224]{2,1,0:T(8,128)(2,1)S(1)}, bf16[1,48,4224]{2,1,0:T(8,128)(2,1)S(1)}, u32[]{:S(2)}, u32[]{:S(2)}) %collective-permute-start.16) | collective-permute-done | bytes 405536 | tf_op jit(solution)/shard_map/ppermute | solution.py:15
  130.1 16.2 %collective-permute-done.15 = bf16[1,48,4224]{2,1,0:T(8,128)(2,1)S(1)} collective-permute-done((bf16[1,48,4224]{2,1,0:T(8,128)(2,1)S(1)}, bf16[1,48,4224]{2,1,0:T(8,128)(2,1)S(1)}, u32[]{:S(2)}, u32[]{:S(2)}) %collective-permute-start.15) | collective-permute-done | bytes 405536 | tf_op jit(solution)/shard_map/ppermute | solution.py:15
  146.7 0.5 multiply_reduce_fusion.1
  147.3 2.6 %fusion.17 = f32[192,1536]{1,0:T(8,128)S(1)} fusion(bf16[192,4096]{1,0:T(8,128)(2,1)S(1)} %bitcast.250, bf16[1,1,4096,1536]{3,2,1,0:T(8,128)(2,1)S(1)} %bitcast.276, f32[192]{0:T(256)S(1)} %add_rsqrt_fusion.1), kind=kOutput, calls=%fused_computation.20 | convolution fusion | flops 2416214016 | bytes 15336192 | tf_op jit(solution)/shard_map/dot_general | solution.py:183
  150.1 0.5 multiply_reduce_fusion
  150.6 2.6 %fusion.20 = f32[192,1536]{1,0:T(8,128)S(1)} fusion(bf16[192,4096]{1,0:T(8,128)(2,1)S(1)} %bitcast.253, bf16[1,1,4096,1536]{3,2,1,0:T(8,128)(2,1)S(1)} %bitcast.276, f32[192]{0:T(256)S(1)} %add_rsqrt_fusion), kind=kOutput, calls=%fused_computation.21 | convolution fusion | flops 2416214016 | bytes 15336192 | tf_op jit(solution)/shard_map/dot_general | solution.py:183
  153.3 1.4 fusion.12
  154.7 0.4 collective-permute-start.18
  155.1 1.4 fusion.10
  156.7 1.4 collective-permute-done.18
  158.2 0.8 fusion.16
  159.1 1.5 collective-permute-start.19
  160.6 0.5 collective-permute-start.21
  161.1 4.8 %collective-permute-start.20 = (bf16[1,48,4096]{2,1,0:T(8,128)(2,1)S(1)}, bf16[1,48,4096]{2,1,0:T(8,128)(2,1)S(1)}, u32[]{:S(2)}, u32[]{:S(2)}) collective-permute-start(bf16[1,48,4096]{2,1,0:T(8,128)(2,1)S(1)} %get-tuple-element.16), channel_id=1, source_target_pairs={{0,14},{2,8},{4,10},{6,12},{8,22},{10,16},{12,18},{14,20},{16,30},... | collective-permute-start | bytes 1179656 | tf_op jit(solution)/shard_map/ppermute | solution.py:219
  165.9 30.7 %collective-permute-done.19 = bf16[1,48,4096]{2,1,0:T(8,128)(2,1)S(1)} collective-permute-done((bf16[1,48,4096]{2,1,0:T(8,128)(2,1)S(1)}, bf16[1,48,4096]{2,1,0:T(8,128)(2,1)S(1)}, u32[]{:S(2)}, u32[]{:S(2)}) %collective-permute-start.19) | collective-permute-done | bytes 393248 | tf_op jit(solution)/shard_map/ppermute | solution.py:219
  196.7 1.5 fusion.15
  (103 shorter events, 3.1 us)
Async XLA Ops:
  0.0 12.3 %copy-start.5 = (s32[1,1,128,1]{2,3,1,0:T(1,128)S(1)}, s32[1,1,128,1]{2,3,1,0:T(1,128)}, u32[]{:S(2)}) copy-start(s32[1,1,128,1]{2,3,1,0:T(1,128)} %param.16) | copy-start | bytes 1540
  0.0 24.2 %collective-permute-start.5 = (bf16[1024,2048]{1,0:T(8,128)(2,1)}, bf16[1024,2048]{1,0:T(8,128)(2,1)}, u32[]{:S(2)}, u32[]{:S(2)}) collective-permute-start(bf16[1024,2048]{1,0:T(8,128)(2,1)} %bitcast.247), channel_id=1, source_target_pairs={{0,1},{1,0},{2,3},{3,2},{4,5},{5,4},{6,7},{7,6},{8,9},{9,8},{10,11... | collective-permute-start | bytes 12582920 | tf_op jit(solution)/shard_map/ppermute | solution.py:15
  0.5 12.3 %copy-start.10 = (f32[1,1,128,1]{2,3,1,0:T(1,128)S(1)}, f32[1,1,128,1]{2,3,1,0:T(1,128)}, u32[]{:S(2)}) copy-start(f32[1,1,128,1]{2,3,1,0:T(1,128)} %param.17) | copy-start | bytes 1540
  0.5 12.3 %copy-start.4 = (f32[1,4096]{1,0:T(1,128)S(1)}, f32[1,4096]{1,0:T(1,128)}, u32[]{:S(2)}) copy-start(f32[1,4096]{1,0:T(1,128)} %param.13) | copy-start | bytes 49156
  1.4 14.8 %collective-permute-start.2 = (bf16[128,256]{1,0:T(8,128)(2,1)S(1)}, bf16[128,256]{1,0:T(8,128)(2,1)S(1)}, u32[]{:S(2)}, u32[]{:S(2)}) collective-permute-start(bf16[128,256]{1,0:T(8,128)(2,1)S(1)} %pad_maximum_fusion.4), channel_id=1, source_target_pairs={{0,6},{2,0},{4,2},{6,4},{1,7},{3,1},{5,3},{7,5},{8,14},{10,8},{12,... | collective-permute-start | bytes 196616 | tf_op jit(solution)/shard_map/ppermute | solution.py:15
  6.3 9.9 %collective-permute-start = (bf16[128,256]{1,0:T(8,128)(2,1)S(1)}, bf16[128,256]{1,0:T(8,128)(2,1)S(1)}, u32[]{:S(2)}, u32[]{:S(2)}) collective-permute-start(bf16[128,256]{1,0:T(8,128)(2,1)S(1)} %pad_maximum_fusion.2), channel_id=1, source_target_pairs={{0,2},{2,4},{4,6},{6,0},{1,3},{3,5},{5,7},{7,1},{8,10},{10,12},{12... | collective-permute-start | bytes 196616 | tf_op jit(solution)/shard_map/ppermute | solution.py:15
  6.3 13.6 %collective-permute-start.1 = (bf16[128,256]{1,0:T(8,128)(2,1)S(1)}, bf16[128,256]{1,0:T(8,128)(2,1)S(1)}, u32[]{:S(2)}, u32[]{:S(2)}) collective-permute-start(bf16[128,256]{1,0:T(8,128)(2,1)S(1)} %pad_maximum_fusion.3), channel_id=1, source_target_pairs={{0,4},{2,6},{4,0},{6,2},{1,5},{3,7},{5,1},{7,3},{8,12},{10,14},{12... | collective-permute-start | bytes 196616 | tf_op jit(solution)/shard_map/ppermute | solution.py:15
  8.8 11.1 %collective-permute-start.3 = (bf16[128,1024]{0,1:T(8,128)(2,1)S(1)}, bf16[128,1024]{0,1:T(8,128)(2,1)S(1)}, u32[]{:S(2)}, u32[]{:S(2)}) collective-permute-start(bf16[128,1024]{0,1:T(8,128)(2,1)S(1)} %bitcast.268), channel_id=1, source_target_pairs={{0,2},{2,4},{4,6},{6,0},{1,3},{3,5},{5,7},{7,1},{8,10},{10,12},{12... | collective-permute-start | bytes 786440 | tf_op jit(solution)/shard_map/ppermute | solution.py:15
  12.8 10.4 %copy-start.7 = (s32[128]{0:T(128)}, s32[128]{0:T(128)S(1)}, u32[]{:S(2)}) copy-start(s32[128]{0:T(128)S(1)} %select_reduce_fusion) | copy-start | bytes 1540
  19.9 43.5 %copy-start.2 = (bf16[512,256]{1,0:T(8,128)(2,1)}, bf16[512,256]{1,0:T(8,128)(2,1)S(1)}, u32[]{:S(2)}) copy-start(bf16[512,256]{1,0:T(8,128)(2,1)S(1)} %pad_maximum_fusion.1) | copy-start | bytes 786436
  19.9 41.2 %collective-permute-start.4 = (bf16[128,1024]{0,1:T(8,128)(2,1)}, bf16[128,1024]{0,1:T(8,128)(2,1)S(1)}, u32[]{:S(2)}, u32[]{:S(2)}) collective-permute-start(bf16[128,1024]{0,1:T(8,128)(2,1)} %bitcast.13), channel_id=1, source_target_pairs={{0,4},{2,6},{4,0},{6,2},{1,5},{3,7},{5,1},{7,3},{8,12},{10,14},{12... | collective-permute-start | bytes 786440 | tf_op jit(solution)/shard_map/ppermute | solution.py:15
  20.9 53.2 %collective-permute-start.9 = (bf16[128,1024]{0,1:T(8,128)(2,1)}, bf16[128,1024]{0,1:T(8,128)(2,1)S(1)}, u32[]{:S(2)}, u32[]{:S(2)}) collective-permute-start(bf16[128,1024]{0,1:T(8,128)(2,1)} %bitcast.33), channel_id=1, source_target_pairs={{0,6},{2,0},{4,2},{6,4},{1,7},{3,1},{5,3},{7,5},{8,14},{10,8},{12,... | collective-permute-start | bytes 786440 | tf_op jit(solution)/shard_map/ppermute | solution.py:15
  24.2 6.1 %copy-start = (bf16[1,1024,2048]{2,1,0:T(8,128)(2,1)S(1)}, bf16[1,1024,2048]{2,1,0:T(8,128)(2,1)}, u32[]{:S(2)}) copy-start(bf16[1,1024,2048]{2,1,0:T(8,128)(2,1)} %param.12) | copy-start | bytes 12582916
  27.8 43.4 %collective-permute-start.7 = (bf16[128,2048]{1,0:T(8,128)(2,1)S(1)}, bf16[128,2048]{1,0:T(8,128)(2,1)S(1)}, u32[]{:S(2)}, u32[]{:S(2)}) collective-permute-start(bf16[128,2048]{1,0:T(8,128)(2,1)S(1)} %fusion.122), channel_id=1, source_target_pairs={{0,2},{2,4},{4,6},{6,0},{1,3},{3,5},{5,7},{7,1},{8,10},{10,12},{12... | collective-permute-start | bytes 1572872 | tf_op jit(solution)/shard_map/ppermute | solution.py:15
  31.6 40.3 %collective-permute-start.6 = (bf16[128,2048]{1,0:T(8,128)(2,1)S(1)}, bf16[128,2048]{1,0:T(8,128)(2,1)S(1)}, u32[]{:S(2)}, u32[]{:S(2)}) collective-permute-start(bf16[128,2048]{1,0:T(8,128)(2,1)S(1)} %broadcast_add_fusion), channel_id=1, source_target_pairs={{0,2},{2,4},{4,6},{6,0},{1,3},{3,5},{5,7},{7,1},{8,10},{10,12},{12... | collective-permute-start | bytes 1572872 | tf_op jit(solution)/shard_map/ppermute | solution.py:15
  71.2 2.9 %copy-start.6 = (s32[1,1,128,1]{2,3,1,0:T(1,128)S(1)}, s32[1,1,128,1]{2,3,1,0:T(1,128)}, u32[]{:S(2)}) copy-start(s32[1,1,128,1]{2,3,1,0:T(1,128)} %param.16) | copy-start | bytes 1540
  71.2 2.9 %copy-start.8 = (s32[128]{0:T(128)S(1)}, s32[128]{0:T(128)}, u32[]{:S(2)}) copy-start(s32[128]{0:T(128)} %copy-done.7) | copy-start | bytes 1540
  71.9 16.1 %collective-permute-start.11 = (bf16[128,2048]{1,0:T(8,128)(2,1)S(1)}, bf16[128,2048]{1,0:T(8,128)(2,1)S(1)}, u32[]{:S(2)}, u32[]{:S(2)}) collective-permute-start(bf16[128,2048]{1,0:T(8,128)(2,1)S(1)} %add_convert_fusion.2), channel_id=1, source_target_pairs={{0,2},{2,4},{4,6},{6,0},{1,3},{3,5},{5,7},{7,1},{8,10},{10,12},{12... | collective-permute-start | bytes 1572872 | tf_op jit(solution)/shard_map/ppermute | solution.py:15
  72.6 23.5 %collective-permute-start.10 = (bf16[128,2048]{1,0:T(8,128)(2,1)S(1)}, bf16[128,2048]{1,0:T(8,128)(2,1)S(1)}, u32[]{:S(2)}, u32[]{:S(2)}) collective-permute-start(bf16[128,2048]{1,0:T(8,128)(2,1)S(1)} %add_convert_fusion.3), channel_id=1, source_target_pairs={{0,2},{2,4},{4,6},{6,0},{1,3},{3,5},{5,7},{7,1},{8,10},{10,12},{12... | collective-permute-start | bytes 1572872 | tf_op jit(solution)/shard_map/ppermute | solution.py:15
  74.1 1.8 copy-start.3
  77.7 7.6 %collective-permute-start.8 = (f32[1,128]{1,0:T(1,128)S(1)}, f32[1,128]{1,0:T(1,128)S(1)}, u32[]{:S(2)}, u32[]{:S(2)}) collective-permute-start(f32[1,128]{1,0:T(1,128)S(1)} %convert_add_fusion), channel_id=1, source_target_pairs={{0,8},{8,16},{16,24},{24,0},{1,9},{9,17},{17,25},{25,1},{2,10},{10... | collective-permute-start | bytes 1544 | tf_op jit(solution)/shard_map/ppermute | solution.py:15
  85.3 11.8 %copy-start.11 = (f32[1,128]{1,0:T(1,128)}, f32[1,128]{1,0:T(1,128)S(1)}, u32[]{:S(2)}) copy-start(f32[1,128]{1,0:T(1,128)S(1)} %collective-permute-done.8) | copy-start | bytes 1540
  88.6 20.0 %collective-permute-start.13 = (bf16[128,2048]{1,0:T(8,128)(2,1)S(1)}, bf16[128,2048]{1,0:T(8,128)(2,1)S(1)}, u32[]{:S(2)}, u32[]{:S(2)}) collective-permute-start(bf16[128,2048]{1,0:T(8,128)(2,1)S(1)} %add_convert_fusion), channel_id=1, source_target_pairs={{0,2},{2,4},{4,6},{6,0},{1,3},{3,5},{5,7},{7,1},{8,10},{10,12},{12... | collective-permute-start | bytes 1572872 | tf_op jit(solution)/shard_map/ppermute | solution.py:15
  98.3 17.0 %collective-permute-start.12 = (bf16[128,2048]{1,0:T(8,128)(2,1)}, bf16[128,2048]{1,0:T(8,128)(2,1)S(1)}, u32[]{:S(2)}, u32[]{:S(2)}) collective-permute-start(bf16[128,2048]{1,0:T(8,128)(2,1)} %add_convert_fusion.1), channel_id=1, source_target_pairs={{0,2},{2,4},{4,6},{6,0},{1,3},{3,5},{5,7},{7,1},{8,10},{10,12},{12... | collective-permute-start | bytes 1572872 | tf_op jit(solution)/shard_map/ppermute | solution.py:15
  100.9 1.8 copy-start.1
  108.6 38.6 %slice-start = ((s8[12582912]{0:T(1024)(128)(4,1)}), s8[4194304]{0:T(1024)(128)(4,1)S(1)}, s32[]{:S(2)}) async-start(s8[12582912]{0:T(1024)(128)(4,1)} %bitcast.275), calls=%async_computation | async-start | bytes 8388608
  115.4 0.6 copy-start.9
  115.4 31.8 %slice-start.1 = ((s8[12582912]{0:T(1024)(128)(4,1)}), s8[4194304]{0:T(1024)(128)(4,1)S(1)}, s32[]{:S(2)}) async-start(s8[12582912]{0:T(1024)(128)(4,1)} %bitcast.275), calls=%async_computation.1 | async-start | bytes 8388608
  116.7 13.4 %collective-permute-start.16 = (bf16[1,48,4224]{2,1,0:T(8,128)(2,1)S(1)}, bf16[1,48,4224]{2,1,0:T(8,128)(2,1)S(1)}, u32[]{:S(2)}, u32[]{:S(2)}) collective-permute-start(bf16[1,48,4224]{2,1,0:T(8,128)(2,1)S(1)} %get-tuple-element.10), channel_id=1, source_target_pairs={{0,6},{2,0},{4,2},{6,4},{1,7},{3,1},{5,3},{7,5},{8,14},{10,8},{12,... | collective-permute-start | bytes 1216520 | tf_op jit(solution)/shard_map/ppermute | solution.py:15
  116.7 30.5 %slice-start.2 = ((s8[12582912]{0:T(1024)(128)(4,1)}), s8[4194304]{0:T(1024)(128)(4,1)S(1)}, s32[]{:S(2)}) async-start(s8[12582912]{0:T(1024)(128)(4,1)} %bitcast.275), calls=%async_computation.2 | async-start | bytes 8388608
  116.8 29.6 %collective-permute-start.15 = (bf16[1,48,4224]{2,1,0:T(8,128)(2,1)S(1)}, bf16[1,48,4224]{2,1,0:T(8,128)(2,1)S(1)}, u32[]{:S(2)}, u32[]{:S(2)}) collective-permute-start(bf16[1,48,4224]{2,1,0:T(8,128)(2,1)S(1)} %get-tuple-element.11), channel_id=1, source_target_pairs={{0,4},{2,6},{4,0},{6,2},{1,5},{3,7},{5,1},{7,3},{8,12},{10,14},{12... | collective-permute-start | bytes 1216520 | tf_op jit(solution)/shard_map/ppermute | solution.py:15
  116.9 29.5 %collective-permute-start.14 = (bf16[1,48,4224]{2,1,0:T(8,128)(2,1)S(1)}, bf16[1,48,4224]{2,1,0:T(8,128)(2,1)S(1)}, u32[]{:S(2)}, u32[]{:S(2)}) collective-permute-start(bf16[1,48,4224]{2,1,0:T(8,128)(2,1)S(1)} %get-tuple-element.12), channel_id=1, source_target_pairs={{0,2},{2,4},{4,6},{6,0},{1,3},{3,5},{5,7},{7,1},{8,10},{10,12},{12... | collective-permute-start | bytes 1216520 | tf_op jit(solution)/shard_map/ppermute | solution.py:15
  146.7 3.5 %collective-permute-start.17 = (bf16[4,48,4096]{2,1,0:T(8,128)(2,1)S(1)}, bf16[4,48,4096]{2,1,0:T(8,128)(2,1)S(1)}, u32[]{:S(2)}, u32[]{:S(2)}) collective-permute-start(bf16[4,48,4096]{2,1,0:T(8,128)(2,1)S(1)} %bitcast.248), channel_id=1, source_target_pairs={{0,1},{1,0},{2,3},{3,2},{4,5},{5,4},{6,7},{7,6},{8,9},{9,8},{10,11... | collective-permute-start | bytes 4718600 | tf_op jit(solution)/shard_map/ppermute | solution.py:15
  149.9 3.4 %slice-start.3 = ((s8[6291456]{0:T(1024)(128)(4,1)}), s8[4194304]{0:T(1024)(128)(4,1)S(1)}, s32[]{:S(2)}) async-start(s8[6291456]{0:T(1024)(128)(4,1)} %bitcast.277), calls=%async_computation.3 | async-start | bytes 8388608
  150.6 2.6 %slice-start.4 = ((s8[6291456]{0:T(1024)(128)(4,1)}), s8[2097152]{0:T(1024)(128)(4,1)S(1)}, s32[]{:S(2)}) async-start(s8[6291456]{0:T(1024)(128)(4,1)} %bitcast.277), calls=%async_computation.4 | async-start | bytes 4194304
  154.7 3.5 %collective-permute-start.18 = (bf16[4,48,4096]{2,1,0:T(8,128)(2,1)S(1)}, bf16[4,48,4096]{2,1,0:T(8,128)(2,1)S(1)}, u32[]{:S(2)}, u32[]{:S(2)}) collective-permute-start(bf16[4,48,4096]{2,1,0:T(8,128)(2,1)S(1)} %bitcast.279), channel_id=1, source_target_pairs={{0,1},{1,0},{2,3},{3,2},{4,5},{5,4},{6,7},{7,6},{8,9},{9,8},{10,11... | collective-permute-start | bytes 4718600 | tf_op jit(solution)/shard_map/ppermute | solution.py:15
  159.0 7.0 %copy-start.12 = (f32[1,128]{1,0:T(1,128)S(1)}, f32[1,128]{1,0:T(1,128)}, u32[]{:S(2)}) copy-start(f32[1,128]{1,0:T(1,128)} %copy-done.11) | copy-start | bytes 1540
  159.1 37.6 %collective-permute-start.19 = (bf16[1,48,4096]{2,1,0:T(8,128)(2,1)S(1)}, bf16[1,48,4096]{2,1,0:T(8,128)(2,1)S(1)}, u32[]{:S(2)}, u32[]{:S(2)}) collective-permute-start(bf16[1,48,4096]{2,1,0:T(8,128)(2,1)S(1)} %get-tuple-element.13), channel_id=1, source_target_pairs={{0,8},{2,10},{4,12},{6,14},{8,16},{10,18},{12,20},{14,22},{16,24},... | collective-permute-start | bytes 1179656 | tf_op jit(solution)/shard_map/ppermute | solution.py:219
  160.6 36.0 %collective-permute-start.22 = (bf16[1,48,4096]{2,1,0:T(8,128)(2,1)S(1)}, bf16[1,48,4096]{2,1,0:T(8,128)(2,1)S(1)}, u32[]{:S(2)}, u32[]{:S(2)}) collective-permute-start(bf16[1,48,4096]{2,1,0:T(8,128)(2,1)S(1)} %get-tuple-element.14), channel_id=1, source_target_pairs={{0,10},{2,12},{4,14},{6,8},{8,18},{10,20},{12,22},{14,16},{16,26},... | collective-permute-start | bytes 1179656 | tf_op jit(solution)/shard_map/ppermute | solution.py:219
  160.6 36.0 %collective-permute-start.21 = (bf16[1,48,4096]{2,1,0:T(8,128)(2,1)S(1)}, bf16[1,48,4096]{2,1,0:T(8,128)(2,1)S(1)}, u32[]{:S(2)}, u32[]{:S(2)}) collective-permute-start(bf16[1,48,4096]{2,1,0:T(8,128)(2,1)S(1)} %get-tuple-element.15), channel_id=1, source_target_pairs={{0,12},{2,14},{4,8},{6,10},{8,20},{10,22},{12,16},{14,18},{16,28},... | collective-permute-start | bytes 1179656 | tf_op jit(solution)/shard_map/ppermute | solution.py:219
  161.1 35.6 %collective-permute-start.20 = (bf16[1,48,4096]{2,1,0:T(8,128)(2,1)S(1)}, bf16[1,48,4096]{2,1,0:T(8,128)(2,1)S(1)}, u32[]{:S(2)}, u32[]{:S(2)}) collective-permute-start(bf16[1,48,4096]{2,1,0:T(8,128)(2,1)S(1)} %get-tuple-element.16), channel_id=1, source_target_pairs={{0,14},{2,8},{4,10},{6,12},{8,22},{10,16},{12,18},{14,20},{16,30},... | collective-permute-start | bytes 1179656 | tf_op jit(solution)/shard_map/ppermute | solution.py:219
